TPU v7x, 32 devices: a whole 2x2x4 slice. The times are simulated.
32 devices in a mesh: parts: 2 (over x), tok: 16 (over z, y, core).
Axes of the slice: x: 2, y: 2, z: 4, core: 2. Of those that a mesh axis runs over, the one named last changes fastest.
Arguments:
- queries: bfloat16 [32768, 1024], P(('parts', 'tok')), parts along dimension 0, may hold values from -6 to 6
- keys: bfloat16 [32768, 1024], P(('parts', 'tok')), parts along dimension 0, may hold values from -6 to 6
- values: bfloat16 [32768, 1024], P(('parts', 'tok')), parts along dimension 0, may hold values from -6 to 6
- step_size: float32 [4, 32768], P(None, ('parts', 'tok')), parts along dimension 1, may hold values from 10 to 100
- fast_in: float32 [4, 256, 1024], P(None, 'tok'), may hold values from -6 to 6
- fast_out: float32 [4, 512, 256], P(None, 'tok'), may hold values from -6 to 6
Outputs:
- output: bfloat16 [32768, 1024], P(('parts', 'tok')), parts along dimension 0
- fast_in_next: float32 [8, 256, 1024], P('parts', 'tok'), parts along dimension 0
- fast_out_next: float32 [8, 512, 256], P('parts', 'tok'), parts along dimension 0
There are 2 independent parts, one for each index of `parts`. A program takes and returns all parts, laid end to end along the dimension named above; an argument that names none is the same for every part. Nothing has to cross between parts.
All inputs are finite; a program needn't handle non-finite values.
Results may differ from a plain program's by a relative error of at most 0.012.
The roundings to bfloat16 on the way count: a program that leaves them out, or rounds other values in their place, can miss the bound.
Values may be sent and summed in bfloat16 or wider, within the bound.
No kernel may reach another device: no remote copies, remote signals or barrier semaphores. Data moves between devices by JAX's collectives and lax.ppermute only.
A program may use at most 128 MiB of HBM per device.

v0:
```python
import math

import jax
import jax.numpy as jnp
from jax import lax
from jax.sharding import PartitionSpec as P


def rms_rows(matrix):
    return matrix * lax.rsqrt(jnp.mean(matrix * matrix, axis=-1, keepdims=True) + 1e-06)


def normalized_heads(tokens, heads, head_size):
    row_count = tokens.shape[0]
    wide = tokens.astype(jnp.float32).reshape(row_count, heads, head_size)
    return rms_rows(wide).astype(jnp.bfloat16)


def head_increments(key_rows, value_rows, rates, weight_in, weight_out, block_root):
    fast = weight_out.shape[0]
    in_root = 1.0 / math.sqrt(weight_in.shape[0])
    out_root = 1.0 / math.sqrt(fast)
    scaled = (rates[:, None] * block_root * value_rows.astype(jnp.float32)).astype(jnp.bfloat16)
    pre = jnp.dot(key_rows, weight_in, preferred_element_type=jnp.float32) * in_root
    gate = pre[:, :fast]
    upper = pre[:, fast:]
    sigma = jax.nn.sigmoid(gate)
    active = gate * sigma
    hidden = (active * upper).astype(jnp.bfloat16)
    back = (
        lax.dot_general(
            scaled, weight_out, (((1,), (1,)), ((), ())), preferred_element_type=jnp.float32
        )
        * out_root
    )
    d_gate = (back * upper * sigma * (1.0 + gate * (1.0 - sigma))).astype(jnp.bfloat16)
    d_up = (back * active).astype(jnp.bfloat16)
    joined = jnp.concatenate([d_gate, d_up], axis=1)
    inc_in = (
        lax.dot_general(
            key_rows, joined, (((0,), (0,)), ((), ())), preferred_element_type=jnp.float32
        )
        * in_root
    )
    inc_out = (
        lax.dot_general(
            hidden, scaled, (((0,), (0,)), ((), ())), preferred_element_type=jnp.float32
        )
        * out_root
    )
    return (inc_in, inc_out)


def local_increments(keyn, values, step_size, weight_in, weight_out, block_root):
    heads = weight_in.shape[0]
    head_size = weight_in.shape[1]
    list_in = []
    list_out = []
    for head_number in range(heads):
        value_rows = values[:, head_number * head_size : (head_number + 1) * head_size]
        part_in, part_out = head_increments(
            keyn[:, head_number, :],
            value_rows,
            step_size[head_number],
            weight_in[head_number],
            weight_out[head_number],
            block_root,
        )
        list_in.append(part_in)
        list_out.append(part_out)
    return (jnp.stack(list_in), jnp.stack(list_out))


def renorm_in(matrix):
    heads, rows_here, double = matrix.shape
    split = matrix.reshape(heads, rows_here, 2, double // 2)
    return rms_rows(split).reshape(heads, rows_here, double)


def apply_head(query_rows, weight_in, weight_out):
    fast = weight_out.shape[0]
    pre = jnp.dot(query_rows, weight_in, preferred_element_type=jnp.float32) * (
        1.0 / math.sqrt(weight_in.shape[0])
    )
    gate = pre[:, :fast]
    hidden = (gate * jax.nn.sigmoid(gate) * pre[:, fast:]).astype(jnp.bfloat16)
    return jnp.dot(hidden, weight_out, preferred_element_type=jnp.float32) * (1.0 / math.sqrt(fast))


def apply_all(queryn, next_in, next_out):
    heads = next_in.shape[0]
    pieces = []
    for head_number in range(heads):
        pieces.append(
            apply_head(queryn[:, head_number, :], next_in[head_number], next_out[head_number])
        )
    return jnp.concatenate(pieces, axis=1).astype(jnp.bfloat16)


def per_device(queries, keys, values, step_size, fast_in, fast_out):
    row_count = keys.shape[0]
    heads = fast_in.shape[0]
    head_size = keys.shape[1] // heads
    block_root = 1.0 / math.sqrt(row_count * lax.axis_size("tok"))
    keyn = normalized_heads(keys, heads, head_size)
    queryn = normalized_heads(queries, heads, head_size)
    master_in, master_out = (
        lax.all_gather(fast_in, "tok", axis=1, tiled=True),
        lax.all_gather(fast_out, "tok", axis=1, tiled=True),
    )
    inc_in, inc_out = local_increments(
        keyn,
        values,
        step_size,
        master_in.astype(jnp.bfloat16),
        master_out.astype(jnp.bfloat16),
        block_root,
    )
    total_in, total_out = lax.psum((inc_in, inc_out), "tok")
    whole_in = renorm_in(master_in + total_in)
    whole_out = rms_rows(master_out + total_out)
    output = apply_all(queryn, whole_in.astype(jnp.bfloat16), whole_out.astype(jnp.bfloat16))
    place = lax.axis_index("tok")
    fast_in_next = lax.dynamic_slice_in_dim(whole_in, place * fast_in.shape[1], fast_in.shape[1], 1)
    fast_out_next = lax.dynamic_slice_in_dim(
        whole_out, place * fast_out.shape[1], fast_out.shape[1], 1
    )
    return (output, fast_in_next, fast_out_next)


def solution(mesh):
    placed = (
        P(("parts", "tok"), None),
        P(("parts", "tok"), None),
        P(("parts", "tok"), None),
        P(None, ("parts", "tok")),
        P(None, "tok", None),
        P(None, "tok", None),
    )
    return jax.shard_map(
        per_device,
        mesh=mesh,
        in_specs=placed,
        out_specs=(P(("parts", "tok"), None), P("parts", "tok", None), P("parts", "tok", None)),
        check_vma=False,
    )
```

profile of v0, /device:TPU:1, one launch (start us, length us, event | category | flops | bytes accessed | tf_op | source)
XLA Modules:
  0.0 323.4 jit_solution(18254454834541211836)
XLA Ops:
  7.2 0.0 all-gather.5.cloned.1.call-start
  7.2 0.7 all-gather.5.cloned.1.call-update
  7.9 0.0 all-gather.3.cloned.1.call-start
  7.9 0.7 all-gather.3.cloned.1.call-update
  8.6 0.0 copy-start.4
  8.7 0.0 all-reduce.3.cloned.1.call-start
  8.7 2.9 copy.52
  11.6 0.0 copy-done.4
  11.6 0.5 fusion.2
  12.1 1.9 fusion.3
  14.0 40.2 %all-gather.5.cloned.1.call-done = f32[4,512,256]{2,1,0:T(8,128)} async-done(((f32[4,32,256]{2,1,0:T(8,128)}), f32[4,512,256]{2,1,0:T(8,128)}) %all-gather.5.cloned.1.call-update) | async-done | bytes 2097168 | tf_op jit(solution)/shard_map/all_gather | solution.py:109
  54.1 1.7 convert_element_type.97
  55.8 0.0 copy-start
  55.9 49.9 %all-gather.3.cloned.1.call-done = f32[4,256,1024]{2,1,0:T(8,128)} async-done(((f32[4,16,1024]{2,1,0:T(8,128)}), f32[4,256,1024]{2,1,0:T(8,128)}) %all-gather.3.cloned.1.call-update) | async-done | bytes 4194320 | tf_op jit(solution)/shard_map/all_gather | solution.py:108
  105.7 2.5 convert_element_type.98
  108.2 0.0 copy-done
  108.2 0.8 convolution_multiply_fusion.4
  109.0 0.0 copy-start.5
  109.0 0.8 convolution_multiply_fusion.5
  109.8 0.8 copy-done.5
  110.6 0.8 fusion.56
  111.4 1.4 multiply_convert_fusion.5
  112.8 0.8 fusion.57
  113.6 1.4 multiply_convert_fusion.7
  115.0 0.8 convolution_multiply_fusion.6
  115.8 0.8 fusion.58
  116.6 1.4 multiply_convert_fusion.9
  118.0 0.8 convolution_multiply_fusion.7
  118.7 0.8 fusion.59
  119.5 1.5 multiply_convert_fusion.11
  121.1 0.7 fusion.31
  121.8 0.7 fusion.37
  122.6 0.7 fusion.43
  123.3 0.7 fusion.49
  124.1 2.3 pad_maximum_fusion
  126.4 1.5 pad_maximum_fusion.1
  127.8 0.0 all-reduce.3.cloned.1.call-update
  127.9 2.9 copy.50
  130.7 0.5 fusion
  131.2 1.9 fusion.1
  133.1 132.3 %all-reduce.3.cloned.1.call-done = (f32[4,256,1024]{2,1,0:T(8,128)}, f32[4,512,256]{2,1,0:T(8,128)}) async-done(((f32[4,256,1024]{2,1,0:T(8,128)}, f32[4,512,256]{2,1,0:T(8,128)}), (f32[4,256,1024]{2,1,0:T(8,128)}, f32[4,512,256]{2,1,0:T(8,128)})) %all-reduce.3.cloned.1.call-update) | async-done | bytes 6291472 | tf_op jit(solution)/shard_map/psum | solution.py:119
  265.4 8.6 %fusion.86 = (f32[4,256,1024]{2,1,0:T(8,128)}, f32[4,256,1024]{2,1,0:T(8,128)}) fusion(f32[4,256,1024]{2,1,0:T(8,128)} %all-gather.3.cloned.1.call-done, f32[4,256,1024]{2,1,0:T(8,128)} %get-tuple-element.18), kind=kLoop, calls=%fused_computation.145 | loop fusion | flops 2097152 | bytes 16777216 | tf_op jit(solution)/shard_map/mul | solution.py:10
  274.0 6.6 %mul.371 = f32[4,256,2,512]{3,2,1,0:T(2,128)} reshape(f32[4,256,1024]{2,1,0:T(8,128)} %get-tuple-element.26) | data formatting | bytes 8388608 | tf_op jit(solution)/shard_map/mul | solution.py:10
  280.6 3.4 %reduce_sum.38 = f32[4,256,2]{2,1,0:T(8,128)S(1)} reduce(f32[4,256,2,512]{3,2,1,0:T(2,128)} %mul.371, f32[]{:T(128)} %constant.14.clone.1), dimensions={3}, to_apply=%region_3.0 | reduce | flops 1046528 | bytes 4202500 | tf_op jit(solution)/shard_map/reduce_sum | solution.py:10
  284.0 0.1 add_rsqrt_fusion
  284.1 3.0 mul.372
  287.2 6.6 %mul.373 = f32[4,256,1024]{2,1,0:T(8,128)} reshape(f32[4,256,2,512]{3,2,1,0:T(2,128)} %mul.372) | data formatting | bytes 8388608 | tf_op jit(solution)/shard_map/mul | solution.py:10
  293.8 7.0 %fusion.85 = (bf16[4,256,1024]{2,1,0:T(8,128)(2,1)S(1)}, f32[4,256,1024]{2,1,0:T(8,128)}) fusion(f32[4,256,1024]{2,1,0:T(8,128)} %get-tuple-element.27, f32[4,256,1024]{2,1,0:T(8,128)} %mul.373), kind=kLoop, calls=%fused_computation.144 | loop fusion | flops 2097152 | bytes 14680064 | tf_op jit(solution)/shard_map/convert_element_type | solution.py:122
  300.8 0.8 convolution_multiply_fusion
  301.6 0.8 convolution_multiply_fusion.1
  302.3 0.8 convolution_multiply_fusion.2
  303.1 0.8 convolution_multiply_fusion.3
  303.9 0.8 copy-done.2
  304.7 0.6 copy-done.3
  305.3 0.4 multiply_reduce_fusion
  305.7 1.7 fusion.84
  307.4 0.8 fusion.55
  308.3 0.9 fusion.54
  309.1 0.9 fusion.53
  310.0 0.9 fusion.52
  310.8 0.2 pad_maximum_fusion.2
  311.1 2.6 copy.66
  313.6 1.6 constant_dynamic-slice_fusion
  315.2 1.7 constant_dynamic-slice_fusion.1
  (8 shorter events, 0.1 us)
Async XLA Ops:
  7.2 47.0 %all-gather.5.cloned.1.call-start = ((), (), s32[]{:S(2)}) async-start(), calls=%async_computation.1 | async-start | bytes 2228224 | tf_op jit(solution)/shard_map/all_gather | solution.py:109
  7.9 97.8 %all-gather.3.cloned.1.call-start = ((), (), s32[]{:S(2)}) async-start(), calls=%async_computation | async-start | bytes 4456448 | tf_op jit(solution)/shard_map/all_gather | solution.py:108
  8.6 2.9 copy-start.4
  8.7 256.8 %all-reduce.3.cloned.1.call-start = ((), (), s32[]{:S(2)}) async-start(), calls=%async_computation.2 | async-start | bytes 12582912 | tf_op jit(solution)/shard_map/psum | solution.py:119
  55.8 52.4 %copy-start = (bf16[1024,4,256]{0,2,1:T(8,128)(2,1)S(1)}, bf16[1024,4,256]{0,2,1:T(8,128)(2,1)}, u32[]{:S(2)}) copy-start(bf16[1024,4,256]{0,2,1:T(8,128)(2,1)} %fusion.3) | copy-start | bytes 6291460
  109.0 1.6 copy-start.5
  293.8 7.0 %copy-start.1 = (bf16[1024,4,256]{0,2,1:T(8,128)(2,1)S(1)}, bf16[1024,4,256]{0,2,1:T(8,128)(2,1)}, u32[]{:S(2)}) copy-start(bf16[1024,4,256]{0,2,1:T(8,128)(2,1)} %fusion.1) | copy-start | bytes 6291460
  303.1 1.6 copy-start.2
  303.1 2.2 copy-start.3
Sparse Core Ops, SparseCore 0:
  10.2 43.9 all-gather.4
  56.3 49.3 all-gather.2
  128.0 137.3 all-reduce.2
where the time goes:
time: 325 us; the launch traced here: 323 us
  waiting for transfers between devices  224 us (69%)
  other arithmetic  34.1 us (10%)
  local copies, waits for them, and re-layouts  30.1 us (9%)
  matrix products  21.4 us (7%)
  between operations  14 us (4%)
    psum x1, waiting for transfers between devices, per_device(): total_in, total_out = lax.psum((inc_in, inc_out), 'tok')  132 us
    all_gather x1, waiting for transfers between devices, per_device(): lax.all_gather(fast_in, 'tok', axis=1, tiled=True)  49.9 us
    all_gather x1, waiting for transfers between devices, per_device(): lax.all_gather(fast_out, 'tok', axis=1, tiled=True)  40.2 us
    unnamed x15, local copies, waits for them, and re-layouts  10.6 us
    mul x2, local copies, waits for them, and re-layouts, rms_rows(): matrix * lax.rsqrt(jnp.mean(matrix * matrix, axis=-1, keepdims=True) + 1e...  9.67 us
    mul x1, other arithmetic, rms_rows(): matrix * matrix  8.56 us
    convert_element_type x1, other arithmetic, per_device(): whole_in.astype(jnp.bfloat16)  7.04 us
    mul x1, local copies, waits for them, and re-layouts, rms_rows(): matrix * matrix  6.61 us
  transfers between devices with their start and end apart: 3, of which 3 were waited for; matrix products, arithmetic and copies ran while one was open for 4% of the time, Pallas kernels for 0%

commit v1 on v0

--- a/solution.py
+++ b/solution.py
@@ -1,9 +1,16 @@
+import functools
 import math
 
 import jax
 import jax.numpy as jnp
 from jax import lax
+from jax.experimental import pallas as pl
+from jax.experimental.pallas import tpu as pltpu
 from jax.sharding import PartitionSpec as P
+
+BF16 = jnp.bfloat16
+F32 = jnp.float32
+VMEM_LIMIT = 48 * 1024 * 1024
 
 
 def rms_rows(matrix):
@@ -97,7 +104,7 @@
     return jnp.concatenate(pieces, axis=1).astype(jnp.bfloat16)
 
 
-def per_device(queries, keys, values, step_size, fast_in, fast_out):
+def per_device_generic(queries, keys, values, step_size, fast_in, fast_out):
     row_count = keys.shape[0]
     heads = fast_in.shape[0]
     head_size = keys.shape[1] // heads
@@ -128,6 +135,366 @@
     return (output, fast_in_next, fast_out_next)
 
 
+def swap(value, bits):
+    count = lax.axis_size("tok")
+    return lax.ppermute(value, "tok", [(place, place ^ bits) for place in range(count)])
+
+
+def compiler_params():
+    return pltpu.CompilerParams(vmem_limit_bytes=VMEM_LIMIT)
+
+
+def normalize_head(block):
+    wide = block.astype(F32)
+    return (wide * lax.rsqrt(jnp.mean(wide * wide, axis=-1, keepdims=True) + 1e-06)).astype(BF16)
+
+
+def prepare_kernel(block_root, heads, ids, k_ref, v_ref, r_ref, k_own, k_send, v_own, v_send):
+    core = ids[1]
+    half = heads // 2
+    size = k_ref.shape[1] // heads
+
+    def work(owner, k_out, v_out):
+        for local in range(half):
+            start = owner * half + local
+            columns = pl.ds(pl.multiple_of(start * size, size), size)
+            into = slice(local * size, (local + 1) * size)
+            k_out[:, into] = normalize_head(k_ref[:, columns])
+            first = r_ref[:, local : local + 1]
+            second = r_ref[:, half + local : half + local + 1]
+            rate = jnp.where(owner == 0, first, second)
+            v_out[:, into] = (rate * block_root * v_ref[:, columns].astype(F32)).astype(BF16)
+
+    work(core, k_own, v_own)
+    work(1 - core, k_send, v_send)
+
+
+def prepare(ids, keys, values, rates, block_root, heads):
+    rows, width = keys.shape
+    step = 256
+    wide = pl.BlockSpec((step, width), lambda i, ids: (i, 0))
+    narrow = pl.BlockSpec((step, width // 2), lambda i, ids: (i, 0))
+    shape = jax.ShapeDtypeStruct((rows, width // 2), BF16)
+    return pl.pallas_call(
+        functools.partial(prepare_kernel, block_root, heads),
+        grid_spec=pltpu.PrefetchScalarGridSpec(
+            num_scalar_prefetch=1,
+            grid=(rows // step,),
+            in_specs=[wide, wide, pl.BlockSpec((step, heads), lambda i, ids: (i, 0))],
+            out_specs=[narrow] * 4,
+        ),
+        out_shape=[shape] * 4,
+        compiler_params=compiler_params(),
+        cost_estimate=pl.CostEstimate(
+            flops=rows * width * 10, bytes_accessed=rows * width * 8, transcendentals=0
+        ),
+        name="prepare",
+    )(ids, keys, values, rates)
+
+
+def normalize_kernel(heads, x_ref, o_ref):
+    size = x_ref.shape[1] // heads
+    for head in range(heads):
+        columns = slice(head * size, (head + 1) * size)
+        o_ref[:, columns] = normalize_head(x_ref[:, columns])
+
+
+def normalize(tokens, heads):
+    rows, width = tokens.shape
+    step = 256
+    spec = pl.BlockSpec((step, width), lambda i: (i, 0))
+    return pl.pallas_call(
+        functools.partial(normalize_kernel, heads),
+        grid=(rows // step,),
+        in_specs=[spec],
+        out_specs=spec,
+        out_shape=jax.ShapeDtypeStruct((rows, width), BF16),
+        compiler_params=compiler_params(),
+        cost_estimate=pl.CostEstimate(
+            flops=rows * width * 5, bytes_accessed=rows * width * 4, transcendentals=0
+        ),
+        name="normalize",
+    )(tokens)
+
+
+def places(chip, core):
+    for side in range(2):
+        for slot in range(4):
+            other = jnp.bitwise_xor(chip, 2 * slot + side)
+            for source in range(2):
+                yield side, slot, source, 2 * other + jnp.bitwise_xor(core, source)
+
+
+def assemble(chip, core, sides, w_in, w_out):
+    size = w_out.shape[1]
+    blocks = w_in.shape[1] // size
+    rows_in = w_in.shape[0] // 16
+    rows_out = w_out.shape[0] // 16
+    for side, slot, source, place in places(chip, core):
+        ref = sides[side]
+        into = pl.ds(pl.multiple_of(place * rows_in, rows_in), rows_in)
+        for block in range(blocks):
+            w_in[into, block * size : (block + 1) * size] = ref[
+                slot, source, block * rows_in : (block + 1) * rows_in, :
+            ]
+        into = pl.ds(pl.multiple_of(place * rows_out, rows_out), rows_out)
+        w_out[into, :] = ref[slot, source, blocks * rows_in :, :]
+
+
+def update_kernel(
+    local, ids, near, far, k_own, v_own, k_got, v_got, keep, send, w_in, w_out, acc_in, acc_out, turned
+):
+    step = pl.program_id(0)
+    steps = pl.num_programs(0)
+    chip, core = ids[0], ids[1]
+    size = w_out.shape[1]
+    fast = w_out.shape[0]
+    in_root = 1.0 / math.sqrt(size)
+    out_root = 1.0 / math.sqrt(fast)
+
+    @pl.when(step == 0)
+    def _():
+        assemble(chip, core, (near, far), w_in, w_out)
+        acc_in[...] = jnp.zeros_like(acc_in)
+        acc_out[...] = jnp.zeros_like(acc_out)
+
+    def work(k_ref, v_ref):
+        keyn = k_ref[...]
+        scaled = v_ref[...]
+        chunk = 256
+        for start in range(0, fast, chunk):
+            gates = slice(start, start + chunk)
+            ups = slice(fast + start, fast + start + chunk)
+            gate = jnp.dot(keyn, w_in[:, gates], preferred_element_type=F32) * in_root
+            upper = jnp.dot(keyn, w_in[:, ups], preferred_element_type=F32) * in_root
+            back = (
+                lax.dot_general(
+                    scaled, w_out[gates, :], (((1,), (1,)), ((), ())), preferred_element_type=F32
+                )
+                * out_root
+            )
+            sigma = jax.nn.sigmoid(gate)
+            active = gate * sigma
+            hidden = (active * upper).astype(BF16)
+            d_gate = (back * upper * sigma * (1.0 + gate * (1.0 - sigma))).astype(BF16)
+            d_up = (back * active).astype(BF16)
+            over = (((0,), (0,)), ((), ()))
+            acc_in[:, gates] += lax.dot_general(keyn, d_gate, over, preferred_element_type=F32)
+            acc_in[:, ups] += lax.dot_general(keyn, d_up, over, preferred_element_type=F32)
+            acc_out[:, gates] += lax.dot_general(scaled, hidden, over, preferred_element_type=F32)
+
+    @pl.when(step < steps // 2)
+    def _():
+        work(k_own, v_own)
+
+    @pl.when(step >= steps // 2)
+    def _():
+        work(k_got, v_got)
+
+    @pl.when(step == steps - 1)
+    def _():
+        turned[...] = acc_out[...].T
+        blocks = acc_in.shape[1] // size
+        rows_in = acc_in.shape[0] // 16
+        rows_out = turned.shape[0] // 16
+        for side, slot, source, place in places(chip, core):
+            ref = (keep, send)[side]
+            rows = pl.ds(pl.multiple_of(place * rows_in, rows_in), rows_in)
+            for block in range(blocks):
+                ref[slot, source, block * rows_in : (block + 1) * rows_in, :] = (
+                    acc_in[rows, block * size : (block + 1) * size] * in_root
+                ).astype(ref.dtype)
+            rows = pl.ds(pl.multiple_of(place * rows_out, rows_out), rows_out)
+            ref[slot, source, blocks * rows_in :, :] = (turned[rows, :] * out_root).astype(ref.dtype)
+
+
+def increments(ids, local, near, far, k_own, v_own, k_got, v_got, fast):
+    rows = k_own.shape[0]
+    size = near.shape[-1]
+    step = 512
+    half = rows // step
+    whole = pl.BlockSpec(near.shape, lambda i, ids: (0, 0, 0, 0))
+    own = pl.BlockSpec((step, size), lambda i, ids: (jnp.minimum(i, half - 1), local))
+    got = pl.BlockSpec((step, size), lambda i, ids: (jnp.maximum(i - half, 0), local))
+    return pl.pallas_call(
+        functools.partial(update_kernel, local),
+        grid_spec=pltpu.PrefetchScalarGridSpec(
+            num_scalar_prefetch=1,
+            grid=(2 * half,),
+            in_specs=[whole, whole, own, own, got, got],
+            out_specs=[whole, whole],
+            scratch_shapes=[
+                pltpu.VMEM((size, 2 * fast), BF16),
+                pltpu.VMEM((fast, size), BF16),
+                pltpu.VMEM((size, 2 * fast), F32),
+                pltpu.VMEM((size, fast), F32),
+                pltpu.VMEM((fast, size), F32),
+            ],
+        ),
+        out_shape=[jax.ShapeDtypeStruct(near.shape, F32), jax.ShapeDtypeStruct(near.shape, BF16)],
+        compiler_params=compiler_params(),
+        cost_estimate=pl.CostEstimate(
+            flops=2 * rows * size * fast * 12, bytes_accessed=rows * size * 8, transcendentals=0
+        ),
+        name="increments",
+    )(ids, near, far, k_own, v_own, k_got, v_got)
+
+
+def renorm_kernel(size_in, master, kept, one, two, three, wide, short):
+    fresh = (
+        master[...]
+        + kept[...]
+        + one[...].astype(F32)
+        + two[...].astype(F32)
+        + three[...].astype(F32)
+    )
+    size = fresh.shape[-1]
+    blocks = 4
+    rows_in = size_in
+    for source in range(2):
+        for part in range(2):
+            first = 2 * part * rows_in
+            left = fresh[source, first : first + rows_in, :]
+            right = fresh[source, first + rows_in : first + 2 * rows_in, :]
+            total = jnp.sum(left * left + right * right, axis=-1, keepdims=True)
+            factor = lax.rsqrt(total * (1.0 / (2 * size)) + 1e-06)
+            for at, value in ((first, left), (first + rows_in, right)):
+                done = value * factor
+                wide[source, at : at + rows_in, :] = done
+                short[source, at : at + rows_in, :] = done.astype(BF16)
+        tail = fresh[source, blocks * rows_in :, :]
+        done = tail * lax.rsqrt(jnp.mean(tail * tail, axis=-1, keepdims=True) + 1e-06)
+        wide[source, blocks * rows_in :, :] = done
+        short[source, blocks * rows_in :, :] = done.astype(BF16)
+
+
+def renorm(master, kept, one, two, three, rows_in):
+    shape = master.shape
+    return pl.pallas_call(
+        functools.partial(renorm_kernel, rows_in),
+        out_shape=[jax.ShapeDtypeStruct(shape, F32), jax.ShapeDtypeStruct(shape, BF16)],
+        compiler_params=compiler_params(),
+        name="renorm",
+    )(master, kept, one, two, three)
+
+
+def apply_kernel(other, ids, near, far, q_ref, *rest):
+    o_ref, w_in, w_out = rest[-3:]
+    chip, core = ids[0], ids[1]
+    fast = w_out.shape[0]
+
+    @pl.when(pl.program_id(0) == 0)
+    def _():
+        assemble(chip, core ^ other, (near, far), w_in, w_out)
+
+    query = q_ref[...]
+    in_root = 1.0 / math.sqrt(w_out.shape[1])
+    gate = jnp.dot(query, w_in[:, :fast], preferred_element_type=F32) * in_root
+    upper = jnp.dot(query, w_in[:, fast:], preferred_element_type=F32) * in_root
+    hidden = (gate * jax.nn.sigmoid(gate) * upper).astype(BF16)
+    result = jnp.dot(hidden, w_out[...], preferred_element_type=F32) * (1.0 / math.sqrt(fast))
+    o_ref[...] = result.astype(BF16)
+
+
+def apply_fast(ids, local, other, near, far, queryn, output, fast, heads):
+    rows, width = queryn.shape
+    size = near.shape[-1]
+    step = 512
+    half = heads // 2
+    whole = pl.BlockSpec(near.shape, lambda i, ids: (0, 0, 0, 0))
+    column = pl.BlockSpec((step, size), lambda i, ids: (i, half * (ids[1] ^ other) + local))
+    operands = [ids, near, far, queryn]
+    specs = [whole, whole, column]
+    aliases = {}
+    if output is not None:
+        operands.append(output)
+        specs.append(pl.BlockSpec(memory_space=pl.ANY))
+        aliases = {4: 0}
+    return pl.pallas_call(
+        functools.partial(apply_kernel, other),
+        grid_spec=pltpu.PrefetchScalarGridSpec(
+            num_scalar_prefetch=1,
+            grid=(rows // step,),
+            in_specs=specs,
+            out_specs=column,
+            scratch_shapes=[pltpu.VMEM((size, 2 * fast), BF16), pltpu.VMEM((fast, size), BF16)],
+        ),
+        out_shape=jax.ShapeDtypeStruct((rows, width), BF16),
+        input_output_aliases=aliases,
+        compiler_params=compiler_params(),
+        cost_estimate=pl.CostEstimate(
+            flops=2 * rows * size * fast * 3, bytes_accessed=rows * size * 4, transcendentals=0
+        ),
+        name="apply",
+    )(*operands)
+
+
+def pack(fast_in, fast_out):
+    heads, rows, double = fast_in.shape
+    size = fast_out.shape[-1]
+    blocks = fast_in.reshape(heads, rows, double // size, size).transpose(0, 2, 1, 3)
+    return jnp.concatenate([blocks.reshape(heads, -1, size), fast_out], axis=1)
+
+
+def unpack(packed, rows):
+    heads, _, size = packed.shape
+    blocks = packed[:, : 4 * rows].reshape(heads, 4, rows, size).transpose(0, 2, 1, 3)
+    return blocks.reshape(heads, rows, 4 * size), packed[:, 4 * rows :]
+
+
+def gather_chips(shard):
+    line = jnp.stack([shard, swap(shard, 4), swap(shard, 8), swap(shard, 12)])
+    return line, swap(line, 2)
+
+
+def per_device_cube(queries, keys, values, step_size, fast_in, fast_out):
+    rows = keys.shape[0]
+    heads = fast_in.shape[0]
+    half = heads // 2
+    fast = fast_in.shape[2] // 2
+    rows_in = fast_in.shape[1]
+    place = lax.axis_index("tok")
+    core = place % 2
+    ids = jnp.stack([place // 2, core]).astype(jnp.int32)
+    block_root = 1.0 / math.sqrt(rows * lax.axis_size("tok"))
+
+    packed = pack(fast_in, fast_out)
+    own = lax.dynamic_slice_in_dim(packed, core * half, half, 0)
+    theirs = lax.dynamic_slice_in_dim(packed, (1 - core) * half, half, 0)
+    got = swap(theirs, 1)
+    masters = [jnp.stack([own[local], got[local]]) for local in range(half)]
+    lines = [gather_chips(master.astype(BF16)) for master in masters]
+
+    k_own, k_send, v_own, v_send = prepare(ids, keys, values, step_size.T, block_root, heads)
+    k_got, v_got = swap(k_send, 1), swap(v_send, 1)
+    queryn = normalize(queries, heads)
+
+    fresh = []
+    for local in range(half):
+        keep, send = increments(ids, local, *lines[local], k_own, v_own, k_got, v_got, fast)
+        total = keep + swap(send, 2).astype(F32)
+        arrived = [swap(total[slot].astype(BF16), 4 * slot) for slot in (1, 2, 3)]
+        fresh.append(renorm(masters[local], total[0], *arrived, rows_in))
+
+    output = None
+    for local in range(half):
+        near, far = gather_chips(fresh[local][1])
+        near_other, far_other = swap(near, 1), swap(far, 1)
+        output = apply_fast(ids, local, 0, near, far, queryn, output, fast, heads)
+        output = apply_fast(ids, local, 1, near_other, far_other, queryn, output, fast, heads)
+
+    mine = jnp.stack([wide[0] for wide, _ in fresh])
+    back = swap(jnp.stack([wide[1] for wide, _ in fresh]), 1)
+    both = jnp.where(core == 0, jnp.concatenate([mine, back]), jnp.concatenate([back, mine]))
+    return (output, *unpack(both, rows_in))
+
+
+def per_device(queries, keys, values, step_size, fast_in, fast_out):
+    fits = lax.axis_size("tok") == 16 and fast_in.shape[1] % 16 == 0 and fast_in.shape[0] % 2 == 0
+    chosen = per_device_cube if fits else per_device_generic
+    return chosen(queries, keys, values, step_size, fast_in, fast_out)
+
+
 def solution(mesh):
     placed = (
         P(("parts", "tok"), None),

time: 325 us -> 122 us (0.38)
  waiting for transfers between devices: 224 us -> 22.4 us
  starting transfers between devices: 0.11 us -> 54.6 us
  Pallas kernels: 0 us -> 35.3 us
  other arithmetic: 34.1 us -> 3.25 us
  local copies, waits for them, and re-layouts: 30.1 us -> 3.47 us
  matrix products: 21.4 us -> 0 us
  between operations: 14 us -> 0.95 us
    psum x1 -> x0, waiting for transfers between devices: 132 us -> none  [per_device(): total_in, total_out = lax.psum((inc_in, inc_out), 'tok')]
    all_gather x2 -> x0, waiting for transfers between devices: 90 us -> none  [the longest x1 49.9 us: per_device(): lax.all_gather(fast_in, 'tok', axis=1, tiled=True)]
    ppermute x0 -> x32, starting transfers between devices: none -> 54.6 us  [swap(): lax.ppermute(value, 'tok', [(place, place ^ bits) for place in range(coun...]
    pallas_call x0 -> x10, Pallas kernels: none -> 35.3 us  [the longest x2 14.6 us: increments(): pl.pallas_call(functools.partial(update_kernel, local), grid_spec=pltpu.P...]
    ppermute x0 -> x32, waiting for transfers between devices: none -> 22.4 us  [swap(): lax.ppermute(value, 'tok', [(place, place ^ bits) for place in range(coun...]
    dot_general x24 -> x0, matrix products: 21.4 us -> none  [the longest x4 5.62 us: head_increments(): lax.dot_general(scaled, weight_out, (((1,), (1,)), ((), ())), preferred_e...]
    convert_element_type x6 -> x2, other arithmetic: 16.7 us -> 0.03 us  [per_device_cube(): lines = [gather_chips(master.astype(BF16)) for master in masters]]
    mul x3 -> x0, local copies, waits for them, and re-layouts: 16.3 us -> none  [the longest x2 9.67 us: rms_rows(): matrix * lax.rsqrt(jnp.mean(matrix * matrix, axis=-1, keepdims=True) + 1e...]
  transfers between devices with their start and end apart: 3 -> 32, of which waited for: 3 -> 11; matrix products, arithmetic and copies ran while one was open for 4% -> 4% of each run, Pallas kernels for 0% -> 26%
where the time goes in v1:
time: 122 us; the launch traced here: 120 us
  starting transfers between devices  54.6 us (45%)
  Pallas kernels  35.3 us (29%)
  waiting for transfers between devices  22.4 us (18%)
  local copies, waits for them, and re-layouts  3.47 us (3%)
  other arithmetic  3.25 us (3%)
    ppermute x32, starting transfers between devices, swap(): lax.ppermute(value, 'tok', [(place, place ^ bits) for place in range(coun...  54.6 us
    ppermute x32, waiting for transfers between devices, swap(): lax.ppermute(value, 'tok', [(place, place ^ bits) for place in range(coun...  22.4 us
    pallas_call x2, Pallas kernels, increments(): pl.pallas_call(functools.partial(update_kernel, local), grid_spec=pltpu.P...  14.6 us
    pallas_call x4, Pallas kernels, apply_fast(): pl.pallas_call(functools.partial(apply_kernel, other), grid_spec=pltpu.Pr...  14.5 us
    pallas_call x1, Pallas kernels, prepare(): pl.pallas_call(functools.partial(prepare_kernel, block_root, heads), grid...  4.97 us
  transfers between devices with their start and end apart: 32, of which 11 were waited for; matrix products, arithmetic and copies ran while one was open for 4% of the time, Pallas kernels for 26%

profile of v1, /device:TPU:1, one launch (start us, length us, event | category | flops | bytes accessed | tf_op | source)
XLA Modules:
  0.0 120.0 jit_solution(16716100281890048185)
XLA Ops:
  0.7 1.0 copy.18
  1.6 0.9 fusion.1
  2.6 0.1 collective-permute-start
  2.7 0.9 copy.13
  3.6 0.1 pad_add_fusion.ids
  3.7 5.0 %prepare.1 = (bf16[1024,512]{1,0:T(8,128)(2,1)S(1)}, bf16[1024,512]{1,0:T(8,128)(2,1)S(1)}, bf16[1024,512]{1,0:T(8,128)(2,1)S(1)}, bf16[1024,512]{1,0:T(8,128)(2,1)S(1)}) custom-call(s32[2]{0:T(128)S(1)} %pad_add_fusion.ids, bf16[1024,1024]{1,0:T(8,128)(2,1)} %k_ref.1, bf16[1024,1024]{1,0:T(8,128)(2,1)} %v_ref.1, f32[1024,4]{1,0:T(8,128)S(1)} %bitcast.53), custom_call_target="tpu_custom_call" | custom-call | flops 10485760 | bytes 8388608 | tf_op jit(solution)/shard_map/prepare/pallas_call | solution.py:178
  8.7 0.5 collective-permute-start.5
  9.2 0.1 collective-permute-start.6
  9.4 2.8 %collective-permute-start.17 = (bf16[2,96,256]{2,1,0:T(8,128)(2,1)S(1)}, bf16[2,96,256]{2,1,0:T(8,128)(2,1)S(1)}, u32[]{:S(2)}, u32[]{:S(2)}) collective-permute-start(bf16[2,96,256]{2,1,0:T(8,128)(2,1)S(1)} %fusion.2), channel_id=1, source_target_pairs={{0,4},{1,5},{2,6},{3,7},{4,0},{5,1},{6,2},{7,3},{8,12},{9,13},{10,... | collective-permute-start | bytes 294920 | tf_op jit(solution)/shard_map/ppermute | solution.py:140
  12.2 2.3 %collective-permute-start.18 = (bf16[2,96,256]{2,1,0:T(8,128)(2,1)S(1)}, bf16[2,96,256]{2,1,0:T(8,128)(2,1)S(1)}, u32[]{:S(2)}, u32[]{:S(2)}) collective-permute-start(bf16[2,96,256]{2,1,0:T(8,128)(2,1)S(1)} %fusion.2), channel_id=1, source_target_pairs={{0,8},{1,9},{2,10},{3,11},{4,12},{5,13},{6,14},{7,15},{8,0},{9,1},... | collective-permute-start | bytes 294920 | tf_op jit(solution)/shard_map/ppermute | solution.py:140
  14.5 0.7 collective-permute-done.17
  15.3 1.9 %collective-permute-done.18 = bf16[2,96,256]{2,1,0:T(8,128)(2,1)S(1)} collective-permute-done((bf16[2,96,256]{2,1,0:T(8,128)(2,1)S(1)}, bf16[2,96,256]{2,1,0:T(8,128)(2,1)S(1)}, u32[]{:S(2)}, u32[]{:S(2)}) %collective-permute-start.18) | collective-permute-done | bytes 98336 | tf_op jit(solution)/shard_map/ppermute | solution.py:140
  17.1 4.4 %collective-permute-done.19 = bf16[2,96,256]{2,1,0:T(8,128)(2,1)S(1)} collective-permute-done((bf16[2,96,256]{2,1,0:T(8,128)(2,1)S(1)}, bf16[2,96,256]{2,1,0:T(8,128)(2,1)S(1)}, u32[]{:S(2)}, u32[]{:S(2)}) %collective-permute-start.19) | collective-permute-done | bytes 98336 | tf_op jit(solution)/shard_map/ppermute | solution.py:140
  21.5 0.1 pad_maximum_fusion.2.near
  21.6 1.3 %collective-permute-start.20 = (bf16[4,2,96,256]{3,2,1,0:T(8,128)(2,1)S(1)}, bf16[4,2,96,256]{3,2,1,0:T(8,128)(2,1)S(1)}, u32[]{:S(2)}, u32[]{:S(2)}) collective-permute-start(bf16[4,2,96,256]{3,2,1,0:T(8,128)(2,1)S(1)} %pad_maximum_fusion.2.near), channel_id=1, source_target_pairs={{0,2},{1,3},{2,0},{3,1},{4,6},{5,7},{6,4},{7,5},{8,10},{9,11},{10,... | collective-permute-start | bytes 1179656 | tf_op jit(solution)/shard_map/ppermute | solution.py:140
  22.9 2.3 %collective-permute-start.1 = (bf16[2,96,256]{2,1,0:T(8,128)(2,1)S(1)}, bf16[2,96,256]{2,1,0:T(8,128)(2,1)S(1)}, u32[]{:S(2)}, u32[]{:S(2)}) collective-permute-start(bf16[2,96,256]{2,1,0:T(8,128)(2,1)S(1)} %fusion.3), channel_id=1, source_target_pairs={{0,4},{1,5},{2,6},{3,7},{4,0},{5,1},{6,2},{7,3},{8,12},{9,13},{10,... | collective-permute-start | bytes 294920 | tf_op jit(solution)/shard_map/ppermute | solution.py:140
  25.2 1.1 collective-permute-start.2
  26.3 1.2 collective-permute-done.1
  27.5 2.2 %collective-permute-start.3 = (bf16[2,96,256]{2,1,0:T(8,128)(2,1)S(1)}, bf16[2,96,256]{2,1,0:T(8,128)(2,1)S(1)}, u32[]{:S(2)}, u32[]{:S(2)}) collective-permute-start(bf16[2,96,256]{2,1,0:T(8,128)(2,1)S(1)} %fusion.3), channel_id=1, source_target_pairs={{0,12},{1,13},{2,14},{3,15},{4,8},{5,9},{6,10},{7,11},{8,4},{9,5},... | collective-permute-start | bytes 294920 | tf_op jit(solution)/shard_map/ppermute | solution.py:140
  29.7 0.9 collective-permute-done.2
  30.6 3.1 %collective-permute-done.3 = bf16[2,96,256]{2,1,0:T(8,128)(2,1)S(1)} collective-permute-done((bf16[2,96,256]{2,1,0:T(8,128)(2,1)S(1)}, bf16[2,96,256]{2,1,0:T(8,128)(2,1)S(1)}, u32[]{:S(2)}, u32[]{:S(2)}) %collective-permute-start.3) | collective-permute-done | bytes 98336 | tf_op jit(solution)/shard_map/ppermute | solution.py:140
  33.7 0.1 pad_maximum_fusion.near
  33.8 0.2 collective-permute-start.4
  34.0 7.3 %increments.3 = (f32[4,2,96,256]{3,2,1,0:T(8,128)S(1)}, bf16[4,2,96,256]{3,2,1,0:T(8,128)(2,1)S(1)}) custom-call(s32[2]{0:T(128)S(1)} %pad_add_fusion.ids, bf16[4,2,96,256]{3,2,1,0:T(8,128)(2,1)S(1)} %pad_maximum_fusion.2.near, bf16[4,2,96,256]{3,2,1,0:T(8,128)(2,1)S(1)} %collective-permute-done.20.far, bf16[1024,512]{1,0:T(8,128)(2,1)S(1)} %get-tuple-element.15.k_own, ...), custom_call_target="tpu_custom_call" | custom-call | flops 3221225472 | bytes 2097152 | tf_op jit(solution)/shard_map/increments/pallas_call | solution.py:319
  41.3 1.4 %collective-permute-start.21 = (bf16[4,2,96,256]{3,2,1,0:T(8,128)(2,1)S(1)}, bf16[4,2,96,256]{3,2,1,0:T(8,128)(2,1)S(1)}, u32[]{:S(2)}, u32[]{:S(2)}) collective-permute-start(bf16[4,2,96,256]{3,2,1,0:T(8,128)(2,1)S(1)} %get-tuple-element.23), channel_id=1, source_target_pairs={{0,2},{1,3},{2,0},{3,1},{4,6},{5,7},{6,4},{7,5},{8,10},{9,11},{10,... | collective-permute-start | bytes 1179656 | tf_op jit(solution)/shard_map/ppermute | solution.py:140
  42.7 7.3 %increments.2 = (f32[4,2,96,256]{3,2,1,0:T(8,128)S(1)}, bf16[4,2,96,256]{3,2,1,0:T(8,128)(2,1)S(1)}) custom-call(s32[2]{0:T(128)S(1)} %pad_add_fusion.ids, bf16[4,2,96,256]{3,2,1,0:T(8,128)(2,1)S(1)} %pad_maximum_fusion.near, bf16[4,2,96,256]{3,2,1,0:T(8,128)(2,1)S(1)} %collective-permute-done.4.far, bf16[1024,512]{1,0:T(8,128)(2,1)S(1)} %get-tuple-element.15.k_own, ...), custom_call_target="tpu_custom_call" | custom-call | flops 3221225472 | bytes 2097152 | tf_op jit(solution)/shard_map/increments/pallas_call | solution.py:319
  50.0 0.2 collective-permute-start.7
  50.2 0.1 fusion.4
  50.3 3.1 %collective-permute-start.22 = (bf16[2,96,256]{2,1,0:T(8,128)(2,1)S(1)}, bf16[2,96,256]{2,1,0:T(8,128)(2,1)S(1)}, u32[]{:S(2)}, u32[]{:S(2)}) collective-permute-start(bf16[2,96,256]{2,1,0:T(8,128)(2,1)S(1)} %get-tuple-element.33), channel_id=1, source_target_pairs={{0,4},{1,5},{2,6},{3,7},{4,0},{5,1},{6,2},{7,3},{8,12},{9,13},{10,... | collective-permute-start | bytes 294920 | tf_op jit(solution)/shard_map/ppermute | solution.py:140
  53.5 2.4 %collective-permute-start.23 = (bf16[2,96,256]{2,1,0:T(8,128)(2,1)S(1)}, bf16[2,96,256]{2,1,0:T(8,128)(2,1)S(1)}, u32[]{:S(2)}, u32[]{:S(2)}) collective-permute-start(bf16[2,96,256]{2,1,0:T(8,128)(2,1)S(1)} %get-tuple-element.32), channel_id=1, source_target_pairs={{0,8},{1,9},{2,10},{3,11},{4,12},{5,13},{6,14},{7,15},{8,0},{9,1},... | collective-permute-start | bytes 294920 | tf_op jit(solution)/shard_map/ppermute | solution.py:140
  55.9 1.1 collective-permute-start.24
  57.0 0.9 collective-permute-done.7
  57.9 0.1 fusion.5
  58.0 1.3 %collective-permute-start.10 = (bf16[2,96,256]{2,1,0:T(8,128)(2,1)S(1)}, bf16[2,96,256]{2,1,0:T(8,128)(2,1)S(1)}, u32[]{:S(2)}, u32[]{:S(2)}) collective-permute-start(bf16[2,96,256]{2,1,0:T(8,128)(2,1)S(1)} %get-tuple-element.34), channel_id=1, source_target_pairs={{0,12},{1,13},{2,14},{3,15},{4,8},{5,9},{6,10},{7,11},{8,4},{9,5},... | collective-permute-start | bytes 294920 | tf_op jit(solution)/shard_map/ppermute | solution.py:140
  59.4 3.0 %collective-permute-start.8 = (bf16[2,96,256]{2,1,0:T(8,128)(2,1)S(1)}, bf16[2,96,256]{2,1,0:T(8,128)(2,1)S(1)}, u32[]{:S(2)}, u32[]{:S(2)}) collective-permute-start(bf16[2,96,256]{2,1,0:T(8,128)(2,1)S(1)} %get-tuple-element.36), channel_id=1, source_target_pairs={{0,4},{1,5},{2,6},{3,7},{4,0},{5,1},{6,2},{7,3},{8,12},{9,13},{10,... | collective-permute-start | bytes 294920 | tf_op jit(solution)/shard_map/ppermute | solution.py:140
  62.4 0.0 copy-start
  62.5 0.2 renorm.3
  62.6 5.6 %collective-permute-start.25 = (bf16[2,96,256]{2,1,0:T(8,128)(2,1)S(1)}, bf16[2,96,256]{2,1,0:T(8,128)(2,1)S(1)}, u32[]{:S(2)}, u32[]{:S(2)}) collective-permute-start(bf16[2,96,256]{2,1,0:T(8,128)(2,1)S(1)} %get-tuple-element.24), channel_id=1, source_target_pairs={{0,4},{1,5},{2,6},{3,7},{4,0},{5,1},{6,2},{7,3},{8,12},{9,13},{10,... | collective-permute-start | bytes 294920 | tf_op jit(solution)/shard_map/ppermute | solution.py:140
  68.2 2.1 %collective-permute-start.26 = (bf16[2,96,256]{2,1,0:T(8,128)(2,1)S(1)}, bf16[2,96,256]{2,1,0:T(8,128)(2,1)S(1)}, u32[]{:S(2)}, u32[]{:S(2)}) collective-permute-start(bf16[2,96,256]{2,1,0:T(8,128)(2,1)S(1)} %get-tuple-element.24), channel_id=1, source_target_pairs={{0,8},{1,9},{2,10},{3,11},{4,12},{5,13},{6,14},{7,15},{8,0},{9,1},... | collective-permute-start | bytes 294920 | tf_op jit(solution)/shard_map/ppermute | solution.py:140
  70.4 1.1 collective-permute-start.27
  71.5 2.1 %collective-permute-done.9.two = bf16[2,96,256]{2,1,0:T(8,128)(2,1)S(1)} collective-permute-done((bf16[2,96,256]{2,1,0:T(8,128)(2,1)S(1)}, bf16[2,96,256]{2,1,0:T(8,128)(2,1)S(1)}, u32[]{:S(2)}, u32[]{:S(2)}) %collective-permute-start.9) | collective-permute-done | bytes 98336 | tf_op jit(solution)/shard_map/ppermute | solution.py:140
  73.6 0.1 renorm.2
  73.7 2.0 %collective-permute-start.11 = (bf16[2,96,256]{2,1,0:T(8,128)(2,1)S(1)}, bf16[2,96,256]{2,1,0:T(8,128)(2,1)S(1)}, u32[]{:S(2)}, u32[]{:S(2)}) collective-permute-start(bf16[2,96,256]{2,1,0:T(8,128)(2,1)S(1)} %get-tuple-element.21), channel_id=1, source_target_pairs={{0,4},{1,5},{2,6},{3,7},{4,0},{5,1},{6,2},{7,3},{8,12},{9,13},{10,... | collective-permute-start | bytes 294920 | tf_op jit(solution)/shard_map/ppermute | solution.py:140
  75.8 3.1 %collective-permute-start.12 = (bf16[2,96,256]{2,1,0:T(8,128)(2,1)S(1)}, bf16[2,96,256]{2,1,0:T(8,128)(2,1)S(1)}, u32[]{:S(2)}, u32[]{:S(2)}) collective-permute-start(bf16[2,96,256]{2,1,0:T(8,128)(2,1)S(1)} %get-tuple-element.21), channel_id=1, source_target_pairs={{0,8},{1,9},{2,10},{3,11},{4,12},{5,13},{6,14},{7,15},{8,0},{9,1},... | collective-permute-start | bytes 294920 | tf_op jit(solution)/shard_map/ppermute | solution.py:140
  78.9 0.1 collective-permute-start.13
  79.0 1.3 %collective-permute-done.26 = bf16[2,96,256]{2,1,0:T(8,128)(2,1)S(1)} collective-permute-done((bf16[2,96,256]{2,1,0:T(8,128)(2,1)S(1)}, bf16[2,96,256]{2,1,0:T(8,128)(2,1)S(1)}, u32[]{:S(2)}, u32[]{:S(2)}) %collective-permute-start.26) | collective-permute-done | bytes 98336 | tf_op jit(solution)/shard_map/ppermute | solution.py:140
  80.3 0.1 pad_maximum_fusion.3.near
  80.3 0.1 collective-permute-start.29
  80.4 0.4 collective-permute-done.11
  80.8 5.4 %collective-permute-done.12 = bf16[2,96,256]{2,1,0:T(8,128)(2,1)S(1)} collective-permute-done((bf16[2,96,256]{2,1,0:T(8,128)(2,1)S(1)}, bf16[2,96,256]{2,1,0:T(8,128)(2,1)S(1)}, u32[]{:S(2)}, u32[]{:S(2)}) %collective-permute-start.12) | collective-permute-done | bytes 98336 | tf_op jit(solution)/shard_map/ppermute | solution.py:140
  86.3 0.1 pad_maximum_fusion.1.near
  86.3 0.1 collective-permute-start.15
  86.5 0.7 pad_maximum_fusion.6
  87.1 5.2 %collective-permute-start.31 = (f32[2,96,256]{2,1,0:T(8,128)}, f32[2,96,256]{2,1,0:T(8,128)}, u32[]{:S(2)}, u32[]{:S(2)}) collective-permute-start(f32[2,96,256]{2,1,0:T(8,128)} %pad_maximum_fusion.6), channel_id=1, source_target_pairs={{0,1},{1,0},{2,3},{3,2},{4,5},{5,4},{6,7},{7,6},{8,9},{9,8},{10,11... | collective-permute-start | bytes 589832 | tf_op jit(solution)/shard_map/ppermute | solution.py:140
  92.4 5.4 %collective-permute-start.30 = (bf16[4,2,96,256]{3,2,1,0:T(8,128)(2,1)}, bf16[4,2,96,256]{3,2,1,0:T(8,128)(2,1)}, u32[]{:S(2)}, u32[]{:S(2)}) collective-permute-start(bf16[4,2,96,256]{3,2,1,0:T(8,128)(2,1)} %collective-permute-done.29.far), channel_id=1, source_target_pairs={{0,1},{1,0},{2,3},{3,2},{4,5},{5,4},{6,7},{7,6},{8,9},{9,8},{10,11... | collective-permute-start | bytes 1179656 | tf_op jit(solution)/shard_map/ppermute | solution.py:140
  97.8 4.2 %collective-permute-start.16 = (bf16[4,2,96,256]{3,2,1,0:T(8,128)(2,1)S(1)}, bf16[4,2,96,256]{3,2,1,0:T(8,128)(2,1)}, u32[]{:S(2)}, u32[]{:S(2)}) collective-permute-start(bf16[4,2,96,256]{3,2,1,0:T(8,128)(2,1)S(1)} %collective-permute-done.15.far), channel_id=1, source_target_pairs={{0,1},{1,0},{2,3},{3,2},{4,5},{5,4},{6,7},{7,6},{8,9},{9,8},{10,11... | collective-permute-start | bytes 1179656 | tf_op jit(solution)/shard_map/ppermute | solution.py:140
  102.0 0.9 normalize.1.q_ref
  103.0 1.1 maximum_select_fusion
  104.1 0.7 slice.91
  104.7 0.7 copy.16
  105.5 3.8 %apply.4.rest_0_ = bf16[1024,1024]{1,0:T(8,128)(2,1)} custom-call(s32[2]{0:T(128)S(1)} %pad_add_fusion.ids, bf16[4,2,96,256]{3,2,1,0:T(8,128)(2,1)S(1)} %pad_maximum_fusion.3.near, bf16[4,2,96,256]{3,2,1,0:T(8,128)(2,1)} %collective-permute-done.29.far, bf16[1024,1024]{1,0:T(8,128)(2,1)S(1)} %normalize.1.q_ref), custom_call_target="tpu_custom_call" | custom-call | flops 805306368 | bytes 1048576 | tf_op jit(solution)/shard_map/apply/pallas_call | solution.py:413
  109.3 3.9 %apply.5.rest_0_ = bf16[1024,1024]{1,0:T(8,128)(2,1)} custom-call(s32[2]{0:T(128)S(1)} %pad_add_fusion.ids, bf16[4,2,96,256]{3,2,1,0:T(8,128)(2,1)} %collective-permute-done.28.near, bf16[4,2,96,256]{3,2,1,0:T(8,128)(2,1)} %collective-permute-done.30.far, bf16[1024,1024]{1,0:T(8,128)(2,1)S(1)} %normalize.1.q_ref, ...), custom_call_target="tpu_custom_call", output_to_operand_aliasing={{}: (4, {})} | custom-call | flops 805306368 | bytes 1048576 | tf_op jit(solution)/shard_map/apply/pallas_call | solution.py:413
  113.2 2.8 %apply.6.rest_0_ = bf16[1024,1024]{1,0:T(8,128)(2,1)} custom-call(s32[2]{0:T(128)S(1)} %pad_add_fusion.ids, bf16[4,2,96,256]{3,2,1,0:T(8,128)(2,1)S(1)} %pad_maximum_fusion.1.near, bf16[4,2,96,256]{3,2,1,0:T(8,128)(2,1)S(1)} %collective-permute-done.15.far, bf16[1024,1024]{1,0:T(8,128)(2,1)S(1)} %normalize.1.q_ref, ...), custom_call_target="tpu_custom_call", output_to_operand_aliasing={{}: (4, {})} | custom-call | flops 805306368 | bytes 1048576 | tf_op jit(solution)/shard_map/apply/pallas_call | solution.py:413
  116.0 3.9 %apply.7 = bf16[1024,1024]{1,0:T(8,128)(2,1)} custom-call(s32[2]{0:T(128)S(1)} %pad_add_fusion.ids, bf16[4,2,96,256]{3,2,1,0:T(8,128)(2,1)} %collective-permute-done.14.near, bf16[4,2,96,256]{3,2,1,0:T(8,128)(2,1)} %collective-permute-done.16.far, bf16[1024,1024]{1,0:T(8,128)(2,1)S(1)} %normalize.1.q_ref, ...), custom_call_target="tpu_custom_call", output_to_operand_aliasing={{}: (4, {})} | custom-call | flops 805306368 | bytes 1048576 | tf_op jit(solution)/shard_map/apply/pallas_call | solution.py:413
  (41 shorter events, 0.3 us)
Async XLA Ops:
  2.6 6.8 %collective-permute-start = (f32[2,96,256]{2,1,0:T(8,128)S(1)}, f32[2,96,256]{2,1,0:T(8,128)S(1)}, u32[]{:S(2)}, u32[]{:S(2)}) collective-permute-start(f32[2,96,256]{2,1,0:T(8,128)S(1)} %get-tuple-element.38), channel_id=1, source_target_pairs={{0,1},{1,0},{2,3},{3,2},{4,5},{5,4},{6,7},{7,6},{8,9},{9,8},{10,11... | collective-permute-start | bytes 589832 | tf_op jit(solution)/shard_map/ppermute | solution.py:140
  8.7 25.3 %collective-permute-start.5 = (bf16[1024,512]{1,0:T(8,128)(2,1)S(1)}, bf16[1024,512]{1,0:T(8,128)(2,1)S(1)}, u32[]{:S(2)}, u32[]{:S(2)}) collective-permute-start(bf16[1024,512]{1,0:T(8,128)(2,1)S(1)} %get-tuple-element.17), channel_id=1, source_target_pairs={{0,1},{1,0},{2,3},{3,2},{4,5},{5,4},{6,7},{7,6},{8,9},{9,8},{10,11... | collective-permute-start | bytes 3145736 | tf_op jit(solution)/shard_map/ppermute | solution.py:140
  9.2 24.7 %collective-permute-start.6 = (bf16[1024,512]{1,0:T(8,128)(2,1)S(1)}, bf16[1024,512]{1,0:T(8,128)(2,1)S(1)}, u32[]{:S(2)}, u32[]{:S(2)}) collective-permute-start(bf16[1024,512]{1,0:T(8,128)(2,1)S(1)} %get-tuple-element.18), channel_id=1, source_target_pairs={{0,1},{1,0},{2,3},{3,2},{4,5},{5,4},{6,7},{7,6},{8,9},{9,8},{10,11... | collective-permute-start | bytes 3145736 | tf_op jit(solution)/shard_map/ppermute | solution.py:140
  9.4 5.9 %collective-permute-start.17 = (bf16[2,96,256]{2,1,0:T(8,128)(2,1)S(1)}, bf16[2,96,256]{2,1,0:T(8,128)(2,1)S(1)}, u32[]{:S(2)}, u32[]{:S(2)}) collective-permute-start(bf16[2,96,256]{2,1,0:T(8,128)(2,1)S(1)} %fusion.2), channel_id=1, source_target_pairs={{0,4},{1,5},{2,6},{3,7},{4,0},{5,1},{6,2},{7,3},{8,12},{9,13},{10,... | collective-permute-start | bytes 294920 | tf_op jit(solution)/shard_map/ppermute | solution.py:140
  12.2 4.9 %collective-permute-start.18 = (bf16[2,96,256]{2,1,0:T(8,128)(2,1)S(1)}, bf16[2,96,256]{2,1,0:T(8,128)(2,1)S(1)}, u32[]{:S(2)}, u32[]{:S(2)}) collective-permute-start(bf16[2,96,256]{2,1,0:T(8,128)(2,1)S(1)} %fusion.2), channel_id=1, source_target_pairs={{0,8},{1,9},{2,10},{3,11},{4,12},{5,13},{6,14},{7,15},{8,0},{9,1},... | collective-permute-start | bytes 294920 | tf_op jit(solution)/shard_map/ppermute | solution.py:140
  14.5 7.0 %collective-permute-start.19 = (bf16[2,96,256]{2,1,0:T(8,128)(2,1)S(1)}, bf16[2,96,256]{2,1,0:T(8,128)(2,1)S(1)}, u32[]{:S(2)}, u32[]{:S(2)}) collective-permute-start(bf16[2,96,256]{2,1,0:T(8,128)(2,1)S(1)} %fusion.2), channel_id=1, source_target_pairs={{0,12},{1,13},{2,14},{3,15},{4,8},{5,9},{6,10},{7,11},{8,4},{9,5},... | collective-permute-start | bytes 294920 | tf_op jit(solution)/shard_map/ppermute | solution.py:140
  21.6 12.4 %collective-permute-start.20 = (bf16[4,2,96,256]{3,2,1,0:T(8,128)(2,1)S(1)}, bf16[4,2,96,256]{3,2,1,0:T(8,128)(2,1)S(1)}, u32[]{:S(2)}, u32[]{:S(2)}) collective-permute-start(bf16[4,2,96,256]{3,2,1,0:T(8,128)(2,1)S(1)} %pad_maximum_fusion.2.near), channel_id=1, source_target_pairs={{0,2},{1,3},{2,0},{3,1},{4,6},{5,7},{6,4},{7,5},{8,10},{9,11},{10,... | collective-permute-start | bytes 1179656 | tf_op jit(solution)/shard_map/ppermute | solution.py:140
  22.9 4.6 %collective-permute-start.1 = (bf16[2,96,256]{2,1,0:T(8,128)(2,1)S(1)}, bf16[2,96,256]{2,1,0:T(8,128)(2,1)S(1)}, u32[]{:S(2)}, u32[]{:S(2)}) collective-permute-start(bf16[2,96,256]{2,1,0:T(8,128)(2,1)S(1)} %fusion.3), channel_id=1, source_target_pairs={{0,4},{1,5},{2,6},{3,7},{4,0},{5,1},{6,2},{7,3},{8,12},{9,13},{10,... | collective-permute-start | bytes 294920 | tf_op jit(solution)/shard_map/ppermute | solution.py:140
  25.2 5.4 %collective-permute-start.2 = (bf16[2,96,256]{2,1,0:T(8,128)(2,1)S(1)}, bf16[2,96,256]{2,1,0:T(8,128)(2,1)S(1)}, u32[]{:S(2)}, u32[]{:S(2)}) collective-permute-start(bf16[2,96,256]{2,1,0:T(8,128)(2,1)S(1)} %fusion.3), channel_id=1, source_target_pairs={{0,8},{1,9},{2,10},{3,11},{4,12},{5,13},{6,14},{7,15},{8,0},{9,1},... | collective-permute-start | bytes 294920 | tf_op jit(solution)/shard_map/ppermute | solution.py:140
  27.5 6.2 %collective-permute-start.3 = (bf16[2,96,256]{2,1,0:T(8,128)(2,1)S(1)}, bf16[2,96,256]{2,1,0:T(8,128)(2,1)S(1)}, u32[]{:S(2)}, u32[]{:S(2)}) collective-permute-start(bf16[2,96,256]{2,1,0:T(8,128)(2,1)S(1)} %fusion.3), channel_id=1, source_target_pairs={{0,12},{1,13},{2,14},{3,15},{4,8},{5,9},{6,10},{7,11},{8,4},{9,5},... | collective-permute-start | bytes 294920 | tf_op jit(solution)/shard_map/ppermute | solution.py:140
  33.8 8.9 %collective-permute-start.4 = (bf16[4,2,96,256]{3,2,1,0:T(8,128)(2,1)S(1)}, bf16[4,2,96,256]{3,2,1,0:T(8,128)(2,1)S(1)}, u32[]{:S(2)}, u32[]{:S(2)}) collective-permute-start(bf16[4,2,96,256]{3,2,1,0:T(8,128)(2,1)S(1)} %pad_maximum_fusion.near), channel_id=1, source_target_pairs={{0,2},{1,3},{2,0},{3,1},{4,6},{5,7},{6,4},{7,5},{8,10},{9,11},{10,... | collective-permute-start | bytes 1179656 | tf_op jit(solution)/shard_map/ppermute | solution.py:140
  41.3 8.9 %collective-permute-start.21 = (bf16[4,2,96,256]{3,2,1,0:T(8,128)(2,1)S(1)}, bf16[4,2,96,256]{3,2,1,0:T(8,128)(2,1)S(1)}, u32[]{:S(2)}, u32[]{:S(2)}) collective-permute-start(bf16[4,2,96,256]{3,2,1,0:T(8,128)(2,1)S(1)} %get-tuple-element.23), channel_id=1, source_target_pairs={{0,2},{1,3},{2,0},{3,1},{4,6},{5,7},{6,4},{7,5},{8,10},{9,11},{10,... | collective-permute-start | bytes 1179656 | tf_op jit(solution)/shard_map/ppermute | solution.py:140
  50.0 7.9 %collective-permute-start.7 = (bf16[4,2,96,256]{3,2,1,0:T(8,128)(2,1)S(1)}, bf16[4,2,96,256]{3,2,1,0:T(8,128)(2,1)S(1)}, u32[]{:S(2)}, u32[]{:S(2)}) collective-permute-start(bf16[4,2,96,256]{3,2,1,0:T(8,128)(2,1)S(1)} %get-tuple-element.20), channel_id=1, source_target_pairs={{0,2},{1,3},{2,0},{3,1},{4,6},{5,7},{6,4},{7,5},{8,10},{9,11},{10,... | collective-permute-start | bytes 1179656 | tf_op jit(solution)/shard_map/ppermute | solution.py:140
  50.3 12.1 %collective-permute-start.22 = (bf16[2,96,256]{2,1,0:T(8,128)(2,1)S(1)}, bf16[2,96,256]{2,1,0:T(8,128)(2,1)S(1)}, u32[]{:S(2)}, u32[]{:S(2)}) collective-permute-start(bf16[2,96,256]{2,1,0:T(8,128)(2,1)S(1)} %get-tuple-element.33), channel_id=1, source_target_pairs={{0,4},{1,5},{2,6},{3,7},{4,0},{5,1},{6,2},{7,3},{8,12},{9,13},{10,... | collective-permute-start | bytes 294920 | tf_op jit(solution)/shard_map/ppermute | solution.py:140
  53.5 9.0 %collective-permute-start.23 = (bf16[2,96,256]{2,1,0:T(8,128)(2,1)S(1)}, bf16[2,96,256]{2,1,0:T(8,128)(2,1)S(1)}, u32[]{:S(2)}, u32[]{:S(2)}) collective-permute-start(bf16[2,96,256]{2,1,0:T(8,128)(2,1)S(1)} %get-tuple-element.32), channel_id=1, source_target_pairs={{0,8},{1,9},{2,10},{3,11},{4,12},{5,13},{6,14},{7,15},{8,0},{9,1},... | collective-permute-start | bytes 294920 | tf_op jit(solution)/shard_map/ppermute | solution.py:140
  55.9 6.6 %collective-permute-start.24 = (bf16[2,96,256]{2,1,0:T(8,128)(2,1)S(1)}, bf16[2,96,256]{2,1,0:T(8,128)(2,1)S(1)}, u32[]{:S(2)}, u32[]{:S(2)}) collective-permute-start(bf16[2,96,256]{2,1,0:T(8,128)(2,1)S(1)} %get-tuple-element.31), channel_id=1, source_target_pairs={{0,12},{1,13},{2,14},{3,15},{4,8},{5,9},{6,10},{7,11},{8,4},{9,5},... | collective-permute-start | bytes 294920 | tf_op jit(solution)/shard_map/ppermute | solution.py:140
  58.0 12.3 %collective-permute-start.10 = (bf16[2,96,256]{2,1,0:T(8,128)(2,1)S(1)}, bf16[2,96,256]{2,1,0:T(8,128)(2,1)S(1)}, u32[]{:S(2)}, u32[]{:S(2)}) collective-permute-start(bf16[2,96,256]{2,1,0:T(8,128)(2,1)S(1)} %get-tuple-element.34), channel_id=1, source_target_pairs={{0,12},{1,13},{2,14},{3,15},{4,8},{5,9},{6,10},{7,11},{8,4},{9,5},... | collective-permute-start | bytes 294920 | tf_op jit(solution)/shard_map/ppermute | solution.py:140
  59.4 12.1 %collective-permute-start.8 = (bf16[2,96,256]{2,1,0:T(8,128)(2,1)S(1)}, bf16[2,96,256]{2,1,0:T(8,128)(2,1)S(1)}, u32[]{:S(2)}, u32[]{:S(2)}) collective-permute-start(bf16[2,96,256]{2,1,0:T(8,128)(2,1)S(1)} %get-tuple-element.36), channel_id=1, source_target_pairs={{0,4},{1,5},{2,6},{3,7},{4,0},{5,1},{6,2},{7,3},{8,12},{9,13},{10,... | collective-permute-start | bytes 294920 | tf_op jit(solution)/shard_map/ppermute | solution.py:140
  62.4 11.2 %collective-permute-start.9 = (bf16[2,96,256]{2,1,0:T(8,128)(2,1)S(1)}, bf16[2,96,256]{2,1,0:T(8,128)(2,1)S(1)}, u32[]{:S(2)}, u32[]{:S(2)}) collective-permute-start(bf16[2,96,256]{2,1,0:T(8,128)(2,1)S(1)} %get-tuple-element.35), channel_id=1, source_target_pairs={{0,8},{1,9},{2,10},{3,11},{4,12},{5,13},{6,14},{7,15},{8,0},{9,1},... | collective-permute-start | bytes 294920 | tf_op jit(solution)/shard_map/ppermute | solution.py:140
  62.4 39.6 %copy-start = (bf16[1024,1024]{1,0:T(8,128)(2,1)S(1)}, bf16[1024,1024]{1,0:T(8,128)(2,1)}, u32[]{:S(2)}) copy-start(bf16[1024,1024]{1,0:T(8,128)(2,1)} %x_ref.1) | copy-start | bytes 6291460
  62.6 16.3 %collective-permute-start.25 = (bf16[2,96,256]{2,1,0:T(8,128)(2,1)S(1)}, bf16[2,96,256]{2,1,0:T(8,128)(2,1)S(1)}, u32[]{:S(2)}, u32[]{:S(2)}) collective-permute-start(bf16[2,96,256]{2,1,0:T(8,128)(2,1)S(1)} %get-tuple-element.24), channel_id=1, source_target_pairs={{0,4},{1,5},{2,6},{3,7},{4,0},{5,1},{6,2},{7,3},{8,12},{9,13},{10,... | collective-permute-start | bytes 294920 | tf_op jit(solution)/shard_map/ppermute | solution.py:140
  68.2 12.0 %collective-permute-start.26 = (bf16[2,96,256]{2,1,0:T(8,128)(2,1)S(1)}, bf16[2,96,256]{2,1,0:T(8,128)(2,1)S(1)}, u32[]{:S(2)}, u32[]{:S(2)}) collective-permute-start(bf16[2,96,256]{2,1,0:T(8,128)(2,1)S(1)} %get-tuple-element.24), channel_id=1, source_target_pairs={{0,8},{1,9},{2,10},{3,11},{4,12},{5,13},{6,14},{7,15},{8,0},{9,1},... | collective-permute-start | bytes 294920 | tf_op jit(solution)/shard_map/ppermute | solution.py:140
  70.4 9.9 %collective-permute-start.27 = (bf16[2,96,256]{2,1,0:T(8,128)(2,1)S(1)}, bf16[2,96,256]{2,1,0:T(8,128)(2,1)S(1)}, u32[]{:S(2)}, u32[]{:S(2)}) collective-permute-start(bf16[2,96,256]{2,1,0:T(8,128)(2,1)S(1)} %get-tuple-element.24), channel_id=1, source_target_pairs={{0,12},{1,13},{2,14},{3,15},{4,8},{5,9},{6,10},{7,11},{8,4},{9,5},... | collective-permute-start | bytes 294920 | tf_op jit(solution)/shard_map/ppermute | solution.py:140
  73.7 7.1 %collective-permute-start.11 = (bf16[2,96,256]{2,1,0:T(8,128)(2,1)S(1)}, bf16[2,96,256]{2,1,0:T(8,128)(2,1)S(1)}, u32[]{:S(2)}, u32[]{:S(2)}) collective-permute-start(bf16[2,96,256]{2,1,0:T(8,128)(2,1)S(1)} %get-tuple-element.21), channel_id=1, source_target_pairs={{0,4},{1,5},{2,6},{3,7},{4,0},{5,1},{6,2},{7,3},{8,12},{9,13},{10,... | collective-permute-start | bytes 294920 | tf_op jit(solution)/shard_map/ppermute | solution.py:140
  75.8 10.5 %collective-permute-start.12 = (bf16[2,96,256]{2,1,0:T(8,128)(2,1)S(1)}, bf16[2,96,256]{2,1,0:T(8,128)(2,1)S(1)}, u32[]{:S(2)}, u32[]{:S(2)}) collective-permute-start(bf16[2,96,256]{2,1,0:T(8,128)(2,1)S(1)} %get-tuple-element.21), channel_id=1, source_target_pairs={{0,8},{1,9},{2,10},{3,11},{4,12},{5,13},{6,14},{7,15},{8,0},{9,1},... | collective-permute-start | bytes 294920 | tf_op jit(solution)/shard_map/ppermute | solution.py:140
  78.9 7.4 %collective-permute-start.13 = (bf16[2,96,256]{2,1,0:T(8,128)(2,1)S(1)}, bf16[2,96,256]{2,1,0:T(8,128)(2,1)S(1)}, u32[]{:S(2)}, u32[]{:S(2)}) collective-permute-start(bf16[2,96,256]{2,1,0:T(8,128)(2,1)S(1)} %get-tuple-element.21), channel_id=1, source_target_pairs={{0,12},{1,13},{2,14},{3,15},{4,8},{5,9},{6,10},{7,11},{8,4},{9,5},... | collective-permute-start | bytes 294920 | tf_op jit(solution)/shard_map/ppermute | solution.py:140
  80.3 12.1 %collective-permute-start.29 = (bf16[4,2,96,256]{3,2,1,0:T(8,128)(2,1)S(1)}, bf16[4,2,96,256]{3,2,1,0:T(8,128)(2,1)}, u32[]{:S(2)}, u32[]{:S(2)}) collective-permute-start(bf16[4,2,96,256]{3,2,1,0:T(8,128)(2,1)S(1)} %pad_maximum_fusion.3.near), channel_id=1, source_target_pairs={{0,2},{1,3},{2,0},{3,1},{4,6},{5,7},{6,4},{7,5},{8,10},{9,11},{10,... | collective-permute-start | bytes 1179656 | tf_op jit(solution)/shard_map/ppermute | solution.py:140
  86.3 11.4 %collective-permute-start.15 = (bf16[4,2,96,256]{3,2,1,0:T(8,128)(2,1)S(1)}, bf16[4,2,96,256]{3,2,1,0:T(8,128)(2,1)S(1)}, u32[]{:S(2)}, u32[]{:S(2)}) collective-permute-start(bf16[4,2,96,256]{3,2,1,0:T(8,128)(2,1)S(1)} %pad_maximum_fusion.1.near), channel_id=1, source_target_pairs={{0,2},{1,3},{2,0},{3,1},{4,6},{5,7},{6,4},{7,5},{8,10},{9,11},{10,... | collective-permute-start | bytes 1179656 | tf_op jit(solution)/shard_map/ppermute | solution.py:140
  87.1 15.8 %collective-permute-start.31 = (f32[2,96,256]{2,1,0:T(8,128)}, f32[2,96,256]{2,1,0:T(8,128)}, u32[]{:S(2)}, u32[]{:S(2)}) collective-permute-start(f32[2,96,256]{2,1,0:T(8,128)} %pad_maximum_fusion.6), channel_id=1, source_target_pairs={{0,1},{1,0},{2,3},{3,2},{4,5},{5,4},{6,7},{7,6},{8,9},{9,8},{10,11... | collective-permute-start | bytes 589832 | tf_op jit(solution)/shard_map/ppermute | solution.py:140
  92.4 16.9 %collective-permute-start.28 = (bf16[4,2,96,256]{3,2,1,0:T(8,128)(2,1)S(1)}, bf16[4,2,96,256]{3,2,1,0:T(8,128)(2,1)}, u32[]{:S(2)}, u32[]{:S(2)}) collective-permute-start(bf16[4,2,96,256]{3,2,1,0:T(8,128)(2,1)S(1)} %pad_maximum_fusion.3.near), channel_id=1, source_target_pairs={{0,1},{1,0},{2,3},{3,2},{4,5},{5,4},{6,7},{7,6},{8,9},{9,8},{10,11... | collective-permute-start | bytes 1179656 | tf_op jit(solution)/shard_map/ppermute | solution.py:140
  92.4 16.9 %collective-permute-start.30 = (bf16[4,2,96,256]{3,2,1,0:T(8,128)(2,1)}, bf16[4,2,96,256]{3,2,1,0:T(8,128)(2,1)}, u32[]{:S(2)}, u32[]{:S(2)}) collective-permute-start(bf16[4,2,96,256]{3,2,1,0:T(8,128)(2,1)} %collective-permute-done.29.far), channel_id=1, source_target_pairs={{0,1},{1,0},{2,3},{3,2},{4,5},{5,4},{6,7},{7,6},{8,9},{9,8},{10,11... | collective-permute-start | bytes 1179656 | tf_op jit(solution)/shard_map/ppermute | solution.py:140
  97.8 18.3 %collective-permute-start.14 = (bf16[4,2,96,256]{3,2,1,0:T(8,128)(2,1)S(1)}, bf16[4,2,96,256]{3,2,1,0:T(8,128)(2,1)}, u32[]{:S(2)}, u32[]{:S(2)}) collective-permute-start(bf16[4,2,96,256]{3,2,1,0:T(8,128)(2,1)S(1)} %pad_maximum_fusion.1.near), channel_id=1, source_target_pairs={{0,1},{1,0},{2,3},{3,2},{4,5},{5,4},{6,7},{7,6},{8,9},{9,8},{10,11... | collective-permute-start | bytes 1179656 | tf_op jit(solution)/shard_map/ppermute | solution.py:140
  97.8 18.3 %collective-permute-start.16 = (bf16[4,2,96,256]{3,2,1,0:T(8,128)(2,1)S(1)}, bf16[4,2,96,256]{3,2,1,0:T(8,128)(2,1)}, u32[]{:S(2)}, u32[]{:S(2)}) collective-permute-start(bf16[4,2,96,256]{3,2,1,0:T(8,128)(2,1)S(1)} %collective-permute-done.15.far), channel_id=1, source_target_pairs={{0,1},{1,0},{2,3},{3,2},{4,5},{5,4},{6,7},{7,6},{8,9},{9,8},{10,11... | collective-permute-start | bytes 1179656 | tf_op jit(solution)/shard_map/ppermute | solution.py:140

commit v2 on v1

v2 whole, which is shorter than its diff:
```python
import functools
import math

import jax
import jax.numpy as jnp
from jax import lax
from jax.experimental import pallas as pl
from jax.experimental.pallas import tpu as pltpu
from jax.sharding import PartitionSpec as P

BF16 = jnp.bfloat16
F32 = jnp.float32
VMEM_LIMIT = 48 * 1024 * 1024


def rms_rows(matrix):
    return matrix * lax.rsqrt(jnp.mean(matrix * matrix, axis=-1, keepdims=True) + 1e-06)


def normalized_heads(tokens, heads, head_size):
    row_count = tokens.shape[0]
    wide = tokens.astype(jnp.float32).reshape(row_count, heads, head_size)
    return rms_rows(wide).astype(jnp.bfloat16)


def head_increments(key_rows, value_rows, rates, weight_in, weight_out, block_root):
    fast = weight_out.shape[0]
    in_root = 1.0 / math.sqrt(weight_in.shape[0])
    out_root = 1.0 / math.sqrt(fast)
    scaled = (rates[:, None] * block_root * value_rows.astype(jnp.float32)).astype(jnp.bfloat16)
    pre = jnp.dot(key_rows, weight_in, preferred_element_type=jnp.float32) * in_root
    gate = pre[:, :fast]
    upper = pre[:, fast:]
    sigma = jax.nn.sigmoid(gate)
    active = gate * sigma
    hidden = (active * upper).astype(jnp.bfloat16)
    back = (
        lax.dot_general(
            scaled, weight_out, (((1,), (1,)), ((), ())), preferred_element_type=jnp.float32
        )
        * out_root
    )
    d_gate = (back * upper * sigma * (1.0 + gate * (1.0 - sigma))).astype(jnp.bfloat16)
    d_up = (back * active).astype(jnp.bfloat16)
    joined = jnp.concatenate([d_gate, d_up], axis=1)
    inc_in = (
        lax.dot_general(
            key_rows, joined, (((0,), (0,)), ((), ())), preferred_element_type=jnp.float32
        )
        * in_root
    )
    inc_out = (
        lax.dot_general(
            hidden, scaled, (((0,), (0,)), ((), ())), preferred_element_type=jnp.float32
        )
        * out_root
    )
    return (inc_in, inc_out)


def local_increments(keyn, values, step_size, weight_in, weight_out, block_root):
    heads = weight_in.shape[0]
    head_size = weight_in.shape[1]
    list_in = []
    list_out = []
    for head_number in range(heads):
        value_rows = values[:, head_number * head_size : (head_number + 1) * head_size]
        part_in, part_out = head_increments(
            keyn[:, head_number, :],
            value_rows,
            step_size[head_number],
            weight_in[head_number],
            weight_out[head_number],
            block_root,
        )
        list_in.append(part_in)
        list_out.append(part_out)
    return (jnp.stack(list_in), jnp.stack(list_out))


def renorm_in(matrix):
    heads, rows_here, double = matrix.shape
    split = matrix.reshape(heads, rows_here, 2, double // 2)
    return rms_rows(split).reshape(heads, rows_here, double)


def apply_head(query_rows, weight_in, weight_out):
    fast = weight_out.shape[0]
    pre = jnp.dot(query_rows, weight_in, preferred_element_type=jnp.float32) * (
        1.0 / math.sqrt(weight_in.shape[0])
    )
    gate = pre[:, :fast]
    hidden = (gate * jax.nn.sigmoid(gate) * pre[:, fast:]).astype(jnp.bfloat16)
    return jnp.dot(hidden, weight_out, preferred_element_type=jnp.float32) * (1.0 / math.sqrt(fast))


def apply_all(queryn, next_in, next_out):
    heads = next_in.shape[0]
    pieces = []
    for head_number in range(heads):
        pieces.append(
            apply_head(queryn[:, head_number, :], next_in[head_number], next_out[head_number])
        )
    return jnp.concatenate(pieces, axis=1).astype(jnp.bfloat16)


def per_device_generic(queries, keys, values, step_size, fast_in, fast_out):
    row_count = keys.shape[0]
    heads = fast_in.shape[0]
    head_size = keys.shape[1] // heads
    block_root = 1.0 / math.sqrt(row_count * lax.axis_size("tok"))
    keyn = normalized_heads(keys, heads, head_size)
    queryn = normalized_heads(queries, heads, head_size)
    master_in, master_out = (
        lax.all_gather(fast_in, "tok", axis=1, tiled=True),
        lax.all_gather(fast_out, "tok", axis=1, tiled=True),
    )
    inc_in, inc_out = local_increments(
        keyn,
        values,
        step_size,
        master_in.astype(jnp.bfloat16),
        master_out.astype(jnp.bfloat16),
        block_root,
    )
    total_in, total_out = lax.psum((inc_in, inc_out), "tok")
    whole_in = renorm_in(master_in + total_in)
    whole_out = rms_rows(master_out + total_out)
    output = apply_all(queryn, whole_in.astype(jnp.bfloat16), whole_out.astype(jnp.bfloat16))
    place = lax.axis_index("tok")
    fast_in_next = lax.dynamic_slice_in_dim(whole_in, place * fast_in.shape[1], fast_in.shape[1], 1)
    fast_out_next = lax.dynamic_slice_in_dim(
        whole_out, place * fast_out.shape[1], fast_out.shape[1], 1
    )
    return (output, fast_in_next, fast_out_next)


def swap(value, bits):
    count = lax.axis_size("tok")
    return lax.ppermute(value, "tok", [(place, place ^ bits) for place in range(count)])


def swap_parts(value):
    return lax.ppermute(value, "parts", [(0, 1), (1, 0)])


def after(value, *before):
    return lax.optimization_barrier((value, before))[0]


def compiler_params():
    return pltpu.CompilerParams(vmem_limit_bytes=VMEM_LIMIT)


def head_of(ids, order, other):
    return 2 * jnp.bitwise_xor(ids[1], other) + jnp.bitwise_xor(ids[2], order)


def normalize_head(block):
    wide = block.astype(F32)
    return (wide * lax.rsqrt(jnp.mean(wide * wide, axis=-1, keepdims=True) + 1e-06)).astype(BF16)


def pack_kernel(ids, in_ref, out_ref, own, theirs):
    size = out_ref.shape[-1]
    rows = in_ref.shape[1]
    for other, ref in ((0, own), (1, theirs)):
        for order in range(2):
            head = head_of(ids, order, other)
            for block in range(in_ref.shape[2] // size):
                ref[order, block * rows : (block + 1) * rows, :] = in_ref[
                    head, :, block * size : (block + 1) * size
                ]
            ref[order, -out_ref.shape[1] :, :] = out_ref[head]


def pack(ids, fast_in, fast_out):
    rows = 4 * fast_in.shape[1] + fast_out.shape[1]
    shape = jax.ShapeDtypeStruct((2, rows, fast_out.shape[2]), F32)
    return pl.pallas_call(
        pack_kernel,
        in_specs=[pl.BlockSpec(memory_space=pltpu.SMEM)] + [pl.BlockSpec(memory_space=pltpu.VMEM)] * 2,
        out_shape=[shape, shape],
        compiler_params=compiler_params(),
        name="pack",
    )(ids, fast_in, fast_out)


def pair_kernel(own, got, master_one, master_two, shard):
    for source, ref in enumerate((own, got)):
        for order, master in enumerate((master_one, master_two)):
            master[source] = ref[order]
        shard[source] = ref[0].astype(BF16)


def pair(own, got):
    wide = jax.ShapeDtypeStruct(own.shape, F32)
    return pl.pallas_call(
        pair_kernel,
        out_shape=[wide, wide, jax.ShapeDtypeStruct(own.shape, BF16)],
        compiler_params=compiler_params(),
        name="pair",
    )(own, got)


def prepare_kernel(heads, ids, x_ref, *rest):
    own, send = rest[-2:]
    core = ids[1]
    half = heads // 2
    size = x_ref.shape[1] // heads

    def work(owner, out):
        for local in range(half):
            columns = pl.ds(pl.multiple_of((owner * half + local) * size, size), size)
            into = slice(local * size, (local + 1) * size)
            if len(rest) == 2:
                out[:, into] = normalize_head(x_ref[:, columns])
            else:
                first = rest[0][:, local : local + 1]
                second = rest[0][:, half + local : half + local + 1]
                rate = jnp.where(owner == 0, first, second)
                out[:, into] = (rate * x_ref[:, columns].astype(F32)).astype(BF16)

    work(core, own)
    work(1 - core, send)


def prepare(ids, tokens, rates, heads, name):
    rows, width = tokens.shape
    step = 256
    wide = pl.BlockSpec((step, width), lambda i, ids: (i, 0))
    narrow = pl.BlockSpec((step, width // 2), lambda i, ids: (i, 0))
    operands, specs = [tokens], [wide]
    if rates is not None:
        operands.append(rates)
        specs.append(pl.BlockSpec((step, heads), lambda i, ids: (i, 0)))
    shape = jax.ShapeDtypeStruct((rows, width // 2), BF16)
    return pl.pallas_call(
        functools.partial(prepare_kernel, heads),
        grid_spec=pltpu.PrefetchScalarGridSpec(
            num_scalar_prefetch=1,
            grid=(rows // step,),
            in_specs=specs,
            out_specs=[narrow] * 2,
        ),
        out_shape=[shape] * 2,
        compiler_params=compiler_params(),
        cost_estimate=pl.CostEstimate(
            flops=rows, bytes_accessed=rows, transcendentals=0
        ),
        name=name,
    )(ids, *operands)


def places(chip, core):
    for side in range(2):
        for slot in range(4):
            other = jnp.bitwise_xor(chip, 2 * slot + side)
            for source in range(2):
                yield side, slot, source, 2 * other + jnp.bitwise_xor(core, source)


def assemble(chip, core, lines, w_in, w_out):
    size = w_out.shape[1]
    blocks = w_in.shape[1] // size
    rows_in = w_in.shape[0] // 16
    rows_out = w_out.shape[0] // 16
    for side, slot, source, place in places(chip, core):
        ref = lines[2 * side + slot // 2].at[slot % 2]
        into = pl.ds(pl.multiple_of(place * rows_in, rows_in), rows_in)
        for block in range(blocks):
            w_in[into, block * size : (block + 1) * size] = ref[
                source, block * rows_in : (block + 1) * rows_in, :
            ]
        into = pl.ds(pl.multiple_of(place * rows_out, rows_out), rows_out)
        w_out[into, :] = ref[source, blocks * rows_in :, :]


def increments_kernel(
    ids, near_low, near_high, far_low, far_high, k_own, v_own, k_got, v_got,
    kept, low, high, w_in, w_out, acc_in, acc_out, turned,
):
    step = pl.program_id(0)
    steps = pl.num_programs(0)
    chip, core = ids[0], ids[1]
    size = w_out.shape[1]
    fast = w_out.shape[0]
    in_root = 1.0 / math.sqrt(size)
    out_root = 1.0 / math.sqrt(fast)

    @pl.when(step == 0)
    def _():
        assemble(chip, core, (near_low, near_high, far_low, far_high), w_in, w_out)

    def work(k_ref, v_ref, start_over):
        keyn = k_ref[...]
        scaled = v_ref[...]
        keyn_t = keyn.T
        scaled_t = scaled.T

        def add(ref, columns, value):
            if start_over:
                ref[:, columns] = value
            else:
                ref[:, columns] += value

        chunk = 256
        for start in range(0, fast, chunk):
            gates = slice(start, start + chunk)
            ups = slice(fast + start, fast + start + chunk)
            gate = jnp.dot(keyn, w_in[:, gates], preferred_element_type=F32) * in_root
            upper = jnp.dot(keyn, w_in[:, ups], preferred_element_type=F32) * in_root
            back = (
                lax.dot_general(
                    scaled, w_out[gates, :], (((1,), (1,)), ((), ())), preferred_element_type=F32
                )
                * out_root
            )
            sigma = 0.5 * jnp.tanh(0.5 * gate) + 0.5
            active = gate * sigma
            hidden = (active * upper).astype(BF16)
            d_gate = (back * upper * (sigma + active * (1.0 - sigma))).astype(BF16)
            d_up = (back * active).astype(BF16)
            add(acc_in, gates, jnp.dot(keyn_t, d_gate, preferred_element_type=F32))
            add(acc_in, ups, jnp.dot(keyn_t, d_up, preferred_element_type=F32))
            add(acc_out, gates, jnp.dot(scaled_t, hidden, preferred_element_type=F32))

    @pl.when(step == 0)
    def _():
        work(k_own, v_own, True)

    if k_own.shape[0] * 2 < 2048:

        @pl.when((step > 0) & (step < steps // 2))
        def _():
            work(k_own, v_own, False)

    @pl.when(step >= steps // 2)
    def _():
        work(k_got, v_got, False)

    @pl.when(step == steps - 1)
    def _():
        turned[...] = acc_out[...].T
        blocks = acc_in.shape[1] // size
        rows_in = acc_in.shape[0] // 16
        rows_out = turned.shape[0] // 16
        for side, slot, source, place in places(chip, core):
            ref = kept.at[slot] if side == 0 else (low, high)[slot // 2].at[slot % 2]
            rows = pl.ds(pl.multiple_of(place * rows_in, rows_in), rows_in)
            for block in range(blocks):
                ref[source, block * rows_in : (block + 1) * rows_in, :] = (
                    acc_in[rows, block * size : (block + 1) * size] * in_root
                ).astype(ref.dtype)
            rows = pl.ds(pl.multiple_of(place * rows_out, rows_out), rows_out)
            ref[source, blocks * rows_in :, :] = (turned[rows, :] * out_root).astype(ref.dtype)


def increments(ids, order, lines, k_own, v_own, k_got, v_got, fast):
    rows = k_own.shape[0]
    pair_shape = lines[0].shape
    size = pair_shape[-1]
    step = rows
    half = rows // step
    whole = pl.BlockSpec(pair_shape, lambda i, ids: (0, 0, 0, 0))
    line_shape = (4,) + pair_shape[1:]
    line = pl.BlockSpec(line_shape, lambda i, ids: (0, 0, 0, 0))
    own = pl.BlockSpec((step, size), lambda i, ids: (jnp.minimum(i, half - 1), ids[2] ^ order))
    got = pl.BlockSpec((step, size), lambda i, ids: (jnp.maximum(i - half, 0), ids[2] ^ order))
    return pl.pallas_call(
        increments_kernel,
        grid_spec=pltpu.PrefetchScalarGridSpec(
            num_scalar_prefetch=1,
            grid=(2 * half,),
            in_specs=[whole] * 4 + [own, own, got, got],
            out_specs=[line, whole, whole],
            scratch_shapes=[
                pltpu.VMEM((size, 2 * fast), BF16),
                pltpu.VMEM((fast, size), BF16),
                pltpu.VMEM((size, 2 * fast), F32),
                pltpu.VMEM((size, fast), F32),
                pltpu.VMEM((fast, size), F32),
            ],
        ),
        out_shape=[
            jax.ShapeDtypeStruct(line_shape, F32),
            jax.ShapeDtypeStruct(pair_shape, BF16),
            jax.ShapeDtypeStruct(pair_shape, BF16),
        ],
        compiler_params=compiler_params(),
        cost_estimate=pl.CostEstimate(
            flops=2 * rows * size * fast * 12, bytes_accessed=rows * size * 8, transcendentals=0
        ),
        name="increments",
    )(ids, *lines, k_own, v_own, k_got, v_got)


def add_kernel(kept, came, first, second):
    first[...] = (kept[0] + came[0].astype(F32)).astype(first.dtype)
    second[...] = (kept[1] + came[1].astype(F32)).astype(second.dtype)


def add_pair(kept, came, which, first_type):
    shape = came.shape
    flat = (0,) * (len(shape) - 1)
    return pl.pallas_call(
        add_kernel,
        grid=(1,),
        in_specs=[
            pl.BlockSpec(shape, lambda i: (which,) + flat),
            pl.BlockSpec(shape, lambda i: (0,) + flat),
        ],
        out_specs=[pl.BlockSpec(shape[1:], lambda i: flat)] * 2,
        out_shape=[
            jax.ShapeDtypeStruct(shape[1:], first_type),
            jax.ShapeDtypeStruct(shape[1:], BF16),
        ],
        compiler_params=compiler_params(),
        name="add_pair",
    )(kept, came)


def renorm_kernel(rows_in, master, kept, one, two, three, wide, short):
    size = master.shape[-1]
    for source in range(2):
        fresh = (
            master[source]
            + kept[source]
            + one[source].astype(F32)
            + two[source].astype(F32)
            + three[source].astype(F32)
        )
        for part in range(2):
            first = 2 * part * rows_in
            left = fresh[first : first + rows_in, :]
            right = fresh[first + rows_in : first + 2 * rows_in, :]
            total = jnp.sum(left * left + right * right, axis=-1, keepdims=True)
            factor = lax.rsqrt(total * (1.0 / (2 * size)) + 1e-06)
            for at, value in ((first, left), (first + rows_in, right)):
                done = value * factor
                wide[source, at : at + rows_in, :] = done
                short[source, at : at + rows_in, :] = done.astype(BF16)
        tail = fresh[4 * rows_in :, :]
        done = tail * lax.rsqrt(jnp.mean(tail * tail, axis=-1, keepdims=True) + 1e-06)
        wide[source, 4 * rows_in :, :] = done
        short[source, 4 * rows_in :, :] = done.astype(BF16)


def renorm(master, kept, one, two, three, rows_in):
    shape = master.shape
    return pl.pallas_call(
        functools.partial(renorm_kernel, rows_in),
        out_shape=[jax.ShapeDtypeStruct(shape, F32), jax.ShapeDtypeStruct(shape, BF16)],
        compiler_params=compiler_params(),
        name="renorm",
    )(master, kept, one, two, three)


def apply_kernel(other, ids, near_low, near_high, far_low, far_high, q_ref, *rest):
    o_ref, w_in, w_out = rest[-3:]
    chip, core = ids[0], ids[1]
    fast = w_out.shape[0]

    @pl.when(pl.program_id(0) == 0)
    def _():
        lines = (near_low, near_high, far_low, far_high)
        assemble(chip, jnp.bitwise_xor(core, other), lines, w_in, w_out)

    query = normalize_head(q_ref[...])
    in_root = 1.0 / math.sqrt(w_out.shape[1])
    gate = jnp.dot(query, w_in[:, :fast], preferred_element_type=F32) * in_root
    upper = jnp.dot(query, w_in[:, fast:], preferred_element_type=F32) * in_root
    hidden = (gate * (0.5 * jnp.tanh(0.5 * gate) + 0.5) * upper).astype(BF16)
    result = jnp.dot(hidden, w_out[...], preferred_element_type=F32) * (1.0 / math.sqrt(fast))
    o_ref[...] = result.astype(BF16)


def apply_fast(ids, order, other, lines, queries, output, fast):
    rows, width = queries.shape
    pair_shape = lines[0].shape
    size = pair_shape[-1]
    step = 512
    whole = pl.BlockSpec(pair_shape, lambda i, ids: (0, 0, 0, 0))
    column = pl.BlockSpec((step, size), lambda i, ids: (i, 2 * (ids[1] ^ other) + (ids[2] ^ order)))
    operands = [ids, *lines, queries]
    specs = [whole] * 4 + [column]
    aliases = {}
    if output is not None:
        operands.append(output)
        specs.append(pl.BlockSpec(memory_space=pl.ANY))
        aliases = {6: 0}
    return pl.pallas_call(
        functools.partial(apply_kernel, other),
        grid_spec=pltpu.PrefetchScalarGridSpec(
            num_scalar_prefetch=1,
            grid=(rows // step,),
            in_specs=specs,
            out_specs=column,
            scratch_shapes=[pltpu.VMEM((size, 2 * fast), BF16), pltpu.VMEM((fast, size), BF16)],
        ),
        out_shape=jax.ShapeDtypeStruct((rows, width), BF16),
        input_output_aliases=aliases,
        compiler_params=compiler_params(),
        cost_estimate=pl.CostEstimate(
            flops=2 * rows * size * fast * 3, bytes_accessed=rows * size * 4, transcendentals=0
        ),
        name="apply",
    )(*operands)


def finish_kernel(rows_in, ids, one, two, came, in_next, out_next):
    size = out_next.shape[-1]
    for order, mine in enumerate((one, two)):
        for other, ref in ((0, mine.at[0]), (1, came.at[order])):
            head = head_of(ids, order, other)
            for block in range(4):
                in_next[head, :, block * size : (block + 1) * size] = ref[
                    block * rows_in : (block + 1) * rows_in, :
                ]
            out_next[head] = ref[4 * rows_in :, :]


def finish(ids, one, two, came, fast_in, fast_out):
    return pl.pallas_call(
        functools.partial(finish_kernel, fast_in.shape[1]),
        in_specs=[pl.BlockSpec(memory_space=pltpu.SMEM)] + [pl.BlockSpec(memory_space=pltpu.VMEM)] * 3,
        out_shape=[
            jax.ShapeDtypeStruct(fast_in.shape, F32),
            jax.ShapeDtypeStruct(fast_out.shape, F32),
        ],
        compiler_params=compiler_params(),
        name="finish",
    )(ids, one, two, came)


def per_device_cube(queries, keys, values, step_size, fast_in, fast_out):
    rows = keys.shape[0]
    heads = fast_in.shape[0]
    fast = fast_in.shape[2] // 2
    rows_in = fast_in.shape[1]
    place = lax.axis_index("tok")
    ids = jnp.stack([place // 2, place % 2, lax.axis_index("parts")]).astype(jnp.int32)
    block_root = 1.0 / math.sqrt(rows * lax.axis_size("tok"))

    own, theirs = pack(ids, fast_in, fast_out)
    got = swap(theirs, 1)
    master_one, master_two, shard = pair(own, got)
    masters = (master_one, master_two)
    z1, z2, z3 = swap(shard, 4), swap(shard, 8), swap(shard, 12)
    near_low = jnp.stack([shard, z1])
    near_high = jnp.stack([z2, z3])
    far_low, far_high = swap(near_low, 2), swap(near_high, 2)
    first = (near_low, near_high, far_low, far_high)
    second = tuple(swap_parts(piece) for piece in first)

    k_own, k_send = prepare(ids, after(keys, shard), None, heads, "keys")
    v_own, v_send = prepare(ids, after(values, z1), step_size.T * block_root, heads, "values")
    k_got, v_got = swap(k_send, 1), swap(v_send, 1)

    kept, low, high = [], [], []
    for order, lines in enumerate((first, second)):
        a, b, c = increments(ids, order, lines, k_own, v_own, k_got, v_got, fast)
        kept.append(a)
        low.append(swap(b, 2))
        high.append(swap(c, 2))
    wide, short = [], []
    for order in range(2):
        sum2, sum3 = add_pair(kept[order], high[order], 1, BF16)
        sum0, sum1 = add_pair(kept[order], low[order], 0, F32)
        three, two, one = swap(sum3, 12), swap(sum2, 8), swap(sum1, 4)
        a, b = renorm(masters[order], sum0, one, two, three, rows_in)
        wide.append(a)
        short.append(b)

    output = None
    for order in range(2):
        shard = short[order]
        z3, z2, z1 = swap(shard, 12), swap(shard, 8), swap(shard, 4)
        near_low = jnp.stack([shard, z1])
        near_high = jnp.stack([z2, z3])
        far = (swap(near_low, 2), swap(near_high, 2))
        if order:
            far = after(far, output)
        mine = (near_low, near_high, *far)
        others = tuple(swap(piece, 1) for piece in mine)
        output = apply_fast(ids, order, 0, mine, queries, output, fast)
        output = apply_fast(ids, order, 1, others, queries, output, fast)

    came = swap(jnp.stack([wide[0][1], wide[1][1]]), 1)
    return (output, *finish(ids, wide[0], wide[1], came, fast_in, fast_out))


def per_device(queries, keys, values, step_size, fast_in, fast_out):
    fits = (
        lax.axis_size("tok") == 16
        and lax.axis_size("parts") == 2
        and fast_in.shape[0] == 4
        and fast_in.shape[1] % 16 == 0
    )
    chosen = per_device_cube if fits else per_device_generic
    return chosen(queries, keys, values, step_size, fast_in, fast_out)


def solution(mesh):
    placed = (
        P(("parts", "tok"), None),
        P(("parts", "tok"), None),
        P(("parts", "tok"), None),
        P(None, ("parts", "tok")),
        P(None, "tok", None),
        P(None, "tok", None),
    )
    return jax.shard_map(
        per_device,
        mesh=mesh,
        in_specs=placed,
        out_specs=(P(("parts", "tok"), None), P("parts", "tok", None), P("parts", "tok", None)),
        check_vma=False,
    )
```

time: 122 us -> 114 us (0.934)
  Pallas kernels: 35.3 us -> 30.4 us
  other arithmetic: 3.25 us -> 0.93 us
  starting transfers between devices: 54.6 us -> 53 us
    ppermute x32 -> x37, starting transfers between devices: 54.6 us -> 49 us  [swap(): lax.ppermute(value, 'tok', [(place, place ^ bits) for place in range(coun...]
    ppermute x0 -> x4, starting transfers between devices: none -> 3.94 us  [swap_parts(): return lax.ppermute(value, 'parts', [(0, 1), (1, 0)])]
    pallas_call x4 -> x11, Pallas kernels: 20.5 us -> 17.9 us  [the longest x2 11.7 us: increments(): pl.pallas_call(increments_kernel, grid_spec=pltpu.PrefetchScalarGridSpec(...]
    unnamed x3 -> x10, local copies, waits for them, and re-layouts: 0.94 us -> 3.46 us
    ppermute x0 -> x4, waiting for transfers between devices: none -> 2.34 us  [swap_parts(): return lax.ppermute(value, 'parts', [(0, 1), (1, 0)])]
    pallas_call x4, Pallas kernels: 14.5 us -> 12.2 us  [apply_fast(): pl.pallas_call(functools.partial(apply_kernel, other), grid_spec=pltpu.Pr...]
    ppermute x32 -> x37, waiting for transfers between devices: 22.4 us -> 20.6 us  [swap(): lax.ppermute(value, 'tok', [(place, place ^ bits) for place in range(coun...]
    reshape x2 -> x0, local copies, waits for them, and re-layouts: 1.69 us -> none  [the longest x1 0.97 us: pack(): fast_in.reshape(heads, rows, double // size, size).transpose(0, 2, 1, 3)]
  transfers between devices with their start and end apart: 32 -> 41, of which waited for: 11 -> 10; matrix products, arithmetic and copies ran while one was open for 4% -> 1% of each run, Pallas kernels for 26% -> 24%
where the time goes in v2:
time: 114 us; the launch traced here: 112 us
  starting transfers between devices  53 us (46%)
  Pallas kernels  30.4 us (27%)
  waiting for transfers between devices  23 us (20%)
  local copies, waits for them, and re-layouts  3.69 us (3%)
    ppermute x37, starting transfers between devices, swap(): lax.ppermute(value, 'tok', [(place, place ^ bits) for place in range(coun...  49 us
    ppermute x37, waiting for transfers between devices, swap(): lax.ppermute(value, 'tok', [(place, place ^ bits) for place in range(coun...  20.6 us
    pallas_call x4, Pallas kernels, apply_fast(): pl.pallas_call(functools.partial(apply_kernel, other), grid_spec=pltpu.Pr...  12.2 us
    pallas_call x2, Pallas kernels, increments(): pl.pallas_call(increments_kernel, grid_spec=pltpu.PrefetchScalarGridSpec(...  11.7 us
    pallas_call x2, Pallas kernels, prepare(): pl.pallas_call(functools.partial(prepare_kernel, heads), grid_spec=pltpu....  4.12 us
    ppermute x4, starting transfers between devices, swap_parts(): return lax.ppermute(value, 'parts', [(0, 1), (1, 0)])  3.94 us
    unnamed x10, local copies, waits for them, and re-layouts  3.46 us
    ppermute x4, waiting for transfers between devices, swap_parts(): return lax.ppermute(value, 'parts', [(0, 1), (1, 0)])  2.34 us
  transfers between devices with their start and end apart: 41, of which 10 were waited for; matrix products, arithmetic and copies ran while one was open for 1% of the time, Pallas kernels for 24%

profile of v2, /device:TPU:1, one launch (start us, length us, event | category | flops | bytes accessed | tf_op | source)
XLA Modules:
  0.0 111.8 jit_solution(13876400471441560686)
XLA Ops:
  0.6 0.1 pad_add_fusion.ids
  0.7 0.9 copy-done.3
  1.7 0.9 copy-done.4
  2.6 0.6 pack.1
  3.2 0.1 collective-permute-start
  3.3 1.4 %collective-permute-done.got = f32[2,96,256]{2,1,0:T(8,128)S(1)} collective-permute-done((f32[2,96,256]{2,1,0:T(8,128)S(1)}, f32[2,96,256]{2,1,0:T(8,128)S(1)}, u32[]{:S(2)}, u32[]{:S(2)}) %collective-permute-start) | collective-permute-done | bytes 196640 | tf_op jit(solution)/shard_map/ppermute | solution.py:140
  4.7 2.5 %collective-permute-start.1 = (bf16[2,96,256]{2,1,0:T(8,128)(2,1)S(1)}, bf16[2,96,256]{2,1,0:T(8,128)(2,1)S(1)}, u32[]{:S(2)}, u32[]{:S(2)}) collective-permute-start(bf16[2,96,256]{2,1,0:T(8,128)(2,1)S(1)} %get-tuple-element.39), channel_id=1, source_target_pairs={{0,4},{1,5},{2,6},{3,7},{4,0},{5,1},{6,2},{7,3},{8,12},{9,13},{10,... | collective-permute-start | bytes 294920 | tf_op jit(solution)/shard_map/ppermute | solution.py:140
  7.2 0.7 broadcast_multiply_fusion
  7.9 0.2 copy.14
  8.2 1.6 %copy-done.1 = bf16[1024,1024]{1,0:T(8,128)(2,1)S(1)} copy-done((bf16[1024,1024]{1,0:T(8,128)(2,1)S(1)}, bf16[1024,1024]{1,0:T(8,128)(2,1)}, u32[]{:S(2)}) %copy-start.1) | copy-done | bytes 2097176
  9.8 1.5 %keys.1 = (bf16[1024,512]{1,0:T(8,128)(2,1)S(1)}, bf16[1024,512]{1,0:T(8,128)(2,1)S(1)}) custom-call(s32[3]{0:T(128)S(1)} %pad_add_fusion.ids, bf16[1024,1024]{1,0:T(8,128)(2,1)S(1)} %copy-done.1), custom_call_target="tpu_custom_call" | custom-call | flops 1024 | bytes 1024 | tf_op jit(solution)/shard_map/keys/pallas_call | solution.py:238
  11.3 0.7 collective-permute-start.10
  12.0 2.6 %values.1 = (bf16[1024,512]{1,0:T(8,128)(2,1)S(1)}, bf16[1024,512]{1,0:T(8,128)(2,1)S(1)}) custom-call(s32[3]{0:T(128)S(1)} %pad_add_fusion.ids, bf16[1024,1024]{1,0:T(8,128)(2,1)S(1)} %copy-done.2, f32[1024,4]{1,0:T(8,128)S(1)} %bitcast.16), custom_call_target="tpu_custom_call" | custom-call | flops 1024 | bytes 1024 | tf_op jit(solution)/shard_map/values/pallas_call | solution.py:238
  14.6 0.1 collective-permute-start.11
  14.7 2.4 %collective-permute-start.3 = (bf16[2,96,256]{2,1,0:T(8,128)(2,1)S(1)}, bf16[2,96,256]{2,1,0:T(8,128)(2,1)S(1)}, u32[]{:S(2)}, u32[]{:S(2)}) collective-permute-start(bf16[2,96,256]{2,1,0:T(8,128)(2,1)S(1)} %get-tuple-element.39), channel_id=1, source_target_pairs={{0,8},{1,9},{2,10},{3,11},{4,12},{5,13},{6,14},{7,15},{8,0},{9,1},... | collective-permute-start | bytes 294920 | tf_op jit(solution)/shard_map/ppermute | solution.py:140
  17.1 0.1 collective-permute-start.4
  17.2 7.3 %collective-permute-done.3 = bf16[2,96,256]{2,1,0:T(8,128)(2,1)S(1)} collective-permute-done((bf16[2,96,256]{2,1,0:T(8,128)(2,1)S(1)}, bf16[2,96,256]{2,1,0:T(8,128)(2,1)S(1)}, u32[]{:S(2)}, u32[]{:S(2)}) %collective-permute-start.3) | collective-permute-done | bytes 98336 | tf_op jit(solution)/shard_map/ppermute | solution.py:140
  24.5 1.3 %collective-permute-start.8 = (bf16[2,2,96,256]{3,2,1,0:T(8,128)(2,1)S(1)}, bf16[2,2,96,256]{3,2,1,0:T(8,128)(2,1)S(1)}, u32[]{:S(2)}, u32[]{:S(2)}) collective-permute-start(bf16[2,2,96,256]{3,2,1,0:T(8,128)(2,1)S(1)} %pad_maximum_fusion.1.near_high), channel_id=1, source_target_pairs={{0,2},{1,3},{2,0},{3,1},{4,6},{5,7},{6,4},{7,5},{8,10},{9,11},{10,... | collective-permute-start | bytes 589832 | tf_op jit(solution)/shard_map/ppermute | solution.py:140
  25.9 0.3 collective-permute-start.6
  26.2 1.2 %collective-permute-start.5 = (bf16[2,2,96,256]{3,2,1,0:T(8,128)(2,1)S(1)}, bf16[2,2,96,256]{3,2,1,0:T(8,128)(2,1)S(1)}, u32[]{:S(2)}, u32[]{:S(2)}) collective-permute-start(bf16[2,2,96,256]{3,2,1,0:T(8,128)(2,1)S(1)} %pad_maximum_fusion.1.near_high), channel_id=1, source_target_pairs={{0,16},{16,0},{1,17},{17,1},{2,18},{18,2},{3,19},{19,3},{4,20},{20... | collective-permute-start | bytes 589832 | tf_op jit(solution)/shard_map/ppermute | solution.py:144
  27.4 2.9 %collective-permute-done.8.far_high = bf16[2,2,96,256]{3,2,1,0:T(8,128)(2,1)S(1)} collective-permute-done((bf16[2,2,96,256]{3,2,1,0:T(8,128)(2,1)S(1)}, bf16[2,2,96,256]{3,2,1,0:T(8,128)(2,1)S(1)}, u32[]{:S(2)}, u32[]{:S(2)}) %collective-permute-start.8) | collective-permute-done | bytes 196640 | tf_op jit(solution)/shard_map/ppermute | solution.py:140
  30.3 1.2 %collective-permute-start.2 = (bf16[2,2,96,256]{3,2,1,0:T(8,128)(2,1)S(1)}, bf16[2,2,96,256]{3,2,1,0:T(8,128)(2,1)S(1)}, u32[]{:S(2)}, u32[]{:S(2)}) collective-permute-start(bf16[2,2,96,256]{3,2,1,0:T(8,128)(2,1)S(1)} %pad_maximum_fusion.near_low), channel_id=1, source_target_pairs={{0,16},{16,0},{1,17},{17,1},{2,18},{18,2},{3,19},{19,3},{4,20},{20... | collective-permute-start | bytes 589832 | tf_op jit(solution)/shard_map/ppermute | solution.py:144
  31.5 3.0 %collective-permute-done.6.far_low = bf16[2,2,96,256]{3,2,1,0:T(8,128)(2,1)S(1)} collective-permute-done((bf16[2,2,96,256]{3,2,1,0:T(8,128)(2,1)S(1)}, bf16[2,2,96,256]{3,2,1,0:T(8,128)(2,1)S(1)}, u32[]{:S(2)}, u32[]{:S(2)}) %collective-permute-start.6) | collective-permute-done | bytes 196640 | tf_op jit(solution)/shard_map/ppermute | solution.py:140
  34.5 1.2 %collective-permute-start.9 = (bf16[2,2,96,256]{3,2,1,0:T(8,128)(2,1)S(1)}, bf16[2,2,96,256]{3,2,1,0:T(8,128)(2,1)S(1)}, u32[]{:S(2)}, u32[]{:S(2)}) collective-permute-start(bf16[2,2,96,256]{3,2,1,0:T(8,128)(2,1)S(1)} %collective-permute-done.8.far_high), channel_id=1, source_target_pairs={{0,16},{16,0},{1,17},{17,1},{2,18},{18,2},{3,19},{19,3},{4,20},{20... | collective-permute-start | bytes 589832 | tf_op jit(solution)/shard_map/ppermute | solution.py:144
  35.8 0.2 collective-permute-start.7
  36.0 5.8 %increments.3 = (f32[4,2,96,256]{3,2,1,0:T(8,128)S(1)}, bf16[2,2,96,256]{3,2,1,0:T(8,128)(2,1)S(1)}, bf16[2,2,96,256]{3,2,1,0:T(8,128)(2,1)S(1)}) custom-call(s32[3]{0:T(128)S(1)} %pad_add_fusion.ids, bf16[2,2,96,256]{3,2,1,0:T(8,128)(2,1)S(1)} %pad_maximum_fusion.near_low, bf16[2,2,96,256]{3,2,1,0:T(8,128)(2,1)S(1)} %pad_maximum_fusion.1.near_high, ...), custom_call_target="tpu_custom_call" | custom-call | flops 3221225472 | bytes 2097152 | tf_op jit(solution)/shard_map/increments/pallas_call | solution.py:370
  41.7 1.3 %collective-permute-start.26 = (bf16[2,2,96,256]{3,2,1,0:T(8,128)(2,1)S(1)}, bf16[2,2,96,256]{3,2,1,0:T(8,128)(2,1)S(1)}, u32[]{:S(2)}, u32[]{:S(2)}) collective-permute-start(bf16[2,2,96,256]{3,2,1,0:T(8,128)(2,1)S(1)} %get-tuple-element.59), channel_id=1, source_target_pairs={{0,2},{1,3},{2,0},{3,1},{4,6},{5,7},{6,4},{7,5},{8,10},{9,11},{10,... | collective-permute-start | bytes 589832 | tf_op jit(solution)/shard_map/ppermute | solution.py:140
  43.1 0.2 collective-permute-start.24
  43.3 2.3 %collective-permute-done.7.far_low = bf16[2,2,96,256]{3,2,1,0:T(8,128)(2,1)S(1)} collective-permute-done((bf16[2,2,96,256]{3,2,1,0:T(8,128)(2,1)S(1)}, bf16[2,2,96,256]{3,2,1,0:T(8,128)(2,1)S(1)}, u32[]{:S(2)}, u32[]{:S(2)}) %collective-permute-start.7) | collective-permute-done | bytes 196640 | tf_op jit(solution)/shard_map/ppermute | solution.py:144
  45.6 5.9 %increments.2 = (f32[4,2,96,256]{3,2,1,0:T(8,128)S(1)}, bf16[2,2,96,256]{3,2,1,0:T(8,128)(2,1)S(1)}, bf16[2,2,96,256]{3,2,1,0:T(8,128)(2,1)S(1)}) custom-call(s32[3]{0:T(128)S(1)} %pad_add_fusion.ids, bf16[2,2,96,256]{3,2,1,0:T(8,128)(2,1)S(1)} %collective-permute-done.2.near_low, bf16[2,2,96,256]{3,2,1,0:T(8,128)(2,1)S(1)} %collective-permute-done.5.near_high, ...), custom_call_target="tpu_custom_call" | custom-call | flops 3221225472 | bytes 2097152 | tf_op jit(solution)/shard_map/increments/pallas_call | solution.py:370
  51.6 1.4 %collective-permute-start.14 = (bf16[2,2,96,256]{3,2,1,0:T(8,128)(2,1)S(1)}, bf16[2,2,96,256]{3,2,1,0:T(8,128)(2,1)S(1)}, u32[]{:S(2)}, u32[]{:S(2)}) collective-permute-start(bf16[2,2,96,256]{3,2,1,0:T(8,128)(2,1)S(1)} %get-tuple-element.50), channel_id=1, source_target_pairs={{0,2},{1,3},{2,0},{3,1},{4,6},{5,7},{6,4},{7,5},{8,10},{9,11},{10,... | collective-permute-start | bytes 589832 | tf_op jit(solution)/shard_map/ppermute | solution.py:140
  52.9 0.2 collective-permute-start.12
  53.2 2.8 %collective-permute-start.27 = (bf16[2,96,256]{2,1,0:T(8,128)(2,1)S(1)}, bf16[2,96,256]{2,1,0:T(8,128)(2,1)S(1)}, u32[]{:S(2)}, u32[]{:S(2)}) collective-permute-start(bf16[2,96,256]{2,1,0:T(8,128)(2,1)S(1)} %get-tuple-element.60), channel_id=1, source_target_pairs={{0,8},{1,9},{2,10},{3,11},{4,12},{5,13},{6,14},{7,15},{8,0},{9,1},... | collective-permute-start | bytes 294920 | tf_op jit(solution)/shard_map/ppermute | solution.py:140
  55.9 1.6 %collective-permute-start.28 = (bf16[2,96,256]{2,1,0:T(8,128)(2,1)S(1)}, bf16[2,96,256]{2,1,0:T(8,128)(2,1)S(1)}, u32[]{:S(2)}, u32[]{:S(2)}) collective-permute-start(bf16[2,96,256]{2,1,0:T(8,128)(2,1)S(1)} %get-tuple-element.61), channel_id=1, source_target_pairs={{0,12},{1,13},{2,14},{3,15},{4,8},{5,9},{6,10},{7,11},{8,4},{9,5},... | collective-permute-start | bytes 294920 | tf_op jit(solution)/shard_map/ppermute | solution.py:140
  57.7 2.0 %collective-permute-start.15 = (bf16[2,96,256]{2,1,0:T(8,128)(2,1)S(1)}, bf16[2,96,256]{2,1,0:T(8,128)(2,1)S(1)}, u32[]{:S(2)}, u32[]{:S(2)}) collective-permute-start(bf16[2,96,256]{2,1,0:T(8,128)(2,1)S(1)} %get-tuple-element.51), channel_id=1, source_target_pairs={{0,8},{1,9},{2,10},{3,11},{4,12},{5,13},{6,14},{7,15},{8,0},{9,1},... | collective-permute-start | bytes 294920 | tf_op jit(solution)/shard_map/ppermute | solution.py:140
  59.7 0.9 collective-permute-done.12.came
  60.6 0.7 collective-permute-start.16
  61.4 1.7 %collective-permute-start.13 = (bf16[2,96,256]{2,1,0:T(8,128)(2,1)S(1)}, bf16[2,96,256]{2,1,0:T(8,128)(2,1)S(1)}, u32[]{:S(2)}, u32[]{:S(2)}) collective-permute-start(bf16[2,96,256]{2,1,0:T(8,128)(2,1)S(1)} %get-tuple-element.49), channel_id=1, source_target_pairs={{0,4},{1,5},{2,6},{3,7},{4,0},{5,1},{6,2},{7,3},{8,12},{9,13},{10,... | collective-permute-start | bytes 294920 | tf_op jit(solution)/shard_map/ppermute | solution.py:140
  63.1 0.4 collective-permute-done.25.one
  63.5 0.1 renorm.3
  63.6 0.9 collective-permute-start.31
  64.5 1.2 %collective-permute-start.32 = (bf16[2,96,256]{2,1,0:T(8,128)(2,1)S(1)}, bf16[2,96,256]{2,1,0:T(8,128)(2,1)S(1)}, u32[]{:S(2)}, u32[]{:S(2)}) collective-permute-start(bf16[2,96,256]{2,1,0:T(8,128)(2,1)S(1)} %get-tuple-element.62), channel_id=1, source_target_pairs={{0,12},{1,13},{2,14},{3,15},{4,8},{5,9},{6,10},{7,11},{8,4},{9,5},... | collective-permute-start | bytes 294920 | tf_op jit(solution)/shard_map/ppermute | solution.py:140
  65.8 1.9 %collective-permute-done.15.two = bf16[2,96,256]{2,1,0:T(8,128)(2,1)S(1)} collective-permute-done((bf16[2,96,256]{2,1,0:T(8,128)(2,1)S(1)}, bf16[2,96,256]{2,1,0:T(8,128)(2,1)S(1)}, u32[]{:S(2)}, u32[]{:S(2)}) %collective-permute-start.15) | collective-permute-done | bytes 98336 | tf_op jit(solution)/shard_map/ppermute | solution.py:140
  67.7 0.8 collective-permute-done.13.one
  68.5 0.1 renorm.2
  68.6 6.6 %collective-permute-start.19 = (bf16[2,96,256]{2,1,0:T(8,128)(2,1)S(1)}, bf16[2,96,256]{2,1,0:T(8,128)(2,1)S(1)}, u32[]{:S(2)}, u32[]{:S(2)}) collective-permute-start(bf16[2,96,256]{2,1,0:T(8,128)(2,1)S(1)} %get-tuple-element.53), channel_id=1, source_target_pairs={{0,8},{1,9},{2,10},{3,11},{4,12},{5,13},{6,14},{7,15},{8,0},{9,1},... | collective-permute-start | bytes 294920 | tf_op jit(solution)/shard_map/ppermute | solution.py:140
  75.2 1.6 %collective-permute-start.20 = (bf16[2,96,256]{2,1,0:T(8,128)(2,1)S(1)}, bf16[2,96,256]{2,1,0:T(8,128)(2,1)S(1)}, u32[]{:S(2)}, u32[]{:S(2)}) collective-permute-start(bf16[2,96,256]{2,1,0:T(8,128)(2,1)S(1)} %get-tuple-element.53), channel_id=1, source_target_pairs={{0,12},{1,13},{2,14},{3,15},{4,8},{5,9},{6,10},{7,11},{8,4},{9,5},... | collective-permute-start | bytes 294920 | tf_op jit(solution)/shard_map/ppermute | solution.py:140
  76.9 1.3 %collective-permute-start.36 = (bf16[2,2,96,256]{3,2,1,0:T(8,128)(2,1)S(1)}, bf16[2,2,96,256]{3,2,1,0:T(8,128)(2,1)S(1)}, u32[]{:S(2)}, u32[]{:S(2)}) collective-permute-start(bf16[2,2,96,256]{3,2,1,0:T(8,128)(2,1)S(1)} %pad_maximum_fusion.5.near_high), channel_id=1, source_target_pairs={{0,2},{1,3},{2,0},{3,1},{4,6},{5,7},{6,4},{7,5},{8,10},{9,11},{10,... | collective-permute-start | bytes 589832 | tf_op jit(solution)/shard_map/ppermute | solution.py:140
  78.3 0.2 collective-permute-start.34
  78.5 6.2 %collective-permute-start.17 = (bf16[2,96,256]{2,1,0:T(8,128)(2,1)S(1)}, bf16[2,96,256]{2,1,0:T(8,128)(2,1)S(1)}, u32[]{:S(2)}, u32[]{:S(2)}) collective-permute-start(bf16[2,96,256]{2,1,0:T(8,128)(2,1)S(1)} %get-tuple-element.53), channel_id=1, source_target_pairs={{0,4},{1,5},{2,6},{3,7},{4,0},{5,1},{6,2},{7,3},{8,12},{9,13},{10,... | collective-permute-start | bytes 294920 | tf_op jit(solution)/shard_map/ppermute | solution.py:140
  84.7 2.0 %collective-permute-done.19 = bf16[2,96,256]{2,1,0:T(8,128)(2,1)S(1)} collective-permute-done((bf16[2,96,256]{2,1,0:T(8,128)(2,1)S(1)}, bf16[2,96,256]{2,1,0:T(8,128)(2,1)S(1)}, u32[]{:S(2)}, u32[]{:S(2)}) %collective-permute-start.19) | collective-permute-done | bytes 98336 | tf_op jit(solution)/shard_map/ppermute | solution.py:140
  86.7 5.3 %collective-permute-start.33 = (bf16[2,2,96,256]{3,2,1,0:T(8,128)(2,1)S(1)}, bf16[2,2,96,256]{3,2,1,0:T(8,128)(2,1)S(1)}, u32[]{:S(2)}, u32[]{:S(2)}) collective-permute-start(bf16[2,2,96,256]{3,2,1,0:T(8,128)(2,1)S(1)} %pad_maximum_fusion.5.near_high), channel_id=1, source_target_pairs={{0,1},{1,0},{2,3},{3,2},{4,5},{5,4},{6,7},{7,6},{8,9},{9,8},{10,11... | collective-permute-start | bytes 589832 | tf_op jit(solution)/shard_map/ppermute | solution.py:140
  91.9 0.1 collective-permute-start.30
  92.1 1.3 %collective-permute-start.23 = (bf16[2,2,96,256]{3,2,1,0:T(8,128)(2,1)S(1)}, bf16[2,2,96,256]{3,2,1,0:T(8,128)(2,1)S(1)}, u32[]{:S(2)}, u32[]{:S(2)}) collective-permute-start(bf16[2,2,96,256]{3,2,1,0:T(8,128)(2,1)S(1)} %pad_maximum_fusion.3.near_high), channel_id=1, source_target_pairs={{0,2},{1,3},{2,0},{3,1},{4,6},{5,7},{6,4},{7,5},{8,10},{9,11},{10,... | collective-permute-start | bytes 589832 | tf_op jit(solution)/shard_map/ppermute | solution.py:140
  93.4 2.6 %collective-permute-start.37 = (bf16[2,2,96,256]{3,2,1,0:T(8,128)(2,1)S(1)}, bf16[2,2,96,256]{3,2,1,0:T(8,128)(2,1)S(1)}, u32[]{:S(2)}, u32[]{:S(2)}) collective-permute-start(bf16[2,2,96,256]{3,2,1,0:T(8,128)(2,1)S(1)} %collective-permute-done.36.far_high), channel_id=1, source_target_pairs={{0,1},{1,0},{2,3},{3,2},{4,5},{5,4},{6,7},{7,6},{8,9},{9,8},{10,11... | collective-permute-start | bytes 589832 | tf_op jit(solution)/shard_map/ppermute | solution.py:140
  96.1 0.2 collective-permute-start.22
  96.4 3.0 %apply.4.rest_0_ = bf16[1024,1024]{1,0:T(8,128)(2,1)} custom-call(s32[3]{0:T(128)S(1)} %pad_add_fusion.ids, bf16[2,2,96,256]{3,2,1,0:T(8,128)(2,1)S(1)} %pad_maximum_fusion.4.near_low, bf16[2,2,96,256]{3,2,1,0:T(8,128)(2,1)S(1)} %pad_maximum_fusion.5.near_high, bf16[2,2,96,256]{3,2,1,0:T(8,128)(2,1)S(1)} %collective-permute-done.34.far_low, ...), custom_call_target="tpu_custom_call" | custom-call | flops 805306368 | bytes 1048576 | tf_op jit(solution)/shard_map/apply/pallas_call | solution.py:492
  99.4 0.7 collective-permute-start.40
  100.2 0.4 collective-permute-start.18
  100.7 3.0 %apply.5.rest_0_ = bf16[1024,1024]{1,0:T(8,128)(2,1)} custom-call(s32[3]{0:T(128)S(1)} %pad_add_fusion.ids, bf16[2,2,96,256]{3,2,1,0:T(8,128)(2,1)S(1)} %collective-permute-done.30.near_low, bf16[2,2,96,256]{3,2,1,0:T(8,128)(2,1)S(1)} %collective-permute-done.33.near_high, ...), custom_call_target="tpu_custom_call", output_to_operand_aliasing={{}: (6, {})} | custom-call | flops 805306368 | bytes 1048576 | tf_op jit(solution)/shard_map/apply/pallas_call | solution.py:492
  103.7 0.6 collective-permute-start.38
  104.3 1.3 %finish.1 = (f32[4,16,1024]{2,1,0:T(8,128)}, f32[4,32,256]{2,1,0:T(8,128)}) custom-call(s32[3]{0:T(128)S(1)} %pad_add_fusion.ids, f32[2,96,256]{2,1,0:T(8,128)S(1)} %get-tuple-element.65.one, f32[2,96,256]{2,1,0:T(8,128)S(1)} %get-tuple-element.66.two, f32[2,96,256]{2,1,0:T(8,128)S(1)} %collective-permute-done.40.came), custom_call_target="tpu_custom_call" | custom-call | tf_op jit(solution)/shard_map/finish/pallas_call | solution.py:524
  105.6 3.0 %apply.6.rest_0_ = bf16[1024,1024]{1,0:T(8,128)(2,1)} custom-call(s32[3]{0:T(128)S(1)} %pad_add_fusion.ids, bf16[2,2,96,256]{3,2,1,0:T(8,128)(2,1)S(1)} %pad_maximum_fusion.2.near_low, bf16[2,2,96,256]{3,2,1,0:T(8,128)(2,1)S(1)} %pad_maximum_fusion.3.near_high, ...), custom_call_target="tpu_custom_call", output_to_operand_aliasing={{}: (6, {})} | custom-call | flops 805306368 | bytes 1048576 | tf_op jit(solution)/shard_map/apply/pallas_call | solution.py:492
  108.7 3.0 %apply.7 = bf16[1024,1024]{1,0:T(8,128)(2,1)} custom-call(s32[3]{0:T(128)S(1)} %pad_add_fusion.ids, bf16[2,2,96,256]{3,2,1,0:T(8,128)(2,1)S(1)} %collective-permute-done.18.near_low, bf16[2,2,96,256]{3,2,1,0:T(8,128)(2,1)S(1)} %collective-permute-done.21.near_high, ...), custom_call_target="tpu_custom_call", output_to_operand_aliasing={{}: (6, {})} | custom-call | flops 805306368 | bytes 1048576 | tf_op jit(solution)/shard_map/apply/pallas_call | solution.py:492
  (57 shorter events, 0.7 us)
Async XLA Ops:
  0.7 1.0 copy-start.3
  1.7 0.9 copy-start.4
  3.2 1.5 %collective-permute-start = (f32[2,96,256]{2,1,0:T(8,128)S(1)}, f32[2,96,256]{2,1,0:T(8,128)S(1)}, u32[]{:S(2)}, u32[]{:S(2)}) collective-permute-start(f32[2,96,256]{2,1,0:T(8,128)S(1)} %get-tuple-element.37), channel_id=1, source_target_pairs={{0,1},{1,0},{2,3},{3,2},{4,5},{5,4},{6,7},{7,6},{8,9},{9,8},{10,11... | collective-permute-start | bytes 589832 | tf_op jit(solution)/shard_map/ppermute | solution.py:140
  4.7 7.3 %collective-permute-start.1 = (bf16[2,96,256]{2,1,0:T(8,128)(2,1)S(1)}, bf16[2,96,256]{2,1,0:T(8,128)(2,1)S(1)}, u32[]{:S(2)}, u32[]{:S(2)}) collective-permute-start(bf16[2,96,256]{2,1,0:T(8,128)(2,1)S(1)} %get-tuple-element.39), channel_id=1, source_target_pairs={{0,4},{1,5},{2,6},{3,7},{4,0},{5,1},{6,2},{7,3},{8,12},{9,13},{10,... | collective-permute-start | bytes 294920 | tf_op jit(solution)/shard_map/ppermute | solution.py:140
  8.2 1.6 %copy-start.1 = (bf16[1024,1024]{1,0:T(8,128)(2,1)S(1)}, bf16[1024,1024]{1,0:T(8,128)(2,1)}, u32[]{:S(2)}) copy-start(bf16[1024,1024]{1,0:T(8,128)(2,1)} %x_ref) | copy-start | bytes 6291460
  9.7 2.2 %copy-start.2 = (bf16[1024,1024]{1,0:T(8,128)(2,1)S(1)}, bf16[1024,1024]{1,0:T(8,128)(2,1)}, u32[]{:S(2)}) copy-start(bf16[1024,1024]{1,0:T(8,128)(2,1)} %x_ref.1) | copy-start | bytes 6291460
  11.3 24.5 %collective-permute-start.10 = (bf16[1024,512]{1,0:T(8,128)(2,1)S(1)}, bf16[1024,512]{1,0:T(8,128)(2,1)S(1)}, u32[]{:S(2)}, u32[]{:S(2)}) collective-permute-start(bf16[1024,512]{1,0:T(8,128)(2,1)S(1)} %get-tuple-element.44), channel_id=1, source_target_pairs={{0,1},{1,0},{2,3},{3,2},{4,5},{5,4},{6,7},{7,6},{8,9},{9,8},{10,11... | collective-permute-start | bytes 3145736 | tf_op jit(solution)/shard_map/ppermute | solution.py:140
  14.6 21.4 %collective-permute-start.11 = (bf16[1024,512]{1,0:T(8,128)(2,1)S(1)}, bf16[1024,512]{1,0:T(8,128)(2,1)S(1)}, u32[]{:S(2)}, u32[]{:S(2)}) collective-permute-start(bf16[1024,512]{1,0:T(8,128)(2,1)S(1)} %get-tuple-element.45), channel_id=1, source_target_pairs={{0,1},{1,0},{2,3},{3,2},{4,5},{5,4},{6,7},{7,6},{8,9},{9,8},{10,11... | collective-permute-start | bytes 3145736 | tf_op jit(solution)/shard_map/ppermute | solution.py:140
  14.7 9.8 %collective-permute-start.3 = (bf16[2,96,256]{2,1,0:T(8,128)(2,1)S(1)}, bf16[2,96,256]{2,1,0:T(8,128)(2,1)S(1)}, u32[]{:S(2)}, u32[]{:S(2)}) collective-permute-start(bf16[2,96,256]{2,1,0:T(8,128)(2,1)S(1)} %get-tuple-element.39), channel_id=1, source_target_pairs={{0,8},{1,9},{2,10},{3,11},{4,12},{5,13},{6,14},{7,15},{8,0},{9,1},... | collective-permute-start | bytes 294920 | tf_op jit(solution)/shard_map/ppermute | solution.py:140
  17.1 7.4 %collective-permute-start.4 = (bf16[2,96,256]{2,1,0:T(8,128)(2,1)S(1)}, bf16[2,96,256]{2,1,0:T(8,128)(2,1)S(1)}, u32[]{:S(2)}, u32[]{:S(2)}) collective-permute-start(bf16[2,96,256]{2,1,0:T(8,128)(2,1)S(1)} %get-tuple-element.39), channel_id=1, source_target_pairs={{0,12},{1,13},{2,14},{3,15},{4,8},{5,9},{6,10},{7,11},{8,4},{9,5},... | collective-permute-start | bytes 294920 | tf_op jit(solution)/shard_map/ppermute | solution.py:140
  24.5 5.8 %collective-permute-start.8 = (bf16[2,2,96,256]{3,2,1,0:T(8,128)(2,1)S(1)}, bf16[2,2,96,256]{3,2,1,0:T(8,128)(2,1)S(1)}, u32[]{:S(2)}, u32[]{:S(2)}) collective-permute-start(bf16[2,2,96,256]{3,2,1,0:T(8,128)(2,1)S(1)} %pad_maximum_fusion.1.near_high), channel_id=1, source_target_pairs={{0,2},{1,3},{2,0},{3,1},{4,6},{5,7},{6,4},{7,5},{8,10},{9,11},{10,... | collective-permute-start | bytes 589832 | tf_op jit(solution)/shard_map/ppermute | solution.py:140
  25.9 8.6 %collective-permute-start.6 = (bf16[2,2,96,256]{3,2,1,0:T(8,128)(2,1)S(1)}, bf16[2,2,96,256]{3,2,1,0:T(8,128)(2,1)S(1)}, u32[]{:S(2)}, u32[]{:S(2)}) collective-permute-start(bf16[2,2,96,256]{3,2,1,0:T(8,128)(2,1)S(1)} %pad_maximum_fusion.near_low), channel_id=1, source_target_pairs={{0,2},{1,3},{2,0},{3,1},{4,6},{5,7},{6,4},{7,5},{8,10},{9,11},{10,... | collective-permute-start | bytes 589832 | tf_op jit(solution)/shard_map/ppermute | solution.py:140
  26.2 16.9 %collective-permute-start.5 = (bf16[2,2,96,256]{3,2,1,0:T(8,128)(2,1)S(1)}, bf16[2,2,96,256]{3,2,1,0:T(8,128)(2,1)S(1)}, u32[]{:S(2)}, u32[]{:S(2)}) collective-permute-start(bf16[2,2,96,256]{3,2,1,0:T(8,128)(2,1)S(1)} %pad_maximum_fusion.1.near_high), channel_id=1, source_target_pairs={{0,16},{16,0},{1,17},{17,1},{2,18},{18,2},{3,19},{19,3},{4,20},{20... | collective-permute-start | bytes 589832 | tf_op jit(solution)/shard_map/ppermute | solution.py:144
  30.3 13.0 %collective-permute-start.2 = (bf16[2,2,96,256]{3,2,1,0:T(8,128)(2,1)S(1)}, bf16[2,2,96,256]{3,2,1,0:T(8,128)(2,1)S(1)}, u32[]{:S(2)}, u32[]{:S(2)}) collective-permute-start(bf16[2,2,96,256]{3,2,1,0:T(8,128)(2,1)S(1)} %pad_maximum_fusion.near_low), channel_id=1, source_target_pairs={{0,16},{16,0},{1,17},{17,1},{2,18},{18,2},{3,19},{19,3},{4,20},{20... | collective-permute-start | bytes 589832 | tf_op jit(solution)/shard_map/ppermute | solution.py:144
  34.5 8.8 %collective-permute-start.9 = (bf16[2,2,96,256]{3,2,1,0:T(8,128)(2,1)S(1)}, bf16[2,2,96,256]{3,2,1,0:T(8,128)(2,1)S(1)}, u32[]{:S(2)}, u32[]{:S(2)}) collective-permute-start(bf16[2,2,96,256]{3,2,1,0:T(8,128)(2,1)S(1)} %collective-permute-done.8.far_high), channel_id=1, source_target_pairs={{0,16},{16,0},{1,17},{17,1},{2,18},{18,2},{3,19},{19,3},{4,20},{20... | collective-permute-start | bytes 589832 | tf_op jit(solution)/shard_map/ppermute | solution.py:144
  35.8 9.9 %collective-permute-start.7 = (bf16[2,2,96,256]{3,2,1,0:T(8,128)(2,1)S(1)}, bf16[2,2,96,256]{3,2,1,0:T(8,128)(2,1)S(1)}, u32[]{:S(2)}, u32[]{:S(2)}) collective-permute-start(bf16[2,2,96,256]{3,2,1,0:T(8,128)(2,1)S(1)} %collective-permute-done.6.far_low), channel_id=1, source_target_pairs={{0,16},{16,0},{1,17},{17,1},{2,18},{18,2},{3,19},{19,3},{4,20},{20... | collective-permute-start | bytes 589832 | tf_op jit(solution)/shard_map/ppermute | solution.py:144
  41.7 11.4 %collective-permute-start.26 = (bf16[2,2,96,256]{3,2,1,0:T(8,128)(2,1)S(1)}, bf16[2,2,96,256]{3,2,1,0:T(8,128)(2,1)S(1)}, u32[]{:S(2)}, u32[]{:S(2)}) collective-permute-start(bf16[2,2,96,256]{3,2,1,0:T(8,128)(2,1)S(1)} %get-tuple-element.59), channel_id=1, source_target_pairs={{0,2},{1,3},{2,0},{3,1},{4,6},{5,7},{6,4},{7,5},{8,10},{9,11},{10,... | collective-permute-start | bytes 589832 | tf_op jit(solution)/shard_map/ppermute | solution.py:140
  43.1 14.5 %collective-permute-start.24 = (bf16[2,2,96,256]{3,2,1,0:T(8,128)(2,1)S(1)}, bf16[2,2,96,256]{3,2,1,0:T(8,128)(2,1)S(1)}, u32[]{:S(2)}, u32[]{:S(2)}) collective-permute-start(bf16[2,2,96,256]{3,2,1,0:T(8,128)(2,1)S(1)} %get-tuple-element.56), channel_id=1, source_target_pairs={{0,2},{1,3},{2,0},{3,1},{4,6},{5,7},{6,4},{7,5},{8,10},{9,11},{10,... | collective-permute-start | bytes 589832 | tf_op jit(solution)/shard_map/ppermute | solution.py:140
  51.6 6.1 %collective-permute-start.14 = (bf16[2,2,96,256]{3,2,1,0:T(8,128)(2,1)S(1)}, bf16[2,2,96,256]{3,2,1,0:T(8,128)(2,1)S(1)}, u32[]{:S(2)}, u32[]{:S(2)}) collective-permute-start(bf16[2,2,96,256]{3,2,1,0:T(8,128)(2,1)S(1)} %get-tuple-element.50), channel_id=1, source_target_pairs={{0,2},{1,3},{2,0},{3,1},{4,6},{5,7},{6,4},{7,5},{8,10},{9,11},{10,... | collective-permute-start | bytes 589832 | tf_op jit(solution)/shard_map/ppermute | solution.py:140
  52.9 7.7 %collective-permute-start.12 = (bf16[2,2,96,256]{3,2,1,0:T(8,128)(2,1)S(1)}, bf16[2,2,96,256]{3,2,1,0:T(8,128)(2,1)S(1)}, u32[]{:S(2)}, u32[]{:S(2)}) collective-permute-start(bf16[2,2,96,256]{3,2,1,0:T(8,128)(2,1)S(1)} %get-tuple-element.47), channel_id=1, source_target_pairs={{0,2},{1,3},{2,0},{3,1},{4,6},{5,7},{6,4},{7,5},{8,10},{9,11},{10,... | collective-permute-start | bytes 589832 | tf_op jit(solution)/shard_map/ppermute | solution.py:140
  53.2 8.3 %collective-permute-start.27 = (bf16[2,96,256]{2,1,0:T(8,128)(2,1)S(1)}, bf16[2,96,256]{2,1,0:T(8,128)(2,1)S(1)}, u32[]{:S(2)}, u32[]{:S(2)}) collective-permute-start(bf16[2,96,256]{2,1,0:T(8,128)(2,1)S(1)} %get-tuple-element.60), channel_id=1, source_target_pairs={{0,8},{1,9},{2,10},{3,11},{4,12},{5,13},{6,14},{7,15},{8,0},{9,1},... | collective-permute-start | bytes 294920 | tf_op jit(solution)/shard_map/ppermute | solution.py:140
  55.9 7.2 %collective-permute-start.28 = (bf16[2,96,256]{2,1,0:T(8,128)(2,1)S(1)}, bf16[2,96,256]{2,1,0:T(8,128)(2,1)S(1)}, u32[]{:S(2)}, u32[]{:S(2)}) collective-permute-start(bf16[2,96,256]{2,1,0:T(8,128)(2,1)S(1)} %get-tuple-element.61), channel_id=1, source_target_pairs={{0,12},{1,13},{2,14},{3,15},{4,8},{5,9},{6,10},{7,11},{8,4},{9,5},... | collective-permute-start | bytes 294920 | tf_op jit(solution)/shard_map/ppermute | solution.py:140
  57.6 5.9 %collective-permute-start.25 = (bf16[2,96,256]{2,1,0:T(8,128)(2,1)S(1)}, bf16[2,96,256]{2,1,0:T(8,128)(2,1)S(1)}, u32[]{:S(2)}, u32[]{:S(2)}) collective-permute-start(bf16[2,96,256]{2,1,0:T(8,128)(2,1)S(1)} %get-tuple-element.58), channel_id=1, source_target_pairs={{0,4},{1,5},{2,6},{3,7},{4,0},{5,1},{6,2},{7,3},{8,12},{9,13},{10,... | collective-permute-start | bytes 294920 | tf_op jit(solution)/shard_map/ppermute | solution.py:140
  57.7 9.9 %collective-permute-start.15 = (bf16[2,96,256]{2,1,0:T(8,128)(2,1)S(1)}, bf16[2,96,256]{2,1,0:T(8,128)(2,1)S(1)}, u32[]{:S(2)}, u32[]{:S(2)}) collective-permute-start(bf16[2,96,256]{2,1,0:T(8,128)(2,1)S(1)} %get-tuple-element.51), channel_id=1, source_target_pairs={{0,8},{1,9},{2,10},{3,11},{4,12},{5,13},{6,14},{7,15},{8,0},{9,1},... | collective-permute-start | bytes 294920 | tf_op jit(solution)/shard_map/ppermute | solution.py:140
  60.6 7.0 %collective-permute-start.16 = (bf16[2,96,256]{2,1,0:T(8,128)(2,1)S(1)}, bf16[2,96,256]{2,1,0:T(8,128)(2,1)S(1)}, u32[]{:S(2)}, u32[]{:S(2)}) collective-permute-start(bf16[2,96,256]{2,1,0:T(8,128)(2,1)S(1)} %get-tuple-element.52), channel_id=1, source_target_pairs={{0,12},{1,13},{2,14},{3,15},{4,8},{5,9},{6,10},{7,11},{8,4},{9,5},... | collective-permute-start | bytes 294920 | tf_op jit(solution)/shard_map/ppermute | solution.py:140
  61.4 35.0 %copy-start = (bf16[1024,1024]{1,0:T(8,128)(2,1)S(1)}, bf16[1024,1024]{1,0:T(8,128)(2,1)}, u32[]{:S(2)}) copy-start(bf16[1024,1024]{1,0:T(8,128)(2,1)} %q_ref.7) | copy-start | bytes 6291460
  61.4 7.1 %collective-permute-start.13 = (bf16[2,96,256]{2,1,0:T(8,128)(2,1)S(1)}, bf16[2,96,256]{2,1,0:T(8,128)(2,1)S(1)}, u32[]{:S(2)}, u32[]{:S(2)}) collective-permute-start(bf16[2,96,256]{2,1,0:T(8,128)(2,1)S(1)} %get-tuple-element.49), channel_id=1, source_target_pairs={{0,4},{1,5},{2,6},{3,7},{4,0},{5,1},{6,2},{7,3},{8,12},{9,13},{10,... | collective-permute-start | bytes 294920 | tf_op jit(solution)/shard_map/ppermute | solution.py:140
  63.6 13.2 %collective-permute-start.31 = (bf16[2,96,256]{2,1,0:T(8,128)(2,1)S(1)}, bf16[2,96,256]{2,1,0:T(8,128)(2,1)S(1)}, u32[]{:S(2)}, u32[]{:S(2)}) collective-permute-start(bf16[2,96,256]{2,1,0:T(8,128)(2,1)S(1)} %get-tuple-element.62), channel_id=1, source_target_pairs={{0,8},{1,9},{2,10},{3,11},{4,12},{5,13},{6,14},{7,15},{8,0},{9,1},... | collective-permute-start | bytes 294920 | tf_op jit(solution)/shard_map/ppermute | solution.py:140
  64.5 12.3 %collective-permute-start.32 = (bf16[2,96,256]{2,1,0:T(8,128)(2,1)S(1)}, bf16[2,96,256]{2,1,0:T(8,128)(2,1)S(1)}, u32[]{:S(2)}, u32[]{:S(2)}) collective-permute-start(bf16[2,96,256]{2,1,0:T(8,128)(2,1)S(1)} %get-tuple-element.62), channel_id=1, source_target_pairs={{0,12},{1,13},{2,14},{3,15},{4,8},{5,9},{6,10},{7,11},{8,4},{9,5},... | collective-permute-start | bytes 294920 | tf_op jit(solution)/shard_map/ppermute | solution.py:140
  67.7 10.6 %collective-permute-start.29 = (bf16[2,96,256]{2,1,0:T(8,128)(2,1)S(1)}, bf16[2,96,256]{2,1,0:T(8,128)(2,1)S(1)}, u32[]{:S(2)}, u32[]{:S(2)}) collective-permute-start(bf16[2,96,256]{2,1,0:T(8,128)(2,1)S(1)} %get-tuple-element.62), channel_id=1, source_target_pairs={{0,4},{1,5},{2,6},{3,7},{4,0},{5,1},{6,2},{7,3},{8,12},{9,13},{10,... | collective-permute-start | bytes 294920 | tf_op jit(solution)/shard_map/ppermute | solution.py:140
  68.6 18.0 %collective-permute-start.19 = (bf16[2,96,256]{2,1,0:T(8,128)(2,1)S(1)}, bf16[2,96,256]{2,1,0:T(8,128)(2,1)S(1)}, u32[]{:S(2)}, u32[]{:S(2)}) collective-permute-start(bf16[2,96,256]{2,1,0:T(8,128)(2,1)S(1)} %get-tuple-element.53), channel_id=1, source_target_pairs={{0,8},{1,9},{2,10},{3,11},{4,12},{5,13},{6,14},{7,15},{8,0},{9,1},... | collective-permute-start | bytes 294920 | tf_op jit(solution)/shard_map/ppermute | solution.py:140
  75.2 16.7 %collective-permute-start.20 = (bf16[2,96,256]{2,1,0:T(8,128)(2,1)S(1)}, bf16[2,96,256]{2,1,0:T(8,128)(2,1)S(1)}, u32[]{:S(2)}, u32[]{:S(2)}) collective-permute-start(bf16[2,96,256]{2,1,0:T(8,128)(2,1)S(1)} %get-tuple-element.53), channel_id=1, source_target_pairs={{0,12},{1,13},{2,14},{3,15},{4,8},{5,9},{6,10},{7,11},{8,4},{9,5},... | collective-permute-start | bytes 294920 | tf_op jit(solution)/shard_map/ppermute | solution.py:140
  76.9 16.5 %collective-permute-start.36 = (bf16[2,2,96,256]{3,2,1,0:T(8,128)(2,1)S(1)}, bf16[2,2,96,256]{3,2,1,0:T(8,128)(2,1)S(1)}, u32[]{:S(2)}, u32[]{:S(2)}) collective-permute-start(bf16[2,2,96,256]{3,2,1,0:T(8,128)(2,1)S(1)} %pad_maximum_fusion.5.near_high), channel_id=1, source_target_pairs={{0,2},{1,3},{2,0},{3,1},{4,6},{5,7},{6,4},{7,5},{8,10},{9,11},{10,... | collective-permute-start | bytes 589832 | tf_op jit(solution)/shard_map/ppermute | solution.py:140
  78.3 17.7 %collective-permute-start.34 = (bf16[2,2,96,256]{3,2,1,0:T(8,128)(2,1)S(1)}, bf16[2,2,96,256]{3,2,1,0:T(8,128)(2,1)S(1)}, u32[]{:S(2)}, u32[]{:S(2)}) collective-permute-start(bf16[2,2,96,256]{3,2,1,0:T(8,128)(2,1)S(1)} %pad_maximum_fusion.4.near_low), channel_id=1, source_target_pairs={{0,2},{1,3},{2,0},{3,1},{4,6},{5,7},{6,4},{7,5},{8,10},{9,11},{10,... | collective-permute-start | bytes 589832 | tf_op jit(solution)/shard_map/ppermute | solution.py:140
  78.5 13.5 %collective-permute-start.17 = (bf16[2,96,256]{2,1,0:T(8,128)(2,1)S(1)}, bf16[2,96,256]{2,1,0:T(8,128)(2,1)S(1)}, u32[]{:S(2)}, u32[]{:S(2)}) collective-permute-start(bf16[2,96,256]{2,1,0:T(8,128)(2,1)S(1)} %get-tuple-element.53), channel_id=1, source_target_pairs={{0,4},{1,5},{2,6},{3,7},{4,0},{5,1},{6,2},{7,3},{8,12},{9,13},{10,... | collective-permute-start | bytes 294920 | tf_op jit(solution)/shard_map/ppermute | solution.py:140
  86.7 9.4 %collective-permute-start.33 = (bf16[2,2,96,256]{3,2,1,0:T(8,128)(2,1)S(1)}, bf16[2,2,96,256]{3,2,1,0:T(8,128)(2,1)S(1)}, u32[]{:S(2)}, u32[]{:S(2)}) collective-permute-start(bf16[2,2,96,256]{3,2,1,0:T(8,128)(2,1)S(1)} %pad_maximum_fusion.5.near_high), channel_id=1, source_target_pairs={{0,1},{1,0},{2,3},{3,2},{4,5},{5,4},{6,7},{7,6},{8,9},{9,8},{10,11... | collective-permute-start | bytes 589832 | tf_op jit(solution)/shard_map/ppermute | solution.py:140
  91.9 7.5 %collective-permute-start.30 = (bf16[2,2,96,256]{3,2,1,0:T(8,128)(2,1)S(1)}, bf16[2,2,96,256]{3,2,1,0:T(8,128)(2,1)S(1)}, u32[]{:S(2)}, u32[]{:S(2)}) collective-permute-start(bf16[2,2,96,256]{3,2,1,0:T(8,128)(2,1)S(1)} %pad_maximum_fusion.4.near_low), channel_id=1, source_target_pairs={{0,1},{1,0},{2,3},{3,2},{4,5},{5,4},{6,7},{7,6},{8,9},{9,8},{10,11... | collective-permute-start | bytes 589832 | tf_op jit(solution)/shard_map/ppermute | solution.py:140
  92.1 11.7 %collective-permute-start.23 = (bf16[2,2,96,256]{3,2,1,0:T(8,128)(2,1)S(1)}, bf16[2,2,96,256]{3,2,1,0:T(8,128)(2,1)S(1)}, u32[]{:S(2)}, u32[]{:S(2)}) collective-permute-start(bf16[2,2,96,256]{3,2,1,0:T(8,128)(2,1)S(1)} %pad_maximum_fusion.3.near_high), channel_id=1, source_target_pairs={{0,2},{1,3},{2,0},{3,1},{4,6},{5,7},{6,4},{7,5},{8,10},{9,11},{10,... | collective-permute-start | bytes 589832 | tf_op jit(solution)/shard_map/ppermute | solution.py:140
  93.4 6.7 %collective-permute-start.37 = (bf16[2,2,96,256]{3,2,1,0:T(8,128)(2,1)S(1)}, bf16[2,2,96,256]{3,2,1,0:T(8,128)(2,1)S(1)}, u32[]{:S(2)}, u32[]{:S(2)}) collective-permute-start(bf16[2,2,96,256]{3,2,1,0:T(8,128)(2,1)S(1)} %collective-permute-done.36.far_high), channel_id=1, source_target_pairs={{0,1},{1,0},{2,3},{3,2},{4,5},{5,4},{6,7},{7,6},{8,9},{9,8},{10,11... | collective-permute-start | bytes 589832 | tf_op jit(solution)/shard_map/ppermute | solution.py:140
  96.0 4.2 %collective-permute-start.35 = (bf16[2,2,96,256]{3,2,1,0:T(8,128)(2,1)S(1)}, bf16[2,2,96,256]{3,2,1,0:T(8,128)(2,1)S(1)}, u32[]{:S(2)}, u32[]{:S(2)}) collective-permute-start(bf16[2,2,96,256]{3,2,1,0:T(8,128)(2,1)S(1)} %collective-permute-done.34.far_low), channel_id=1, source_target_pairs={{0,1},{1,0},{2,3},{3,2},{4,5},{5,4},{6,7},{7,6},{8,9},{9,8},{10,11... | collective-permute-start | bytes 589832 | tf_op jit(solution)/shard_map/ppermute | solution.py:140
  96.1 7.6 %collective-permute-start.22 = (bf16[2,2,96,256]{3,2,1,0:T(8,128)(2,1)S(1)}, bf16[2,2,96,256]{3,2,1,0:T(8,128)(2,1)S(1)}, u32[]{:S(2)}, u32[]{:S(2)}) collective-permute-start(bf16[2,2,96,256]{3,2,1,0:T(8,128)(2,1)S(1)} %pad_maximum_fusion.2.near_low), channel_id=1, source_target_pairs={{0,2},{1,3},{2,0},{3,1},{4,6},{5,7},{6,4},{7,5},{8,10},{9,11},{10,... | collective-permute-start | bytes 589832 | tf_op jit(solution)/shard_map/ppermute | solution.py:140
  99.4 4.9 %collective-permute-start.40 = (f32[2,96,256]{2,1,0:T(8,128)S(1)}, f32[2,96,256]{2,1,0:T(8,128)S(1)}, u32[]{:S(2)}, u32[]{:S(2)}) collective-permute-start(f32[2,96,256]{2,1,0:T(8,128)S(1)} %pad_maximum_fusion.6), channel_id=1, source_target_pairs={{0,1},{1,0},{2,3},{3,2},{4,5},{5,4},{6,7},{7,6},{8,9},{9,8},{10,11... | collective-permute-start | bytes 589832 | tf_op jit(solution)/shard_map/ppermute | solution.py:140
  100.2 8.5 %collective-permute-start.21 = (bf16[2,2,96,256]{3,2,1,0:T(8,128)(2,1)S(1)}, bf16[2,2,96,256]{3,2,1,0:T(8,128)(2,1)S(1)}, u32[]{:S(2)}, u32[]{:S(2)}) collective-permute-start(bf16[2,2,96,256]{3,2,1,0:T(8,128)(2,1)S(1)} %pad_maximum_fusion.3.near_high), channel_id=1, source_target_pairs={{0,1},{1,0},{2,3},{3,2},{4,5},{5,4},{6,7},{7,6},{8,9},{9,8},{10,11... | collective-permute-start | bytes 589832 | tf_op jit(solution)/shard_map/ppermute | solution.py:140
  100.2 8.5 %collective-permute-start.18 = (bf16[2,2,96,256]{3,2,1,0:T(8,128)(2,1)S(1)}, bf16[2,2,96,256]{3,2,1,0:T(8,128)(2,1)S(1)}, u32[]{:S(2)}, u32[]{:S(2)}) collective-permute-start(bf16[2,2,96,256]{3,2,1,0:T(8,128)(2,1)S(1)} %pad_maximum_fusion.2.near_low), channel_id=1, source_target_pairs={{0,1},{1,0},{2,3},{3,2},{4,5},{5,4},{6,7},{7,6},{8,9},{9,8},{10,11... | collective-permute-start | bytes 589832 | tf_op jit(solution)/shard_map/ppermute | solution.py:140
  103.7 5.0 %collective-permute-start.38 = (bf16[2,2,96,256]{3,2,1,0:T(8,128)(2,1)S(1)}, bf16[2,2,96,256]{3,2,1,0:T(8,128)(2,1)S(1)}, u32[]{:S(2)}, u32[]{:S(2)}) collective-permute-start(bf16[2,2,96,256]{3,2,1,0:T(8,128)(2,1)S(1)} %collective-permute-done.22.far_low), channel_id=1, source_target_pairs={{0,1},{1,0},{2,3},{3,2},{4,5},{5,4},{6,7},{7,6},{8,9},{9,8},{10,11... | collective-permute-start | bytes 589832 | tf_op jit(solution)/shard_map/ppermute | solution.py:140
  104.3 4.4 %collective-permute-start.39 = (bf16[2,2,96,256]{3,2,1,0:T(8,128)(2,1)S(1)}, bf16[2,2,96,256]{3,2,1,0:T(8,128)(2,1)S(1)}, u32[]{:S(2)}, u32[]{:S(2)}) collective-permute-start(bf16[2,2,96,256]{3,2,1,0:T(8,128)(2,1)S(1)} %collective-permute-done.23.far_high), channel_id=1, source_target_pairs={{0,1},{1,0},{2,3},{3,2},{4,5},{5,4},{6,7},{7,6},{8,9},{9,8},{10,11... | collective-permute-start | bytes 589832 | tf_op jit(solution)/shard_map/ppermute | solution.py:140

commit v3 on v2

--- a/solution.py
+++ b/solution.py
@@ -11,6 +11,7 @@
 BF16 = jnp.bfloat16
 F32 = jnp.float32
 VMEM_LIMIT = 48 * 1024 * 1024
+VMEM_ALL = 63 * 1024 * 1024
 
 
 def rms_rows(matrix):
@@ -148,8 +149,8 @@
     return lax.optimization_barrier((value, before))[0]
 
 
-def compiler_params():
-    return pltpu.CompilerParams(vmem_limit_bytes=VMEM_LIMIT)
+def compiler_params(limit=VMEM_LIMIT):
+    return pltpu.CompilerParams(vmem_limit_bytes=limit)
 
 
 def head_of(ids, order, other):
@@ -161,7 +162,15 @@
     return (wide * lax.rsqrt(jnp.mean(wide * wide, axis=-1, keepdims=True) + 1e-06)).astype(BF16)
 
 
-def pack_kernel(ids, in_ref, out_ref, own, theirs):
+def pack_kernel(ids, in_hbm, out_hbm, own, theirs, in_ref, out_ref, arrived):
+    copies = [
+        pltpu.make_async_copy(in_hbm, in_ref, arrived.at[0]),
+        pltpu.make_async_copy(out_hbm, out_ref, arrived.at[1]),
+    ]
+    for copy in copies:
+        copy.start()
+    for copy in copies:
+        copy.wait()
     size = out_ref.shape[-1]
     rows = in_ref.shape[1]
     for other, ref in ((0, own), (1, theirs)):
@@ -179,9 +188,14 @@
     shape = jax.ShapeDtypeStruct((2, rows, fast_out.shape[2]), F32)
     return pl.pallas_call(
         pack_kernel,
-        in_specs=[pl.BlockSpec(memory_space=pltpu.SMEM)] + [pl.BlockSpec(memory_space=pltpu.VMEM)] * 2,
+        in_specs=[pl.BlockSpec(memory_space=pltpu.SMEM)] + [pl.BlockSpec(memory_space=pltpu.HBM)] * 2,
         out_shape=[shape, shape],
-        compiler_params=compiler_params(),
+        scratch_shapes=[
+            pltpu.VMEM(fast_in.shape, F32),
+            pltpu.VMEM(fast_out.shape, F32),
+            pltpu.SemaphoreType.DMA((2,)),
+        ],
+        compiler_params=compiler_params(VMEM_ALL),
         name="pack",
     )(ids, fast_in, fast_out)
 
@@ -244,9 +258,9 @@
             out_specs=[narrow] * 2,
         ),
         out_shape=[shape] * 2,
-        compiler_params=compiler_params(),
+        compiler_params=compiler_params(VMEM_ALL),
         cost_estimate=pl.CostEstimate(
-            flops=rows, bytes_accessed=rows, transcendentals=0
+            flops=rows * width * 5, bytes_accessed=rows * width * 4, transcendentals=0
         ),
         name=name,
     )(ids, *operands)
@@ -533,6 +547,14 @@
     )(ids, one, two, came)
 
 
+def gather_chips(shard):
+    z1, z3, z2 = swap(shard, 4), swap(shard, 12), swap(shard, 8)
+    near_low, near_high = jnp.stack([shard, z1]), jnp.stack([z2, z3])
+    far_low = swap(near_low, 2)
+    near_high = after(near_high, far_low)
+    return near_low, near_high, far_low, swap(near_high, 2)
+
+
 def per_device_cube(queries, keys, values, step_size, fast_in, fast_out):
     rows = keys.shape[0]
     heads = fast_in.shape[0]
@@ -544,17 +566,14 @@
 
     own, theirs = pack(ids, fast_in, fast_out)
     got = swap(theirs, 1)
+    later = after(ids, own)
+    k_own, k_send = prepare(later, keys, None, heads, "keys")
+    v_own, v_send = prepare(later, values, (step_size * block_root).T, heads, "values")
+    got = after(got, k_send, v_send)
     master_one, master_two, shard = pair(own, got)
     masters = (master_one, master_two)
-    z1, z2, z3 = swap(shard, 4), swap(shard, 8), swap(shard, 12)
-    near_low = jnp.stack([shard, z1])
-    near_high = jnp.stack([z2, z3])
-    far_low, far_high = swap(near_low, 2), swap(near_high, 2)
-    first = (near_low, near_high, far_low, far_high)
+    first = gather_chips(shard)
     second = tuple(swap_parts(piece) for piece in first)
-
-    k_own, k_send = prepare(ids, after(keys, shard), None, heads, "keys")
-    v_own, v_send = prepare(ids, after(values, z1), step_size.T * block_root, heads, "values")
     k_got, v_got = swap(k_send, 1), swap(v_send, 1)
 
     kept, low, high = [], [], []
@@ -572,19 +591,19 @@
         wide.append(a)
         short.append(b)
 
-    output = None
-    for order in range(2):
-        shard = short[order]
-        z3, z2, z1 = swap(shard, 12), swap(shard, 8), swap(shard, 4)
-        near_low = jnp.stack([shard, z1])
-        near_high = jnp.stack([z2, z3])
-        far = (swap(near_low, 2), swap(near_high, 2))
-        if order:
-            far = after(far, output)
-        mine = (near_low, near_high, *far)
-        others = tuple(swap(piece, 1) for piece in mine)
-        output = apply_fast(ids, order, 0, mine, queries, output, fast)
-        output = apply_fast(ids, order, 1, others, queries, output, fast)
+    lines = [gather_chips(shard) for shard in short]
+    near_low, near_high, far_low, far_high = lines[0]
+    far_low, far_high = after((far_low, far_high), *lines[1][:2])
+    mine = (near_low, near_high, far_low, far_high)
+    others = tuple(swap(piece, 1) for piece in mine)
+    output = apply_fast(ids, 0, 0, mine, queries, None, fast)
+    output = apply_fast(ids, 0, 1, others, queries, output, fast)
+    near_low, near_high, far_low, far_high = lines[1]
+    far_high = after(far_high, output)
+    mine = (near_low, near_high, far_low, far_high)
+    others = tuple(swap(piece, 1) for piece in mine)
+    output = apply_fast(ids, 1, 0, mine, queries, output, fast)
+    output = apply_fast(ids, 1, 1, others, queries, output, fast)
 
     came = swap(jnp.stack([wide[0][1], wide[1][1]]), 1)
     return (output, *finish(ids, wide[0], wide[1], came, fast_in, fast_out))

time: 114 us -> 124 us (1.088); the launches traced: 112 us -> 123 us
  Pallas kernels: 30.4 us -> 40.1 us
  starting transfers between devices: 53 us -> 55 us
    pallas_call x2, Pallas kernels: 4.12 us -> 10.1 us  [prepare(): pl.pallas_call(functools.partial(prepare_kernel, heads), grid_spec=pltpu....]
    ppermute x37, starting transfers between devices: 49 us -> 52.1 us  [swap(): lax.ppermute(value, 'tok', [(place, place ^ bits) for place in range(coun...]
    pallas_call x2, Pallas kernels: 11.7 us -> 13.6 us  [increments(): pl.pallas_call(increments_kernel, grid_spec=pltpu.PrefetchScalarGridSpec(...]
    pallas_call x1, Pallas kernels: 0.57 us -> 2.43 us  [pack(): pl.pallas_call(pack_kernel, in_specs=[pl.BlockSpec(memory_space=pltpu.SME...]
    ppermute x4, waiting for transfers between devices: 2.34 us -> 0.95 us  [swap_parts(): return lax.ppermute(value, 'parts', [(0, 1), (1, 0)])]
    unnamed x10 -> x12, local copies, waits for them, and re-layouts: 3.46 us -> 2.47 us
  transfers between devices with their start and end apart: 41 -> 41, of which waited for: 10 -> 10; matrix products, arithmetic and copies ran while one was open for 1% -> 0% of each run, Pallas kernels for 24% -> 24%
where the time goes in v3:
time: 124 us; the launch traced here: 123 us
  starting transfers between devices  55 us (44%)
  Pallas kernels  40.1 us (32%)
  waiting for transfers between devices  22.3 us (18%)
  local copies, waits for them, and re-layouts  3.51 us (3%)
  other arithmetic  1.45 us (1%)
    ppermute x37, starting transfers between devices, swap(): lax.ppermute(value, 'tok', [(place, place ^ bits) for place in range(coun...  52.1 us
    ppermute x37, waiting for transfers between devices, swap(): lax.ppermute(value, 'tok', [(place, place ^ bits) for place in range(coun...  21.3 us
    pallas_call x2, Pallas kernels, increments(): pl.pallas_call(increments_kernel, grid_spec=pltpu.PrefetchScalarGridSpec(...  13.6 us
    pallas_call x4, Pallas kernels, apply_fast(): pl.pallas_call(functools.partial(apply_kernel, other), grid_spec=pltpu.Pr...  12.2 us
    pallas_call x2, Pallas kernels, prepare(): pl.pallas_call(functools.partial(prepare_kernel, heads), grid_spec=pltpu....  10.1 us
    ppermute x4, starting transfers between devices, swap_parts(): return lax.ppermute(value, 'parts', [(0, 1), (1, 0)])  2.93 us
  transfers between devices with their start and end apart: 41, of which 10 were waited for; matrix products, arithmetic and copies ran while one was open for 0% of the time, Pallas kernels for 24%

profile of v3, /device:TPU:1, one launch (start us, length us, event | category | flops | bytes accessed | tf_op | source)
XLA Modules:
  0.0 123.2 jit_solution(1624859284152404850)
XLA Ops:
  0.6 0.6 pad_add_fusion.ids
  1.2 2.4 %pack.1 = (f32[2,96,256]{2,1,0:T(8,128)}, f32[2,96,256]{2,1,0:T(8,128)}) custom-call(s32[3]{0:T(128)} %pad_add_fusion.ids, f32[4,16,1024]{2,1,0:T(8,128)} %in_hbm.1, f32[4,32,256]{2,1,0:T(8,128)} %out_hbm.1), custom_call_target="tpu_custom_call" | custom-call | tf_op jit(solution)/shard_map/pack/pallas_call | solution.py:189
  3.7 0.7 broadcast_multiply_fusion
  4.4 1.0 copy.14
  5.4 5.4 %values.1 = (bf16[1024,512]{1,0:T(8,128)(2,1)}, bf16[1024,512]{1,0:T(8,128)(2,1)}) custom-call(s32[3]{0:T(128)} %pad_add_fusion.ids, bf16[1024,1024]{1,0:T(8,128)(2,1)} %x_ref.3, f32[1024,4]{1,0:T(8,128)} %bitcast.19), custom_call_target="tpu_custom_call" | custom-call | flops 5242880 | bytes 4194304 | tf_op jit(solution)/shard_map/values/pallas_call | solution.py:252
  10.9 4.7 %keys.1 = (bf16[1024,512]{1,0:T(8,128)(2,1)}, bf16[1024,512]{1,0:T(8,128)(2,1)}) custom-call(s32[3]{0:T(128)} %pad_add_fusion.ids, bf16[1024,1024]{1,0:T(8,128)(2,1)} %x_ref.2), custom_call_target="tpu_custom_call" | custom-call | flops 5242880 | bytes 4194304 | tf_op jit(solution)/shard_map/keys/pallas_call | solution.py:252
  15.6 0.4 collective-permute-start.10
  16.0 0.1 collective-permute-start
  16.1 2.4 %collective-permute-done.got = f32[2,96,256]{2,1,0:T(8,128)S(1)} collective-permute-done((f32[2,96,256]{2,1,0:T(8,128)S(1)}, f32[2,96,256]{2,1,0:T(8,128)S(1)}, u32[]{:S(2)}, u32[]{:S(2)}) %collective-permute-start) | collective-permute-done | bytes 196640 | tf_op jit(solution)/shard_map/ppermute | solution.py:141
  18.6 2.5 %collective-permute-start.1 = (bf16[2,96,256]{2,1,0:T(8,128)(2,1)S(1)}, bf16[2,96,256]{2,1,0:T(8,128)(2,1)S(1)}, u32[]{:S(2)}, u32[]{:S(2)}) collective-permute-start(bf16[2,96,256]{2,1,0:T(8,128)(2,1)S(1)} %get-tuple-element.47), channel_id=1, source_target_pairs={{0,4},{1,5},{2,6},{3,7},{4,0},{5,1},{6,2},{7,3},{8,12},{9,13},{10,... | collective-permute-start | bytes 294920 | tf_op jit(solution)/shard_map/ppermute | solution.py:141
  21.1 2.3 %collective-permute-start.3 = (bf16[2,96,256]{2,1,0:T(8,128)(2,1)S(1)}, bf16[2,96,256]{2,1,0:T(8,128)(2,1)S(1)}, u32[]{:S(2)}, u32[]{:S(2)}) collective-permute-start(bf16[2,96,256]{2,1,0:T(8,128)(2,1)S(1)} %get-tuple-element.47), channel_id=1, source_target_pairs={{0,8},{1,9},{2,10},{3,11},{4,12},{5,13},{6,14},{7,15},{8,0},{9,1},... | collective-permute-start | bytes 294920 | tf_op jit(solution)/shard_map/ppermute | solution.py:141
  23.4 0.6 collective-permute-done.1
  24.0 1.2 collective-permute-start.5
  25.1 0.3 collective-permute-done.3
  25.4 4.6 %collective-permute-done.4 = bf16[2,96,256]{2,1,0:T(8,128)(2,1)S(1)} collective-permute-done((bf16[2,96,256]{2,1,0:T(8,128)(2,1)S(1)}, bf16[2,96,256]{2,1,0:T(8,128)(2,1)S(1)}, u32[]{:S(2)}, u32[]{:S(2)}) %collective-permute-start.4) | collective-permute-done | bytes 98336 | tf_op jit(solution)/shard_map/ppermute | solution.py:141
  30.1 1.3 %collective-permute-start.8 = (bf16[2,2,96,256]{3,2,1,0:T(8,128)(2,1)S(1)}, bf16[2,2,96,256]{3,2,1,0:T(8,128)(2,1)S(1)}, u32[]{:S(2)}, u32[]{:S(2)}) collective-permute-start(bf16[2,2,96,256]{3,2,1,0:T(8,128)(2,1)S(1)} %pad_maximum_fusion.1.near_high), channel_id=1, source_target_pairs={{0,2},{1,3},{2,0},{3,1},{4,6},{5,7},{6,4},{7,5},{8,10},{9,11},{10,... | collective-permute-start | bytes 589832 | tf_op jit(solution)/shard_map/ppermute | solution.py:141
  31.4 1.2 collective-permute-start.2
  32.6 0.3 collective-permute-start.6
  32.9 1.8 %collective-permute-done.8.far_high = bf16[2,2,96,256]{3,2,1,0:T(8,128)(2,1)S(1)} collective-permute-done((bf16[2,2,96,256]{3,2,1,0:T(8,128)(2,1)S(1)}, bf16[2,2,96,256]{3,2,1,0:T(8,128)(2,1)S(1)}, u32[]{:S(2)}, u32[]{:S(2)}) %collective-permute-start.8) | collective-permute-done | bytes 196640 | tf_op jit(solution)/shard_map/ppermute | solution.py:141
  34.7 1.2 collective-permute-start.7
  35.9 0.3 collective-permute-start.9
  36.2 1.2 copy-done.3
  37.4 1.2 copy-done.4
  38.6 6.7 %increments.3 = (f32[4,2,96,256]{3,2,1,0:T(8,128)S(1)}, bf16[2,2,96,256]{3,2,1,0:T(8,128)(2,1)S(1)}, bf16[2,2,96,256]{3,2,1,0:T(8,128)(2,1)S(1)}) custom-call(s32[3]{0:T(128)S(1)} %copy-done.2, bf16[2,2,96,256]{3,2,1,0:T(8,128)(2,1)S(1)} %pad_maximum_fusion.near_low, bf16[2,2,96,256]{3,2,1,0:T(8,128)(2,1)S(1)} %pad_maximum_fusion.1.near_high, ...), custom_call_target="tpu_custom_call" | custom-call | flops 3221225472 | bytes 2097152 | tf_op jit(solution)/shard_map/increments/pallas_call | solution.py:384
  45.3 1.3 %collective-permute-start.27 = (bf16[2,2,96,256]{3,2,1,0:T(8,128)(2,1)S(1)}, bf16[2,2,96,256]{3,2,1,0:T(8,128)(2,1)S(1)}, u32[]{:S(2)}, u32[]{:S(2)}) collective-permute-start(bf16[2,2,96,256]{3,2,1,0:T(8,128)(2,1)S(1)} %get-tuple-element.65), channel_id=1, source_target_pairs={{0,2},{1,3},{2,0},{3,1},{4,6},{5,7},{6,4},{7,5},{8,10},{9,11},{10,... | collective-permute-start | bytes 589832 | tf_op jit(solution)/shard_map/ppermute | solution.py:141
  46.6 0.2 collective-permute-start.25
  46.9 0.9 collective-permute-done.9.far_high
  47.8 6.9 %increments.2 = (f32[4,2,96,256]{3,2,1,0:T(8,128)S(1)}, bf16[2,2,96,256]{3,2,1,0:T(8,128)(2,1)S(1)}, bf16[2,2,96,256]{3,2,1,0:T(8,128)(2,1)S(1)}) custom-call(s32[3]{0:T(128)S(1)} %copy-done.2, bf16[2,2,96,256]{3,2,1,0:T(8,128)(2,1)S(1)} %collective-permute-done.2.near_low, bf16[2,2,96,256]{3,2,1,0:T(8,128)(2,1)S(1)} %collective-permute-done.6.near_high, ...), custom_call_target="tpu_custom_call" | custom-call | flops 3221225472 | bytes 2097152 | tf_op jit(solution)/shard_map/increments/pallas_call | solution.py:384
  54.7 0.4 collective-permute-start.14
  55.1 1.2 collective-permute-start.12
  56.3 4.3 %collective-permute-start.28 = (bf16[2,96,256]{2,1,0:T(8,128)(2,1)S(1)}, bf16[2,96,256]{2,1,0:T(8,128)(2,1)S(1)}, u32[]{:S(2)}, u32[]{:S(2)}) collective-permute-start(bf16[2,96,256]{2,1,0:T(8,128)(2,1)S(1)} %get-tuple-element.66), channel_id=1, source_target_pairs={{0,8},{1,9},{2,10},{3,11},{4,12},{5,13},{6,14},{7,15},{8,0},{9,1},... | collective-permute-start | bytes 294920 | tf_op jit(solution)/shard_map/ppermute | solution.py:141
  60.6 1.3 %collective-permute-start.29 = (bf16[2,96,256]{2,1,0:T(8,128)(2,1)S(1)}, bf16[2,96,256]{2,1,0:T(8,128)(2,1)S(1)}, u32[]{:S(2)}, u32[]{:S(2)}) collective-permute-start(bf16[2,96,256]{2,1,0:T(8,128)(2,1)S(1)} %get-tuple-element.67), channel_id=1, source_target_pairs={{0,12},{1,13},{2,14},{3,15},{4,8},{5,9},{6,10},{7,11},{8,4},{9,5},... | collective-permute-start | bytes 294920 | tf_op jit(solution)/shard_map/ppermute | solution.py:141
  61.9 0.1 collective-permute-start.26
  62.1 2.3 %collective-permute-start.15 = (bf16[2,96,256]{2,1,0:T(8,128)(2,1)S(1)}, bf16[2,96,256]{2,1,0:T(8,128)(2,1)S(1)}, u32[]{:S(2)}, u32[]{:S(2)}) collective-permute-start(bf16[2,96,256]{2,1,0:T(8,128)(2,1)S(1)} %get-tuple-element.56), channel_id=1, source_target_pairs={{0,8},{1,9},{2,10},{3,11},{4,12},{5,13},{6,14},{7,15},{8,0},{9,1},... | collective-permute-start | bytes 294920 | tf_op jit(solution)/shard_map/ppermute | solution.py:141
  64.3 1.3 %collective-permute-start.16 = (bf16[2,96,256]{2,1,0:T(8,128)(2,1)S(1)}, bf16[2,96,256]{2,1,0:T(8,128)(2,1)S(1)}, u32[]{:S(2)}, u32[]{:S(2)}) collective-permute-start(bf16[2,96,256]{2,1,0:T(8,128)(2,1)S(1)} %get-tuple-element.57), channel_id=1, source_target_pairs={{0,12},{1,13},{2,14},{3,15},{4,8},{5,9},{6,10},{7,11},{8,4},{9,5},... | collective-permute-start | bytes 294920 | tf_op jit(solution)/shard_map/ppermute | solution.py:141
  65.7 1.6 %collective-permute-start.13 = (bf16[2,96,256]{2,1,0:T(8,128)(2,1)S(1)}, bf16[2,96,256]{2,1,0:T(8,128)(2,1)S(1)}, u32[]{:S(2)}, u32[]{:S(2)}) collective-permute-start(bf16[2,96,256]{2,1,0:T(8,128)(2,1)S(1)} %get-tuple-element.54), channel_id=1, source_target_pairs={{0,4},{1,5},{2,6},{3,7},{4,0},{5,1},{6,2},{7,3},{8,12},{9,13},{10,... | collective-permute-start | bytes 294920 | tf_op jit(solution)/shard_map/ppermute | solution.py:141
  67.3 0.6 collective-permute-done.26.one
  67.9 0.1 renorm.3
  68.1 0.1 collective-permute-start.30
  68.1 2.0 %collective-permute-start.32 = (bf16[2,96,256]{2,1,0:T(8,128)(2,1)S(1)}, bf16[2,96,256]{2,1,0:T(8,128)(2,1)S(1)}, u32[]{:S(2)}, u32[]{:S(2)}) collective-permute-start(bf16[2,96,256]{2,1,0:T(8,128)(2,1)S(1)} %get-tuple-element.68), channel_id=1, source_target_pairs={{0,8},{1,9},{2,10},{3,11},{4,12},{5,13},{6,14},{7,15},{8,0},{9,1},... | collective-permute-start | bytes 294920 | tf_op jit(solution)/shard_map/ppermute | solution.py:141
  70.2 2.3 %collective-permute-done.15.two = bf16[2,96,256]{2,1,0:T(8,128)(2,1)S(1)} collective-permute-done((bf16[2,96,256]{2,1,0:T(8,128)(2,1)S(1)}, bf16[2,96,256]{2,1,0:T(8,128)(2,1)S(1)}, u32[]{:S(2)}, u32[]{:S(2)}) %collective-permute-start.15) | collective-permute-done | bytes 98336 | tf_op jit(solution)/shard_map/ppermute | solution.py:141
  72.5 1.4 %collective-permute-start.33 = (bf16[2,96,256]{2,1,0:T(8,128)(2,1)S(1)}, bf16[2,96,256]{2,1,0:T(8,128)(2,1)S(1)}, u32[]{:S(2)}, u32[]{:S(2)}) collective-permute-start(bf16[2,96,256]{2,1,0:T(8,128)(2,1)S(1)} %get-tuple-element.68), channel_id=1, source_target_pairs={{0,12},{1,13},{2,14},{3,15},{4,8},{5,9},{6,10},{7,11},{8,4},{9,5},... | collective-permute-start | bytes 294920 | tf_op jit(solution)/shard_map/ppermute | solution.py:141
  73.9 0.1 renorm.2
  74.0 2.1 %collective-permute-start.19 = (bf16[2,96,256]{2,1,0:T(8,128)(2,1)S(1)}, bf16[2,96,256]{2,1,0:T(8,128)(2,1)S(1)}, u32[]{:S(2)}, u32[]{:S(2)}) collective-permute-start(bf16[2,96,256]{2,1,0:T(8,128)(2,1)S(1)} %get-tuple-element.58), channel_id=1, source_target_pairs={{0,8},{1,9},{2,10},{3,11},{4,12},{5,13},{6,14},{7,15},{8,0},{9,1},... | collective-permute-start | bytes 294920 | tf_op jit(solution)/shard_map/ppermute | solution.py:141
  76.2 2.3 %collective-permute-start.20 = (bf16[2,96,256]{2,1,0:T(8,128)(2,1)S(1)}, bf16[2,96,256]{2,1,0:T(8,128)(2,1)S(1)}, u32[]{:S(2)}, u32[]{:S(2)}) collective-permute-start(bf16[2,96,256]{2,1,0:T(8,128)(2,1)S(1)} %get-tuple-element.58), channel_id=1, source_target_pairs={{0,12},{1,13},{2,14},{3,15},{4,8},{5,9},{6,10},{7,11},{8,4},{9,5},... | collective-permute-start | bytes 294920 | tf_op jit(solution)/shard_map/ppermute | solution.py:141
  78.5 5.4 %collective-permute-done.17 = bf16[2,96,256]{2,1,0:T(8,128)(2,1)S(1)} collective-permute-done((bf16[2,96,256]{2,1,0:T(8,128)(2,1)S(1)}, bf16[2,96,256]{2,1,0:T(8,128)(2,1)S(1)}, u32[]{:S(2)}, u32[]{:S(2)}) %collective-permute-start.17) | collective-permute-done | bytes 98336 | tf_op jit(solution)/shard_map/ppermute | solution.py:141
  83.9 0.5 collective-permute-start.34
  84.4 1.1 collective-permute-start.21
  85.5 3.2 %collective-permute-done.34.far_low = bf16[2,2,96,256]{3,2,1,0:T(8,128)(2,1)S(1)} collective-permute-done((bf16[2,2,96,256]{3,2,1,0:T(8,128)(2,1)S(1)}, bf16[2,2,96,256]{3,2,1,0:T(8,128)(2,1)S(1)}, u32[]{:S(2)}, u32[]{:S(2)}) %collective-permute-start.34) | collective-permute-done | bytes 196640 | tf_op jit(solution)/shard_map/ppermute | solution.py:141
  88.7 0.5 collective-permute-start.36
  89.2 13.2 %collective-permute-start.31 = (bf16[2,2,96,256]{3,2,1,0:T(8,128)(2,1)S(1)}, bf16[2,2,96,256]{3,2,1,0:T(8,128)(2,1)S(1)}, u32[]{:S(2)}, u32[]{:S(2)}) collective-permute-start(bf16[2,2,96,256]{3,2,1,0:T(8,128)(2,1)S(1)} %pad_maximum_fusion.4.near_low), channel_id=1, source_target_pairs={{0,1},{1,0},{2,3},{3,2},{4,5},{5,4},{6,7},{7,6},{8,9},{9,8},{10,11... | collective-permute-start | bytes 589832 | tf_op jit(solution)/shard_map/ppermute | solution.py:141
  102.4 0.1 collective-permute-start.35
  102.5 5.0 %collective-permute-start.37 = (bf16[2,2,96,256]{3,2,1,0:T(8,128)(2,1)S(1)}, bf16[2,2,96,256]{3,2,1,0:T(8,128)(2,1)S(1)}, u32[]{:S(2)}, u32[]{:S(2)}) collective-permute-start(bf16[2,2,96,256]{3,2,1,0:T(8,128)(2,1)S(1)} %collective-permute-done.34.far_low), channel_id=1, source_target_pairs={{0,1},{1,0},{2,3},{3,2},{4,5},{5,4},{6,7},{7,6},{8,9},{9,8},{10,11... | collective-permute-start | bytes 589832 | tf_op jit(solution)/shard_map/ppermute | solution.py:141
  107.6 0.3 collective-permute-start.24
  107.9 3.0 %apply.4.rest_0_ = bf16[1024,1024]{1,0:T(8,128)(2,1)} custom-call(s32[3]{0:T(128)S(1)} %copy-done.2, bf16[2,2,96,256]{3,2,1,0:T(8,128)(2,1)S(1)} %pad_maximum_fusion.4.near_low, bf16[2,2,96,256]{3,2,1,0:T(8,128)(2,1)S(1)} %pad_maximum_fusion.5.near_high, bf16[2,2,96,256]{3,2,1,0:T(8,128)(2,1)S(1)} %collective-permute-done.34.far_low, ...), custom_call_target="tpu_custom_call" | custom-call | flops 805306368 | bytes 1048576 | tf_op jit(solution)/shard_map/apply/pallas_call | solution.py:506
  110.9 0.8 collective-permute-start.40
  111.7 0.1 collective-permute-start.18
  111.8 0.4 collective-permute-start.22
  112.2 0.1 collective-permute-start.23
  112.3 3.0 %apply.5.rest_0_ = bf16[1024,1024]{1,0:T(8,128)(2,1)} custom-call(s32[3]{0:T(128)S(1)} %copy-done.2, bf16[2,2,96,256]{3,2,1,0:T(8,128)(2,1)S(1)} %collective-permute-done.31.near_low, bf16[2,2,96,256]{3,2,1,0:T(8,128)(2,1)S(1)} %collective-permute-done.35.near_high, ...), custom_call_target="tpu_custom_call", output_to_operand_aliasing={{}: (6, {})} | custom-call | flops 805306368 | bytes 1048576 | tf_op jit(solution)/shard_map/apply/pallas_call | solution.py:506
  115.3 0.4 collective-permute-start.39
  115.8 1.3 %finish.1 = (f32[4,16,1024]{2,1,0:T(8,128)}, f32[4,32,256]{2,1,0:T(8,128)}) custom-call(s32[3]{0:T(128)S(1)} %copy-done.2, f32[2,96,256]{2,1,0:T(8,128)S(1)} %get-tuple-element.73.one, f32[2,96,256]{2,1,0:T(8,128)S(1)} %get-tuple-element.74.two, f32[2,96,256]{2,1,0:T(8,128)S(1)} %collective-permute-done.40.came), custom_call_target="tpu_custom_call" | custom-call | tf_op jit(solution)/shard_map/finish/pallas_call | solution.py:538
  117.1 3.0 %apply.6.rest_0_ = bf16[1024,1024]{1,0:T(8,128)(2,1)} custom-call(s32[3]{0:T(128)S(1)} %copy-done.2, bf16[2,2,96,256]{3,2,1,0:T(8,128)(2,1)S(1)} %pad_maximum_fusion.2.near_low, bf16[2,2,96,256]{3,2,1,0:T(8,128)(2,1)S(1)} %pad_maximum_fusion.3.near_high, bf16[2,2,96,256]{3,2,1,0:T(8,128)(2,1)S(1)} %collective-permute-done.21.far_low, ...), custom_call_target="tpu_custom_call", output_to_operand_aliasing={{}: (6, {})} | custom-call | flops 805306368 | bytes 1048576 | tf_op jit(solution)/shard_map/apply/pallas_call | solution.py:506
  120.2 3.0 %apply.7 = bf16[1024,1024]{1,0:T(8,128)(2,1)} custom-call(s32[3]{0:T(128)S(1)} %copy-done.2, bf16[2,2,96,256]{3,2,1,0:T(8,128)(2,1)S(1)} %collective-permute-done.18.near_low, bf16[2,2,96,256]{3,2,1,0:T(8,128)(2,1)S(1)} %collective-permute-done.22.near_high, ...), custom_call_target="tpu_custom_call", output_to_operand_aliasing={{}: (6, {})} | custom-call | flops 805306368 | bytes 1048576 | tf_op jit(solution)/shard_map/apply/pallas_call | solution.py:506
  (59 shorter events, 0.5 us)
Async XLA Ops:
  5.4 10.6 %copy-start.5 = (f32[2,96,256]{2,1,0:T(8,128)S(1)}, f32[2,96,256]{2,1,0:T(8,128)}, u32[]{:S(2)}) copy-start(f32[2,96,256]{2,1,0:T(8,128)} %get-tuple-element.41) | copy-start | bytes 589828
  5.4 13.1 %copy-start.1 = (f32[2,96,256]{2,1,0:T(8,128)S(1)}, f32[2,96,256]{2,1,0:T(8,128)}, u32[]{:S(2)}) copy-start(f32[2,96,256]{2,1,0:T(8,128)} %get-tuple-element.40.own) | copy-start | bytes 589828
  10.9 25.3 %copy-start.2 = (s32[3]{0:T(128)S(1)}, s32[3]{0:T(128)}, u32[]{:S(2)}) copy-start(s32[3]{0:T(128)} %pad_add_fusion.ids) | copy-start | bytes 40
  10.9 25.0 %collective-permute-start.11 = (bf16[1024,512]{1,0:T(8,128)(2,1)}, bf16[1024,512]{1,0:T(8,128)(2,1)}, u32[]{:S(2)}, u32[]{:S(2)}) collective-permute-start(bf16[1024,512]{1,0:T(8,128)(2,1)} %get-tuple-element.44), channel_id=1, source_target_pairs={{0,1},{1,0},{2,3},{3,2},{4,5},{5,4},{6,7},{7,6},{8,9},{9,8},{10,11... | collective-permute-start | bytes 3145736 | tf_op jit(solution)/shard_map/ppermute | solution.py:141
  15.6 20.6 %collective-permute-start.10 = (bf16[1024,512]{1,0:T(8,128)(2,1)}, bf16[1024,512]{1,0:T(8,128)(2,1)S(1)}, u32[]{:S(2)}, u32[]{:S(2)}) collective-permute-start(bf16[1024,512]{1,0:T(8,128)(2,1)} %get-tuple-element.43), channel_id=1, source_target_pairs={{0,1},{1,0},{2,3},{3,2},{4,5},{5,4},{6,7},{7,6},{8,9},{9,8},{10,11... | collective-permute-start | bytes 3145736 | tf_op jit(solution)/shard_map/ppermute | solution.py:141
  16.0 2.5 %collective-permute-start = (f32[2,96,256]{2,1,0:T(8,128)S(1)}, f32[2,96,256]{2,1,0:T(8,128)S(1)}, u32[]{:S(2)}, u32[]{:S(2)}) collective-permute-start(f32[2,96,256]{2,1,0:T(8,128)S(1)} %copy-done.5), channel_id=1, source_target_pairs={{0,1},{1,0},{2,3},{3,2},{4,5},{5,4},{6,7},{7,6},{8,9},{9,8},{10,11... | collective-permute-start | bytes 589832 | tf_op jit(solution)/shard_map/ppermute | solution.py:141
  18.6 5.4 %collective-permute-start.1 = (bf16[2,96,256]{2,1,0:T(8,128)(2,1)S(1)}, bf16[2,96,256]{2,1,0:T(8,128)(2,1)S(1)}, u32[]{:S(2)}, u32[]{:S(2)}) collective-permute-start(bf16[2,96,256]{2,1,0:T(8,128)(2,1)S(1)} %get-tuple-element.47), channel_id=1, source_target_pairs={{0,4},{1,5},{2,6},{3,7},{4,0},{5,1},{6,2},{7,3},{8,12},{9,13},{10,... | collective-permute-start | bytes 294920 | tf_op jit(solution)/shard_map/ppermute | solution.py:141
  21.1 4.4 %collective-permute-start.3 = (bf16[2,96,256]{2,1,0:T(8,128)(2,1)S(1)}, bf16[2,96,256]{2,1,0:T(8,128)(2,1)S(1)}, u32[]{:S(2)}, u32[]{:S(2)}) collective-permute-start(bf16[2,96,256]{2,1,0:T(8,128)(2,1)S(1)} %get-tuple-element.47), channel_id=1, source_target_pairs={{0,8},{1,9},{2,10},{3,11},{4,12},{5,13},{6,14},{7,15},{8,0},{9,1},... | collective-permute-start | bytes 294920 | tf_op jit(solution)/shard_map/ppermute | solution.py:141
  23.4 6.7 %collective-permute-start.4 = (bf16[2,96,256]{2,1,0:T(8,128)(2,1)S(1)}, bf16[2,96,256]{2,1,0:T(8,128)(2,1)S(1)}, u32[]{:S(2)}, u32[]{:S(2)}) collective-permute-start(bf16[2,96,256]{2,1,0:T(8,128)(2,1)S(1)} %get-tuple-element.47), channel_id=1, source_target_pairs={{0,12},{1,13},{2,14},{3,15},{4,8},{5,9},{6,10},{7,11},{8,4},{9,5},... | collective-permute-start | bytes 294920 | tf_op jit(solution)/shard_map/ppermute | solution.py:141
  24.0 6.1 %collective-permute-start.5 = (bf16[2,2,96,256]{3,2,1,0:T(8,128)(2,1)S(1)}, bf16[2,2,96,256]{3,2,1,0:T(8,128)(2,1)S(1)}, u32[]{:S(2)}, u32[]{:S(2)}) collective-permute-start(bf16[2,2,96,256]{3,2,1,0:T(8,128)(2,1)S(1)} %pad_maximum_fusion.near_low), channel_id=1, source_target_pairs={{0,2},{1,3},{2,0},{3,1},{4,6},{5,7},{6,4},{7,5},{8,10},{9,11},{10,... | collective-permute-start | bytes 589832 | tf_op jit(solution)/shard_map/ppermute | solution.py:141
  30.1 4.6 %collective-permute-start.8 = (bf16[2,2,96,256]{3,2,1,0:T(8,128)(2,1)S(1)}, bf16[2,2,96,256]{3,2,1,0:T(8,128)(2,1)S(1)}, u32[]{:S(2)}, u32[]{:S(2)}) collective-permute-start(bf16[2,2,96,256]{3,2,1,0:T(8,128)(2,1)S(1)} %pad_maximum_fusion.1.near_high), channel_id=1, source_target_pairs={{0,2},{1,3},{2,0},{3,1},{4,6},{5,7},{6,4},{7,5},{8,10},{9,11},{10,... | collective-permute-start | bytes 589832 | tf_op jit(solution)/shard_map/ppermute | solution.py:141
  31.4 15.2 %collective-permute-start.2 = (bf16[2,2,96,256]{3,2,1,0:T(8,128)(2,1)S(1)}, bf16[2,2,96,256]{3,2,1,0:T(8,128)(2,1)S(1)}, u32[]{:S(2)}, u32[]{:S(2)}) collective-permute-start(bf16[2,2,96,256]{3,2,1,0:T(8,128)(2,1)S(1)} %pad_maximum_fusion.near_low), channel_id=1, source_target_pairs={{0,16},{16,0},{1,17},{17,1},{2,18},{18,2},{3,19},{19,3},{4,20},{20... | collective-permute-start | bytes 589832 | tf_op jit(solution)/shard_map/ppermute | solution.py:145
  32.6 14.3 %collective-permute-start.6 = (bf16[2,2,96,256]{3,2,1,0:T(8,128)(2,1)S(1)}, bf16[2,2,96,256]{3,2,1,0:T(8,128)(2,1)S(1)}, u32[]{:S(2)}, u32[]{:S(2)}) collective-permute-start(bf16[2,2,96,256]{3,2,1,0:T(8,128)(2,1)S(1)} %pad_maximum_fusion.1.near_high), channel_id=1, source_target_pairs={{0,16},{16,0},{1,17},{17,1},{2,18},{18,2},{3,19},{19,3},{4,20},{20... | collective-permute-start | bytes 589832 | tf_op jit(solution)/shard_map/ppermute | solution.py:145
  34.7 12.2 %collective-permute-start.7 = (bf16[2,2,96,256]{3,2,1,0:T(8,128)(2,1)S(1)}, bf16[2,2,96,256]{3,2,1,0:T(8,128)(2,1)S(1)}, u32[]{:S(2)}, u32[]{:S(2)}) collective-permute-start(bf16[2,2,96,256]{3,2,1,0:T(8,128)(2,1)S(1)} %collective-permute-done.5.far_low), channel_id=1, source_target_pairs={{0,16},{16,0},{1,17},{17,1},{2,18},{18,2},{3,19},{19,3},{4,20},{20... | collective-permute-start | bytes 589832 | tf_op jit(solution)/shard_map/ppermute | solution.py:145
  35.9 11.9 %collective-permute-start.9 = (bf16[2,2,96,256]{3,2,1,0:T(8,128)(2,1)S(1)}, bf16[2,2,96,256]{3,2,1,0:T(8,128)(2,1)S(1)}, u32[]{:S(2)}, u32[]{:S(2)}) collective-permute-start(bf16[2,2,96,256]{3,2,1,0:T(8,128)(2,1)S(1)} %collective-permute-done.8.far_high), channel_id=1, source_target_pairs={{0,16},{16,0},{1,17},{17,1},{2,18},{18,2},{3,19},{19,3},{4,20},{20... | collective-permute-start | bytes 589832 | tf_op jit(solution)/shard_map/ppermute | solution.py:145
  36.2 1.2 copy-start.3
  37.4 1.2 copy-start.4
  45.3 10.9 %collective-permute-start.27 = (bf16[2,2,96,256]{3,2,1,0:T(8,128)(2,1)S(1)}, bf16[2,2,96,256]{3,2,1,0:T(8,128)(2,1)S(1)}, u32[]{:S(2)}, u32[]{:S(2)}) collective-permute-start(bf16[2,2,96,256]{3,2,1,0:T(8,128)(2,1)S(1)} %get-tuple-element.65), channel_id=1, source_target_pairs={{0,2},{1,3},{2,0},{3,1},{4,6},{5,7},{6,4},{7,5},{8,10},{9,11},{10,... | collective-permute-start | bytes 589832 | tf_op jit(solution)/shard_map/ppermute | solution.py:141
  46.6 15.2 %collective-permute-start.25 = (bf16[2,2,96,256]{3,2,1,0:T(8,128)(2,1)S(1)}, bf16[2,2,96,256]{3,2,1,0:T(8,128)(2,1)S(1)}, u32[]{:S(2)}, u32[]{:S(2)}) collective-permute-start(bf16[2,2,96,256]{3,2,1,0:T(8,128)(2,1)S(1)} %get-tuple-element.62), channel_id=1, source_target_pairs={{0,2},{1,3},{2,0},{3,1},{4,6},{5,7},{6,4},{7,5},{8,10},{9,11},{10,... | collective-permute-start | bytes 589832 | tf_op jit(solution)/shard_map/ppermute | solution.py:141
  54.7 7.3 %collective-permute-start.14 = (bf16[2,2,96,256]{3,2,1,0:T(8,128)(2,1)S(1)}, bf16[2,2,96,256]{3,2,1,0:T(8,128)(2,1)S(1)}, u32[]{:S(2)}, u32[]{:S(2)}) collective-permute-start(bf16[2,2,96,256]{3,2,1,0:T(8,128)(2,1)S(1)} %get-tuple-element.55), channel_id=1, source_target_pairs={{0,2},{1,3},{2,0},{3,1},{4,6},{5,7},{6,4},{7,5},{8,10},{9,11},{10,... | collective-permute-start | bytes 589832 | tf_op jit(solution)/shard_map/ppermute | solution.py:141
  55.1 9.2 %collective-permute-start.12 = (bf16[2,2,96,256]{3,2,1,0:T(8,128)(2,1)S(1)}, bf16[2,2,96,256]{3,2,1,0:T(8,128)(2,1)S(1)}, u32[]{:S(2)}, u32[]{:S(2)}) collective-permute-start(bf16[2,2,96,256]{3,2,1,0:T(8,128)(2,1)S(1)} %get-tuple-element.52), channel_id=1, source_target_pairs={{0,2},{1,3},{2,0},{3,1},{4,6},{5,7},{6,4},{7,5},{8,10},{9,11},{10,... | collective-permute-start | bytes 589832 | tf_op jit(solution)/shard_map/ppermute | solution.py:141
  56.3 9.4 %collective-permute-start.28 = (bf16[2,96,256]{2,1,0:T(8,128)(2,1)S(1)}, bf16[2,96,256]{2,1,0:T(8,128)(2,1)S(1)}, u32[]{:S(2)}, u32[]{:S(2)}) collective-permute-start(bf16[2,96,256]{2,1,0:T(8,128)(2,1)S(1)} %get-tuple-element.66), channel_id=1, source_target_pairs={{0,8},{1,9},{2,10},{3,11},{4,12},{5,13},{6,14},{7,15},{8,0},{9,1},... | collective-permute-start | bytes 294920 | tf_op jit(solution)/shard_map/ppermute | solution.py:141
  60.6 6.8 %collective-permute-start.29 = (bf16[2,96,256]{2,1,0:T(8,128)(2,1)S(1)}, bf16[2,96,256]{2,1,0:T(8,128)(2,1)S(1)}, u32[]{:S(2)}, u32[]{:S(2)}) collective-permute-start(bf16[2,96,256]{2,1,0:T(8,128)(2,1)S(1)} %get-tuple-element.67), channel_id=1, source_target_pairs={{0,12},{1,13},{2,14},{3,15},{4,8},{5,9},{6,10},{7,11},{8,4},{9,5},... | collective-permute-start | bytes 294920 | tf_op jit(solution)/shard_map/ppermute | solution.py:141
  61.9 6.0 %collective-permute-start.26 = (bf16[2,96,256]{2,1,0:T(8,128)(2,1)S(1)}, bf16[2,96,256]{2,1,0:T(8,128)(2,1)S(1)}, u32[]{:S(2)}, u32[]{:S(2)}) collective-permute-start(bf16[2,96,256]{2,1,0:T(8,128)(2,1)S(1)} %get-tuple-element.64), channel_id=1, source_target_pairs={{0,4},{1,5},{2,6},{3,7},{4,0},{5,1},{6,2},{7,3},{8,12},{9,13},{10,... | collective-permute-start | bytes 294920 | tf_op jit(solution)/shard_map/ppermute | solution.py:141
  62.1 10.4 %collective-permute-start.15 = (bf16[2,96,256]{2,1,0:T(8,128)(2,1)S(1)}, bf16[2,96,256]{2,1,0:T(8,128)(2,1)S(1)}, u32[]{:S(2)}, u32[]{:S(2)}) collective-permute-start(bf16[2,96,256]{2,1,0:T(8,128)(2,1)S(1)} %get-tuple-element.56), channel_id=1, source_target_pairs={{0,8},{1,9},{2,10},{3,11},{4,12},{5,13},{6,14},{7,15},{8,0},{9,1},... | collective-permute-start | bytes 294920 | tf_op jit(solution)/shard_map/ppermute | solution.py:141
  64.3 9.5 %collective-permute-start.16 = (bf16[2,96,256]{2,1,0:T(8,128)(2,1)S(1)}, bf16[2,96,256]{2,1,0:T(8,128)(2,1)S(1)}, u32[]{:S(2)}, u32[]{:S(2)}) collective-permute-start(bf16[2,96,256]{2,1,0:T(8,128)(2,1)S(1)} %get-tuple-element.57), channel_id=1, source_target_pairs={{0,12},{1,13},{2,14},{3,15},{4,8},{5,9},{6,10},{7,11},{8,4},{9,5},... | collective-permute-start | bytes 294920 | tf_op jit(solution)/shard_map/ppermute | solution.py:141
  65.7 42.2 %copy-start = (bf16[1024,1024]{1,0:T(8,128)(2,1)S(1)}, bf16[1024,1024]{1,0:T(8,128)(2,1)}, u32[]{:S(2)}) copy-start(bf16[1024,1024]{1,0:T(8,128)(2,1)} %q_ref.7) | copy-start | bytes 6291460
  65.7 8.1 %collective-permute-start.13 = (bf16[2,96,256]{2,1,0:T(8,128)(2,1)S(1)}, bf16[2,96,256]{2,1,0:T(8,128)(2,1)S(1)}, u32[]{:S(2)}, u32[]{:S(2)}) collective-permute-start(bf16[2,96,256]{2,1,0:T(8,128)(2,1)S(1)} %get-tuple-element.54), channel_id=1, source_target_pairs={{0,4},{1,5},{2,6},{3,7},{4,0},{5,1},{6,2},{7,3},{8,12},{9,13},{10,... | collective-permute-start | bytes 294920 | tf_op jit(solution)/shard_map/ppermute | solution.py:141
  68.1 10.4 %collective-permute-start.30 = (bf16[2,96,256]{2,1,0:T(8,128)(2,1)S(1)}, bf16[2,96,256]{2,1,0:T(8,128)(2,1)S(1)}, u32[]{:S(2)}, u32[]{:S(2)}) collective-permute-start(bf16[2,96,256]{2,1,0:T(8,128)(2,1)S(1)} %get-tuple-element.68), channel_id=1, source_target_pairs={{0,4},{1,5},{2,6},{3,7},{4,0},{5,1},{6,2},{7,3},{8,12},{9,13},{10,... | collective-permute-start | bytes 294920 | tf_op jit(solution)/shard_map/ppermute | solution.py:141
  68.1 16.3 %collective-permute-start.32 = (bf16[2,96,256]{2,1,0:T(8,128)(2,1)S(1)}, bf16[2,96,256]{2,1,0:T(8,128)(2,1)S(1)}, u32[]{:S(2)}, u32[]{:S(2)}) collective-permute-start(bf16[2,96,256]{2,1,0:T(8,128)(2,1)S(1)} %get-tuple-element.68), channel_id=1, source_target_pairs={{0,8},{1,9},{2,10},{3,11},{4,12},{5,13},{6,14},{7,15},{8,0},{9,1},... | collective-permute-start | bytes 294920 | tf_op jit(solution)/shard_map/ppermute | solution.py:141
  72.5 13.0 %collective-permute-start.33 = (bf16[2,96,256]{2,1,0:T(8,128)(2,1)S(1)}, bf16[2,96,256]{2,1,0:T(8,128)(2,1)S(1)}, u32[]{:S(2)}, u32[]{:S(2)}) collective-permute-start(bf16[2,96,256]{2,1,0:T(8,128)(2,1)S(1)} %get-tuple-element.68), channel_id=1, source_target_pairs={{0,12},{1,13},{2,14},{3,15},{4,8},{5,9},{6,10},{7,11},{8,4},{9,5},... | collective-permute-start | bytes 294920 | tf_op jit(solution)/shard_map/ppermute | solution.py:141
  74.0 28.4 %collective-permute-start.19 = (bf16[2,96,256]{2,1,0:T(8,128)(2,1)S(1)}, bf16[2,96,256]{2,1,0:T(8,128)(2,1)S(1)}, u32[]{:S(2)}, u32[]{:S(2)}) collective-permute-start(bf16[2,96,256]{2,1,0:T(8,128)(2,1)S(1)} %get-tuple-element.58), channel_id=1, source_target_pairs={{0,8},{1,9},{2,10},{3,11},{4,12},{5,13},{6,14},{7,15},{8,0},{9,1},... | collective-permute-start | bytes 294920 | tf_op jit(solution)/shard_map/ppermute | solution.py:141
  76.2 26.2 %collective-permute-start.20 = (bf16[2,96,256]{2,1,0:T(8,128)(2,1)S(1)}, bf16[2,96,256]{2,1,0:T(8,128)(2,1)S(1)}, u32[]{:S(2)}, u32[]{:S(2)}) collective-permute-start(bf16[2,96,256]{2,1,0:T(8,128)(2,1)S(1)} %get-tuple-element.58), channel_id=1, source_target_pairs={{0,12},{1,13},{2,14},{3,15},{4,8},{5,9},{6,10},{7,11},{8,4},{9,5},... | collective-permute-start | bytes 294920 | tf_op jit(solution)/shard_map/ppermute | solution.py:141
  78.5 5.4 %collective-permute-start.17 = (bf16[2,96,256]{2,1,0:T(8,128)(2,1)S(1)}, bf16[2,96,256]{2,1,0:T(8,128)(2,1)S(1)}, u32[]{:S(2)}, u32[]{:S(2)}) collective-permute-start(bf16[2,96,256]{2,1,0:T(8,128)(2,1)S(1)} %get-tuple-element.58), channel_id=1, source_target_pairs={{0,4},{1,5},{2,6},{3,7},{4,0},{5,1},{6,2},{7,3},{8,12},{9,13},{10,... | collective-permute-start | bytes 294920 | tf_op jit(solution)/shard_map/ppermute | solution.py:141
  83.9 4.8 %collective-permute-start.34 = (bf16[2,2,96,256]{3,2,1,0:T(8,128)(2,1)S(1)}, bf16[2,2,96,256]{3,2,1,0:T(8,128)(2,1)S(1)}, u32[]{:S(2)}, u32[]{:S(2)}) collective-permute-start(bf16[2,2,96,256]{3,2,1,0:T(8,128)(2,1)S(1)} %pad_maximum_fusion.4.near_low), channel_id=1, source_target_pairs={{0,2},{1,3},{2,0},{3,1},{4,6},{5,7},{6,4},{7,5},{8,10},{9,11},{10,... | collective-permute-start | bytes 589832 | tf_op jit(solution)/shard_map/ppermute | solution.py:141
  84.4 18.1 %collective-permute-start.21 = (bf16[2,2,96,256]{3,2,1,0:T(8,128)(2,1)S(1)}, bf16[2,2,96,256]{3,2,1,0:T(8,128)(2,1)S(1)}, u32[]{:S(2)}, u32[]{:S(2)}) collective-permute-start(bf16[2,2,96,256]{3,2,1,0:T(8,128)(2,1)S(1)} %pad_maximum_fusion.2.near_low), channel_id=1, source_target_pairs={{0,2},{1,3},{2,0},{3,1},{4,6},{5,7},{6,4},{7,5},{8,10},{9,11},{10,... | collective-permute-start | bytes 589832 | tf_op jit(solution)/shard_map/ppermute | solution.py:141
  88.7 13.8 %collective-permute-start.36 = (bf16[2,2,96,256]{3,2,1,0:T(8,128)(2,1)S(1)}, bf16[2,2,96,256]{3,2,1,0:T(8,128)(2,1)S(1)}, u32[]{:S(2)}, u32[]{:S(2)}) collective-permute-start(bf16[2,2,96,256]{3,2,1,0:T(8,128)(2,1)S(1)} %pad_maximum_fusion.5.near_high), channel_id=1, source_target_pairs={{0,2},{1,3},{2,0},{3,1},{4,6},{5,7},{6,4},{7,5},{8,10},{9,11},{10,... | collective-permute-start | bytes 589832 | tf_op jit(solution)/shard_map/ppermute | solution.py:141
  89.2 21.7 %collective-permute-start.31 = (bf16[2,2,96,256]{3,2,1,0:T(8,128)(2,1)S(1)}, bf16[2,2,96,256]{3,2,1,0:T(8,128)(2,1)S(1)}, u32[]{:S(2)}, u32[]{:S(2)}) collective-permute-start(bf16[2,2,96,256]{3,2,1,0:T(8,128)(2,1)S(1)} %pad_maximum_fusion.4.near_low), channel_id=1, source_target_pairs={{0,1},{1,0},{2,3},{3,2},{4,5},{5,4},{6,7},{7,6},{8,9},{9,8},{10,11... | collective-permute-start | bytes 589832 | tf_op jit(solution)/shard_map/ppermute | solution.py:141
  102.4 9.3 %collective-permute-start.35 = (bf16[2,2,96,256]{3,2,1,0:T(8,128)(2,1)S(1)}, bf16[2,2,96,256]{3,2,1,0:T(8,128)(2,1)S(1)}, u32[]{:S(2)}, u32[]{:S(2)}) collective-permute-start(bf16[2,2,96,256]{3,2,1,0:T(8,128)(2,1)S(1)} %pad_maximum_fusion.5.near_high), channel_id=1, source_target_pairs={{0,1},{1,0},{2,3},{3,2},{4,5},{5,4},{6,7},{7,6},{8,9},{9,8},{10,11... | collective-permute-start | bytes 589832 | tf_op jit(solution)/shard_map/ppermute | solution.py:141
  102.5 9.3 %collective-permute-start.37 = (bf16[2,2,96,256]{3,2,1,0:T(8,128)(2,1)S(1)}, bf16[2,2,96,256]{3,2,1,0:T(8,128)(2,1)S(1)}, u32[]{:S(2)}, u32[]{:S(2)}) collective-permute-start(bf16[2,2,96,256]{3,2,1,0:T(8,128)(2,1)S(1)} %collective-permute-done.34.far_low), channel_id=1, source_target_pairs={{0,1},{1,0},{2,3},{3,2},{4,5},{5,4},{6,7},{7,6},{8,9},{9,8},{10,11... | collective-permute-start | bytes 589832 | tf_op jit(solution)/shard_map/ppermute | solution.py:141
  107.5 4.7 %collective-permute-start.38 = (bf16[2,2,96,256]{3,2,1,0:T(8,128)(2,1)S(1)}, bf16[2,2,96,256]{3,2,1,0:T(8,128)(2,1)S(1)}, u32[]{:S(2)}, u32[]{:S(2)}) collective-permute-start(bf16[2,2,96,256]{3,2,1,0:T(8,128)(2,1)S(1)} %collective-permute-done.36.far_high), channel_id=1, source_target_pairs={{0,1},{1,0},{2,3},{3,2},{4,5},{5,4},{6,7},{7,6},{8,9},{9,8},{10,11... | collective-permute-start | bytes 589832 | tf_op jit(solution)/shard_map/ppermute | solution.py:141
  107.6 7.8 %collective-permute-start.24 = (bf16[2,2,96,256]{3,2,1,0:T(8,128)(2,1)S(1)}, bf16[2,2,96,256]{3,2,1,0:T(8,128)(2,1)S(1)}, u32[]{:S(2)}, u32[]{:S(2)}) collective-permute-start(bf16[2,2,96,256]{3,2,1,0:T(8,128)(2,1)S(1)} %pad_maximum_fusion.3.near_high), channel_id=1, source_target_pairs={{0,2},{1,3},{2,0},{3,1},{4,6},{5,7},{6,4},{7,5},{8,10},{9,11},{10,... | collective-permute-start | bytes 589832 | tf_op jit(solution)/shard_map/ppermute | solution.py:141
  110.9 4.9 %collective-permute-start.40 = (f32[2,96,256]{2,1,0:T(8,128)S(1)}, f32[2,96,256]{2,1,0:T(8,128)S(1)}, u32[]{:S(2)}, u32[]{:S(2)}) collective-permute-start(f32[2,96,256]{2,1,0:T(8,128)S(1)} %pad_maximum_fusion.6), channel_id=1, source_target_pairs={{0,1},{1,0},{2,3},{3,2},{4,5},{5,4},{6,7},{7,6},{8,9},{9,8},{10,11... | collective-permute-start | bytes 589832 | tf_op jit(solution)/shard_map/ppermute | solution.py:141
  111.7 8.4 %collective-permute-start.18 = (bf16[2,2,96,256]{3,2,1,0:T(8,128)(2,1)S(1)}, bf16[2,2,96,256]{3,2,1,0:T(8,128)(2,1)S(1)}, u32[]{:S(2)}, u32[]{:S(2)}) collective-permute-start(bf16[2,2,96,256]{3,2,1,0:T(8,128)(2,1)S(1)} %pad_maximum_fusion.2.near_low), channel_id=1, source_target_pairs={{0,1},{1,0},{2,3},{3,2},{4,5},{5,4},{6,7},{7,6},{8,9},{9,8},{10,11... | collective-permute-start | bytes 589832 | tf_op jit(solution)/shard_map/ppermute | solution.py:141
  111.8 8.4 %collective-permute-start.22 = (bf16[2,2,96,256]{3,2,1,0:T(8,128)(2,1)S(1)}, bf16[2,2,96,256]{3,2,1,0:T(8,128)(2,1)S(1)}, u32[]{:S(2)}, u32[]{:S(2)}) collective-permute-start(bf16[2,2,96,256]{3,2,1,0:T(8,128)(2,1)S(1)} %pad_maximum_fusion.3.near_high), channel_id=1, source_target_pairs={{0,1},{1,0},{2,3},{3,2},{4,5},{5,4},{6,7},{7,6},{8,9},{9,8},{10,11... | collective-permute-start | bytes 589832 | tf_op jit(solution)/shard_map/ppermute | solution.py:141
  112.2 7.9 %collective-permute-start.23 = (bf16[2,2,96,256]{3,2,1,0:T(8,128)(2,1)S(1)}, bf16[2,2,96,256]{3,2,1,0:T(8,128)(2,1)S(1)}, u32[]{:S(2)}, u32[]{:S(2)}) collective-permute-start(bf16[2,2,96,256]{3,2,1,0:T(8,128)(2,1)S(1)} %collective-permute-done.21.far_low), channel_id=1, source_target_pairs={{0,1},{1,0},{2,3},{3,2},{4,5},{5,4},{6,7},{7,6},{8,9},{9,8},{10,11... | collective-permute-start | bytes 589832 | tf_op jit(solution)/shard_map/ppermute | solution.py:141
  115.3 4.8 %collective-permute-start.39 = (bf16[2,2,96,256]{3,2,1,0:T(8,128)(2,1)S(1)}, bf16[2,2,96,256]{3,2,1,0:T(8,128)(2,1)S(1)}, u32[]{:S(2)}, u32[]{:S(2)}) collective-permute-start(bf16[2,2,96,256]{3,2,1,0:T(8,128)(2,1)S(1)} %collective-permute-done.24.far_high), channel_id=1, source_target_pairs={{0,1},{1,0},{2,3},{3,2},{4,5},{5,4},{6,7},{7,6},{8,9},{9,8},{10,11... | collective-permute-start | bytes 589832 | tf_op jit(solution)/shard_map/ppermute | solution.py:141

commit v4 on v3

--- a/solution.py
+++ b/solution.py
@@ -10,8 +10,7 @@
 
 BF16 = jnp.bfloat16
 F32 = jnp.float32
-VMEM_LIMIT = 48 * 1024 * 1024
-VMEM_ALL = 63 * 1024 * 1024
+VMEM_LIMIT = 32 * 1024 * 1024
 
 
 def rms_rows(matrix):
@@ -149,8 +148,8 @@
     return lax.optimization_barrier((value, before))[0]
 
 
-def compiler_params(limit=VMEM_LIMIT):
-    return pltpu.CompilerParams(vmem_limit_bytes=limit)
+def compiler_params():
+    return pltpu.CompilerParams(vmem_limit_bytes=VMEM_LIMIT)
 
 
 def head_of(ids, order, other):
@@ -195,7 +194,7 @@
             pltpu.VMEM(fast_out.shape, F32),
             pltpu.SemaphoreType.DMA((2,)),
         ],
-        compiler_params=compiler_params(VMEM_ALL),
+        compiler_params=compiler_params(),
         name="pack",
     )(ids, fast_in, fast_out)
 
@@ -217,11 +216,15 @@
     )(own, got)
 
 
-def prepare_kernel(heads, ids, x_ref, *rest):
+def prepare_kernel(heads, block_root, ids, x_ref, *rest):
     own, send = rest[-2:]
     core = ids[1]
     half = heads // 2
     size = x_ref.shape[1] // heads
+
+    if len(rest) == 3:
+        rates = rest[0][...]
+        columns_of = jnp.concatenate([rates, rates], axis=0).T
 
     def work(owner, out):
         for local in range(half):
@@ -230,16 +233,16 @@
             if len(rest) == 2:
                 out[:, into] = normalize_head(x_ref[:, columns])
             else:
-                first = rest[0][:, local : local + 1]
-                second = rest[0][:, half + local : half + local + 1]
-                rate = jnp.where(owner == 0, first, second)
+                first = columns_of[:, local : local + 1]
+                second = columns_of[:, half + local : half + local + 1]
+                rate = jnp.where(owner == 0, first, second) * block_root
                 out[:, into] = (rate * x_ref[:, columns].astype(F32)).astype(BF16)
 
     work(core, own)
     work(1 - core, send)
 
 
-def prepare(ids, tokens, rates, heads, name):
+def prepare(ids, tokens, rates, heads, block_root, name):
     rows, width = tokens.shape
     step = 256
     wide = pl.BlockSpec((step, width), lambda i, ids: (i, 0))
@@ -247,10 +250,10 @@
     operands, specs = [tokens], [wide]
     if rates is not None:
         operands.append(rates)
-        specs.append(pl.BlockSpec((step, heads), lambda i, ids: (i, 0)))
+        specs.append(pl.BlockSpec((heads, step), lambda i, ids: (0, i)))
     shape = jax.ShapeDtypeStruct((rows, width // 2), BF16)
     return pl.pallas_call(
-        functools.partial(prepare_kernel, heads),
+        functools.partial(prepare_kernel, heads, block_root),
         grid_spec=pltpu.PrefetchScalarGridSpec(
             num_scalar_prefetch=1,
             grid=(rows // step,),
@@ -258,7 +261,7 @@
             out_specs=[narrow] * 2,
         ),
         out_shape=[shape] * 2,
-        compiler_params=compiler_params(VMEM_ALL),
+        compiler_params=compiler_params(),
         cost_estimate=pl.CostEstimate(
             flops=rows * width * 5, bytes_accessed=rows * width * 4, transcendentals=0
         ),
@@ -567,8 +570,8 @@
     own, theirs = pack(ids, fast_in, fast_out)
     got = swap(theirs, 1)
     later = after(ids, own)
-    k_own, k_send = prepare(later, keys, None, heads, "keys")
-    v_own, v_send = prepare(later, values, (step_size * block_root).T, heads, "values")
+    k_own, k_send = prepare(later, keys, None, heads, None, "keys")
+    v_own, v_send = prepare(later, values, step_size, heads, block_root, "values")
     got = after(got, k_send, v_send)
     master_one, master_two, shard = pair(own, got)
     masters = (master_one, master_two)
@@ -591,14 +594,21 @@
         wide.append(a)
         short.append(b)
 
-    lines = [gather_chips(shard) for shard in short]
-    near_low, near_high, far_low, far_high = lines[0]
-    far_low, far_high = after((far_low, far_high), *lines[1][:2])
+    z1, z3, z2 = swap(short[0], 4), swap(short[0], 12), swap(short[0], 8)
+    near_low, near_high = jnp.stack([short[0], z1]), jnp.stack([z2, z3])
+    far_low, far_high = swap(near_low, 2), swap(near_high, 2)
+    second = after(short[1], near_low)
+    z1 = swap(second, 4)
+    second_low = after(jnp.stack([second, z1]), near_high)
+    later = after(short[1], second_low)
+    z3, z2 = swap(later, 12), swap(later, 8)
+    second_high = jnp.stack([z2, z3])
     mine = (near_low, near_high, far_low, far_high)
     others = tuple(swap(piece, 1) for piece in mine)
     output = apply_fast(ids, 0, 0, mine, queries, None, fast)
+    near_low, near_high = second_low, after(second_high, output)
     output = apply_fast(ids, 0, 1, others, queries, output, fast)
-    near_low, near_high, far_low, far_high = lines[1]
+    far_low, far_high = swap(near_low, 2), swap(near_high, 2)
     far_high = after(far_high, output)
     mine = (near_low, near_high, far_low, far_high)
     others = tuple(swap(piece, 1) for piece in mine)

time: 124 us -> 112 us (0.903)
  Pallas kernels: 40.1 us -> 30.2 us
  starting transfers between devices: 55 us -> 52.2 us
  waiting for transfers between devices: 22.3 us -> 25 us
  other arithmetic: 1.45 us -> 0.21 us
    pallas_call x2, Pallas kernels: 10.1 us -> 3.78 us  [prepare(): pl.pallas_call(functools.partial(prepare_kernel, heads, block_root), grid...]
    ppermute x4, waiting for transfers between devices: 0.95 us -> 4.81 us  [swap_parts(): return lax.ppermute(value, 'parts', [(0, 1), (1, 0)])]
    ppermute x37, starting transfers between devices: 52.1 us -> 49.2 us  [swap(): lax.ppermute(value, 'tok', [(place, place ^ bits) for place in range(coun...]
    pallas_call x2, Pallas kernels: 13.6 us -> 11.7 us  [increments(): pl.pallas_call(increments_kernel, grid_spec=pltpu.PrefetchScalarGridSpec(...]
    pallas_call x1, Pallas kernels: 2.43 us -> 0.78 us  [pack(): pl.pallas_call(pack_kernel, in_specs=[pl.BlockSpec(memory_space=pltpu.SME...]
  transfers between devices with their start and end apart: 41 -> 41, of which waited for: 10 -> 11; matrix products, arithmetic and copies ran while one was open for 0% -> 0% of each run, Pallas kernels for 24% -> 22%
where the time goes in v4:
time: 112 us
  starting transfers between devices  52.2 us (47%)
  Pallas kernels  30.2 us (27%)
  waiting for transfers between devices  25 us (22%)
  local copies, waits for them, and re-layouts  3.47 us (3%)
    ppermute x37, starting transfers between devices, swap(): lax.ppermute(value, 'tok', [(place, place ^ bits) for place in range(coun...  49.2 us
    ppermute x37, waiting for transfers between devices, swap(): lax.ppermute(value, 'tok', [(place, place ^ bits) for place in range(coun...  20.2 us
    pallas_call x4, Pallas kernels, apply_fast(): pl.pallas_call(functools.partial(apply_kernel, other), grid_spec=pltpu.Pr...  12.2 us
    pallas_call x2, Pallas kernels, increments(): pl.pallas_call(increments_kernel, grid_spec=pltpu.PrefetchScalarGridSpec(...  11.7 us
    ppermute x4, waiting for transfers between devices, swap_parts(): return lax.ppermute(value, 'parts', [(0, 1), (1, 0)])  4.81 us
    pallas_call x2, Pallas kernels, prepare(): pl.pallas_call(functools.partial(prepare_kernel, heads, block_root), grid...  3.78 us
    unnamed x12, local copies, waits for them, and re-layouts  3.46 us
    ppermute x4, starting transfers between devices, swap_parts(): return lax.ppermute(value, 'parts', [(0, 1), (1, 0)])  2.93 us
  transfers between devices with their start and end apart: 41, of which 11 were waited for; matrix products, arithmetic and copies ran while one was open for 0% of the time, Pallas kernels for 22%

profile of v4, /device:TPU:1, one launch (start us, length us, event | category | flops | bytes accessed | tf_op | source)
XLA Modules:
  0.0 111.9 jit_solution(5068715254588044028)
XLA Ops:
  0.7 0.9 copy-done.3
  1.7 0.9 copy-done.4
  2.6 0.8 pack.1
  3.4 1.6 %copy-done.1 = bf16[1024,1024]{1,0:T(8,128)(2,1)S(1)} copy-done((bf16[1024,1024]{1,0:T(8,128)(2,1)S(1)}, bf16[1024,1024]{1,0:T(8,128)(2,1)}, u32[]{:S(2)}) %copy-start.1) | copy-done | bytes 2097176
  5.0 1.5 %keys.1 = (bf16[1024,512]{1,0:T(8,128)(2,1)S(1)}, bf16[1024,512]{1,0:T(8,128)(2,1)S(1)}) custom-call(s32[3]{0:T(128)S(1)} %pad_add_fusion.ids, bf16[1024,1024]{1,0:T(8,128)(2,1)S(1)} %copy-done.1), custom_call_target="tpu_custom_call" | custom-call | flops 5242880 | bytes 4194304 | tf_op jit(solution)/shard_map/keys/pallas_call | solution.py:255
  6.5 0.1 collective-permute-start.10
  6.6 2.3 %values.1 = (bf16[1024,512]{1,0:T(8,128)(2,1)S(1)}, bf16[1024,512]{1,0:T(8,128)(2,1)S(1)}) custom-call(s32[3]{0:T(128)S(1)} %pad_add_fusion.ids, bf16[1024,1024]{1,0:T(8,128)(2,1)S(1)} %copy-done.2, f32[4,1024]{1,0:T(4,128)S(1)} %copy-done.5), custom_call_target="tpu_custom_call" | custom-call | flops 5242880 | bytes 4194304 | tf_op jit(solution)/shard_map/values/pallas_call | solution.py:255
  8.9 0.5 collective-permute-start.11
  9.5 2.5 %collective-permute-done.got = f32[2,96,256]{2,1,0:T(8,128)S(1)} collective-permute-done((f32[2,96,256]{2,1,0:T(8,128)S(1)}, f32[2,96,256]{2,1,0:T(8,128)S(1)}, u32[]{:S(2)}, u32[]{:S(2)}) %collective-permute-start) | collective-permute-done | bytes 196640 | tf_op jit(solution)/shard_map/ppermute | solution.py:140
  12.0 2.7 %collective-permute-start.1 = (bf16[2,96,256]{2,1,0:T(8,128)(2,1)S(1)}, bf16[2,96,256]{2,1,0:T(8,128)(2,1)S(1)}, u32[]{:S(2)}, u32[]{:S(2)}) collective-permute-start(bf16[2,96,256]{2,1,0:T(8,128)(2,1)S(1)} %get-tuple-element.47), channel_id=1, source_target_pairs={{0,4},{1,5},{2,6},{3,7},{4,0},{5,1},{6,2},{7,3},{8,12},{9,13},{10,... | collective-permute-start | bytes 294920 | tf_op jit(solution)/shard_map/ppermute | solution.py:140
  14.8 2.3 %collective-permute-start.3 = (bf16[2,96,256]{2,1,0:T(8,128)(2,1)S(1)}, bf16[2,96,256]{2,1,0:T(8,128)(2,1)S(1)}, u32[]{:S(2)}, u32[]{:S(2)}) collective-permute-start(bf16[2,96,256]{2,1,0:T(8,128)(2,1)S(1)} %get-tuple-element.47), channel_id=1, source_target_pairs={{0,8},{1,9},{2,10},{3,11},{4,12},{5,13},{6,14},{7,15},{8,0},{9,1},... | collective-permute-start | bytes 294920 | tf_op jit(solution)/shard_map/ppermute | solution.py:140
  17.1 0.7 collective-permute-done.1
  17.8 1.2 %collective-permute-start.5 = (bf16[2,2,96,256]{3,2,1,0:T(8,128)(2,1)S(1)}, bf16[2,2,96,256]{3,2,1,0:T(8,128)(2,1)S(1)}, u32[]{:S(2)}, u32[]{:S(2)}) collective-permute-start(bf16[2,2,96,256]{3,2,1,0:T(8,128)(2,1)S(1)} %pad_maximum_fusion.near_low), channel_id=1, source_target_pairs={{0,2},{1,3},{2,0},{3,1},{4,6},{5,7},{6,4},{7,5},{8,10},{9,11},{10,... | collective-permute-start | bytes 589832 | tf_op jit(solution)/shard_map/ppermute | solution.py:140
  19.0 0.5 collective-permute-done.3
  19.6 4.4 %collective-permute-done.4 = bf16[2,96,256]{2,1,0:T(8,128)(2,1)S(1)} collective-permute-done((bf16[2,96,256]{2,1,0:T(8,128)(2,1)S(1)}, bf16[2,96,256]{2,1,0:T(8,128)(2,1)S(1)}, u32[]{:S(2)}, u32[]{:S(2)}) %collective-permute-start.4) | collective-permute-done | bytes 98336 | tf_op jit(solution)/shard_map/ppermute | solution.py:140
  24.0 1.3 %collective-permute-start.8 = (bf16[2,2,96,256]{3,2,1,0:T(8,128)(2,1)S(1)}, bf16[2,2,96,256]{3,2,1,0:T(8,128)(2,1)S(1)}, u32[]{:S(2)}, u32[]{:S(2)}) collective-permute-start(bf16[2,2,96,256]{3,2,1,0:T(8,128)(2,1)S(1)} %pad_maximum_fusion.1.near_high), channel_id=1, source_target_pairs={{0,2},{1,3},{2,0},{3,1},{4,6},{5,7},{6,4},{7,5},{8,10},{9,11},{10,... | collective-permute-start | bytes 589832 | tf_op jit(solution)/shard_map/ppermute | solution.py:140
  25.3 1.2 %collective-permute-start.2 = (bf16[2,2,96,256]{3,2,1,0:T(8,128)(2,1)S(1)}, bf16[2,2,96,256]{3,2,1,0:T(8,128)(2,1)S(1)}, u32[]{:S(2)}, u32[]{:S(2)}) collective-permute-start(bf16[2,2,96,256]{3,2,1,0:T(8,128)(2,1)S(1)} %pad_maximum_fusion.near_low), channel_id=1, source_target_pairs={{0,16},{16,0},{1,17},{17,1},{2,18},{18,2},{3,19},{19,3},{4,20},{20... | collective-permute-start | bytes 589832 | tf_op jit(solution)/shard_map/ppermute | solution.py:144
  26.5 0.3 collective-permute-start.6
  26.8 1.8 %collective-permute-done.8.far_high = bf16[2,2,96,256]{3,2,1,0:T(8,128)(2,1)S(1)} collective-permute-done((bf16[2,2,96,256]{3,2,1,0:T(8,128)(2,1)S(1)}, bf16[2,2,96,256]{3,2,1,0:T(8,128)(2,1)S(1)}, u32[]{:S(2)}, u32[]{:S(2)}) %collective-permute-start.8) | collective-permute-done | bytes 196640 | tf_op jit(solution)/shard_map/ppermute | solution.py:140
  28.6 1.2 %collective-permute-start.7 = (bf16[2,2,96,256]{3,2,1,0:T(8,128)(2,1)S(1)}, bf16[2,2,96,256]{3,2,1,0:T(8,128)(2,1)S(1)}, u32[]{:S(2)}, u32[]{:S(2)}) collective-permute-start(bf16[2,2,96,256]{3,2,1,0:T(8,128)(2,1)S(1)} %collective-permute-done.5.far_low), channel_id=1, source_target_pairs={{0,16},{16,0},{1,17},{17,1},{2,18},{18,2},{3,19},{19,3},{4,20},{20... | collective-permute-start | bytes 589832 | tf_op jit(solution)/shard_map/ppermute | solution.py:144
  29.8 0.3 collective-permute-start.9
  30.1 5.8 %increments.3 = (f32[4,2,96,256]{3,2,1,0:T(8,128)S(1)}, bf16[2,2,96,256]{3,2,1,0:T(8,128)(2,1)S(1)}, bf16[2,2,96,256]{3,2,1,0:T(8,128)(2,1)S(1)}) custom-call(s32[3]{0:T(128)S(1)} %pad_add_fusion.ids, bf16[2,2,96,256]{3,2,1,0:T(8,128)(2,1)S(1)} %pad_maximum_fusion.near_low, bf16[2,2,96,256]{3,2,1,0:T(8,128)(2,1)S(1)} %pad_maximum_fusion.1.near_high, ...), custom_call_target="tpu_custom_call" | custom-call | flops 3221225472 | bytes 2097152 | tf_op jit(solution)/shard_map/increments/pallas_call | solution.py:387
  35.9 1.3 %collective-permute-start.19 = (bf16[2,2,96,256]{3,2,1,0:T(8,128)(2,1)S(1)}, bf16[2,2,96,256]{3,2,1,0:T(8,128)(2,1)S(1)}, u32[]{:S(2)}, u32[]{:S(2)}) collective-permute-start(bf16[2,2,96,256]{3,2,1,0:T(8,128)(2,1)S(1)} %get-tuple-element.64), channel_id=1, source_target_pairs={{0,2},{1,3},{2,0},{3,1},{4,6},{5,7},{6,4},{7,5},{8,10},{9,11},{10,... | collective-permute-start | bytes 589832 | tf_op jit(solution)/shard_map/ppermute | solution.py:140
  37.2 0.2 collective-permute-start.17
  37.4 0.6 collective-permute-done.7.far_low
  38.0 4.2 %collective-permute-done.9.far_high = bf16[2,2,96,256]{3,2,1,0:T(8,128)(2,1)S(1)} collective-permute-done((bf16[2,2,96,256]{3,2,1,0:T(8,128)(2,1)S(1)}, bf16[2,2,96,256]{3,2,1,0:T(8,128)(2,1)S(1)}, u32[]{:S(2)}, u32[]{:S(2)}) %collective-permute-start.9) | collective-permute-done | bytes 196640 | tf_op jit(solution)/shard_map/ppermute | solution.py:144
  42.2 5.9 %increments.2 = (f32[4,2,96,256]{3,2,1,0:T(8,128)S(1)}, bf16[2,2,96,256]{3,2,1,0:T(8,128)(2,1)S(1)}, bf16[2,2,96,256]{3,2,1,0:T(8,128)(2,1)S(1)}) custom-call(s32[3]{0:T(128)S(1)} %pad_add_fusion.ids, bf16[2,2,96,256]{3,2,1,0:T(8,128)(2,1)S(1)} %collective-permute-done.2.near_low, bf16[2,2,96,256]{3,2,1,0:T(8,128)(2,1)S(1)} %collective-permute-done.6.near_high, ...), custom_call_target="tpu_custom_call" | custom-call | flops 3221225472 | bytes 2097152 | tf_op jit(solution)/shard_map/increments/pallas_call | solution.py:387
  48.1 0.3 collective-permute-start.14
  48.4 1.2 %collective-permute-start.12 = (bf16[2,2,96,256]{3,2,1,0:T(8,128)(2,1)S(1)}, bf16[2,2,96,256]{3,2,1,0:T(8,128)(2,1)S(1)}, u32[]{:S(2)}, u32[]{:S(2)}) collective-permute-start(bf16[2,2,96,256]{3,2,1,0:T(8,128)(2,1)S(1)} %get-tuple-element.52), channel_id=1, source_target_pairs={{0,2},{1,3},{2,0},{3,1},{4,6},{5,7},{6,4},{7,5},{8,10},{9,11},{10,... | collective-permute-start | bytes 589832 | tf_op jit(solution)/shard_map/ppermute | solution.py:140
  49.7 3.9 %collective-permute-start.20 = (bf16[2,96,256]{2,1,0:T(8,128)(2,1)S(1)}, bf16[2,96,256]{2,1,0:T(8,128)(2,1)S(1)}, u32[]{:S(2)}, u32[]{:S(2)}) collective-permute-start(bf16[2,96,256]{2,1,0:T(8,128)(2,1)S(1)} %get-tuple-element.65), channel_id=1, source_target_pairs={{0,8},{1,9},{2,10},{3,11},{4,12},{5,13},{6,14},{7,15},{8,0},{9,1},... | collective-permute-start | bytes 294920 | tf_op jit(solution)/shard_map/ppermute | solution.py:140
  53.7 1.2 %collective-permute-start.21 = (bf16[2,96,256]{2,1,0:T(8,128)(2,1)S(1)}, bf16[2,96,256]{2,1,0:T(8,128)(2,1)S(1)}, u32[]{:S(2)}, u32[]{:S(2)}) collective-permute-start(bf16[2,96,256]{2,1,0:T(8,128)(2,1)S(1)} %get-tuple-element.66), channel_id=1, source_target_pairs={{0,12},{1,13},{2,14},{3,15},{4,8},{5,9},{6,10},{7,11},{8,4},{9,5},... | collective-permute-start | bytes 294920 | tf_op jit(solution)/shard_map/ppermute | solution.py:140
  55.0 2.4 %collective-permute-start.15 = (bf16[2,96,256]{2,1,0:T(8,128)(2,1)S(1)}, bf16[2,96,256]{2,1,0:T(8,128)(2,1)S(1)}, u32[]{:S(2)}, u32[]{:S(2)}) collective-permute-start(bf16[2,96,256]{2,1,0:T(8,128)(2,1)S(1)} %get-tuple-element.56), channel_id=1, source_target_pairs={{0,8},{1,9},{2,10},{3,11},{4,12},{5,13},{6,14},{7,15},{8,0},{9,1},... | collective-permute-start | bytes 294920 | tf_op jit(solution)/shard_map/ppermute | solution.py:140
  57.5 1.9 %collective-permute-start.16 = (bf16[2,96,256]{2,1,0:T(8,128)(2,1)S(1)}, bf16[2,96,256]{2,1,0:T(8,128)(2,1)S(1)}, u32[]{:S(2)}, u32[]{:S(2)}) collective-permute-start(bf16[2,96,256]{2,1,0:T(8,128)(2,1)S(1)} %get-tuple-element.57), channel_id=1, source_target_pairs={{0,12},{1,13},{2,14},{3,15},{4,8},{5,9},{6,10},{7,11},{8,4},{9,5},... | collective-permute-start | bytes 294920 | tf_op jit(solution)/shard_map/ppermute | solution.py:140
  59.4 1.2 %collective-permute-start.13 = (bf16[2,96,256]{2,1,0:T(8,128)(2,1)S(1)}, bf16[2,96,256]{2,1,0:T(8,128)(2,1)S(1)}, u32[]{:S(2)}, u32[]{:S(2)}) collective-permute-start(bf16[2,96,256]{2,1,0:T(8,128)(2,1)S(1)} %get-tuple-element.54), channel_id=1, source_target_pairs={{0,4},{1,5},{2,6},{3,7},{4,0},{5,1},{6,2},{7,3},{8,12},{9,13},{10,... | collective-permute-start | bytes 294920 | tf_op jit(solution)/shard_map/ppermute | solution.py:140
  60.6 0.1 renorm.3
  60.8 0.4 collective-permute-start.22
  61.1 1.4 %collective-permute-start.24 = (bf16[2,96,256]{2,1,0:T(8,128)(2,1)S(1)}, bf16[2,96,256]{2,1,0:T(8,128)(2,1)S(1)}, u32[]{:S(2)}, u32[]{:S(2)}) collective-permute-start(bf16[2,96,256]{2,1,0:T(8,128)(2,1)S(1)} %get-tuple-element.67), channel_id=1, source_target_pairs={{0,8},{1,9},{2,10},{3,11},{4,12},{5,13},{6,14},{7,15},{8,0},{9,1},... | collective-permute-start | bytes 294920 | tf_op jit(solution)/shard_map/ppermute | solution.py:140
  62.5 3.0 %collective-permute-done.15.two = bf16[2,96,256]{2,1,0:T(8,128)(2,1)S(1)} collective-permute-done((bf16[2,96,256]{2,1,0:T(8,128)(2,1)S(1)}, bf16[2,96,256]{2,1,0:T(8,128)(2,1)S(1)}, u32[]{:S(2)}, u32[]{:S(2)}) %collective-permute-start.15) | collective-permute-done | bytes 98336 | tf_op jit(solution)/shard_map/ppermute | solution.py:140
  65.5 2.0 %collective-permute-start.25 = (bf16[2,96,256]{2,1,0:T(8,128)(2,1)S(1)}, bf16[2,96,256]{2,1,0:T(8,128)(2,1)S(1)}, u32[]{:S(2)}, u32[]{:S(2)}) collective-permute-start(bf16[2,96,256]{2,1,0:T(8,128)(2,1)S(1)} %get-tuple-element.67), channel_id=1, source_target_pairs={{0,12},{1,13},{2,14},{3,15},{4,8},{5,9},{6,10},{7,11},{8,4},{9,5},... | collective-permute-start | bytes 294920 | tf_op jit(solution)/shard_map/ppermute | solution.py:140
  67.5 0.1 renorm.2
  67.7 3.5 %collective-permute-start.23 = (bf16[2,96,256]{2,1,0:T(8,128)(2,1)S(1)}, bf16[2,96,256]{2,1,0:T(8,128)(2,1)S(1)}, u32[]{:S(2)}, u32[]{:S(2)}) collective-permute-start(bf16[2,96,256]{2,1,0:T(8,128)(2,1)S(1)} %get-tuple-element.70), channel_id=1, source_target_pairs={{0,4},{1,5},{2,6},{3,7},{4,0},{5,1},{6,2},{7,3},{8,12},{9,13},{10,... | collective-permute-start | bytes 294920 | tf_op jit(solution)/shard_map/ppermute | solution.py:140
  71.2 2.7 %collective-permute-done.24 = bf16[2,96,256]{2,1,0:T(8,128)(2,1)S(1)} collective-permute-done((bf16[2,96,256]{2,1,0:T(8,128)(2,1)S(1)}, bf16[2,96,256]{2,1,0:T(8,128)(2,1)S(1)}, u32[]{:S(2)}, u32[]{:S(2)}) %collective-permute-start.24) | collective-permute-done | bytes 98336 | tf_op jit(solution)/shard_map/ppermute | solution.py:140
  74.0 2.3 %collective-permute-done.23 = bf16[2,96,256]{2,1,0:T(8,128)(2,1)S(1)} collective-permute-done((bf16[2,96,256]{2,1,0:T(8,128)(2,1)S(1)}, bf16[2,96,256]{2,1,0:T(8,128)(2,1)S(1)}, u32[]{:S(2)}, u32[]{:S(2)}) %collective-permute-start.23) | collective-permute-done | bytes 98336 | tf_op jit(solution)/shard_map/ppermute | solution.py:140
  76.3 2.0 %collective-permute-start.27 = (bf16[2,96,256]{2,1,0:T(8,128)(2,1)S(1)}, bf16[2,96,256]{2,1,0:T(8,128)(2,1)S(1)}, u32[]{:S(2)}, u32[]{:S(2)}) collective-permute-start(bf16[2,96,256]{2,1,0:T(8,128)(2,1)S(1)} %get-tuple-element.70), channel_id=1, source_target_pairs={{0,8},{1,9},{2,10},{3,11},{4,12},{5,13},{6,14},{7,15},{8,0},{9,1},... | collective-permute-start | bytes 294920 | tf_op jit(solution)/shard_map/ppermute | solution.py:140
  78.3 0.3 collective-permute-start.28
  78.6 0.2 collective-permute-start.30
  78.8 1.2 %collective-permute-start.29 = (bf16[2,2,96,256]{3,2,1,0:T(8,128)(2,1)S(1)}, bf16[2,2,96,256]{3,2,1,0:T(8,128)(2,1)S(1)}, u32[]{:S(2)}, u32[]{:S(2)}) collective-permute-start(bf16[2,2,96,256]{3,2,1,0:T(8,128)(2,1)S(1)} %pad_maximum_fusion.2.near_low), channel_id=1, source_target_pairs={{0,2},{1,3},{2,0},{3,1},{4,6},{5,7},{6,4},{7,5},{8,10},{9,11},{10,... | collective-permute-start | bytes 589832 | tf_op jit(solution)/shard_map/ppermute | solution.py:140
  80.0 7.4 %collective-permute-start.36 = (bf16[2,2,96,256]{3,2,1,0:T(8,128)(2,1)S(1)}, bf16[2,2,96,256]{3,2,1,0:T(8,128)(2,1)S(1)}, u32[]{:S(2)}, u32[]{:S(2)}) collective-permute-start(bf16[2,2,96,256]{3,2,1,0:T(8,128)(2,1)S(1)} %pad_maximum_fusion.4.near_high), channel_id=1, source_target_pairs={{0,1},{1,0},{2,3},{3,2},{4,5},{5,4},{6,7},{7,6},{8,9},{9,8},{10,11... | collective-permute-start | bytes 589832 | tf_op jit(solution)/shard_map/ppermute | solution.py:140
  87.4 1.6 %collective-permute-start.35 = (bf16[2,2,96,256]{3,2,1,0:T(8,128)(2,1)S(1)}, bf16[2,2,96,256]{3,2,1,0:T(8,128)(2,1)S(1)}, u32[]{:S(2)}, u32[]{:S(2)}) collective-permute-start(bf16[2,2,96,256]{3,2,1,0:T(8,128)(2,1)S(1)} %pad_maximum_fusion.2.near_low), channel_id=1, source_target_pairs={{0,1},{1,0},{2,3},{3,2},{4,5},{5,4},{6,7},{7,6},{8,9},{9,8},{10,11... | collective-permute-start | bytes 589832 | tf_op jit(solution)/shard_map/ppermute | solution.py:140
  89.1 0.2 collective-permute-start.32
  89.3 1.8 %collective-permute-start.38 = (bf16[2,2,96,256]{3,2,1,0:T(8,128)(2,1)S(1)}, bf16[2,2,96,256]{3,2,1,0:T(8,128)(2,1)S(1)}, u32[]{:S(2)}, u32[]{:S(2)}) collective-permute-start(bf16[2,2,96,256]{3,2,1,0:T(8,128)(2,1)S(1)} %collective-permute-done.30.far_high), channel_id=1, source_target_pairs={{0,1},{1,0},{2,3},{3,2},{4,5},{5,4},{6,7},{7,6},{8,9},{9,8},{10,11... | collective-permute-start | bytes 589832 | tf_op jit(solution)/shard_map/ppermute | solution.py:140
  91.1 3.1 %collective-permute-start.37 = (bf16[2,2,96,256]{3,2,1,0:T(8,128)(2,1)S(1)}, bf16[2,2,96,256]{3,2,1,0:T(8,128)(2,1)S(1)}, u32[]{:S(2)}, u32[]{:S(2)}) collective-permute-start(bf16[2,2,96,256]{3,2,1,0:T(8,128)(2,1)S(1)} %collective-permute-done.29.far_low), channel_id=1, source_target_pairs={{0,1},{1,0},{2,3},{3,2},{4,5},{5,4},{6,7},{7,6},{8,9},{9,8},{10,11... | collective-permute-start | bytes 589832 | tf_op jit(solution)/shard_map/ppermute | solution.py:140
  94.2 3.0 %apply.4.rest_0_ = bf16[1024,1024]{1,0:T(8,128)(2,1)} custom-call(s32[3]{0:T(128)S(1)} %pad_add_fusion.ids, bf16[2,2,96,256]{3,2,1,0:T(8,128)(2,1)S(1)} %pad_maximum_fusion.2.near_low, bf16[2,2,96,256]{3,2,1,0:T(8,128)(2,1)S(1)} %pad_maximum_fusion.4.near_high, bf16[2,2,96,256]{3,2,1,0:T(8,128)(2,1)S(1)} %collective-permute-done.29.far_low, ...), custom_call_target="tpu_custom_call" | custom-call | flops 805306368 | bytes 1048576 | tf_op jit(solution)/shard_map/apply/pallas_call | solution.py:509
  97.2 0.2 collective-permute-start.34
  97.5 0.3 collective-permute-start.40
  97.8 0.2 collective-permute-start.26
  98.1 0.3 collective-permute-start.31
  98.3 0.2 collective-permute-start.33
  98.6 3.0 %apply.5.rest_0_ = bf16[1024,1024]{1,0:T(8,128)(2,1)} custom-call(s32[3]{0:T(128)S(1)} %pad_add_fusion.ids, bf16[2,2,96,256]{3,2,1,0:T(8,128)(2,1)S(1)} %collective-permute-done.35.near_low, bf16[2,2,96,256]{3,2,1,0:T(8,128)(2,1)S(1)} %collective-permute-done.36.near_high, ...), custom_call_target="tpu_custom_call", output_to_operand_aliasing={{}: (6, {})} | custom-call | flops 805306368 | bytes 1048576 | tf_op jit(solution)/shard_map/apply/pallas_call | solution.py:509
  101.6 2.1 %collective-permute-done.34.far_high = bf16[2,2,96,256]{3,2,1,0:T(8,128)(2,1)S(1)} collective-permute-done((bf16[2,2,96,256]{3,2,1,0:T(8,128)(2,1)S(1)}, bf16[2,2,96,256]{3,2,1,0:T(8,128)(2,1)S(1)}, u32[]{:S(2)}, u32[]{:S(2)}) %collective-permute-start.34) | collective-permute-done | bytes 196640 | tf_op jit(solution)/shard_map/ppermute | solution.py:140
  103.7 0.8 collective-permute-start.39
  104.5 1.3 %finish.1 = (f32[4,16,1024]{2,1,0:T(8,128)}, f32[4,32,256]{2,1,0:T(8,128)}) custom-call(s32[3]{0:T(128)S(1)} %pad_add_fusion.ids, f32[2,96,256]{2,1,0:T(8,128)S(1)} %get-tuple-element.73.one, f32[2,96,256]{2,1,0:T(8,128)S(1)} %get-tuple-element.74.two, f32[2,96,256]{2,1,0:T(8,128)S(1)} %collective-permute-done.40.came), custom_call_target="tpu_custom_call" | custom-call | tf_op jit(solution)/shard_map/finish/pallas_call | solution.py:541
  105.8 3.0 %apply.6.rest_0_ = bf16[1024,1024]{1,0:T(8,128)(2,1)} custom-call(s32[3]{0:T(128)S(1)} %pad_add_fusion.ids, bf16[2,2,96,256]{3,2,1,0:T(8,128)(2,1)S(1)} %pad_maximum_fusion.3.near_low, bf16[2,2,96,256]{3,2,1,0:T(8,128)(2,1)S(1)} %pad_maximum_fusion.5.near_high, ...), custom_call_target="tpu_custom_call", output_to_operand_aliasing={{}: (6, {})} | custom-call | flops 805306368 | bytes 1048576 | tf_op jit(solution)/shard_map/apply/pallas_call | solution.py:509
  108.9 3.0 %apply.7 = bf16[1024,1024]{1,0:T(8,128)(2,1)} custom-call(s32[3]{0:T(128)S(1)} %pad_add_fusion.ids, bf16[2,2,96,256]{3,2,1,0:T(8,128)(2,1)S(1)} %collective-permute-done.26.near_low, bf16[2,2,96,256]{3,2,1,0:T(8,128)(2,1)S(1)} %collective-permute-done.31.near_high, ...), custom_call_target="tpu_custom_call", output_to_operand_aliasing={{}: (6, {})} | custom-call | flops 805306368 | bytes 1048576 | tf_op jit(solution)/shard_map/apply/pallas_call | solution.py:509
  (57 shorter events, 0.7 us)
Async XLA Ops:
  0.6 6.0 %copy-start.5 = (f32[4,1024]{1,0:T(4,128)S(1)}, f32[4,1024]{1,0:T(4,128)}, u32[]{:S(2)}) copy-start(f32[4,1024]{1,0:T(4,128)} %rest_0_.1) | copy-start | bytes 49156
  0.7 1.0 copy-start.3
  1.7 0.9 copy-start.4
  3.4 1.6 %copy-start.1 = (bf16[1024,1024]{1,0:T(8,128)(2,1)S(1)}, bf16[1024,1024]{1,0:T(8,128)(2,1)}, u32[]{:S(2)}) copy-start(bf16[1024,1024]{1,0:T(8,128)(2,1)} %x_ref.2) | copy-start | bytes 6291460
  5.0 1.6 %copy-start.2 = (bf16[1024,1024]{1,0:T(8,128)(2,1)S(1)}, bf16[1024,1024]{1,0:T(8,128)(2,1)}, u32[]{:S(2)}) copy-start(bf16[1024,1024]{1,0:T(8,128)(2,1)} %x_ref.3) | copy-start | bytes 6291460
  6.5 23.3 %collective-permute-start.10 = (bf16[1024,512]{1,0:T(8,128)(2,1)S(1)}, bf16[1024,512]{1,0:T(8,128)(2,1)S(1)}, u32[]{:S(2)}, u32[]{:S(2)}) collective-permute-start(bf16[1024,512]{1,0:T(8,128)(2,1)S(1)} %get-tuple-element.43), channel_id=1, source_target_pairs={{0,1},{1,0},{2,3},{3,2},{4,5},{5,4},{6,7},{7,6},{8,9},{9,8},{10,11... | collective-permute-start | bytes 3145736 | tf_op jit(solution)/shard_map/ppermute | solution.py:140
  8.9 21.2 %collective-permute-start.11 = (bf16[1024,512]{1,0:T(8,128)(2,1)S(1)}, bf16[1024,512]{1,0:T(8,128)(2,1)S(1)}, u32[]{:S(2)}, u32[]{:S(2)}) collective-permute-start(bf16[1024,512]{1,0:T(8,128)(2,1)S(1)} %get-tuple-element.44), channel_id=1, source_target_pairs={{0,1},{1,0},{2,3},{3,2},{4,5},{5,4},{6,7},{7,6},{8,9},{9,8},{10,11... | collective-permute-start | bytes 3145736 | tf_op jit(solution)/shard_map/ppermute | solution.py:140
  9.4 2.6 %collective-permute-start = (f32[2,96,256]{2,1,0:T(8,128)S(1)}, f32[2,96,256]{2,1,0:T(8,128)S(1)}, u32[]{:S(2)}, u32[]{:S(2)}) collective-permute-start(f32[2,96,256]{2,1,0:T(8,128)S(1)} %get-tuple-element.41), channel_id=1, source_target_pairs={{0,1},{1,0},{2,3},{3,2},{4,5},{5,4},{6,7},{7,6},{8,9},{9,8},{10,11... | collective-permute-start | bytes 589832 | tf_op jit(solution)/shard_map/ppermute | solution.py:140
  12.0 5.8 %collective-permute-start.1 = (bf16[2,96,256]{2,1,0:T(8,128)(2,1)S(1)}, bf16[2,96,256]{2,1,0:T(8,128)(2,1)S(1)}, u32[]{:S(2)}, u32[]{:S(2)}) collective-permute-start(bf16[2,96,256]{2,1,0:T(8,128)(2,1)S(1)} %get-tuple-element.47), channel_id=1, source_target_pairs={{0,4},{1,5},{2,6},{3,7},{4,0},{5,1},{6,2},{7,3},{8,12},{9,13},{10,... | collective-permute-start | bytes 294920 | tf_op jit(solution)/shard_map/ppermute | solution.py:140
  14.8 4.8 %collective-permute-start.3 = (bf16[2,96,256]{2,1,0:T(8,128)(2,1)S(1)}, bf16[2,96,256]{2,1,0:T(8,128)(2,1)S(1)}, u32[]{:S(2)}, u32[]{:S(2)}) collective-permute-start(bf16[2,96,256]{2,1,0:T(8,128)(2,1)S(1)} %get-tuple-element.47), channel_id=1, source_target_pairs={{0,8},{1,9},{2,10},{3,11},{4,12},{5,13},{6,14},{7,15},{8,0},{9,1},... | collective-permute-start | bytes 294920 | tf_op jit(solution)/shard_map/ppermute | solution.py:140
  17.1 6.9 %collective-permute-start.4 = (bf16[2,96,256]{2,1,0:T(8,128)(2,1)S(1)}, bf16[2,96,256]{2,1,0:T(8,128)(2,1)S(1)}, u32[]{:S(2)}, u32[]{:S(2)}) collective-permute-start(bf16[2,96,256]{2,1,0:T(8,128)(2,1)S(1)} %get-tuple-element.47), channel_id=1, source_target_pairs={{0,12},{1,13},{2,14},{3,15},{4,8},{5,9},{6,10},{7,11},{8,4},{9,5},... | collective-permute-start | bytes 294920 | tf_op jit(solution)/shard_map/ppermute | solution.py:140
  17.8 6.2 %collective-permute-start.5 = (bf16[2,2,96,256]{3,2,1,0:T(8,128)(2,1)S(1)}, bf16[2,2,96,256]{3,2,1,0:T(8,128)(2,1)S(1)}, u32[]{:S(2)}, u32[]{:S(2)}) collective-permute-start(bf16[2,2,96,256]{3,2,1,0:T(8,128)(2,1)S(1)} %pad_maximum_fusion.near_low), channel_id=1, source_target_pairs={{0,2},{1,3},{2,0},{3,1},{4,6},{5,7},{6,4},{7,5},{8,10},{9,11},{10,... | collective-permute-start | bytes 589832 | tf_op jit(solution)/shard_map/ppermute | solution.py:140
  24.0 4.6 %collective-permute-start.8 = (bf16[2,2,96,256]{3,2,1,0:T(8,128)(2,1)S(1)}, bf16[2,2,96,256]{3,2,1,0:T(8,128)(2,1)S(1)}, u32[]{:S(2)}, u32[]{:S(2)}) collective-permute-start(bf16[2,2,96,256]{3,2,1,0:T(8,128)(2,1)S(1)} %pad_maximum_fusion.1.near_high), channel_id=1, source_target_pairs={{0,2},{1,3},{2,0},{3,1},{4,6},{5,7},{6,4},{7,5},{8,10},{9,11},{10,... | collective-permute-start | bytes 589832 | tf_op jit(solution)/shard_map/ppermute | solution.py:140
  25.3 11.8 %collective-permute-start.2 = (bf16[2,2,96,256]{3,2,1,0:T(8,128)(2,1)S(1)}, bf16[2,2,96,256]{3,2,1,0:T(8,128)(2,1)S(1)}, u32[]{:S(2)}, u32[]{:S(2)}) collective-permute-start(bf16[2,2,96,256]{3,2,1,0:T(8,128)(2,1)S(1)} %pad_maximum_fusion.near_low), channel_id=1, source_target_pairs={{0,16},{16,0},{1,17},{17,1},{2,18},{18,2},{3,19},{19,3},{4,20},{20... | collective-permute-start | bytes 589832 | tf_op jit(solution)/shard_map/ppermute | solution.py:144
  26.5 10.8 %collective-permute-start.6 = (bf16[2,2,96,256]{3,2,1,0:T(8,128)(2,1)S(1)}, bf16[2,2,96,256]{3,2,1,0:T(8,128)(2,1)S(1)}, u32[]{:S(2)}, u32[]{:S(2)}) collective-permute-start(bf16[2,2,96,256]{3,2,1,0:T(8,128)(2,1)S(1)} %pad_maximum_fusion.1.near_high), channel_id=1, source_target_pairs={{0,16},{16,0},{1,17},{17,1},{2,18},{18,2},{3,19},{19,3},{4,20},{20... | collective-permute-start | bytes 589832 | tf_op jit(solution)/shard_map/ppermute | solution.py:144
  28.6 9.4 %collective-permute-start.7 = (bf16[2,2,96,256]{3,2,1,0:T(8,128)(2,1)S(1)}, bf16[2,2,96,256]{3,2,1,0:T(8,128)(2,1)S(1)}, u32[]{:S(2)}, u32[]{:S(2)}) collective-permute-start(bf16[2,2,96,256]{3,2,1,0:T(8,128)(2,1)S(1)} %collective-permute-done.5.far_low), channel_id=1, source_target_pairs={{0,16},{16,0},{1,17},{17,1},{2,18},{18,2},{3,19},{19,3},{4,20},{20... | collective-permute-start | bytes 589832 | tf_op jit(solution)/shard_map/ppermute | solution.py:144
  29.8 12.4 %collective-permute-start.9 = (bf16[2,2,96,256]{3,2,1,0:T(8,128)(2,1)S(1)}, bf16[2,2,96,256]{3,2,1,0:T(8,128)(2,1)S(1)}, u32[]{:S(2)}, u32[]{:S(2)}) collective-permute-start(bf16[2,2,96,256]{3,2,1,0:T(8,128)(2,1)S(1)} %collective-permute-done.8.far_high), channel_id=1, source_target_pairs={{0,16},{16,0},{1,17},{17,1},{2,18},{18,2},{3,19},{19,3},{4,20},{20... | collective-permute-start | bytes 589832 | tf_op jit(solution)/shard_map/ppermute | solution.py:144
  35.9 13.8 %collective-permute-start.19 = (bf16[2,2,96,256]{3,2,1,0:T(8,128)(2,1)S(1)}, bf16[2,2,96,256]{3,2,1,0:T(8,128)(2,1)S(1)}, u32[]{:S(2)}, u32[]{:S(2)}) collective-permute-start(bf16[2,2,96,256]{3,2,1,0:T(8,128)(2,1)S(1)} %get-tuple-element.64), channel_id=1, source_target_pairs={{0,2},{1,3},{2,0},{3,1},{4,6},{5,7},{6,4},{7,5},{8,10},{9,11},{10,... | collective-permute-start | bytes 589832 | tf_op jit(solution)/shard_map/ppermute | solution.py:140
  37.2 17.7 %collective-permute-start.17 = (bf16[2,2,96,256]{3,2,1,0:T(8,128)(2,1)S(1)}, bf16[2,2,96,256]{3,2,1,0:T(8,128)(2,1)S(1)}, u32[]{:S(2)}, u32[]{:S(2)}) collective-permute-start(bf16[2,2,96,256]{3,2,1,0:T(8,128)(2,1)S(1)} %get-tuple-element.61), channel_id=1, source_target_pairs={{0,2},{1,3},{2,0},{3,1},{4,6},{5,7},{6,4},{7,5},{8,10},{9,11},{10,... | collective-permute-start | bytes 589832 | tf_op jit(solution)/shard_map/ppermute | solution.py:140
  48.1 6.8 %collective-permute-start.14 = (bf16[2,2,96,256]{3,2,1,0:T(8,128)(2,1)S(1)}, bf16[2,2,96,256]{3,2,1,0:T(8,128)(2,1)S(1)}, u32[]{:S(2)}, u32[]{:S(2)}) collective-permute-start(bf16[2,2,96,256]{3,2,1,0:T(8,128)(2,1)S(1)} %get-tuple-element.55), channel_id=1, source_target_pairs={{0,2},{1,3},{2,0},{3,1},{4,6},{5,7},{6,4},{7,5},{8,10},{9,11},{10,... | collective-permute-start | bytes 589832 | tf_op jit(solution)/shard_map/ppermute | solution.py:140
  48.4 9.0 %collective-permute-start.12 = (bf16[2,2,96,256]{3,2,1,0:T(8,128)(2,1)S(1)}, bf16[2,2,96,256]{3,2,1,0:T(8,128)(2,1)S(1)}, u32[]{:S(2)}, u32[]{:S(2)}) collective-permute-start(bf16[2,2,96,256]{3,2,1,0:T(8,128)(2,1)S(1)} %get-tuple-element.52), channel_id=1, source_target_pairs={{0,2},{1,3},{2,0},{3,1},{4,6},{5,7},{6,4},{7,5},{8,10},{9,11},{10,... | collective-permute-start | bytes 589832 | tf_op jit(solution)/shard_map/ppermute | solution.py:140
  49.7 9.7 %collective-permute-start.20 = (bf16[2,96,256]{2,1,0:T(8,128)(2,1)S(1)}, bf16[2,96,256]{2,1,0:T(8,128)(2,1)S(1)}, u32[]{:S(2)}, u32[]{:S(2)}) collective-permute-start(bf16[2,96,256]{2,1,0:T(8,128)(2,1)S(1)} %get-tuple-element.65), channel_id=1, source_target_pairs={{0,8},{1,9},{2,10},{3,11},{4,12},{5,13},{6,14},{7,15},{8,0},{9,1},... | collective-permute-start | bytes 294920 | tf_op jit(solution)/shard_map/ppermute | solution.py:140
  53.7 7.0 %collective-permute-start.21 = (bf16[2,96,256]{2,1,0:T(8,128)(2,1)S(1)}, bf16[2,96,256]{2,1,0:T(8,128)(2,1)S(1)}, u32[]{:S(2)}, u32[]{:S(2)}) collective-permute-start(bf16[2,96,256]{2,1,0:T(8,128)(2,1)S(1)} %get-tuple-element.66), channel_id=1, source_target_pairs={{0,12},{1,13},{2,14},{3,15},{4,8},{5,9},{6,10},{7,11},{8,4},{9,5},... | collective-permute-start | bytes 294920 | tf_op jit(solution)/shard_map/ppermute | solution.py:140
  54.9 5.8 %collective-permute-start.18 = (bf16[2,96,256]{2,1,0:T(8,128)(2,1)S(1)}, bf16[2,96,256]{2,1,0:T(8,128)(2,1)S(1)}, u32[]{:S(2)}, u32[]{:S(2)}) collective-permute-start(bf16[2,96,256]{2,1,0:T(8,128)(2,1)S(1)} %get-tuple-element.63), channel_id=1, source_target_pairs={{0,4},{1,5},{2,6},{3,7},{4,0},{5,1},{6,2},{7,3},{8,12},{9,13},{10,... | collective-permute-start | bytes 294920 | tf_op jit(solution)/shard_map/ppermute | solution.py:140
  55.0 39.1 %copy-start = (bf16[1024,1024]{1,0:T(8,128)(2,1)S(1)}, bf16[1024,1024]{1,0:T(8,128)(2,1)}, u32[]{:S(2)}) copy-start(bf16[1024,1024]{1,0:T(8,128)(2,1)} %q_ref.7) | copy-start | bytes 6291460
  55.0 10.5 %collective-permute-start.15 = (bf16[2,96,256]{2,1,0:T(8,128)(2,1)S(1)}, bf16[2,96,256]{2,1,0:T(8,128)(2,1)S(1)}, u32[]{:S(2)}, u32[]{:S(2)}) collective-permute-start(bf16[2,96,256]{2,1,0:T(8,128)(2,1)S(1)} %get-tuple-element.56), channel_id=1, source_target_pairs={{0,8},{1,9},{2,10},{3,11},{4,12},{5,13},{6,14},{7,15},{8,0},{9,1},... | collective-permute-start | bytes 294920 | tf_op jit(solution)/shard_map/ppermute | solution.py:140
  57.5 10.0 %collective-permute-start.16 = (bf16[2,96,256]{2,1,0:T(8,128)(2,1)S(1)}, bf16[2,96,256]{2,1,0:T(8,128)(2,1)S(1)}, u32[]{:S(2)}, u32[]{:S(2)}) collective-permute-start(bf16[2,96,256]{2,1,0:T(8,128)(2,1)S(1)} %get-tuple-element.57), channel_id=1, source_target_pairs={{0,12},{1,13},{2,14},{3,15},{4,8},{5,9},{6,10},{7,11},{8,4},{9,5},... | collective-permute-start | bytes 294920 | tf_op jit(solution)/shard_map/ppermute | solution.py:140
  59.4 8.1 %collective-permute-start.13 = (bf16[2,96,256]{2,1,0:T(8,128)(2,1)S(1)}, bf16[2,96,256]{2,1,0:T(8,128)(2,1)S(1)}, u32[]{:S(2)}, u32[]{:S(2)}) collective-permute-start(bf16[2,96,256]{2,1,0:T(8,128)(2,1)S(1)} %get-tuple-element.54), channel_id=1, source_target_pairs={{0,4},{1,5},{2,6},{3,7},{4,0},{5,1},{6,2},{7,3},{8,12},{9,13},{10,... | collective-permute-start | bytes 294920 | tf_op jit(solution)/shard_map/ppermute | solution.py:140
  60.8 6.9 %collective-permute-start.22 = (bf16[2,96,256]{2,1,0:T(8,128)(2,1)S(1)}, bf16[2,96,256]{2,1,0:T(8,128)(2,1)S(1)}, u32[]{:S(2)}, u32[]{:S(2)}) collective-permute-start(bf16[2,96,256]{2,1,0:T(8,128)(2,1)S(1)} %get-tuple-element.67), channel_id=1, source_target_pairs={{0,4},{1,5},{2,6},{3,7},{4,0},{5,1},{6,2},{7,3},{8,12},{9,13},{10,... | collective-permute-start | bytes 294920 | tf_op jit(solution)/shard_map/ppermute | solution.py:140
  61.1 12.8 %collective-permute-start.24 = (bf16[2,96,256]{2,1,0:T(8,128)(2,1)S(1)}, bf16[2,96,256]{2,1,0:T(8,128)(2,1)S(1)}, u32[]{:S(2)}, u32[]{:S(2)}) collective-permute-start(bf16[2,96,256]{2,1,0:T(8,128)(2,1)S(1)} %get-tuple-element.67), channel_id=1, source_target_pairs={{0,8},{1,9},{2,10},{3,11},{4,12},{5,13},{6,14},{7,15},{8,0},{9,1},... | collective-permute-start | bytes 294920 | tf_op jit(solution)/shard_map/ppermute | solution.py:140
  65.5 8.4 %collective-permute-start.25 = (bf16[2,96,256]{2,1,0:T(8,128)(2,1)S(1)}, bf16[2,96,256]{2,1,0:T(8,128)(2,1)S(1)}, u32[]{:S(2)}, u32[]{:S(2)}) collective-permute-start(bf16[2,96,256]{2,1,0:T(8,128)(2,1)S(1)} %get-tuple-element.67), channel_id=1, source_target_pairs={{0,12},{1,13},{2,14},{3,15},{4,8},{5,9},{6,10},{7,11},{8,4},{9,5},... | collective-permute-start | bytes 294920 | tf_op jit(solution)/shard_map/ppermute | solution.py:140
  67.7 8.6 %collective-permute-start.23 = (bf16[2,96,256]{2,1,0:T(8,128)(2,1)S(1)}, bf16[2,96,256]{2,1,0:T(8,128)(2,1)S(1)}, u32[]{:S(2)}, u32[]{:S(2)}) collective-permute-start(bf16[2,96,256]{2,1,0:T(8,128)(2,1)S(1)} %get-tuple-element.70), channel_id=1, source_target_pairs={{0,4},{1,5},{2,6},{3,7},{4,0},{5,1},{6,2},{7,3},{8,12},{9,13},{10,... | collective-permute-start | bytes 294920 | tf_op jit(solution)/shard_map/ppermute | solution.py:140
  76.3 11.2 %collective-permute-start.27 = (bf16[2,96,256]{2,1,0:T(8,128)(2,1)S(1)}, bf16[2,96,256]{2,1,0:T(8,128)(2,1)S(1)}, u32[]{:S(2)}, u32[]{:S(2)}) collective-permute-start(bf16[2,96,256]{2,1,0:T(8,128)(2,1)S(1)} %get-tuple-element.70), channel_id=1, source_target_pairs={{0,8},{1,9},{2,10},{3,11},{4,12},{5,13},{6,14},{7,15},{8,0},{9,1},... | collective-permute-start | bytes 294920 | tf_op jit(solution)/shard_map/ppermute | solution.py:140
  78.3 10.8 %collective-permute-start.28 = (bf16[2,96,256]{2,1,0:T(8,128)(2,1)S(1)}, bf16[2,96,256]{2,1,0:T(8,128)(2,1)S(1)}, u32[]{:S(2)}, u32[]{:S(2)}) collective-permute-start(bf16[2,96,256]{2,1,0:T(8,128)(2,1)S(1)} %get-tuple-element.70), channel_id=1, source_target_pairs={{0,12},{1,13},{2,14},{3,15},{4,8},{5,9},{6,10},{7,11},{8,4},{9,5},... | collective-permute-start | bytes 294920 | tf_op jit(solution)/shard_map/ppermute | solution.py:140
  78.6 10.8 %collective-permute-start.30 = (bf16[2,2,96,256]{3,2,1,0:T(8,128)(2,1)S(1)}, bf16[2,2,96,256]{3,2,1,0:T(8,128)(2,1)S(1)}, u32[]{:S(2)}, u32[]{:S(2)}) collective-permute-start(bf16[2,2,96,256]{3,2,1,0:T(8,128)(2,1)S(1)} %pad_maximum_fusion.4.near_high), channel_id=1, source_target_pairs={{0,2},{1,3},{2,0},{3,1},{4,6},{5,7},{6,4},{7,5},{8,10},{9,11},{10,... | collective-permute-start | bytes 589832 | tf_op jit(solution)/shard_map/ppermute | solution.py:140
  78.8 12.3 %collective-permute-start.29 = (bf16[2,2,96,256]{3,2,1,0:T(8,128)(2,1)S(1)}, bf16[2,2,96,256]{3,2,1,0:T(8,128)(2,1)S(1)}, u32[]{:S(2)}, u32[]{:S(2)}) collective-permute-start(bf16[2,2,96,256]{3,2,1,0:T(8,128)(2,1)S(1)} %pad_maximum_fusion.2.near_low), channel_id=1, source_target_pairs={{0,2},{1,3},{2,0},{3,1},{4,6},{5,7},{6,4},{7,5},{8,10},{9,11},{10,... | collective-permute-start | bytes 589832 | tf_op jit(solution)/shard_map/ppermute | solution.py:140
  80.0 17.2 %collective-permute-start.36 = (bf16[2,2,96,256]{3,2,1,0:T(8,128)(2,1)S(1)}, bf16[2,2,96,256]{3,2,1,0:T(8,128)(2,1)S(1)}, u32[]{:S(2)}, u32[]{:S(2)}) collective-permute-start(bf16[2,2,96,256]{3,2,1,0:T(8,128)(2,1)S(1)} %pad_maximum_fusion.4.near_high), channel_id=1, source_target_pairs={{0,1},{1,0},{2,3},{3,2},{4,5},{5,4},{6,7},{7,6},{8,9},{9,8},{10,11... | collective-permute-start | bytes 589832 | tf_op jit(solution)/shard_map/ppermute | solution.py:140
  87.4 10.0 %collective-permute-start.35 = (bf16[2,2,96,256]{3,2,1,0:T(8,128)(2,1)S(1)}, bf16[2,2,96,256]{3,2,1,0:T(8,128)(2,1)S(1)}, u32[]{:S(2)}, u32[]{:S(2)}) collective-permute-start(bf16[2,2,96,256]{3,2,1,0:T(8,128)(2,1)S(1)} %pad_maximum_fusion.2.near_low), channel_id=1, source_target_pairs={{0,1},{1,0},{2,3},{3,2},{4,5},{5,4},{6,7},{7,6},{8,9},{9,8},{10,11... | collective-permute-start | bytes 589832 | tf_op jit(solution)/shard_map/ppermute | solution.py:140
  89.1 8.8 %collective-permute-start.32 = (bf16[2,2,96,256]{3,2,1,0:T(8,128)(2,1)S(1)}, bf16[2,2,96,256]{3,2,1,0:T(8,128)(2,1)S(1)}, u32[]{:S(2)}, u32[]{:S(2)}) collective-permute-start(bf16[2,2,96,256]{3,2,1,0:T(8,128)(2,1)S(1)} %pad_maximum_fusion.3.near_low), channel_id=1, source_target_pairs={{0,2},{1,3},{2,0},{3,1},{4,6},{5,7},{6,4},{7,5},{8,10},{9,11},{10,... | collective-permute-start | bytes 589832 | tf_op jit(solution)/shard_map/ppermute | solution.py:140
  89.3 8.7 %collective-permute-start.38 = (bf16[2,2,96,256]{3,2,1,0:T(8,128)(2,1)S(1)}, bf16[2,2,96,256]{3,2,1,0:T(8,128)(2,1)S(1)}, u32[]{:S(2)}, u32[]{:S(2)}) collective-permute-start(bf16[2,2,96,256]{3,2,1,0:T(8,128)(2,1)S(1)} %collective-permute-done.30.far_high), channel_id=1, source_target_pairs={{0,1},{1,0},{2,3},{3,2},{4,5},{5,4},{6,7},{7,6},{8,9},{9,8},{10,11... | collective-permute-start | bytes 589832 | tf_op jit(solution)/shard_map/ppermute | solution.py:140
  91.1 7.3 %collective-permute-start.37 = (bf16[2,2,96,256]{3,2,1,0:T(8,128)(2,1)S(1)}, bf16[2,2,96,256]{3,2,1,0:T(8,128)(2,1)S(1)}, u32[]{:S(2)}, u32[]{:S(2)}) collective-permute-start(bf16[2,2,96,256]{3,2,1,0:T(8,128)(2,1)S(1)} %collective-permute-done.29.far_low), channel_id=1, source_target_pairs={{0,1},{1,0},{2,3},{3,2},{4,5},{5,4},{6,7},{7,6},{8,9},{9,8},{10,11... | collective-permute-start | bytes 589832 | tf_op jit(solution)/shard_map/ppermute | solution.py:140
  97.2 6.5 %collective-permute-start.34 = (bf16[2,2,96,256]{3,2,1,0:T(8,128)(2,1)S(1)}, bf16[2,2,96,256]{3,2,1,0:T(8,128)(2,1)S(1)}, u32[]{:S(2)}, u32[]{:S(2)}) collective-permute-start(bf16[2,2,96,256]{3,2,1,0:T(8,128)(2,1)S(1)} %pad_maximum_fusion.5.near_high), channel_id=1, source_target_pairs={{0,2},{1,3},{2,0},{3,1},{4,6},{5,7},{6,4},{7,5},{8,10},{9,11},{10,... | collective-permute-start | bytes 589832 | tf_op jit(solution)/shard_map/ppermute | solution.py:140
  97.5 7.0 %collective-permute-start.40 = (f32[2,96,256]{2,1,0:T(8,128)S(1)}, f32[2,96,256]{2,1,0:T(8,128)S(1)}, u32[]{:S(2)}, u32[]{:S(2)}) collective-permute-start(f32[2,96,256]{2,1,0:T(8,128)S(1)} %pad_maximum_fusion.6), channel_id=1, source_target_pairs={{0,1},{1,0},{2,3},{3,2},{4,5},{5,4},{6,7},{7,6},{8,9},{9,8},{10,11... | collective-permute-start | bytes 589832 | tf_op jit(solution)/shard_map/ppermute | solution.py:140
  97.8 11.0 %collective-permute-start.26 = (bf16[2,2,96,256]{3,2,1,0:T(8,128)(2,1)S(1)}, bf16[2,2,96,256]{3,2,1,0:T(8,128)(2,1)S(1)}, u32[]{:S(2)}, u32[]{:S(2)}) collective-permute-start(bf16[2,2,96,256]{3,2,1,0:T(8,128)(2,1)S(1)} %pad_maximum_fusion.3.near_low), channel_id=1, source_target_pairs={{0,1},{1,0},{2,3},{3,2},{4,5},{5,4},{6,7},{7,6},{8,9},{9,8},{10,11... | collective-permute-start | bytes 589832 | tf_op jit(solution)/shard_map/ppermute | solution.py:140
  98.1 10.8 %collective-permute-start.31 = (bf16[2,2,96,256]{3,2,1,0:T(8,128)(2,1)S(1)}, bf16[2,2,96,256]{3,2,1,0:T(8,128)(2,1)S(1)}, u32[]{:S(2)}, u32[]{:S(2)}) collective-permute-start(bf16[2,2,96,256]{3,2,1,0:T(8,128)(2,1)S(1)} %pad_maximum_fusion.5.near_high), channel_id=1, source_target_pairs={{0,1},{1,0},{2,3},{3,2},{4,5},{5,4},{6,7},{7,6},{8,9},{9,8},{10,11... | collective-permute-start | bytes 589832 | tf_op jit(solution)/shard_map/ppermute | solution.py:140
  98.3 10.5 %collective-permute-start.33 = (bf16[2,2,96,256]{3,2,1,0:T(8,128)(2,1)S(1)}, bf16[2,2,96,256]{3,2,1,0:T(8,128)(2,1)S(1)}, u32[]{:S(2)}, u32[]{:S(2)}) collective-permute-start(bf16[2,2,96,256]{3,2,1,0:T(8,128)(2,1)S(1)} %collective-permute-done.32.far_low), channel_id=1, source_target_pairs={{0,1},{1,0},{2,3},{3,2},{4,5},{5,4},{6,7},{7,6},{8,9},{9,8},{10,11... | collective-permute-start | bytes 589832 | tf_op jit(solution)/shard_map/ppermute | solution.py:140
  103.7 5.2 %collective-permute-start.39 = (bf16[2,2,96,256]{3,2,1,0:T(8,128)(2,1)S(1)}, bf16[2,2,96,256]{3,2,1,0:T(8,128)(2,1)S(1)}, u32[]{:S(2)}, u32[]{:S(2)}) collective-permute-start(bf16[2,2,96,256]{3,2,1,0:T(8,128)(2,1)S(1)} %collective-permute-done.34.far_high), channel_id=1, source_target_pairs={{0,1},{1,0},{2,3},{3,2},{4,5},{5,4},{6,7},{7,6},{8,9},{9,8},{10,11... | collective-permute-start | bytes 589832 | tf_op jit(solution)/shard_map/ppermute | solution.py:140

commit v5 on v4

--- a/solution.py
+++ b/solution.py
@@ -473,46 +473,44 @@
     )(master, kept, one, two, three)
 
 
-def apply_kernel(other, ids, near_low, near_high, far_low, far_high, q_ref, *rest):
+def apply_kernel(order, other, ids, near_low, near_high, far_low, far_high, q_ref, *rest):
     o_ref, w_in, w_out = rest[-3:]
     chip, core = ids[0], ids[1]
-    fast = w_out.shape[0]
-
-    @pl.when(pl.program_id(0) == 0)
-    def _():
-        lines = (near_low, near_high, far_low, far_high)
-        assemble(chip, jnp.bitwise_xor(core, other), lines, w_in, w_out)
-
-    query = normalize_head(q_ref[...])
-    in_root = 1.0 / math.sqrt(w_out.shape[1])
-    gate = jnp.dot(query, w_in[:, :fast], preferred_element_type=F32) * in_root
-    upper = jnp.dot(query, w_in[:, fast:], preferred_element_type=F32) * in_root
-    hidden = (gate * (0.5 * jnp.tanh(0.5 * gate) + 0.5) * upper).astype(BF16)
-    result = jnp.dot(hidden, w_out[...], preferred_element_type=F32) * (1.0 / math.sqrt(fast))
-    o_ref[...] = result.astype(BF16)
+    fast, size = w_out.shape
+    lines = (near_low, near_high, far_low, far_high)
+    assemble(chip, jnp.bitwise_xor(core, other), lines, w_in, w_out)
+    columns = pl.ds(pl.multiple_of(head_of(ids, order, other) * size, size), size)
+    in_root = 1.0 / math.sqrt(size)
+    out_root = 1.0 / math.sqrt(fast)
+    step = 512
+    for start in range(0, q_ref.shape[0], step):
+        rows = slice(start, start + step)
+        query = normalize_head(q_ref[rows, columns])
+        gate = jnp.dot(query, w_in[:, :fast], preferred_element_type=F32) * in_root
+        upper = jnp.dot(query, w_in[:, fast:], preferred_element_type=F32) * in_root
+        hidden = (gate * (0.5 * jnp.tanh(0.5 * gate) + 0.5) * upper).astype(BF16)
+        result = jnp.dot(hidden, w_out[...], preferred_element_type=F32) * out_root
+        o_ref[rows, :] = result.astype(BF16)
 
 
 def apply_fast(ids, order, other, lines, queries, output, fast):
     rows, width = queries.shape
-    pair_shape = lines[0].shape
-    size = pair_shape[-1]
-    step = 512
-    whole = pl.BlockSpec(pair_shape, lambda i, ids: (0, 0, 0, 0))
-    column = pl.BlockSpec((step, size), lambda i, ids: (i, 2 * (ids[1] ^ other) + (ids[2] ^ order)))
+    size = lines[0].shape[-1]
+    inside = pl.BlockSpec(memory_space=pltpu.VMEM)
     operands = [ids, *lines, queries]
-    specs = [whole] * 4 + [column]
+    specs = [inside] * 5
     aliases = {}
     if output is not None:
         operands.append(output)
         specs.append(pl.BlockSpec(memory_space=pl.ANY))
         aliases = {6: 0}
     return pl.pallas_call(
-        functools.partial(apply_kernel, other),
+        functools.partial(apply_kernel, order, other),
         grid_spec=pltpu.PrefetchScalarGridSpec(
             num_scalar_prefetch=1,
-            grid=(rows // step,),
+            grid=(1,),
             in_specs=specs,
-            out_specs=column,
+            out_specs=pl.BlockSpec((rows, size), lambda i, ids: (0, head_of(ids, order, other))),
             scratch_shapes=[pltpu.VMEM((size, 2 * fast), BF16), pltpu.VMEM((fast, size), BF16)],
         ),
         out_shape=jax.ShapeDtypeStruct((rows, width), BF16),
@@ -579,16 +577,13 @@
     second = tuple(swap_parts(piece) for piece in first)
     k_got, v_got = swap(k_send, 1), swap(v_send, 1)
 
-    kept, low, high = [], [], []
-    for order, lines in enumerate((first, second)):
-        a, b, c = increments(ids, order, lines, k_own, v_own, k_got, v_got, fast)
-        kept.append(a)
-        low.append(swap(b, 2))
-        high.append(swap(c, 2))
     wide, short = [], []
     for order in range(2):
-        sum2, sum3 = add_pair(kept[order], high[order], 1, BF16)
-        sum0, sum1 = add_pair(kept[order], low[order], 0, F32)
+        lines = second if order else first
+        kept, low, high = increments(ids, order, lines, k_own, v_own, k_got, v_got, fast)
+        high, low = swap(high, 2), swap(low, 2)
+        sum2, sum3 = add_pair(kept, high, 1, BF16)
+        sum0, sum1 = add_pair(kept, low, 0, F32)
         three, two, one = swap(sum3, 12), swap(sum2, 8), swap(sum1, 4)
         a, b = renorm(masters[order], sum0, one, two, three, rows_in)
         wide.append(a)
@@ -606,7 +601,10 @@
     mine = (near_low, near_high, far_low, far_high)
     others = tuple(swap(piece, 1) for piece in mine)
     output = apply_fast(ids, 0, 0, mine, queries, None, fast)
-    near_low, near_high = second_low, after(second_high, output)
+    near_low, near_high = second_low, second_high
+    came = swap(jnp.stack([wide[0][1], wide[1][1]]), 1)
+    updated = finish(ids, wide[0], wide[1], came, fast_in, fast_out)
+    output = after(output, *updated)
     output = apply_fast(ids, 0, 1, others, queries, output, fast)
     far_low, far_high = swap(near_low, 2), swap(near_high, 2)
     far_high = after(far_high, output)
@@ -615,8 +613,7 @@
     output = apply_fast(ids, 1, 0, mine, queries, output, fast)
     output = apply_fast(ids, 1, 1, others, queries, output, fast)
 
-    came = swap(jnp.stack([wide[0][1], wide[1][1]]), 1)
-    return (output, *finish(ids, wide[0], wide[1], came, fast_in, fast_out))
+    return (output, *updated)
 
 
 def per_device(queries, keys, values, step_size, fast_in, fast_out):

time: 112 us -> 110 us (0.982)
  waiting for transfers between devices: 25 us -> 20.6 us
  starting transfers between devices: 52.2 us -> 56.3 us
  Pallas kernels: 30.2 us -> 28.4 us
    ppermute x37, waiting for transfers between devices: 20.2 us -> 15.8 us  [swap(): lax.ppermute(value, 'tok', [(place, place ^ bits) for place in range(coun...]
    ppermute x37, starting transfers between devices: 49.2 us -> 53.4 us  [swap(): lax.ppermute(value, 'tok', [(place, place ^ bits) for place in range(coun...]
    pallas_call x4, Pallas kernels: 12.2 us -> 10.3 us  [apply_fast(): pl.pallas_call(functools.partial(apply_kernel, order, other), grid_spec=p...]
  transfers between devices with their start and end apart: 41 -> 41, of which waited for: 11 -> 10; matrix products, arithmetic and copies ran while one was open for 0% -> 0% of each run, Pallas kernels for 22% -> 21%
where the time goes in v5:
time: 110 us
  starting transfers between devices  56.3 us (51%)
  Pallas kernels  28.4 us (26%)
  waiting for transfers between devices  20.6 us (19%)
  local copies, waits for them, and re-layouts  3.47 us (3%)
    ppermute x37, starting transfers between devices, swap(): lax.ppermute(value, 'tok', [(place, place ^ bits) for place in range(coun...  53.4 us
    ppermute x37, waiting for transfers between devices, swap(): lax.ppermute(value, 'tok', [(place, place ^ bits) for place in range(coun...  15.8 us
    pallas_call x2, Pallas kernels, increments(): pl.pallas_call(increments_kernel, grid_spec=pltpu.PrefetchScalarGridSpec(...  11.7 us
    pallas_call x4, Pallas kernels, apply_fast(): pl.pallas_call(functools.partial(apply_kernel, order, other), grid_spec=p...  10.3 us
    ppermute x4, waiting for transfers between devices, swap_parts(): return lax.ppermute(value, 'parts', [(0, 1), (1, 0)])  4.81 us
    pallas_call x2, Pallas kernels, prepare(): pl.pallas_call(functools.partial(prepare_kernel, heads, block_root), grid...  3.78 us
    unnamed x12, local copies, waits for them, and re-layouts  3.45 us
    ppermute x4, starting transfers between devices, swap_parts(): return lax.ppermute(value, 'parts', [(0, 1), (1, 0)])  2.93 us
  transfers between devices with their start and end apart: 41, of which 10 were waited for; matrix products, arithmetic and copies ran while one was open for 0% of the time, Pallas kernels for 21%

profile of v5, /device:TPU:1, one launch (start us, length us, event | category | flops | bytes accessed | tf_op | source)
XLA Modules:
  0.0 109.9 jit_solution(11205261561276918468)
XLA Ops:
  0.7 0.1 pad_add_fusion.ids
  0.7 0.9 copy-done.3
  1.7 0.9 copy-done.4
  2.6 0.8 pack.1
  3.4 1.6 %copy-done.1 = bf16[1024,1024]{1,0:T(8,128)(2,1)S(1)} copy-done((bf16[1024,1024]{1,0:T(8,128)(2,1)S(1)}, bf16[1024,1024]{1,0:T(8,128)(2,1)}, u32[]{:S(2)}) %copy-start.1) | copy-done | bytes 2097176
  5.0 1.5 %keys.1 = (bf16[1024,512]{1,0:T(8,128)(2,1)S(1)}, bf16[1024,512]{1,0:T(8,128)(2,1)S(1)}) custom-call(s32[3]{0:T(128)S(1)} %pad_add_fusion.ids, bf16[1024,1024]{1,0:T(8,128)(2,1)S(1)} %copy-done.1), custom_call_target="tpu_custom_call" | custom-call | flops 5242880 | bytes 4194304 | tf_op jit(solution)/shard_map/keys/pallas_call | solution.py:255
  6.5 0.1 collective-permute-start.10
  6.6 2.3 %values.1 = (bf16[1024,512]{1,0:T(8,128)(2,1)S(1)}, bf16[1024,512]{1,0:T(8,128)(2,1)S(1)}) custom-call(s32[3]{0:T(128)S(1)} %pad_add_fusion.ids, bf16[1024,1024]{1,0:T(8,128)(2,1)S(1)} %copy-done.2, f32[4,1024]{1,0:T(4,128)S(1)} %copy-done.5), custom_call_target="tpu_custom_call" | custom-call | flops 5242880 | bytes 4194304 | tf_op jit(solution)/shard_map/values/pallas_call | solution.py:255
  8.9 0.5 collective-permute-start.11
  9.4 0.1 collective-permute-start
  9.5 2.5 %collective-permute-done.got = f32[2,96,256]{2,1,0:T(8,128)S(1)} collective-permute-done((f32[2,96,256]{2,1,0:T(8,128)S(1)}, f32[2,96,256]{2,1,0:T(8,128)S(1)}, u32[]{:S(2)}, u32[]{:S(2)}) %collective-permute-start) | collective-permute-done | bytes 196640 | tf_op jit(solution)/shard_map/ppermute | solution.py:140
  12.0 2.7 %collective-permute-start.1 = (bf16[2,96,256]{2,1,0:T(8,128)(2,1)S(1)}, bf16[2,96,256]{2,1,0:T(8,128)(2,1)S(1)}, u32[]{:S(2)}, u32[]{:S(2)}) collective-permute-start(bf16[2,96,256]{2,1,0:T(8,128)(2,1)S(1)} %get-tuple-element.47), channel_id=1, source_target_pairs={{0,4},{1,5},{2,6},{3,7},{4,0},{5,1},{6,2},{7,3},{8,12},{9,13},{10,... | collective-permute-start | bytes 294920 | tf_op jit(solution)/shard_map/ppermute | solution.py:140
  14.8 2.3 %collective-permute-start.3 = (bf16[2,96,256]{2,1,0:T(8,128)(2,1)S(1)}, bf16[2,96,256]{2,1,0:T(8,128)(2,1)S(1)}, u32[]{:S(2)}, u32[]{:S(2)}) collective-permute-start(bf16[2,96,256]{2,1,0:T(8,128)(2,1)S(1)} %get-tuple-element.47), channel_id=1, source_target_pairs={{0,8},{1,9},{2,10},{3,11},{4,12},{5,13},{6,14},{7,15},{8,0},{9,1},... | collective-permute-start | bytes 294920 | tf_op jit(solution)/shard_map/ppermute | solution.py:140
  17.1 0.7 collective-permute-done.1
  17.8 1.2 %collective-permute-start.5 = (bf16[2,2,96,256]{3,2,1,0:T(8,128)(2,1)S(1)}, bf16[2,2,96,256]{3,2,1,0:T(8,128)(2,1)S(1)}, u32[]{:S(2)}, u32[]{:S(2)}) collective-permute-start(bf16[2,2,96,256]{3,2,1,0:T(8,128)(2,1)S(1)} %pad_maximum_fusion.near_low), channel_id=1, source_target_pairs={{0,2},{1,3},{2,0},{3,1},{4,6},{5,7},{6,4},{7,5},{8,10},{9,11},{10,... | collective-permute-start | bytes 589832 | tf_op jit(solution)/shard_map/ppermute | solution.py:140
  19.0 0.5 collective-permute-done.3
  19.6 4.4 %collective-permute-done.4 = bf16[2,96,256]{2,1,0:T(8,128)(2,1)S(1)} collective-permute-done((bf16[2,96,256]{2,1,0:T(8,128)(2,1)S(1)}, bf16[2,96,256]{2,1,0:T(8,128)(2,1)S(1)}, u32[]{:S(2)}, u32[]{:S(2)}) %collective-permute-start.4) | collective-permute-done | bytes 98336 | tf_op jit(solution)/shard_map/ppermute | solution.py:140
  24.0 1.3 %collective-permute-start.8 = (bf16[2,2,96,256]{3,2,1,0:T(8,128)(2,1)S(1)}, bf16[2,2,96,256]{3,2,1,0:T(8,128)(2,1)S(1)}, u32[]{:S(2)}, u32[]{:S(2)}) collective-permute-start(bf16[2,2,96,256]{3,2,1,0:T(8,128)(2,1)S(1)} %pad_maximum_fusion.1.near_high), channel_id=1, source_target_pairs={{0,2},{1,3},{2,0},{3,1},{4,6},{5,7},{6,4},{7,5},{8,10},{9,11},{10,... | collective-permute-start | bytes 589832 | tf_op jit(solution)/shard_map/ppermute | solution.py:140
  25.3 1.2 %collective-permute-start.2 = (bf16[2,2,96,256]{3,2,1,0:T(8,128)(2,1)S(1)}, bf16[2,2,96,256]{3,2,1,0:T(8,128)(2,1)S(1)}, u32[]{:S(2)}, u32[]{:S(2)}) collective-permute-start(bf16[2,2,96,256]{3,2,1,0:T(8,128)(2,1)S(1)} %pad_maximum_fusion.near_low), channel_id=1, source_target_pairs={{0,16},{16,0},{1,17},{17,1},{2,18},{18,2},{3,19},{19,3},{4,20},{20... | collective-permute-start | bytes 589832 | tf_op jit(solution)/shard_map/ppermute | solution.py:144
  26.5 0.3 collective-permute-start.6
  26.8 1.8 %collective-permute-done.8.far_high = bf16[2,2,96,256]{3,2,1,0:T(8,128)(2,1)S(1)} collective-permute-done((bf16[2,2,96,256]{3,2,1,0:T(8,128)(2,1)S(1)}, bf16[2,2,96,256]{3,2,1,0:T(8,128)(2,1)S(1)}, u32[]{:S(2)}, u32[]{:S(2)}) %collective-permute-start.8) | collective-permute-done | bytes 196640 | tf_op jit(solution)/shard_map/ppermute | solution.py:140
  28.6 1.2 %collective-permute-start.7 = (bf16[2,2,96,256]{3,2,1,0:T(8,128)(2,1)S(1)}, bf16[2,2,96,256]{3,2,1,0:T(8,128)(2,1)S(1)}, u32[]{:S(2)}, u32[]{:S(2)}) collective-permute-start(bf16[2,2,96,256]{3,2,1,0:T(8,128)(2,1)S(1)} %collective-permute-done.5.far_low), channel_id=1, source_target_pairs={{0,16},{16,0},{1,17},{17,1},{2,18},{18,2},{3,19},{19,3},{4,20},{20... | collective-permute-start | bytes 589832 | tf_op jit(solution)/shard_map/ppermute | solution.py:144
  29.8 0.3 collective-permute-start.9
  30.1 5.8 %increments.3 = (f32[4,2,96,256]{3,2,1,0:T(8,128)S(1)}, bf16[2,2,96,256]{3,2,1,0:T(8,128)(2,1)S(1)}, bf16[2,2,96,256]{3,2,1,0:T(8,128)(2,1)S(1)}) custom-call(s32[3]{0:T(128)S(1)} %pad_add_fusion.ids, bf16[2,2,96,256]{3,2,1,0:T(8,128)(2,1)S(1)} %pad_maximum_fusion.near_low, bf16[2,2,96,256]{3,2,1,0:T(8,128)(2,1)S(1)} %pad_maximum_fusion.1.near_high, ...), custom_call_target="tpu_custom_call" | custom-call | flops 3221225472 | bytes 2097152 | tf_op jit(solution)/shard_map/increments/pallas_call | solution.py:387
  35.9 1.3 %collective-permute-start.19 = (bf16[2,2,96,256]{3,2,1,0:T(8,128)(2,1)S(1)}, bf16[2,2,96,256]{3,2,1,0:T(8,128)(2,1)S(1)}, u32[]{:S(2)}, u32[]{:S(2)}) collective-permute-start(bf16[2,2,96,256]{3,2,1,0:T(8,128)(2,1)S(1)} %get-tuple-element.64), channel_id=1, source_target_pairs={{0,2},{1,3},{2,0},{3,1},{4,6},{5,7},{6,4},{7,5},{8,10},{9,11},{10,... | collective-permute-start | bytes 589832 | tf_op jit(solution)/shard_map/ppermute | solution.py:140
  37.2 0.2 collective-permute-start.17
  37.4 0.6 collective-permute-done.7.far_low
  38.0 4.2 %collective-permute-done.9.far_high = bf16[2,2,96,256]{3,2,1,0:T(8,128)(2,1)S(1)} collective-permute-done((bf16[2,2,96,256]{3,2,1,0:T(8,128)(2,1)S(1)}, bf16[2,2,96,256]{3,2,1,0:T(8,128)(2,1)S(1)}, u32[]{:S(2)}, u32[]{:S(2)}) %collective-permute-start.9) | collective-permute-done | bytes 196640 | tf_op jit(solution)/shard_map/ppermute | solution.py:144
  42.2 5.9 %increments.2 = (f32[4,2,96,256]{3,2,1,0:T(8,128)S(1)}, bf16[2,2,96,256]{3,2,1,0:T(8,128)(2,1)S(1)}, bf16[2,2,96,256]{3,2,1,0:T(8,128)(2,1)S(1)}) custom-call(s32[3]{0:T(128)S(1)} %pad_add_fusion.ids, bf16[2,2,96,256]{3,2,1,0:T(8,128)(2,1)S(1)} %collective-permute-done.2.near_low, bf16[2,2,96,256]{3,2,1,0:T(8,128)(2,1)S(1)} %collective-permute-done.6.near_high, ...), custom_call_target="tpu_custom_call" | custom-call | flops 3221225472 | bytes 2097152 | tf_op jit(solution)/shard_map/increments/pallas_call | solution.py:387
  48.1 0.3 collective-permute-start.14
  48.4 1.2 %collective-permute-start.12 = (bf16[2,2,96,256]{3,2,1,0:T(8,128)(2,1)S(1)}, bf16[2,2,96,256]{3,2,1,0:T(8,128)(2,1)S(1)}, u32[]{:S(2)}, u32[]{:S(2)}) collective-permute-start(bf16[2,2,96,256]{3,2,1,0:T(8,128)(2,1)S(1)} %get-tuple-element.52), channel_id=1, source_target_pairs={{0,2},{1,3},{2,0},{3,1},{4,6},{5,7},{6,4},{7,5},{8,10},{9,11},{10,... | collective-permute-start | bytes 589832 | tf_op jit(solution)/shard_map/ppermute | solution.py:140
  49.7 3.9 %collective-permute-start.20 = (bf16[2,96,256]{2,1,0:T(8,128)(2,1)S(1)}, bf16[2,96,256]{2,1,0:T(8,128)(2,1)S(1)}, u32[]{:S(2)}, u32[]{:S(2)}) collective-permute-start(bf16[2,96,256]{2,1,0:T(8,128)(2,1)S(1)} %get-tuple-element.65), channel_id=1, source_target_pairs={{0,8},{1,9},{2,10},{3,11},{4,12},{5,13},{6,14},{7,15},{8,0},{9,1},... | collective-permute-start | bytes 294920 | tf_op jit(solution)/shard_map/ppermute | solution.py:140
  53.7 1.2 %collective-permute-start.21 = (bf16[2,96,256]{2,1,0:T(8,128)(2,1)S(1)}, bf16[2,96,256]{2,1,0:T(8,128)(2,1)S(1)}, u32[]{:S(2)}, u32[]{:S(2)}) collective-permute-start(bf16[2,96,256]{2,1,0:T(8,128)(2,1)S(1)} %get-tuple-element.66), channel_id=1, source_target_pairs={{0,12},{1,13},{2,14},{3,15},{4,8},{5,9},{6,10},{7,11},{8,4},{9,5},... | collective-permute-start | bytes 294920 | tf_op jit(solution)/shard_map/ppermute | solution.py:140
  54.9 0.1 collective-permute-start.18
  55.0 2.4 %collective-permute-start.15 = (bf16[2,96,256]{2,1,0:T(8,128)(2,1)S(1)}, bf16[2,96,256]{2,1,0:T(8,128)(2,1)S(1)}, u32[]{:S(2)}, u32[]{:S(2)}) collective-permute-start(bf16[2,96,256]{2,1,0:T(8,128)(2,1)S(1)} %get-tuple-element.56), channel_id=1, source_target_pairs={{0,8},{1,9},{2,10},{3,11},{4,12},{5,13},{6,14},{7,15},{8,0},{9,1},... | collective-permute-start | bytes 294920 | tf_op jit(solution)/shard_map/ppermute | solution.py:140
  57.4 1.9 %collective-permute-start.16 = (bf16[2,96,256]{2,1,0:T(8,128)(2,1)S(1)}, bf16[2,96,256]{2,1,0:T(8,128)(2,1)S(1)}, u32[]{:S(2)}, u32[]{:S(2)}) collective-permute-start(bf16[2,96,256]{2,1,0:T(8,128)(2,1)S(1)} %get-tuple-element.57), channel_id=1, source_target_pairs={{0,12},{1,13},{2,14},{3,15},{4,8},{5,9},{6,10},{7,11},{8,4},{9,5},... | collective-permute-start | bytes 294920 | tf_op jit(solution)/shard_map/ppermute | solution.py:140
  59.4 1.2 %collective-permute-start.13 = (bf16[2,96,256]{2,1,0:T(8,128)(2,1)S(1)}, bf16[2,96,256]{2,1,0:T(8,128)(2,1)S(1)}, u32[]{:S(2)}, u32[]{:S(2)}) collective-permute-start(bf16[2,96,256]{2,1,0:T(8,128)(2,1)S(1)} %get-tuple-element.54), channel_id=1, source_target_pairs={{0,4},{1,5},{2,6},{3,7},{4,0},{5,1},{6,2},{7,3},{8,12},{9,13},{10,... | collective-permute-start | bytes 294920 | tf_op jit(solution)/shard_map/ppermute | solution.py:140
  60.6 0.2 renorm.3
  60.8 0.8 collective-permute-start.24
  61.6 1.6 %collective-permute-start.25 = (bf16[2,96,256]{2,1,0:T(8,128)(2,1)S(1)}, bf16[2,96,256]{2,1,0:T(8,128)(2,1)S(1)}, u32[]{:S(2)}, u32[]{:S(2)}) collective-permute-start(bf16[2,96,256]{2,1,0:T(8,128)(2,1)S(1)} %get-tuple-element.67), channel_id=1, source_target_pairs={{0,12},{1,13},{2,14},{3,15},{4,8},{5,9},{6,10},{7,11},{8,4},{9,5},... | collective-permute-start | bytes 294920 | tf_op jit(solution)/shard_map/ppermute | solution.py:140
  63.3 2.3 %collective-permute-done.15.two = bf16[2,96,256]{2,1,0:T(8,128)(2,1)S(1)} collective-permute-done((bf16[2,96,256]{2,1,0:T(8,128)(2,1)S(1)}, bf16[2,96,256]{2,1,0:T(8,128)(2,1)S(1)}, u32[]{:S(2)}, u32[]{:S(2)}) %collective-permute-start.15) | collective-permute-done | bytes 98336 | tf_op jit(solution)/shard_map/ppermute | solution.py:140
  65.5 1.1 collective-permute-done.13.one
  66.6 0.1 renorm.2
  66.8 9.0 %collective-permute-start.39 = (f32[2,96,256]{2,1,0:T(8,128)S(1)}, f32[2,96,256]{2,1,0:T(8,128)S(1)}, u32[]{:S(2)}, u32[]{:S(2)}) collective-permute-start(f32[2,96,256]{2,1,0:T(8,128)S(1)} %pad_maximum_fusion.6), channel_id=1, source_target_pairs={{0,1},{1,0},{2,3},{3,2},{4,5},{5,4},{6,7},{7,6},{8,9},{9,8},{10,11... | collective-permute-start | bytes 589832 | tf_op jit(solution)/shard_map/ppermute | solution.py:140
  75.8 0.3 collective-permute-start.35
  76.1 1.7 %collective-permute-start.23 = (bf16[2,96,256]{2,1,0:T(8,128)(2,1)S(1)}, bf16[2,96,256]{2,1,0:T(8,128)(2,1)S(1)}, u32[]{:S(2)}, u32[]{:S(2)}) collective-permute-start(bf16[2,96,256]{2,1,0:T(8,128)(2,1)S(1)} %get-tuple-element.70), channel_id=1, source_target_pairs={{0,4},{1,5},{2,6},{3,7},{4,0},{5,1},{6,2},{7,3},{8,12},{9,13},{10,... | collective-permute-start | bytes 294920 | tf_op jit(solution)/shard_map/ppermute | solution.py:140
  77.9 1.2 %collective-permute-start.37 = (bf16[2,2,96,256]{3,2,1,0:T(8,128)(2,1)S(1)}, bf16[2,2,96,256]{3,2,1,0:T(8,128)(2,1)S(1)}, u32[]{:S(2)}, u32[]{:S(2)}) collective-permute-start(bf16[2,2,96,256]{3,2,1,0:T(8,128)(2,1)S(1)} %pad_maximum_fusion.4.near_high), channel_id=1, source_target_pairs={{0,2},{1,3},{2,0},{3,1},{4,6},{5,7},{6,4},{7,5},{8,10},{9,11},{10,... | collective-permute-start | bytes 589832 | tf_op jit(solution)/shard_map/ppermute | solution.py:140
  79.1 2.4 %collective-permute-done.23 = bf16[2,96,256]{2,1,0:T(8,128)(2,1)S(1)} collective-permute-done((bf16[2,96,256]{2,1,0:T(8,128)(2,1)S(1)}, bf16[2,96,256]{2,1,0:T(8,128)(2,1)S(1)}, u32[]{:S(2)}, u32[]{:S(2)}) %collective-permute-start.23) | collective-permute-done | bytes 98336 | tf_op jit(solution)/shard_map/ppermute | solution.py:140
  81.6 0.6 collective-permute-start.27
  82.1 1.4 %collective-permute-start.28 = (bf16[2,96,256]{2,1,0:T(8,128)(2,1)S(1)}, bf16[2,96,256]{2,1,0:T(8,128)(2,1)S(1)}, u32[]{:S(2)}, u32[]{:S(2)}) collective-permute-start(bf16[2,96,256]{2,1,0:T(8,128)(2,1)S(1)} %get-tuple-element.70), channel_id=1, source_target_pairs={{0,12},{1,13},{2,14},{3,15},{4,8},{5,9},{6,10},{7,11},{8,4},{9,5},... | collective-permute-start | bytes 294920 | tf_op jit(solution)/shard_map/ppermute | solution.py:140
  83.5 7.6 %collective-permute-start.34 = (bf16[2,2,96,256]{3,2,1,0:T(8,128)(2,1)S(1)}, bf16[2,2,96,256]{3,2,1,0:T(8,128)(2,1)S(1)}, u32[]{:S(2)}, u32[]{:S(2)}) collective-permute-start(bf16[2,2,96,256]{3,2,1,0:T(8,128)(2,1)S(1)} %pad_maximum_fusion.4.near_high), channel_id=1, source_target_pairs={{0,1},{1,0},{2,3},{3,2},{4,5},{5,4},{6,7},{7,6},{8,9},{9,8},{10,11... | collective-permute-start | bytes 589832 | tf_op jit(solution)/shard_map/ppermute | solution.py:140
  91.1 0.1 collective-permute-start.33
  91.2 0.9 collective-permute-start.30
  92.1 3.7 %collective-permute-start.38 = (bf16[2,2,96,256]{3,2,1,0:T(8,128)(2,1)S(1)}, bf16[2,2,96,256]{3,2,1,0:T(8,128)(2,1)S(1)}, u32[]{:S(2)}, u32[]{:S(2)}) collective-permute-start(bf16[2,2,96,256]{3,2,1,0:T(8,128)(2,1)S(1)} %collective-permute-done.37.far_high), channel_id=1, source_target_pairs={{0,1},{1,0},{2,3},{3,2},{4,5},{5,4},{6,7},{7,6},{8,9},{9,8},{10,11... | collective-permute-start | bytes 589832 | tf_op jit(solution)/shard_map/ppermute | solution.py:140
  95.8 1.0 collective-permute-start.32
  96.8 1.3 %finish.1 = (f32[4,16,1024]{2,1,0:T(8,128)}, f32[4,32,256]{2,1,0:T(8,128)}) custom-call(s32[3]{0:T(128)S(1)} %pad_add_fusion.ids, f32[2,96,256]{2,1,0:T(8,128)S(1)} %get-tuple-element.71.one, f32[2,96,256]{2,1,0:T(8,128)S(1)} %get-tuple-element.72.two, f32[2,96,256]{2,1,0:T(8,128)S(1)} %collective-permute-done.39.came), custom_call_target="tpu_custom_call" | custom-call | tf_op jit(solution)/shard_map/finish/pallas_call | solution.py:539
  98.1 2.6 %apply.4.rest_0_ = bf16[1024,1024]{1,0:T(8,128)(2,1)} custom-call(s32[3]{0:T(128)S(1)} %pad_add_fusion.ids, bf16[2,2,96,256]{3,2,1,0:T(8,128)(2,1)S(1)} %pad_maximum_fusion.2.near_low, bf16[2,2,96,256]{3,2,1,0:T(8,128)(2,1)S(1)} %pad_maximum_fusion.4.near_high, bf16[2,2,96,256]{3,2,1,0:T(8,128)(2,1)S(1)} %collective-permute-done.35.far_low, ...), custom_call_target="tpu_custom_call" | custom-call | flops 805306368 | bytes 1048576 | tf_op jit(solution)/shard_map/apply/pallas_call | solution.py:507
  100.7 0.8 collective-permute-start.26
  101.5 0.1 collective-permute-start.29
  101.5 0.4 collective-permute-start.31
  102.0 2.6 %apply.5.rest_0_ = bf16[1024,1024]{1,0:T(8,128)(2,1)} custom-call(s32[3]{0:T(128)S(1)} %pad_add_fusion.ids, bf16[2,2,96,256]{3,2,1,0:T(8,128)(2,1)S(1)} %collective-permute-done.33.near_low, bf16[2,2,96,256]{3,2,1,0:T(8,128)(2,1)S(1)} %collective-permute-done.34.near_high, ...), custom_call_target="tpu_custom_call", output_to_operand_aliasing={{}: (6, {})} | custom-call | flops 805306368 | bytes 1048576 | tf_op jit(solution)/shard_map/apply/pallas_call | solution.py:507
  104.6 0.1 collective-permute-start.40
  104.7 2.6 %apply.6.rest_0_ = bf16[1024,1024]{1,0:T(8,128)(2,1)} custom-call(s32[3]{0:T(128)S(1)} %pad_add_fusion.ids, bf16[2,2,96,256]{3,2,1,0:T(8,128)(2,1)S(1)} %pad_maximum_fusion.3.near_low, bf16[2,2,96,256]{3,2,1,0:T(8,128)(2,1)S(1)} %pad_maximum_fusion.5.near_high, ...), custom_call_target="tpu_custom_call", output_to_operand_aliasing={{}: (6, {})} | custom-call | flops 805306368 | bytes 1048576 | tf_op jit(solution)/shard_map/apply/pallas_call | solution.py:507
  107.3 2.6 %apply.7 = bf16[1024,1024]{1,0:T(8,128)(2,1)} custom-call(s32[3]{0:T(128)S(1)} %pad_add_fusion.ids, bf16[2,2,96,256]{3,2,1,0:T(8,128)(2,1)S(1)} %collective-permute-done.26.near_low, bf16[2,2,96,256]{3,2,1,0:T(8,128)(2,1)S(1)} %collective-permute-done.29.near_high, ...), custom_call_target="tpu_custom_call", output_to_operand_aliasing={{}: (6, {})} | custom-call | flops 805306368 | bytes 1048576 | tf_op jit(solution)/shard_map/apply/pallas_call | solution.py:507
  (57 shorter events, 0.5 us)
Async XLA Ops:
  0.6 6.0 %copy-start.5 = (f32[4,1024]{1,0:T(4,128)S(1)}, f32[4,1024]{1,0:T(4,128)}, u32[]{:S(2)}) copy-start(f32[4,1024]{1,0:T(4,128)} %rest_0_.1) | copy-start | bytes 49156
  0.7 1.0 copy-start.3
  1.7 0.9 copy-start.4
  3.4 1.6 %copy-start.1 = (bf16[1024,1024]{1,0:T(8,128)(2,1)S(1)}, bf16[1024,1024]{1,0:T(8,128)(2,1)}, u32[]{:S(2)}) copy-start(bf16[1024,1024]{1,0:T(8,128)(2,1)} %x_ref.2) | copy-start | bytes 6291460
  5.0 1.6 %copy-start.2 = (bf16[1024,1024]{1,0:T(8,128)(2,1)S(1)}, bf16[1024,1024]{1,0:T(8,128)(2,1)}, u32[]{:S(2)}) copy-start(bf16[1024,1024]{1,0:T(8,128)(2,1)} %x_ref.3) | copy-start | bytes 6291460
  6.5 23.3 %collective-permute-start.10 = (bf16[1024,512]{1,0:T(8,128)(2,1)S(1)}, bf16[1024,512]{1,0:T(8,128)(2,1)S(1)}, u32[]{:S(2)}, u32[]{:S(2)}) collective-permute-start(bf16[1024,512]{1,0:T(8,128)(2,1)S(1)} %get-tuple-element.43), channel_id=1, source_target_pairs={{0,1},{1,0},{2,3},{3,2},{4,5},{5,4},{6,7},{7,6},{8,9},{9,8},{10,11... | collective-permute-start | bytes 3145736 | tf_op jit(solution)/shard_map/ppermute | solution.py:140
  8.9 21.2 %collective-permute-start.11 = (bf16[1024,512]{1,0:T(8,128)(2,1)S(1)}, bf16[1024,512]{1,0:T(8,128)(2,1)S(1)}, u32[]{:S(2)}, u32[]{:S(2)}) collective-permute-start(bf16[1024,512]{1,0:T(8,128)(2,1)S(1)} %get-tuple-element.44), channel_id=1, source_target_pairs={{0,1},{1,0},{2,3},{3,2},{4,5},{5,4},{6,7},{7,6},{8,9},{9,8},{10,11... | collective-permute-start | bytes 3145736 | tf_op jit(solution)/shard_map/ppermute | solution.py:140
  9.4 2.6 %collective-permute-start = (f32[2,96,256]{2,1,0:T(8,128)S(1)}, f32[2,96,256]{2,1,0:T(8,128)S(1)}, u32[]{:S(2)}, u32[]{:S(2)}) collective-permute-start(f32[2,96,256]{2,1,0:T(8,128)S(1)} %get-tuple-element.41), channel_id=1, source_target_pairs={{0,1},{1,0},{2,3},{3,2},{4,5},{5,4},{6,7},{7,6},{8,9},{9,8},{10,11... | collective-permute-start | bytes 589832 | tf_op jit(solution)/shard_map/ppermute | solution.py:140
  12.0 5.8 %collective-permute-start.1 = (bf16[2,96,256]{2,1,0:T(8,128)(2,1)S(1)}, bf16[2,96,256]{2,1,0:T(8,128)(2,1)S(1)}, u32[]{:S(2)}, u32[]{:S(2)}) collective-permute-start(bf16[2,96,256]{2,1,0:T(8,128)(2,1)S(1)} %get-tuple-element.47), channel_id=1, source_target_pairs={{0,4},{1,5},{2,6},{3,7},{4,0},{5,1},{6,2},{7,3},{8,12},{9,13},{10,... | collective-permute-start | bytes 294920 | tf_op jit(solution)/shard_map/ppermute | solution.py:140
  14.8 4.8 %collective-permute-start.3 = (bf16[2,96,256]{2,1,0:T(8,128)(2,1)S(1)}, bf16[2,96,256]{2,1,0:T(8,128)(2,1)S(1)}, u32[]{:S(2)}, u32[]{:S(2)}) collective-permute-start(bf16[2,96,256]{2,1,0:T(8,128)(2,1)S(1)} %get-tuple-element.47), channel_id=1, source_target_pairs={{0,8},{1,9},{2,10},{3,11},{4,12},{5,13},{6,14},{7,15},{8,0},{9,1},... | collective-permute-start | bytes 294920 | tf_op jit(solution)/shard_map/ppermute | solution.py:140
  17.1 6.9 %collective-permute-start.4 = (bf16[2,96,256]{2,1,0:T(8,128)(2,1)S(1)}, bf16[2,96,256]{2,1,0:T(8,128)(2,1)S(1)}, u32[]{:S(2)}, u32[]{:S(2)}) collective-permute-start(bf16[2,96,256]{2,1,0:T(8,128)(2,1)S(1)} %get-tuple-element.47), channel_id=1, source_target_pairs={{0,12},{1,13},{2,14},{3,15},{4,8},{5,9},{6,10},{7,11},{8,4},{9,5},... | collective-permute-start | bytes 294920 | tf_op jit(solution)/shard_map/ppermute | solution.py:140
  17.8 6.2 %collective-permute-start.5 = (bf16[2,2,96,256]{3,2,1,0:T(8,128)(2,1)S(1)}, bf16[2,2,96,256]{3,2,1,0:T(8,128)(2,1)S(1)}, u32[]{:S(2)}, u32[]{:S(2)}) collective-permute-start(bf16[2,2,96,256]{3,2,1,0:T(8,128)(2,1)S(1)} %pad_maximum_fusion.near_low), channel_id=1, source_target_pairs={{0,2},{1,3},{2,0},{3,1},{4,6},{5,7},{6,4},{7,5},{8,10},{9,11},{10,... | collective-permute-start | bytes 589832 | tf_op jit(solution)/shard_map/ppermute | solution.py:140
  24.0 4.6 %collective-permute-start.8 = (bf16[2,2,96,256]{3,2,1,0:T(8,128)(2,1)S(1)}, bf16[2,2,96,256]{3,2,1,0:T(8,128)(2,1)S(1)}, u32[]{:S(2)}, u32[]{:S(2)}) collective-permute-start(bf16[2,2,96,256]{3,2,1,0:T(8,128)(2,1)S(1)} %pad_maximum_fusion.1.near_high), channel_id=1, source_target_pairs={{0,2},{1,3},{2,0},{3,1},{4,6},{5,7},{6,4},{7,5},{8,10},{9,11},{10,... | collective-permute-start | bytes 589832 | tf_op jit(solution)/shard_map/ppermute | solution.py:140
  25.3 11.8 %collective-permute-start.2 = (bf16[2,2,96,256]{3,2,1,0:T(8,128)(2,1)S(1)}, bf16[2,2,96,256]{3,2,1,0:T(8,128)(2,1)S(1)}, u32[]{:S(2)}, u32[]{:S(2)}) collective-permute-start(bf16[2,2,96,256]{3,2,1,0:T(8,128)(2,1)S(1)} %pad_maximum_fusion.near_low), channel_id=1, source_target_pairs={{0,16},{16,0},{1,17},{17,1},{2,18},{18,2},{3,19},{19,3},{4,20},{20... | collective-permute-start | bytes 589832 | tf_op jit(solution)/shard_map/ppermute | solution.py:144
  26.5 10.8 %collective-permute-start.6 = (bf16[2,2,96,256]{3,2,1,0:T(8,128)(2,1)S(1)}, bf16[2,2,96,256]{3,2,1,0:T(8,128)(2,1)S(1)}, u32[]{:S(2)}, u32[]{:S(2)}) collective-permute-start(bf16[2,2,96,256]{3,2,1,0:T(8,128)(2,1)S(1)} %pad_maximum_fusion.1.near_high), channel_id=1, source_target_pairs={{0,16},{16,0},{1,17},{17,1},{2,18},{18,2},{3,19},{19,3},{4,20},{20... | collective-permute-start | bytes 589832 | tf_op jit(solution)/shard_map/ppermute | solution.py:144
  28.6 9.4 %collective-permute-start.7 = (bf16[2,2,96,256]{3,2,1,0:T(8,128)(2,1)S(1)}, bf16[2,2,96,256]{3,2,1,0:T(8,128)(2,1)S(1)}, u32[]{:S(2)}, u32[]{:S(2)}) collective-permute-start(bf16[2,2,96,256]{3,2,1,0:T(8,128)(2,1)S(1)} %collective-permute-done.5.far_low), channel_id=1, source_target_pairs={{0,16},{16,0},{1,17},{17,1},{2,18},{18,2},{3,19},{19,3},{4,20},{20... | collective-permute-start | bytes 589832 | tf_op jit(solution)/shard_map/ppermute | solution.py:144
  29.8 12.4 %collective-permute-start.9 = (bf16[2,2,96,256]{3,2,1,0:T(8,128)(2,1)S(1)}, bf16[2,2,96,256]{3,2,1,0:T(8,128)(2,1)S(1)}, u32[]{:S(2)}, u32[]{:S(2)}) collective-permute-start(bf16[2,2,96,256]{3,2,1,0:T(8,128)(2,1)S(1)} %collective-permute-done.8.far_high), channel_id=1, source_target_pairs={{0,16},{16,0},{1,17},{17,1},{2,18},{18,2},{3,19},{19,3},{4,20},{20... | collective-permute-start | bytes 589832 | tf_op jit(solution)/shard_map/ppermute | solution.py:144
  35.9 13.8 %collective-permute-start.19 = (bf16[2,2,96,256]{3,2,1,0:T(8,128)(2,1)S(1)}, bf16[2,2,96,256]{3,2,1,0:T(8,128)(2,1)S(1)}, u32[]{:S(2)}, u32[]{:S(2)}) collective-permute-start(bf16[2,2,96,256]{3,2,1,0:T(8,128)(2,1)S(1)} %get-tuple-element.64), channel_id=1, source_target_pairs={{0,2},{1,3},{2,0},{3,1},{4,6},{5,7},{6,4},{7,5},{8,10},{9,11},{10,... | collective-permute-start | bytes 589832 | tf_op jit(solution)/shard_map/ppermute | solution.py:140
  37.2 17.7 %collective-permute-start.17 = (bf16[2,2,96,256]{3,2,1,0:T(8,128)(2,1)S(1)}, bf16[2,2,96,256]{3,2,1,0:T(8,128)(2,1)S(1)}, u32[]{:S(2)}, u32[]{:S(2)}) collective-permute-start(bf16[2,2,96,256]{3,2,1,0:T(8,128)(2,1)S(1)} %get-tuple-element.61), channel_id=1, source_target_pairs={{0,2},{1,3},{2,0},{3,1},{4,6},{5,7},{6,4},{7,5},{8,10},{9,11},{10,... | collective-permute-start | bytes 589832 | tf_op jit(solution)/shard_map/ppermute | solution.py:140
  48.1 6.8 %collective-permute-start.14 = (bf16[2,2,96,256]{3,2,1,0:T(8,128)(2,1)S(1)}, bf16[2,2,96,256]{3,2,1,0:T(8,128)(2,1)S(1)}, u32[]{:S(2)}, u32[]{:S(2)}) collective-permute-start(bf16[2,2,96,256]{3,2,1,0:T(8,128)(2,1)S(1)} %get-tuple-element.55), channel_id=1, source_target_pairs={{0,2},{1,3},{2,0},{3,1},{4,6},{5,7},{6,4},{7,5},{8,10},{9,11},{10,... | collective-permute-start | bytes 589832 | tf_op jit(solution)/shard_map/ppermute | solution.py:140
  48.4 9.0 %collective-permute-start.12 = (bf16[2,2,96,256]{3,2,1,0:T(8,128)(2,1)S(1)}, bf16[2,2,96,256]{3,2,1,0:T(8,128)(2,1)S(1)}, u32[]{:S(2)}, u32[]{:S(2)}) collective-permute-start(bf16[2,2,96,256]{3,2,1,0:T(8,128)(2,1)S(1)} %get-tuple-element.52), channel_id=1, source_target_pairs={{0,2},{1,3},{2,0},{3,1},{4,6},{5,7},{6,4},{7,5},{8,10},{9,11},{10,... | collective-permute-start | bytes 589832 | tf_op jit(solution)/shard_map/ppermute | solution.py:140
  49.7 9.7 %collective-permute-start.20 = (bf16[2,96,256]{2,1,0:T(8,128)(2,1)S(1)}, bf16[2,96,256]{2,1,0:T(8,128)(2,1)S(1)}, u32[]{:S(2)}, u32[]{:S(2)}) collective-permute-start(bf16[2,96,256]{2,1,0:T(8,128)(2,1)S(1)} %get-tuple-element.65), channel_id=1, source_target_pairs={{0,8},{1,9},{2,10},{3,11},{4,12},{5,13},{6,14},{7,15},{8,0},{9,1},... | collective-permute-start | bytes 294920 | tf_op jit(solution)/shard_map/ppermute | solution.py:140
  53.7 7.0 %collective-permute-start.21 = (bf16[2,96,256]{2,1,0:T(8,128)(2,1)S(1)}, bf16[2,96,256]{2,1,0:T(8,128)(2,1)S(1)}, u32[]{:S(2)}, u32[]{:S(2)}) collective-permute-start(bf16[2,96,256]{2,1,0:T(8,128)(2,1)S(1)} %get-tuple-element.66), channel_id=1, source_target_pairs={{0,12},{1,13},{2,14},{3,15},{4,8},{5,9},{6,10},{7,11},{8,4},{9,5},... | collective-permute-start | bytes 294920 | tf_op jit(solution)/shard_map/ppermute | solution.py:140
  54.9 5.8 %collective-permute-start.18 = (bf16[2,96,256]{2,1,0:T(8,128)(2,1)S(1)}, bf16[2,96,256]{2,1,0:T(8,128)(2,1)S(1)}, u32[]{:S(2)}, u32[]{:S(2)}) collective-permute-start(bf16[2,96,256]{2,1,0:T(8,128)(2,1)S(1)} %get-tuple-element.63), channel_id=1, source_target_pairs={{0,4},{1,5},{2,6},{3,7},{4,0},{5,1},{6,2},{7,3},{8,12},{9,13},{10,... | collective-permute-start | bytes 294920 | tf_op jit(solution)/shard_map/ppermute | solution.py:140
  55.0 10.5 %collective-permute-start.15 = (bf16[2,96,256]{2,1,0:T(8,128)(2,1)S(1)}, bf16[2,96,256]{2,1,0:T(8,128)(2,1)S(1)}, u32[]{:S(2)}, u32[]{:S(2)}) collective-permute-start(bf16[2,96,256]{2,1,0:T(8,128)(2,1)S(1)} %get-tuple-element.56), channel_id=1, source_target_pairs={{0,8},{1,9},{2,10},{3,11},{4,12},{5,13},{6,14},{7,15},{8,0},{9,1},... | collective-permute-start | bytes 294920 | tf_op jit(solution)/shard_map/ppermute | solution.py:140
  57.4 8.1 %collective-permute-start.16 = (bf16[2,96,256]{2,1,0:T(8,128)(2,1)S(1)}, bf16[2,96,256]{2,1,0:T(8,128)(2,1)S(1)}, u32[]{:S(2)}, u32[]{:S(2)}) collective-permute-start(bf16[2,96,256]{2,1,0:T(8,128)(2,1)S(1)} %get-tuple-element.57), channel_id=1, source_target_pairs={{0,12},{1,13},{2,14},{3,15},{4,8},{5,9},{6,10},{7,11},{8,4},{9,5},... | collective-permute-start | bytes 294920 | tf_op jit(solution)/shard_map/ppermute | solution.py:140
  59.4 7.2 %collective-permute-start.13 = (bf16[2,96,256]{2,1,0:T(8,128)(2,1)S(1)}, bf16[2,96,256]{2,1,0:T(8,128)(2,1)S(1)}, u32[]{:S(2)}, u32[]{:S(2)}) collective-permute-start(bf16[2,96,256]{2,1,0:T(8,128)(2,1)S(1)} %get-tuple-element.54), channel_id=1, source_target_pairs={{0,4},{1,5},{2,6},{3,7},{4,0},{5,1},{6,2},{7,3},{8,12},{9,13},{10,... | collective-permute-start | bytes 294920 | tf_op jit(solution)/shard_map/ppermute | solution.py:140
  60.6 37.5 %copy-start = (bf16[1024,1024]{1,0:T(8,128)(2,1)S(1)}, bf16[1024,1024]{1,0:T(8,128)(2,1)}, u32[]{:S(2)}) copy-start(bf16[1024,1024]{1,0:T(8,128)(2,1)} %q_ref.7) | copy-start | bytes 6291460
  60.8 17.1 %collective-permute-start.24 = (bf16[2,96,256]{2,1,0:T(8,128)(2,1)S(1)}, bf16[2,96,256]{2,1,0:T(8,128)(2,1)S(1)}, u32[]{:S(2)}, u32[]{:S(2)}) collective-permute-start(bf16[2,96,256]{2,1,0:T(8,128)(2,1)S(1)} %get-tuple-element.67), channel_id=1, source_target_pairs={{0,8},{1,9},{2,10},{3,11},{4,12},{5,13},{6,14},{7,15},{8,0},{9,1},... | collective-permute-start | bytes 294920 | tf_op jit(solution)/shard_map/ppermute | solution.py:140
  61.6 16.2 %collective-permute-start.25 = (bf16[2,96,256]{2,1,0:T(8,128)(2,1)S(1)}, bf16[2,96,256]{2,1,0:T(8,128)(2,1)S(1)}, u32[]{:S(2)}, u32[]{:S(2)}) collective-permute-start(bf16[2,96,256]{2,1,0:T(8,128)(2,1)S(1)} %get-tuple-element.67), channel_id=1, source_target_pairs={{0,12},{1,13},{2,14},{3,15},{4,8},{5,9},{6,10},{7,11},{8,4},{9,5},... | collective-permute-start | bytes 294920 | tf_op jit(solution)/shard_map/ppermute | solution.py:140
  65.5 10.2 %collective-permute-start.22 = (bf16[2,96,256]{2,1,0:T(8,128)(2,1)S(1)}, bf16[2,96,256]{2,1,0:T(8,128)(2,1)S(1)}, u32[]{:S(2)}, u32[]{:S(2)}) collective-permute-start(bf16[2,96,256]{2,1,0:T(8,128)(2,1)S(1)} %get-tuple-element.67), channel_id=1, source_target_pairs={{0,4},{1,5},{2,6},{3,7},{4,0},{5,1},{6,2},{7,3},{8,12},{9,13},{10,... | collective-permute-start | bytes 294920 | tf_op jit(solution)/shard_map/ppermute | solution.py:140
  66.8 16.8 %collective-permute-start.39 = (f32[2,96,256]{2,1,0:T(8,128)S(1)}, f32[2,96,256]{2,1,0:T(8,128)S(1)}, u32[]{:S(2)}, u32[]{:S(2)}) collective-permute-start(f32[2,96,256]{2,1,0:T(8,128)S(1)} %pad_maximum_fusion.6), channel_id=1, source_target_pairs={{0,1},{1,0},{2,3},{3,2},{4,5},{5,4},{6,7},{7,6},{8,9},{9,8},{10,11... | collective-permute-start | bytes 589832 | tf_op jit(solution)/shard_map/ppermute | solution.py:140
  75.8 15.4 %collective-permute-start.35 = (bf16[2,2,96,256]{3,2,1,0:T(8,128)(2,1)S(1)}, bf16[2,2,96,256]{3,2,1,0:T(8,128)(2,1)S(1)}, u32[]{:S(2)}, u32[]{:S(2)}) collective-permute-start(bf16[2,2,96,256]{3,2,1,0:T(8,128)(2,1)S(1)} %pad_maximum_fusion.2.near_low), channel_id=1, source_target_pairs={{0,2},{1,3},{2,0},{3,1},{4,6},{5,7},{6,4},{7,5},{8,10},{9,11},{10,... | collective-permute-start | bytes 589832 | tf_op jit(solution)/shard_map/ppermute | solution.py:140
  76.1 5.4 %collective-permute-start.23 = (bf16[2,96,256]{2,1,0:T(8,128)(2,1)S(1)}, bf16[2,96,256]{2,1,0:T(8,128)(2,1)S(1)}, u32[]{:S(2)}, u32[]{:S(2)}) collective-permute-start(bf16[2,96,256]{2,1,0:T(8,128)(2,1)S(1)} %get-tuple-element.70), channel_id=1, source_target_pairs={{0,4},{1,5},{2,6},{3,7},{4,0},{5,1},{6,2},{7,3},{8,12},{9,13},{10,... | collective-permute-start | bytes 294920 | tf_op jit(solution)/shard_map/ppermute | solution.py:140
  77.9 13.2 %collective-permute-start.37 = (bf16[2,2,96,256]{3,2,1,0:T(8,128)(2,1)S(1)}, bf16[2,2,96,256]{3,2,1,0:T(8,128)(2,1)S(1)}, u32[]{:S(2)}, u32[]{:S(2)}) collective-permute-start(bf16[2,2,96,256]{3,2,1,0:T(8,128)(2,1)S(1)} %pad_maximum_fusion.4.near_high), channel_id=1, source_target_pairs={{0,2},{1,3},{2,0},{3,1},{4,6},{5,7},{6,4},{7,5},{8,10},{9,11},{10,... | collective-permute-start | bytes 589832 | tf_op jit(solution)/shard_map/ppermute | solution.py:140
  81.6 10.5 %collective-permute-start.27 = (bf16[2,96,256]{2,1,0:T(8,128)(2,1)S(1)}, bf16[2,96,256]{2,1,0:T(8,128)(2,1)S(1)}, u32[]{:S(2)}, u32[]{:S(2)}) collective-permute-start(bf16[2,96,256]{2,1,0:T(8,128)(2,1)S(1)} %get-tuple-element.70), channel_id=1, source_target_pairs={{0,8},{1,9},{2,10},{3,11},{4,12},{5,13},{6,14},{7,15},{8,0},{9,1},... | collective-permute-start | bytes 294920 | tf_op jit(solution)/shard_map/ppermute | solution.py:140
  82.1 13.6 %collective-permute-start.28 = (bf16[2,96,256]{2,1,0:T(8,128)(2,1)S(1)}, bf16[2,96,256]{2,1,0:T(8,128)(2,1)S(1)}, u32[]{:S(2)}, u32[]{:S(2)}) collective-permute-start(bf16[2,96,256]{2,1,0:T(8,128)(2,1)S(1)} %get-tuple-element.70), channel_id=1, source_target_pairs={{0,12},{1,13},{2,14},{3,15},{4,8},{5,9},{6,10},{7,11},{8,4},{9,5},... | collective-permute-start | bytes 294920 | tf_op jit(solution)/shard_map/ppermute | solution.py:140
  83.5 12.2 %collective-permute-start.34 = (bf16[2,2,96,256]{3,2,1,0:T(8,128)(2,1)S(1)}, bf16[2,2,96,256]{3,2,1,0:T(8,128)(2,1)S(1)}, u32[]{:S(2)}, u32[]{:S(2)}) collective-permute-start(bf16[2,2,96,256]{3,2,1,0:T(8,128)(2,1)S(1)} %pad_maximum_fusion.4.near_high), channel_id=1, source_target_pairs={{0,1},{1,0},{2,3},{3,2},{4,5},{5,4},{6,7},{7,6},{8,9},{9,8},{10,11... | collective-permute-start | bytes 589832 | tf_op jit(solution)/shard_map/ppermute | solution.py:140
  91.1 9.6 %collective-permute-start.33 = (bf16[2,2,96,256]{3,2,1,0:T(8,128)(2,1)S(1)}, bf16[2,2,96,256]{3,2,1,0:T(8,128)(2,1)S(1)}, u32[]{:S(2)}, u32[]{:S(2)}) collective-permute-start(bf16[2,2,96,256]{3,2,1,0:T(8,128)(2,1)S(1)} %pad_maximum_fusion.2.near_low), channel_id=1, source_target_pairs={{0,1},{1,0},{2,3},{3,2},{4,5},{5,4},{6,7},{7,6},{8,9},{9,8},{10,11... | collective-permute-start | bytes 589832 | tf_op jit(solution)/shard_map/ppermute | solution.py:140
  91.2 10.3 %collective-permute-start.30 = (bf16[2,2,96,256]{3,2,1,0:T(8,128)(2,1)S(1)}, bf16[2,2,96,256]{3,2,1,0:T(8,128)(2,1)S(1)}, u32[]{:S(2)}, u32[]{:S(2)}) collective-permute-start(bf16[2,2,96,256]{3,2,1,0:T(8,128)(2,1)S(1)} %pad_maximum_fusion.3.near_low), channel_id=1, source_target_pairs={{0,2},{1,3},{2,0},{3,1},{4,6},{5,7},{6,4},{7,5},{8,10},{9,11},{10,... | collective-permute-start | bytes 589832 | tf_op jit(solution)/shard_map/ppermute | solution.py:140
  92.1 9.5 %collective-permute-start.38 = (bf16[2,2,96,256]{3,2,1,0:T(8,128)(2,1)S(1)}, bf16[2,2,96,256]{3,2,1,0:T(8,128)(2,1)S(1)}, u32[]{:S(2)}, u32[]{:S(2)}) collective-permute-start(bf16[2,2,96,256]{3,2,1,0:T(8,128)(2,1)S(1)} %collective-permute-done.37.far_high), channel_id=1, source_target_pairs={{0,1},{1,0},{2,3},{3,2},{4,5},{5,4},{6,7},{7,6},{8,9},{9,8},{10,11... | collective-permute-start | bytes 589832 | tf_op jit(solution)/shard_map/ppermute | solution.py:140
  95.8 6.2 %collective-permute-start.36 = (bf16[2,2,96,256]{3,2,1,0:T(8,128)(2,1)S(1)}, bf16[2,2,96,256]{3,2,1,0:T(8,128)(2,1)S(1)}, u32[]{:S(2)}, u32[]{:S(2)}) collective-permute-start(bf16[2,2,96,256]{3,2,1,0:T(8,128)(2,1)S(1)} %collective-permute-done.35.far_low), channel_id=1, source_target_pairs={{0,1},{1,0},{2,3},{3,2},{4,5},{5,4},{6,7},{7,6},{8,9},{9,8},{10,11... | collective-permute-start | bytes 589832 | tf_op jit(solution)/shard_map/ppermute | solution.py:140
  95.8 8.8 %collective-permute-start.32 = (bf16[2,2,96,256]{3,2,1,0:T(8,128)(2,1)S(1)}, bf16[2,2,96,256]{3,2,1,0:T(8,128)(2,1)S(1)}, u32[]{:S(2)}, u32[]{:S(2)}) collective-permute-start(bf16[2,2,96,256]{3,2,1,0:T(8,128)(2,1)S(1)} %pad_maximum_fusion.5.near_high), channel_id=1, source_target_pairs={{0,2},{1,3},{2,0},{3,1},{4,6},{5,7},{6,4},{7,5},{8,10},{9,11},{10,... | collective-permute-start | bytes 589832 | tf_op jit(solution)/shard_map/ppermute | solution.py:140
  100.7 6.6 %collective-permute-start.26 = (bf16[2,2,96,256]{3,2,1,0:T(8,128)(2,1)S(1)}, bf16[2,2,96,256]{3,2,1,0:T(8,128)(2,1)S(1)}, u32[]{:S(2)}, u32[]{:S(2)}) collective-permute-start(bf16[2,2,96,256]{3,2,1,0:T(8,128)(2,1)S(1)} %pad_maximum_fusion.3.near_low), channel_id=1, source_target_pairs={{0,1},{1,0},{2,3},{3,2},{4,5},{5,4},{6,7},{7,6},{8,9},{9,8},{10,11... | collective-permute-start | bytes 589832 | tf_op jit(solution)/shard_map/ppermute | solution.py:140
  101.5 5.8 %collective-permute-start.29 = (bf16[2,2,96,256]{3,2,1,0:T(8,128)(2,1)S(1)}, bf16[2,2,96,256]{3,2,1,0:T(8,128)(2,1)S(1)}, u32[]{:S(2)}, u32[]{:S(2)}) collective-permute-start(bf16[2,2,96,256]{3,2,1,0:T(8,128)(2,1)S(1)} %pad_maximum_fusion.5.near_high), channel_id=1, source_target_pairs={{0,1},{1,0},{2,3},{3,2},{4,5},{5,4},{6,7},{7,6},{8,9},{9,8},{10,11... | collective-permute-start | bytes 589832 | tf_op jit(solution)/shard_map/ppermute | solution.py:140
  101.5 5.7 %collective-permute-start.31 = (bf16[2,2,96,256]{3,2,1,0:T(8,128)(2,1)S(1)}, bf16[2,2,96,256]{3,2,1,0:T(8,128)(2,1)S(1)}, u32[]{:S(2)}, u32[]{:S(2)}) collective-permute-start(bf16[2,2,96,256]{3,2,1,0:T(8,128)(2,1)S(1)} %collective-permute-done.30.far_low), channel_id=1, source_target_pairs={{0,1},{1,0},{2,3},{3,2},{4,5},{5,4},{6,7},{7,6},{8,9},{9,8},{10,11... | collective-permute-start | bytes 589832 | tf_op jit(solution)/shard_map/ppermute | solution.py:140
  104.6 2.7 %collective-permute-start.40 = (bf16[2,2,96,256]{3,2,1,0:T(8,128)(2,1)S(1)}, bf16[2,2,96,256]{3,2,1,0:T(8,128)(2,1)S(1)}, u32[]{:S(2)}, u32[]{:S(2)}) collective-permute-start(bf16[2,2,96,256]{3,2,1,0:T(8,128)(2,1)S(1)} %collective-permute-done.32.far_high), channel_id=1, source_target_pairs={{0,1},{1,0},{2,3},{3,2},{4,5},{5,4},{6,7},{7,6},{8,9},{9,8},{10,11... | collective-permute-start | bytes 589832 | tf_op jit(solution)/shard_map/ppermute | solution.py:140

commit v6 on v5

--- a/solution.py
+++ b/solution.py
@@ -548,14 +548,6 @@
     )(ids, one, two, came)
 
 
-def gather_chips(shard):
-    z1, z3, z2 = swap(shard, 4), swap(shard, 12), swap(shard, 8)
-    near_low, near_high = jnp.stack([shard, z1]), jnp.stack([z2, z3])
-    far_low = swap(near_low, 2)
-    near_high = after(near_high, far_low)
-    return near_low, near_high, far_low, swap(near_high, 2)
-
-
 def per_device_cube(queries, keys, values, step_size, fast_in, fast_out):
     rows = keys.shape[0]
     heads = fast_in.shape[0]
@@ -573,14 +565,20 @@
     got = after(got, k_send, v_send)
     master_one, master_two, shard = pair(own, got)
     masters = (master_one, master_two)
-    first = gather_chips(shard)
-    second = tuple(swap_parts(piece) for piece in first)
     k_got, v_got = swap(k_send, 1), swap(v_send, 1)
+    z1, z3, z2 = swap(shard, 4), swap(shard, 12), swap(shard, 8)
+    near_low = after(jnp.stack([shard, z1]), k_got, v_got)
+    far_low, other_near_low = swap(near_low, 2), swap_parts(near_low)
+    near_high = after(jnp.stack([z2, z3]), far_low, other_near_low)
+    far_high = swap(near_high, 2)
+    first = (near_low, near_high, far_low, far_high)
+    second = (other_near_low, *(swap_parts(piece) for piece in first[1:]))
 
     wide, short = [], []
     for order in range(2):
         lines = second if order else first
-        kept, low, high = increments(ids, order, lines, k_own, v_own, k_got, v_got, fast)
+        later = ids if order else after(ids, second[2])
+        kept, low, high = increments(later, order, lines, k_own, v_own, k_got, v_got, fast)
         high, low = swap(high, 2), swap(low, 2)
         sum2, sum3 = add_pair(kept, high, 1, BF16)
         sum0, sum1 = add_pair(kept, low, 0, F32)

time: 110 us -> 106 us (0.964)
  starting transfers between devices: 56.3 us -> 53.8 us
  waiting for transfers between devices: 20.6 us -> 19.2 us
    ppermute x37, starting transfers between devices: 53.4 us -> 49.8 us  [swap(): lax.ppermute(value, 'tok', [(place, place ^ bits) for place in range(coun...]
    ppermute x4, waiting for transfers between devices: 4.81 us -> 2.07 us  [swap_parts(): return lax.ppermute(value, 'parts', [(0, 1), (1, 0)])]
    ppermute x37, waiting for transfers between devices: 15.8 us -> 17.1 us  [swap(): lax.ppermute(value, 'tok', [(place, place ^ bits) for place in range(coun...]
  transfers between devices with their start and end apart: 41 -> 41, of which waited for: 10 -> 8; matrix products, arithmetic and copies ran while one was open for 0% -> 0% of each run, Pallas kernels for 21% -> 17%
where the time goes in v6:
time: 106 us
  starting transfers between devices  53.8 us (51%)
  Pallas kernels  28.4 us (27%)
  waiting for transfers between devices  19.2 us (18%)
  local copies, waits for them, and re-layouts  3.47 us (3%)
    ppermute x37, starting transfers between devices, swap(): lax.ppermute(value, 'tok', [(place, place ^ bits) for place in range(coun...  49.8 us
    ppermute x37, waiting for transfers between devices, swap(): lax.ppermute(value, 'tok', [(place, place ^ bits) for place in range(coun...  17.1 us
    pallas_call x2, Pallas kernels, increments(): pl.pallas_call(increments_kernel, grid_spec=pltpu.PrefetchScalarGridSpec(...  11.7 us
    pallas_call x4, Pallas kernels, apply_fast(): pl.pallas_call(functools.partial(apply_kernel, order, other), grid_spec=p...  10.4 us
    ppermute x4, starting transfers between devices, swap_parts(): return lax.ppermute(value, 'parts', [(0, 1), (1, 0)])  3.95 us
    pallas_call x2, Pallas kernels, prepare(): pl.pallas_call(functools.partial(prepare_kernel, heads, block_root), grid...  3.78 us
    unnamed x12, local copies, waits for them, and re-layouts  3.46 us
  transfers between devices with their start and end apart: 41, of which 8 were waited for; matrix products, arithmetic and copies ran while one was open for 0% of the time, Pallas kernels for 17%

profile of v6, /device:TPU:1, one launch (start us, length us, event | category | flops | bytes accessed | tf_op | source)
XLA Modules:
  0.0 105.9 jit_solution(1313581035655205135)
XLA Ops:
  0.7 0.1 pad_add_fusion.ids
  0.7 0.9 copy-done.3
  1.7 0.9 copy-done.4
  2.6 0.8 pack.1
  3.4 0.0 copy-start.1
  3.4 1.6 %copy-done.1 = bf16[1024,1024]{1,0:T(8,128)(2,1)S(1)} copy-done((bf16[1024,1024]{1,0:T(8,128)(2,1)S(1)}, bf16[1024,1024]{1,0:T(8,128)(2,1)}, u32[]{:S(2)}) %copy-start.1) | copy-done | bytes 2097176
  5.0 1.5 %keys.1 = (bf16[1024,512]{1,0:T(8,128)(2,1)S(1)}, bf16[1024,512]{1,0:T(8,128)(2,1)S(1)}) custom-call(s32[3]{0:T(128)S(1)} %pad_add_fusion.ids, bf16[1024,1024]{1,0:T(8,128)(2,1)S(1)} %copy-done.1), custom_call_target="tpu_custom_call" | custom-call | flops 5242880 | bytes 4194304 | tf_op jit(solution)/shard_map/keys/pallas_call | solution.py:255
  6.5 0.1 collective-permute-start.2
  6.6 2.3 %values.1 = (bf16[1024,512]{1,0:T(8,128)(2,1)S(1)}, bf16[1024,512]{1,0:T(8,128)(2,1)S(1)}) custom-call(s32[3]{0:T(128)S(1)} %pad_add_fusion.ids, bf16[1024,1024]{1,0:T(8,128)(2,1)S(1)} %copy-done.2, f32[4,1024]{1,0:T(4,128)S(1)} %copy-done.5), custom_call_target="tpu_custom_call" | custom-call | flops 5242880 | bytes 4194304 | tf_op jit(solution)/shard_map/values/pallas_call | solution.py:255
  8.9 0.5 collective-permute-start.3
  9.4 0.1 collective-permute-start
  9.5 2.5 %collective-permute-done.got = f32[2,96,256]{2,1,0:T(8,128)S(1)} collective-permute-done((f32[2,96,256]{2,1,0:T(8,128)S(1)}, f32[2,96,256]{2,1,0:T(8,128)S(1)}, u32[]{:S(2)}, u32[]{:S(2)}) %collective-permute-start) | collective-permute-done | bytes 196640 | tf_op jit(solution)/shard_map/ppermute | solution.py:140
  12.0 2.7 %collective-permute-start.1 = (bf16[2,96,256]{2,1,0:T(8,128)(2,1)S(1)}, bf16[2,96,256]{2,1,0:T(8,128)(2,1)S(1)}, u32[]{:S(2)}, u32[]{:S(2)}) collective-permute-start(bf16[2,96,256]{2,1,0:T(8,128)(2,1)S(1)} %get-tuple-element.49), channel_id=1, source_target_pairs={{0,4},{1,5},{2,6},{3,7},{4,0},{5,1},{6,2},{7,3},{8,12},{9,13},{10,... | collective-permute-start | bytes 294920 | tf_op jit(solution)/shard_map/ppermute | solution.py:140
  14.8 2.3 %collective-permute-start.5 = (bf16[2,96,256]{2,1,0:T(8,128)(2,1)S(1)}, bf16[2,96,256]{2,1,0:T(8,128)(2,1)S(1)}, u32[]{:S(2)}, u32[]{:S(2)}) collective-permute-start(bf16[2,96,256]{2,1,0:T(8,128)(2,1)S(1)} %get-tuple-element.49), channel_id=1, source_target_pairs={{0,8},{1,9},{2,10},{3,11},{4,12},{5,13},{6,14},{7,15},{8,0},{9,1},... | collective-permute-start | bytes 294920 | tf_op jit(solution)/shard_map/ppermute | solution.py:140
  17.1 0.7 collective-permute-done.1
  17.8 1.2 %collective-permute-start.7 = (bf16[2,2,96,256]{3,2,1,0:T(8,128)(2,1)S(1)}, bf16[2,2,96,256]{3,2,1,0:T(8,128)(2,1)S(1)}, u32[]{:S(2)}, u32[]{:S(2)}) collective-permute-start(bf16[2,2,96,256]{3,2,1,0:T(8,128)(2,1)S(1)} %pad_maximum_fusion.near_low), channel_id=1, source_target_pairs={{0,2},{1,3},{2,0},{3,1},{4,6},{5,7},{6,4},{7,5},{8,10},{9,11},{10,... | collective-permute-start | bytes 589832 | tf_op jit(solution)/shard_map/ppermute | solution.py:140
  19.1 1.2 %collective-permute-start.4 = (bf16[2,2,96,256]{3,2,1,0:T(8,128)(2,1)S(1)}, bf16[2,2,96,256]{3,2,1,0:T(8,128)(2,1)S(1)}, u32[]{:S(2)}, u32[]{:S(2)}) collective-permute-start(bf16[2,2,96,256]{3,2,1,0:T(8,128)(2,1)S(1)} %pad_maximum_fusion.near_low), channel_id=1, source_target_pairs={{0,16},{16,0},{1,17},{17,1},{2,18},{18,2},{3,19},{19,3},{4,20},{20... | collective-permute-start | bytes 589832 | tf_op jit(solution)/shard_map/ppermute | solution.py:144
  20.3 3.7 %collective-permute-done.6 = bf16[2,96,256]{2,1,0:T(8,128)(2,1)S(1)} collective-permute-done((bf16[2,96,256]{2,1,0:T(8,128)(2,1)S(1)}, bf16[2,96,256]{2,1,0:T(8,128)(2,1)S(1)}, u32[]{:S(2)}, u32[]{:S(2)}) %collective-permute-start.6) | collective-permute-done | bytes 98336 | tf_op jit(solution)/shard_map/ppermute | solution.py:140
  24.0 1.3 %collective-permute-start.9 = (bf16[2,2,96,256]{3,2,1,0:T(8,128)(2,1)S(1)}, bf16[2,2,96,256]{3,2,1,0:T(8,128)(2,1)S(1)}, u32[]{:S(2)}, u32[]{:S(2)}) collective-permute-start(bf16[2,2,96,256]{3,2,1,0:T(8,128)(2,1)S(1)} %collective-permute-done.7.far_low), channel_id=1, source_target_pairs={{0,16},{16,0},{1,17},{17,1},{2,18},{18,2},{3,19},{19,3},{4,20},{20... | collective-permute-start | bytes 589832 | tf_op jit(solution)/shard_map/ppermute | solution.py:144
  25.3 1.2 %collective-permute-start.10 = (bf16[2,2,96,256]{3,2,1,0:T(8,128)(2,1)S(1)}, bf16[2,2,96,256]{3,2,1,0:T(8,128)(2,1)S(1)}, u32[]{:S(2)}, u32[]{:S(2)}) collective-permute-start(bf16[2,2,96,256]{3,2,1,0:T(8,128)(2,1)S(1)} %pad_maximum_fusion.1.near_high), channel_id=1, source_target_pairs={{0,2},{1,3},{2,0},{3,1},{4,6},{5,7},{6,4},{7,5},{8,10},{9,11},{10,... | collective-permute-start | bytes 589832 | tf_op jit(solution)/shard_map/ppermute | solution.py:140
  26.5 2.1 %collective-permute-done.9.far_low = bf16[2,2,96,256]{3,2,1,0:T(8,128)(2,1)S(1)} collective-permute-done((bf16[2,2,96,256]{3,2,1,0:T(8,128)(2,1)S(1)}, bf16[2,2,96,256]{3,2,1,0:T(8,128)(2,1)S(1)}, u32[]{:S(2)}, u32[]{:S(2)}) %collective-permute-start.9) | collective-permute-done | bytes 196640 | tf_op jit(solution)/shard_map/ppermute | solution.py:144
  28.6 1.5 %collective-permute-done.10.far_high = bf16[2,2,96,256]{3,2,1,0:T(8,128)(2,1)S(1)} collective-permute-done((bf16[2,2,96,256]{3,2,1,0:T(8,128)(2,1)S(1)}, bf16[2,2,96,256]{3,2,1,0:T(8,128)(2,1)S(1)}, u32[]{:S(2)}, u32[]{:S(2)}) %collective-permute-start.10) | collective-permute-done | bytes 196640 | tf_op jit(solution)/shard_map/ppermute | solution.py:140
  30.1 5.8 %increments.3 = (f32[4,2,96,256]{3,2,1,0:T(8,128)S(1)}, bf16[2,2,96,256]{3,2,1,0:T(8,128)(2,1)S(1)}, bf16[2,2,96,256]{3,2,1,0:T(8,128)(2,1)S(1)}) custom-call(s32[3]{0:T(128)S(1)} %pad_add_fusion.ids, bf16[2,2,96,256]{3,2,1,0:T(8,128)(2,1)S(1)} %pad_maximum_fusion.near_low, bf16[2,2,96,256]{3,2,1,0:T(8,128)(2,1)S(1)} %pad_maximum_fusion.1.near_high, ...), custom_call_target="tpu_custom_call" | custom-call | flops 3221225472 | bytes 2097152 | tf_op jit(solution)/shard_map/increments/pallas_call | solution.py:387
  35.9 1.3 %collective-permute-start.19 = (bf16[2,2,96,256]{3,2,1,0:T(8,128)(2,1)S(1)}, bf16[2,2,96,256]{3,2,1,0:T(8,128)(2,1)S(1)}, u32[]{:S(2)}, u32[]{:S(2)}) collective-permute-start(bf16[2,2,96,256]{3,2,1,0:T(8,128)(2,1)S(1)} %get-tuple-element.68), channel_id=1, source_target_pairs={{0,2},{1,3},{2,0},{3,1},{4,6},{5,7},{6,4},{7,5},{8,10},{9,11},{10,... | collective-permute-start | bytes 589832 | tf_op jit(solution)/shard_map/ppermute | solution.py:140
  37.2 0.3 collective-permute-start.8
  37.4 1.2 %collective-permute-start.11 = (bf16[2,2,96,256]{3,2,1,0:T(8,128)(2,1)S(1)}, bf16[2,2,96,256]{3,2,1,0:T(8,128)(2,1)S(1)}, u32[]{:S(2)}, u32[]{:S(2)}) collective-permute-start(bf16[2,2,96,256]{3,2,1,0:T(8,128)(2,1)S(1)} %collective-permute-done.10.far_high), channel_id=1, source_target_pairs={{0,16},{16,0},{1,17},{17,1},{2,18},{18,2},{3,19},{19,3},{4,20},{20... | collective-permute-start | bytes 589832 | tf_op jit(solution)/shard_map/ppermute | solution.py:144
  38.7 0.2 collective-permute-start.17
  38.9 1.6 %collective-permute-done.19.came = bf16[2,2,96,256]{3,2,1,0:T(8,128)(2,1)S(1)} collective-permute-done((bf16[2,2,96,256]{3,2,1,0:T(8,128)(2,1)S(1)}, bf16[2,2,96,256]{3,2,1,0:T(8,128)(2,1)S(1)}, u32[]{:S(2)}, u32[]{:S(2)}) %collective-permute-start.19) | collective-permute-done | bytes 196640 | tf_op jit(solution)/shard_map/ppermute | solution.py:140
  40.5 3.3 %collective-permute-start.20 = (bf16[2,96,256]{2,1,0:T(8,128)(2,1)S(1)}, bf16[2,96,256]{2,1,0:T(8,128)(2,1)S(1)}, u32[]{:S(2)}, u32[]{:S(2)}) collective-permute-start(bf16[2,96,256]{2,1,0:T(8,128)(2,1)S(1)} %get-tuple-element.69), channel_id=1, source_target_pairs={{0,8},{1,9},{2,10},{3,11},{4,12},{5,13},{6,14},{7,15},{8,0},{9,1},... | collective-permute-start | bytes 294920 | tf_op jit(solution)/shard_map/ppermute | solution.py:140
  43.9 1.2 %collective-permute-start.21 = (bf16[2,96,256]{2,1,0:T(8,128)(2,1)S(1)}, bf16[2,96,256]{2,1,0:T(8,128)(2,1)S(1)}, u32[]{:S(2)}, u32[]{:S(2)}) collective-permute-start(bf16[2,96,256]{2,1,0:T(8,128)(2,1)S(1)} %get-tuple-element.70), channel_id=1, source_target_pairs={{0,12},{1,13},{2,14},{3,15},{4,8},{5,9},{6,10},{7,11},{8,4},{9,5},... | collective-permute-start | bytes 294920 | tf_op jit(solution)/shard_map/ppermute | solution.py:140
  45.0 5.9 %increments.2 = (f32[4,2,96,256]{3,2,1,0:T(8,128)S(1)}, bf16[2,2,96,256]{3,2,1,0:T(8,128)(2,1)S(1)}, bf16[2,2,96,256]{3,2,1,0:T(8,128)(2,1)S(1)}) custom-call(s32[3]{0:T(128)S(1)} %pad_add_fusion.ids, bf16[2,2,96,256]{3,2,1,0:T(8,128)(2,1)S(1)} %collective-permute-done.4.near_low, bf16[2,2,96,256]{3,2,1,0:T(8,128)(2,1)S(1)} %collective-permute-done.8.near_high, ...), custom_call_target="tpu_custom_call" | custom-call | flops 3221225472 | bytes 2097152 | tf_op jit(solution)/shard_map/increments/pallas_call | solution.py:387
  51.0 1.3 %collective-permute-start.14 = (bf16[2,2,96,256]{3,2,1,0:T(8,128)(2,1)S(1)}, bf16[2,2,96,256]{3,2,1,0:T(8,128)(2,1)S(1)}, u32[]{:S(2)}, u32[]{:S(2)}) collective-permute-start(bf16[2,2,96,256]{3,2,1,0:T(8,128)(2,1)S(1)} %get-tuple-element.58), channel_id=1, source_target_pairs={{0,2},{1,3},{2,0},{3,1},{4,6},{5,7},{6,4},{7,5},{8,10},{9,11},{10,... | collective-permute-start | bytes 589832 | tf_op jit(solution)/shard_map/ppermute | solution.py:140
  52.3 1.5 %collective-permute-start.18 = (bf16[2,96,256]{2,1,0:T(8,128)(2,1)S(1)}, bf16[2,96,256]{2,1,0:T(8,128)(2,1)S(1)}, u32[]{:S(2)}, u32[]{:S(2)}) collective-permute-start(bf16[2,96,256]{2,1,0:T(8,128)(2,1)S(1)} %get-tuple-element.67), channel_id=1, source_target_pairs={{0,4},{1,5},{2,6},{3,7},{4,0},{5,1},{6,2},{7,3},{8,12},{9,13},{10,... | collective-permute-start | bytes 294920 | tf_op jit(solution)/shard_map/ppermute | solution.py:140
  53.8 1.2 %collective-permute-start.12 = (bf16[2,2,96,256]{3,2,1,0:T(8,128)(2,1)S(1)}, bf16[2,2,96,256]{3,2,1,0:T(8,128)(2,1)S(1)}, u32[]{:S(2)}, u32[]{:S(2)}) collective-permute-start(bf16[2,2,96,256]{3,2,1,0:T(8,128)(2,1)S(1)} %get-tuple-element.55), channel_id=1, source_target_pairs={{0,2},{1,3},{2,0},{3,1},{4,6},{5,7},{6,4},{7,5},{8,10},{9,11},{10,... | collective-permute-start | bytes 589832 | tf_op jit(solution)/shard_map/ppermute | solution.py:140
  55.1 1.4 %collective-permute-done.18.one = bf16[2,96,256]{2,1,0:T(8,128)(2,1)S(1)} collective-permute-done((bf16[2,96,256]{2,1,0:T(8,128)(2,1)S(1)}, bf16[2,96,256]{2,1,0:T(8,128)(2,1)S(1)}, u32[]{:S(2)}, u32[]{:S(2)}) %collective-permute-start.18) | collective-permute-done | bytes 98336 | tf_op jit(solution)/shard_map/ppermute | solution.py:140
  56.4 0.1 renorm.3
  56.6 0.9 collective-permute-start.22
  57.5 1.0 collective-permute-start.24
  58.5 1.7 %collective-permute-start.25 = (bf16[2,96,256]{2,1,0:T(8,128)(2,1)S(1)}, bf16[2,96,256]{2,1,0:T(8,128)(2,1)S(1)}, u32[]{:S(2)}, u32[]{:S(2)}) collective-permute-start(bf16[2,96,256]{2,1,0:T(8,128)(2,1)S(1)} %get-tuple-element.71), channel_id=1, source_target_pairs={{0,12},{1,13},{2,14},{3,15},{4,8},{5,9},{6,10},{7,11},{8,4},{9,5},... | collective-permute-start | bytes 294920 | tf_op jit(solution)/shard_map/ppermute | solution.py:140
  60.3 0.9 collective-permute-start.15
  61.2 1.2 %collective-permute-start.16 = (bf16[2,96,256]{2,1,0:T(8,128)(2,1)S(1)}, bf16[2,96,256]{2,1,0:T(8,128)(2,1)S(1)}, u32[]{:S(2)}, u32[]{:S(2)}) collective-permute-start(bf16[2,96,256]{2,1,0:T(8,128)(2,1)S(1)} %get-tuple-element.60), channel_id=1, source_target_pairs={{0,12},{1,13},{2,14},{3,15},{4,8},{5,9},{6,10},{7,11},{8,4},{9,5},... | collective-permute-start | bytes 294920 | tf_op jit(solution)/shard_map/ppermute | solution.py:140
  62.4 0.7 collective-permute-start.13
  63.1 5.6 %collective-permute-done.15.two = bf16[2,96,256]{2,1,0:T(8,128)(2,1)S(1)} collective-permute-done((bf16[2,96,256]{2,1,0:T(8,128)(2,1)S(1)}, bf16[2,96,256]{2,1,0:T(8,128)(2,1)S(1)}, u32[]{:S(2)}, u32[]{:S(2)}) %collective-permute-start.15) | collective-permute-done | bytes 98336 | tf_op jit(solution)/shard_map/ppermute | solution.py:140
  68.8 1.6 %collective-permute-start.35 = (bf16[2,2,96,256]{3,2,1,0:T(8,128)(2,1)S(1)}, bf16[2,2,96,256]{3,2,1,0:T(8,128)(2,1)S(1)}, u32[]{:S(2)}, u32[]{:S(2)}) collective-permute-start(bf16[2,2,96,256]{3,2,1,0:T(8,128)(2,1)S(1)} %pad_maximum_fusion.2.near_low), channel_id=1, source_target_pairs={{0,2},{1,3},{2,0},{3,1},{4,6},{5,7},{6,4},{7,5},{8,10},{9,11},{10,... | collective-permute-start | bytes 589832 | tf_op jit(solution)/shard_map/ppermute | solution.py:140
  70.4 0.1 renorm.2
  70.5 2.8 %collective-permute-start.23 = (bf16[2,96,256]{2,1,0:T(8,128)(2,1)S(1)}, bf16[2,96,256]{2,1,0:T(8,128)(2,1)S(1)}, u32[]{:S(2)}, u32[]{:S(2)}) collective-permute-start(bf16[2,96,256]{2,1,0:T(8,128)(2,1)S(1)} %get-tuple-element.74), channel_id=1, source_target_pairs={{0,4},{1,5},{2,6},{3,7},{4,0},{5,1},{6,2},{7,3},{8,12},{9,13},{10,... | collective-permute-start | bytes 294920 | tf_op jit(solution)/shard_map/ppermute | solution.py:140
  73.4 3.9 %collective-permute-start.37 = (bf16[2,2,96,256]{3,2,1,0:T(8,128)(2,1)S(1)}, bf16[2,2,96,256]{3,2,1,0:T(8,128)(2,1)S(1)}, u32[]{:S(2)}, u32[]{:S(2)}) collective-permute-start(bf16[2,2,96,256]{3,2,1,0:T(8,128)(2,1)S(1)} %pad_maximum_fusion.4.near_high), channel_id=1, source_target_pairs={{0,2},{1,3},{2,0},{3,1},{4,6},{5,7},{6,4},{7,5},{8,10},{9,11},{10,... | collective-permute-start | bytes 589832 | tf_op jit(solution)/shard_map/ppermute | solution.py:140
  77.3 3.5 %collective-permute-start.34 = (bf16[2,2,96,256]{3,2,1,0:T(8,128)(2,1)S(1)}, bf16[2,2,96,256]{3,2,1,0:T(8,128)(2,1)S(1)}, u32[]{:S(2)}, u32[]{:S(2)}) collective-permute-start(bf16[2,2,96,256]{3,2,1,0:T(8,128)(2,1)S(1)} %pad_maximum_fusion.4.near_high), channel_id=1, source_target_pairs={{0,1},{1,0},{2,3},{3,2},{4,5},{5,4},{6,7},{7,6},{8,9},{9,8},{10,11... | collective-permute-start | bytes 589832 | tf_op jit(solution)/shard_map/ppermute | solution.py:140
  80.9 1.6 %collective-permute-start.27 = (bf16[2,96,256]{2,1,0:T(8,128)(2,1)S(1)}, bf16[2,96,256]{2,1,0:T(8,128)(2,1)S(1)}, u32[]{:S(2)}, u32[]{:S(2)}) collective-permute-start(bf16[2,96,256]{2,1,0:T(8,128)(2,1)S(1)} %get-tuple-element.74), channel_id=1, source_target_pairs={{0,8},{1,9},{2,10},{3,11},{4,12},{5,13},{6,14},{7,15},{8,0},{9,1},... | collective-permute-start | bytes 294920 | tf_op jit(solution)/shard_map/ppermute | solution.py:140
  82.4 1.3 %collective-permute-start.28 = (bf16[2,96,256]{2,1,0:T(8,128)(2,1)S(1)}, bf16[2,96,256]{2,1,0:T(8,128)(2,1)S(1)}, u32[]{:S(2)}, u32[]{:S(2)}) collective-permute-start(bf16[2,96,256]{2,1,0:T(8,128)(2,1)S(1)} %get-tuple-element.74), channel_id=1, source_target_pairs={{0,12},{1,13},{2,14},{3,15},{4,8},{5,9},{6,10},{7,11},{8,4},{9,5},... | collective-permute-start | bytes 294920 | tf_op jit(solution)/shard_map/ppermute | solution.py:140
  83.7 2.6 %collective-permute-start.39 = (f32[2,96,256]{2,1,0:T(8,128)S(1)}, f32[2,96,256]{2,1,0:T(8,128)S(1)}, u32[]{:S(2)}, u32[]{:S(2)}) collective-permute-start(f32[2,96,256]{2,1,0:T(8,128)S(1)} %pad_maximum_fusion.6), channel_id=1, source_target_pairs={{0,1},{1,0},{2,3},{3,2},{4,5},{5,4},{6,7},{7,6},{8,9},{9,8},{10,11... | collective-permute-start | bytes 589832 | tf_op jit(solution)/shard_map/ppermute | solution.py:140
  86.4 0.1 collective-permute-start.33
  86.4 1.3 %collective-permute-start.30 = (bf16[2,2,96,256]{3,2,1,0:T(8,128)(2,1)S(1)}, bf16[2,2,96,256]{3,2,1,0:T(8,128)(2,1)S(1)}, u32[]{:S(2)}, u32[]{:S(2)}) collective-permute-start(bf16[2,2,96,256]{3,2,1,0:T(8,128)(2,1)S(1)} %pad_maximum_fusion.3.near_low), channel_id=1, source_target_pairs={{0,2},{1,3},{2,0},{3,1},{4,6},{5,7},{6,4},{7,5},{8,10},{9,11},{10,... | collective-permute-start | bytes 589832 | tf_op jit(solution)/shard_map/ppermute | solution.py:140
  87.7 4.6 %collective-permute-start.38 = (bf16[2,2,96,256]{3,2,1,0:T(8,128)(2,1)S(1)}, bf16[2,2,96,256]{3,2,1,0:T(8,128)(2,1)S(1)}, u32[]{:S(2)}, u32[]{:S(2)}) collective-permute-start(bf16[2,2,96,256]{3,2,1,0:T(8,128)(2,1)S(1)} %collective-permute-done.37.far_high), channel_id=1, source_target_pairs={{0,1},{1,0},{2,3},{3,2},{4,5},{5,4},{6,7},{7,6},{8,9},{9,8},{10,11... | collective-permute-start | bytes 589832 | tf_op jit(solution)/shard_map/ppermute | solution.py:140
  92.4 0.5 collective-permute-start.32
  92.9 2.6 %apply.4.rest_0_ = bf16[1024,1024]{1,0:T(8,128)(2,1)} custom-call(s32[3]{0:T(128)S(1)} %pad_add_fusion.ids, bf16[2,2,96,256]{3,2,1,0:T(8,128)(2,1)S(1)} %pad_maximum_fusion.2.near_low, bf16[2,2,96,256]{3,2,1,0:T(8,128)(2,1)S(1)} %pad_maximum_fusion.4.near_high, bf16[2,2,96,256]{3,2,1,0:T(8,128)(2,1)S(1)} %collective-permute-done.35.far_low, ...), custom_call_target="tpu_custom_call" | custom-call | flops 805306368 | bytes 1048576 | tf_op jit(solution)/shard_map/apply/pallas_call | solution.py:507
  95.5 1.3 %finish.1 = (f32[4,16,1024]{2,1,0:T(8,128)}, f32[4,32,256]{2,1,0:T(8,128)}) custom-call(s32[3]{0:T(128)S(1)} %pad_add_fusion.ids, f32[2,96,256]{2,1,0:T(8,128)S(1)} %get-tuple-element.75.one, f32[2,96,256]{2,1,0:T(8,128)S(1)} %get-tuple-element.76.two, f32[2,96,256]{2,1,0:T(8,128)S(1)} %collective-permute-done.39.came), custom_call_target="tpu_custom_call" | custom-call | tf_op jit(solution)/shard_map/finish/pallas_call | solution.py:539
  96.8 0.8 collective-permute-start.26
  97.6 0.1 collective-permute-start.29
  97.6 0.4 collective-permute-start.31
  98.1 2.6 %apply.5.rest_0_ = bf16[1024,1024]{1,0:T(8,128)(2,1)} custom-call(s32[3]{0:T(128)S(1)} %pad_add_fusion.ids, bf16[2,2,96,256]{3,2,1,0:T(8,128)(2,1)S(1)} %collective-permute-done.33.near_low, bf16[2,2,96,256]{3,2,1,0:T(8,128)(2,1)S(1)} %collective-permute-done.34.near_high, ...), custom_call_target="tpu_custom_call", output_to_operand_aliasing={{}: (6, {})} | custom-call | flops 805306368 | bytes 1048576 | tf_op jit(solution)/shard_map/apply/pallas_call | solution.py:507
  100.7 0.1 collective-permute-start.40
  100.7 2.6 %apply.6.rest_0_ = bf16[1024,1024]{1,0:T(8,128)(2,1)} custom-call(s32[3]{0:T(128)S(1)} %pad_add_fusion.ids, bf16[2,2,96,256]{3,2,1,0:T(8,128)(2,1)S(1)} %pad_maximum_fusion.3.near_low, bf16[2,2,96,256]{3,2,1,0:T(8,128)(2,1)S(1)} %pad_maximum_fusion.5.near_high, ...), custom_call_target="tpu_custom_call", output_to_operand_aliasing={{}: (6, {})} | custom-call | flops 805306368 | bytes 1048576 | tf_op jit(solution)/shard_map/apply/pallas_call | solution.py:507
  103.3 2.6 %apply.7 = bf16[1024,1024]{1,0:T(8,128)(2,1)} custom-call(s32[3]{0:T(128)S(1)} %pad_add_fusion.ids, bf16[2,2,96,256]{3,2,1,0:T(8,128)(2,1)S(1)} %collective-permute-done.26.near_low, bf16[2,2,96,256]{3,2,1,0:T(8,128)(2,1)S(1)} %collective-permute-done.29.near_high, ...), custom_call_target="tpu_custom_call", output_to_operand_aliasing={{}: (6, {})} | custom-call | flops 805306368 | bytes 1048576 | tf_op jit(solution)/shard_map/apply/pallas_call | solution.py:507
  (57 shorter events, 0.5 us)
Async XLA Ops:
  0.6 6.0 %copy-start.5 = (f32[4,1024]{1,0:T(4,128)S(1)}, f32[4,1024]{1,0:T(4,128)}, u32[]{:S(2)}) copy-start(f32[4,1024]{1,0:T(4,128)} %rest_0_.1) | copy-start | bytes 49156
  0.7 1.0 copy-start.3
  1.7 0.9 copy-start.4
  3.4 1.6 %copy-start.1 = (bf16[1024,1024]{1,0:T(8,128)(2,1)S(1)}, bf16[1024,1024]{1,0:T(8,128)(2,1)}, u32[]{:S(2)}) copy-start(bf16[1024,1024]{1,0:T(8,128)(2,1)} %x_ref.2) | copy-start | bytes 6291460
  5.0 1.6 %copy-start.2 = (bf16[1024,1024]{1,0:T(8,128)(2,1)S(1)}, bf16[1024,1024]{1,0:T(8,128)(2,1)}, u32[]{:S(2)}) copy-start(bf16[1024,1024]{1,0:T(8,128)(2,1)} %x_ref.3) | copy-start | bytes 6291460
  6.5 11.3 %collective-permute-start.2 = (bf16[1024,512]{1,0:T(8,128)(2,1)S(1)}, bf16[1024,512]{1,0:T(8,128)(2,1)S(1)}, u32[]{:S(2)}, u32[]{:S(2)}) collective-permute-start(bf16[1024,512]{1,0:T(8,128)(2,1)S(1)} %get-tuple-element.45), channel_id=1, source_target_pairs={{0,1},{1,0},{2,3},{3,2},{4,5},{5,4},{6,7},{7,6},{8,9},{9,8},{10,11... | collective-permute-start | bytes 3145736 | tf_op jit(solution)/shard_map/ppermute | solution.py:140
  8.9 8.9 %collective-permute-start.3 = (bf16[1024,512]{1,0:T(8,128)(2,1)S(1)}, bf16[1024,512]{1,0:T(8,128)(2,1)S(1)}, u32[]{:S(2)}, u32[]{:S(2)}) collective-permute-start(bf16[1024,512]{1,0:T(8,128)(2,1)S(1)} %get-tuple-element.46), channel_id=1, source_target_pairs={{0,1},{1,0},{2,3},{3,2},{4,5},{5,4},{6,7},{7,6},{8,9},{9,8},{10,11... | collective-permute-start | bytes 3145736 | tf_op jit(solution)/shard_map/ppermute | solution.py:140
  9.4 2.6 %collective-permute-start = (f32[2,96,256]{2,1,0:T(8,128)S(1)}, f32[2,96,256]{2,1,0:T(8,128)S(1)}, u32[]{:S(2)}, u32[]{:S(2)}) collective-permute-start(f32[2,96,256]{2,1,0:T(8,128)S(1)} %get-tuple-element.43), channel_id=1, source_target_pairs={{0,1},{1,0},{2,3},{3,2},{4,5},{5,4},{6,7},{7,6},{8,9},{9,8},{10,11... | collective-permute-start | bytes 589832 | tf_op jit(solution)/shard_map/ppermute | solution.py:140
  12.0 5.8 %collective-permute-start.1 = (bf16[2,96,256]{2,1,0:T(8,128)(2,1)S(1)}, bf16[2,96,256]{2,1,0:T(8,128)(2,1)S(1)}, u32[]{:S(2)}, u32[]{:S(2)}) collective-permute-start(bf16[2,96,256]{2,1,0:T(8,128)(2,1)S(1)} %get-tuple-element.49), channel_id=1, source_target_pairs={{0,4},{1,5},{2,6},{3,7},{4,0},{5,1},{6,2},{7,3},{8,12},{9,13},{10,... | collective-permute-start | bytes 294920 | tf_op jit(solution)/shard_map/ppermute | solution.py:140
  14.8 5.5 %collective-permute-start.5 = (bf16[2,96,256]{2,1,0:T(8,128)(2,1)S(1)}, bf16[2,96,256]{2,1,0:T(8,128)(2,1)S(1)}, u32[]{:S(2)}, u32[]{:S(2)}) collective-permute-start(bf16[2,96,256]{2,1,0:T(8,128)(2,1)S(1)} %get-tuple-element.49), channel_id=1, source_target_pairs={{0,8},{1,9},{2,10},{3,11},{4,12},{5,13},{6,14},{7,15},{8,0},{9,1},... | collective-permute-start | bytes 294920 | tf_op jit(solution)/shard_map/ppermute | solution.py:140
  17.1 6.9 %collective-permute-start.6 = (bf16[2,96,256]{2,1,0:T(8,128)(2,1)S(1)}, bf16[2,96,256]{2,1,0:T(8,128)(2,1)S(1)}, u32[]{:S(2)}, u32[]{:S(2)}) collective-permute-start(bf16[2,96,256]{2,1,0:T(8,128)(2,1)S(1)} %get-tuple-element.49), channel_id=1, source_target_pairs={{0,12},{1,13},{2,14},{3,15},{4,8},{5,9},{6,10},{7,11},{8,4},{9,5},... | collective-permute-start | bytes 294920 | tf_op jit(solution)/shard_map/ppermute | solution.py:140
  17.8 6.2 %collective-permute-start.7 = (bf16[2,2,96,256]{3,2,1,0:T(8,128)(2,1)S(1)}, bf16[2,2,96,256]{3,2,1,0:T(8,128)(2,1)S(1)}, u32[]{:S(2)}, u32[]{:S(2)}) collective-permute-start(bf16[2,2,96,256]{3,2,1,0:T(8,128)(2,1)S(1)} %pad_maximum_fusion.near_low), channel_id=1, source_target_pairs={{0,2},{1,3},{2,0},{3,1},{4,6},{5,7},{6,4},{7,5},{8,10},{9,11},{10,... | collective-permute-start | bytes 589832 | tf_op jit(solution)/shard_map/ppermute | solution.py:140
  19.1 6.2 %collective-permute-start.4 = (bf16[2,2,96,256]{3,2,1,0:T(8,128)(2,1)S(1)}, bf16[2,2,96,256]{3,2,1,0:T(8,128)(2,1)S(1)}, u32[]{:S(2)}, u32[]{:S(2)}) collective-permute-start(bf16[2,2,96,256]{3,2,1,0:T(8,128)(2,1)S(1)} %pad_maximum_fusion.near_low), channel_id=1, source_target_pairs={{0,16},{16,0},{1,17},{17,1},{2,18},{18,2},{3,19},{19,3},{4,20},{20... | collective-permute-start | bytes 589832 | tf_op jit(solution)/shard_map/ppermute | solution.py:144
  24.0 4.6 %collective-permute-start.9 = (bf16[2,2,96,256]{3,2,1,0:T(8,128)(2,1)S(1)}, bf16[2,2,96,256]{3,2,1,0:T(8,128)(2,1)S(1)}, u32[]{:S(2)}, u32[]{:S(2)}) collective-permute-start(bf16[2,2,96,256]{3,2,1,0:T(8,128)(2,1)S(1)} %collective-permute-done.7.far_low), channel_id=1, source_target_pairs={{0,16},{16,0},{1,17},{17,1},{2,18},{18,2},{3,19},{19,3},{4,20},{20... | collective-permute-start | bytes 589832 | tf_op jit(solution)/shard_map/ppermute | solution.py:144
  25.3 4.8 %collective-permute-start.10 = (bf16[2,2,96,256]{3,2,1,0:T(8,128)(2,1)S(1)}, bf16[2,2,96,256]{3,2,1,0:T(8,128)(2,1)S(1)}, u32[]{:S(2)}, u32[]{:S(2)}) collective-permute-start(bf16[2,2,96,256]{3,2,1,0:T(8,128)(2,1)S(1)} %pad_maximum_fusion.1.near_high), channel_id=1, source_target_pairs={{0,2},{1,3},{2,0},{3,1},{4,6},{5,7},{6,4},{7,5},{8,10},{9,11},{10,... | collective-permute-start | bytes 589832 | tf_op jit(solution)/shard_map/ppermute | solution.py:140
  35.9 4.6 %collective-permute-start.19 = (bf16[2,2,96,256]{3,2,1,0:T(8,128)(2,1)S(1)}, bf16[2,2,96,256]{3,2,1,0:T(8,128)(2,1)S(1)}, u32[]{:S(2)}, u32[]{:S(2)}) collective-permute-start(bf16[2,2,96,256]{3,2,1,0:T(8,128)(2,1)S(1)} %get-tuple-element.68), channel_id=1, source_target_pairs={{0,2},{1,3},{2,0},{3,1},{4,6},{5,7},{6,4},{7,5},{8,10},{9,11},{10,... | collective-permute-start | bytes 589832 | tf_op jit(solution)/shard_map/ppermute | solution.py:140
  37.2 7.8 %collective-permute-start.8 = (bf16[2,2,96,256]{3,2,1,0:T(8,128)(2,1)S(1)}, bf16[2,2,96,256]{3,2,1,0:T(8,128)(2,1)S(1)}, u32[]{:S(2)}, u32[]{:S(2)}) collective-permute-start(bf16[2,2,96,256]{3,2,1,0:T(8,128)(2,1)S(1)} %pad_maximum_fusion.1.near_high), channel_id=1, source_target_pairs={{0,16},{16,0},{1,17},{17,1},{2,18},{18,2},{3,19},{19,3},{4,20},{20... | collective-permute-start | bytes 589832 | tf_op jit(solution)/shard_map/ppermute | solution.py:144
  37.4 7.6 %collective-permute-start.11 = (bf16[2,2,96,256]{3,2,1,0:T(8,128)(2,1)S(1)}, bf16[2,2,96,256]{3,2,1,0:T(8,128)(2,1)S(1)}, u32[]{:S(2)}, u32[]{:S(2)}) collective-permute-start(bf16[2,2,96,256]{3,2,1,0:T(8,128)(2,1)S(1)} %collective-permute-done.10.far_high), channel_id=1, source_target_pairs={{0,16},{16,0},{1,17},{17,1},{2,18},{18,2},{3,19},{19,3},{4,20},{20... | collective-permute-start | bytes 589832 | tf_op jit(solution)/shard_map/ppermute | solution.py:144
  38.7 13.6 %collective-permute-start.17 = (bf16[2,2,96,256]{3,2,1,0:T(8,128)(2,1)S(1)}, bf16[2,2,96,256]{3,2,1,0:T(8,128)(2,1)S(1)}, u32[]{:S(2)}, u32[]{:S(2)}) collective-permute-start(bf16[2,2,96,256]{3,2,1,0:T(8,128)(2,1)S(1)} %get-tuple-element.65), channel_id=1, source_target_pairs={{0,2},{1,3},{2,0},{3,1},{4,6},{5,7},{6,4},{7,5},{8,10},{9,11},{10,... | collective-permute-start | bytes 589832 | tf_op jit(solution)/shard_map/ppermute | solution.py:140
  40.5 14.5 %collective-permute-start.20 = (bf16[2,96,256]{2,1,0:T(8,128)(2,1)S(1)}, bf16[2,96,256]{2,1,0:T(8,128)(2,1)S(1)}, u32[]{:S(2)}, u32[]{:S(2)}) collective-permute-start(bf16[2,96,256]{2,1,0:T(8,128)(2,1)S(1)} %get-tuple-element.69), channel_id=1, source_target_pairs={{0,8},{1,9},{2,10},{3,11},{4,12},{5,13},{6,14},{7,15},{8,0},{9,1},... | collective-permute-start | bytes 294920 | tf_op jit(solution)/shard_map/ppermute | solution.py:140
  43.9 11.2 %collective-permute-start.21 = (bf16[2,96,256]{2,1,0:T(8,128)(2,1)S(1)}, bf16[2,96,256]{2,1,0:T(8,128)(2,1)S(1)}, u32[]{:S(2)}, u32[]{:S(2)}) collective-permute-start(bf16[2,96,256]{2,1,0:T(8,128)(2,1)S(1)} %get-tuple-element.70), channel_id=1, source_target_pairs={{0,12},{1,13},{2,14},{3,15},{4,8},{5,9},{6,10},{7,11},{8,4},{9,5},... | collective-permute-start | bytes 294920 | tf_op jit(solution)/shard_map/ppermute | solution.py:140
  51.0 9.2 %collective-permute-start.14 = (bf16[2,2,96,256]{3,2,1,0:T(8,128)(2,1)S(1)}, bf16[2,2,96,256]{3,2,1,0:T(8,128)(2,1)S(1)}, u32[]{:S(2)}, u32[]{:S(2)}) collective-permute-start(bf16[2,2,96,256]{3,2,1,0:T(8,128)(2,1)S(1)} %get-tuple-element.58), channel_id=1, source_target_pairs={{0,2},{1,3},{2,0},{3,1},{4,6},{5,7},{6,4},{7,5},{8,10},{9,11},{10,... | collective-permute-start | bytes 589832 | tf_op jit(solution)/shard_map/ppermute | solution.py:140
  52.3 4.1 %collective-permute-start.18 = (bf16[2,96,256]{2,1,0:T(8,128)(2,1)S(1)}, bf16[2,96,256]{2,1,0:T(8,128)(2,1)S(1)}, u32[]{:S(2)}, u32[]{:S(2)}) collective-permute-start(bf16[2,96,256]{2,1,0:T(8,128)(2,1)S(1)} %get-tuple-element.67), channel_id=1, source_target_pairs={{0,4},{1,5},{2,6},{3,7},{4,0},{5,1},{6,2},{7,3},{8,12},{9,13},{10,... | collective-permute-start | bytes 294920 | tf_op jit(solution)/shard_map/ppermute | solution.py:140
  53.8 7.3 %collective-permute-start.12 = (bf16[2,2,96,256]{3,2,1,0:T(8,128)(2,1)S(1)}, bf16[2,2,96,256]{3,2,1,0:T(8,128)(2,1)S(1)}, u32[]{:S(2)}, u32[]{:S(2)}) collective-permute-start(bf16[2,2,96,256]{3,2,1,0:T(8,128)(2,1)S(1)} %get-tuple-element.55), channel_id=1, source_target_pairs={{0,2},{1,3},{2,0},{3,1},{4,6},{5,7},{6,4},{7,5},{8,10},{9,11},{10,... | collective-permute-start | bytes 589832 | tf_op jit(solution)/shard_map/ppermute | solution.py:140
  56.6 5.9 %collective-permute-start.22 = (bf16[2,96,256]{2,1,0:T(8,128)(2,1)S(1)}, bf16[2,96,256]{2,1,0:T(8,128)(2,1)S(1)}, u32[]{:S(2)}, u32[]{:S(2)}) collective-permute-start(bf16[2,96,256]{2,1,0:T(8,128)(2,1)S(1)} %get-tuple-element.71), channel_id=1, source_target_pairs={{0,4},{1,5},{2,6},{3,7},{4,0},{5,1},{6,2},{7,3},{8,12},{9,13},{10,... | collective-permute-start | bytes 294920 | tf_op jit(solution)/shard_map/ppermute | solution.py:140
  57.5 15.9 %collective-permute-start.24 = (bf16[2,96,256]{2,1,0:T(8,128)(2,1)S(1)}, bf16[2,96,256]{2,1,0:T(8,128)(2,1)S(1)}, u32[]{:S(2)}, u32[]{:S(2)}) collective-permute-start(bf16[2,96,256]{2,1,0:T(8,128)(2,1)S(1)} %get-tuple-element.71), channel_id=1, source_target_pairs={{0,8},{1,9},{2,10},{3,11},{4,12},{5,13},{6,14},{7,15},{8,0},{9,1},... | collective-permute-start | bytes 294920 | tf_op jit(solution)/shard_map/ppermute | solution.py:140
  58.5 14.9 %collective-permute-start.25 = (bf16[2,96,256]{2,1,0:T(8,128)(2,1)S(1)}, bf16[2,96,256]{2,1,0:T(8,128)(2,1)S(1)}, u32[]{:S(2)}, u32[]{:S(2)}) collective-permute-start(bf16[2,96,256]{2,1,0:T(8,128)(2,1)S(1)} %get-tuple-element.71), channel_id=1, source_target_pairs={{0,12},{1,13},{2,14},{3,15},{4,8},{5,9},{6,10},{7,11},{8,4},{9,5},... | collective-permute-start | bytes 294920 | tf_op jit(solution)/shard_map/ppermute | solution.py:140
  60.3 32.6 %copy-start = (bf16[1024,1024]{1,0:T(8,128)(2,1)S(1)}, bf16[1024,1024]{1,0:T(8,128)(2,1)}, u32[]{:S(2)}) copy-start(bf16[1024,1024]{1,0:T(8,128)(2,1)} %q_ref.7) | copy-start | bytes 6291460
  60.3 8.5 %collective-permute-start.15 = (bf16[2,96,256]{2,1,0:T(8,128)(2,1)S(1)}, bf16[2,96,256]{2,1,0:T(8,128)(2,1)S(1)}, u32[]{:S(2)}, u32[]{:S(2)}) collective-permute-start(bf16[2,96,256]{2,1,0:T(8,128)(2,1)S(1)} %get-tuple-element.59), channel_id=1, source_target_pairs={{0,8},{1,9},{2,10},{3,11},{4,12},{5,13},{6,14},{7,15},{8,0},{9,1},... | collective-permute-start | bytes 294920 | tf_op jit(solution)/shard_map/ppermute | solution.py:140
  61.2 9.2 %collective-permute-start.16 = (bf16[2,96,256]{2,1,0:T(8,128)(2,1)S(1)}, bf16[2,96,256]{2,1,0:T(8,128)(2,1)S(1)}, u32[]{:S(2)}, u32[]{:S(2)}) collective-permute-start(bf16[2,96,256]{2,1,0:T(8,128)(2,1)S(1)} %get-tuple-element.60), channel_id=1, source_target_pairs={{0,12},{1,13},{2,14},{3,15},{4,8},{5,9},{6,10},{7,11},{8,4},{9,5},... | collective-permute-start | bytes 294920 | tf_op jit(solution)/shard_map/ppermute | solution.py:140
  62.4 7.9 %collective-permute-start.13 = (bf16[2,96,256]{2,1,0:T(8,128)(2,1)S(1)}, bf16[2,96,256]{2,1,0:T(8,128)(2,1)S(1)}, u32[]{:S(2)}, u32[]{:S(2)}) collective-permute-start(bf16[2,96,256]{2,1,0:T(8,128)(2,1)S(1)} %get-tuple-element.57), channel_id=1, source_target_pairs={{0,4},{1,5},{2,6},{3,7},{4,0},{5,1},{6,2},{7,3},{8,12},{9,13},{10,... | collective-permute-start | bytes 294920 | tf_op jit(solution)/shard_map/ppermute | solution.py:140
  68.8 17.6 %collective-permute-start.35 = (bf16[2,2,96,256]{3,2,1,0:T(8,128)(2,1)S(1)}, bf16[2,2,96,256]{3,2,1,0:T(8,128)(2,1)S(1)}, u32[]{:S(2)}, u32[]{:S(2)}) collective-permute-start(bf16[2,2,96,256]{3,2,1,0:T(8,128)(2,1)S(1)} %pad_maximum_fusion.2.near_low), channel_id=1, source_target_pairs={{0,2},{1,3},{2,0},{3,1},{4,6},{5,7},{6,4},{7,5},{8,10},{9,11},{10,... | collective-permute-start | bytes 589832 | tf_op jit(solution)/shard_map/ppermute | solution.py:140
  70.5 10.3 %collective-permute-start.23 = (bf16[2,96,256]{2,1,0:T(8,128)(2,1)S(1)}, bf16[2,96,256]{2,1,0:T(8,128)(2,1)S(1)}, u32[]{:S(2)}, u32[]{:S(2)}) collective-permute-start(bf16[2,96,256]{2,1,0:T(8,128)(2,1)S(1)} %get-tuple-element.74), channel_id=1, source_target_pairs={{0,4},{1,5},{2,6},{3,7},{4,0},{5,1},{6,2},{7,3},{8,12},{9,13},{10,... | collective-permute-start | bytes 294920 | tf_op jit(solution)/shard_map/ppermute | solution.py:140
  73.4 10.3 %collective-permute-start.37 = (bf16[2,2,96,256]{3,2,1,0:T(8,128)(2,1)S(1)}, bf16[2,2,96,256]{3,2,1,0:T(8,128)(2,1)S(1)}, u32[]{:S(2)}, u32[]{:S(2)}) collective-permute-start(bf16[2,2,96,256]{3,2,1,0:T(8,128)(2,1)S(1)} %pad_maximum_fusion.4.near_high), channel_id=1, source_target_pairs={{0,2},{1,3},{2,0},{3,1},{4,6},{5,7},{6,4},{7,5},{8,10},{9,11},{10,... | collective-permute-start | bytes 589832 | tf_op jit(solution)/shard_map/ppermute | solution.py:140
  77.3 9.1 %collective-permute-start.34 = (bf16[2,2,96,256]{3,2,1,0:T(8,128)(2,1)S(1)}, bf16[2,2,96,256]{3,2,1,0:T(8,128)(2,1)S(1)}, u32[]{:S(2)}, u32[]{:S(2)}) collective-permute-start(bf16[2,2,96,256]{3,2,1,0:T(8,128)(2,1)S(1)} %pad_maximum_fusion.4.near_high), channel_id=1, source_target_pairs={{0,1},{1,0},{2,3},{3,2},{4,5},{5,4},{6,7},{7,6},{8,9},{9,8},{10,11... | collective-permute-start | bytes 589832 | tf_op jit(solution)/shard_map/ppermute | solution.py:140
  80.9 6.8 %collective-permute-start.27 = (bf16[2,96,256]{2,1,0:T(8,128)(2,1)S(1)}, bf16[2,96,256]{2,1,0:T(8,128)(2,1)S(1)}, u32[]{:S(2)}, u32[]{:S(2)}) collective-permute-start(bf16[2,96,256]{2,1,0:T(8,128)(2,1)S(1)} %get-tuple-element.74), channel_id=1, source_target_pairs={{0,8},{1,9},{2,10},{3,11},{4,12},{5,13},{6,14},{7,15},{8,0},{9,1},... | collective-permute-start | bytes 294920 | tf_op jit(solution)/shard_map/ppermute | solution.py:140
  82.4 9.9 %collective-permute-start.28 = (bf16[2,96,256]{2,1,0:T(8,128)(2,1)S(1)}, bf16[2,96,256]{2,1,0:T(8,128)(2,1)S(1)}, u32[]{:S(2)}, u32[]{:S(2)}) collective-permute-start(bf16[2,96,256]{2,1,0:T(8,128)(2,1)S(1)} %get-tuple-element.74), channel_id=1, source_target_pairs={{0,12},{1,13},{2,14},{3,15},{4,8},{5,9},{6,10},{7,11},{8,4},{9,5},... | collective-permute-start | bytes 294920 | tf_op jit(solution)/shard_map/ppermute | solution.py:140
  83.7 8.6 %collective-permute-start.39 = (f32[2,96,256]{2,1,0:T(8,128)S(1)}, f32[2,96,256]{2,1,0:T(8,128)S(1)}, u32[]{:S(2)}, u32[]{:S(2)}) collective-permute-start(f32[2,96,256]{2,1,0:T(8,128)S(1)} %pad_maximum_fusion.6), channel_id=1, source_target_pairs={{0,1},{1,0},{2,3},{3,2},{4,5},{5,4},{6,7},{7,6},{8,9},{9,8},{10,11... | collective-permute-start | bytes 589832 | tf_op jit(solution)/shard_map/ppermute | solution.py:140
  86.4 10.4 %collective-permute-start.33 = (bf16[2,2,96,256]{3,2,1,0:T(8,128)(2,1)S(1)}, bf16[2,2,96,256]{3,2,1,0:T(8,128)(2,1)S(1)}, u32[]{:S(2)}, u32[]{:S(2)}) collective-permute-start(bf16[2,2,96,256]{3,2,1,0:T(8,128)(2,1)S(1)} %pad_maximum_fusion.2.near_low), channel_id=1, source_target_pairs={{0,1},{1,0},{2,3},{3,2},{4,5},{5,4},{6,7},{7,6},{8,9},{9,8},{10,11... | collective-permute-start | bytes 589832 | tf_op jit(solution)/shard_map/ppermute | solution.py:140
  86.4 11.2 %collective-permute-start.30 = (bf16[2,2,96,256]{3,2,1,0:T(8,128)(2,1)S(1)}, bf16[2,2,96,256]{3,2,1,0:T(8,128)(2,1)S(1)}, u32[]{:S(2)}, u32[]{:S(2)}) collective-permute-start(bf16[2,2,96,256]{3,2,1,0:T(8,128)(2,1)S(1)} %pad_maximum_fusion.3.near_low), channel_id=1, source_target_pairs={{0,2},{1,3},{2,0},{3,1},{4,6},{5,7},{6,4},{7,5},{8,10},{9,11},{10,... | collective-permute-start | bytes 589832 | tf_op jit(solution)/shard_map/ppermute | solution.py:140
  87.7 9.8 %collective-permute-start.38 = (bf16[2,2,96,256]{3,2,1,0:T(8,128)(2,1)S(1)}, bf16[2,2,96,256]{3,2,1,0:T(8,128)(2,1)S(1)}, u32[]{:S(2)}, u32[]{:S(2)}) collective-permute-start(bf16[2,2,96,256]{3,2,1,0:T(8,128)(2,1)S(1)} %collective-permute-done.37.far_high), channel_id=1, source_target_pairs={{0,1},{1,0},{2,3},{3,2},{4,5},{5,4},{6,7},{7,6},{8,9},{9,8},{10,11... | collective-permute-start | bytes 589832 | tf_op jit(solution)/shard_map/ppermute | solution.py:140
  92.3 5.8 %collective-permute-start.36 = (bf16[2,2,96,256]{3,2,1,0:T(8,128)(2,1)S(1)}, bf16[2,2,96,256]{3,2,1,0:T(8,128)(2,1)S(1)}, u32[]{:S(2)}, u32[]{:S(2)}) collective-permute-start(bf16[2,2,96,256]{3,2,1,0:T(8,128)(2,1)S(1)} %collective-permute-done.35.far_low), channel_id=1, source_target_pairs={{0,1},{1,0},{2,3},{3,2},{4,5},{5,4},{6,7},{7,6},{8,9},{9,8},{10,11... | collective-permute-start | bytes 589832 | tf_op jit(solution)/shard_map/ppermute | solution.py:140
  92.4 8.3 %collective-permute-start.32 = (bf16[2,2,96,256]{3,2,1,0:T(8,128)(2,1)S(1)}, bf16[2,2,96,256]{3,2,1,0:T(8,128)(2,1)S(1)}, u32[]{:S(2)}, u32[]{:S(2)}) collective-permute-start(bf16[2,2,96,256]{3,2,1,0:T(8,128)(2,1)S(1)} %pad_maximum_fusion.5.near_high), channel_id=1, source_target_pairs={{0,2},{1,3},{2,0},{3,1},{4,6},{5,7},{6,4},{7,5},{8,10},{9,11},{10,... | collective-permute-start | bytes 589832 | tf_op jit(solution)/shard_map/ppermute | solution.py:140
  96.8 6.5 %collective-permute-start.26 = (bf16[2,2,96,256]{3,2,1,0:T(8,128)(2,1)S(1)}, bf16[2,2,96,256]{3,2,1,0:T(8,128)(2,1)S(1)}, u32[]{:S(2)}, u32[]{:S(2)}) collective-permute-start(bf16[2,2,96,256]{3,2,1,0:T(8,128)(2,1)S(1)} %pad_maximum_fusion.3.near_low), channel_id=1, source_target_pairs={{0,1},{1,0},{2,3},{3,2},{4,5},{5,4},{6,7},{7,6},{8,9},{9,8},{10,11... | collective-permute-start | bytes 589832 | tf_op jit(solution)/shard_map/ppermute | solution.py:140
  97.6 5.8 %collective-permute-start.29 = (bf16[2,2,96,256]{3,2,1,0:T(8,128)(2,1)S(1)}, bf16[2,2,96,256]{3,2,1,0:T(8,128)(2,1)S(1)}, u32[]{:S(2)}, u32[]{:S(2)}) collective-permute-start(bf16[2,2,96,256]{3,2,1,0:T(8,128)(2,1)S(1)} %pad_maximum_fusion.5.near_high), channel_id=1, source_target_pairs={{0,1},{1,0},{2,3},{3,2},{4,5},{5,4},{6,7},{7,6},{8,9},{9,8},{10,11... | collective-permute-start | bytes 589832 | tf_op jit(solution)/shard_map/ppermute | solution.py:140
  97.6 5.7 %collective-permute-start.31 = (bf16[2,2,96,256]{3,2,1,0:T(8,128)(2,1)S(1)}, bf16[2,2,96,256]{3,2,1,0:T(8,128)(2,1)S(1)}, u32[]{:S(2)}, u32[]{:S(2)}) collective-permute-start(bf16[2,2,96,256]{3,2,1,0:T(8,128)(2,1)S(1)} %collective-permute-done.30.far_low), channel_id=1, source_target_pairs={{0,1},{1,0},{2,3},{3,2},{4,5},{5,4},{6,7},{7,6},{8,9},{9,8},{10,11... | collective-permute-start | bytes 589832 | tf_op jit(solution)/shard_map/ppermute | solution.py:140
  100.7 2.7 %collective-permute-start.40 = (bf16[2,2,96,256]{3,2,1,0:T(8,128)(2,1)S(1)}, bf16[2,2,96,256]{3,2,1,0:T(8,128)(2,1)S(1)}, u32[]{:S(2)}, u32[]{:S(2)}) collective-permute-start(bf16[2,2,96,256]{3,2,1,0:T(8,128)(2,1)S(1)} %collective-permute-done.32.far_high), channel_id=1, source_target_pairs={{0,1},{1,0},{2,3},{3,2},{4,5},{5,4},{6,7},{7,6},{8,9},{9,8},{10,11... | collective-permute-start | bytes 589832 | tf_op jit(solution)/shard_map/ppermute | solution.py:140

commit v7 on v6

--- a/solution.py
+++ b/solution.py
@@ -559,11 +559,10 @@
 
     own, theirs = pack(ids, fast_in, fast_out)
     got = swap(theirs, 1)
-    later = after(ids, own)
+    later = after(ids, got)
     k_own, k_send = prepare(later, keys, None, heads, None, "keys")
     v_own, v_send = prepare(later, values, step_size, heads, block_root, "values")
-    got = after(got, k_send, v_send)
-    master_one, master_two, shard = pair(own, got)
+    master_one, master_two, shard = pair(own, after(got, k_send, v_send))
     masters = (master_one, master_two)
     k_got, v_got = swap(k_send, 1), swap(v_send, 1)
     z1, z3, z2 = swap(shard, 4), swap(shard, 12), swap(shard, 8)
@@ -599,10 +598,9 @@
     mine = (near_low, near_high, far_low, far_high)
     others = tuple(swap(piece, 1) for piece in mine)
     output = apply_fast(ids, 0, 0, mine, queries, None, fast)
-    near_low, near_high = second_low, second_high
     came = swap(jnp.stack([wide[0][1], wide[1][1]]), 1)
     updated = finish(ids, wide[0], wide[1], came, fast_in, fast_out)
-    output = after(output, *updated)
+    near_low, near_high = second_low, after(second_high, *updated)
     output = apply_fast(ids, 0, 1, others, queries, output, fast)
     far_low, far_high = swap(near_low, 2), swap(near_high, 2)
     far_high = after(far_high, output)

time: 106 us -> 104 us (0.981)
  starting transfers between devices: 53.8 us -> 45.5 us
  waiting for transfers between devices: 19.2 us -> 24.7 us
    ppermute x37, starting transfers between devices: 49.8 us -> 42.4 us  [swap(): lax.ppermute(value, 'tok', [(place, place ^ bits) for place in range(coun...]
    ppermute x37, waiting for transfers between devices: 17.1 us -> 21.7 us  [swap(): lax.ppermute(value, 'tok', [(place, place ^ bits) for place in range(coun...]
  transfers between devices with their start and end apart: 41 -> 41, of which waited for: 8 -> 11; matrix products, arithmetic and copies ran while one was open for 0% -> 0% of each run, Pallas kernels for 17% -> 23%
where the time goes in v7:
time: 104 us; the launch traced here: 103 us
  starting transfers between devices  45.5 us (44%)
  Pallas kernels  28.4 us (27%)
  waiting for transfers between devices  24.7 us (24%)
  local copies, waits for them, and re-layouts  3.48 us (3%)
    ppermute x37, starting transfers between devices, swap(): lax.ppermute(value, 'tok', [(place, place ^ bits) for place in range(coun...  42.4 us
    ppermute x37, waiting for transfers between devices, swap(): lax.ppermute(value, 'tok', [(place, place ^ bits) for place in range(coun...  21.7 us
    pallas_call x2, Pallas kernels, increments(): pl.pallas_call(increments_kernel, grid_spec=pltpu.PrefetchScalarGridSpec(...  11.7 us
    pallas_call x4, Pallas kernels, apply_fast(): pl.pallas_call(functools.partial(apply_kernel, order, other), grid_spec=p...  10.4 us
    pallas_call x2, Pallas kernels, prepare(): pl.pallas_call(functools.partial(prepare_kernel, heads, block_root), grid...  3.78 us
    unnamed x12, local copies, waits for them, and re-layouts  3.46 us
    ppermute x4, starting transfers between devices, swap_parts(): return lax.ppermute(value, 'parts', [(0, 1), (1, 0)])  3.06 us
    ppermute x4, waiting for transfers between devices, swap_parts(): return lax.ppermute(value, 'parts', [(0, 1), (1, 0)])  3 us
  transfers between devices with their start and end apart: 41, of which 11 were waited for; matrix products, arithmetic and copies ran while one was open for 0% of the time, Pallas kernels for 23%

profile of v7, /device:TPU:1, one launch (start us, length us, event | category | flops | bytes accessed | tf_op | source)
XLA Modules:
  0.0 103.2 jit_solution(12064727562995394463)
XLA Ops:
  0.7 0.9 copy-done.3
  1.7 0.9 copy-done.4
  2.6 0.8 pack.1
  3.4 0.1 collective-permute-start
  3.5 1.4 %collective-permute-done.got = f32[2,96,256]{2,1,0:T(8,128)S(1)} collective-permute-done((f32[2,96,256]{2,1,0:T(8,128)S(1)}, f32[2,96,256]{2,1,0:T(8,128)S(1)}, u32[]{:S(2)}, u32[]{:S(2)}) %collective-permute-start) | collective-permute-done | bytes 196640 | tf_op jit(solution)/shard_map/ppermute | solution.py:140
  4.9 1.6 %copy-done.1 = bf16[1024,1024]{1,0:T(8,128)(2,1)S(1)} copy-done((bf16[1024,1024]{1,0:T(8,128)(2,1)S(1)}, bf16[1024,1024]{1,0:T(8,128)(2,1)}, u32[]{:S(2)}) %copy-start.1) | copy-done | bytes 2097176
  6.5 1.5 %keys.1 = (bf16[1024,512]{1,0:T(8,128)(2,1)S(1)}, bf16[1024,512]{1,0:T(8,128)(2,1)S(1)}) custom-call(s32[3]{0:T(128)S(1)} %pad_add_fusion.ids, bf16[1024,1024]{1,0:T(8,128)(2,1)S(1)} %copy-done.1), custom_call_target="tpu_custom_call" | custom-call | flops 5242880 | bytes 4194304 | tf_op jit(solution)/shard_map/keys/pallas_call | solution.py:255
  8.0 0.2 collective-permute-start.2
  8.2 2.3 %values.1 = (bf16[1024,512]{1,0:T(8,128)(2,1)S(1)}, bf16[1024,512]{1,0:T(8,128)(2,1)S(1)}) custom-call(s32[3]{0:T(128)S(1)} %pad_add_fusion.ids, bf16[1024,1024]{1,0:T(8,128)(2,1)S(1)} %copy-done.2, f32[4,1024]{1,0:T(4,128)S(1)} %copy-done.5), custom_call_target="tpu_custom_call" | custom-call | flops 5242880 | bytes 4194304 | tf_op jit(solution)/shard_map/values/pallas_call | solution.py:255
  10.5 0.4 collective-permute-start.3
  11.0 2.5 %collective-permute-start.1 = (bf16[2,96,256]{2,1,0:T(8,128)(2,1)S(1)}, bf16[2,96,256]{2,1,0:T(8,128)(2,1)S(1)}, u32[]{:S(2)}, u32[]{:S(2)}) collective-permute-start(bf16[2,96,256]{2,1,0:T(8,128)(2,1)S(1)} %get-tuple-element.49), channel_id=1, source_target_pairs={{0,4},{1,5},{2,6},{3,7},{4,0},{5,1},{6,2},{7,3},{8,12},{9,13},{10,... | collective-permute-start | bytes 294920 | tf_op jit(solution)/shard_map/ppermute | solution.py:140
  13.5 2.2 %collective-permute-start.6 = (bf16[2,96,256]{2,1,0:T(8,128)(2,1)S(1)}, bf16[2,96,256]{2,1,0:T(8,128)(2,1)S(1)}, u32[]{:S(2)}, u32[]{:S(2)}) collective-permute-start(bf16[2,96,256]{2,1,0:T(8,128)(2,1)S(1)} %get-tuple-element.49), channel_id=1, source_target_pairs={{0,12},{1,13},{2,14},{3,15},{4,8},{5,9},{6,10},{7,11},{8,4},{9,5},... | collective-permute-start | bytes 294920 | tf_op jit(solution)/shard_map/ppermute | solution.py:140
  15.6 0.1 collective-permute-start.5
  15.8 0.6 collective-permute-done.1
  16.4 1.2 %collective-permute-start.7 = (bf16[2,2,96,256]{3,2,1,0:T(8,128)(2,1)S(1)}, bf16[2,2,96,256]{3,2,1,0:T(8,128)(2,1)S(1)}, u32[]{:S(2)}, u32[]{:S(2)}) collective-permute-start(bf16[2,2,96,256]{3,2,1,0:T(8,128)(2,1)S(1)} %pad_maximum_fusion.near_low), channel_id=1, source_target_pairs={{0,2},{1,3},{2,0},{3,1},{4,6},{5,7},{6,4},{7,5},{8,10},{9,11},{10,... | collective-permute-start | bytes 589832 | tf_op jit(solution)/shard_map/ppermute | solution.py:140
  17.5 1.2 %collective-permute-start.4 = (bf16[2,2,96,256]{3,2,1,0:T(8,128)(2,1)S(1)}, bf16[2,2,96,256]{3,2,1,0:T(8,128)(2,1)S(1)}, u32[]{:S(2)}, u32[]{:S(2)}) collective-permute-start(bf16[2,2,96,256]{3,2,1,0:T(8,128)(2,1)S(1)} %pad_maximum_fusion.near_low), channel_id=1, source_target_pairs={{0,16},{16,0},{1,17},{17,1},{2,18},{18,2},{3,19},{19,3},{4,20},{20... | collective-permute-start | bytes 589832 | tf_op jit(solution)/shard_map/ppermute | solution.py:144
  18.7 1.6 %collective-permute-done.6 = bf16[2,96,256]{2,1,0:T(8,128)(2,1)S(1)} collective-permute-done((bf16[2,96,256]{2,1,0:T(8,128)(2,1)S(1)}, bf16[2,96,256]{2,1,0:T(8,128)(2,1)S(1)}, u32[]{:S(2)}, u32[]{:S(2)}) %collective-permute-start.6) | collective-permute-done | bytes 98336 | tf_op jit(solution)/shard_map/ppermute | solution.py:140
  20.3 4.8 %collective-permute-done.5 = bf16[2,96,256]{2,1,0:T(8,128)(2,1)S(1)} collective-permute-done((bf16[2,96,256]{2,1,0:T(8,128)(2,1)S(1)}, bf16[2,96,256]{2,1,0:T(8,128)(2,1)S(1)}, u32[]{:S(2)}, u32[]{:S(2)}) %collective-permute-start.5) | collective-permute-done | bytes 98336 | tf_op jit(solution)/shard_map/ppermute | solution.py:140
  25.1 1.3 %collective-permute-start.9 = (bf16[2,2,96,256]{3,2,1,0:T(8,128)(2,1)S(1)}, bf16[2,2,96,256]{3,2,1,0:T(8,128)(2,1)S(1)}, u32[]{:S(2)}, u32[]{:S(2)}) collective-permute-start(bf16[2,2,96,256]{3,2,1,0:T(8,128)(2,1)S(1)} %collective-permute-done.7.far_low), channel_id=1, source_target_pairs={{0,16},{16,0},{1,17},{17,1},{2,18},{18,2},{3,19},{19,3},{4,20},{20... | collective-permute-start | bytes 589832 | tf_op jit(solution)/shard_map/ppermute | solution.py:144
  26.4 1.2 %collective-permute-start.10 = (bf16[2,2,96,256]{3,2,1,0:T(8,128)(2,1)S(1)}, bf16[2,2,96,256]{3,2,1,0:T(8,128)(2,1)S(1)}, u32[]{:S(2)}, u32[]{:S(2)}) collective-permute-start(bf16[2,2,96,256]{3,2,1,0:T(8,128)(2,1)S(1)} %pad_maximum_fusion.1.near_high), channel_id=1, source_target_pairs={{0,2},{1,3},{2,0},{3,1},{4,6},{5,7},{6,4},{7,5},{8,10},{9,11},{10,... | collective-permute-start | bytes 589832 | tf_op jit(solution)/shard_map/ppermute | solution.py:140
  27.7 0.3 collective-permute-start.8
  27.9 3.0 %collective-permute-done.9.far_low = bf16[2,2,96,256]{3,2,1,0:T(8,128)(2,1)S(1)} collective-permute-done((bf16[2,2,96,256]{3,2,1,0:T(8,128)(2,1)S(1)}, bf16[2,2,96,256]{3,2,1,0:T(8,128)(2,1)S(1)}, u32[]{:S(2)}, u32[]{:S(2)}) %collective-permute-start.9) | collective-permute-done | bytes 196640 | tf_op jit(solution)/shard_map/ppermute | solution.py:144
  30.9 0.9 collective-permute-done.10.far_high
  31.8 0.3 collective-permute-start.11
  32.1 5.8 %increments.3 = (f32[4,2,96,256]{3,2,1,0:T(8,128)S(1)}, bf16[2,2,96,256]{3,2,1,0:T(8,128)(2,1)S(1)}, bf16[2,2,96,256]{3,2,1,0:T(8,128)(2,1)S(1)}) custom-call(s32[3]{0:T(128)S(1)} %pad_add_fusion.ids, bf16[2,2,96,256]{3,2,1,0:T(8,128)(2,1)S(1)} %pad_maximum_fusion.near_low, bf16[2,2,96,256]{3,2,1,0:T(8,128)(2,1)S(1)} %pad_maximum_fusion.1.near_high, ...), custom_call_target="tpu_custom_call" | custom-call | flops 3221225472 | bytes 2097152 | tf_op jit(solution)/shard_map/increments/pallas_call | solution.py:387
  37.9 1.3 %collective-permute-start.17 = (bf16[2,2,96,256]{3,2,1,0:T(8,128)(2,1)S(1)}, bf16[2,2,96,256]{3,2,1,0:T(8,128)(2,1)S(1)}, u32[]{:S(2)}, u32[]{:S(2)}) collective-permute-start(bf16[2,2,96,256]{3,2,1,0:T(8,128)(2,1)S(1)} %get-tuple-element.65), channel_id=1, source_target_pairs={{0,2},{1,3},{2,0},{3,1},{4,6},{5,7},{6,4},{7,5},{8,10},{9,11},{10,... | collective-permute-start | bytes 589832 | tf_op jit(solution)/shard_map/ppermute | solution.py:140
  39.2 0.2 collective-permute-start.19
  39.4 5.9 %increments.2 = (f32[4,2,96,256]{3,2,1,0:T(8,128)S(1)}, bf16[2,2,96,256]{3,2,1,0:T(8,128)(2,1)S(1)}, bf16[2,2,96,256]{3,2,1,0:T(8,128)(2,1)S(1)}) custom-call(s32[3]{0:T(128)S(1)} %pad_add_fusion.ids, bf16[2,2,96,256]{3,2,1,0:T(8,128)(2,1)S(1)} %collective-permute-done.4.near_low, bf16[2,2,96,256]{3,2,1,0:T(8,128)(2,1)S(1)} %collective-permute-done.8.near_high, ...), custom_call_target="tpu_custom_call" | custom-call | flops 3221225472 | bytes 2097152 | tf_op jit(solution)/shard_map/increments/pallas_call | solution.py:387
  45.4 1.3 %collective-permute-start.12 = (bf16[2,2,96,256]{3,2,1,0:T(8,128)(2,1)S(1)}, bf16[2,2,96,256]{3,2,1,0:T(8,128)(2,1)S(1)}, u32[]{:S(2)}, u32[]{:S(2)}) collective-permute-start(bf16[2,2,96,256]{3,2,1,0:T(8,128)(2,1)S(1)} %get-tuple-element.55), channel_id=1, source_target_pairs={{0,2},{1,3},{2,0},{3,1},{4,6},{5,7},{6,4},{7,5},{8,10},{9,11},{10,... | collective-permute-start | bytes 589832 | tf_op jit(solution)/shard_map/ppermute | solution.py:140
  46.8 1.5 %collective-permute-start.20 = (bf16[2,96,256]{2,1,0:T(8,128)(2,1)S(1)}, bf16[2,96,256]{2,1,0:T(8,128)(2,1)S(1)}, u32[]{:S(2)}, u32[]{:S(2)}) collective-permute-start(bf16[2,96,256]{2,1,0:T(8,128)(2,1)S(1)} %get-tuple-element.69), channel_id=1, source_target_pairs={{0,8},{1,9},{2,10},{3,11},{4,12},{5,13},{6,14},{7,15},{8,0},{9,1},... | collective-permute-start | bytes 294920 | tf_op jit(solution)/shard_map/ppermute | solution.py:140
  48.4 2.1 %collective-permute-start.21 = (bf16[2,96,256]{2,1,0:T(8,128)(2,1)S(1)}, bf16[2,96,256]{2,1,0:T(8,128)(2,1)S(1)}, u32[]{:S(2)}, u32[]{:S(2)}) collective-permute-start(bf16[2,96,256]{2,1,0:T(8,128)(2,1)S(1)} %get-tuple-element.70), channel_id=1, source_target_pairs={{0,12},{1,13},{2,14},{3,15},{4,8},{5,9},{6,10},{7,11},{8,4},{9,5},... | collective-permute-start | bytes 294920 | tf_op jit(solution)/shard_map/ppermute | solution.py:140
  50.4 0.2 collective-permute-start.14
  50.7 0.6 collective-permute-done.20.two
  51.3 2.4 %collective-permute-done.21.three = bf16[2,96,256]{2,1,0:T(8,128)(2,1)S(1)} collective-permute-done((bf16[2,96,256]{2,1,0:T(8,128)(2,1)S(1)}, bf16[2,96,256]{2,1,0:T(8,128)(2,1)S(1)}, u32[]{:S(2)}, u32[]{:S(2)}) %collective-permute-start.21) | collective-permute-done | bytes 98336 | tf_op jit(solution)/shard_map/ppermute | solution.py:140
  53.7 0.1 renorm.3
  53.9 1.4 %collective-permute-start.22 = (bf16[2,96,256]{2,1,0:T(8,128)(2,1)S(1)}, bf16[2,96,256]{2,1,0:T(8,128)(2,1)S(1)}, u32[]{:S(2)}, u32[]{:S(2)}) collective-permute-start(bf16[2,96,256]{2,1,0:T(8,128)(2,1)S(1)} %get-tuple-element.71), channel_id=1, source_target_pairs={{0,4},{1,5},{2,6},{3,7},{4,0},{5,1},{6,2},{7,3},{8,12},{9,13},{10,... | collective-permute-start | bytes 294920 | tf_op jit(solution)/shard_map/ppermute | solution.py:140
  55.2 1.4 %collective-permute-start.25 = (bf16[2,96,256]{2,1,0:T(8,128)(2,1)S(1)}, bf16[2,96,256]{2,1,0:T(8,128)(2,1)S(1)}, u32[]{:S(2)}, u32[]{:S(2)}) collective-permute-start(bf16[2,96,256]{2,1,0:T(8,128)(2,1)S(1)} %get-tuple-element.71), channel_id=1, source_target_pairs={{0,12},{1,13},{2,14},{3,15},{4,8},{5,9},{6,10},{7,11},{8,4},{9,5},... | collective-permute-start | bytes 294920 | tf_op jit(solution)/shard_map/ppermute | solution.py:140
  56.6 0.2 collective-permute-start.24
  56.9 2.0 %collective-permute-start.13 = (bf16[2,96,256]{2,1,0:T(8,128)(2,1)S(1)}, bf16[2,96,256]{2,1,0:T(8,128)(2,1)S(1)}, u32[]{:S(2)}, u32[]{:S(2)}) collective-permute-start(bf16[2,96,256]{2,1,0:T(8,128)(2,1)S(1)} %get-tuple-element.57), channel_id=1, source_target_pairs={{0,4},{1,5},{2,6},{3,7},{4,0},{5,1},{6,2},{7,3},{8,12},{9,13},{10,... | collective-permute-start | bytes 294920 | tf_op jit(solution)/shard_map/ppermute | solution.py:140
  59.0 0.8 collective-permute-start.15
  59.8 1.4 %collective-permute-start.16 = (bf16[2,96,256]{2,1,0:T(8,128)(2,1)S(1)}, bf16[2,96,256]{2,1,0:T(8,128)(2,1)S(1)}, u32[]{:S(2)}, u32[]{:S(2)}) collective-permute-start(bf16[2,96,256]{2,1,0:T(8,128)(2,1)S(1)} %get-tuple-element.60), channel_id=1, source_target_pairs={{0,12},{1,13},{2,14},{3,15},{4,8},{5,9},{6,10},{7,11},{8,4},{9,5},... | collective-permute-start | bytes 294920 | tf_op jit(solution)/shard_map/ppermute | solution.py:140
  61.2 0.9 collective-permute-done.13.one
  62.0 0.2 collective-permute-start.36
  62.3 7.2 %collective-permute-done.15.two = bf16[2,96,256]{2,1,0:T(8,128)(2,1)S(1)} collective-permute-done((bf16[2,96,256]{2,1,0:T(8,128)(2,1)S(1)}, bf16[2,96,256]{2,1,0:T(8,128)(2,1)S(1)}, u32[]{:S(2)}, u32[]{:S(2)}) %collective-permute-start.15) | collective-permute-done | bytes 98336 | tf_op jit(solution)/shard_map/ppermute | solution.py:140
  69.4 0.1 renorm.2
  69.6 3.5 %collective-permute-start.23 = (bf16[2,96,256]{2,1,0:T(8,128)(2,1)S(1)}, bf16[2,96,256]{2,1,0:T(8,128)(2,1)S(1)}, u32[]{:S(2)}, u32[]{:S(2)}) collective-permute-start(bf16[2,96,256]{2,1,0:T(8,128)(2,1)S(1)} %get-tuple-element.74), channel_id=1, source_target_pairs={{0,4},{1,5},{2,6},{3,7},{4,0},{5,1},{6,2},{7,3},{8,12},{9,13},{10,... | collective-permute-start | bytes 294920 | tf_op jit(solution)/shard_map/ppermute | solution.py:140
  73.1 4.6 %collective-permute-start.29 = (f32[2,96,256]{2,1,0:T(8,128)S(1)}, f32[2,96,256]{2,1,0:T(8,128)S(1)}, u32[]{:S(2)}, u32[]{:S(2)}) collective-permute-start(f32[2,96,256]{2,1,0:T(8,128)S(1)} %pad_maximum_fusion.6), channel_id=1, source_target_pairs={{0,1},{1,0},{2,3},{3,2},{4,5},{5,4},{6,7},{7,6},{8,9},{9,8},{10,11... | collective-permute-start | bytes 589832 | tf_op jit(solution)/shard_map/ppermute | solution.py:140
  77.7 0.5 collective-permute-start.38
  78.2 2.4 %collective-permute-start.28 = (bf16[2,96,256]{2,1,0:T(8,128)(2,1)S(1)}, bf16[2,96,256]{2,1,0:T(8,128)(2,1)S(1)}, u32[]{:S(2)}, u32[]{:S(2)}) collective-permute-start(bf16[2,96,256]{2,1,0:T(8,128)(2,1)S(1)} %get-tuple-element.74), channel_id=1, source_target_pairs={{0,12},{1,13},{2,14},{3,15},{4,8},{5,9},{6,10},{7,11},{8,4},{9,5},... | collective-permute-start | bytes 294920 | tf_op jit(solution)/shard_map/ppermute | solution.py:140
  80.7 3.1 %collective-permute-start.34 = (bf16[2,2,96,256]{3,2,1,0:T(8,128)(2,1)S(1)}, bf16[2,2,96,256]{3,2,1,0:T(8,128)(2,1)S(1)}, u32[]{:S(2)}, u32[]{:S(2)}) collective-permute-start(bf16[2,2,96,256]{3,2,1,0:T(8,128)(2,1)S(1)} %pad_maximum_fusion.2.near_low), channel_id=1, source_target_pairs={{0,1},{1,0},{2,3},{3,2},{4,5},{5,4},{6,7},{7,6},{8,9},{9,8},{10,11... | collective-permute-start | bytes 589832 | tf_op jit(solution)/shard_map/ppermute | solution.py:140
  83.8 1.3 %finish.1 = (f32[4,16,1024]{2,1,0:T(8,128)}, f32[4,32,256]{2,1,0:T(8,128)}) custom-call(s32[3]{0:T(128)S(1)} %pad_add_fusion.ids, f32[2,96,256]{2,1,0:T(8,128)S(1)} %get-tuple-element.75.one, f32[2,96,256]{2,1,0:T(8,128)S(1)} %get-tuple-element.76.two, f32[2,96,256]{2,1,0:T(8,128)S(1)} %collective-permute-done.29.came), custom_call_target="tpu_custom_call" | custom-call | tf_op jit(solution)/shard_map/finish/pallas_call | solution.py:539
  85.1 0.5 collective-permute-start.31
  85.6 1.8 %collective-permute-start.37 = (bf16[2,2,96,256]{3,2,1,0:T(8,128)(2,1)S(1)}, bf16[2,2,96,256]{3,2,1,0:T(8,128)(2,1)S(1)}, u32[]{:S(2)}, u32[]{:S(2)}) collective-permute-start(bf16[2,2,96,256]{3,2,1,0:T(8,128)(2,1)S(1)} %collective-permute-done.36.far_low), channel_id=1, source_target_pairs={{0,1},{1,0},{2,3},{3,2},{4,5},{5,4},{6,7},{7,6},{8,9},{9,8},{10,11... | collective-permute-start | bytes 589832 | tf_op jit(solution)/shard_map/ppermute | solution.py:140
  87.3 1.4 %collective-permute-done.27 = bf16[2,96,256]{2,1,0:T(8,128)(2,1)S(1)} collective-permute-done((bf16[2,96,256]{2,1,0:T(8,128)(2,1)S(1)}, bf16[2,96,256]{2,1,0:T(8,128)(2,1)S(1)}, u32[]{:S(2)}, u32[]{:S(2)}) %collective-permute-start.27) | collective-permute-done | bytes 98336 | tf_op jit(solution)/shard_map/ppermute | solution.py:140
  88.7 1.8 %collective-permute-start.39 = (bf16[2,2,96,256]{3,2,1,0:T(8,128)(2,1)S(1)}, bf16[2,2,96,256]{3,2,1,0:T(8,128)(2,1)S(1)}, u32[]{:S(2)}, u32[]{:S(2)}) collective-permute-start(bf16[2,2,96,256]{3,2,1,0:T(8,128)(2,1)S(1)} %collective-permute-done.38.far_high), channel_id=1, source_target_pairs={{0,1},{1,0},{2,3},{3,2},{4,5},{5,4},{6,7},{7,6},{8,9},{9,8},{10,11... | collective-permute-start | bytes 589832 | tf_op jit(solution)/shard_map/ppermute | solution.py:140
  90.6 1.1 %collective-permute-start.33 = (bf16[2,2,96,256]{3,2,1,0:T(8,128)(2,1)S(1)}, bf16[2,2,96,256]{3,2,1,0:T(8,128)(2,1)S(1)}, u32[]{:S(2)}, u32[]{:S(2)}) collective-permute-start(bf16[2,2,96,256]{3,2,1,0:T(8,128)(2,1)S(1)} %pad_maximum_fusion.5.near_high), channel_id=1, source_target_pairs={{0,2},{1,3},{2,0},{3,1},{4,6},{5,7},{6,4},{7,5},{8,10},{9,11},{10,... | collective-permute-start | bytes 589832 | tf_op jit(solution)/shard_map/ppermute | solution.py:140
  91.7 2.6 %apply.4.rest_0_ = bf16[1024,1024]{1,0:T(8,128)(2,1)} custom-call(s32[3]{0:T(128)S(1)} %pad_add_fusion.ids, bf16[2,2,96,256]{3,2,1,0:T(8,128)(2,1)S(1)} %pad_maximum_fusion.2.near_low, bf16[2,2,96,256]{3,2,1,0:T(8,128)(2,1)S(1)} %pad_maximum_fusion.4.near_high, bf16[2,2,96,256]{3,2,1,0:T(8,128)(2,1)S(1)} %collective-permute-done.36.far_low, ...), custom_call_target="tpu_custom_call" | custom-call | flops 805306368 | bytes 1048576 | tf_op jit(solution)/shard_map/apply/pallas_call | solution.py:507
  94.3 0.3 collective-permute-start.26
  94.6 0.2 collective-permute-start.30
  94.8 0.3 collective-permute-start.32
  95.1 2.6 %apply.5.rest_0_ = bf16[1024,1024]{1,0:T(8,128)(2,1)} custom-call(s32[3]{0:T(128)S(1)} %pad_add_fusion.ids, bf16[2,2,96,256]{3,2,1,0:T(8,128)(2,1)S(1)} %collective-permute-done.34.near_low, bf16[2,2,96,256]{3,2,1,0:T(8,128)(2,1)S(1)} %collective-permute-done.35.near_high, ...), custom_call_target="tpu_custom_call", output_to_operand_aliasing={{}: (6, {})} | custom-call | flops 805306368 | bytes 1048576 | tf_op jit(solution)/shard_map/apply/pallas_call | solution.py:507
  97.7 0.3 collective-permute-start.40
  98.0 2.6 %apply.6.rest_0_ = bf16[1024,1024]{1,0:T(8,128)(2,1)} custom-call(s32[3]{0:T(128)S(1)} %pad_add_fusion.ids, bf16[2,2,96,256]{3,2,1,0:T(8,128)(2,1)S(1)} %pad_maximum_fusion.3.near_low, bf16[2,2,96,256]{3,2,1,0:T(8,128)(2,1)S(1)} %pad_maximum_fusion.5.near_high, ...), custom_call_target="tpu_custom_call", output_to_operand_aliasing={{}: (6, {})} | custom-call | flops 805306368 | bytes 1048576 | tf_op jit(solution)/shard_map/apply/pallas_call | solution.py:507
  100.6 2.6 %apply.7 = bf16[1024,1024]{1,0:T(8,128)(2,1)} custom-call(s32[3]{0:T(128)S(1)} %pad_add_fusion.ids, bf16[2,2,96,256]{3,2,1,0:T(8,128)(2,1)S(1)} %collective-permute-done.26.near_low, bf16[2,2,96,256]{3,2,1,0:T(8,128)(2,1)S(1)} %collective-permute-done.30.near_high, ...), custom_call_target="tpu_custom_call", output_to_operand_aliasing={{}: (6, {})} | custom-call | flops 805306368 | bytes 1048576 | tf_op jit(solution)/shard_map/apply/pallas_call | solution.py:507
  (57 shorter events, 0.6 us)
Async XLA Ops:
  0.6 7.6 %copy-start.5 = (f32[4,1024]{1,0:T(4,128)S(1)}, f32[4,1024]{1,0:T(4,128)}, u32[]{:S(2)}) copy-start(f32[4,1024]{1,0:T(4,128)} %rest_0_.1) | copy-start | bytes 49156
  0.7 1.0 copy-start.3
  1.7 0.9 copy-start.4
  3.4 1.5 %collective-permute-start = (f32[2,96,256]{2,1,0:T(8,128)S(1)}, f32[2,96,256]{2,1,0:T(8,128)S(1)}, u32[]{:S(2)}, u32[]{:S(2)}) collective-permute-start(f32[2,96,256]{2,1,0:T(8,128)S(1)} %get-tuple-element.43), channel_id=1, source_target_pairs={{0,1},{1,0},{2,3},{3,2},{4,5},{5,4},{6,7},{7,6},{8,9},{9,8},{10,11... | collective-permute-start | bytes 589832 | tf_op jit(solution)/shard_map/ppermute | solution.py:140
  4.9 1.6 %copy-start.1 = (bf16[1024,1024]{1,0:T(8,128)(2,1)S(1)}, bf16[1024,1024]{1,0:T(8,128)(2,1)}, u32[]{:S(2)}) copy-start(bf16[1024,1024]{1,0:T(8,128)(2,1)} %x_ref.2) | copy-start | bytes 6291460
  6.5 1.7 %copy-start.2 = (bf16[1024,1024]{1,0:T(8,128)(2,1)S(1)}, bf16[1024,1024]{1,0:T(8,128)(2,1)}, u32[]{:S(2)}) copy-start(bf16[1024,1024]{1,0:T(8,128)(2,1)} %x_ref.3) | copy-start | bytes 6291460
  8.0 8.4 %collective-permute-start.2 = (bf16[1024,512]{1,0:T(8,128)(2,1)S(1)}, bf16[1024,512]{1,0:T(8,128)(2,1)S(1)}, u32[]{:S(2)}, u32[]{:S(2)}) collective-permute-start(bf16[1024,512]{1,0:T(8,128)(2,1)S(1)} %get-tuple-element.45), channel_id=1, source_target_pairs={{0,1},{1,0},{2,3},{3,2},{4,5},{5,4},{6,7},{7,6},{8,9},{9,8},{10,11... | collective-permute-start | bytes 3145736 | tf_op jit(solution)/shard_map/ppermute | solution.py:140
  10.5 5.9 %collective-permute-start.3 = (bf16[1024,512]{1,0:T(8,128)(2,1)S(1)}, bf16[1024,512]{1,0:T(8,128)(2,1)S(1)}, u32[]{:S(2)}, u32[]{:S(2)}) collective-permute-start(bf16[1024,512]{1,0:T(8,128)(2,1)S(1)} %get-tuple-element.46), channel_id=1, source_target_pairs={{0,1},{1,0},{2,3},{3,2},{4,5},{5,4},{6,7},{7,6},{8,9},{9,8},{10,11... | collective-permute-start | bytes 3145736 | tf_op jit(solution)/shard_map/ppermute | solution.py:140
  11.0 5.4 %collective-permute-start.1 = (bf16[2,96,256]{2,1,0:T(8,128)(2,1)S(1)}, bf16[2,96,256]{2,1,0:T(8,128)(2,1)S(1)}, u32[]{:S(2)}, u32[]{:S(2)}) collective-permute-start(bf16[2,96,256]{2,1,0:T(8,128)(2,1)S(1)} %get-tuple-element.49), channel_id=1, source_target_pairs={{0,4},{1,5},{2,6},{3,7},{4,0},{5,1},{6,2},{7,3},{8,12},{9,13},{10,... | collective-permute-start | bytes 294920 | tf_op jit(solution)/shard_map/ppermute | solution.py:140
  13.5 6.8 %collective-permute-start.6 = (bf16[2,96,256]{2,1,0:T(8,128)(2,1)S(1)}, bf16[2,96,256]{2,1,0:T(8,128)(2,1)S(1)}, u32[]{:S(2)}, u32[]{:S(2)}) collective-permute-start(bf16[2,96,256]{2,1,0:T(8,128)(2,1)S(1)} %get-tuple-element.49), channel_id=1, source_target_pairs={{0,12},{1,13},{2,14},{3,15},{4,8},{5,9},{6,10},{7,11},{8,4},{9,5},... | collective-permute-start | bytes 294920 | tf_op jit(solution)/shard_map/ppermute | solution.py:140
  15.6 9.4 %collective-permute-start.5 = (bf16[2,96,256]{2,1,0:T(8,128)(2,1)S(1)}, bf16[2,96,256]{2,1,0:T(8,128)(2,1)S(1)}, u32[]{:S(2)}, u32[]{:S(2)}) collective-permute-start(bf16[2,96,256]{2,1,0:T(8,128)(2,1)S(1)} %get-tuple-element.49), channel_id=1, source_target_pairs={{0,8},{1,9},{2,10},{3,11},{4,12},{5,13},{6,14},{7,15},{8,0},{9,1},... | collective-permute-start | bytes 294920 | tf_op jit(solution)/shard_map/ppermute | solution.py:140
  16.4 8.8 %collective-permute-start.7 = (bf16[2,2,96,256]{3,2,1,0:T(8,128)(2,1)S(1)}, bf16[2,2,96,256]{3,2,1,0:T(8,128)(2,1)S(1)}, u32[]{:S(2)}, u32[]{:S(2)}) collective-permute-start(bf16[2,2,96,256]{3,2,1,0:T(8,128)(2,1)S(1)} %pad_maximum_fusion.near_low), channel_id=1, source_target_pairs={{0,2},{1,3},{2,0},{3,1},{4,6},{5,7},{6,4},{7,5},{8,10},{9,11},{10,... | collective-permute-start | bytes 589832 | tf_op jit(solution)/shard_map/ppermute | solution.py:140
  17.5 8.9 %collective-permute-start.4 = (bf16[2,2,96,256]{3,2,1,0:T(8,128)(2,1)S(1)}, bf16[2,2,96,256]{3,2,1,0:T(8,128)(2,1)S(1)}, u32[]{:S(2)}, u32[]{:S(2)}) collective-permute-start(bf16[2,2,96,256]{3,2,1,0:T(8,128)(2,1)S(1)} %pad_maximum_fusion.near_low), channel_id=1, source_target_pairs={{0,16},{16,0},{1,17},{17,1},{2,18},{18,2},{3,19},{19,3},{4,20},{20... | collective-permute-start | bytes 589832 | tf_op jit(solution)/shard_map/ppermute | solution.py:144
  25.1 5.8 %collective-permute-start.9 = (bf16[2,2,96,256]{3,2,1,0:T(8,128)(2,1)S(1)}, bf16[2,2,96,256]{3,2,1,0:T(8,128)(2,1)S(1)}, u32[]{:S(2)}, u32[]{:S(2)}) collective-permute-start(bf16[2,2,96,256]{3,2,1,0:T(8,128)(2,1)S(1)} %collective-permute-done.7.far_low), channel_id=1, source_target_pairs={{0,16},{16,0},{1,17},{17,1},{2,18},{18,2},{3,19},{19,3},{4,20},{20... | collective-permute-start | bytes 589832 | tf_op jit(solution)/shard_map/ppermute | solution.py:144
  26.4 5.4 %collective-permute-start.10 = (bf16[2,2,96,256]{3,2,1,0:T(8,128)(2,1)S(1)}, bf16[2,2,96,256]{3,2,1,0:T(8,128)(2,1)S(1)}, u32[]{:S(2)}, u32[]{:S(2)}) collective-permute-start(bf16[2,2,96,256]{3,2,1,0:T(8,128)(2,1)S(1)} %pad_maximum_fusion.1.near_high), channel_id=1, source_target_pairs={{0,2},{1,3},{2,0},{3,1},{4,6},{5,7},{6,4},{7,5},{8,10},{9,11},{10,... | collective-permute-start | bytes 589832 | tf_op jit(solution)/shard_map/ppermute | solution.py:140
  27.7 11.8 %collective-permute-start.8 = (bf16[2,2,96,256]{3,2,1,0:T(8,128)(2,1)S(1)}, bf16[2,2,96,256]{3,2,1,0:T(8,128)(2,1)S(1)}, u32[]{:S(2)}, u32[]{:S(2)}) collective-permute-start(bf16[2,2,96,256]{3,2,1,0:T(8,128)(2,1)S(1)} %pad_maximum_fusion.1.near_high), channel_id=1, source_target_pairs={{0,16},{16,0},{1,17},{17,1},{2,18},{18,2},{3,19},{19,3},{4,20},{20... | collective-permute-start | bytes 589832 | tf_op jit(solution)/shard_map/ppermute | solution.py:144
  31.8 7.6 %collective-permute-start.11 = (bf16[2,2,96,256]{3,2,1,0:T(8,128)(2,1)S(1)}, bf16[2,2,96,256]{3,2,1,0:T(8,128)(2,1)S(1)}, u32[]{:S(2)}, u32[]{:S(2)}) collective-permute-start(bf16[2,2,96,256]{3,2,1,0:T(8,128)(2,1)S(1)} %collective-permute-done.10.far_high), channel_id=1, source_target_pairs={{0,16},{16,0},{1,17},{17,1},{2,18},{18,2},{3,19},{19,3},{4,20},{20... | collective-permute-start | bytes 589832 | tf_op jit(solution)/shard_map/ppermute | solution.py:144
  37.9 8.8 %collective-permute-start.17 = (bf16[2,2,96,256]{3,2,1,0:T(8,128)(2,1)S(1)}, bf16[2,2,96,256]{3,2,1,0:T(8,128)(2,1)S(1)}, u32[]{:S(2)}, u32[]{:S(2)}) collective-permute-start(bf16[2,2,96,256]{3,2,1,0:T(8,128)(2,1)S(1)} %get-tuple-element.65), channel_id=1, source_target_pairs={{0,2},{1,3},{2,0},{3,1},{4,6},{5,7},{6,4},{7,5},{8,10},{9,11},{10,... | collective-permute-start | bytes 589832 | tf_op jit(solution)/shard_map/ppermute | solution.py:140
  39.2 7.6 %collective-permute-start.19 = (bf16[2,2,96,256]{3,2,1,0:T(8,128)(2,1)S(1)}, bf16[2,2,96,256]{3,2,1,0:T(8,128)(2,1)S(1)}, u32[]{:S(2)}, u32[]{:S(2)}) collective-permute-start(bf16[2,2,96,256]{3,2,1,0:T(8,128)(2,1)S(1)} %get-tuple-element.68), channel_id=1, source_target_pairs={{0,2},{1,3},{2,0},{3,1},{4,6},{5,7},{6,4},{7,5},{8,10},{9,11},{10,... | collective-permute-start | bytes 589832 | tf_op jit(solution)/shard_map/ppermute | solution.py:140
  45.4 11.5 %collective-permute-start.12 = (bf16[2,2,96,256]{3,2,1,0:T(8,128)(2,1)S(1)}, bf16[2,2,96,256]{3,2,1,0:T(8,128)(2,1)S(1)}, u32[]{:S(2)}, u32[]{:S(2)}) collective-permute-start(bf16[2,2,96,256]{3,2,1,0:T(8,128)(2,1)S(1)} %get-tuple-element.55), channel_id=1, source_target_pairs={{0,2},{1,3},{2,0},{3,1},{4,6},{5,7},{6,4},{7,5},{8,10},{9,11},{10,... | collective-permute-start | bytes 589832 | tf_op jit(solution)/shard_map/ppermute | solution.py:140
  46.7 4.0 %collective-permute-start.18 = (bf16[2,96,256]{2,1,0:T(8,128)(2,1)S(1)}, bf16[2,96,256]{2,1,0:T(8,128)(2,1)S(1)}, u32[]{:S(2)}, u32[]{:S(2)}) collective-permute-start(bf16[2,96,256]{2,1,0:T(8,128)(2,1)S(1)} %get-tuple-element.67), channel_id=1, source_target_pairs={{0,4},{1,5},{2,6},{3,7},{4,0},{5,1},{6,2},{7,3},{8,12},{9,13},{10,... | collective-permute-start | bytes 294920 | tf_op jit(solution)/shard_map/ppermute | solution.py:140
  46.8 4.5 %collective-permute-start.20 = (bf16[2,96,256]{2,1,0:T(8,128)(2,1)S(1)}, bf16[2,96,256]{2,1,0:T(8,128)(2,1)S(1)}, u32[]{:S(2)}, u32[]{:S(2)}) collective-permute-start(bf16[2,96,256]{2,1,0:T(8,128)(2,1)S(1)} %get-tuple-element.69), channel_id=1, source_target_pairs={{0,8},{1,9},{2,10},{3,11},{4,12},{5,13},{6,14},{7,15},{8,0},{9,1},... | collective-permute-start | bytes 294920 | tf_op jit(solution)/shard_map/ppermute | solution.py:140
  48.4 5.3 %collective-permute-start.21 = (bf16[2,96,256]{2,1,0:T(8,128)(2,1)S(1)}, bf16[2,96,256]{2,1,0:T(8,128)(2,1)S(1)}, u32[]{:S(2)}, u32[]{:S(2)}) collective-permute-start(bf16[2,96,256]{2,1,0:T(8,128)(2,1)S(1)} %get-tuple-element.70), channel_id=1, source_target_pairs={{0,12},{1,13},{2,14},{3,15},{4,8},{5,9},{6,10},{7,11},{8,4},{9,5},... | collective-permute-start | bytes 294920 | tf_op jit(solution)/shard_map/ppermute | solution.py:140
  50.4 8.5 %collective-permute-start.14 = (bf16[2,2,96,256]{3,2,1,0:T(8,128)(2,1)S(1)}, bf16[2,2,96,256]{3,2,1,0:T(8,128)(2,1)S(1)}, u32[]{:S(2)}, u32[]{:S(2)}) collective-permute-start(bf16[2,2,96,256]{3,2,1,0:T(8,128)(2,1)S(1)} %get-tuple-element.58), channel_id=1, source_target_pairs={{0,2},{1,3},{2,0},{3,1},{4,6},{5,7},{6,4},{7,5},{8,10},{9,11},{10,... | collective-permute-start | bytes 589832 | tf_op jit(solution)/shard_map/ppermute | solution.py:140
  53.9 5.9 %collective-permute-start.22 = (bf16[2,96,256]{2,1,0:T(8,128)(2,1)S(1)}, bf16[2,96,256]{2,1,0:T(8,128)(2,1)S(1)}, u32[]{:S(2)}, u32[]{:S(2)}) collective-permute-start(bf16[2,96,256]{2,1,0:T(8,128)(2,1)S(1)} %get-tuple-element.71), channel_id=1, source_target_pairs={{0,4},{1,5},{2,6},{3,7},{4,0},{5,1},{6,2},{7,3},{8,12},{9,13},{10,... | collective-permute-start | bytes 294920 | tf_op jit(solution)/shard_map/ppermute | solution.py:140
  55.2 22.5 %collective-permute-start.25 = (bf16[2,96,256]{2,1,0:T(8,128)(2,1)S(1)}, bf16[2,96,256]{2,1,0:T(8,128)(2,1)S(1)}, u32[]{:S(2)}, u32[]{:S(2)}) collective-permute-start(bf16[2,96,256]{2,1,0:T(8,128)(2,1)S(1)} %get-tuple-element.71), channel_id=1, source_target_pairs={{0,12},{1,13},{2,14},{3,15},{4,8},{5,9},{6,10},{7,11},{8,4},{9,5},... | collective-permute-start | bytes 294920 | tf_op jit(solution)/shard_map/ppermute | solution.py:140
  56.6 21.1 %collective-permute-start.24 = (bf16[2,96,256]{2,1,0:T(8,128)(2,1)S(1)}, bf16[2,96,256]{2,1,0:T(8,128)(2,1)S(1)}, u32[]{:S(2)}, u32[]{:S(2)}) collective-permute-start(bf16[2,96,256]{2,1,0:T(8,128)(2,1)S(1)} %get-tuple-element.71), channel_id=1, source_target_pairs={{0,8},{1,9},{2,10},{3,11},{4,12},{5,13},{6,14},{7,15},{8,0},{9,1},... | collective-permute-start | bytes 294920 | tf_op jit(solution)/shard_map/ppermute | solution.py:140
  56.9 34.8 %copy-start = (bf16[1024,1024]{1,0:T(8,128)(2,1)S(1)}, bf16[1024,1024]{1,0:T(8,128)(2,1)}, u32[]{:S(2)}) copy-start(bf16[1024,1024]{1,0:T(8,128)(2,1)} %q_ref.7) | copy-start | bytes 6291460
  56.9 5.1 %collective-permute-start.13 = (bf16[2,96,256]{2,1,0:T(8,128)(2,1)S(1)}, bf16[2,96,256]{2,1,0:T(8,128)(2,1)S(1)}, u32[]{:S(2)}, u32[]{:S(2)}) collective-permute-start(bf16[2,96,256]{2,1,0:T(8,128)(2,1)S(1)} %get-tuple-element.57), channel_id=1, source_target_pairs={{0,4},{1,5},{2,6},{3,7},{4,0},{5,1},{6,2},{7,3},{8,12},{9,13},{10,... | collective-permute-start | bytes 294920 | tf_op jit(solution)/shard_map/ppermute | solution.py:140
  59.0 10.4 %collective-permute-start.15 = (bf16[2,96,256]{2,1,0:T(8,128)(2,1)S(1)}, bf16[2,96,256]{2,1,0:T(8,128)(2,1)S(1)}, u32[]{:S(2)}, u32[]{:S(2)}) collective-permute-start(bf16[2,96,256]{2,1,0:T(8,128)(2,1)S(1)} %get-tuple-element.59), channel_id=1, source_target_pairs={{0,8},{1,9},{2,10},{3,11},{4,12},{5,13},{6,14},{7,15},{8,0},{9,1},... | collective-permute-start | bytes 294920 | tf_op jit(solution)/shard_map/ppermute | solution.py:140
  59.8 9.7 %collective-permute-start.16 = (bf16[2,96,256]{2,1,0:T(8,128)(2,1)S(1)}, bf16[2,96,256]{2,1,0:T(8,128)(2,1)S(1)}, u32[]{:S(2)}, u32[]{:S(2)}) collective-permute-start(bf16[2,96,256]{2,1,0:T(8,128)(2,1)S(1)} %get-tuple-element.60), channel_id=1, source_target_pairs={{0,12},{1,13},{2,14},{3,15},{4,8},{5,9},{6,10},{7,11},{8,4},{9,5},... | collective-permute-start | bytes 294920 | tf_op jit(solution)/shard_map/ppermute | solution.py:140
  62.0 23.1 %collective-permute-start.36 = (bf16[2,2,96,256]{3,2,1,0:T(8,128)(2,1)S(1)}, bf16[2,2,96,256]{3,2,1,0:T(8,128)(2,1)S(1)}, u32[]{:S(2)}, u32[]{:S(2)}) collective-permute-start(bf16[2,2,96,256]{3,2,1,0:T(8,128)(2,1)S(1)} %pad_maximum_fusion.2.near_low), channel_id=1, source_target_pairs={{0,2},{1,3},{2,0},{3,1},{4,6},{5,7},{6,4},{7,5},{8,10},{9,11},{10,... | collective-permute-start | bytes 589832 | tf_op jit(solution)/shard_map/ppermute | solution.py:140
  69.6 8.6 %collective-permute-start.23 = (bf16[2,96,256]{2,1,0:T(8,128)(2,1)S(1)}, bf16[2,96,256]{2,1,0:T(8,128)(2,1)S(1)}, u32[]{:S(2)}, u32[]{:S(2)}) collective-permute-start(bf16[2,96,256]{2,1,0:T(8,128)(2,1)S(1)} %get-tuple-element.74), channel_id=1, source_target_pairs={{0,4},{1,5},{2,6},{3,7},{4,0},{5,1},{6,2},{7,3},{8,12},{9,13},{10,... | collective-permute-start | bytes 294920 | tf_op jit(solution)/shard_map/ppermute | solution.py:140
  73.1 7.6 %collective-permute-start.29 = (f32[2,96,256]{2,1,0:T(8,128)S(1)}, f32[2,96,256]{2,1,0:T(8,128)S(1)}, u32[]{:S(2)}, u32[]{:S(2)}) collective-permute-start(f32[2,96,256]{2,1,0:T(8,128)S(1)} %pad_maximum_fusion.6), channel_id=1, source_target_pairs={{0,1},{1,0},{2,3},{3,2},{4,5},{5,4},{6,7},{7,6},{8,9},{9,8},{10,11... | collective-permute-start | bytes 589832 | tf_op jit(solution)/shard_map/ppermute | solution.py:140
  77.7 7.4 %collective-permute-start.38 = (bf16[2,2,96,256]{3,2,1,0:T(8,128)(2,1)S(1)}, bf16[2,2,96,256]{3,2,1,0:T(8,128)(2,1)S(1)}, u32[]{:S(2)}, u32[]{:S(2)}) collective-permute-start(bf16[2,2,96,256]{3,2,1,0:T(8,128)(2,1)S(1)} %pad_maximum_fusion.4.near_high), channel_id=1, source_target_pairs={{0,2},{1,3},{2,0},{3,1},{4,6},{5,7},{6,4},{7,5},{8,10},{9,11},{10,... | collective-permute-start | bytes 589832 | tf_op jit(solution)/shard_map/ppermute | solution.py:140
  78.2 7.3 %collective-permute-start.28 = (bf16[2,96,256]{2,1,0:T(8,128)(2,1)S(1)}, bf16[2,96,256]{2,1,0:T(8,128)(2,1)S(1)}, u32[]{:S(2)}, u32[]{:S(2)}) collective-permute-start(bf16[2,96,256]{2,1,0:T(8,128)(2,1)S(1)} %get-tuple-element.74), channel_id=1, source_target_pairs={{0,12},{1,13},{2,14},{3,15},{4,8},{5,9},{6,10},{7,11},{8,4},{9,5},... | collective-permute-start | bytes 294920 | tf_op jit(solution)/shard_map/ppermute | solution.py:140
  80.6 8.1 %collective-permute-start.27 = (bf16[2,96,256]{2,1,0:T(8,128)(2,1)S(1)}, bf16[2,96,256]{2,1,0:T(8,128)(2,1)S(1)}, u32[]{:S(2)}, u32[]{:S(2)}) collective-permute-start(bf16[2,96,256]{2,1,0:T(8,128)(2,1)S(1)} %get-tuple-element.74), channel_id=1, source_target_pairs={{0,8},{1,9},{2,10},{3,11},{4,12},{5,13},{6,14},{7,15},{8,0},{9,1},... | collective-permute-start | bytes 294920 | tf_op jit(solution)/shard_map/ppermute | solution.py:140
  80.7 9.9 %collective-permute-start.34 = (bf16[2,2,96,256]{3,2,1,0:T(8,128)(2,1)S(1)}, bf16[2,2,96,256]{3,2,1,0:T(8,128)(2,1)S(1)}, u32[]{:S(2)}, u32[]{:S(2)}) collective-permute-start(bf16[2,2,96,256]{3,2,1,0:T(8,128)(2,1)S(1)} %pad_maximum_fusion.2.near_low), channel_id=1, source_target_pairs={{0,1},{1,0},{2,3},{3,2},{4,5},{5,4},{6,7},{7,6},{8,9},{9,8},{10,11... | collective-permute-start | bytes 589832 | tf_op jit(solution)/shard_map/ppermute | solution.py:140
  85.1 9.2 %collective-permute-start.35 = (bf16[2,2,96,256]{3,2,1,0:T(8,128)(2,1)S(1)}, bf16[2,2,96,256]{3,2,1,0:T(8,128)(2,1)S(1)}, u32[]{:S(2)}, u32[]{:S(2)}) collective-permute-start(bf16[2,2,96,256]{3,2,1,0:T(8,128)(2,1)S(1)} %pad_maximum_fusion.4.near_high), channel_id=1, source_target_pairs={{0,1},{1,0},{2,3},{3,2},{4,5},{5,4},{6,7},{7,6},{8,9},{9,8},{10,11... | collective-permute-start | bytes 589832 | tf_op jit(solution)/shard_map/ppermute | solution.py:140
  85.1 9.5 %collective-permute-start.31 = (bf16[2,2,96,256]{3,2,1,0:T(8,128)(2,1)S(1)}, bf16[2,2,96,256]{3,2,1,0:T(8,128)(2,1)S(1)}, u32[]{:S(2)}, u32[]{:S(2)}) collective-permute-start(bf16[2,2,96,256]{3,2,1,0:T(8,128)(2,1)S(1)} %pad_maximum_fusion.3.near_low), channel_id=1, source_target_pairs={{0,2},{1,3},{2,0},{3,1},{4,6},{5,7},{6,4},{7,5},{8,10},{9,11},{10,... | collective-permute-start | bytes 589832 | tf_op jit(solution)/shard_map/ppermute | solution.py:140
  85.6 9.3 %collective-permute-start.37 = (bf16[2,2,96,256]{3,2,1,0:T(8,128)(2,1)S(1)}, bf16[2,2,96,256]{3,2,1,0:T(8,128)(2,1)S(1)}, u32[]{:S(2)}, u32[]{:S(2)}) collective-permute-start(bf16[2,2,96,256]{3,2,1,0:T(8,128)(2,1)S(1)} %collective-permute-done.36.far_low), channel_id=1, source_target_pairs={{0,1},{1,0},{2,3},{3,2},{4,5},{5,4},{6,7},{7,6},{8,9},{9,8},{10,11... | collective-permute-start | bytes 589832 | tf_op jit(solution)/shard_map/ppermute | solution.py:140
  88.7 6.4 %collective-permute-start.39 = (bf16[2,2,96,256]{3,2,1,0:T(8,128)(2,1)S(1)}, bf16[2,2,96,256]{3,2,1,0:T(8,128)(2,1)S(1)}, u32[]{:S(2)}, u32[]{:S(2)}) collective-permute-start(bf16[2,2,96,256]{3,2,1,0:T(8,128)(2,1)S(1)} %collective-permute-done.38.far_high), channel_id=1, source_target_pairs={{0,1},{1,0},{2,3},{3,2},{4,5},{5,4},{6,7},{7,6},{8,9},{9,8},{10,11... | collective-permute-start | bytes 589832 | tf_op jit(solution)/shard_map/ppermute | solution.py:140
  90.6 7.1 %collective-permute-start.33 = (bf16[2,2,96,256]{3,2,1,0:T(8,128)(2,1)S(1)}, bf16[2,2,96,256]{3,2,1,0:T(8,128)(2,1)S(1)}, u32[]{:S(2)}, u32[]{:S(2)}) collective-permute-start(bf16[2,2,96,256]{3,2,1,0:T(8,128)(2,1)S(1)} %pad_maximum_fusion.5.near_high), channel_id=1, source_target_pairs={{0,2},{1,3},{2,0},{3,1},{4,6},{5,7},{6,4},{7,5},{8,10},{9,11},{10,... | collective-permute-start | bytes 589832 | tf_op jit(solution)/shard_map/ppermute | solution.py:140
  94.3 6.2 %collective-permute-start.26 = (bf16[2,2,96,256]{3,2,1,0:T(8,128)(2,1)S(1)}, bf16[2,2,96,256]{3,2,1,0:T(8,128)(2,1)S(1)}, u32[]{:S(2)}, u32[]{:S(2)}) collective-permute-start(bf16[2,2,96,256]{3,2,1,0:T(8,128)(2,1)S(1)} %pad_maximum_fusion.3.near_low), channel_id=1, source_target_pairs={{0,1},{1,0},{2,3},{3,2},{4,5},{5,4},{6,7},{7,6},{8,9},{9,8},{10,11... | collective-permute-start | bytes 589832 | tf_op jit(solution)/shard_map/ppermute | solution.py:140
  94.6 6.0 %collective-permute-start.30 = (bf16[2,2,96,256]{3,2,1,0:T(8,128)(2,1)S(1)}, bf16[2,2,96,256]{3,2,1,0:T(8,128)(2,1)S(1)}, u32[]{:S(2)}, u32[]{:S(2)}) collective-permute-start(bf16[2,2,96,256]{3,2,1,0:T(8,128)(2,1)S(1)} %pad_maximum_fusion.5.near_high), channel_id=1, source_target_pairs={{0,1},{1,0},{2,3},{3,2},{4,5},{5,4},{6,7},{7,6},{8,9},{9,8},{10,11... | collective-permute-start | bytes 589832 | tf_op jit(solution)/shard_map/ppermute | solution.py:140
  94.8 5.7 %collective-permute-start.32 = (bf16[2,2,96,256]{3,2,1,0:T(8,128)(2,1)S(1)}, bf16[2,2,96,256]{3,2,1,0:T(8,128)(2,1)S(1)}, u32[]{:S(2)}, u32[]{:S(2)}) collective-permute-start(bf16[2,2,96,256]{3,2,1,0:T(8,128)(2,1)S(1)} %collective-permute-done.31.far_low), channel_id=1, source_target_pairs={{0,1},{1,0},{2,3},{3,2},{4,5},{5,4},{6,7},{7,6},{8,9},{9,8},{10,11... | collective-permute-start | bytes 589832 | tf_op jit(solution)/shard_map/ppermute | solution.py:140
  97.7 2.9 %collective-permute-start.40 = (bf16[2,2,96,256]{3,2,1,0:T(8,128)(2,1)S(1)}, bf16[2,2,96,256]{3,2,1,0:T(8,128)(2,1)S(1)}, u32[]{:S(2)}, u32[]{:S(2)}) collective-permute-start(bf16[2,2,96,256]{3,2,1,0:T(8,128)(2,1)S(1)} %collective-permute-done.33.far_high), channel_id=1, source_target_pairs={{0,1},{1,0},{2,3},{3,2},{4,5},{5,4},{6,7},{7,6},{8,9},{9,8},{10,11... | collective-permute-start | bytes 589832 | tf_op jit(solution)/shard_map/ppermute | solution.py:140

commit v8 on v7

--- a/solution.py
+++ b/solution.py
@@ -474,7 +474,7 @@
 
 
 def apply_kernel(order, other, ids, near_low, near_high, far_low, far_high, q_ref, *rest):
-    o_ref, w_in, w_out = rest[-3:]
+    o_hbm, w_in, w_out, o_ref, sent = rest[-5:]
     chip, core = ids[0], ids[1]
     fast, size = w_out.shape
     lines = (near_low, near_high, far_low, far_high)
@@ -483,14 +483,22 @@
     in_root = 1.0 / math.sqrt(size)
     out_root = 1.0 / math.sqrt(fast)
     step = 512
+    copies = []
     for start in range(0, q_ref.shape[0], step):
-        rows = slice(start, start + step)
+        rows = pl.ds(start, step)
         query = normalize_head(q_ref[rows, columns])
         gate = jnp.dot(query, w_in[:, :fast], preferred_element_type=F32) * in_root
         upper = jnp.dot(query, w_in[:, fast:], preferred_element_type=F32) * in_root
         hidden = (gate * (0.5 * jnp.tanh(0.5 * gate) + 0.5) * upper).astype(BF16)
         result = jnp.dot(hidden, w_out[...], preferred_element_type=F32) * out_root
         o_ref[rows, :] = result.astype(BF16)
+        at = start // step
+        copies.append(
+            pltpu.make_async_copy(o_ref.at[rows, :], o_hbm.at[rows, columns], sent.at[at])
+        )
+        copies[-1].start()
+    for copy in copies:
+        copy.wait()
 
 
 def apply_fast(ids, order, other, lines, queries, output, fast):
@@ -510,8 +518,13 @@
             num_scalar_prefetch=1,
             grid=(1,),
             in_specs=specs,
-            out_specs=pl.BlockSpec((rows, size), lambda i, ids: (0, head_of(ids, order, other))),
-            scratch_shapes=[pltpu.VMEM((size, 2 * fast), BF16), pltpu.VMEM((fast, size), BF16)],
+            out_specs=pl.BlockSpec(memory_space=pl.ANY),
+            scratch_shapes=[
+                pltpu.VMEM((size, 2 * fast), BF16),
+                pltpu.VMEM((fast, size), BF16),
+                pltpu.VMEM((rows, size), BF16),
+                pltpu.SemaphoreType.DMA((rows // 512,)),
+            ],
         ),
         out_shape=jax.ShapeDtypeStruct((rows, width), BF16),
         input_output_aliases=aliases,

time: 104 us -> 104 us (level)
  no operation moved by 1% of the time
where the time goes in v8:
time: 104 us; the launch traced here: 103 us
  starting transfers between devices  45.6 us (44%)
  Pallas kernels  28.1 us (27%)
  waiting for transfers between devices  24.7 us (24%)
  local copies, waits for them, and re-layouts  3.48 us (3%)
  between operations  1.09 us (1%)
    ppermute x37, starting transfers between devices, swap(): lax.ppermute(value, 'tok', [(place, place ^ bits) for place in range(coun...  42.5 us
    ppermute x37, waiting for transfers between devices, swap(): lax.ppermute(value, 'tok', [(place, place ^ bits) for place in range(coun...  21.7 us
    pallas_call x2, Pallas kernels, increments(): pl.pallas_call(increments_kernel, grid_spec=pltpu.PrefetchScalarGridSpec(...  11.7 us
    pallas_call x4, Pallas kernels, apply_fast(): pl.pallas_call(functools.partial(apply_kernel, order, other), grid_spec=p...  10 us
    pallas_call x2, Pallas kernels, prepare(): pl.pallas_call(functools.partial(prepare_kernel, heads, block_root), grid...  3.78 us
    unnamed x12, local copies, waits for them, and re-layouts  3.46 us
    ppermute x4, starting transfers between devices, swap_parts(): return lax.ppermute(value, 'parts', [(0, 1), (1, 0)])  3.06 us
    ppermute x4, waiting for transfers between devices, swap_parts(): return lax.ppermute(value, 'parts', [(0, 1), (1, 0)])  3 us
  transfers between devices with their start and end apart: 41, of which 11 were waited for; matrix products, arithmetic and copies ran while one was open for 0% of the time, Pallas kernels for 23%

profile of v8, /device:TPU:1, one launch (start us, length us, event | category | flops | bytes accessed | tf_op | source)
XLA Modules:
  0.0 103.2 jit_solution(10817318101140752995)
XLA Ops:
  0.7 0.9 copy-done.3
  1.7 0.9 copy-done.4
  2.6 0.8 pack.1
  3.4 0.1 collective-permute-start
  3.5 1.4 %collective-permute-done.got = f32[2,96,256]{2,1,0:T(8,128)S(1)} collective-permute-done((f32[2,96,256]{2,1,0:T(8,128)S(1)}, f32[2,96,256]{2,1,0:T(8,128)S(1)}, u32[]{:S(2)}, u32[]{:S(2)}) %collective-permute-start) | collective-permute-done | bytes 196640 | tf_op jit(solution)/shard_map/ppermute | solution.py:140
  4.9 1.6 %copy-done.1 = bf16[1024,1024]{1,0:T(8,128)(2,1)S(1)} copy-done((bf16[1024,1024]{1,0:T(8,128)(2,1)S(1)}, bf16[1024,1024]{1,0:T(8,128)(2,1)}, u32[]{:S(2)}) %copy-start.1) | copy-done | bytes 2097176
  6.5 1.5 %keys.1 = (bf16[1024,512]{1,0:T(8,128)(2,1)S(1)}, bf16[1024,512]{1,0:T(8,128)(2,1)S(1)}) custom-call(s32[3]{0:T(128)S(1)} %pad_add_fusion.ids, bf16[1024,1024]{1,0:T(8,128)(2,1)S(1)} %copy-done.1), custom_call_target="tpu_custom_call" | custom-call | flops 5242880 | bytes 4194304 | tf_op jit(solution)/shard_map/keys/pallas_call | solution.py:255
  8.0 0.2 collective-permute-start.2
  8.2 2.3 %values.1 = (bf16[1024,512]{1,0:T(8,128)(2,1)S(1)}, bf16[1024,512]{1,0:T(8,128)(2,1)S(1)}) custom-call(s32[3]{0:T(128)S(1)} %pad_add_fusion.ids, bf16[1024,1024]{1,0:T(8,128)(2,1)S(1)} %copy-done.2, f32[4,1024]{1,0:T(4,128)S(1)} %copy-done.5), custom_call_target="tpu_custom_call" | custom-call | flops 5242880 | bytes 4194304 | tf_op jit(solution)/shard_map/values/pallas_call | solution.py:255
  10.5 0.4 collective-permute-start.3
  11.0 2.5 %collective-permute-start.1 = (bf16[2,96,256]{2,1,0:T(8,128)(2,1)S(1)}, bf16[2,96,256]{2,1,0:T(8,128)(2,1)S(1)}, u32[]{:S(2)}, u32[]{:S(2)}) collective-permute-start(bf16[2,96,256]{2,1,0:T(8,128)(2,1)S(1)} %get-tuple-element.49), channel_id=1, source_target_pairs={{0,4},{1,5},{2,6},{3,7},{4,0},{5,1},{6,2},{7,3},{8,12},{9,13},{10,... | collective-permute-start | bytes 294920 | tf_op jit(solution)/shard_map/ppermute | solution.py:140
  13.5 2.2 %collective-permute-start.6 = (bf16[2,96,256]{2,1,0:T(8,128)(2,1)S(1)}, bf16[2,96,256]{2,1,0:T(8,128)(2,1)S(1)}, u32[]{:S(2)}, u32[]{:S(2)}) collective-permute-start(bf16[2,96,256]{2,1,0:T(8,128)(2,1)S(1)} %get-tuple-element.49), channel_id=1, source_target_pairs={{0,12},{1,13},{2,14},{3,15},{4,8},{5,9},{6,10},{7,11},{8,4},{9,5},... | collective-permute-start | bytes 294920 | tf_op jit(solution)/shard_map/ppermute | solution.py:140
  15.6 0.1 collective-permute-start.5
  15.8 0.6 collective-permute-done.1
  16.4 1.2 %collective-permute-start.7 = (bf16[2,2,96,256]{3,2,1,0:T(8,128)(2,1)S(1)}, bf16[2,2,96,256]{3,2,1,0:T(8,128)(2,1)S(1)}, u32[]{:S(2)}, u32[]{:S(2)}) collective-permute-start(bf16[2,2,96,256]{3,2,1,0:T(8,128)(2,1)S(1)} %pad_maximum_fusion.near_low), channel_id=1, source_target_pairs={{0,2},{1,3},{2,0},{3,1},{4,6},{5,7},{6,4},{7,5},{8,10},{9,11},{10,... | collective-permute-start | bytes 589832 | tf_op jit(solution)/shard_map/ppermute | solution.py:140
  17.5 1.2 %collective-permute-start.4 = (bf16[2,2,96,256]{3,2,1,0:T(8,128)(2,1)S(1)}, bf16[2,2,96,256]{3,2,1,0:T(8,128)(2,1)S(1)}, u32[]{:S(2)}, u32[]{:S(2)}) collective-permute-start(bf16[2,2,96,256]{3,2,1,0:T(8,128)(2,1)S(1)} %pad_maximum_fusion.near_low), channel_id=1, source_target_pairs={{0,16},{16,0},{1,17},{17,1},{2,18},{18,2},{3,19},{19,3},{4,20},{20... | collective-permute-start | bytes 589832 | tf_op jit(solution)/shard_map/ppermute | solution.py:144
  18.7 1.6 %collective-permute-done.6 = bf16[2,96,256]{2,1,0:T(8,128)(2,1)S(1)} collective-permute-done((bf16[2,96,256]{2,1,0:T(8,128)(2,1)S(1)}, bf16[2,96,256]{2,1,0:T(8,128)(2,1)S(1)}, u32[]{:S(2)}, u32[]{:S(2)}) %collective-permute-start.6) | collective-permute-done | bytes 98336 | tf_op jit(solution)/shard_map/ppermute | solution.py:140
  20.3 4.8 %collective-permute-done.5 = bf16[2,96,256]{2,1,0:T(8,128)(2,1)S(1)} collective-permute-done((bf16[2,96,256]{2,1,0:T(8,128)(2,1)S(1)}, bf16[2,96,256]{2,1,0:T(8,128)(2,1)S(1)}, u32[]{:S(2)}, u32[]{:S(2)}) %collective-permute-start.5) | collective-permute-done | bytes 98336 | tf_op jit(solution)/shard_map/ppermute | solution.py:140
  25.1 1.3 %collective-permute-start.9 = (bf16[2,2,96,256]{3,2,1,0:T(8,128)(2,1)S(1)}, bf16[2,2,96,256]{3,2,1,0:T(8,128)(2,1)S(1)}, u32[]{:S(2)}, u32[]{:S(2)}) collective-permute-start(bf16[2,2,96,256]{3,2,1,0:T(8,128)(2,1)S(1)} %collective-permute-done.7.far_low), channel_id=1, source_target_pairs={{0,16},{16,0},{1,17},{17,1},{2,18},{18,2},{3,19},{19,3},{4,20},{20... | collective-permute-start | bytes 589832 | tf_op jit(solution)/shard_map/ppermute | solution.py:144
  26.4 1.2 %collective-permute-start.10 = (bf16[2,2,96,256]{3,2,1,0:T(8,128)(2,1)S(1)}, bf16[2,2,96,256]{3,2,1,0:T(8,128)(2,1)S(1)}, u32[]{:S(2)}, u32[]{:S(2)}) collective-permute-start(bf16[2,2,96,256]{3,2,1,0:T(8,128)(2,1)S(1)} %pad_maximum_fusion.1.near_high), channel_id=1, source_target_pairs={{0,2},{1,3},{2,0},{3,1},{4,6},{5,7},{6,4},{7,5},{8,10},{9,11},{10,... | collective-permute-start | bytes 589832 | tf_op jit(solution)/shard_map/ppermute | solution.py:140
  27.7 0.3 collective-permute-start.8
  27.9 3.0 %collective-permute-done.9.far_low = bf16[2,2,96,256]{3,2,1,0:T(8,128)(2,1)S(1)} collective-permute-done((bf16[2,2,96,256]{3,2,1,0:T(8,128)(2,1)S(1)}, bf16[2,2,96,256]{3,2,1,0:T(8,128)(2,1)S(1)}, u32[]{:S(2)}, u32[]{:S(2)}) %collective-permute-start.9) | collective-permute-done | bytes 196640 | tf_op jit(solution)/shard_map/ppermute | solution.py:144
  30.9 0.9 collective-permute-done.10.far_high
  31.8 0.3 collective-permute-start.11
  32.1 5.8 %increments.3 = (f32[4,2,96,256]{3,2,1,0:T(8,128)S(1)}, bf16[2,2,96,256]{3,2,1,0:T(8,128)(2,1)S(1)}, bf16[2,2,96,256]{3,2,1,0:T(8,128)(2,1)S(1)}) custom-call(s32[3]{0:T(128)S(1)} %pad_add_fusion.ids, bf16[2,2,96,256]{3,2,1,0:T(8,128)(2,1)S(1)} %pad_maximum_fusion.near_low, bf16[2,2,96,256]{3,2,1,0:T(8,128)(2,1)S(1)} %pad_maximum_fusion.1.near_high, ...), custom_call_target="tpu_custom_call" | custom-call | flops 3221225472 | bytes 2097152 | tf_op jit(solution)/shard_map/increments/pallas_call | solution.py:387
  37.9 1.3 %collective-permute-start.17 = (bf16[2,2,96,256]{3,2,1,0:T(8,128)(2,1)S(1)}, bf16[2,2,96,256]{3,2,1,0:T(8,128)(2,1)S(1)}, u32[]{:S(2)}, u32[]{:S(2)}) collective-permute-start(bf16[2,2,96,256]{3,2,1,0:T(8,128)(2,1)S(1)} %get-tuple-element.65), channel_id=1, source_target_pairs={{0,2},{1,3},{2,0},{3,1},{4,6},{5,7},{6,4},{7,5},{8,10},{9,11},{10,... | collective-permute-start | bytes 589832 | tf_op jit(solution)/shard_map/ppermute | solution.py:140
  39.2 0.2 collective-permute-start.19
  39.4 5.9 %increments.2 = (f32[4,2,96,256]{3,2,1,0:T(8,128)S(1)}, bf16[2,2,96,256]{3,2,1,0:T(8,128)(2,1)S(1)}, bf16[2,2,96,256]{3,2,1,0:T(8,128)(2,1)S(1)}) custom-call(s32[3]{0:T(128)S(1)} %pad_add_fusion.ids, bf16[2,2,96,256]{3,2,1,0:T(8,128)(2,1)S(1)} %collective-permute-done.4.near_low, bf16[2,2,96,256]{3,2,1,0:T(8,128)(2,1)S(1)} %collective-permute-done.8.near_high, ...), custom_call_target="tpu_custom_call" | custom-call | flops 3221225472 | bytes 2097152 | tf_op jit(solution)/shard_map/increments/pallas_call | solution.py:387
  45.4 1.3 %collective-permute-start.12 = (bf16[2,2,96,256]{3,2,1,0:T(8,128)(2,1)S(1)}, bf16[2,2,96,256]{3,2,1,0:T(8,128)(2,1)S(1)}, u32[]{:S(2)}, u32[]{:S(2)}) collective-permute-start(bf16[2,2,96,256]{3,2,1,0:T(8,128)(2,1)S(1)} %get-tuple-element.55), channel_id=1, source_target_pairs={{0,2},{1,3},{2,0},{3,1},{4,6},{5,7},{6,4},{7,5},{8,10},{9,11},{10,... | collective-permute-start | bytes 589832 | tf_op jit(solution)/shard_map/ppermute | solution.py:140
  46.8 1.5 %collective-permute-start.20 = (bf16[2,96,256]{2,1,0:T(8,128)(2,1)S(1)}, bf16[2,96,256]{2,1,0:T(8,128)(2,1)S(1)}, u32[]{:S(2)}, u32[]{:S(2)}) collective-permute-start(bf16[2,96,256]{2,1,0:T(8,128)(2,1)S(1)} %get-tuple-element.69), channel_id=1, source_target_pairs={{0,8},{1,9},{2,10},{3,11},{4,12},{5,13},{6,14},{7,15},{8,0},{9,1},... | collective-permute-start | bytes 294920 | tf_op jit(solution)/shard_map/ppermute | solution.py:140
  48.4 2.1 %collective-permute-start.21 = (bf16[2,96,256]{2,1,0:T(8,128)(2,1)S(1)}, bf16[2,96,256]{2,1,0:T(8,128)(2,1)S(1)}, u32[]{:S(2)}, u32[]{:S(2)}) collective-permute-start(bf16[2,96,256]{2,1,0:T(8,128)(2,1)S(1)} %get-tuple-element.70), channel_id=1, source_target_pairs={{0,12},{1,13},{2,14},{3,15},{4,8},{5,9},{6,10},{7,11},{8,4},{9,5},... | collective-permute-start | bytes 294920 | tf_op jit(solution)/shard_map/ppermute | solution.py:140
  50.4 0.2 collective-permute-start.14
  50.7 0.6 collective-permute-done.20.two
  51.3 2.4 %collective-permute-done.21.three = bf16[2,96,256]{2,1,0:T(8,128)(2,1)S(1)} collective-permute-done((bf16[2,96,256]{2,1,0:T(8,128)(2,1)S(1)}, bf16[2,96,256]{2,1,0:T(8,128)(2,1)S(1)}, u32[]{:S(2)}, u32[]{:S(2)}) %collective-permute-start.21) | collective-permute-done | bytes 98336 | tf_op jit(solution)/shard_map/ppermute | solution.py:140
  53.7 0.1 renorm.3
  53.9 1.4 %collective-permute-start.22 = (bf16[2,96,256]{2,1,0:T(8,128)(2,1)S(1)}, bf16[2,96,256]{2,1,0:T(8,128)(2,1)S(1)}, u32[]{:S(2)}, u32[]{:S(2)}) collective-permute-start(bf16[2,96,256]{2,1,0:T(8,128)(2,1)S(1)} %get-tuple-element.71), channel_id=1, source_target_pairs={{0,4},{1,5},{2,6},{3,7},{4,0},{5,1},{6,2},{7,3},{8,12},{9,13},{10,... | collective-permute-start | bytes 294920 | tf_op jit(solution)/shard_map/ppermute | solution.py:140
  55.2 1.4 %collective-permute-start.25 = (bf16[2,96,256]{2,1,0:T(8,128)(2,1)S(1)}, bf16[2,96,256]{2,1,0:T(8,128)(2,1)S(1)}, u32[]{:S(2)}, u32[]{:S(2)}) collective-permute-start(bf16[2,96,256]{2,1,0:T(8,128)(2,1)S(1)} %get-tuple-element.71), channel_id=1, source_target_pairs={{0,12},{1,13},{2,14},{3,15},{4,8},{5,9},{6,10},{7,11},{8,4},{9,5},... | collective-permute-start | bytes 294920 | tf_op jit(solution)/shard_map/ppermute | solution.py:140
  56.6 0.2 collective-permute-start.24
  56.9 2.0 %collective-permute-start.13 = (bf16[2,96,256]{2,1,0:T(8,128)(2,1)S(1)}, bf16[2,96,256]{2,1,0:T(8,128)(2,1)S(1)}, u32[]{:S(2)}, u32[]{:S(2)}) collective-permute-start(bf16[2,96,256]{2,1,0:T(8,128)(2,1)S(1)} %get-tuple-element.57), channel_id=1, source_target_pairs={{0,4},{1,5},{2,6},{3,7},{4,0},{5,1},{6,2},{7,3},{8,12},{9,13},{10,... | collective-permute-start | bytes 294920 | tf_op jit(solution)/shard_map/ppermute | solution.py:140
  59.0 0.8 collective-permute-start.15
  59.8 1.4 %collective-permute-start.16 = (bf16[2,96,256]{2,1,0:T(8,128)(2,1)S(1)}, bf16[2,96,256]{2,1,0:T(8,128)(2,1)S(1)}, u32[]{:S(2)}, u32[]{:S(2)}) collective-permute-start(bf16[2,96,256]{2,1,0:T(8,128)(2,1)S(1)} %get-tuple-element.60), channel_id=1, source_target_pairs={{0,12},{1,13},{2,14},{3,15},{4,8},{5,9},{6,10},{7,11},{8,4},{9,5},... | collective-permute-start | bytes 294920 | tf_op jit(solution)/shard_map/ppermute | solution.py:140
  61.2 0.9 collective-permute-done.13.one
  62.0 0.2 collective-permute-start.36
  62.3 7.2 %collective-permute-done.15.two = bf16[2,96,256]{2,1,0:T(8,128)(2,1)S(1)} collective-permute-done((bf16[2,96,256]{2,1,0:T(8,128)(2,1)S(1)}, bf16[2,96,256]{2,1,0:T(8,128)(2,1)S(1)}, u32[]{:S(2)}, u32[]{:S(2)}) %collective-permute-start.15) | collective-permute-done | bytes 98336 | tf_op jit(solution)/shard_map/ppermute | solution.py:140
  69.4 0.1 renorm.2
  69.6 3.5 %collective-permute-start.23 = (bf16[2,96,256]{2,1,0:T(8,128)(2,1)S(1)}, bf16[2,96,256]{2,1,0:T(8,128)(2,1)S(1)}, u32[]{:S(2)}, u32[]{:S(2)}) collective-permute-start(bf16[2,96,256]{2,1,0:T(8,128)(2,1)S(1)} %get-tuple-element.74), channel_id=1, source_target_pairs={{0,4},{1,5},{2,6},{3,7},{4,0},{5,1},{6,2},{7,3},{8,12},{9,13},{10,... | collective-permute-start | bytes 294920 | tf_op jit(solution)/shard_map/ppermute | solution.py:140
  73.1 4.6 %collective-permute-start.29 = (f32[2,96,256]{2,1,0:T(8,128)S(1)}, f32[2,96,256]{2,1,0:T(8,128)S(1)}, u32[]{:S(2)}, u32[]{:S(2)}) collective-permute-start(f32[2,96,256]{2,1,0:T(8,128)S(1)} %pad_maximum_fusion.6), channel_id=1, source_target_pairs={{0,1},{1,0},{2,3},{3,2},{4,5},{5,4},{6,7},{7,6},{8,9},{9,8},{10,11... | collective-permute-start | bytes 589832 | tf_op jit(solution)/shard_map/ppermute | solution.py:140
  77.7 0.5 collective-permute-start.38
  78.2 2.4 %collective-permute-start.28 = (bf16[2,96,256]{2,1,0:T(8,128)(2,1)S(1)}, bf16[2,96,256]{2,1,0:T(8,128)(2,1)S(1)}, u32[]{:S(2)}, u32[]{:S(2)}) collective-permute-start(bf16[2,96,256]{2,1,0:T(8,128)(2,1)S(1)} %get-tuple-element.74), channel_id=1, source_target_pairs={{0,12},{1,13},{2,14},{3,15},{4,8},{5,9},{6,10},{7,11},{8,4},{9,5},... | collective-permute-start | bytes 294920 | tf_op jit(solution)/shard_map/ppermute | solution.py:140
  80.7 3.1 %collective-permute-start.34 = (bf16[2,2,96,256]{3,2,1,0:T(8,128)(2,1)S(1)}, bf16[2,2,96,256]{3,2,1,0:T(8,128)(2,1)S(1)}, u32[]{:S(2)}, u32[]{:S(2)}) collective-permute-start(bf16[2,2,96,256]{3,2,1,0:T(8,128)(2,1)S(1)} %pad_maximum_fusion.2.near_low), channel_id=1, source_target_pairs={{0,1},{1,0},{2,3},{3,2},{4,5},{5,4},{6,7},{7,6},{8,9},{9,8},{10,11... | collective-permute-start | bytes 589832 | tf_op jit(solution)/shard_map/ppermute | solution.py:140
  83.8 1.3 %finish.1 = (f32[4,16,1024]{2,1,0:T(8,128)}, f32[4,32,256]{2,1,0:T(8,128)}) custom-call(s32[3]{0:T(128)S(1)} %pad_add_fusion.ids, f32[2,96,256]{2,1,0:T(8,128)S(1)} %get-tuple-element.75.one, f32[2,96,256]{2,1,0:T(8,128)S(1)} %get-tuple-element.76.two, f32[2,96,256]{2,1,0:T(8,128)S(1)} %collective-permute-done.29.came), custom_call_target="tpu_custom_call" | custom-call | tf_op jit(solution)/shard_map/finish/pallas_call | solution.py:552
  85.1 0.5 collective-permute-start.31
  85.6 1.8 %collective-permute-start.37 = (bf16[2,2,96,256]{3,2,1,0:T(8,128)(2,1)S(1)}, bf16[2,2,96,256]{3,2,1,0:T(8,128)(2,1)S(1)}, u32[]{:S(2)}, u32[]{:S(2)}) collective-permute-start(bf16[2,2,96,256]{3,2,1,0:T(8,128)(2,1)S(1)} %collective-permute-done.36.far_low), channel_id=1, source_target_pairs={{0,1},{1,0},{2,3},{3,2},{4,5},{5,4},{6,7},{7,6},{8,9},{9,8},{10,11... | collective-permute-start | bytes 589832 | tf_op jit(solution)/shard_map/ppermute | solution.py:140
  87.3 1.4 %collective-permute-done.27 = bf16[2,96,256]{2,1,0:T(8,128)(2,1)S(1)} collective-permute-done((bf16[2,96,256]{2,1,0:T(8,128)(2,1)S(1)}, bf16[2,96,256]{2,1,0:T(8,128)(2,1)S(1)}, u32[]{:S(2)}, u32[]{:S(2)}) %collective-permute-start.27) | collective-permute-done | bytes 98336 | tf_op jit(solution)/shard_map/ppermute | solution.py:140
  88.7 1.8 %collective-permute-start.39 = (bf16[2,2,96,256]{3,2,1,0:T(8,128)(2,1)S(1)}, bf16[2,2,96,256]{3,2,1,0:T(8,128)(2,1)S(1)}, u32[]{:S(2)}, u32[]{:S(2)}) collective-permute-start(bf16[2,2,96,256]{3,2,1,0:T(8,128)(2,1)S(1)} %collective-permute-done.38.far_high), channel_id=1, source_target_pairs={{0,1},{1,0},{2,3},{3,2},{4,5},{5,4},{6,7},{7,6},{8,9},{9,8},{10,11... | collective-permute-start | bytes 589832 | tf_op jit(solution)/shard_map/ppermute | solution.py:140
  90.6 1.1 %collective-permute-start.33 = (bf16[2,2,96,256]{3,2,1,0:T(8,128)(2,1)S(1)}, bf16[2,2,96,256]{3,2,1,0:T(8,128)(2,1)S(1)}, u32[]{:S(2)}, u32[]{:S(2)}) collective-permute-start(bf16[2,2,96,256]{3,2,1,0:T(8,128)(2,1)S(1)} %pad_maximum_fusion.5.near_high), channel_id=1, source_target_pairs={{0,2},{1,3},{2,0},{3,1},{4,6},{5,7},{6,4},{7,5},{8,10},{9,11},{10,... | collective-permute-start | bytes 589832 | tf_op jit(solution)/shard_map/ppermute | solution.py:140
  91.7 2.5 %apply.4.rest_0_ = bf16[1024,1024]{1,0:T(8,128)(2,1)} custom-call(s32[3]{0:T(128)S(1)} %pad_add_fusion.ids, bf16[2,2,96,256]{3,2,1,0:T(8,128)(2,1)S(1)} %pad_maximum_fusion.2.near_low, bf16[2,2,96,256]{3,2,1,0:T(8,128)(2,1)S(1)} %pad_maximum_fusion.4.near_high, bf16[2,2,96,256]{3,2,1,0:T(8,128)(2,1)S(1)} %collective-permute-done.36.far_low, ...), custom_call_target="tpu_custom_call" | custom-call | flops 805306368 | bytes 1048576 | tf_op jit(solution)/shard_map/apply/pallas_call | solution.py:515
  94.3 0.3 collective-permute-start.26
  94.6 0.2 collective-permute-start.30
  94.8 0.3 collective-permute-start.32
  95.1 2.5 %apply.5.rest_0_ = bf16[1024,1024]{1,0:T(8,128)(2,1)} custom-call(s32[3]{0:T(128)S(1)} %pad_add_fusion.ids, bf16[2,2,96,256]{3,2,1,0:T(8,128)(2,1)S(1)} %collective-permute-done.34.near_low, bf16[2,2,96,256]{3,2,1,0:T(8,128)(2,1)S(1)} %collective-permute-done.35.near_high, ...), custom_call_target="tpu_custom_call", output_to_operand_aliasing={{}: (6, {})} | custom-call | flops 805306368 | bytes 1048576 | tf_op jit(solution)/shard_map/apply/pallas_call | solution.py:515
  97.6 0.3 collective-permute-start.40
  98.0 2.5 %apply.6.rest_0_ = bf16[1024,1024]{1,0:T(8,128)(2,1)} custom-call(s32[3]{0:T(128)S(1)} %pad_add_fusion.ids, bf16[2,2,96,256]{3,2,1,0:T(8,128)(2,1)S(1)} %pad_maximum_fusion.3.near_low, bf16[2,2,96,256]{3,2,1,0:T(8,128)(2,1)S(1)} %pad_maximum_fusion.5.near_high, ...), custom_call_target="tpu_custom_call", output_to_operand_aliasing={{}: (6, {})} | custom-call | flops 805306368 | bytes 1048576 | tf_op jit(solution)/shard_map/apply/pallas_call | solution.py:515
  100.5 2.5 %apply.7 = bf16[1024,1024]{1,0:T(8,128)(2,1)} custom-call(s32[3]{0:T(128)S(1)} %pad_add_fusion.ids, bf16[2,2,96,256]{3,2,1,0:T(8,128)(2,1)S(1)} %collective-permute-done.26.near_low, bf16[2,2,96,256]{3,2,1,0:T(8,128)(2,1)S(1)} %collective-permute-done.30.near_high, ...), custom_call_target="tpu_custom_call", output_to_operand_aliasing={{}: (6, {})} | custom-call | flops 805306368 | bytes 1048576 | tf_op jit(solution)/shard_map/apply/pallas_call | solution.py:515
  (57 shorter events, 0.6 us)
Async XLA Ops:
  0.6 7.6 %copy-start.5 = (f32[4,1024]{1,0:T(4,128)S(1)}, f32[4,1024]{1,0:T(4,128)}, u32[]{:S(2)}) copy-start(f32[4,1024]{1,0:T(4,128)} %rest_0_.1) | copy-start | bytes 49156
  0.7 1.0 copy-start.3
  1.7 0.9 copy-start.4
  3.4 1.5 %collective-permute-start = (f32[2,96,256]{2,1,0:T(8,128)S(1)}, f32[2,96,256]{2,1,0:T(8,128)S(1)}, u32[]{:S(2)}, u32[]{:S(2)}) collective-permute-start(f32[2,96,256]{2,1,0:T(8,128)S(1)} %get-tuple-element.43), channel_id=1, source_target_pairs={{0,1},{1,0},{2,3},{3,2},{4,5},{5,4},{6,7},{7,6},{8,9},{9,8},{10,11... | collective-permute-start | bytes 589832 | tf_op jit(solution)/shard_map/ppermute | solution.py:140
  4.9 1.6 %copy-start.1 = (bf16[1024,1024]{1,0:T(8,128)(2,1)S(1)}, bf16[1024,1024]{1,0:T(8,128)(2,1)}, u32[]{:S(2)}) copy-start(bf16[1024,1024]{1,0:T(8,128)(2,1)} %x_ref.2) | copy-start | bytes 6291460
  6.5 1.7 %copy-start.2 = (bf16[1024,1024]{1,0:T(8,128)(2,1)S(1)}, bf16[1024,1024]{1,0:T(8,128)(2,1)}, u32[]{:S(2)}) copy-start(bf16[1024,1024]{1,0:T(8,128)(2,1)} %x_ref.3) | copy-start | bytes 6291460
  8.0 8.4 %collective-permute-start.2 = (bf16[1024,512]{1,0:T(8,128)(2,1)S(1)}, bf16[1024,512]{1,0:T(8,128)(2,1)S(1)}, u32[]{:S(2)}, u32[]{:S(2)}) collective-permute-start(bf16[1024,512]{1,0:T(8,128)(2,1)S(1)} %get-tuple-element.45), channel_id=1, source_target_pairs={{0,1},{1,0},{2,3},{3,2},{4,5},{5,4},{6,7},{7,6},{8,9},{9,8},{10,11... | collective-permute-start | bytes 3145736 | tf_op jit(solution)/shard_map/ppermute | solution.py:140
  10.5 5.9 %collective-permute-start.3 = (bf16[1024,512]{1,0:T(8,128)(2,1)S(1)}, bf16[1024,512]{1,0:T(8,128)(2,1)S(1)}, u32[]{:S(2)}, u32[]{:S(2)}) collective-permute-start(bf16[1024,512]{1,0:T(8,128)(2,1)S(1)} %get-tuple-element.46), channel_id=1, source_target_pairs={{0,1},{1,0},{2,3},{3,2},{4,5},{5,4},{6,7},{7,6},{8,9},{9,8},{10,11... | collective-permute-start | bytes 3145736 | tf_op jit(solution)/shard_map/ppermute | solution.py:140
  11.0 5.4 %collective-permute-start.1 = (bf16[2,96,256]{2,1,0:T(8,128)(2,1)S(1)}, bf16[2,96,256]{2,1,0:T(8,128)(2,1)S(1)}, u32[]{:S(2)}, u32[]{:S(2)}) collective-permute-start(bf16[2,96,256]{2,1,0:T(8,128)(2,1)S(1)} %get-tuple-element.49), channel_id=1, source_target_pairs={{0,4},{1,5},{2,6},{3,7},{4,0},{5,1},{6,2},{7,3},{8,12},{9,13},{10,... | collective-permute-start | bytes 294920 | tf_op jit(solution)/shard_map/ppermute | solution.py:140
  13.5 6.8 %collective-permute-start.6 = (bf16[2,96,256]{2,1,0:T(8,128)(2,1)S(1)}, bf16[2,96,256]{2,1,0:T(8,128)(2,1)S(1)}, u32[]{:S(2)}, u32[]{:S(2)}) collective-permute-start(bf16[2,96,256]{2,1,0:T(8,128)(2,1)S(1)} %get-tuple-element.49), channel_id=1, source_target_pairs={{0,12},{1,13},{2,14},{3,15},{4,8},{5,9},{6,10},{7,11},{8,4},{9,5},... | collective-permute-start | bytes 294920 | tf_op jit(solution)/shard_map/ppermute | solution.py:140
  15.6 9.4 %collective-permute-start.5 = (bf16[2,96,256]{2,1,0:T(8,128)(2,1)S(1)}, bf16[2,96,256]{2,1,0:T(8,128)(2,1)S(1)}, u32[]{:S(2)}, u32[]{:S(2)}) collective-permute-start(bf16[2,96,256]{2,1,0:T(8,128)(2,1)S(1)} %get-tuple-element.49), channel_id=1, source_target_pairs={{0,8},{1,9},{2,10},{3,11},{4,12},{5,13},{6,14},{7,15},{8,0},{9,1},... | collective-permute-start | bytes 294920 | tf_op jit(solution)/shard_map/ppermute | solution.py:140
  16.4 8.8 %collective-permute-start.7 = (bf16[2,2,96,256]{3,2,1,0:T(8,128)(2,1)S(1)}, bf16[2,2,96,256]{3,2,1,0:T(8,128)(2,1)S(1)}, u32[]{:S(2)}, u32[]{:S(2)}) collective-permute-start(bf16[2,2,96,256]{3,2,1,0:T(8,128)(2,1)S(1)} %pad_maximum_fusion.near_low), channel_id=1, source_target_pairs={{0,2},{1,3},{2,0},{3,1},{4,6},{5,7},{6,4},{7,5},{8,10},{9,11},{10,... | collective-permute-start | bytes 589832 | tf_op jit(solution)/shard_map/ppermute | solution.py:140
  17.5 8.9 %collective-permute-start.4 = (bf16[2,2,96,256]{3,2,1,0:T(8,128)(2,1)S(1)}, bf16[2,2,96,256]{3,2,1,0:T(8,128)(2,1)S(1)}, u32[]{:S(2)}, u32[]{:S(2)}) collective-permute-start(bf16[2,2,96,256]{3,2,1,0:T(8,128)(2,1)S(1)} %pad_maximum_fusion.near_low), channel_id=1, source_target_pairs={{0,16},{16,0},{1,17},{17,1},{2,18},{18,2},{3,19},{19,3},{4,20},{20... | collective-permute-start | bytes 589832 | tf_op jit(solution)/shard_map/ppermute | solution.py:144
  25.1 5.8 %collective-permute-start.9 = (bf16[2,2,96,256]{3,2,1,0:T(8,128)(2,1)S(1)}, bf16[2,2,96,256]{3,2,1,0:T(8,128)(2,1)S(1)}, u32[]{:S(2)}, u32[]{:S(2)}) collective-permute-start(bf16[2,2,96,256]{3,2,1,0:T(8,128)(2,1)S(1)} %collective-permute-done.7.far_low), channel_id=1, source_target_pairs={{0,16},{16,0},{1,17},{17,1},{2,18},{18,2},{3,19},{19,3},{4,20},{20... | collective-permute-start | bytes 589832 | tf_op jit(solution)/shard_map/ppermute | solution.py:144
  26.4 5.4 %collective-permute-start.10 = (bf16[2,2,96,256]{3,2,1,0:T(8,128)(2,1)S(1)}, bf16[2,2,96,256]{3,2,1,0:T(8,128)(2,1)S(1)}, u32[]{:S(2)}, u32[]{:S(2)}) collective-permute-start(bf16[2,2,96,256]{3,2,1,0:T(8,128)(2,1)S(1)} %pad_maximum_fusion.1.near_high), channel_id=1, source_target_pairs={{0,2},{1,3},{2,0},{3,1},{4,6},{5,7},{6,4},{7,5},{8,10},{9,11},{10,... | collective-permute-start | bytes 589832 | tf_op jit(solution)/shard_map/ppermute | solution.py:140
  27.7 11.8 %collective-permute-start.8 = (bf16[2,2,96,256]{3,2,1,0:T(8,128)(2,1)S(1)}, bf16[2,2,96,256]{3,2,1,0:T(8,128)(2,1)S(1)}, u32[]{:S(2)}, u32[]{:S(2)}) collective-permute-start(bf16[2,2,96,256]{3,2,1,0:T(8,128)(2,1)S(1)} %pad_maximum_fusion.1.near_high), channel_id=1, source_target_pairs={{0,16},{16,0},{1,17},{17,1},{2,18},{18,2},{3,19},{19,3},{4,20},{20... | collective-permute-start | bytes 589832 | tf_op jit(solution)/shard_map/ppermute | solution.py:144
  31.8 7.6 %collective-permute-start.11 = (bf16[2,2,96,256]{3,2,1,0:T(8,128)(2,1)S(1)}, bf16[2,2,96,256]{3,2,1,0:T(8,128)(2,1)S(1)}, u32[]{:S(2)}, u32[]{:S(2)}) collective-permute-start(bf16[2,2,96,256]{3,2,1,0:T(8,128)(2,1)S(1)} %collective-permute-done.10.far_high), channel_id=1, source_target_pairs={{0,16},{16,0},{1,17},{17,1},{2,18},{18,2},{3,19},{19,3},{4,20},{20... | collective-permute-start | bytes 589832 | tf_op jit(solution)/shard_map/ppermute | solution.py:144
  37.9 8.8 %collective-permute-start.17 = (bf16[2,2,96,256]{3,2,1,0:T(8,128)(2,1)S(1)}, bf16[2,2,96,256]{3,2,1,0:T(8,128)(2,1)S(1)}, u32[]{:S(2)}, u32[]{:S(2)}) collective-permute-start(bf16[2,2,96,256]{3,2,1,0:T(8,128)(2,1)S(1)} %get-tuple-element.65), channel_id=1, source_target_pairs={{0,2},{1,3},{2,0},{3,1},{4,6},{5,7},{6,4},{7,5},{8,10},{9,11},{10,... | collective-permute-start | bytes 589832 | tf_op jit(solution)/shard_map/ppermute | solution.py:140
  39.2 7.6 %collective-permute-start.19 = (bf16[2,2,96,256]{3,2,1,0:T(8,128)(2,1)S(1)}, bf16[2,2,96,256]{3,2,1,0:T(8,128)(2,1)S(1)}, u32[]{:S(2)}, u32[]{:S(2)}) collective-permute-start(bf16[2,2,96,256]{3,2,1,0:T(8,128)(2,1)S(1)} %get-tuple-element.68), channel_id=1, source_target_pairs={{0,2},{1,3},{2,0},{3,1},{4,6},{5,7},{6,4},{7,5},{8,10},{9,11},{10,... | collective-permute-start | bytes 589832 | tf_op jit(solution)/shard_map/ppermute | solution.py:140
  45.4 11.5 %collective-permute-start.12 = (bf16[2,2,96,256]{3,2,1,0:T(8,128)(2,1)S(1)}, bf16[2,2,96,256]{3,2,1,0:T(8,128)(2,1)S(1)}, u32[]{:S(2)}, u32[]{:S(2)}) collective-permute-start(bf16[2,2,96,256]{3,2,1,0:T(8,128)(2,1)S(1)} %get-tuple-element.55), channel_id=1, source_target_pairs={{0,2},{1,3},{2,0},{3,1},{4,6},{5,7},{6,4},{7,5},{8,10},{9,11},{10,... | collective-permute-start | bytes 589832 | tf_op jit(solution)/shard_map/ppermute | solution.py:140
  46.7 4.0 %collective-permute-start.18 = (bf16[2,96,256]{2,1,0:T(8,128)(2,1)S(1)}, bf16[2,96,256]{2,1,0:T(8,128)(2,1)S(1)}, u32[]{:S(2)}, u32[]{:S(2)}) collective-permute-start(bf16[2,96,256]{2,1,0:T(8,128)(2,1)S(1)} %get-tuple-element.67), channel_id=1, source_target_pairs={{0,4},{1,5},{2,6},{3,7},{4,0},{5,1},{6,2},{7,3},{8,12},{9,13},{10,... | collective-permute-start | bytes 294920 | tf_op jit(solution)/shard_map/ppermute | solution.py:140
  46.8 4.5 %collective-permute-start.20 = (bf16[2,96,256]{2,1,0:T(8,128)(2,1)S(1)}, bf16[2,96,256]{2,1,0:T(8,128)(2,1)S(1)}, u32[]{:S(2)}, u32[]{:S(2)}) collective-permute-start(bf16[2,96,256]{2,1,0:T(8,128)(2,1)S(1)} %get-tuple-element.69), channel_id=1, source_target_pairs={{0,8},{1,9},{2,10},{3,11},{4,12},{5,13},{6,14},{7,15},{8,0},{9,1},... | collective-permute-start | bytes 294920 | tf_op jit(solution)/shard_map/ppermute | solution.py:140
  48.4 5.3 %collective-permute-start.21 = (bf16[2,96,256]{2,1,0:T(8,128)(2,1)S(1)}, bf16[2,96,256]{2,1,0:T(8,128)(2,1)S(1)}, u32[]{:S(2)}, u32[]{:S(2)}) collective-permute-start(bf16[2,96,256]{2,1,0:T(8,128)(2,1)S(1)} %get-tuple-element.70), channel_id=1, source_target_pairs={{0,12},{1,13},{2,14},{3,15},{4,8},{5,9},{6,10},{7,11},{8,4},{9,5},... | collective-permute-start | bytes 294920 | tf_op jit(solution)/shard_map/ppermute | solution.py:140
  50.4 8.5 %collective-permute-start.14 = (bf16[2,2,96,256]{3,2,1,0:T(8,128)(2,1)S(1)}, bf16[2,2,96,256]{3,2,1,0:T(8,128)(2,1)S(1)}, u32[]{:S(2)}, u32[]{:S(2)}) collective-permute-start(bf16[2,2,96,256]{3,2,1,0:T(8,128)(2,1)S(1)} %get-tuple-element.58), channel_id=1, source_target_pairs={{0,2},{1,3},{2,0},{3,1},{4,6},{5,7},{6,4},{7,5},{8,10},{9,11},{10,... | collective-permute-start | bytes 589832 | tf_op jit(solution)/shard_map/ppermute | solution.py:140
  53.9 5.9 %collective-permute-start.22 = (bf16[2,96,256]{2,1,0:T(8,128)(2,1)S(1)}, bf16[2,96,256]{2,1,0:T(8,128)(2,1)S(1)}, u32[]{:S(2)}, u32[]{:S(2)}) collective-permute-start(bf16[2,96,256]{2,1,0:T(8,128)(2,1)S(1)} %get-tuple-element.71), channel_id=1, source_target_pairs={{0,4},{1,5},{2,6},{3,7},{4,0},{5,1},{6,2},{7,3},{8,12},{9,13},{10,... | collective-permute-start | bytes 294920 | tf_op jit(solution)/shard_map/ppermute | solution.py:140
  55.2 22.5 %collective-permute-start.25 = (bf16[2,96,256]{2,1,0:T(8,128)(2,1)S(1)}, bf16[2,96,256]{2,1,0:T(8,128)(2,1)S(1)}, u32[]{:S(2)}, u32[]{:S(2)}) collective-permute-start(bf16[2,96,256]{2,1,0:T(8,128)(2,1)S(1)} %get-tuple-element.71), channel_id=1, source_target_pairs={{0,12},{1,13},{2,14},{3,15},{4,8},{5,9},{6,10},{7,11},{8,4},{9,5},... | collective-permute-start | bytes 294920 | tf_op jit(solution)/shard_map/ppermute | solution.py:140
  56.6 21.1 %collective-permute-start.24 = (bf16[2,96,256]{2,1,0:T(8,128)(2,1)S(1)}, bf16[2,96,256]{2,1,0:T(8,128)(2,1)S(1)}, u32[]{:S(2)}, u32[]{:S(2)}) collective-permute-start(bf16[2,96,256]{2,1,0:T(8,128)(2,1)S(1)} %get-tuple-element.71), channel_id=1, source_target_pairs={{0,8},{1,9},{2,10},{3,11},{4,12},{5,13},{6,14},{7,15},{8,0},{9,1},... | collective-permute-start | bytes 294920 | tf_op jit(solution)/shard_map/ppermute | solution.py:140
  56.9 34.8 %copy-start = (bf16[1024,1024]{1,0:T(8,128)(2,1)S(1)}, bf16[1024,1024]{1,0:T(8,128)(2,1)}, u32[]{:S(2)}) copy-start(bf16[1024,1024]{1,0:T(8,128)(2,1)} %q_ref.7) | copy-start | bytes 6291460
  56.9 5.1 %collective-permute-start.13 = (bf16[2,96,256]{2,1,0:T(8,128)(2,1)S(1)}, bf16[2,96,256]{2,1,0:T(8,128)(2,1)S(1)}, u32[]{:S(2)}, u32[]{:S(2)}) collective-permute-start(bf16[2,96,256]{2,1,0:T(8,128)(2,1)S(1)} %get-tuple-element.57), channel_id=1, source_target_pairs={{0,4},{1,5},{2,6},{3,7},{4,0},{5,1},{6,2},{7,3},{8,12},{9,13},{10,... | collective-permute-start | bytes 294920 | tf_op jit(solution)/shard_map/ppermute | solution.py:140
  59.0 10.4 %collective-permute-start.15 = (bf16[2,96,256]{2,1,0:T(8,128)(2,1)S(1)}, bf16[2,96,256]{2,1,0:T(8,128)(2,1)S(1)}, u32[]{:S(2)}, u32[]{:S(2)}) collective-permute-start(bf16[2,96,256]{2,1,0:T(8,128)(2,1)S(1)} %get-tuple-element.59), channel_id=1, source_target_pairs={{0,8},{1,9},{2,10},{3,11},{4,12},{5,13},{6,14},{7,15},{8,0},{9,1},... | collective-permute-start | bytes 294920 | tf_op jit(solution)/shard_map/ppermute | solution.py:140
  59.8 9.7 %collective-permute-start.16 = (bf16[2,96,256]{2,1,0:T(8,128)(2,1)S(1)}, bf16[2,96,256]{2,1,0:T(8,128)(2,1)S(1)}, u32[]{:S(2)}, u32[]{:S(2)}) collective-permute-start(bf16[2,96,256]{2,1,0:T(8,128)(2,1)S(1)} %get-tuple-element.60), channel_id=1, source_target_pairs={{0,12},{1,13},{2,14},{3,15},{4,8},{5,9},{6,10},{7,11},{8,4},{9,5},... | collective-permute-start | bytes 294920 | tf_op jit(solution)/shard_map/ppermute | solution.py:140
  62.0 23.1 %collective-permute-start.36 = (bf16[2,2,96,256]{3,2,1,0:T(8,128)(2,1)S(1)}, bf16[2,2,96,256]{3,2,1,0:T(8,128)(2,1)S(1)}, u32[]{:S(2)}, u32[]{:S(2)}) collective-permute-start(bf16[2,2,96,256]{3,2,1,0:T(8,128)(2,1)S(1)} %pad_maximum_fusion.2.near_low), channel_id=1, source_target_pairs={{0,2},{1,3},{2,0},{3,1},{4,6},{5,7},{6,4},{7,5},{8,10},{9,11},{10,... | collective-permute-start | bytes 589832 | tf_op jit(solution)/shard_map/ppermute | solution.py:140
  69.6 8.6 %collective-permute-start.23 = (bf16[2,96,256]{2,1,0:T(8,128)(2,1)S(1)}, bf16[2,96,256]{2,1,0:T(8,128)(2,1)S(1)}, u32[]{:S(2)}, u32[]{:S(2)}) collective-permute-start(bf16[2,96,256]{2,1,0:T(8,128)(2,1)S(1)} %get-tuple-element.74), channel_id=1, source_target_pairs={{0,4},{1,5},{2,6},{3,7},{4,0},{5,1},{6,2},{7,3},{8,12},{9,13},{10,... | collective-permute-start | bytes 294920 | tf_op jit(solution)/shard_map/ppermute | solution.py:140
  73.1 7.6 %collective-permute-start.29 = (f32[2,96,256]{2,1,0:T(8,128)S(1)}, f32[2,96,256]{2,1,0:T(8,128)S(1)}, u32[]{:S(2)}, u32[]{:S(2)}) collective-permute-start(f32[2,96,256]{2,1,0:T(8,128)S(1)} %pad_maximum_fusion.6), channel_id=1, source_target_pairs={{0,1},{1,0},{2,3},{3,2},{4,5},{5,4},{6,7},{7,6},{8,9},{9,8},{10,11... | collective-permute-start | bytes 589832 | tf_op jit(solution)/shard_map/ppermute | solution.py:140
  77.7 7.4 %collective-permute-start.38 = (bf16[2,2,96,256]{3,2,1,0:T(8,128)(2,1)S(1)}, bf16[2,2,96,256]{3,2,1,0:T(8,128)(2,1)S(1)}, u32[]{:S(2)}, u32[]{:S(2)}) collective-permute-start(bf16[2,2,96,256]{3,2,1,0:T(8,128)(2,1)S(1)} %pad_maximum_fusion.4.near_high), channel_id=1, source_target_pairs={{0,2},{1,3},{2,0},{3,1},{4,6},{5,7},{6,4},{7,5},{8,10},{9,11},{10,... | collective-permute-start | bytes 589832 | tf_op jit(solution)/shard_map/ppermute | solution.py:140
  78.2 7.3 %collective-permute-start.28 = (bf16[2,96,256]{2,1,0:T(8,128)(2,1)S(1)}, bf16[2,96,256]{2,1,0:T(8,128)(2,1)S(1)}, u32[]{:S(2)}, u32[]{:S(2)}) collective-permute-start(bf16[2,96,256]{2,1,0:T(8,128)(2,1)S(1)} %get-tuple-element.74), channel_id=1, source_target_pairs={{0,12},{1,13},{2,14},{3,15},{4,8},{5,9},{6,10},{7,11},{8,4},{9,5},... | collective-permute-start | bytes 294920 | tf_op jit(solution)/shard_map/ppermute | solution.py:140
  80.6 8.1 %collective-permute-start.27 = (bf16[2,96,256]{2,1,0:T(8,128)(2,1)S(1)}, bf16[2,96,256]{2,1,0:T(8,128)(2,1)S(1)}, u32[]{:S(2)}, u32[]{:S(2)}) collective-permute-start(bf16[2,96,256]{2,1,0:T(8,128)(2,1)S(1)} %get-tuple-element.74), channel_id=1, source_target_pairs={{0,8},{1,9},{2,10},{3,11},{4,12},{5,13},{6,14},{7,15},{8,0},{9,1},... | collective-permute-start | bytes 294920 | tf_op jit(solution)/shard_map/ppermute | solution.py:140
  80.7 9.9 %collective-permute-start.34 = (bf16[2,2,96,256]{3,2,1,0:T(8,128)(2,1)S(1)}, bf16[2,2,96,256]{3,2,1,0:T(8,128)(2,1)S(1)}, u32[]{:S(2)}, u32[]{:S(2)}) collective-permute-start(bf16[2,2,96,256]{3,2,1,0:T(8,128)(2,1)S(1)} %pad_maximum_fusion.2.near_low), channel_id=1, source_target_pairs={{0,1},{1,0},{2,3},{3,2},{4,5},{5,4},{6,7},{7,6},{8,9},{9,8},{10,11... | collective-permute-start | bytes 589832 | tf_op jit(solution)/shard_map/ppermute | solution.py:140
  85.1 9.2 %collective-permute-start.35 = (bf16[2,2,96,256]{3,2,1,0:T(8,128)(2,1)S(1)}, bf16[2,2,96,256]{3,2,1,0:T(8,128)(2,1)S(1)}, u32[]{:S(2)}, u32[]{:S(2)}) collective-permute-start(bf16[2,2,96,256]{3,2,1,0:T(8,128)(2,1)S(1)} %pad_maximum_fusion.4.near_high), channel_id=1, source_target_pairs={{0,1},{1,0},{2,3},{3,2},{4,5},{5,4},{6,7},{7,6},{8,9},{9,8},{10,11... | collective-permute-start | bytes 589832 | tf_op jit(solution)/shard_map/ppermute | solution.py:140
  85.1 9.5 %collective-permute-start.31 = (bf16[2,2,96,256]{3,2,1,0:T(8,128)(2,1)S(1)}, bf16[2,2,96,256]{3,2,1,0:T(8,128)(2,1)S(1)}, u32[]{:S(2)}, u32[]{:S(2)}) collective-permute-start(bf16[2,2,96,256]{3,2,1,0:T(8,128)(2,1)S(1)} %pad_maximum_fusion.3.near_low), channel_id=1, source_target_pairs={{0,2},{1,3},{2,0},{3,1},{4,6},{5,7},{6,4},{7,5},{8,10},{9,11},{10,... | collective-permute-start | bytes 589832 | tf_op jit(solution)/shard_map/ppermute | solution.py:140
  85.6 9.3 %collective-permute-start.37 = (bf16[2,2,96,256]{3,2,1,0:T(8,128)(2,1)S(1)}, bf16[2,2,96,256]{3,2,1,0:T(8,128)(2,1)S(1)}, u32[]{:S(2)}, u32[]{:S(2)}) collective-permute-start(bf16[2,2,96,256]{3,2,1,0:T(8,128)(2,1)S(1)} %collective-permute-done.36.far_low), channel_id=1, source_target_pairs={{0,1},{1,0},{2,3},{3,2},{4,5},{5,4},{6,7},{7,6},{8,9},{9,8},{10,11... | collective-permute-start | bytes 589832 | tf_op jit(solution)/shard_map/ppermute | solution.py:140
  88.7 6.4 %collective-permute-start.39 = (bf16[2,2,96,256]{3,2,1,0:T(8,128)(2,1)S(1)}, bf16[2,2,96,256]{3,2,1,0:T(8,128)(2,1)S(1)}, u32[]{:S(2)}, u32[]{:S(2)}) collective-permute-start(bf16[2,2,96,256]{3,2,1,0:T(8,128)(2,1)S(1)} %collective-permute-done.38.far_high), channel_id=1, source_target_pairs={{0,1},{1,0},{2,3},{3,2},{4,5},{5,4},{6,7},{7,6},{8,9},{9,8},{10,11... | collective-permute-start | bytes 589832 | tf_op jit(solution)/shard_map/ppermute | solution.py:140
  90.6 7.0 %collective-permute-start.33 = (bf16[2,2,96,256]{3,2,1,0:T(8,128)(2,1)S(1)}, bf16[2,2,96,256]{3,2,1,0:T(8,128)(2,1)S(1)}, u32[]{:S(2)}, u32[]{:S(2)}) collective-permute-start(bf16[2,2,96,256]{3,2,1,0:T(8,128)(2,1)S(1)} %pad_maximum_fusion.5.near_high), channel_id=1, source_target_pairs={{0,2},{1,3},{2,0},{3,1},{4,6},{5,7},{6,4},{7,5},{8,10},{9,11},{10,... | collective-permute-start | bytes 589832 | tf_op jit(solution)/shard_map/ppermute | solution.py:140
  94.3 6.2 %collective-permute-start.26 = (bf16[2,2,96,256]{3,2,1,0:T(8,128)(2,1)S(1)}, bf16[2,2,96,256]{3,2,1,0:T(8,128)(2,1)S(1)}, u32[]{:S(2)}, u32[]{:S(2)}) collective-permute-start(bf16[2,2,96,256]{3,2,1,0:T(8,128)(2,1)S(1)} %pad_maximum_fusion.3.near_low), channel_id=1, source_target_pairs={{0,1},{1,0},{2,3},{3,2},{4,5},{5,4},{6,7},{7,6},{8,9},{9,8},{10,11... | collective-permute-start | bytes 589832 | tf_op jit(solution)/shard_map/ppermute | solution.py:140
  94.6 5.9 %collective-permute-start.30 = (bf16[2,2,96,256]{3,2,1,0:T(8,128)(2,1)S(1)}, bf16[2,2,96,256]{3,2,1,0:T(8,128)(2,1)S(1)}, u32[]{:S(2)}, u32[]{:S(2)}) collective-permute-start(bf16[2,2,96,256]{3,2,1,0:T(8,128)(2,1)S(1)} %pad_maximum_fusion.5.near_high), channel_id=1, source_target_pairs={{0,1},{1,0},{2,3},{3,2},{4,5},{5,4},{6,7},{7,6},{8,9},{9,8},{10,11... | collective-permute-start | bytes 589832 | tf_op jit(solution)/shard_map/ppermute | solution.py:140
  94.8 5.7 %collective-permute-start.32 = (bf16[2,2,96,256]{3,2,1,0:T(8,128)(2,1)S(1)}, bf16[2,2,96,256]{3,2,1,0:T(8,128)(2,1)S(1)}, u32[]{:S(2)}, u32[]{:S(2)}) collective-permute-start(bf16[2,2,96,256]{3,2,1,0:T(8,128)(2,1)S(1)} %collective-permute-done.31.far_low), channel_id=1, source_target_pairs={{0,1},{1,0},{2,3},{3,2},{4,5},{5,4},{6,7},{7,6},{8,9},{9,8},{10,11... | collective-permute-start | bytes 589832 | tf_op jit(solution)/shard_map/ppermute | solution.py:140
  97.6 2.9 %collective-permute-start.40 = (bf16[2,2,96,256]{3,2,1,0:T(8,128)(2,1)S(1)}, bf16[2,2,96,256]{3,2,1,0:T(8,128)(2,1)S(1)}, u32[]{:S(2)}, u32[]{:S(2)}) collective-permute-start(bf16[2,2,96,256]{3,2,1,0:T(8,128)(2,1)S(1)} %collective-permute-done.33.far_high), channel_id=1, source_target_pairs={{0,1},{1,0},{2,3},{3,2},{4,5},{5,4},{6,7},{7,6},{8,9},{9,8},{10,11... | collective-permute-start | bytes 589832 | tf_op jit(solution)/shard_map/ppermute | solution.py:140

commit v9 on v8

--- a/solution.py
+++ b/solution.py
@@ -282,13 +282,14 @@
     blocks = w_in.shape[1] // size
     rows_in = w_in.shape[0] // 16
     rows_out = w_out.shape[0] // 16
+    in_root = 1.0 / math.sqrt(size)
     for side, slot, source, place in places(chip, core):
         ref = lines[2 * side + slot // 2].at[slot % 2]
         into = pl.ds(pl.multiple_of(place * rows_in, rows_in), rows_in)
         for block in range(blocks):
-            w_in[into, block * size : (block + 1) * size] = ref[
-                source, block * rows_in : (block + 1) * rows_in, :
-            ]
+            factor = in_root * (0.5 if block < blocks // 2 else 1.0)
+            piece = ref[source, block * rows_in : (block + 1) * rows_in, :].astype(F32)
+            w_in[into, block * size : (block + 1) * size] = (piece * factor).astype(BF16)
         into = pl.ds(pl.multiple_of(place * rows_out, rows_out), rows_out)
         w_out[into, :] = ref[source, blocks * rows_in :, :]
 
@@ -325,18 +326,18 @@
         for start in range(0, fast, chunk):
             gates = slice(start, start + chunk)
             ups = slice(fast + start, fast + start + chunk)
-            gate = jnp.dot(keyn, w_in[:, gates], preferred_element_type=F32) * in_root
-            upper = jnp.dot(keyn, w_in[:, ups], preferred_element_type=F32) * in_root
+            gate = jnp.dot(keyn, w_in[:, gates], preferred_element_type=F32)
+            upper = jnp.dot(keyn, w_in[:, ups], preferred_element_type=F32)
             back = (
                 lax.dot_general(
                     scaled, w_out[gates, :], (((1,), (1,)), ((), ())), preferred_element_type=F32
                 )
                 * out_root
             )
-            sigma = 0.5 * jnp.tanh(0.5 * gate) + 0.5
-            active = gate * sigma
+            twice = jnp.tanh(gate) + 1.0
+            active = gate * twice
             hidden = (active * upper).astype(BF16)
-            d_gate = (back * upper * (sigma + active * (1.0 - sigma))).astype(BF16)
+            d_gate = (back * upper * (twice + active * (2.0 - twice))).astype(BF16)
             d_up = (back * active).astype(BF16)
             add(acc_in, gates, jnp.dot(keyn_t, d_gate, preferred_element_type=F32))
             add(acc_in, ups, jnp.dot(keyn_t, d_up, preferred_element_type=F32))
@@ -367,7 +368,8 @@
             rows = pl.ds(pl.multiple_of(place * rows_in, rows_in), rows_in)
             for block in range(blocks):
                 ref[source, block * rows_in : (block + 1) * rows_in, :] = (
-                    acc_in[rows, block * size : (block + 1) * size] * in_root
+                    acc_in[rows, block * size : (block + 1) * size]
+                    * (in_root * (0.5 if block < blocks // 2 else 1.0))
                 ).astype(ref.dtype)
             rows = pl.ds(pl.multiple_of(place * rows_out, rows_out), rows_out)
             ref[source, blocks * rows_in :, :] = (turned[rows, :] * out_root).astype(ref.dtype)
@@ -480,16 +482,15 @@
     lines = (near_low, near_high, far_low, far_high)
     assemble(chip, jnp.bitwise_xor(core, other), lines, w_in, w_out)
     columns = pl.ds(pl.multiple_of(head_of(ids, order, other) * size, size), size)
-    in_root = 1.0 / math.sqrt(size)
     out_root = 1.0 / math.sqrt(fast)
     step = 512
     copies = []
     for start in range(0, q_ref.shape[0], step):
         rows = pl.ds(start, step)
         query = normalize_head(q_ref[rows, columns])
-        gate = jnp.dot(query, w_in[:, :fast], preferred_element_type=F32) * in_root
-        upper = jnp.dot(query, w_in[:, fast:], preferred_element_type=F32) * in_root
-        hidden = (gate * (0.5 * jnp.tanh(0.5 * gate) + 0.5) * upper).astype(BF16)
+        gate = jnp.dot(query, w_in[:, :fast], preferred_element_type=F32)
+        upper = jnp.dot(query, w_in[:, fast:], preferred_element_type=F32)
+        hidden = (gate * (jnp.tanh(gate) + 1.0) * upper).astype(BF16)
         result = jnp.dot(hidden, w_out[...], preferred_element_type=F32) * out_root
         o_ref[rows, :] = result.astype(BF16)
         at = start // step
@@ -570,10 +571,10 @@
     ids = jnp.stack([place // 2, place % 2, lax.axis_index("parts")]).astype(jnp.int32)
     block_root = 1.0 / math.sqrt(rows * lax.axis_size("tok"))
 
-    own, theirs = pack(ids, fast_in, fast_out)
+    k_own, k_send = prepare(ids, keys, None, heads, None, "keys")
+    own, theirs = pack(after(ids, k_own), fast_in, fast_out)
     got = swap(theirs, 1)
     later = after(ids, got)
-    k_own, k_send = prepare(later, keys, None, heads, None, "keys")
     v_own, v_send = prepare(later, values, step_size, heads, block_root, "values")
     master_one, master_two, shard = pair(own, after(got, k_send, v_send))
     masters = (master_one, master_two)

time: 104 us -> 103 us (level); the launches traced: 103 us -> 103 us
  starting transfers between devices: 45.6 us -> 47.5 us
  waiting for transfers between devices: 24.7 us -> 23.3 us
    ppermute x37, starting transfers between devices: 42.5 us -> 44.4 us  [swap(): lax.ppermute(value, 'tok', [(place, place ^ bits) for place in range(coun...]
    ppermute x37, waiting for transfers between devices: 21.7 us -> 20.1 us  [swap(): lax.ppermute(value, 'tok', [(place, place ^ bits) for place in range(coun...]
  transfers between devices with their start and end apart: 41 -> 41, of which waited for: 11 -> 11; matrix products, arithmetic and copies ran while one was open for 0% -> 0% of each run, Pallas kernels for 23% -> 22%
where the time goes in v9:
time: 103 us
  starting transfers between devices  47.5 us (46%)
  Pallas kernels  27.8 us (27%)
  waiting for transfers between devices  23.3 us (23%)
  local copies, waits for them, and re-layouts  3.47 us (3%)
  between operations  1.09 us (1%)
    ppermute x37, starting transfers between devices, swap(): lax.ppermute(value, 'tok', [(place, place ^ bits) for place in range(coun...  44.4 us
    ppermute x37, waiting for transfers between devices, swap(): lax.ppermute(value, 'tok', [(place, place ^ bits) for place in range(coun...  20.1 us
    pallas_call x2, Pallas kernels, increments(): pl.pallas_call(increments_kernel, grid_spec=pltpu.PrefetchScalarGridSpec(...  11.4 us
    pallas_call x4, Pallas kernels, apply_fast(): pl.pallas_call(functools.partial(apply_kernel, order, other), grid_spec=p...  9.98 us
    pallas_call x2, Pallas kernels, prepare(): pl.pallas_call(functools.partial(prepare_kernel, heads, block_root), grid...  3.78 us
    unnamed x12, local copies, waits for them, and re-layouts  3.46 us
    ppermute x4, waiting for transfers between devices, swap_parts(): return lax.ppermute(value, 'parts', [(0, 1), (1, 0)])  3.19 us
    ppermute x4, starting transfers between devices, swap_parts(): return lax.ppermute(value, 'parts', [(0, 1), (1, 0)])  3.06 us
  transfers between devices with their start and end apart: 41, of which 11 were waited for; matrix products, arithmetic and copies ran while one was open for 0% of the time, Pallas kernels for 22%

profile of v9, /device:TPU:1, one launch (start us, length us, event | category | flops | bytes accessed | tf_op | source)
XLA Modules:
  0.0 103.3 jit_solution(2768450203492752515)
XLA Ops:
  0.7 1.6 %copy-done.1 = bf16[1024,1024]{1,0:T(8,128)(2,1)S(1)} copy-done((bf16[1024,1024]{1,0:T(8,128)(2,1)S(1)}, bf16[1024,1024]{1,0:T(8,128)(2,1)}, u32[]{:S(2)}) %copy-start.1) | copy-done | bytes 2097176
  2.3 1.5 %keys.1 = (bf16[1024,512]{1,0:T(8,128)(2,1)S(1)}, bf16[1024,512]{1,0:T(8,128)(2,1)S(1)}) custom-call(s32[3]{0:T(128)S(1)} %pad_add_fusion.ids, bf16[1024,1024]{1,0:T(8,128)(2,1)S(1)} %copy-done.1), custom_call_target="tpu_custom_call" | custom-call | flops 5242880 | bytes 4194304 | tf_op jit(solution)/shard_map/keys/pallas_call | solution.py:255
  3.9 0.9 copy-done.3
  4.8 0.9 copy-done.4
  5.7 0.8 pack.1
  6.5 0.1 collective-permute-start
  6.6 0.5 collective-permute-start.2
  7.1 0.9 collective-permute-done.got
  8.0 2.3 %values.1 = (bf16[1024,512]{1,0:T(8,128)(2,1)S(1)}, bf16[1024,512]{1,0:T(8,128)(2,1)S(1)}) custom-call(s32[3]{0:T(128)S(1)} %pad_add_fusion.ids, bf16[1024,1024]{1,0:T(8,128)(2,1)S(1)} %copy-done.2, f32[4,1024]{1,0:T(4,128)S(1)} %copy-done.5), custom_call_target="tpu_custom_call" | custom-call | flops 5242880 | bytes 4194304 | tf_op jit(solution)/shard_map/values/pallas_call | solution.py:255
  10.3 0.2 collective-permute-start.3
  10.5 2.7 %collective-permute-start.1 = (bf16[2,96,256]{2,1,0:T(8,128)(2,1)S(1)}, bf16[2,96,256]{2,1,0:T(8,128)(2,1)S(1)}, u32[]{:S(2)}, u32[]{:S(2)}) collective-permute-start(bf16[2,96,256]{2,1,0:T(8,128)(2,1)S(1)} %get-tuple-element.52), channel_id=1, source_target_pairs={{0,4},{1,5},{2,6},{3,7},{4,0},{5,1},{6,2},{7,3},{8,12},{9,13},{10,... | collective-permute-start | bytes 294920 | tf_op jit(solution)/shard_map/ppermute | solution.py:140
  13.3 2.2 %collective-permute-start.6 = (bf16[2,96,256]{2,1,0:T(8,128)(2,1)S(1)}, bf16[2,96,256]{2,1,0:T(8,128)(2,1)S(1)}, u32[]{:S(2)}, u32[]{:S(2)}) collective-permute-start(bf16[2,96,256]{2,1,0:T(8,128)(2,1)S(1)} %get-tuple-element.52), channel_id=1, source_target_pairs={{0,12},{1,13},{2,14},{3,15},{4,8},{5,9},{6,10},{7,11},{8,4},{9,5},... | collective-permute-start | bytes 294920 | tf_op jit(solution)/shard_map/ppermute | solution.py:140
  15.4 0.1 collective-permute-start.5
  15.6 0.7 collective-permute-done.1
  16.3 1.2 %collective-permute-start.7 = (bf16[2,2,96,256]{3,2,1,0:T(8,128)(2,1)S(1)}, bf16[2,2,96,256]{3,2,1,0:T(8,128)(2,1)S(1)}, u32[]{:S(2)}, u32[]{:S(2)}) collective-permute-start(bf16[2,2,96,256]{3,2,1,0:T(8,128)(2,1)S(1)} %pad_maximum_fusion.near_low), channel_id=1, source_target_pairs={{0,2},{1,3},{2,0},{3,1},{4,6},{5,7},{6,4},{7,5},{8,10},{9,11},{10,... | collective-permute-start | bytes 589832 | tf_op jit(solution)/shard_map/ppermute | solution.py:140
  17.6 1.2 %collective-permute-start.4 = (bf16[2,2,96,256]{3,2,1,0:T(8,128)(2,1)S(1)}, bf16[2,2,96,256]{3,2,1,0:T(8,128)(2,1)S(1)}, u32[]{:S(2)}, u32[]{:S(2)}) collective-permute-start(bf16[2,2,96,256]{3,2,1,0:T(8,128)(2,1)S(1)} %pad_maximum_fusion.near_low), channel_id=1, source_target_pairs={{0,16},{16,0},{1,17},{17,1},{2,18},{18,2},{3,19},{19,3},{4,20},{20... | collective-permute-start | bytes 589832 | tf_op jit(solution)/shard_map/ppermute | solution.py:144
  18.8 1.6 %collective-permute-done.6 = bf16[2,96,256]{2,1,0:T(8,128)(2,1)S(1)} collective-permute-done((bf16[2,96,256]{2,1,0:T(8,128)(2,1)S(1)}, bf16[2,96,256]{2,1,0:T(8,128)(2,1)S(1)}, u32[]{:S(2)}, u32[]{:S(2)}) %collective-permute-start.6) | collective-permute-done | bytes 98336 | tf_op jit(solution)/shard_map/ppermute | solution.py:140
  20.4 4.6 %collective-permute-done.5 = bf16[2,96,256]{2,1,0:T(8,128)(2,1)S(1)} collective-permute-done((bf16[2,96,256]{2,1,0:T(8,128)(2,1)S(1)}, bf16[2,96,256]{2,1,0:T(8,128)(2,1)S(1)}, u32[]{:S(2)}, u32[]{:S(2)}) %collective-permute-start.5) | collective-permute-done | bytes 98336 | tf_op jit(solution)/shard_map/ppermute | solution.py:140
  25.1 1.3 %collective-permute-start.9 = (bf16[2,2,96,256]{3,2,1,0:T(8,128)(2,1)S(1)}, bf16[2,2,96,256]{3,2,1,0:T(8,128)(2,1)S(1)}, u32[]{:S(2)}, u32[]{:S(2)}) collective-permute-start(bf16[2,2,96,256]{3,2,1,0:T(8,128)(2,1)S(1)} %collective-permute-done.7.far_low), channel_id=1, source_target_pairs={{0,16},{16,0},{1,17},{17,1},{2,18},{18,2},{3,19},{19,3},{4,20},{20... | collective-permute-start | bytes 589832 | tf_op jit(solution)/shard_map/ppermute | solution.py:144
  26.3 1.2 %collective-permute-start.10 = (bf16[2,2,96,256]{3,2,1,0:T(8,128)(2,1)S(1)}, bf16[2,2,96,256]{3,2,1,0:T(8,128)(2,1)S(1)}, u32[]{:S(2)}, u32[]{:S(2)}) collective-permute-start(bf16[2,2,96,256]{3,2,1,0:T(8,128)(2,1)S(1)} %pad_maximum_fusion.1.near_high), channel_id=1, source_target_pairs={{0,2},{1,3},{2,0},{3,1},{4,6},{5,7},{6,4},{7,5},{8,10},{9,11},{10,... | collective-permute-start | bytes 589832 | tf_op jit(solution)/shard_map/ppermute | solution.py:140
  27.6 0.3 collective-permute-start.8
  27.8 3.1 %collective-permute-done.9.far_low = bf16[2,2,96,256]{3,2,1,0:T(8,128)(2,1)S(1)} collective-permute-done((bf16[2,2,96,256]{3,2,1,0:T(8,128)(2,1)S(1)}, bf16[2,2,96,256]{3,2,1,0:T(8,128)(2,1)S(1)}, u32[]{:S(2)}, u32[]{:S(2)}) %collective-permute-start.9) | collective-permute-done | bytes 196640 | tf_op jit(solution)/shard_map/ppermute | solution.py:144
  31.0 0.9 collective-permute-done.10.far_high
  31.9 0.3 collective-permute-start.11
  32.2 5.6 %increments.3 = (f32[4,2,96,256]{3,2,1,0:T(8,128)S(1)}, bf16[2,2,96,256]{3,2,1,0:T(8,128)(2,1)S(1)}, bf16[2,2,96,256]{3,2,1,0:T(8,128)(2,1)S(1)}) custom-call(s32[3]{0:T(128)S(1)} %pad_add_fusion.ids, bf16[2,2,96,256]{3,2,1,0:T(8,128)(2,1)S(1)} %pad_maximum_fusion.near_low, bf16[2,2,96,256]{3,2,1,0:T(8,128)(2,1)S(1)} %pad_maximum_fusion.1.near_high, ...), custom_call_target="tpu_custom_call" | custom-call | flops 3221225472 | bytes 2097152 | tf_op jit(solution)/shard_map/increments/pallas_call | solution.py:389
  37.8 1.3 %collective-permute-start.17 = (bf16[2,2,96,256]{3,2,1,0:T(8,128)(2,1)S(1)}, bf16[2,2,96,256]{3,2,1,0:T(8,128)(2,1)S(1)}, u32[]{:S(2)}, u32[]{:S(2)}) collective-permute-start(bf16[2,2,96,256]{3,2,1,0:T(8,128)(2,1)S(1)} %get-tuple-element.67), channel_id=1, source_target_pairs={{0,2},{1,3},{2,0},{3,1},{4,6},{5,7},{6,4},{7,5},{8,10},{9,11},{10,... | collective-permute-start | bytes 589832 | tf_op jit(solution)/shard_map/ppermute | solution.py:140
  39.1 0.2 collective-permute-start.19
  39.4 5.8 %increments.2 = (f32[4,2,96,256]{3,2,1,0:T(8,128)S(1)}, bf16[2,2,96,256]{3,2,1,0:T(8,128)(2,1)S(1)}, bf16[2,2,96,256]{3,2,1,0:T(8,128)(2,1)S(1)}) custom-call(s32[3]{0:T(128)S(1)} %pad_add_fusion.ids, bf16[2,2,96,256]{3,2,1,0:T(8,128)(2,1)S(1)} %collective-permute-done.4.near_low, bf16[2,2,96,256]{3,2,1,0:T(8,128)(2,1)S(1)} %collective-permute-done.8.near_high, ...), custom_call_target="tpu_custom_call" | custom-call | flops 3221225472 | bytes 2097152 | tf_op jit(solution)/shard_map/increments/pallas_call | solution.py:389
  45.2 1.3 %collective-permute-start.12 = (bf16[2,2,96,256]{3,2,1,0:T(8,128)(2,1)S(1)}, bf16[2,2,96,256]{3,2,1,0:T(8,128)(2,1)S(1)}, u32[]{:S(2)}, u32[]{:S(2)}) collective-permute-start(bf16[2,2,96,256]{3,2,1,0:T(8,128)(2,1)S(1)} %get-tuple-element.57), channel_id=1, source_target_pairs={{0,2},{1,3},{2,0},{3,1},{4,6},{5,7},{6,4},{7,5},{8,10},{9,11},{10,... | collective-permute-start | bytes 589832 | tf_op jit(solution)/shard_map/ppermute | solution.py:140
  46.7 1.3 %collective-permute-start.20 = (bf16[2,96,256]{2,1,0:T(8,128)(2,1)S(1)}, bf16[2,96,256]{2,1,0:T(8,128)(2,1)S(1)}, u32[]{:S(2)}, u32[]{:S(2)}) collective-permute-start(bf16[2,96,256]{2,1,0:T(8,128)(2,1)S(1)} %get-tuple-element.71), channel_id=1, source_target_pairs={{0,8},{1,9},{2,10},{3,11},{4,12},{5,13},{6,14},{7,15},{8,0},{9,1},... | collective-permute-start | bytes 294920 | tf_op jit(solution)/shard_map/ppermute | solution.py:140
  48.0 2.3 %collective-permute-start.21 = (bf16[2,96,256]{2,1,0:T(8,128)(2,1)S(1)}, bf16[2,96,256]{2,1,0:T(8,128)(2,1)S(1)}, u32[]{:S(2)}, u32[]{:S(2)}) collective-permute-start(bf16[2,96,256]{2,1,0:T(8,128)(2,1)S(1)} %get-tuple-element.72), channel_id=1, source_target_pairs={{0,12},{1,13},{2,14},{3,15},{4,8},{5,9},{6,10},{7,11},{8,4},{9,5},... | collective-permute-start | bytes 294920 | tf_op jit(solution)/shard_map/ppermute | solution.py:140
  50.3 0.2 collective-permute-start.14
  50.5 0.6 collective-permute-done.20.two
  51.2 2.3 %collective-permute-done.21.three = bf16[2,96,256]{2,1,0:T(8,128)(2,1)S(1)} collective-permute-done((bf16[2,96,256]{2,1,0:T(8,128)(2,1)S(1)}, bf16[2,96,256]{2,1,0:T(8,128)(2,1)S(1)}, u32[]{:S(2)}, u32[]{:S(2)}) %collective-permute-start.21) | collective-permute-done | bytes 98336 | tf_op jit(solution)/shard_map/ppermute | solution.py:140
  53.5 0.1 renorm.3
  53.7 1.5 %collective-permute-start.22 = (bf16[2,96,256]{2,1,0:T(8,128)(2,1)S(1)}, bf16[2,96,256]{2,1,0:T(8,128)(2,1)S(1)}, u32[]{:S(2)}, u32[]{:S(2)}) collective-permute-start(bf16[2,96,256]{2,1,0:T(8,128)(2,1)S(1)} %get-tuple-element.73), channel_id=1, source_target_pairs={{0,4},{1,5},{2,6},{3,7},{4,0},{5,1},{6,2},{7,3},{8,12},{9,13},{10,... | collective-permute-start | bytes 294920 | tf_op jit(solution)/shard_map/ppermute | solution.py:140
  55.1 1.7 %collective-permute-start.25 = (bf16[2,96,256]{2,1,0:T(8,128)(2,1)S(1)}, bf16[2,96,256]{2,1,0:T(8,128)(2,1)S(1)}, u32[]{:S(2)}, u32[]{:S(2)}) collective-permute-start(bf16[2,96,256]{2,1,0:T(8,128)(2,1)S(1)} %get-tuple-element.73), channel_id=1, source_target_pairs={{0,12},{1,13},{2,14},{3,15},{4,8},{5,9},{6,10},{7,11},{8,4},{9,5},... | collective-permute-start | bytes 294920 | tf_op jit(solution)/shard_map/ppermute | solution.py:140
  56.8 0.2 collective-permute-start.24
  57.1 1.8 %collective-permute-start.13 = (bf16[2,96,256]{2,1,0:T(8,128)(2,1)S(1)}, bf16[2,96,256]{2,1,0:T(8,128)(2,1)S(1)}, u32[]{:S(2)}, u32[]{:S(2)}) collective-permute-start(bf16[2,96,256]{2,1,0:T(8,128)(2,1)S(1)} %get-tuple-element.59), channel_id=1, source_target_pairs={{0,4},{1,5},{2,6},{3,7},{4,0},{5,1},{6,2},{7,3},{8,12},{9,13},{10,... | collective-permute-start | bytes 294920 | tf_op jit(solution)/shard_map/ppermute | solution.py:140
  58.9 1.0 collective-permute-start.15
  59.9 1.6 %collective-permute-start.16 = (bf16[2,96,256]{2,1,0:T(8,128)(2,1)S(1)}, bf16[2,96,256]{2,1,0:T(8,128)(2,1)S(1)}, u32[]{:S(2)}, u32[]{:S(2)}) collective-permute-start(bf16[2,96,256]{2,1,0:T(8,128)(2,1)S(1)} %get-tuple-element.62), channel_id=1, source_target_pairs={{0,12},{1,13},{2,14},{3,15},{4,8},{5,9},{6,10},{7,11},{8,4},{9,5},... | collective-permute-start | bytes 294920 | tf_op jit(solution)/shard_map/ppermute | solution.py:140
  61.5 0.4 collective-permute-done.13.one
  61.9 0.9 collective-permute-start.36
  62.8 6.0 %collective-permute-done.15.two = bf16[2,96,256]{2,1,0:T(8,128)(2,1)S(1)} collective-permute-done((bf16[2,96,256]{2,1,0:T(8,128)(2,1)S(1)}, bf16[2,96,256]{2,1,0:T(8,128)(2,1)S(1)}, u32[]{:S(2)}, u32[]{:S(2)}) %collective-permute-start.15) | collective-permute-done | bytes 98336 | tf_op jit(solution)/shard_map/ppermute | solution.py:140
  68.8 0.1 renorm.2
  68.9 3.5 %collective-permute-start.23 = (bf16[2,96,256]{2,1,0:T(8,128)(2,1)S(1)}, bf16[2,96,256]{2,1,0:T(8,128)(2,1)S(1)}, u32[]{:S(2)}, u32[]{:S(2)}) collective-permute-start(bf16[2,96,256]{2,1,0:T(8,128)(2,1)S(1)} %get-tuple-element.76), channel_id=1, source_target_pairs={{0,4},{1,5},{2,6},{3,7},{4,0},{5,1},{6,2},{7,3},{8,12},{9,13},{10,... | collective-permute-start | bytes 294920 | tf_op jit(solution)/shard_map/ppermute | solution.py:140
  72.5 5.0 %collective-permute-start.29 = (f32[2,96,256]{2,1,0:T(8,128)S(1)}, f32[2,96,256]{2,1,0:T(8,128)S(1)}, u32[]{:S(2)}, u32[]{:S(2)}) collective-permute-start(f32[2,96,256]{2,1,0:T(8,128)S(1)} %pad_maximum_fusion.6), channel_id=1, source_target_pairs={{0,1},{1,0},{2,3},{3,2},{4,5},{5,4},{6,7},{7,6},{8,9},{9,8},{10,11... | collective-permute-start | bytes 589832 | tf_op jit(solution)/shard_map/ppermute | solution.py:140
  77.5 0.8 collective-permute-start.38
  78.3 2.0 %collective-permute-start.28 = (bf16[2,96,256]{2,1,0:T(8,128)(2,1)S(1)}, bf16[2,96,256]{2,1,0:T(8,128)(2,1)S(1)}, u32[]{:S(2)}, u32[]{:S(2)}) collective-permute-start(bf16[2,96,256]{2,1,0:T(8,128)(2,1)S(1)} %get-tuple-element.76), channel_id=1, source_target_pairs={{0,12},{1,13},{2,14},{3,15},{4,8},{5,9},{6,10},{7,11},{8,4},{9,5},... | collective-permute-start | bytes 294920 | tf_op jit(solution)/shard_map/ppermute | solution.py:140
  80.4 3.2 %collective-permute-start.34 = (bf16[2,2,96,256]{3,2,1,0:T(8,128)(2,1)S(1)}, bf16[2,2,96,256]{3,2,1,0:T(8,128)(2,1)S(1)}, u32[]{:S(2)}, u32[]{:S(2)}) collective-permute-start(bf16[2,2,96,256]{3,2,1,0:T(8,128)(2,1)S(1)} %pad_maximum_fusion.2.near_low), channel_id=1, source_target_pairs={{0,1},{1,0},{2,3},{3,2},{4,5},{5,4},{6,7},{7,6},{8,9},{9,8},{10,11... | collective-permute-start | bytes 589832 | tf_op jit(solution)/shard_map/ppermute | solution.py:140
  83.5 1.3 %finish.1 = (f32[4,16,1024]{2,1,0:T(8,128)}, f32[4,32,256]{2,1,0:T(8,128)}) custom-call(s32[3]{0:T(128)S(1)} %pad_add_fusion.ids, f32[2,96,256]{2,1,0:T(8,128)S(1)} %get-tuple-element.77.one, f32[2,96,256]{2,1,0:T(8,128)S(1)} %get-tuple-element.78.two, f32[2,96,256]{2,1,0:T(8,128)S(1)} %collective-permute-done.29.came), custom_call_target="tpu_custom_call" | custom-call | tf_op jit(solution)/shard_map/finish/pallas_call | solution.py:553
  84.9 0.8 collective-permute-start.31
  85.7 1.3 %collective-permute-start.37 = (bf16[2,2,96,256]{3,2,1,0:T(8,128)(2,1)S(1)}, bf16[2,2,96,256]{3,2,1,0:T(8,128)(2,1)S(1)}, u32[]{:S(2)}, u32[]{:S(2)}) collective-permute-start(bf16[2,2,96,256]{3,2,1,0:T(8,128)(2,1)S(1)} %collective-permute-done.36.far_low), channel_id=1, source_target_pairs={{0,1},{1,0},{2,3},{3,2},{4,5},{5,4},{6,7},{7,6},{8,9},{9,8},{10,11... | collective-permute-start | bytes 589832 | tf_op jit(solution)/shard_map/ppermute | solution.py:140
  87.0 1.9 %collective-permute-done.27 = bf16[2,96,256]{2,1,0:T(8,128)(2,1)S(1)} collective-permute-done((bf16[2,96,256]{2,1,0:T(8,128)(2,1)S(1)}, bf16[2,96,256]{2,1,0:T(8,128)(2,1)S(1)}, u32[]{:S(2)}, u32[]{:S(2)}) %collective-permute-start.27) | collective-permute-done | bytes 98336 | tf_op jit(solution)/shard_map/ppermute | solution.py:140
  88.9 1.8 %collective-permute-start.39 = (bf16[2,2,96,256]{3,2,1,0:T(8,128)(2,1)S(1)}, bf16[2,2,96,256]{3,2,1,0:T(8,128)(2,1)S(1)}, u32[]{:S(2)}, u32[]{:S(2)}) collective-permute-start(bf16[2,2,96,256]{3,2,1,0:T(8,128)(2,1)S(1)} %collective-permute-done.38.far_high), channel_id=1, source_target_pairs={{0,1},{1,0},{2,3},{3,2},{4,5},{5,4},{6,7},{7,6},{8,9},{9,8},{10,11... | collective-permute-start | bytes 589832 | tf_op jit(solution)/shard_map/ppermute | solution.py:140
  90.7 0.8 collective-permute-start.33
  91.5 2.5 %apply.4.rest_0_ = bf16[1024,1024]{1,0:T(8,128)(2,1)} custom-call(s32[3]{0:T(128)S(1)} %pad_add_fusion.ids, bf16[2,2,96,256]{3,2,1,0:T(8,128)(2,1)S(1)} %pad_maximum_fusion.2.near_low, bf16[2,2,96,256]{3,2,1,0:T(8,128)(2,1)S(1)} %pad_maximum_fusion.4.near_high, bf16[2,2,96,256]{3,2,1,0:T(8,128)(2,1)S(1)} %collective-permute-done.36.far_low, ...), custom_call_target="tpu_custom_call" | custom-call | flops 805306368 | bytes 1048576 | tf_op jit(solution)/shard_map/apply/pallas_call | solution.py:516
  94.0 0.3 collective-permute-start.26
  94.3 0.2 collective-permute-start.30
  94.6 0.3 collective-permute-start.32
  94.9 2.5 %apply.5.rest_0_ = bf16[1024,1024]{1,0:T(8,128)(2,1)} custom-call(s32[3]{0:T(128)S(1)} %pad_add_fusion.ids, bf16[2,2,96,256]{3,2,1,0:T(8,128)(2,1)S(1)} %collective-permute-done.34.near_low, bf16[2,2,96,256]{3,2,1,0:T(8,128)(2,1)S(1)} %collective-permute-done.35.near_high, ...), custom_call_target="tpu_custom_call", output_to_operand_aliasing={{}: (6, {})} | custom-call | flops 805306368 | bytes 1048576 | tf_op jit(solution)/shard_map/apply/pallas_call | solution.py:516
  97.4 0.7 collective-permute-start.40
  98.1 2.5 %apply.6.rest_0_ = bf16[1024,1024]{1,0:T(8,128)(2,1)} custom-call(s32[3]{0:T(128)S(1)} %pad_add_fusion.ids, bf16[2,2,96,256]{3,2,1,0:T(8,128)(2,1)S(1)} %pad_maximum_fusion.3.near_low, bf16[2,2,96,256]{3,2,1,0:T(8,128)(2,1)S(1)} %pad_maximum_fusion.5.near_high, ...), custom_call_target="tpu_custom_call", output_to_operand_aliasing={{}: (6, {})} | custom-call | flops 805306368 | bytes 1048576 | tf_op jit(solution)/shard_map/apply/pallas_call | solution.py:516
  100.6 2.5 %apply.7 = bf16[1024,1024]{1,0:T(8,128)(2,1)} custom-call(s32[3]{0:T(128)S(1)} %pad_add_fusion.ids, bf16[2,2,96,256]{3,2,1,0:T(8,128)(2,1)S(1)} %collective-permute-done.26.near_low, bf16[2,2,96,256]{3,2,1,0:T(8,128)(2,1)S(1)} %collective-permute-done.30.near_high, ...), custom_call_target="tpu_custom_call", output_to_operand_aliasing={{}: (6, {})} | custom-call | flops 805306368 | bytes 1048576 | tf_op jit(solution)/shard_map/apply/pallas_call | solution.py:516
  (57 shorter events, 0.6 us)
Async XLA Ops:
  0.6 7.4 %copy-start.5 = (f32[4,1024]{1,0:T(4,128)S(1)}, f32[4,1024]{1,0:T(4,128)}, u32[]{:S(2)}) copy-start(f32[4,1024]{1,0:T(4,128)} %rest_0_.1) | copy-start | bytes 49156
  0.7 1.6 %copy-start.1 = (bf16[1024,1024]{1,0:T(8,128)(2,1)S(1)}, bf16[1024,1024]{1,0:T(8,128)(2,1)}, u32[]{:S(2)}) copy-start(bf16[1024,1024]{1,0:T(8,128)(2,1)} %x_ref.2) | copy-start | bytes 6291460
  2.3 5.7 %copy-start.2 = (bf16[1024,1024]{1,0:T(8,128)(2,1)S(1)}, bf16[1024,1024]{1,0:T(8,128)(2,1)}, u32[]{:S(2)}) copy-start(bf16[1024,1024]{1,0:T(8,128)(2,1)} %x_ref.3) | copy-start | bytes 6291460
  3.8 1.0 copy-start.3
  4.8 0.9 copy-start.4
  6.5 1.5 %collective-permute-start = (f32[2,96,256]{2,1,0:T(8,128)S(1)}, f32[2,96,256]{2,1,0:T(8,128)S(1)}, u32[]{:S(2)}, u32[]{:S(2)}) collective-permute-start(f32[2,96,256]{2,1,0:T(8,128)S(1)} %get-tuple-element.46), channel_id=1, source_target_pairs={{0,1},{1,0},{2,3},{3,2},{4,5},{5,4},{6,7},{7,6},{8,9},{9,8},{10,11... | collective-permute-start | bytes 589832 | tf_op jit(solution)/shard_map/ppermute | solution.py:140
  6.6 9.7 %collective-permute-start.2 = (bf16[1024,512]{1,0:T(8,128)(2,1)S(1)}, bf16[1024,512]{1,0:T(8,128)(2,1)S(1)}, u32[]{:S(2)}, u32[]{:S(2)}) collective-permute-start(bf16[1024,512]{1,0:T(8,128)(2,1)S(1)} %get-tuple-element.47), channel_id=1, source_target_pairs={{0,1},{1,0},{2,3},{3,2},{4,5},{5,4},{6,7},{7,6},{8,9},{9,8},{10,11... | collective-permute-start | bytes 3145736 | tf_op jit(solution)/shard_map/ppermute | solution.py:140
  10.3 6.0 %collective-permute-start.3 = (bf16[1024,512]{1,0:T(8,128)(2,1)S(1)}, bf16[1024,512]{1,0:T(8,128)(2,1)S(1)}, u32[]{:S(2)}, u32[]{:S(2)}) collective-permute-start(bf16[1024,512]{1,0:T(8,128)(2,1)S(1)} %get-tuple-element.49), channel_id=1, source_target_pairs={{0,1},{1,0},{2,3},{3,2},{4,5},{5,4},{6,7},{7,6},{8,9},{9,8},{10,11... | collective-permute-start | bytes 3145736 | tf_op jit(solution)/shard_map/ppermute | solution.py:140
  10.5 5.8 %collective-permute-start.1 = (bf16[2,96,256]{2,1,0:T(8,128)(2,1)S(1)}, bf16[2,96,256]{2,1,0:T(8,128)(2,1)S(1)}, u32[]{:S(2)}, u32[]{:S(2)}) collective-permute-start(bf16[2,96,256]{2,1,0:T(8,128)(2,1)S(1)} %get-tuple-element.52), channel_id=1, source_target_pairs={{0,4},{1,5},{2,6},{3,7},{4,0},{5,1},{6,2},{7,3},{8,12},{9,13},{10,... | collective-permute-start | bytes 294920 | tf_op jit(solution)/shard_map/ppermute | solution.py:140
  13.3 7.1 %collective-permute-start.6 = (bf16[2,96,256]{2,1,0:T(8,128)(2,1)S(1)}, bf16[2,96,256]{2,1,0:T(8,128)(2,1)S(1)}, u32[]{:S(2)}, u32[]{:S(2)}) collective-permute-start(bf16[2,96,256]{2,1,0:T(8,128)(2,1)S(1)} %get-tuple-element.52), channel_id=1, source_target_pairs={{0,12},{1,13},{2,14},{3,15},{4,8},{5,9},{6,10},{7,11},{8,4},{9,5},... | collective-permute-start | bytes 294920 | tf_op jit(solution)/shard_map/ppermute | solution.py:140
  15.4 9.6 %collective-permute-start.5 = (bf16[2,96,256]{2,1,0:T(8,128)(2,1)S(1)}, bf16[2,96,256]{2,1,0:T(8,128)(2,1)S(1)}, u32[]{:S(2)}, u32[]{:S(2)}) collective-permute-start(bf16[2,96,256]{2,1,0:T(8,128)(2,1)S(1)} %get-tuple-element.52), channel_id=1, source_target_pairs={{0,8},{1,9},{2,10},{3,11},{4,12},{5,13},{6,14},{7,15},{8,0},{9,1},... | collective-permute-start | bytes 294920 | tf_op jit(solution)/shard_map/ppermute | solution.py:140
  16.3 8.7 %collective-permute-start.7 = (bf16[2,2,96,256]{3,2,1,0:T(8,128)(2,1)S(1)}, bf16[2,2,96,256]{3,2,1,0:T(8,128)(2,1)S(1)}, u32[]{:S(2)}, u32[]{:S(2)}) collective-permute-start(bf16[2,2,96,256]{3,2,1,0:T(8,128)(2,1)S(1)} %pad_maximum_fusion.near_low), channel_id=1, source_target_pairs={{0,2},{1,3},{2,0},{3,1},{4,6},{5,7},{6,4},{7,5},{8,10},{9,11},{10,... | collective-permute-start | bytes 589832 | tf_op jit(solution)/shard_map/ppermute | solution.py:140
  17.6 8.8 %collective-permute-start.4 = (bf16[2,2,96,256]{3,2,1,0:T(8,128)(2,1)S(1)}, bf16[2,2,96,256]{3,2,1,0:T(8,128)(2,1)S(1)}, u32[]{:S(2)}, u32[]{:S(2)}) collective-permute-start(bf16[2,2,96,256]{3,2,1,0:T(8,128)(2,1)S(1)} %pad_maximum_fusion.near_low), channel_id=1, source_target_pairs={{0,16},{16,0},{1,17},{17,1},{2,18},{18,2},{3,19},{19,3},{4,20},{20... | collective-permute-start | bytes 589832 | tf_op jit(solution)/shard_map/ppermute | solution.py:144
  25.1 5.9 %collective-permute-start.9 = (bf16[2,2,96,256]{3,2,1,0:T(8,128)(2,1)S(1)}, bf16[2,2,96,256]{3,2,1,0:T(8,128)(2,1)S(1)}, u32[]{:S(2)}, u32[]{:S(2)}) collective-permute-start(bf16[2,2,96,256]{3,2,1,0:T(8,128)(2,1)S(1)} %collective-permute-done.7.far_low), channel_id=1, source_target_pairs={{0,16},{16,0},{1,17},{17,1},{2,18},{18,2},{3,19},{19,3},{4,20},{20... | collective-permute-start | bytes 589832 | tf_op jit(solution)/shard_map/ppermute | solution.py:144
  26.3 5.5 %collective-permute-start.10 = (bf16[2,2,96,256]{3,2,1,0:T(8,128)(2,1)S(1)}, bf16[2,2,96,256]{3,2,1,0:T(8,128)(2,1)S(1)}, u32[]{:S(2)}, u32[]{:S(2)}) collective-permute-start(bf16[2,2,96,256]{3,2,1,0:T(8,128)(2,1)S(1)} %pad_maximum_fusion.1.near_high), channel_id=1, source_target_pairs={{0,2},{1,3},{2,0},{3,1},{4,6},{5,7},{6,4},{7,5},{8,10},{9,11},{10,... | collective-permute-start | bytes 589832 | tf_op jit(solution)/shard_map/ppermute | solution.py:140
  27.6 11.8 %collective-permute-start.8 = (bf16[2,2,96,256]{3,2,1,0:T(8,128)(2,1)S(1)}, bf16[2,2,96,256]{3,2,1,0:T(8,128)(2,1)S(1)}, u32[]{:S(2)}, u32[]{:S(2)}) collective-permute-start(bf16[2,2,96,256]{3,2,1,0:T(8,128)(2,1)S(1)} %pad_maximum_fusion.1.near_high), channel_id=1, source_target_pairs={{0,16},{16,0},{1,17},{17,1},{2,18},{18,2},{3,19},{19,3},{4,20},{20... | collective-permute-start | bytes 589832 | tf_op jit(solution)/shard_map/ppermute | solution.py:144
  31.9 7.5 %collective-permute-start.11 = (bf16[2,2,96,256]{3,2,1,0:T(8,128)(2,1)S(1)}, bf16[2,2,96,256]{3,2,1,0:T(8,128)(2,1)S(1)}, u32[]{:S(2)}, u32[]{:S(2)}) collective-permute-start(bf16[2,2,96,256]{3,2,1,0:T(8,128)(2,1)S(1)} %collective-permute-done.10.far_high), channel_id=1, source_target_pairs={{0,16},{16,0},{1,17},{17,1},{2,18},{18,2},{3,19},{19,3},{4,20},{20... | collective-permute-start | bytes 589832 | tf_op jit(solution)/shard_map/ppermute | solution.py:144
  37.8 8.7 %collective-permute-start.17 = (bf16[2,2,96,256]{3,2,1,0:T(8,128)(2,1)S(1)}, bf16[2,2,96,256]{3,2,1,0:T(8,128)(2,1)S(1)}, u32[]{:S(2)}, u32[]{:S(2)}) collective-permute-start(bf16[2,2,96,256]{3,2,1,0:T(8,128)(2,1)S(1)} %get-tuple-element.67), channel_id=1, source_target_pairs={{0,2},{1,3},{2,0},{3,1},{4,6},{5,7},{6,4},{7,5},{8,10},{9,11},{10,... | collective-permute-start | bytes 589832 | tf_op jit(solution)/shard_map/ppermute | solution.py:140
  39.1 7.5 %collective-permute-start.19 = (bf16[2,2,96,256]{3,2,1,0:T(8,128)(2,1)S(1)}, bf16[2,2,96,256]{3,2,1,0:T(8,128)(2,1)S(1)}, u32[]{:S(2)}, u32[]{:S(2)}) collective-permute-start(bf16[2,2,96,256]{3,2,1,0:T(8,128)(2,1)S(1)} %get-tuple-element.70), channel_id=1, source_target_pairs={{0,2},{1,3},{2,0},{3,1},{4,6},{5,7},{6,4},{7,5},{8,10},{9,11},{10,... | collective-permute-start | bytes 589832 | tf_op jit(solution)/shard_map/ppermute | solution.py:140
  45.2 11.8 %collective-permute-start.12 = (bf16[2,2,96,256]{3,2,1,0:T(8,128)(2,1)S(1)}, bf16[2,2,96,256]{3,2,1,0:T(8,128)(2,1)S(1)}, u32[]{:S(2)}, u32[]{:S(2)}) collective-permute-start(bf16[2,2,96,256]{3,2,1,0:T(8,128)(2,1)S(1)} %get-tuple-element.57), channel_id=1, source_target_pairs={{0,2},{1,3},{2,0},{3,1},{4,6},{5,7},{6,4},{7,5},{8,10},{9,11},{10,... | collective-permute-start | bytes 589832 | tf_op jit(solution)/shard_map/ppermute | solution.py:140
  46.6 4.0 %collective-permute-start.18 = (bf16[2,96,256]{2,1,0:T(8,128)(2,1)S(1)}, bf16[2,96,256]{2,1,0:T(8,128)(2,1)S(1)}, u32[]{:S(2)}, u32[]{:S(2)}) collective-permute-start(bf16[2,96,256]{2,1,0:T(8,128)(2,1)S(1)} %get-tuple-element.69), channel_id=1, source_target_pairs={{0,4},{1,5},{2,6},{3,7},{4,0},{5,1},{6,2},{7,3},{8,12},{9,13},{10,... | collective-permute-start | bytes 294920 | tf_op jit(solution)/shard_map/ppermute | solution.py:140
  46.7 4.5 %collective-permute-start.20 = (bf16[2,96,256]{2,1,0:T(8,128)(2,1)S(1)}, bf16[2,96,256]{2,1,0:T(8,128)(2,1)S(1)}, u32[]{:S(2)}, u32[]{:S(2)}) collective-permute-start(bf16[2,96,256]{2,1,0:T(8,128)(2,1)S(1)} %get-tuple-element.71), channel_id=1, source_target_pairs={{0,8},{1,9},{2,10},{3,11},{4,12},{5,13},{6,14},{7,15},{8,0},{9,1},... | collective-permute-start | bytes 294920 | tf_op jit(solution)/shard_map/ppermute | solution.py:140
  48.0 5.5 %collective-permute-start.21 = (bf16[2,96,256]{2,1,0:T(8,128)(2,1)S(1)}, bf16[2,96,256]{2,1,0:T(8,128)(2,1)S(1)}, u32[]{:S(2)}, u32[]{:S(2)}) collective-permute-start(bf16[2,96,256]{2,1,0:T(8,128)(2,1)S(1)} %get-tuple-element.72), channel_id=1, source_target_pairs={{0,12},{1,13},{2,14},{3,15},{4,8},{5,9},{6,10},{7,11},{8,4},{9,5},... | collective-permute-start | bytes 294920 | tf_op jit(solution)/shard_map/ppermute | solution.py:140
  50.3 8.5 %collective-permute-start.14 = (bf16[2,2,96,256]{3,2,1,0:T(8,128)(2,1)S(1)}, bf16[2,2,96,256]{3,2,1,0:T(8,128)(2,1)S(1)}, u32[]{:S(2)}, u32[]{:S(2)}) collective-permute-start(bf16[2,2,96,256]{3,2,1,0:T(8,128)(2,1)S(1)} %get-tuple-element.60), channel_id=1, source_target_pairs={{0,2},{1,3},{2,0},{3,1},{4,6},{5,7},{6,4},{7,5},{8,10},{9,11},{10,... | collective-permute-start | bytes 589832 | tf_op jit(solution)/shard_map/ppermute | solution.py:140
  53.7 6.3 %collective-permute-start.22 = (bf16[2,96,256]{2,1,0:T(8,128)(2,1)S(1)}, bf16[2,96,256]{2,1,0:T(8,128)(2,1)S(1)}, u32[]{:S(2)}, u32[]{:S(2)}) collective-permute-start(bf16[2,96,256]{2,1,0:T(8,128)(2,1)S(1)} %get-tuple-element.73), channel_id=1, source_target_pairs={{0,4},{1,5},{2,6},{3,7},{4,0},{5,1},{6,2},{7,3},{8,12},{9,13},{10,... | collective-permute-start | bytes 294920 | tf_op jit(solution)/shard_map/ppermute | solution.py:140
  55.1 22.3 %collective-permute-start.25 = (bf16[2,96,256]{2,1,0:T(8,128)(2,1)S(1)}, bf16[2,96,256]{2,1,0:T(8,128)(2,1)S(1)}, u32[]{:S(2)}, u32[]{:S(2)}) collective-permute-start(bf16[2,96,256]{2,1,0:T(8,128)(2,1)S(1)} %get-tuple-element.73), channel_id=1, source_target_pairs={{0,12},{1,13},{2,14},{3,15},{4,8},{5,9},{6,10},{7,11},{8,4},{9,5},... | collective-permute-start | bytes 294920 | tf_op jit(solution)/shard_map/ppermute | solution.py:140
  56.8 20.7 %collective-permute-start.24 = (bf16[2,96,256]{2,1,0:T(8,128)(2,1)S(1)}, bf16[2,96,256]{2,1,0:T(8,128)(2,1)S(1)}, u32[]{:S(2)}, u32[]{:S(2)}) collective-permute-start(bf16[2,96,256]{2,1,0:T(8,128)(2,1)S(1)} %get-tuple-element.73), channel_id=1, source_target_pairs={{0,8},{1,9},{2,10},{3,11},{4,12},{5,13},{6,14},{7,15},{8,0},{9,1},... | collective-permute-start | bytes 294920 | tf_op jit(solution)/shard_map/ppermute | solution.py:140
  57.1 34.4 %copy-start = (bf16[1024,1024]{1,0:T(8,128)(2,1)S(1)}, bf16[1024,1024]{1,0:T(8,128)(2,1)}, u32[]{:S(2)}) copy-start(bf16[1024,1024]{1,0:T(8,128)(2,1)} %q_ref.7) | copy-start | bytes 6291460
  57.1 4.9 %collective-permute-start.13 = (bf16[2,96,256]{2,1,0:T(8,128)(2,1)S(1)}, bf16[2,96,256]{2,1,0:T(8,128)(2,1)S(1)}, u32[]{:S(2)}, u32[]{:S(2)}) collective-permute-start(bf16[2,96,256]{2,1,0:T(8,128)(2,1)S(1)} %get-tuple-element.59), channel_id=1, source_target_pairs={{0,4},{1,5},{2,6},{3,7},{4,0},{5,1},{6,2},{7,3},{8,12},{9,13},{10,... | collective-permute-start | bytes 294920 | tf_op jit(solution)/shard_map/ppermute | solution.py:140
  58.9 9.9 %collective-permute-start.15 = (bf16[2,96,256]{2,1,0:T(8,128)(2,1)S(1)}, bf16[2,96,256]{2,1,0:T(8,128)(2,1)S(1)}, u32[]{:S(2)}, u32[]{:S(2)}) collective-permute-start(bf16[2,96,256]{2,1,0:T(8,128)(2,1)S(1)} %get-tuple-element.61), channel_id=1, source_target_pairs={{0,8},{1,9},{2,10},{3,11},{4,12},{5,13},{6,14},{7,15},{8,0},{9,1},... | collective-permute-start | bytes 294920 | tf_op jit(solution)/shard_map/ppermute | solution.py:140
  59.9 8.9 %collective-permute-start.16 = (bf16[2,96,256]{2,1,0:T(8,128)(2,1)S(1)}, bf16[2,96,256]{2,1,0:T(8,128)(2,1)S(1)}, u32[]{:S(2)}, u32[]{:S(2)}) collective-permute-start(bf16[2,96,256]{2,1,0:T(8,128)(2,1)S(1)} %get-tuple-element.62), channel_id=1, source_target_pairs={{0,12},{1,13},{2,14},{3,15},{4,8},{5,9},{6,10},{7,11},{8,4},{9,5},... | collective-permute-start | bytes 294920 | tf_op jit(solution)/shard_map/ppermute | solution.py:140
  61.9 22.9 %collective-permute-start.36 = (bf16[2,2,96,256]{3,2,1,0:T(8,128)(2,1)S(1)}, bf16[2,2,96,256]{3,2,1,0:T(8,128)(2,1)S(1)}, u32[]{:S(2)}, u32[]{:S(2)}) collective-permute-start(bf16[2,2,96,256]{3,2,1,0:T(8,128)(2,1)S(1)} %pad_maximum_fusion.2.near_low), channel_id=1, source_target_pairs={{0,2},{1,3},{2,0},{3,1},{4,6},{5,7},{6,4},{7,5},{8,10},{9,11},{10,... | collective-permute-start | bytes 589832 | tf_op jit(solution)/shard_map/ppermute | solution.py:140
  68.9 9.4 %collective-permute-start.23 = (bf16[2,96,256]{2,1,0:T(8,128)(2,1)S(1)}, bf16[2,96,256]{2,1,0:T(8,128)(2,1)S(1)}, u32[]{:S(2)}, u32[]{:S(2)}) collective-permute-start(bf16[2,96,256]{2,1,0:T(8,128)(2,1)S(1)} %get-tuple-element.76), channel_id=1, source_target_pairs={{0,4},{1,5},{2,6},{3,7},{4,0},{5,1},{6,2},{7,3},{8,12},{9,13},{10,... | collective-permute-start | bytes 294920 | tf_op jit(solution)/shard_map/ppermute | solution.py:140
  72.5 7.9 %collective-permute-start.29 = (f32[2,96,256]{2,1,0:T(8,128)S(1)}, f32[2,96,256]{2,1,0:T(8,128)S(1)}, u32[]{:S(2)}, u32[]{:S(2)}) collective-permute-start(f32[2,96,256]{2,1,0:T(8,128)S(1)} %pad_maximum_fusion.6), channel_id=1, source_target_pairs={{0,1},{1,0},{2,3},{3,2},{4,5},{5,4},{6,7},{7,6},{8,9},{9,8},{10,11... | collective-permute-start | bytes 589832 | tf_op jit(solution)/shard_map/ppermute | solution.py:140
  77.5 7.4 %collective-permute-start.38 = (bf16[2,2,96,256]{3,2,1,0:T(8,128)(2,1)S(1)}, bf16[2,2,96,256]{3,2,1,0:T(8,128)(2,1)S(1)}, u32[]{:S(2)}, u32[]{:S(2)}) collective-permute-start(bf16[2,2,96,256]{3,2,1,0:T(8,128)(2,1)S(1)} %pad_maximum_fusion.4.near_high), channel_id=1, source_target_pairs={{0,2},{1,3},{2,0},{3,1},{4,6},{5,7},{6,4},{7,5},{8,10},{9,11},{10,... | collective-permute-start | bytes 589832 | tf_op jit(solution)/shard_map/ppermute | solution.py:140
  78.3 7.3 %collective-permute-start.28 = (bf16[2,96,256]{2,1,0:T(8,128)(2,1)S(1)}, bf16[2,96,256]{2,1,0:T(8,128)(2,1)S(1)}, u32[]{:S(2)}, u32[]{:S(2)}) collective-permute-start(bf16[2,96,256]{2,1,0:T(8,128)(2,1)S(1)} %get-tuple-element.76), channel_id=1, source_target_pairs={{0,12},{1,13},{2,14},{3,15},{4,8},{5,9},{6,10},{7,11},{8,4},{9,5},... | collective-permute-start | bytes 294920 | tf_op jit(solution)/shard_map/ppermute | solution.py:140
  80.4 8.5 %collective-permute-start.27 = (bf16[2,96,256]{2,1,0:T(8,128)(2,1)S(1)}, bf16[2,96,256]{2,1,0:T(8,128)(2,1)S(1)}, u32[]{:S(2)}, u32[]{:S(2)}) collective-permute-start(bf16[2,96,256]{2,1,0:T(8,128)(2,1)S(1)} %get-tuple-element.76), channel_id=1, source_target_pairs={{0,8},{1,9},{2,10},{3,11},{4,12},{5,13},{6,14},{7,15},{8,0},{9,1},... | collective-permute-start | bytes 294920 | tf_op jit(solution)/shard_map/ppermute | solution.py:140
  80.4 10.3 %collective-permute-start.34 = (bf16[2,2,96,256]{3,2,1,0:T(8,128)(2,1)S(1)}, bf16[2,2,96,256]{3,2,1,0:T(8,128)(2,1)S(1)}, u32[]{:S(2)}, u32[]{:S(2)}) collective-permute-start(bf16[2,2,96,256]{3,2,1,0:T(8,128)(2,1)S(1)} %pad_maximum_fusion.2.near_low), channel_id=1, source_target_pairs={{0,1},{1,0},{2,3},{3,2},{4,5},{5,4},{6,7},{7,6},{8,9},{9,8},{10,11... | collective-permute-start | bytes 589832 | tf_op jit(solution)/shard_map/ppermute | solution.py:140
  84.8 9.1 %collective-permute-start.35 = (bf16[2,2,96,256]{3,2,1,0:T(8,128)(2,1)S(1)}, bf16[2,2,96,256]{3,2,1,0:T(8,128)(2,1)S(1)}, u32[]{:S(2)}, u32[]{:S(2)}) collective-permute-start(bf16[2,2,96,256]{3,2,1,0:T(8,128)(2,1)S(1)} %pad_maximum_fusion.4.near_high), channel_id=1, source_target_pairs={{0,1},{1,0},{2,3},{3,2},{4,5},{5,4},{6,7},{7,6},{8,9},{9,8},{10,11... | collective-permute-start | bytes 589832 | tf_op jit(solution)/shard_map/ppermute | solution.py:140
  84.9 9.5 %collective-permute-start.31 = (bf16[2,2,96,256]{3,2,1,0:T(8,128)(2,1)S(1)}, bf16[2,2,96,256]{3,2,1,0:T(8,128)(2,1)S(1)}, u32[]{:S(2)}, u32[]{:S(2)}) collective-permute-start(bf16[2,2,96,256]{3,2,1,0:T(8,128)(2,1)S(1)} %pad_maximum_fusion.3.near_low), channel_id=1, source_target_pairs={{0,2},{1,3},{2,0},{3,1},{4,6},{5,7},{6,4},{7,5},{8,10},{9,11},{10,... | collective-permute-start | bytes 589832 | tf_op jit(solution)/shard_map/ppermute | solution.py:140
  85.7 8.9 %collective-permute-start.37 = (bf16[2,2,96,256]{3,2,1,0:T(8,128)(2,1)S(1)}, bf16[2,2,96,256]{3,2,1,0:T(8,128)(2,1)S(1)}, u32[]{:S(2)}, u32[]{:S(2)}) collective-permute-start(bf16[2,2,96,256]{3,2,1,0:T(8,128)(2,1)S(1)} %collective-permute-done.36.far_low), channel_id=1, source_target_pairs={{0,1},{1,0},{2,3},{3,2},{4,5},{5,4},{6,7},{7,6},{8,9},{9,8},{10,11... | collective-permute-start | bytes 589832 | tf_op jit(solution)/shard_map/ppermute | solution.py:140
  88.9 6.0 %collective-permute-start.39 = (bf16[2,2,96,256]{3,2,1,0:T(8,128)(2,1)S(1)}, bf16[2,2,96,256]{3,2,1,0:T(8,128)(2,1)S(1)}, u32[]{:S(2)}, u32[]{:S(2)}) collective-permute-start(bf16[2,2,96,256]{3,2,1,0:T(8,128)(2,1)S(1)} %collective-permute-done.38.far_high), channel_id=1, source_target_pairs={{0,1},{1,0},{2,3},{3,2},{4,5},{5,4},{6,7},{7,6},{8,9},{9,8},{10,11... | collective-permute-start | bytes 589832 | tf_op jit(solution)/shard_map/ppermute | solution.py:140
  90.7 6.7 %collective-permute-start.33 = (bf16[2,2,96,256]{3,2,1,0:T(8,128)(2,1)S(1)}, bf16[2,2,96,256]{3,2,1,0:T(8,128)(2,1)S(1)}, u32[]{:S(2)}, u32[]{:S(2)}) collective-permute-start(bf16[2,2,96,256]{3,2,1,0:T(8,128)(2,1)S(1)} %pad_maximum_fusion.5.near_high), channel_id=1, source_target_pairs={{0,2},{1,3},{2,0},{3,1},{4,6},{5,7},{6,4},{7,5},{8,10},{9,11},{10,... | collective-permute-start | bytes 589832 | tf_op jit(solution)/shard_map/ppermute | solution.py:140
  94.0 6.6 %collective-permute-start.26 = (bf16[2,2,96,256]{3,2,1,0:T(8,128)(2,1)S(1)}, bf16[2,2,96,256]{3,2,1,0:T(8,128)(2,1)S(1)}, u32[]{:S(2)}, u32[]{:S(2)}) collective-permute-start(bf16[2,2,96,256]{3,2,1,0:T(8,128)(2,1)S(1)} %pad_maximum_fusion.3.near_low), channel_id=1, source_target_pairs={{0,1},{1,0},{2,3},{3,2},{4,5},{5,4},{6,7},{7,6},{8,9},{9,8},{10,11... | collective-permute-start | bytes 589832 | tf_op jit(solution)/shard_map/ppermute | solution.py:140
  94.3 6.2 %collective-permute-start.30 = (bf16[2,2,96,256]{3,2,1,0:T(8,128)(2,1)S(1)}, bf16[2,2,96,256]{3,2,1,0:T(8,128)(2,1)S(1)}, u32[]{:S(2)}, u32[]{:S(2)}) collective-permute-start(bf16[2,2,96,256]{3,2,1,0:T(8,128)(2,1)S(1)} %pad_maximum_fusion.5.near_high), channel_id=1, source_target_pairs={{0,1},{1,0},{2,3},{3,2},{4,5},{5,4},{6,7},{7,6},{8,9},{9,8},{10,11... | collective-permute-start | bytes 589832 | tf_op jit(solution)/shard_map/ppermute | solution.py:140
  94.6 6.0 %collective-permute-start.32 = (bf16[2,2,96,256]{3,2,1,0:T(8,128)(2,1)S(1)}, bf16[2,2,96,256]{3,2,1,0:T(8,128)(2,1)S(1)}, u32[]{:S(2)}, u32[]{:S(2)}) collective-permute-start(bf16[2,2,96,256]{3,2,1,0:T(8,128)(2,1)S(1)} %collective-permute-done.31.far_low), channel_id=1, source_target_pairs={{0,1},{1,0},{2,3},{3,2},{4,5},{5,4},{6,7},{7,6},{8,9},{9,8},{10,11... | collective-permute-start | bytes 589832 | tf_op jit(solution)/shard_map/ppermute | solution.py:140
  97.4 3.2 %collective-permute-start.40 = (bf16[2,2,96,256]{3,2,1,0:T(8,128)(2,1)S(1)}, bf16[2,2,96,256]{3,2,1,0:T(8,128)(2,1)S(1)}, u32[]{:S(2)}, u32[]{:S(2)}) collective-permute-start(bf16[2,2,96,256]{3,2,1,0:T(8,128)(2,1)S(1)} %collective-permute-done.33.far_high), channel_id=1, source_target_pairs={{0,1},{1,0},{2,3},{3,2},{4,5},{5,4},{6,7},{7,6},{8,9},{9,8},{10,11... | collective-permute-start | bytes 589832 | tf_op jit(solution)/shard_map/ppermute | solution.py:140

commit v10 on v9

--- a/solution.py
+++ b/solution.py
@@ -283,8 +283,9 @@
     rows_in = w_in.shape[0] // 16
     rows_out = w_out.shape[0] // 16
     in_root = 1.0 / math.sqrt(size)
+    slots = [line.at[index] for line in lines for index in range(line.shape[0])]
     for side, slot, source, place in places(chip, core):
-        ref = lines[2 * side + slot // 2].at[slot % 2]
+        ref = slots[4 * side + slot]
         into = pl.ds(pl.multiple_of(place * rows_in, rows_in), rows_in)
         for block in range(blocks):
             factor = in_root * (0.5 if block < blocks // 2 else 1.0)
@@ -475,11 +476,11 @@
     )(master, kept, one, two, three)
 
 
-def apply_kernel(order, other, ids, near_low, near_high, far_low, far_high, q_ref, *rest):
+def apply_kernel(order, other, count, ids, *rest):
+    lines, q_ref = rest[:count], rest[count]
     o_hbm, w_in, w_out, o_ref, sent = rest[-5:]
     chip, core = ids[0], ids[1]
     fast, size = w_out.shape
-    lines = (near_low, near_high, far_low, far_high)
     assemble(chip, jnp.bitwise_xor(core, other), lines, w_in, w_out)
     columns = pl.ds(pl.multiple_of(head_of(ids, order, other) * size, size), size)
     out_root = 1.0 / math.sqrt(fast)
@@ -507,14 +508,14 @@
     size = lines[0].shape[-1]
     inside = pl.BlockSpec(memory_space=pltpu.VMEM)
     operands = [ids, *lines, queries]
-    specs = [inside] * 5
+    specs = [inside] * (len(lines) + 1)
     aliases = {}
     if output is not None:
         operands.append(output)
         specs.append(pl.BlockSpec(memory_space=pl.ANY))
-        aliases = {6: 0}
-    return pl.pallas_call(
-        functools.partial(apply_kernel, order, other),
+        aliases = {len(lines) + 2: 0}
+    return pl.pallas_call(
+        functools.partial(apply_kernel, order, other, len(lines)),
         grid_spec=pltpu.PrefetchScalarGridSpec(
             num_scalar_prefetch=1,
             grid=(1,),
@@ -587,34 +588,38 @@
     first = (near_low, near_high, far_low, far_high)
     second = (other_near_low, *(swap_parts(piece) for piece in first[1:]))
 
+    kept_one, low_one, high_one = increments(
+        after(ids, second[2]), 0, first, k_own, v_own, k_got, v_got, fast
+    )
+    kept_two, low_two, high_two = increments(ids, 1, second, k_own, v_own, k_got, v_got, fast)
+    low_one, high_one = after((swap(low_one, 2), swap(high_one, 2)), kept_two)
+    low_two, high_two = swap(low_two, 2), swap(high_two, 2)
     wide, short = [], []
-    for order in range(2):
-        lines = second if order else first
-        later = ids if order else after(ids, second[2])
-        kept, low, high = increments(later, order, lines, k_own, v_own, k_got, v_got, fast)
-        high, low = swap(high, 2), swap(low, 2)
+    for order, (kept, low, high) in enumerate(
+        ((kept_one, low_one, high_one), (kept_two, low_two, high_two))
+    ):
         sum2, sum3 = add_pair(kept, high, 1, BF16)
         sum0, sum1 = add_pair(kept, low, 0, F32)
+        sums = (sum1, sum2, sum3)
         three, two, one = swap(sum3, 12), swap(sum2, 8), swap(sum1, 4)
         a, b = renorm(masters[order], sum0, one, two, three, rows_in)
         wide.append(a)
         short.append(b)
 
-    z1, z3, z2 = swap(short[0], 4), swap(short[0], 12), swap(short[0], 8)
-    near_low, near_high = jnp.stack([short[0], z1]), jnp.stack([z2, z3])
-    far_low, far_high = swap(near_low, 2), swap(near_high, 2)
-    second = after(short[1], near_low)
-    z1 = swap(second, 4)
-    second_low = after(jnp.stack([second, z1]), near_high)
-    later = after(short[1], second_low)
-    z3, z2 = swap(later, 12), swap(later, 8)
-    second_high = jnp.stack([z2, z3])
-    mine = (near_low, near_high, far_low, far_high)
+    shard = after(short[0], low_two, high_two)
+    z1, z3, z2 = swap(shard, 4), swap(shard, 12), swap(shard, 8)
+    near = after(jnp.stack([shard, z1, z2, z3]), short[1])
+    far = swap(near, 2)
+    second = short[1]
+    z1, z3, z2 = swap(second, 4), swap(second, 12), swap(second, 8)
+    second_low, second_high = jnp.stack([second, z1]), jnp.stack([z2, z3])
+    mine = (near, far)
     others = tuple(swap(piece, 1) for piece in mine)
     output = apply_fast(ids, 0, 0, mine, queries, None, fast)
     came = swap(jnp.stack([wide[0][1], wide[1][1]]), 1)
     updated = finish(ids, wide[0], wide[1], came, fast_in, fast_out)
-    near_low, near_high = second_low, after(second_high, *updated)
+    near_low, near_high = second_low, second_high
+    output = after(output, *updated)
     output = apply_fast(ids, 0, 1, others, queries, output, fast)
     far_low, far_high = swap(near_low, 2), swap(near_high, 2)
     far_high = after(far_high, output)

time: 103 us -> 107 us (1.039)
  starting transfers between devices: 47.5 us -> 53.3 us
  waiting for transfers between devices: 23.3 us -> 21.3 us
    ppermute x37 -> x34, starting transfers between devices: 44.4 us -> 50.2 us  [swap(): lax.ppermute(value, 'tok', [(place, place ^ bits) for place in range(coun...]
    ppermute x37 -> x34, waiting for transfers between devices: 20.1 us -> 18.2 us  [swap(): lax.ppermute(value, 'tok', [(place, place ^ bits) for place in range(coun...]
  transfers between devices with their start and end apart: 41 -> 38, of which waited for: 11 -> 15; matrix products, arithmetic and copies ran while one was open for 0% -> 0% of each run, Pallas kernels for 22% -> 21%
where the time goes in v10:
time: 107 us
  starting transfers between devices  53.3 us (50%)
  Pallas kernels  27.8 us (26%)
  waiting for transfers between devices  21.3 us (20%)
  local copies, waits for them, and re-layouts  3.47 us (3%)
  between operations  1.09 us (1%)
    ppermute x34, starting transfers between devices, swap(): lax.ppermute(value, 'tok', [(place, place ^ bits) for place in range(coun...  50.2 us
    ppermute x34, waiting for transfers between devices, swap(): lax.ppermute(value, 'tok', [(place, place ^ bits) for place in range(coun...  18.2 us
    pallas_call x2, Pallas kernels, increments(): pl.pallas_call(increments_kernel, grid_spec=pltpu.PrefetchScalarGridSpec(...  11.4 us
    pallas_call x4, Pallas kernels, apply_fast(): pl.pallas_call(functools.partial(apply_kernel, order, other, len(lines)),...  9.97 us
    pallas_call x2, Pallas kernels, prepare(): pl.pallas_call(functools.partial(prepare_kernel, heads, block_root), grid...  3.78 us
    unnamed x12, local copies, waits for them, and re-layouts  3.45 us
    ppermute x4, waiting for transfers between devices, swap_parts(): return lax.ppermute(value, 'parts', [(0, 1), (1, 0)])  3.19 us
    ppermute x4, starting transfers between devices, swap_parts(): return lax.ppermute(value, 'parts', [(0, 1), (1, 0)])  3.06 us
  transfers between devices with their start and end apart: 38, of which 15 were waited for; matrix products, arithmetic and copies ran while one was open for 0% of the time, Pallas kernels for 21%

profile of v10, /device:TPU:1, one launch (start us, length us, event | category | flops | bytes accessed | tf_op | source)
XLA Modules:
  0.0 107.1 jit_solution(5112226306608070725)
XLA Ops:
  0.7 0.1 pad_add_fusion.ids
  0.7 1.6 %copy-done.1 = bf16[1024,1024]{1,0:T(8,128)(2,1)S(1)} copy-done((bf16[1024,1024]{1,0:T(8,128)(2,1)S(1)}, bf16[1024,1024]{1,0:T(8,128)(2,1)}, u32[]{:S(2)}) %copy-start.1) | copy-done | bytes 2097176
  2.3 1.5 %keys.1 = (bf16[1024,512]{1,0:T(8,128)(2,1)S(1)}, bf16[1024,512]{1,0:T(8,128)(2,1)S(1)}) custom-call(s32[3]{0:T(128)S(1)} %pad_add_fusion.ids, bf16[1024,1024]{1,0:T(8,128)(2,1)S(1)} %copy-done.1), custom_call_target="tpu_custom_call" | custom-call | flops 5242880 | bytes 4194304 | tf_op jit(solution)/shard_map/keys/pallas_call | solution.py:255
  3.9 0.9 copy-done.3
  4.8 0.9 copy-done.4
  5.7 0.8 pack.1
  6.5 0.1 collective-permute-start
  6.6 0.5 collective-permute-start.2
  7.1 0.9 collective-permute-done.got
  8.0 2.3 %values.1 = (bf16[1024,512]{1,0:T(8,128)(2,1)S(1)}, bf16[1024,512]{1,0:T(8,128)(2,1)S(1)}) custom-call(s32[3]{0:T(128)S(1)} %pad_add_fusion.ids, bf16[1024,1024]{1,0:T(8,128)(2,1)S(1)} %copy-done.2, f32[4,1024]{1,0:T(4,128)S(1)} %copy-done.5), custom_call_target="tpu_custom_call" | custom-call | flops 5242880 | bytes 4194304 | tf_op jit(solution)/shard_map/values/pallas_call | solution.py:255
  10.3 0.2 collective-permute-start.3
  10.5 2.7 %collective-permute-start.1 = (bf16[2,96,256]{2,1,0:T(8,128)(2,1)S(1)}, bf16[2,96,256]{2,1,0:T(8,128)(2,1)S(1)}, u32[]{:S(2)}, u32[]{:S(2)}) collective-permute-start(bf16[2,96,256]{2,1,0:T(8,128)(2,1)S(1)} %get-tuple-element.53), channel_id=1, source_target_pairs={{0,4},{1,5},{2,6},{3,7},{4,0},{5,1},{6,2},{7,3},{8,12},{9,13},{10,... | collective-permute-start | bytes 294920 | tf_op jit(solution)/shard_map/ppermute | solution.py:140
  13.3 2.2 %collective-permute-start.6 = (bf16[2,96,256]{2,1,0:T(8,128)(2,1)S(1)}, bf16[2,96,256]{2,1,0:T(8,128)(2,1)S(1)}, u32[]{:S(2)}, u32[]{:S(2)}) collective-permute-start(bf16[2,96,256]{2,1,0:T(8,128)(2,1)S(1)} %get-tuple-element.53), channel_id=1, source_target_pairs={{0,12},{1,13},{2,14},{3,15},{4,8},{5,9},{6,10},{7,11},{8,4},{9,5},... | collective-permute-start | bytes 294920 | tf_op jit(solution)/shard_map/ppermute | solution.py:140
  15.4 0.1 collective-permute-start.5
  15.6 0.7 collective-permute-done.1
  16.3 1.2 %collective-permute-start.7 = (bf16[2,2,96,256]{3,2,1,0:T(8,128)(2,1)S(1)}, bf16[2,2,96,256]{3,2,1,0:T(8,128)(2,1)S(1)}, u32[]{:S(2)}, u32[]{:S(2)}) collective-permute-start(bf16[2,2,96,256]{3,2,1,0:T(8,128)(2,1)S(1)} %pad_maximum_fusion.1.near_low), channel_id=1, source_target_pairs={{0,2},{1,3},{2,0},{3,1},{4,6},{5,7},{6,4},{7,5},{8,10},{9,11},{10,... | collective-permute-start | bytes 589832 | tf_op jit(solution)/shard_map/ppermute | solution.py:140
  17.6 1.2 %collective-permute-start.4 = (bf16[2,2,96,256]{3,2,1,0:T(8,128)(2,1)S(1)}, bf16[2,2,96,256]{3,2,1,0:T(8,128)(2,1)S(1)}, u32[]{:S(2)}, u32[]{:S(2)}) collective-permute-start(bf16[2,2,96,256]{3,2,1,0:T(8,128)(2,1)S(1)} %pad_maximum_fusion.1.near_low), channel_id=1, source_target_pairs={{0,16},{16,0},{1,17},{17,1},{2,18},{18,2},{3,19},{19,3},{4,20},{20... | collective-permute-start | bytes 589832 | tf_op jit(solution)/shard_map/ppermute | solution.py:144
  18.8 1.6 %collective-permute-done.6 = bf16[2,96,256]{2,1,0:T(8,128)(2,1)S(1)} collective-permute-done((bf16[2,96,256]{2,1,0:T(8,128)(2,1)S(1)}, bf16[2,96,256]{2,1,0:T(8,128)(2,1)S(1)}, u32[]{:S(2)}, u32[]{:S(2)}) %collective-permute-start.6) | collective-permute-done | bytes 98336 | tf_op jit(solution)/shard_map/ppermute | solution.py:140
  20.4 4.6 %collective-permute-done.5 = bf16[2,96,256]{2,1,0:T(8,128)(2,1)S(1)} collective-permute-done((bf16[2,96,256]{2,1,0:T(8,128)(2,1)S(1)}, bf16[2,96,256]{2,1,0:T(8,128)(2,1)S(1)}, u32[]{:S(2)}, u32[]{:S(2)}) %collective-permute-start.5) | collective-permute-done | bytes 98336 | tf_op jit(solution)/shard_map/ppermute | solution.py:140
  25.1 1.3 %collective-permute-start.9 = (bf16[2,2,96,256]{3,2,1,0:T(8,128)(2,1)S(1)}, bf16[2,2,96,256]{3,2,1,0:T(8,128)(2,1)S(1)}, u32[]{:S(2)}, u32[]{:S(2)}) collective-permute-start(bf16[2,2,96,256]{3,2,1,0:T(8,128)(2,1)S(1)} %collective-permute-done.7.far_low), channel_id=1, source_target_pairs={{0,16},{16,0},{1,17},{17,1},{2,18},{18,2},{3,19},{19,3},{4,20},{20... | collective-permute-start | bytes 589832 | tf_op jit(solution)/shard_map/ppermute | solution.py:144
  26.3 1.2 %collective-permute-start.10 = (bf16[2,2,96,256]{3,2,1,0:T(8,128)(2,1)S(1)}, bf16[2,2,96,256]{3,2,1,0:T(8,128)(2,1)S(1)}, u32[]{:S(2)}, u32[]{:S(2)}) collective-permute-start(bf16[2,2,96,256]{3,2,1,0:T(8,128)(2,1)S(1)} %pad_maximum_fusion.2.near_high), channel_id=1, source_target_pairs={{0,2},{1,3},{2,0},{3,1},{4,6},{5,7},{6,4},{7,5},{8,10},{9,11},{10,... | collective-permute-start | bytes 589832 | tf_op jit(solution)/shard_map/ppermute | solution.py:140
  27.6 0.3 collective-permute-start.8
  27.8 3.1 %collective-permute-done.9.far_low = bf16[2,2,96,256]{3,2,1,0:T(8,128)(2,1)S(1)} collective-permute-done((bf16[2,2,96,256]{3,2,1,0:T(8,128)(2,1)S(1)}, bf16[2,2,96,256]{3,2,1,0:T(8,128)(2,1)S(1)}, u32[]{:S(2)}, u32[]{:S(2)}) %collective-permute-start.9) | collective-permute-done | bytes 196640 | tf_op jit(solution)/shard_map/ppermute | solution.py:144
  31.0 0.9 collective-permute-done.10.far_high
  31.9 0.3 collective-permute-start.11
  32.2 5.6 %increments.3 = (f32[4,2,96,256]{3,2,1,0:T(8,128)S(1)}, bf16[2,2,96,256]{3,2,1,0:T(8,128)(2,1)S(1)}, bf16[2,2,96,256]{3,2,1,0:T(8,128)(2,1)S(1)}) custom-call(s32[3]{0:T(128)S(1)} %pad_add_fusion.ids, bf16[2,2,96,256]{3,2,1,0:T(8,128)(2,1)S(1)} %pad_maximum_fusion.1.near_low, bf16[2,2,96,256]{3,2,1,0:T(8,128)(2,1)S(1)} %pad_maximum_fusion.2.near_high, ...), custom_call_target="tpu_custom_call" | custom-call | flops 3221225472 | bytes 2097152 | tf_op jit(solution)/shard_map/increments/pallas_call | solution.py:390
  37.8 1.3 %collective-permute-start.25 = (bf16[2,2,96,256]{3,2,1,0:T(8,128)(2,1)S(1)}, bf16[2,2,96,256]{3,2,1,0:T(8,128)(2,1)S(1)}, u32[]{:S(2)}, u32[]{:S(2)}) collective-permute-start(bf16[2,2,96,256]{3,2,1,0:T(8,128)(2,1)S(1)} %get-tuple-element.68), channel_id=1, source_target_pairs={{0,2},{1,3},{2,0},{3,1},{4,6},{5,7},{6,4},{7,5},{8,10},{9,11},{10,... | collective-permute-start | bytes 589832 | tf_op jit(solution)/shard_map/ppermute | solution.py:140
  39.2 0.2 collective-permute-start.26
  39.4 5.8 %increments.2 = (f32[4,2,96,256]{3,2,1,0:T(8,128)S(1)}, bf16[2,2,96,256]{3,2,1,0:T(8,128)(2,1)S(1)}, bf16[2,2,96,256]{3,2,1,0:T(8,128)(2,1)S(1)}) custom-call(s32[3]{0:T(128)S(1)} %pad_add_fusion.ids, bf16[2,2,96,256]{3,2,1,0:T(8,128)(2,1)S(1)} %collective-permute-done.4.near_low, bf16[2,2,96,256]{3,2,1,0:T(8,128)(2,1)S(1)} %collective-permute-done.8.near_high, ...), custom_call_target="tpu_custom_call" | custom-call | flops 3221225472 | bytes 2097152 | tf_op jit(solution)/shard_map/increments/pallas_call | solution.py:390
  45.2 1.3 %collective-permute-start.12 = (bf16[2,2,96,256]{3,2,1,0:T(8,128)(2,1)S(1)}, bf16[2,2,96,256]{3,2,1,0:T(8,128)(2,1)S(1)}, u32[]{:S(2)}, u32[]{:S(2)}) collective-permute-start(bf16[2,2,96,256]{3,2,1,0:T(8,128)(2,1)S(1)} %get-tuple-element.58), channel_id=1, source_target_pairs={{0,2},{1,3},{2,0},{3,1},{4,6},{5,7},{6,4},{7,5},{8,10},{9,11},{10,... | collective-permute-start | bytes 589832 | tf_op jit(solution)/shard_map/ppermute | solution.py:140
  46.5 0.2 collective-permute-start.14
  46.9 1.3 %collective-permute-start.28 = (bf16[2,96,256]{2,1,0:T(8,128)(2,1)S(1)}, bf16[2,96,256]{2,1,0:T(8,128)(2,1)S(1)}, u32[]{:S(2)}, u32[]{:S(2)}) collective-permute-start(bf16[2,96,256]{2,1,0:T(8,128)(2,1)S(1)} %get-tuple-element.74), channel_id=1, source_target_pairs={{0,8},{1,9},{2,10},{3,11},{4,12},{5,13},{6,14},{7,15},{8,0},{9,1},... | collective-permute-start | bytes 294920 | tf_op jit(solution)/shard_map/ppermute | solution.py:140
  48.2 2.3 %collective-permute-start.29 = (bf16[2,96,256]{2,1,0:T(8,128)(2,1)S(1)}, bf16[2,96,256]{2,1,0:T(8,128)(2,1)S(1)}, u32[]{:S(2)}, u32[]{:S(2)}) collective-permute-start(bf16[2,96,256]{2,1,0:T(8,128)(2,1)S(1)} %get-tuple-element.75), channel_id=1, source_target_pairs={{0,12},{1,13},{2,14},{3,15},{4,8},{5,9},{6,10},{7,11},{8,4},{9,5},... | collective-permute-start | bytes 294920 | tf_op jit(solution)/shard_map/ppermute | solution.py:140
  50.5 1.0 collective-permute-done.28.two
  51.4 2.2 %collective-permute-done.29.three = bf16[2,96,256]{2,1,0:T(8,128)(2,1)S(1)} collective-permute-done((bf16[2,96,256]{2,1,0:T(8,128)(2,1)S(1)}, bf16[2,96,256]{2,1,0:T(8,128)(2,1)S(1)}, u32[]{:S(2)}, u32[]{:S(2)}) %collective-permute-start.29) | collective-permute-done | bytes 98336 | tf_op jit(solution)/shard_map/ppermute | solution.py:140
  53.6 0.1 renorm.3
  53.8 0.8 collective-permute-done.14.came
  54.6 1.9 %collective-permute-start.32 = (bf16[2,96,256]{2,1,0:T(8,128)(2,1)S(1)}, bf16[2,96,256]{2,1,0:T(8,128)(2,1)S(1)}, u32[]{:S(2)}, u32[]{:S(2)}) collective-permute-start(bf16[2,96,256]{2,1,0:T(8,128)(2,1)S(1)} %get-tuple-element.77), channel_id=1, source_target_pairs={{0,12},{1,13},{2,14},{3,15},{4,8},{5,9},{6,10},{7,11},{8,4},{9,5},... | collective-permute-start | bytes 294920 | tf_op jit(solution)/shard_map/ppermute | solution.py:140
  56.5 1.6 %collective-permute-start.30 = (bf16[2,96,256]{2,1,0:T(8,128)(2,1)S(1)}, bf16[2,96,256]{2,1,0:T(8,128)(2,1)S(1)}, u32[]{:S(2)}, u32[]{:S(2)}) collective-permute-start(bf16[2,96,256]{2,1,0:T(8,128)(2,1)S(1)} %get-tuple-element.77), channel_id=1, source_target_pairs={{0,4},{1,5},{2,6},{3,7},{4,0},{5,1},{6,2},{7,3},{8,12},{9,13},{10,... | collective-permute-start | bytes 294920 | tf_op jit(solution)/shard_map/ppermute | solution.py:140
  58.2 0.8 collective-permute-start.15
  59.0 1.4 %collective-permute-start.16 = (bf16[2,96,256]{2,1,0:T(8,128)(2,1)S(1)}, bf16[2,96,256]{2,1,0:T(8,128)(2,1)S(1)}, u32[]{:S(2)}, u32[]{:S(2)}) collective-permute-start(bf16[2,96,256]{2,1,0:T(8,128)(2,1)S(1)} %get-tuple-element.63), channel_id=1, source_target_pairs={{0,12},{1,13},{2,14},{3,15},{4,8},{5,9},{6,10},{7,11},{8,4},{9,5},... | collective-permute-start | bytes 294920 | tf_op jit(solution)/shard_map/ppermute | solution.py:140
  60.4 0.7 collective-permute-done.32
  61.1 4.0 %collective-permute-start.13 = (bf16[2,96,256]{2,1,0:T(8,128)(2,1)S(1)}, bf16[2,96,256]{2,1,0:T(8,128)(2,1)S(1)}, u32[]{:S(2)}, u32[]{:S(2)}) collective-permute-start(bf16[2,96,256]{2,1,0:T(8,128)(2,1)S(1)} %get-tuple-element.60), channel_id=1, source_target_pairs={{0,4},{1,5},{2,6},{3,7},{4,0},{5,1},{6,2},{7,3},{8,12},{9,13},{10,... | collective-permute-start | bytes 294920 | tf_op jit(solution)/shard_map/ppermute | solution.py:140
  65.2 0.4 collective-permute-done.31
  65.6 1.3 %collective-permute-done.15.two = bf16[2,96,256]{2,1,0:T(8,128)(2,1)S(1)} collective-permute-done((bf16[2,96,256]{2,1,0:T(8,128)(2,1)S(1)}, bf16[2,96,256]{2,1,0:T(8,128)(2,1)S(1)}, u32[]{:S(2)}, u32[]{:S(2)}) %collective-permute-start.15) | collective-permute-done | bytes 98336 | tf_op jit(solution)/shard_map/ppermute | solution.py:140
  66.9 1.8 %collective-permute-done.13.one = bf16[2,96,256]{2,1,0:T(8,128)(2,1)S(1)} collective-permute-done((bf16[2,96,256]{2,1,0:T(8,128)(2,1)S(1)}, bf16[2,96,256]{2,1,0:T(8,128)(2,1)S(1)}, u32[]{:S(2)}, u32[]{:S(2)}) %collective-permute-start.13) | collective-permute-done | bytes 98336 | tf_op jit(solution)/shard_map/ppermute | solution.py:140
  68.7 0.1 renorm.2
  68.9 1.3 %collective-permute-start.34 = (bf16[4,2,96,256]{3,2,1,0:T(8,128)(2,1)S(1)}, bf16[4,2,96,256]{3,2,1,0:T(8,128)(2,1)S(1)}, u32[]{:S(2)}, u32[]{:S(2)}) collective-permute-start(bf16[4,2,96,256]{3,2,1,0:T(8,128)(2,1)S(1)} %pad_maximum_fusion.rest_0_), channel_id=1, source_target_pairs={{0,2},{1,3},{2,0},{3,1},{4,6},{5,7},{6,4},{7,5},{8,10},{9,11},{10,... | collective-permute-start | bytes 1179656 | tf_op jit(solution)/shard_map/ppermute | solution.py:140
  70.2 2.2 %collective-permute-start.20 = (bf16[2,96,256]{2,1,0:T(8,128)(2,1)S(1)}, bf16[2,96,256]{2,1,0:T(8,128)(2,1)S(1)}, u32[]{:S(2)}, u32[]{:S(2)}) collective-permute-start(bf16[2,96,256]{2,1,0:T(8,128)(2,1)S(1)} %get-tuple-element.64), channel_id=1, source_target_pairs={{0,12},{1,13},{2,14},{3,15},{4,8},{5,9},{6,10},{7,11},{8,4},{9,5},... | collective-permute-start | bytes 294920 | tf_op jit(solution)/shard_map/ppermute | solution.py:140
  72.4 1.4 %collective-permute-start.17 = (bf16[2,96,256]{2,1,0:T(8,128)(2,1)S(1)}, bf16[2,96,256]{2,1,0:T(8,128)(2,1)S(1)}, u32[]{:S(2)}, u32[]{:S(2)}) collective-permute-start(bf16[2,96,256]{2,1,0:T(8,128)(2,1)S(1)} %get-tuple-element.64), channel_id=1, source_target_pairs={{0,4},{1,5},{2,6},{3,7},{4,0},{5,1},{6,2},{7,3},{8,12},{9,13},{10,... | collective-permute-start | bytes 294920 | tf_op jit(solution)/shard_map/ppermute | solution.py:140
  73.8 12.0 %collective-permute-start.33 = (bf16[4,2,96,256]{3,2,1,0:T(8,128)(2,1)S(1)}, bf16[4,2,96,256]{3,2,1,0:T(8,128)(2,1)S(1)}, u32[]{:S(2)}, u32[]{:S(2)}) collective-permute-start(bf16[4,2,96,256]{3,2,1,0:T(8,128)(2,1)S(1)} %pad_maximum_fusion.rest_0_), channel_id=1, source_target_pairs={{0,1},{1,0},{2,3},{3,2},{4,5},{5,4},{6,7},{7,6},{8,9},{9,8},{10,11... | collective-permute-start | bytes 1179656 | tf_op jit(solution)/shard_map/ppermute | solution.py:140
  85.8 2.1 %collective-permute-start.35 = (bf16[4,2,96,256]{3,2,1,0:T(8,128)(2,1)S(1)}, bf16[4,2,96,256]{3,2,1,0:T(8,128)(2,1)S(1)}, u32[]{:S(2)}, u32[]{:S(2)}) collective-permute-start(bf16[4,2,96,256]{3,2,1,0:T(8,128)(2,1)S(1)} %collective-permute-done.34.rest_1_), channel_id=1, source_target_pairs={{0,1},{1,0},{2,3},{3,2},{4,5},{5,4},{6,7},{7,6},{8,9},{9,8},{10,11... | collective-permute-start | bytes 1179656 | tf_op jit(solution)/shard_map/ppermute | solution.py:140
  87.9 2.4 %collective-permute-start.36 = (f32[2,96,256]{2,1,0:T(8,128)S(1)}, f32[2,96,256]{2,1,0:T(8,128)S(1)}, u32[]{:S(2)}, u32[]{:S(2)}) collective-permute-start(f32[2,96,256]{2,1,0:T(8,128)S(1)} %pad_maximum_fusion.5), channel_id=1, source_target_pairs={{0,1},{1,0},{2,3},{3,2},{4,5},{5,4},{6,7},{7,6},{8,9},{9,8},{10,11... | collective-permute-start | bytes 589832 | tf_op jit(solution)/shard_map/ppermute | solution.py:140
  90.5 1.5 %collective-permute-start.24 = (bf16[2,2,96,256]{3,2,1,0:T(8,128)(2,1)S(1)}, bf16[2,2,96,256]{3,2,1,0:T(8,128)(2,1)S(1)}, u32[]{:S(2)}, u32[]{:S(2)}) collective-permute-start(bf16[2,2,96,256]{3,2,1,0:T(8,128)(2,1)S(1)} %pad_maximum_fusion.4.rest_1_), channel_id=1, source_target_pairs={{0,2},{1,3},{2,0},{3,1},{4,6},{5,7},{6,4},{7,5},{8,10},{9,11},{10,... | collective-permute-start | bytes 589832 | tf_op jit(solution)/shard_map/ppermute | solution.py:140
  92.0 0.6 collective-permute-start.18
  92.5 1.3 %finish.1 = (f32[4,16,1024]{2,1,0:T(8,128)}, f32[4,32,256]{2,1,0:T(8,128)}) custom-call(s32[3]{0:T(128)S(1)} %pad_add_fusion.ids, f32[2,96,256]{2,1,0:T(8,128)S(1)} %get-tuple-element.79.one, f32[2,96,256]{2,1,0:T(8,128)S(1)} %get-tuple-element.80.two, f32[2,96,256]{2,1,0:T(8,128)S(1)} %collective-permute-done.36.came), custom_call_target="tpu_custom_call" | custom-call | tf_op jit(solution)/shard_map/finish/pallas_call | solution.py:554
  93.9 2.5 %apply.4.rest_3_ = bf16[1024,1024]{1,0:T(8,128)(2,1)} custom-call(s32[3]{0:T(128)S(1)} %pad_add_fusion.ids, bf16[4,2,96,256]{3,2,1,0:T(8,128)(2,1)S(1)} %pad_maximum_fusion.rest_0_, bf16[4,2,96,256]{3,2,1,0:T(8,128)(2,1)S(1)} %collective-permute-done.34.rest_1_, bf16[1024,1024]{1,0:T(8,128)(2,1)S(1)} %copy-done), custom_call_target="tpu_custom_call" | custom-call | flops 805306368 | bytes 1048576 | tf_op jit(solution)/shard_map/apply/pallas_call | solution.py:517
  96.4 0.6 collective-permute-done.22.rest_2_
  97.0 1.2 %collective-permute-start.21 = (bf16[2,2,96,256]{3,2,1,0:T(8,128)(2,1)S(1)}, bf16[2,2,96,256]{3,2,1,0:T(8,128)(2,1)S(1)}, u32[]{:S(2)}, u32[]{:S(2)}) collective-permute-start(bf16[2,2,96,256]{3,2,1,0:T(8,128)(2,1)S(1)} %pad_maximum_fusion.4.rest_1_), channel_id=1, source_target_pairs={{0,1},{1,0},{2,3},{3,2},{4,5},{5,4},{6,7},{7,6},{8,9},{9,8},{10,11... | collective-permute-start | bytes 589832 | tf_op jit(solution)/shard_map/ppermute | solution.py:140
  98.1 2.5 %apply.5.rest_5_ = bf16[1024,1024]{1,0:T(8,128)(2,1)} custom-call(s32[3]{0:T(128)S(1)} %pad_add_fusion.ids, bf16[4,2,96,256]{3,2,1,0:T(8,128)(2,1)S(1)} %collective-permute-done.33.rest_0_, bf16[4,2,96,256]{3,2,1,0:T(8,128)(2,1)S(1)} %collective-permute-done.35.rest_1_, bf16[1024,1024]{1,0:T(8,128)(2,1)S(1)} %copy-done, ...), custom_call_target="tpu_custom_call", output_to_operand_aliasing={{}: (4, {})} | custom-call | flops 805306368 | bytes 1048576 | tf_op jit(solution)/shard_map/apply/pallas_call | solution.py:517
  100.6 0.5 collective-permute-done.24.rest_3_
  101.2 0.8 collective-permute-start.37
  102.0 2.5 %apply.6.rest_5_ = bf16[1024,1024]{1,0:T(8,128)(2,1)} custom-call(s32[3]{0:T(128)S(1)} %pad_add_fusion.ids, bf16[2,2,96,256]{3,2,1,0:T(8,128)(2,1)S(1)} %pad_maximum_fusion.3.rest_0_, bf16[2,2,96,256]{3,2,1,0:T(8,128)(2,1)S(1)} %pad_maximum_fusion.4.rest_1_, ...), custom_call_target="tpu_custom_call", output_to_operand_aliasing={{}: (6, {})} | custom-call | flops 805306368 | bytes 1048576 | tf_op jit(solution)/shard_map/apply/pallas_call | solution.py:517
  104.5 2.5 %apply.7 = bf16[1024,1024]{1,0:T(8,128)(2,1)} custom-call(s32[3]{0:T(128)S(1)} %pad_add_fusion.ids, bf16[2,2,96,256]{3,2,1,0:T(8,128)(2,1)S(1)} %collective-permute-done.18.rest_0_, bf16[2,2,96,256]{3,2,1,0:T(8,128)(2,1)S(1)} %collective-permute-done.21.rest_1_, ...), custom_call_target="tpu_custom_call", output_to_operand_aliasing={{}: (6, {})} | custom-call | flops 805306368 | bytes 1048576 | tf_op jit(solution)/shard_map/apply/pallas_call | solution.py:517
  (50 shorter events, 0.6 us)
Async XLA Ops:
  0.6 7.4 %copy-start.5 = (f32[4,1024]{1,0:T(4,128)S(1)}, f32[4,1024]{1,0:T(4,128)}, u32[]{:S(2)}) copy-start(f32[4,1024]{1,0:T(4,128)} %rest_0_.1) | copy-start | bytes 49156
  0.7 1.6 %copy-start.1 = (bf16[1024,1024]{1,0:T(8,128)(2,1)S(1)}, bf16[1024,1024]{1,0:T(8,128)(2,1)}, u32[]{:S(2)}) copy-start(bf16[1024,1024]{1,0:T(8,128)(2,1)} %x_ref.2) | copy-start | bytes 6291460
  2.3 5.7 %copy-start.2 = (bf16[1024,1024]{1,0:T(8,128)(2,1)S(1)}, bf16[1024,1024]{1,0:T(8,128)(2,1)}, u32[]{:S(2)}) copy-start(bf16[1024,1024]{1,0:T(8,128)(2,1)} %x_ref.3) | copy-start | bytes 6291460
  3.8 1.0 copy-start.3
  4.8 0.9 copy-start.4
  6.5 1.5 %collective-permute-start = (f32[2,96,256]{2,1,0:T(8,128)S(1)}, f32[2,96,256]{2,1,0:T(8,128)S(1)}, u32[]{:S(2)}, u32[]{:S(2)}) collective-permute-start(f32[2,96,256]{2,1,0:T(8,128)S(1)} %get-tuple-element.47), channel_id=1, source_target_pairs={{0,1},{1,0},{2,3},{3,2},{4,5},{5,4},{6,7},{7,6},{8,9},{9,8},{10,11... | collective-permute-start | bytes 589832 | tf_op jit(solution)/shard_map/ppermute | solution.py:140
  6.6 9.7 %collective-permute-start.2 = (bf16[1024,512]{1,0:T(8,128)(2,1)S(1)}, bf16[1024,512]{1,0:T(8,128)(2,1)S(1)}, u32[]{:S(2)}, u32[]{:S(2)}) collective-permute-start(bf16[1024,512]{1,0:T(8,128)(2,1)S(1)} %get-tuple-element.48), channel_id=1, source_target_pairs={{0,1},{1,0},{2,3},{3,2},{4,5},{5,4},{6,7},{7,6},{8,9},{9,8},{10,11... | collective-permute-start | bytes 3145736 | tf_op jit(solution)/shard_map/ppermute | solution.py:140
  10.3 6.0 %collective-permute-start.3 = (bf16[1024,512]{1,0:T(8,128)(2,1)S(1)}, bf16[1024,512]{1,0:T(8,128)(2,1)S(1)}, u32[]{:S(2)}, u32[]{:S(2)}) collective-permute-start(bf16[1024,512]{1,0:T(8,128)(2,1)S(1)} %get-tuple-element.50), channel_id=1, source_target_pairs={{0,1},{1,0},{2,3},{3,2},{4,5},{5,4},{6,7},{7,6},{8,9},{9,8},{10,11... | collective-permute-start | bytes 3145736 | tf_op jit(solution)/shard_map/ppermute | solution.py:140
  10.5 5.8 %collective-permute-start.1 = (bf16[2,96,256]{2,1,0:T(8,128)(2,1)S(1)}, bf16[2,96,256]{2,1,0:T(8,128)(2,1)S(1)}, u32[]{:S(2)}, u32[]{:S(2)}) collective-permute-start(bf16[2,96,256]{2,1,0:T(8,128)(2,1)S(1)} %get-tuple-element.53), channel_id=1, source_target_pairs={{0,4},{1,5},{2,6},{3,7},{4,0},{5,1},{6,2},{7,3},{8,12},{9,13},{10,... | collective-permute-start | bytes 294920 | tf_op jit(solution)/shard_map/ppermute | solution.py:140
  13.3 7.1 %collective-permute-start.6 = (bf16[2,96,256]{2,1,0:T(8,128)(2,1)S(1)}, bf16[2,96,256]{2,1,0:T(8,128)(2,1)S(1)}, u32[]{:S(2)}, u32[]{:S(2)}) collective-permute-start(bf16[2,96,256]{2,1,0:T(8,128)(2,1)S(1)} %get-tuple-element.53), channel_id=1, source_target_pairs={{0,12},{1,13},{2,14},{3,15},{4,8},{5,9},{6,10},{7,11},{8,4},{9,5},... | collective-permute-start | bytes 294920 | tf_op jit(solution)/shard_map/ppermute | solution.py:140
  15.4 9.6 %collective-permute-start.5 = (bf16[2,96,256]{2,1,0:T(8,128)(2,1)S(1)}, bf16[2,96,256]{2,1,0:T(8,128)(2,1)S(1)}, u32[]{:S(2)}, u32[]{:S(2)}) collective-permute-start(bf16[2,96,256]{2,1,0:T(8,128)(2,1)S(1)} %get-tuple-element.53), channel_id=1, source_target_pairs={{0,8},{1,9},{2,10},{3,11},{4,12},{5,13},{6,14},{7,15},{8,0},{9,1},... | collective-permute-start | bytes 294920 | tf_op jit(solution)/shard_map/ppermute | solution.py:140
  16.3 8.7 %collective-permute-start.7 = (bf16[2,2,96,256]{3,2,1,0:T(8,128)(2,1)S(1)}, bf16[2,2,96,256]{3,2,1,0:T(8,128)(2,1)S(1)}, u32[]{:S(2)}, u32[]{:S(2)}) collective-permute-start(bf16[2,2,96,256]{3,2,1,0:T(8,128)(2,1)S(1)} %pad_maximum_fusion.1.near_low), channel_id=1, source_target_pairs={{0,2},{1,3},{2,0},{3,1},{4,6},{5,7},{6,4},{7,5},{8,10},{9,11},{10,... | collective-permute-start | bytes 589832 | tf_op jit(solution)/shard_map/ppermute | solution.py:140
  17.6 8.8 %collective-permute-start.4 = (bf16[2,2,96,256]{3,2,1,0:T(8,128)(2,1)S(1)}, bf16[2,2,96,256]{3,2,1,0:T(8,128)(2,1)S(1)}, u32[]{:S(2)}, u32[]{:S(2)}) collective-permute-start(bf16[2,2,96,256]{3,2,1,0:T(8,128)(2,1)S(1)} %pad_maximum_fusion.1.near_low), channel_id=1, source_target_pairs={{0,16},{16,0},{1,17},{17,1},{2,18},{18,2},{3,19},{19,3},{4,20},{20... | collective-permute-start | bytes 589832 | tf_op jit(solution)/shard_map/ppermute | solution.py:144
  25.1 5.9 %collective-permute-start.9 = (bf16[2,2,96,256]{3,2,1,0:T(8,128)(2,1)S(1)}, bf16[2,2,96,256]{3,2,1,0:T(8,128)(2,1)S(1)}, u32[]{:S(2)}, u32[]{:S(2)}) collective-permute-start(bf16[2,2,96,256]{3,2,1,0:T(8,128)(2,1)S(1)} %collective-permute-done.7.far_low), channel_id=1, source_target_pairs={{0,16},{16,0},{1,17},{17,1},{2,18},{18,2},{3,19},{19,3},{4,20},{20... | collective-permute-start | bytes 589832 | tf_op jit(solution)/shard_map/ppermute | solution.py:144
  26.3 5.5 %collective-permute-start.10 = (bf16[2,2,96,256]{3,2,1,0:T(8,128)(2,1)S(1)}, bf16[2,2,96,256]{3,2,1,0:T(8,128)(2,1)S(1)}, u32[]{:S(2)}, u32[]{:S(2)}) collective-permute-start(bf16[2,2,96,256]{3,2,1,0:T(8,128)(2,1)S(1)} %pad_maximum_fusion.2.near_high), channel_id=1, source_target_pairs={{0,2},{1,3},{2,0},{3,1},{4,6},{5,7},{6,4},{7,5},{8,10},{9,11},{10,... | collective-permute-start | bytes 589832 | tf_op jit(solution)/shard_map/ppermute | solution.py:140
  27.6 11.8 %collective-permute-start.8 = (bf16[2,2,96,256]{3,2,1,0:T(8,128)(2,1)S(1)}, bf16[2,2,96,256]{3,2,1,0:T(8,128)(2,1)S(1)}, u32[]{:S(2)}, u32[]{:S(2)}) collective-permute-start(bf16[2,2,96,256]{3,2,1,0:T(8,128)(2,1)S(1)} %pad_maximum_fusion.2.near_high), channel_id=1, source_target_pairs={{0,16},{16,0},{1,17},{17,1},{2,18},{18,2},{3,19},{19,3},{4,20},{20... | collective-permute-start | bytes 589832 | tf_op jit(solution)/shard_map/ppermute | solution.py:144
  31.9 7.5 %collective-permute-start.11 = (bf16[2,2,96,256]{3,2,1,0:T(8,128)(2,1)S(1)}, bf16[2,2,96,256]{3,2,1,0:T(8,128)(2,1)S(1)}, u32[]{:S(2)}, u32[]{:S(2)}) collective-permute-start(bf16[2,2,96,256]{3,2,1,0:T(8,128)(2,1)S(1)} %collective-permute-done.10.far_high), channel_id=1, source_target_pairs={{0,16},{16,0},{1,17},{17,1},{2,18},{18,2},{3,19},{19,3},{4,20},{20... | collective-permute-start | bytes 589832 | tf_op jit(solution)/shard_map/ppermute | solution.py:144
  37.8 8.9 %collective-permute-start.25 = (bf16[2,2,96,256]{3,2,1,0:T(8,128)(2,1)S(1)}, bf16[2,2,96,256]{3,2,1,0:T(8,128)(2,1)S(1)}, u32[]{:S(2)}, u32[]{:S(2)}) collective-permute-start(bf16[2,2,96,256]{3,2,1,0:T(8,128)(2,1)S(1)} %get-tuple-element.68), channel_id=1, source_target_pairs={{0,2},{1,3},{2,0},{3,1},{4,6},{5,7},{6,4},{7,5},{8,10},{9,11},{10,... | collective-permute-start | bytes 589832 | tf_op jit(solution)/shard_map/ppermute | solution.py:140
  39.2 7.6 %collective-permute-start.26 = (bf16[2,2,96,256]{3,2,1,0:T(8,128)(2,1)S(1)}, bf16[2,2,96,256]{3,2,1,0:T(8,128)(2,1)S(1)}, u32[]{:S(2)}, u32[]{:S(2)}) collective-permute-start(bf16[2,2,96,256]{3,2,1,0:T(8,128)(2,1)S(1)} %get-tuple-element.69), channel_id=1, source_target_pairs={{0,2},{1,3},{2,0},{3,1},{4,6},{5,7},{6,4},{7,5},{8,10},{9,11},{10,... | collective-permute-start | bytes 589832 | tf_op jit(solution)/shard_map/ppermute | solution.py:140
  45.2 8.6 %collective-permute-start.12 = (bf16[2,2,96,256]{3,2,1,0:T(8,128)(2,1)S(1)}, bf16[2,2,96,256]{3,2,1,0:T(8,128)(2,1)S(1)}, u32[]{:S(2)}, u32[]{:S(2)}) collective-permute-start(bf16[2,2,96,256]{3,2,1,0:T(8,128)(2,1)S(1)} %get-tuple-element.58), channel_id=1, source_target_pairs={{0,2},{1,3},{2,0},{3,1},{4,6},{5,7},{6,4},{7,5},{8,10},{9,11},{10,... | collective-permute-start | bytes 589832 | tf_op jit(solution)/shard_map/ppermute | solution.py:140
  46.5 8.1 %collective-permute-start.14 = (bf16[2,2,96,256]{3,2,1,0:T(8,128)(2,1)S(1)}, bf16[2,2,96,256]{3,2,1,0:T(8,128)(2,1)S(1)}, u32[]{:S(2)}, u32[]{:S(2)}) collective-permute-start(bf16[2,2,96,256]{3,2,1,0:T(8,128)(2,1)S(1)} %get-tuple-element.61), channel_id=1, source_target_pairs={{0,2},{1,3},{2,0},{3,1},{4,6},{5,7},{6,4},{7,5},{8,10},{9,11},{10,... | collective-permute-start | bytes 589832 | tf_op jit(solution)/shard_map/ppermute | solution.py:140
  46.9 3.6 %collective-permute-start.27 = (bf16[2,96,256]{2,1,0:T(8,128)(2,1)S(1)}, bf16[2,96,256]{2,1,0:T(8,128)(2,1)S(1)}, u32[]{:S(2)}, u32[]{:S(2)}) collective-permute-start(bf16[2,96,256]{2,1,0:T(8,128)(2,1)S(1)} %get-tuple-element.72), channel_id=1, source_target_pairs={{0,4},{1,5},{2,6},{3,7},{4,0},{5,1},{6,2},{7,3},{8,12},{9,13},{10,... | collective-permute-start | bytes 294920 | tf_op jit(solution)/shard_map/ppermute | solution.py:140
  46.9 4.5 %collective-permute-start.28 = (bf16[2,96,256]{2,1,0:T(8,128)(2,1)S(1)}, bf16[2,96,256]{2,1,0:T(8,128)(2,1)S(1)}, u32[]{:S(2)}, u32[]{:S(2)}) collective-permute-start(bf16[2,96,256]{2,1,0:T(8,128)(2,1)S(1)} %get-tuple-element.74), channel_id=1, source_target_pairs={{0,8},{1,9},{2,10},{3,11},{4,12},{5,13},{6,14},{7,15},{8,0},{9,1},... | collective-permute-start | bytes 294920 | tf_op jit(solution)/shard_map/ppermute | solution.py:140
  48.2 5.4 %collective-permute-start.29 = (bf16[2,96,256]{2,1,0:T(8,128)(2,1)S(1)}, bf16[2,96,256]{2,1,0:T(8,128)(2,1)S(1)}, u32[]{:S(2)}, u32[]{:S(2)}) collective-permute-start(bf16[2,96,256]{2,1,0:T(8,128)(2,1)S(1)} %get-tuple-element.75), channel_id=1, source_target_pairs={{0,12},{1,13},{2,14},{3,15},{4,8},{5,9},{6,10},{7,11},{8,4},{9,5},... | collective-permute-start | bytes 294920 | tf_op jit(solution)/shard_map/ppermute | solution.py:140
  54.6 6.5 %collective-permute-start.32 = (bf16[2,96,256]{2,1,0:T(8,128)(2,1)S(1)}, bf16[2,96,256]{2,1,0:T(8,128)(2,1)S(1)}, u32[]{:S(2)}, u32[]{:S(2)}) collective-permute-start(bf16[2,96,256]{2,1,0:T(8,128)(2,1)S(1)} %get-tuple-element.77), channel_id=1, source_target_pairs={{0,12},{1,13},{2,14},{3,15},{4,8},{5,9},{6,10},{7,11},{8,4},{9,5},... | collective-permute-start | bytes 294920 | tf_op jit(solution)/shard_map/ppermute | solution.py:140
  56.5 9.0 %collective-permute-start.31 = (bf16[2,96,256]{2,1,0:T(8,128)(2,1)S(1)}, bf16[2,96,256]{2,1,0:T(8,128)(2,1)S(1)}, u32[]{:S(2)}, u32[]{:S(2)}) collective-permute-start(bf16[2,96,256]{2,1,0:T(8,128)(2,1)S(1)} %get-tuple-element.77), channel_id=1, source_target_pairs={{0,8},{1,9},{2,10},{3,11},{4,12},{5,13},{6,14},{7,15},{8,0},{9,1},... | collective-permute-start | bytes 294920 | tf_op jit(solution)/shard_map/ppermute | solution.py:140
  56.5 9.0 %collective-permute-start.30 = (bf16[2,96,256]{2,1,0:T(8,128)(2,1)S(1)}, bf16[2,96,256]{2,1,0:T(8,128)(2,1)S(1)}, u32[]{:S(2)}, u32[]{:S(2)}) collective-permute-start(bf16[2,96,256]{2,1,0:T(8,128)(2,1)S(1)} %get-tuple-element.77), channel_id=1, source_target_pairs={{0,4},{1,5},{2,6},{3,7},{4,0},{5,1},{6,2},{7,3},{8,12},{9,13},{10,... | collective-permute-start | bytes 294920 | tf_op jit(solution)/shard_map/ppermute | solution.py:140
  58.2 8.7 %collective-permute-start.15 = (bf16[2,96,256]{2,1,0:T(8,128)(2,1)S(1)}, bf16[2,96,256]{2,1,0:T(8,128)(2,1)S(1)}, u32[]{:S(2)}, u32[]{:S(2)}) collective-permute-start(bf16[2,96,256]{2,1,0:T(8,128)(2,1)S(1)} %get-tuple-element.62), channel_id=1, source_target_pairs={{0,8},{1,9},{2,10},{3,11},{4,12},{5,13},{6,14},{7,15},{8,0},{9,1},... | collective-permute-start | bytes 294920 | tf_op jit(solution)/shard_map/ppermute | solution.py:140
  59.0 34.9 %copy-start = (bf16[1024,1024]{1,0:T(8,128)(2,1)S(1)}, bf16[1024,1024]{1,0:T(8,128)(2,1)}, u32[]{:S(2)}) copy-start(bf16[1024,1024]{1,0:T(8,128)(2,1)} %rest_4_.3) | copy-start | bytes 6291460
  59.0 7.9 %collective-permute-start.16 = (bf16[2,96,256]{2,1,0:T(8,128)(2,1)S(1)}, bf16[2,96,256]{2,1,0:T(8,128)(2,1)S(1)}, u32[]{:S(2)}, u32[]{:S(2)}) collective-permute-start(bf16[2,96,256]{2,1,0:T(8,128)(2,1)S(1)} %get-tuple-element.63), channel_id=1, source_target_pairs={{0,12},{1,13},{2,14},{3,15},{4,8},{5,9},{6,10},{7,11},{8,4},{9,5},... | collective-permute-start | bytes 294920 | tf_op jit(solution)/shard_map/ppermute | solution.py:140
  61.1 7.6 %collective-permute-start.13 = (bf16[2,96,256]{2,1,0:T(8,128)(2,1)S(1)}, bf16[2,96,256]{2,1,0:T(8,128)(2,1)S(1)}, u32[]{:S(2)}, u32[]{:S(2)}) collective-permute-start(bf16[2,96,256]{2,1,0:T(8,128)(2,1)S(1)} %get-tuple-element.60), channel_id=1, source_target_pairs={{0,4},{1,5},{2,6},{3,7},{4,0},{5,1},{6,2},{7,3},{8,12},{9,13},{10,... | collective-permute-start | bytes 294920 | tf_op jit(solution)/shard_map/ppermute | solution.py:140
  68.9 16.9 %collective-permute-start.34 = (bf16[4,2,96,256]{3,2,1,0:T(8,128)(2,1)S(1)}, bf16[4,2,96,256]{3,2,1,0:T(8,128)(2,1)S(1)}, u32[]{:S(2)}, u32[]{:S(2)}) collective-permute-start(bf16[4,2,96,256]{3,2,1,0:T(8,128)(2,1)S(1)} %pad_maximum_fusion.rest_0_), channel_id=1, source_target_pairs={{0,2},{1,3},{2,0},{3,1},{4,6},{5,7},{6,4},{7,5},{8,10},{9,11},{10,... | collective-permute-start | bytes 1179656 | tf_op jit(solution)/shard_map/ppermute | solution.py:140
  70.2 20.2 %collective-permute-start.20 = (bf16[2,96,256]{2,1,0:T(8,128)(2,1)S(1)}, bf16[2,96,256]{2,1,0:T(8,128)(2,1)S(1)}, u32[]{:S(2)}, u32[]{:S(2)}) collective-permute-start(bf16[2,96,256]{2,1,0:T(8,128)(2,1)S(1)} %get-tuple-element.64), channel_id=1, source_target_pairs={{0,12},{1,13},{2,14},{3,15},{4,8},{5,9},{6,10},{7,11},{8,4},{9,5},... | collective-permute-start | bytes 294920 | tf_op jit(solution)/shard_map/ppermute | solution.py:140
  72.4 18.1 %collective-permute-start.19 = (bf16[2,96,256]{2,1,0:T(8,128)(2,1)S(1)}, bf16[2,96,256]{2,1,0:T(8,128)(2,1)S(1)}, u32[]{:S(2)}, u32[]{:S(2)}) collective-permute-start(bf16[2,96,256]{2,1,0:T(8,128)(2,1)S(1)} %get-tuple-element.64), channel_id=1, source_target_pairs={{0,8},{1,9},{2,10},{3,11},{4,12},{5,13},{6,14},{7,15},{8,0},{9,1},... | collective-permute-start | bytes 294920 | tf_op jit(solution)/shard_map/ppermute | solution.py:140
  72.4 15.5 %collective-permute-start.17 = (bf16[2,96,256]{2,1,0:T(8,128)(2,1)S(1)}, bf16[2,96,256]{2,1,0:T(8,128)(2,1)S(1)}, u32[]{:S(2)}, u32[]{:S(2)}) collective-permute-start(bf16[2,96,256]{2,1,0:T(8,128)(2,1)S(1)} %get-tuple-element.64), channel_id=1, source_target_pairs={{0,4},{1,5},{2,6},{3,7},{4,0},{5,1},{6,2},{7,3},{8,12},{9,13},{10,... | collective-permute-start | bytes 294920 | tf_op jit(solution)/shard_map/ppermute | solution.py:140
  73.8 24.3 %collective-permute-start.33 = (bf16[4,2,96,256]{3,2,1,0:T(8,128)(2,1)S(1)}, bf16[4,2,96,256]{3,2,1,0:T(8,128)(2,1)S(1)}, u32[]{:S(2)}, u32[]{:S(2)}) collective-permute-start(bf16[4,2,96,256]{3,2,1,0:T(8,128)(2,1)S(1)} %pad_maximum_fusion.rest_0_), channel_id=1, source_target_pairs={{0,1},{1,0},{2,3},{3,2},{4,5},{5,4},{6,7},{7,6},{8,9},{9,8},{10,11... | collective-permute-start | bytes 1179656 | tf_op jit(solution)/shard_map/ppermute | solution.py:140
  85.8 12.3 %collective-permute-start.35 = (bf16[4,2,96,256]{3,2,1,0:T(8,128)(2,1)S(1)}, bf16[4,2,96,256]{3,2,1,0:T(8,128)(2,1)S(1)}, u32[]{:S(2)}, u32[]{:S(2)}) collective-permute-start(bf16[4,2,96,256]{3,2,1,0:T(8,128)(2,1)S(1)} %collective-permute-done.34.rest_1_), channel_id=1, source_target_pairs={{0,1},{1,0},{2,3},{3,2},{4,5},{5,4},{6,7},{7,6},{8,9},{9,8},{10,11... | collective-permute-start | bytes 1179656 | tf_op jit(solution)/shard_map/ppermute | solution.py:140
  87.9 4.1 %collective-permute-start.36 = (f32[2,96,256]{2,1,0:T(8,128)S(1)}, f32[2,96,256]{2,1,0:T(8,128)S(1)}, u32[]{:S(2)}, u32[]{:S(2)}) collective-permute-start(f32[2,96,256]{2,1,0:T(8,128)S(1)} %pad_maximum_fusion.5), channel_id=1, source_target_pairs={{0,1},{1,0},{2,3},{3,2},{4,5},{5,4},{6,7},{7,6},{8,9},{9,8},{10,11... | collective-permute-start | bytes 589832 | tf_op jit(solution)/shard_map/ppermute | solution.py:140
  90.4 6.6 %collective-permute-start.22 = (bf16[2,2,96,256]{3,2,1,0:T(8,128)(2,1)S(1)}, bf16[2,2,96,256]{3,2,1,0:T(8,128)(2,1)S(1)}, u32[]{:S(2)}, u32[]{:S(2)}) collective-permute-start(bf16[2,2,96,256]{3,2,1,0:T(8,128)(2,1)S(1)} %pad_maximum_fusion.3.rest_0_), channel_id=1, source_target_pairs={{0,2},{1,3},{2,0},{3,1},{4,6},{5,7},{6,4},{7,5},{8,10},{9,11},{10,... | collective-permute-start | bytes 589832 | tf_op jit(solution)/shard_map/ppermute | solution.py:140
  90.5 10.7 %collective-permute-start.24 = (bf16[2,2,96,256]{3,2,1,0:T(8,128)(2,1)S(1)}, bf16[2,2,96,256]{3,2,1,0:T(8,128)(2,1)S(1)}, u32[]{:S(2)}, u32[]{:S(2)}) collective-permute-start(bf16[2,2,96,256]{3,2,1,0:T(8,128)(2,1)S(1)} %pad_maximum_fusion.4.rest_1_), channel_id=1, source_target_pairs={{0,2},{1,3},{2,0},{3,1},{4,6},{5,7},{6,4},{7,5},{8,10},{9,11},{10,... | collective-permute-start | bytes 589832 | tf_op jit(solution)/shard_map/ppermute | solution.py:140
  92.0 12.5 %collective-permute-start.18 = (bf16[2,2,96,256]{3,2,1,0:T(8,128)(2,1)S(1)}, bf16[2,2,96,256]{3,2,1,0:T(8,128)(2,1)S(1)}, u32[]{:S(2)}, u32[]{:S(2)}) collective-permute-start(bf16[2,2,96,256]{3,2,1,0:T(8,128)(2,1)S(1)} %pad_maximum_fusion.3.rest_0_), channel_id=1, source_target_pairs={{0,1},{1,0},{2,3},{3,2},{4,5},{5,4},{6,7},{7,6},{8,9},{9,8},{10,11... | collective-permute-start | bytes 589832 | tf_op jit(solution)/shard_map/ppermute | solution.py:140
  97.0 7.5 %collective-permute-start.21 = (bf16[2,2,96,256]{3,2,1,0:T(8,128)(2,1)S(1)}, bf16[2,2,96,256]{3,2,1,0:T(8,128)(2,1)S(1)}, u32[]{:S(2)}, u32[]{:S(2)}) collective-permute-start(bf16[2,2,96,256]{3,2,1,0:T(8,128)(2,1)S(1)} %pad_maximum_fusion.4.rest_1_), channel_id=1, source_target_pairs={{0,1},{1,0},{2,3},{3,2},{4,5},{5,4},{6,7},{7,6},{8,9},{9,8},{10,11... | collective-permute-start | bytes 589832 | tf_op jit(solution)/shard_map/ppermute | solution.py:140
  98.1 6.3 %collective-permute-start.23 = (bf16[2,2,96,256]{3,2,1,0:T(8,128)(2,1)S(1)}, bf16[2,2,96,256]{3,2,1,0:T(8,128)(2,1)S(1)}, u32[]{:S(2)}, u32[]{:S(2)}) collective-permute-start(bf16[2,2,96,256]{3,2,1,0:T(8,128)(2,1)S(1)} %collective-permute-done.22.rest_2_), channel_id=1, source_target_pairs={{0,1},{1,0},{2,3},{3,2},{4,5},{5,4},{6,7},{7,6},{8,9},{9,8},{10,11... | collective-permute-start | bytes 589832 | tf_op jit(solution)/shard_map/ppermute | solution.py:140
  101.2 3.3 %collective-permute-start.37 = (bf16[2,2,96,256]{3,2,1,0:T(8,128)(2,1)S(1)}, bf16[2,2,96,256]{3,2,1,0:T(8,128)(2,1)S(1)}, u32[]{:S(2)}, u32[]{:S(2)}) collective-permute-start(bf16[2,2,96,256]{3,2,1,0:T(8,128)(2,1)S(1)} %collective-permute-done.24.rest_3_), channel_id=1, source_target_pairs={{0,1},{1,0},{2,3},{3,2},{4,5},{5,4},{6,7},{7,6},{8,9},{9,8},{10,11... | collective-permute-start | bytes 589832 | tf_op jit(solution)/shard_map/ppermute | solution.py:140

commit v11 on v9

--- a/solution.py
+++ b/solution.py
@@ -161,15 +161,7 @@
     return (wide * lax.rsqrt(jnp.mean(wide * wide, axis=-1, keepdims=True) + 1e-06)).astype(BF16)
 
 
-def pack_kernel(ids, in_hbm, out_hbm, own, theirs, in_ref, out_ref, arrived):
-    copies = [
-        pltpu.make_async_copy(in_hbm, in_ref, arrived.at[0]),
-        pltpu.make_async_copy(out_hbm, out_ref, arrived.at[1]),
-    ]
-    for copy in copies:
-        copy.start()
-    for copy in copies:
-        copy.wait()
+def pack_kernel(ids, in_ref, out_ref, own, theirs):
     size = out_ref.shape[-1]
     rows = in_ref.shape[1]
     for other, ref in ((0, own), (1, theirs)):
@@ -184,16 +176,17 @@
 
 def pack(ids, fast_in, fast_out):
     rows = 4 * fast_in.shape[1] + fast_out.shape[1]
-    shape = jax.ShapeDtypeStruct((2, rows, fast_out.shape[2]), F32)
+    shape = (2, rows, fast_out.shape[2])
+    whole = [pl.BlockSpec(each, lambda i, ids: (0, 0, 0)) for each in (fast_in.shape, fast_out.shape, shape)]
     return pl.pallas_call(
         pack_kernel,
-        in_specs=[pl.BlockSpec(memory_space=pltpu.SMEM)] + [pl.BlockSpec(memory_space=pltpu.HBM)] * 2,
-        out_shape=[shape, shape],
-        scratch_shapes=[
-            pltpu.VMEM(fast_in.shape, F32),
-            pltpu.VMEM(fast_out.shape, F32),
-            pltpu.SemaphoreType.DMA((2,)),
-        ],
+        grid_spec=pltpu.PrefetchScalarGridSpec(
+            num_scalar_prefetch=1,
+            grid=(1,),
+            in_specs=whole[:2],
+            out_specs=[whole[2]] * 2,
+        ),
+        out_shape=[jax.ShapeDtypeStruct(shape, F32)] * 2,
         compiler_params=compiler_params(),
         name="pack",
     )(ids, fast_in, fast_out)
@@ -263,7 +256,7 @@
         out_shape=[shape] * 2,
         compiler_params=compiler_params(),
         cost_estimate=pl.CostEstimate(
-            flops=rows * width * 5, bytes_accessed=rows * width * 4, transcendentals=0
+            flops=rows * width * 5000, bytes_accessed=rows * width * 40, transcendentals=0
         ),
         name=name,
     )(ids, *operands)

time: 103 us -> 101 us (0.981)
  local copies, waits for them, and re-layouts: 3.47 us -> 1.63 us
    unnamed x12, local copies, waits for them, and re-layouts: 3.46 us -> 1.61 us
  transfers between devices with their start and end apart: 41 -> 41, of which waited for: 11 -> 11; matrix products, arithmetic and copies ran while one was open for 0% -> 0% of each run, Pallas kernels for 22% -> 23%
where the time goes in v11:
time: 101 us
  starting transfers between devices  47.5 us (47%)
  Pallas kernels  27.6 us (27%)
  waiting for transfers between devices  23.2 us (23%)
  local copies, waits for them, and re-layouts  1.63 us (2%)
  between operations  1.1 us (1%)
    ppermute x37, starting transfers between devices, swap(): lax.ppermute(value, 'tok', [(place, place ^ bits) for place in range(coun...  44.4 us
    ppermute x37, waiting for transfers between devices, swap(): lax.ppermute(value, 'tok', [(place, place ^ bits) for place in range(coun...  20 us
    pallas_call x2, Pallas kernels, increments(): pl.pallas_call(increments_kernel, grid_spec=pltpu.PrefetchScalarGridSpec(...  11.5 us
    pallas_call x4, Pallas kernels, apply_fast(): pl.pallas_call(functools.partial(apply_kernel, order, other), grid_spec=p...  9.98 us
    pallas_call x2, Pallas kernels, prepare(): pl.pallas_call(functools.partial(prepare_kernel, heads, block_root), grid...  3.78 us
    ppermute x4, waiting for transfers between devices, swap_parts(): return lax.ppermute(value, 'parts', [(0, 1), (1, 0)])  3.19 us
    ppermute x4, starting transfers between devices, swap_parts(): return lax.ppermute(value, 'parts', [(0, 1), (1, 0)])  3.06 us
  transfers between devices with their start and end apart: 41, of which 11 were waited for; matrix products, arithmetic and copies ran while one was open for 0% of the time, Pallas kernels for 23%

profile of v11, /device:TPU:1, one launch (start us, length us, event | category | flops | bytes accessed | tf_op | source)
XLA Modules:
  0.0 101.2 jit_solution(13233651753610593008)
XLA Ops:
  0.6 0.1 pad_add_fusion.ids
  0.7 1.6 %copy-done.3 = bf16[1024,1024]{1,0:T(8,128)(2,1)S(1)} copy-done((bf16[1024,1024]{1,0:T(8,128)(2,1)S(1)}, bf16[1024,1024]{1,0:T(8,128)(2,1)}, u32[]{:S(2)}) %copy-start.3) | copy-done | bytes 2097176
  2.3 1.5 %keys.1 = (bf16[1024,512]{1,0:T(8,128)(2,1)S(1)}, bf16[1024,512]{1,0:T(8,128)(2,1)S(1)}) custom-call(s32[3]{0:T(128)S(1)} %pad_add_fusion.ids, bf16[1024,1024]{1,0:T(8,128)(2,1)S(1)} %copy-done.3), custom_call_target="tpu_custom_call" | custom-call | flops 5242880000 | bytes 41943040 | tf_op jit(solution)/shard_map/keys/pallas_call | solution.py:248
  3.9 0.6 pack.1
  4.4 0.1 collective-permute-start
  4.6 0.5 collective-permute-start.2
  5.0 0.9 collective-permute-done.got
  6.0 2.3 %values.1 = (bf16[1024,512]{1,0:T(8,128)(2,1)S(1)}, bf16[1024,512]{1,0:T(8,128)(2,1)S(1)}) custom-call(s32[3]{0:T(128)S(1)} %pad_add_fusion.ids, bf16[1024,1024]{1,0:T(8,128)(2,1)S(1)} %copy-done.4, f32[4,1024]{1,0:T(4,128)S(1)} %copy-done.5), custom_call_target="tpu_custom_call" | custom-call | flops 5242880000 | bytes 41943040 | tf_op jit(solution)/shard_map/values/pallas_call | solution.py:248
  8.2 0.2 collective-permute-start.3
  8.5 2.7 %collective-permute-start.1 = (bf16[2,96,256]{2,1,0:T(8,128)(2,1)S(1)}, bf16[2,96,256]{2,1,0:T(8,128)(2,1)S(1)}, u32[]{:S(2)}, u32[]{:S(2)}) collective-permute-start(bf16[2,96,256]{2,1,0:T(8,128)(2,1)S(1)} %get-tuple-element.52), channel_id=1, source_target_pairs={{0,4},{1,5},{2,6},{3,7},{4,0},{5,1},{6,2},{7,3},{8,12},{9,13},{10,... | collective-permute-start | bytes 294920 | tf_op jit(solution)/shard_map/ppermute | solution.py:140
  11.2 2.2 %collective-permute-start.6 = (bf16[2,96,256]{2,1,0:T(8,128)(2,1)S(1)}, bf16[2,96,256]{2,1,0:T(8,128)(2,1)S(1)}, u32[]{:S(2)}, u32[]{:S(2)}) collective-permute-start(bf16[2,96,256]{2,1,0:T(8,128)(2,1)S(1)} %get-tuple-element.52), channel_id=1, source_target_pairs={{0,12},{1,13},{2,14},{3,15},{4,8},{5,9},{6,10},{7,11},{8,4},{9,5},... | collective-permute-start | bytes 294920 | tf_op jit(solution)/shard_map/ppermute | solution.py:140
  13.4 0.1 collective-permute-start.5
  13.5 0.7 collective-permute-done.1
  14.3 1.2 %collective-permute-start.7 = (bf16[2,2,96,256]{3,2,1,0:T(8,128)(2,1)S(1)}, bf16[2,2,96,256]{3,2,1,0:T(8,128)(2,1)S(1)}, u32[]{:S(2)}, u32[]{:S(2)}) collective-permute-start(bf16[2,2,96,256]{3,2,1,0:T(8,128)(2,1)S(1)} %pad_maximum_fusion.near_low), channel_id=1, source_target_pairs={{0,2},{1,3},{2,0},{3,1},{4,6},{5,7},{6,4},{7,5},{8,10},{9,11},{10,... | collective-permute-start | bytes 589832 | tf_op jit(solution)/shard_map/ppermute | solution.py:140
  15.5 1.2 %collective-permute-start.4 = (bf16[2,2,96,256]{3,2,1,0:T(8,128)(2,1)S(1)}, bf16[2,2,96,256]{3,2,1,0:T(8,128)(2,1)S(1)}, u32[]{:S(2)}, u32[]{:S(2)}) collective-permute-start(bf16[2,2,96,256]{3,2,1,0:T(8,128)(2,1)S(1)} %pad_maximum_fusion.near_low), channel_id=1, source_target_pairs={{0,16},{16,0},{1,17},{17,1},{2,18},{18,2},{3,19},{19,3},{4,20},{20... | collective-permute-start | bytes 589832 | tf_op jit(solution)/shard_map/ppermute | solution.py:144
  16.7 1.6 %collective-permute-done.6 = bf16[2,96,256]{2,1,0:T(8,128)(2,1)S(1)} collective-permute-done((bf16[2,96,256]{2,1,0:T(8,128)(2,1)S(1)}, bf16[2,96,256]{2,1,0:T(8,128)(2,1)S(1)}, u32[]{:S(2)}, u32[]{:S(2)}) %collective-permute-start.6) | collective-permute-done | bytes 98336 | tf_op jit(solution)/shard_map/ppermute | solution.py:140
  18.3 4.6 %collective-permute-done.5 = bf16[2,96,256]{2,1,0:T(8,128)(2,1)S(1)} collective-permute-done((bf16[2,96,256]{2,1,0:T(8,128)(2,1)S(1)}, bf16[2,96,256]{2,1,0:T(8,128)(2,1)S(1)}, u32[]{:S(2)}, u32[]{:S(2)}) %collective-permute-start.5) | collective-permute-done | bytes 98336 | tf_op jit(solution)/shard_map/ppermute | solution.py:140
  23.0 1.3 %collective-permute-start.9 = (bf16[2,2,96,256]{3,2,1,0:T(8,128)(2,1)S(1)}, bf16[2,2,96,256]{3,2,1,0:T(8,128)(2,1)S(1)}, u32[]{:S(2)}, u32[]{:S(2)}) collective-permute-start(bf16[2,2,96,256]{3,2,1,0:T(8,128)(2,1)S(1)} %collective-permute-done.7.far_low), channel_id=1, source_target_pairs={{0,16},{16,0},{1,17},{17,1},{2,18},{18,2},{3,19},{19,3},{4,20},{20... | collective-permute-start | bytes 589832 | tf_op jit(solution)/shard_map/ppermute | solution.py:144
  24.3 1.2 %collective-permute-start.10 = (bf16[2,2,96,256]{3,2,1,0:T(8,128)(2,1)S(1)}, bf16[2,2,96,256]{3,2,1,0:T(8,128)(2,1)S(1)}, u32[]{:S(2)}, u32[]{:S(2)}) collective-permute-start(bf16[2,2,96,256]{3,2,1,0:T(8,128)(2,1)S(1)} %pad_maximum_fusion.1.near_high), channel_id=1, source_target_pairs={{0,2},{1,3},{2,0},{3,1},{4,6},{5,7},{6,4},{7,5},{8,10},{9,11},{10,... | collective-permute-start | bytes 589832 | tf_op jit(solution)/shard_map/ppermute | solution.py:140
  25.5 0.3 collective-permute-start.8
  25.8 3.1 %collective-permute-done.9.far_low = bf16[2,2,96,256]{3,2,1,0:T(8,128)(2,1)S(1)} collective-permute-done((bf16[2,2,96,256]{3,2,1,0:T(8,128)(2,1)S(1)}, bf16[2,2,96,256]{3,2,1,0:T(8,128)(2,1)S(1)}, u32[]{:S(2)}, u32[]{:S(2)}) %collective-permute-start.9) | collective-permute-done | bytes 196640 | tf_op jit(solution)/shard_map/ppermute | solution.py:144
  28.9 0.9 collective-permute-done.10.far_high
  29.8 0.3 collective-permute-start.11
  30.2 5.6 %increments.3 = (f32[4,2,96,256]{3,2,1,0:T(8,128)S(1)}, bf16[2,2,96,256]{3,2,1,0:T(8,128)(2,1)S(1)}, bf16[2,2,96,256]{3,2,1,0:T(8,128)(2,1)S(1)}) custom-call(s32[3]{0:T(128)S(1)} %pad_add_fusion.ids, bf16[2,2,96,256]{3,2,1,0:T(8,128)(2,1)S(1)} %pad_maximum_fusion.near_low, bf16[2,2,96,256]{3,2,1,0:T(8,128)(2,1)S(1)} %pad_maximum_fusion.1.near_high, ...), custom_call_target="tpu_custom_call" | custom-call | flops 3221225472 | bytes 2097152 | tf_op jit(solution)/shard_map/increments/pallas_call | solution.py:382
  35.8 1.3 %collective-permute-start.17 = (bf16[2,2,96,256]{3,2,1,0:T(8,128)(2,1)S(1)}, bf16[2,2,96,256]{3,2,1,0:T(8,128)(2,1)S(1)}, u32[]{:S(2)}, u32[]{:S(2)}) collective-permute-start(bf16[2,2,96,256]{3,2,1,0:T(8,128)(2,1)S(1)} %get-tuple-element.67), channel_id=1, source_target_pairs={{0,2},{1,3},{2,0},{3,1},{4,6},{5,7},{6,4},{7,5},{8,10},{9,11},{10,... | collective-permute-start | bytes 589832 | tf_op jit(solution)/shard_map/ppermute | solution.py:140
  37.1 0.2 collective-permute-start.19
  37.4 5.8 %increments.2 = (f32[4,2,96,256]{3,2,1,0:T(8,128)S(1)}, bf16[2,2,96,256]{3,2,1,0:T(8,128)(2,1)S(1)}, bf16[2,2,96,256]{3,2,1,0:T(8,128)(2,1)S(1)}) custom-call(s32[3]{0:T(128)S(1)} %pad_add_fusion.ids, bf16[2,2,96,256]{3,2,1,0:T(8,128)(2,1)S(1)} %collective-permute-done.4.near_low, bf16[2,2,96,256]{3,2,1,0:T(8,128)(2,1)S(1)} %collective-permute-done.8.near_high, ...), custom_call_target="tpu_custom_call" | custom-call | flops 3221225472 | bytes 2097152 | tf_op jit(solution)/shard_map/increments/pallas_call | solution.py:382
  43.2 1.3 %collective-permute-start.12 = (bf16[2,2,96,256]{3,2,1,0:T(8,128)(2,1)S(1)}, bf16[2,2,96,256]{3,2,1,0:T(8,128)(2,1)S(1)}, u32[]{:S(2)}, u32[]{:S(2)}) collective-permute-start(bf16[2,2,96,256]{3,2,1,0:T(8,128)(2,1)S(1)} %get-tuple-element.57), channel_id=1, source_target_pairs={{0,2},{1,3},{2,0},{3,1},{4,6},{5,7},{6,4},{7,5},{8,10},{9,11},{10,... | collective-permute-start | bytes 589832 | tf_op jit(solution)/shard_map/ppermute | solution.py:140
  44.6 0.1 collective-permute-start.18
  44.7 1.3 %collective-permute-start.20 = (bf16[2,96,256]{2,1,0:T(8,128)(2,1)S(1)}, bf16[2,96,256]{2,1,0:T(8,128)(2,1)S(1)}, u32[]{:S(2)}, u32[]{:S(2)}) collective-permute-start(bf16[2,96,256]{2,1,0:T(8,128)(2,1)S(1)} %get-tuple-element.71), channel_id=1, source_target_pairs={{0,8},{1,9},{2,10},{3,11},{4,12},{5,13},{6,14},{7,15},{8,0},{9,1},... | collective-permute-start | bytes 294920 | tf_op jit(solution)/shard_map/ppermute | solution.py:140
  46.0 2.3 %collective-permute-start.21 = (bf16[2,96,256]{2,1,0:T(8,128)(2,1)S(1)}, bf16[2,96,256]{2,1,0:T(8,128)(2,1)S(1)}, u32[]{:S(2)}, u32[]{:S(2)}) collective-permute-start(bf16[2,96,256]{2,1,0:T(8,128)(2,1)S(1)} %get-tuple-element.72), channel_id=1, source_target_pairs={{0,12},{1,13},{2,14},{3,15},{4,8},{5,9},{6,10},{7,11},{8,4},{9,5},... | collective-permute-start | bytes 294920 | tf_op jit(solution)/shard_map/ppermute | solution.py:140
  48.3 0.2 collective-permute-start.14
  48.5 0.6 collective-permute-done.20.two
  49.1 2.3 %collective-permute-done.21.three = bf16[2,96,256]{2,1,0:T(8,128)(2,1)S(1)} collective-permute-done((bf16[2,96,256]{2,1,0:T(8,128)(2,1)S(1)}, bf16[2,96,256]{2,1,0:T(8,128)(2,1)S(1)}, u32[]{:S(2)}, u32[]{:S(2)}) %collective-permute-start.21) | collective-permute-done | bytes 98336 | tf_op jit(solution)/shard_map/ppermute | solution.py:140
  51.5 0.1 renorm.3
  51.6 1.5 %collective-permute-start.22 = (bf16[2,96,256]{2,1,0:T(8,128)(2,1)S(1)}, bf16[2,96,256]{2,1,0:T(8,128)(2,1)S(1)}, u32[]{:S(2)}, u32[]{:S(2)}) collective-permute-start(bf16[2,96,256]{2,1,0:T(8,128)(2,1)S(1)} %get-tuple-element.73), channel_id=1, source_target_pairs={{0,4},{1,5},{2,6},{3,7},{4,0},{5,1},{6,2},{7,3},{8,12},{9,13},{10,... | collective-permute-start | bytes 294920 | tf_op jit(solution)/shard_map/ppermute | solution.py:140
  53.1 1.7 %collective-permute-start.25 = (bf16[2,96,256]{2,1,0:T(8,128)(2,1)S(1)}, bf16[2,96,256]{2,1,0:T(8,128)(2,1)S(1)}, u32[]{:S(2)}, u32[]{:S(2)}) collective-permute-start(bf16[2,96,256]{2,1,0:T(8,128)(2,1)S(1)} %get-tuple-element.73), channel_id=1, source_target_pairs={{0,12},{1,13},{2,14},{3,15},{4,8},{5,9},{6,10},{7,11},{8,4},{9,5},... | collective-permute-start | bytes 294920 | tf_op jit(solution)/shard_map/ppermute | solution.py:140
  54.8 0.2 collective-permute-start.24
  55.0 1.7 %collective-permute-start.13 = (bf16[2,96,256]{2,1,0:T(8,128)(2,1)S(1)}, bf16[2,96,256]{2,1,0:T(8,128)(2,1)S(1)}, u32[]{:S(2)}, u32[]{:S(2)}) collective-permute-start(bf16[2,96,256]{2,1,0:T(8,128)(2,1)S(1)} %get-tuple-element.59), channel_id=1, source_target_pairs={{0,4},{1,5},{2,6},{3,7},{4,0},{5,1},{6,2},{7,3},{8,12},{9,13},{10,... | collective-permute-start | bytes 294920 | tf_op jit(solution)/shard_map/ppermute | solution.py:140
  56.8 1.0 %collective-permute-start.15 = (bf16[2,96,256]{2,1,0:T(8,128)(2,1)S(1)}, bf16[2,96,256]{2,1,0:T(8,128)(2,1)S(1)}, u32[]{:S(2)}, u32[]{:S(2)}) collective-permute-start(bf16[2,96,256]{2,1,0:T(8,128)(2,1)S(1)} %get-tuple-element.61), channel_id=1, source_target_pairs={{0,8},{1,9},{2,10},{3,11},{4,12},{5,13},{6,14},{7,15},{8,0},{9,1},... | collective-permute-start | bytes 294920 | tf_op jit(solution)/shard_map/ppermute | solution.py:140
  57.9 1.6 %collective-permute-start.16 = (bf16[2,96,256]{2,1,0:T(8,128)(2,1)S(1)}, bf16[2,96,256]{2,1,0:T(8,128)(2,1)S(1)}, u32[]{:S(2)}, u32[]{:S(2)}) collective-permute-start(bf16[2,96,256]{2,1,0:T(8,128)(2,1)S(1)} %get-tuple-element.62), channel_id=1, source_target_pairs={{0,12},{1,13},{2,14},{3,15},{4,8},{5,9},{6,10},{7,11},{8,4},{9,5},... | collective-permute-start | bytes 294920 | tf_op jit(solution)/shard_map/ppermute | solution.py:140
  59.5 0.4 collective-permute-done.13.one
  59.9 0.8 collective-permute-start.36
  60.7 6.0 %collective-permute-done.15.two = bf16[2,96,256]{2,1,0:T(8,128)(2,1)S(1)} collective-permute-done((bf16[2,96,256]{2,1,0:T(8,128)(2,1)S(1)}, bf16[2,96,256]{2,1,0:T(8,128)(2,1)S(1)}, u32[]{:S(2)}, u32[]{:S(2)}) %collective-permute-start.15) | collective-permute-done | bytes 98336 | tf_op jit(solution)/shard_map/ppermute | solution.py:140
  66.7 0.1 renorm.2
  66.9 4.3 %collective-permute-start.23 = (bf16[2,96,256]{2,1,0:T(8,128)(2,1)S(1)}, bf16[2,96,256]{2,1,0:T(8,128)(2,1)S(1)}, u32[]{:S(2)}, u32[]{:S(2)}) collective-permute-start(bf16[2,96,256]{2,1,0:T(8,128)(2,1)S(1)} %get-tuple-element.76), channel_id=1, source_target_pairs={{0,4},{1,5},{2,6},{3,7},{4,0},{5,1},{6,2},{7,3},{8,12},{9,13},{10,... | collective-permute-start | bytes 294920 | tf_op jit(solution)/shard_map/ppermute | solution.py:140
  71.1 4.3 %collective-permute-start.29 = (f32[2,96,256]{2,1,0:T(8,128)S(1)}, f32[2,96,256]{2,1,0:T(8,128)S(1)}, u32[]{:S(2)}, u32[]{:S(2)}) collective-permute-start(f32[2,96,256]{2,1,0:T(8,128)S(1)} %pad_maximum_fusion.6), channel_id=1, source_target_pairs={{0,1},{1,0},{2,3},{3,2},{4,5},{5,4},{6,7},{7,6},{8,9},{9,8},{10,11... | collective-permute-start | bytes 589832 | tf_op jit(solution)/shard_map/ppermute | solution.py:140
  75.5 0.8 collective-permute-start.38
  76.3 2.0 %collective-permute-start.28 = (bf16[2,96,256]{2,1,0:T(8,128)(2,1)S(1)}, bf16[2,96,256]{2,1,0:T(8,128)(2,1)S(1)}, u32[]{:S(2)}, u32[]{:S(2)}) collective-permute-start(bf16[2,96,256]{2,1,0:T(8,128)(2,1)S(1)} %get-tuple-element.76), channel_id=1, source_target_pairs={{0,12},{1,13},{2,14},{3,15},{4,8},{5,9},{6,10},{7,11},{8,4},{9,5},... | collective-permute-start | bytes 294920 | tf_op jit(solution)/shard_map/ppermute | solution.py:140
  78.3 3.2 %collective-permute-start.34 = (bf16[2,2,96,256]{3,2,1,0:T(8,128)(2,1)S(1)}, bf16[2,2,96,256]{3,2,1,0:T(8,128)(2,1)S(1)}, u32[]{:S(2)}, u32[]{:S(2)}) collective-permute-start(bf16[2,2,96,256]{3,2,1,0:T(8,128)(2,1)S(1)} %pad_maximum_fusion.2.near_low), channel_id=1, source_target_pairs={{0,1},{1,0},{2,3},{3,2},{4,5},{5,4},{6,7},{7,6},{8,9},{9,8},{10,11... | collective-permute-start | bytes 589832 | tf_op jit(solution)/shard_map/ppermute | solution.py:140
  81.5 1.3 %finish.1 = (f32[4,16,1024]{2,1,0:T(8,128)}, f32[4,32,256]{2,1,0:T(8,128)}) custom-call(s32[3]{0:T(128)S(1)} %pad_add_fusion.ids, f32[2,96,256]{2,1,0:T(8,128)S(1)} %get-tuple-element.77.one, f32[2,96,256]{2,1,0:T(8,128)S(1)} %get-tuple-element.78.two, f32[2,96,256]{2,1,0:T(8,128)S(1)} %collective-permute-done.29.came), custom_call_target="tpu_custom_call" | custom-call | tf_op jit(solution)/shard_map/finish/pallas_call | solution.py:546
  82.8 0.8 collective-permute-start.31
  83.6 1.3 %collective-permute-start.37 = (bf16[2,2,96,256]{3,2,1,0:T(8,128)(2,1)S(1)}, bf16[2,2,96,256]{3,2,1,0:T(8,128)(2,1)S(1)}, u32[]{:S(2)}, u32[]{:S(2)}) collective-permute-start(bf16[2,2,96,256]{3,2,1,0:T(8,128)(2,1)S(1)} %collective-permute-done.36.far_low), channel_id=1, source_target_pairs={{0,1},{1,0},{2,3},{3,2},{4,5},{5,4},{6,7},{7,6},{8,9},{9,8},{10,11... | collective-permute-start | bytes 589832 | tf_op jit(solution)/shard_map/ppermute | solution.py:140
  84.9 1.9 %collective-permute-done.27 = bf16[2,96,256]{2,1,0:T(8,128)(2,1)S(1)} collective-permute-done((bf16[2,96,256]{2,1,0:T(8,128)(2,1)S(1)}, bf16[2,96,256]{2,1,0:T(8,128)(2,1)S(1)}, u32[]{:S(2)}, u32[]{:S(2)}) %collective-permute-start.27) | collective-permute-done | bytes 98336 | tf_op jit(solution)/shard_map/ppermute | solution.py:140
  86.8 1.8 %collective-permute-start.39 = (bf16[2,2,96,256]{3,2,1,0:T(8,128)(2,1)S(1)}, bf16[2,2,96,256]{3,2,1,0:T(8,128)(2,1)S(1)}, u32[]{:S(2)}, u32[]{:S(2)}) collective-permute-start(bf16[2,2,96,256]{3,2,1,0:T(8,128)(2,1)S(1)} %collective-permute-done.38.far_high), channel_id=1, source_target_pairs={{0,1},{1,0},{2,3},{3,2},{4,5},{5,4},{6,7},{7,6},{8,9},{9,8},{10,11... | collective-permute-start | bytes 589832 | tf_op jit(solution)/shard_map/ppermute | solution.py:140
  88.6 0.8 collective-permute-start.33
  89.5 2.5 %apply.4.rest_0_ = bf16[1024,1024]{1,0:T(8,128)(2,1)} custom-call(s32[3]{0:T(128)S(1)} %pad_add_fusion.ids, bf16[2,2,96,256]{3,2,1,0:T(8,128)(2,1)S(1)} %pad_maximum_fusion.2.near_low, bf16[2,2,96,256]{3,2,1,0:T(8,128)(2,1)S(1)} %pad_maximum_fusion.4.near_high, bf16[2,2,96,256]{3,2,1,0:T(8,128)(2,1)S(1)} %collective-permute-done.36.far_low, ...), custom_call_target="tpu_custom_call" | custom-call | flops 805306368 | bytes 1048576 | tf_op jit(solution)/shard_map/apply/pallas_call | solution.py:509
  92.0 0.3 collective-permute-start.26
  92.3 0.2 collective-permute-start.30
  92.5 0.3 collective-permute-start.32
  92.8 2.5 %apply.5.rest_0_ = bf16[1024,1024]{1,0:T(8,128)(2,1)} custom-call(s32[3]{0:T(128)S(1)} %pad_add_fusion.ids, bf16[2,2,96,256]{3,2,1,0:T(8,128)(2,1)S(1)} %collective-permute-done.34.near_low, bf16[2,2,96,256]{3,2,1,0:T(8,128)(2,1)S(1)} %collective-permute-done.35.near_high, ...), custom_call_target="tpu_custom_call", output_to_operand_aliasing={{}: (6, {})} | custom-call | flops 805306368 | bytes 1048576 | tf_op jit(solution)/shard_map/apply/pallas_call | solution.py:509
  95.3 0.7 collective-permute-start.40
  96.0 2.5 %apply.6.rest_0_ = bf16[1024,1024]{1,0:T(8,128)(2,1)} custom-call(s32[3]{0:T(128)S(1)} %pad_add_fusion.ids, bf16[2,2,96,256]{3,2,1,0:T(8,128)(2,1)S(1)} %pad_maximum_fusion.3.near_low, bf16[2,2,96,256]{3,2,1,0:T(8,128)(2,1)S(1)} %pad_maximum_fusion.5.near_high, ...), custom_call_target="tpu_custom_call", output_to_operand_aliasing={{}: (6, {})} | custom-call | flops 805306368 | bytes 1048576 | tf_op jit(solution)/shard_map/apply/pallas_call | solution.py:509
  98.6 2.5 %apply.7 = bf16[1024,1024]{1,0:T(8,128)(2,1)} custom-call(s32[3]{0:T(128)S(1)} %pad_add_fusion.ids, bf16[2,2,96,256]{3,2,1,0:T(8,128)(2,1)S(1)} %collective-permute-done.26.near_low, bf16[2,2,96,256]{3,2,1,0:T(8,128)(2,1)S(1)} %collective-permute-done.30.near_high, ...), custom_call_target="tpu_custom_call", output_to_operand_aliasing={{}: (6, {})} | custom-call | flops 805306368 | bytes 1048576 | tf_op jit(solution)/shard_map/apply/pallas_call | solution.py:509
  (57 shorter events, 0.5 us)
Async XLA Ops:
  0.7 1.6 %copy-start.3 = (bf16[1024,1024]{1,0:T(8,128)(2,1)S(1)}, bf16[1024,1024]{1,0:T(8,128)(2,1)}, u32[]{:S(2)}) copy-start(bf16[1024,1024]{1,0:T(8,128)(2,1)} %x_ref.2) | copy-start | bytes 6291460
  2.3 1.5 %copy-start.1 = (f32[4,16,1024]{2,1,0:T(8,128)S(1)}, f32[4,16,1024]{2,1,0:T(8,128)}, u32[]{:S(2)}) copy-start(f32[4,16,1024]{2,1,0:T(8,128)} %in_ref.1) | copy-start | bytes 786436
  2.3 1.5 %copy-start.2 = (f32[4,32,256]{2,1,0:T(8,128)S(1)}, f32[4,32,256]{2,1,0:T(8,128)}, u32[]{:S(2)}) copy-start(f32[4,32,256]{2,1,0:T(8,128)} %out_ref.1) | copy-start | bytes 393220
  2.3 3.6 %copy-start.4 = (bf16[1024,1024]{1,0:T(8,128)(2,1)S(1)}, bf16[1024,1024]{1,0:T(8,128)(2,1)}, u32[]{:S(2)}) copy-start(bf16[1024,1024]{1,0:T(8,128)(2,1)} %x_ref.3) | copy-start | bytes 6291460
  2.3 3.6 %copy-start.5 = (f32[4,1024]{1,0:T(4,128)S(1)}, f32[4,1024]{1,0:T(4,128)}, u32[]{:S(2)}) copy-start(f32[4,1024]{1,0:T(4,128)} %rest_0_.1) | copy-start | bytes 49156
  4.4 1.5 %collective-permute-start = (f32[2,96,256]{2,1,0:T(8,128)S(1)}, f32[2,96,256]{2,1,0:T(8,128)S(1)}, u32[]{:S(2)}, u32[]{:S(2)}) collective-permute-start(f32[2,96,256]{2,1,0:T(8,128)S(1)} %get-tuple-element.46), channel_id=1, source_target_pairs={{0,1},{1,0},{2,3},{3,2},{4,5},{5,4},{6,7},{7,6},{8,9},{9,8},{10,11... | collective-permute-start | bytes 589832 | tf_op jit(solution)/shard_map/ppermute | solution.py:140
  4.6 9.7 %collective-permute-start.2 = (bf16[1024,512]{1,0:T(8,128)(2,1)S(1)}, bf16[1024,512]{1,0:T(8,128)(2,1)S(1)}, u32[]{:S(2)}, u32[]{:S(2)}) collective-permute-start(bf16[1024,512]{1,0:T(8,128)(2,1)S(1)} %get-tuple-element.47), channel_id=1, source_target_pairs={{0,1},{1,0},{2,3},{3,2},{4,5},{5,4},{6,7},{7,6},{8,9},{9,8},{10,11... | collective-permute-start | bytes 3145736 | tf_op jit(solution)/shard_map/ppermute | solution.py:140
  8.2 6.0 %collective-permute-start.3 = (bf16[1024,512]{1,0:T(8,128)(2,1)S(1)}, bf16[1024,512]{1,0:T(8,128)(2,1)S(1)}, u32[]{:S(2)}, u32[]{:S(2)}) collective-permute-start(bf16[1024,512]{1,0:T(8,128)(2,1)S(1)} %get-tuple-element.49), channel_id=1, source_target_pairs={{0,1},{1,0},{2,3},{3,2},{4,5},{5,4},{6,7},{7,6},{8,9},{9,8},{10,11... | collective-permute-start | bytes 3145736 | tf_op jit(solution)/shard_map/ppermute | solution.py:140
  8.5 5.8 %collective-permute-start.1 = (bf16[2,96,256]{2,1,0:T(8,128)(2,1)S(1)}, bf16[2,96,256]{2,1,0:T(8,128)(2,1)S(1)}, u32[]{:S(2)}, u32[]{:S(2)}) collective-permute-start(bf16[2,96,256]{2,1,0:T(8,128)(2,1)S(1)} %get-tuple-element.52), channel_id=1, source_target_pairs={{0,4},{1,5},{2,6},{3,7},{4,0},{5,1},{6,2},{7,3},{8,12},{9,13},{10,... | collective-permute-start | bytes 294920 | tf_op jit(solution)/shard_map/ppermute | solution.py:140
  11.2 7.1 %collective-permute-start.6 = (bf16[2,96,256]{2,1,0:T(8,128)(2,1)S(1)}, bf16[2,96,256]{2,1,0:T(8,128)(2,1)S(1)}, u32[]{:S(2)}, u32[]{:S(2)}) collective-permute-start(bf16[2,96,256]{2,1,0:T(8,128)(2,1)S(1)} %get-tuple-element.52), channel_id=1, source_target_pairs={{0,12},{1,13},{2,14},{3,15},{4,8},{5,9},{6,10},{7,11},{8,4},{9,5},... | collective-permute-start | bytes 294920 | tf_op jit(solution)/shard_map/ppermute | solution.py:140
  13.4 9.6 %collective-permute-start.5 = (bf16[2,96,256]{2,1,0:T(8,128)(2,1)S(1)}, bf16[2,96,256]{2,1,0:T(8,128)(2,1)S(1)}, u32[]{:S(2)}, u32[]{:S(2)}) collective-permute-start(bf16[2,96,256]{2,1,0:T(8,128)(2,1)S(1)} %get-tuple-element.52), channel_id=1, source_target_pairs={{0,8},{1,9},{2,10},{3,11},{4,12},{5,13},{6,14},{7,15},{8,0},{9,1},... | collective-permute-start | bytes 294920 | tf_op jit(solution)/shard_map/ppermute | solution.py:140
  14.3 8.7 %collective-permute-start.7 = (bf16[2,2,96,256]{3,2,1,0:T(8,128)(2,1)S(1)}, bf16[2,2,96,256]{3,2,1,0:T(8,128)(2,1)S(1)}, u32[]{:S(2)}, u32[]{:S(2)}) collective-permute-start(bf16[2,2,96,256]{3,2,1,0:T(8,128)(2,1)S(1)} %pad_maximum_fusion.near_low), channel_id=1, source_target_pairs={{0,2},{1,3},{2,0},{3,1},{4,6},{5,7},{6,4},{7,5},{8,10},{9,11},{10,... | collective-permute-start | bytes 589832 | tf_op jit(solution)/shard_map/ppermute | solution.py:140
  15.5 8.8 %collective-permute-start.4 = (bf16[2,2,96,256]{3,2,1,0:T(8,128)(2,1)S(1)}, bf16[2,2,96,256]{3,2,1,0:T(8,128)(2,1)S(1)}, u32[]{:S(2)}, u32[]{:S(2)}) collective-permute-start(bf16[2,2,96,256]{3,2,1,0:T(8,128)(2,1)S(1)} %pad_maximum_fusion.near_low), channel_id=1, source_target_pairs={{0,16},{16,0},{1,17},{17,1},{2,18},{18,2},{3,19},{19,3},{4,20},{20... | collective-permute-start | bytes 589832 | tf_op jit(solution)/shard_map/ppermute | solution.py:144
  23.0 5.9 %collective-permute-start.9 = (bf16[2,2,96,256]{3,2,1,0:T(8,128)(2,1)S(1)}, bf16[2,2,96,256]{3,2,1,0:T(8,128)(2,1)S(1)}, u32[]{:S(2)}, u32[]{:S(2)}) collective-permute-start(bf16[2,2,96,256]{3,2,1,0:T(8,128)(2,1)S(1)} %collective-permute-done.7.far_low), channel_id=1, source_target_pairs={{0,16},{16,0},{1,17},{17,1},{2,18},{18,2},{3,19},{19,3},{4,20},{20... | collective-permute-start | bytes 589832 | tf_op jit(solution)/shard_map/ppermute | solution.py:144
  24.3 5.5 %collective-permute-start.10 = (bf16[2,2,96,256]{3,2,1,0:T(8,128)(2,1)S(1)}, bf16[2,2,96,256]{3,2,1,0:T(8,128)(2,1)S(1)}, u32[]{:S(2)}, u32[]{:S(2)}) collective-permute-start(bf16[2,2,96,256]{3,2,1,0:T(8,128)(2,1)S(1)} %pad_maximum_fusion.1.near_high), channel_id=1, source_target_pairs={{0,2},{1,3},{2,0},{3,1},{4,6},{5,7},{6,4},{7,5},{8,10},{9,11},{10,... | collective-permute-start | bytes 589832 | tf_op jit(solution)/shard_map/ppermute | solution.py:140
  25.5 11.8 %collective-permute-start.8 = (bf16[2,2,96,256]{3,2,1,0:T(8,128)(2,1)S(1)}, bf16[2,2,96,256]{3,2,1,0:T(8,128)(2,1)S(1)}, u32[]{:S(2)}, u32[]{:S(2)}) collective-permute-start(bf16[2,2,96,256]{3,2,1,0:T(8,128)(2,1)S(1)} %pad_maximum_fusion.1.near_high), channel_id=1, source_target_pairs={{0,16},{16,0},{1,17},{17,1},{2,18},{18,2},{3,19},{19,3},{4,20},{20... | collective-permute-start | bytes 589832 | tf_op jit(solution)/shard_map/ppermute | solution.py:144
  29.8 7.5 %collective-permute-start.11 = (bf16[2,2,96,256]{3,2,1,0:T(8,128)(2,1)S(1)}, bf16[2,2,96,256]{3,2,1,0:T(8,128)(2,1)S(1)}, u32[]{:S(2)}, u32[]{:S(2)}) collective-permute-start(bf16[2,2,96,256]{3,2,1,0:T(8,128)(2,1)S(1)} %collective-permute-done.10.far_high), channel_id=1, source_target_pairs={{0,16},{16,0},{1,17},{17,1},{2,18},{18,2},{3,19},{19,3},{4,20},{20... | collective-permute-start | bytes 589832 | tf_op jit(solution)/shard_map/ppermute | solution.py:144
  35.8 8.7 %collective-permute-start.17 = (bf16[2,2,96,256]{3,2,1,0:T(8,128)(2,1)S(1)}, bf16[2,2,96,256]{3,2,1,0:T(8,128)(2,1)S(1)}, u32[]{:S(2)}, u32[]{:S(2)}) collective-permute-start(bf16[2,2,96,256]{3,2,1,0:T(8,128)(2,1)S(1)} %get-tuple-element.67), channel_id=1, source_target_pairs={{0,2},{1,3},{2,0},{3,1},{4,6},{5,7},{6,4},{7,5},{8,10},{9,11},{10,... | collective-permute-start | bytes 589832 | tf_op jit(solution)/shard_map/ppermute | solution.py:140
  37.1 7.5 %collective-permute-start.19 = (bf16[2,2,96,256]{3,2,1,0:T(8,128)(2,1)S(1)}, bf16[2,2,96,256]{3,2,1,0:T(8,128)(2,1)S(1)}, u32[]{:S(2)}, u32[]{:S(2)}) collective-permute-start(bf16[2,2,96,256]{3,2,1,0:T(8,128)(2,1)S(1)} %get-tuple-element.70), channel_id=1, source_target_pairs={{0,2},{1,3},{2,0},{3,1},{4,6},{5,7},{6,4},{7,5},{8,10},{9,11},{10,... | collective-permute-start | bytes 589832 | tf_op jit(solution)/shard_map/ppermute | solution.py:140
  43.2 11.8 %collective-permute-start.12 = (bf16[2,2,96,256]{3,2,1,0:T(8,128)(2,1)S(1)}, bf16[2,2,96,256]{3,2,1,0:T(8,128)(2,1)S(1)}, u32[]{:S(2)}, u32[]{:S(2)}) collective-permute-start(bf16[2,2,96,256]{3,2,1,0:T(8,128)(2,1)S(1)} %get-tuple-element.57), channel_id=1, source_target_pairs={{0,2},{1,3},{2,0},{3,1},{4,6},{5,7},{6,4},{7,5},{8,10},{9,11},{10,... | collective-permute-start | bytes 589832 | tf_op jit(solution)/shard_map/ppermute | solution.py:140
  44.6 4.0 %collective-permute-start.18 = (bf16[2,96,256]{2,1,0:T(8,128)(2,1)S(1)}, bf16[2,96,256]{2,1,0:T(8,128)(2,1)S(1)}, u32[]{:S(2)}, u32[]{:S(2)}) collective-permute-start(bf16[2,96,256]{2,1,0:T(8,128)(2,1)S(1)} %get-tuple-element.69), channel_id=1, source_target_pairs={{0,4},{1,5},{2,6},{3,7},{4,0},{5,1},{6,2},{7,3},{8,12},{9,13},{10,... | collective-permute-start | bytes 294920 | tf_op jit(solution)/shard_map/ppermute | solution.py:140
  44.7 4.5 %collective-permute-start.20 = (bf16[2,96,256]{2,1,0:T(8,128)(2,1)S(1)}, bf16[2,96,256]{2,1,0:T(8,128)(2,1)S(1)}, u32[]{:S(2)}, u32[]{:S(2)}) collective-permute-start(bf16[2,96,256]{2,1,0:T(8,128)(2,1)S(1)} %get-tuple-element.71), channel_id=1, source_target_pairs={{0,8},{1,9},{2,10},{3,11},{4,12},{5,13},{6,14},{7,15},{8,0},{9,1},... | collective-permute-start | bytes 294920 | tf_op jit(solution)/shard_map/ppermute | solution.py:140
  46.0 5.5 %collective-permute-start.21 = (bf16[2,96,256]{2,1,0:T(8,128)(2,1)S(1)}, bf16[2,96,256]{2,1,0:T(8,128)(2,1)S(1)}, u32[]{:S(2)}, u32[]{:S(2)}) collective-permute-start(bf16[2,96,256]{2,1,0:T(8,128)(2,1)S(1)} %get-tuple-element.72), channel_id=1, source_target_pairs={{0,12},{1,13},{2,14},{3,15},{4,8},{5,9},{6,10},{7,11},{8,4},{9,5},... | collective-permute-start | bytes 294920 | tf_op jit(solution)/shard_map/ppermute | solution.py:140
  48.3 8.5 %collective-permute-start.14 = (bf16[2,2,96,256]{3,2,1,0:T(8,128)(2,1)S(1)}, bf16[2,2,96,256]{3,2,1,0:T(8,128)(2,1)S(1)}, u32[]{:S(2)}, u32[]{:S(2)}) collective-permute-start(bf16[2,2,96,256]{3,2,1,0:T(8,128)(2,1)S(1)} %get-tuple-element.60), channel_id=1, source_target_pairs={{0,2},{1,3},{2,0},{3,1},{4,6},{5,7},{6,4},{7,5},{8,10},{9,11},{10,... | collective-permute-start | bytes 589832 | tf_op jit(solution)/shard_map/ppermute | solution.py:140
  51.6 6.3 %collective-permute-start.22 = (bf16[2,96,256]{2,1,0:T(8,128)(2,1)S(1)}, bf16[2,96,256]{2,1,0:T(8,128)(2,1)S(1)}, u32[]{:S(2)}, u32[]{:S(2)}) collective-permute-start(bf16[2,96,256]{2,1,0:T(8,128)(2,1)S(1)} %get-tuple-element.73), channel_id=1, source_target_pairs={{0,4},{1,5},{2,6},{3,7},{4,0},{5,1},{6,2},{7,3},{8,12},{9,13},{10,... | collective-permute-start | bytes 294920 | tf_op jit(solution)/shard_map/ppermute | solution.py:140
  53.1 22.4 %collective-permute-start.25 = (bf16[2,96,256]{2,1,0:T(8,128)(2,1)S(1)}, bf16[2,96,256]{2,1,0:T(8,128)(2,1)S(1)}, u32[]{:S(2)}, u32[]{:S(2)}) collective-permute-start(bf16[2,96,256]{2,1,0:T(8,128)(2,1)S(1)} %get-tuple-element.73), channel_id=1, source_target_pairs={{0,12},{1,13},{2,14},{3,15},{4,8},{5,9},{6,10},{7,11},{8,4},{9,5},... | collective-permute-start | bytes 294920 | tf_op jit(solution)/shard_map/ppermute | solution.py:140
  54.8 20.7 %collective-permute-start.24 = (bf16[2,96,256]{2,1,0:T(8,128)(2,1)S(1)}, bf16[2,96,256]{2,1,0:T(8,128)(2,1)S(1)}, u32[]{:S(2)}, u32[]{:S(2)}) collective-permute-start(bf16[2,96,256]{2,1,0:T(8,128)(2,1)S(1)} %get-tuple-element.73), channel_id=1, source_target_pairs={{0,8},{1,9},{2,10},{3,11},{4,12},{5,13},{6,14},{7,15},{8,0},{9,1},... | collective-permute-start | bytes 294920 | tf_op jit(solution)/shard_map/ppermute | solution.py:140
  55.0 34.4 %copy-start = (bf16[1024,1024]{1,0:T(8,128)(2,1)S(1)}, bf16[1024,1024]{1,0:T(8,128)(2,1)}, u32[]{:S(2)}) copy-start(bf16[1024,1024]{1,0:T(8,128)(2,1)} %q_ref.7) | copy-start | bytes 6291460
  55.0 4.9 %collective-permute-start.13 = (bf16[2,96,256]{2,1,0:T(8,128)(2,1)S(1)}, bf16[2,96,256]{2,1,0:T(8,128)(2,1)S(1)}, u32[]{:S(2)}, u32[]{:S(2)}) collective-permute-start(bf16[2,96,256]{2,1,0:T(8,128)(2,1)S(1)} %get-tuple-element.59), channel_id=1, source_target_pairs={{0,4},{1,5},{2,6},{3,7},{4,0},{5,1},{6,2},{7,3},{8,12},{9,13},{10,... | collective-permute-start | bytes 294920 | tf_op jit(solution)/shard_map/ppermute | solution.py:140
  56.8 9.9 %collective-permute-start.15 = (bf16[2,96,256]{2,1,0:T(8,128)(2,1)S(1)}, bf16[2,96,256]{2,1,0:T(8,128)(2,1)S(1)}, u32[]{:S(2)}, u32[]{:S(2)}) collective-permute-start(bf16[2,96,256]{2,1,0:T(8,128)(2,1)S(1)} %get-tuple-element.61), channel_id=1, source_target_pairs={{0,8},{1,9},{2,10},{3,11},{4,12},{5,13},{6,14},{7,15},{8,0},{9,1},... | collective-permute-start | bytes 294920 | tf_op jit(solution)/shard_map/ppermute | solution.py:140
  57.9 8.8 %collective-permute-start.16 = (bf16[2,96,256]{2,1,0:T(8,128)(2,1)S(1)}, bf16[2,96,256]{2,1,0:T(8,128)(2,1)S(1)}, u32[]{:S(2)}, u32[]{:S(2)}) collective-permute-start(bf16[2,96,256]{2,1,0:T(8,128)(2,1)S(1)} %get-tuple-element.62), channel_id=1, source_target_pairs={{0,12},{1,13},{2,14},{3,15},{4,8},{5,9},{6,10},{7,11},{8,4},{9,5},... | collective-permute-start | bytes 294920 | tf_op jit(solution)/shard_map/ppermute | solution.py:140
  59.9 22.9 %collective-permute-start.36 = (bf16[2,2,96,256]{3,2,1,0:T(8,128)(2,1)S(1)}, bf16[2,2,96,256]{3,2,1,0:T(8,128)(2,1)S(1)}, u32[]{:S(2)}, u32[]{:S(2)}) collective-permute-start(bf16[2,2,96,256]{3,2,1,0:T(8,128)(2,1)S(1)} %pad_maximum_fusion.2.near_low), channel_id=1, source_target_pairs={{0,2},{1,3},{2,0},{3,1},{4,6},{5,7},{6,4},{7,5},{8,10},{9,11},{10,... | collective-permute-start | bytes 589832 | tf_op jit(solution)/shard_map/ppermute | solution.py:140
  66.9 9.4 %collective-permute-start.23 = (bf16[2,96,256]{2,1,0:T(8,128)(2,1)S(1)}, bf16[2,96,256]{2,1,0:T(8,128)(2,1)S(1)}, u32[]{:S(2)}, u32[]{:S(2)}) collective-permute-start(bf16[2,96,256]{2,1,0:T(8,128)(2,1)S(1)} %get-tuple-element.76), channel_id=1, source_target_pairs={{0,4},{1,5},{2,6},{3,7},{4,0},{5,1},{6,2},{7,3},{8,12},{9,13},{10,... | collective-permute-start | bytes 294920 | tf_op jit(solution)/shard_map/ppermute | solution.py:140
  71.1 7.1 %collective-permute-start.29 = (f32[2,96,256]{2,1,0:T(8,128)S(1)}, f32[2,96,256]{2,1,0:T(8,128)S(1)}, u32[]{:S(2)}, u32[]{:S(2)}) collective-permute-start(f32[2,96,256]{2,1,0:T(8,128)S(1)} %pad_maximum_fusion.6), channel_id=1, source_target_pairs={{0,1},{1,0},{2,3},{3,2},{4,5},{5,4},{6,7},{7,6},{8,9},{9,8},{10,11... | collective-permute-start | bytes 589832 | tf_op jit(solution)/shard_map/ppermute | solution.py:140
  75.5 7.4 %collective-permute-start.38 = (bf16[2,2,96,256]{3,2,1,0:T(8,128)(2,1)S(1)}, bf16[2,2,96,256]{3,2,1,0:T(8,128)(2,1)S(1)}, u32[]{:S(2)}, u32[]{:S(2)}) collective-permute-start(bf16[2,2,96,256]{3,2,1,0:T(8,128)(2,1)S(1)} %pad_maximum_fusion.4.near_high), channel_id=1, source_target_pairs={{0,2},{1,3},{2,0},{3,1},{4,6},{5,7},{6,4},{7,5},{8,10},{9,11},{10,... | collective-permute-start | bytes 589832 | tf_op jit(solution)/shard_map/ppermute | solution.py:140
  76.3 7.3 %collective-permute-start.28 = (bf16[2,96,256]{2,1,0:T(8,128)(2,1)S(1)}, bf16[2,96,256]{2,1,0:T(8,128)(2,1)S(1)}, u32[]{:S(2)}, u32[]{:S(2)}) collective-permute-start(bf16[2,96,256]{2,1,0:T(8,128)(2,1)S(1)} %get-tuple-element.76), channel_id=1, source_target_pairs={{0,12},{1,13},{2,14},{3,15},{4,8},{5,9},{6,10},{7,11},{8,4},{9,5},... | collective-permute-start | bytes 294920 | tf_op jit(solution)/shard_map/ppermute | solution.py:140
  78.3 8.5 %collective-permute-start.27 = (bf16[2,96,256]{2,1,0:T(8,128)(2,1)S(1)}, bf16[2,96,256]{2,1,0:T(8,128)(2,1)S(1)}, u32[]{:S(2)}, u32[]{:S(2)}) collective-permute-start(bf16[2,96,256]{2,1,0:T(8,128)(2,1)S(1)} %get-tuple-element.76), channel_id=1, source_target_pairs={{0,8},{1,9},{2,10},{3,11},{4,12},{5,13},{6,14},{7,15},{8,0},{9,1},... | collective-permute-start | bytes 294920 | tf_op jit(solution)/shard_map/ppermute | solution.py:140
  78.3 10.3 %collective-permute-start.34 = (bf16[2,2,96,256]{3,2,1,0:T(8,128)(2,1)S(1)}, bf16[2,2,96,256]{3,2,1,0:T(8,128)(2,1)S(1)}, u32[]{:S(2)}, u32[]{:S(2)}) collective-permute-start(bf16[2,2,96,256]{3,2,1,0:T(8,128)(2,1)S(1)} %pad_maximum_fusion.2.near_low), channel_id=1, source_target_pairs={{0,1},{1,0},{2,3},{3,2},{4,5},{5,4},{6,7},{7,6},{8,9},{9,8},{10,11... | collective-permute-start | bytes 589832 | tf_op jit(solution)/shard_map/ppermute | solution.py:140
  82.8 9.1 %collective-permute-start.35 = (bf16[2,2,96,256]{3,2,1,0:T(8,128)(2,1)S(1)}, bf16[2,2,96,256]{3,2,1,0:T(8,128)(2,1)S(1)}, u32[]{:S(2)}, u32[]{:S(2)}) collective-permute-start(bf16[2,2,96,256]{3,2,1,0:T(8,128)(2,1)S(1)} %pad_maximum_fusion.4.near_high), channel_id=1, source_target_pairs={{0,1},{1,0},{2,3},{3,2},{4,5},{5,4},{6,7},{7,6},{8,9},{9,8},{10,11... | collective-permute-start | bytes 589832 | tf_op jit(solution)/shard_map/ppermute | solution.py:140
  82.8 9.5 %collective-permute-start.31 = (bf16[2,2,96,256]{3,2,1,0:T(8,128)(2,1)S(1)}, bf16[2,2,96,256]{3,2,1,0:T(8,128)(2,1)S(1)}, u32[]{:S(2)}, u32[]{:S(2)}) collective-permute-start(bf16[2,2,96,256]{3,2,1,0:T(8,128)(2,1)S(1)} %pad_maximum_fusion.3.near_low), channel_id=1, source_target_pairs={{0,2},{1,3},{2,0},{3,1},{4,6},{5,7},{6,4},{7,5},{8,10},{9,11},{10,... | collective-permute-start | bytes 589832 | tf_op jit(solution)/shard_map/ppermute | solution.py:140
  83.6 8.9 %collective-permute-start.37 = (bf16[2,2,96,256]{3,2,1,0:T(8,128)(2,1)S(1)}, bf16[2,2,96,256]{3,2,1,0:T(8,128)(2,1)S(1)}, u32[]{:S(2)}, u32[]{:S(2)}) collective-permute-start(bf16[2,2,96,256]{3,2,1,0:T(8,128)(2,1)S(1)} %collective-permute-done.36.far_low), channel_id=1, source_target_pairs={{0,1},{1,0},{2,3},{3,2},{4,5},{5,4},{6,7},{7,6},{8,9},{9,8},{10,11... | collective-permute-start | bytes 589832 | tf_op jit(solution)/shard_map/ppermute | solution.py:140
  86.8 6.1 %collective-permute-start.39 = (bf16[2,2,96,256]{3,2,1,0:T(8,128)(2,1)S(1)}, bf16[2,2,96,256]{3,2,1,0:T(8,128)(2,1)S(1)}, u32[]{:S(2)}, u32[]{:S(2)}) collective-permute-start(bf16[2,2,96,256]{3,2,1,0:T(8,128)(2,1)S(1)} %collective-permute-done.38.far_high), channel_id=1, source_target_pairs={{0,1},{1,0},{2,3},{3,2},{4,5},{5,4},{6,7},{7,6},{8,9},{9,8},{10,11... | collective-permute-start | bytes 589832 | tf_op jit(solution)/shard_map/ppermute | solution.py:140
  88.6 6.7 %collective-permute-start.33 = (bf16[2,2,96,256]{3,2,1,0:T(8,128)(2,1)S(1)}, bf16[2,2,96,256]{3,2,1,0:T(8,128)(2,1)S(1)}, u32[]{:S(2)}, u32[]{:S(2)}) collective-permute-start(bf16[2,2,96,256]{3,2,1,0:T(8,128)(2,1)S(1)} %pad_maximum_fusion.5.near_high), channel_id=1, source_target_pairs={{0,2},{1,3},{2,0},{3,1},{4,6},{5,7},{6,4},{7,5},{8,10},{9,11},{10,... | collective-permute-start | bytes 589832 | tf_op jit(solution)/shard_map/ppermute | solution.py:140
  92.0 6.5 %collective-permute-start.26 = (bf16[2,2,96,256]{3,2,1,0:T(8,128)(2,1)S(1)}, bf16[2,2,96,256]{3,2,1,0:T(8,128)(2,1)S(1)}, u32[]{:S(2)}, u32[]{:S(2)}) collective-permute-start(bf16[2,2,96,256]{3,2,1,0:T(8,128)(2,1)S(1)} %pad_maximum_fusion.3.near_low), channel_id=1, source_target_pairs={{0,1},{1,0},{2,3},{3,2},{4,5},{5,4},{6,7},{7,6},{8,9},{9,8},{10,11... | collective-permute-start | bytes 589832 | tf_op jit(solution)/shard_map/ppermute | solution.py:140
  92.3 6.2 %collective-permute-start.30 = (bf16[2,2,96,256]{3,2,1,0:T(8,128)(2,1)S(1)}, bf16[2,2,96,256]{3,2,1,0:T(8,128)(2,1)S(1)}, u32[]{:S(2)}, u32[]{:S(2)}) collective-permute-start(bf16[2,2,96,256]{3,2,1,0:T(8,128)(2,1)S(1)} %pad_maximum_fusion.5.near_high), channel_id=1, source_target_pairs={{0,1},{1,0},{2,3},{3,2},{4,5},{5,4},{6,7},{7,6},{8,9},{9,8},{10,11... | collective-permute-start | bytes 589832 | tf_op jit(solution)/shard_map/ppermute | solution.py:140
  92.5 6.0 %collective-permute-start.32 = (bf16[2,2,96,256]{3,2,1,0:T(8,128)(2,1)S(1)}, bf16[2,2,96,256]{3,2,1,0:T(8,128)(2,1)S(1)}, u32[]{:S(2)}, u32[]{:S(2)}) collective-permute-start(bf16[2,2,96,256]{3,2,1,0:T(8,128)(2,1)S(1)} %collective-permute-done.31.far_low), channel_id=1, source_target_pairs={{0,1},{1,0},{2,3},{3,2},{4,5},{5,4},{6,7},{7,6},{8,9},{9,8},{10,11... | collective-permute-start | bytes 589832 | tf_op jit(solution)/shard_map/ppermute | solution.py:140
  95.3 3.2 %collective-permute-start.40 = (bf16[2,2,96,256]{3,2,1,0:T(8,128)(2,1)S(1)}, bf16[2,2,96,256]{3,2,1,0:T(8,128)(2,1)S(1)}, u32[]{:S(2)}, u32[]{:S(2)}) collective-permute-start(bf16[2,2,96,256]{3,2,1,0:T(8,128)(2,1)S(1)} %collective-permute-done.33.far_high), channel_id=1, source_target_pairs={{0,1},{1,0},{2,3},{3,2},{4,5},{5,4},{6,7},{7,6},{8,9},{9,8},{10,11... | collective-permute-start | bytes 589832 | tf_op jit(solution)/shard_map/ppermute | solution.py:140

commit v12 on v11

--- a/solution.py
+++ b/solution.py
@@ -566,17 +566,17 @@
 
     k_own, k_send = prepare(ids, keys, None, heads, None, "keys")
     own, theirs = pack(after(ids, k_own), fast_in, fast_out)
-    got = swap(theirs, 1)
-    later = after(ids, got)
-    v_own, v_send = prepare(later, values, step_size, heads, block_root, "values")
-    master_one, master_two, shard = pair(own, after(got, k_send, v_send))
+    master_one, master_two, shard = pair(own, swap(theirs, 1))
     masters = (master_one, master_two)
-    k_got, v_got = swap(k_send, 1), swap(v_send, 1)
+    k_got = swap(k_send, 1)
     z1, z3, z2 = swap(shard, 4), swap(shard, 12), swap(shard, 8)
-    near_low = after(jnp.stack([shard, z1]), k_got, v_got)
+    near_low = after(jnp.stack([shard, z1]), k_got)
     far_low, other_near_low = swap(near_low, 2), swap_parts(near_low)
     near_high = after(jnp.stack([z2, z3]), far_low, other_near_low)
     far_high = swap(near_high, 2)
+    later = after(ids, near_high)
+    v_own, v_send = prepare(later, values, step_size, heads, block_root, "values")
+    v_got = swap(v_send, 1)
     first = (near_low, near_high, far_low, far_high)
     second = (other_near_low, *(swap_parts(piece) for piece in first[1:]))
 

time: 101 us -> 107 us (1.059)
  starting transfers between devices: 47.5 us -> 50.3 us
  waiting for transfers between devices: 23.2 us -> 25.6 us
    ppermute x37, starting transfers between devices: 44.4 us -> 47.4 us  [swap(): lax.ppermute(value, 'tok', [(place, place ^ bits) for place in range(coun...]
    ppermute x37, waiting for transfers between devices: 20 us -> 21.8 us  [swap(): lax.ppermute(value, 'tok', [(place, place ^ bits) for place in range(coun...]
  transfers between devices with their start and end apart: 41 -> 41, of which waited for: 11 -> 11; matrix products, arithmetic and copies ran while one was open for 0% -> 0% of each run, Pallas kernels for 23% -> 20%
where the time goes in v12:
time: 107 us; the launch traced here: 106 us
  starting transfers between devices  50.3 us (47%)
  Pallas kernels  27.6 us (26%)
  waiting for transfers between devices  25.6 us (24%)
  local copies, waits for them, and re-layouts  1.63 us (2%)
  between operations  1.09 us (1%)
    ppermute x37, starting transfers between devices, swap(): lax.ppermute(value, 'tok', [(place, place ^ bits) for place in range(coun...  47.4 us
    ppermute x37, waiting for transfers between devices, swap(): lax.ppermute(value, 'tok', [(place, place ^ bits) for place in range(coun...  21.8 us
    pallas_call x2, Pallas kernels, increments(): pl.pallas_call(increments_kernel, grid_spec=pltpu.PrefetchScalarGridSpec(...  11.5 us
    pallas_call x4, Pallas kernels, apply_fast(): pl.pallas_call(functools.partial(apply_kernel, order, other), grid_spec=p...  9.98 us
    pallas_call x2, Pallas kernels, prepare(): pl.pallas_call(functools.partial(prepare_kernel, heads, block_root), grid...  3.78 us
    ppermute x4, waiting for transfers between devices, swap_parts(): return lax.ppermute(value, 'parts', [(0, 1), (1, 0)])  3.77 us
    ppermute x4, starting transfers between devices, swap_parts(): return lax.ppermute(value, 'parts', [(0, 1), (1, 0)])  2.93 us
  transfers between devices with their start and end apart: 41, of which 11 were waited for; matrix products, arithmetic and copies ran while one was open for 0% of the time, Pallas kernels for 20%

profile of v12, /device:TPU:1, one launch (start us, length us, event | category | flops | bytes accessed | tf_op | source)
XLA Modules:
  0.0 106.4 jit_solution(14914411994261072377)
XLA Ops:
  0.6 0.1 pad_add_fusion.ids
  0.7 1.6 %copy-done.3 = bf16[1024,1024]{1,0:T(8,128)(2,1)S(1)} copy-done((bf16[1024,1024]{1,0:T(8,128)(2,1)S(1)}, bf16[1024,1024]{1,0:T(8,128)(2,1)}, u32[]{:S(2)}) %copy-start.3) | copy-done | bytes 2097176
  2.3 1.5 %keys.1 = (bf16[1024,512]{1,0:T(8,128)(2,1)S(1)}, bf16[1024,512]{1,0:T(8,128)(2,1)S(1)}) custom-call(s32[3]{0:T(128)S(1)} %pad_add_fusion.ids, bf16[1024,1024]{1,0:T(8,128)(2,1)S(1)} %copy-done.3), custom_call_target="tpu_custom_call" | custom-call | flops 5242880000 | bytes 41943040 | tf_op jit(solution)/shard_map/keys/pallas_call | solution.py:248
  3.8 0.1 collective-permute-start.2
  4.0 0.6 pack.1
  4.6 0.5 collective-permute-start
  5.1 1.8 %collective-permute-done.got = f32[2,96,256]{2,1,0:T(8,128)S(1)} collective-permute-done((f32[2,96,256]{2,1,0:T(8,128)S(1)}, f32[2,96,256]{2,1,0:T(8,128)S(1)}, u32[]{:S(2)}, u32[]{:S(2)}) %collective-permute-start) | collective-permute-done | bytes 196640 | tf_op jit(solution)/shard_map/ppermute | solution.py:140
  6.9 2.5 %collective-permute-start.1 = (bf16[2,96,256]{2,1,0:T(8,128)(2,1)S(1)}, bf16[2,96,256]{2,1,0:T(8,128)(2,1)S(1)}, u32[]{:S(2)}, u32[]{:S(2)}) collective-permute-start(bf16[2,96,256]{2,1,0:T(8,128)(2,1)S(1)} %get-tuple-element.47), channel_id=1, source_target_pairs={{0,4},{1,5},{2,6},{3,7},{4,0},{5,1},{6,2},{7,3},{8,12},{9,13},{10,... | collective-permute-start | bytes 294920 | tf_op jit(solution)/shard_map/ppermute | solution.py:140
  9.4 2.2 %collective-permute-start.5 = (bf16[2,96,256]{2,1,0:T(8,128)(2,1)S(1)}, bf16[2,96,256]{2,1,0:T(8,128)(2,1)S(1)}, u32[]{:S(2)}, u32[]{:S(2)}) collective-permute-start(bf16[2,96,256]{2,1,0:T(8,128)(2,1)S(1)} %get-tuple-element.47), channel_id=1, source_target_pairs={{0,12},{1,13},{2,14},{3,15},{4,8},{5,9},{6,10},{7,11},{8,4},{9,5},... | collective-permute-start | bytes 294920 | tf_op jit(solution)/shard_map/ppermute | solution.py:140
  11.6 0.1 collective-permute-start.4
  11.7 0.6 collective-permute-done.1
  12.3 1.1 %collective-permute-start.3 = (bf16[2,2,96,256]{3,2,1,0:T(8,128)(2,1)S(1)}, bf16[2,2,96,256]{3,2,1,0:T(8,128)(2,1)S(1)}, u32[]{:S(2)}, u32[]{:S(2)}) collective-permute-start(bf16[2,2,96,256]{3,2,1,0:T(8,128)(2,1)S(1)} %pad_maximum_fusion.near_low), channel_id=1, source_target_pairs={{0,16},{16,0},{1,17},{17,1},{2,18},{18,2},{3,19},{19,3},{4,20},{20... | collective-permute-start | bytes 589832 | tf_op jit(solution)/shard_map/ppermute | solution.py:144
  13.4 1.2 %collective-permute-start.6 = (bf16[2,2,96,256]{3,2,1,0:T(8,128)(2,1)S(1)}, bf16[2,2,96,256]{3,2,1,0:T(8,128)(2,1)S(1)}, u32[]{:S(2)}, u32[]{:S(2)}) collective-permute-start(bf16[2,2,96,256]{3,2,1,0:T(8,128)(2,1)S(1)} %pad_maximum_fusion.near_low), channel_id=1, source_target_pairs={{0,2},{1,3},{2,0},{3,1},{4,6},{5,7},{6,4},{7,5},{8,10},{9,11},{10,... | collective-permute-start | bytes 589832 | tf_op jit(solution)/shard_map/ppermute | solution.py:140
  14.6 1.6 %collective-permute-done.5 = bf16[2,96,256]{2,1,0:T(8,128)(2,1)S(1)} collective-permute-done((bf16[2,96,256]{2,1,0:T(8,128)(2,1)S(1)}, bf16[2,96,256]{2,1,0:T(8,128)(2,1)S(1)}, u32[]{:S(2)}, u32[]{:S(2)}) %collective-permute-start.5) | collective-permute-done | bytes 98336 | tf_op jit(solution)/shard_map/ppermute | solution.py:140
  16.2 4.8 %collective-permute-done.4 = bf16[2,96,256]{2,1,0:T(8,128)(2,1)S(1)} collective-permute-done((bf16[2,96,256]{2,1,0:T(8,128)(2,1)S(1)}, bf16[2,96,256]{2,1,0:T(8,128)(2,1)S(1)}, u32[]{:S(2)}, u32[]{:S(2)}) %collective-permute-start.4) | collective-permute-done | bytes 98336 | tf_op jit(solution)/shard_map/ppermute | solution.py:140
  21.1 2.3 %values.1 = (bf16[1024,512]{1,0:T(8,128)(2,1)S(1)}, bf16[1024,512]{1,0:T(8,128)(2,1)S(1)}) custom-call(s32[3]{0:T(128)S(1)} %pad_add_fusion.ids, bf16[1024,1024]{1,0:T(8,128)(2,1)S(1)} %copy-done.4, f32[4,1024]{1,0:T(4,128)S(1)} %copy-done.5), custom_call_target="tpu_custom_call" | custom-call | flops 5242880000 | bytes 41943040 | tf_op jit(solution)/shard_map/values/pallas_call | solution.py:248
  23.4 0.8 collective-permute-start.11
  24.2 1.2 %collective-permute-start.8 = (bf16[2,2,96,256]{3,2,1,0:T(8,128)(2,1)S(1)}, bf16[2,2,96,256]{3,2,1,0:T(8,128)(2,1)S(1)}, u32[]{:S(2)}, u32[]{:S(2)}) collective-permute-start(bf16[2,2,96,256]{3,2,1,0:T(8,128)(2,1)S(1)} %collective-permute-done.6.far_low), channel_id=1, source_target_pairs={{0,16},{16,0},{1,17},{17,1},{2,18},{18,2},{3,19},{19,3},{4,20},{20... | collective-permute-start | bytes 589832 | tf_op jit(solution)/shard_map/ppermute | solution.py:144
  25.4 1.2 %collective-permute-start.9 = (bf16[2,2,96,256]{3,2,1,0:T(8,128)(2,1)S(1)}, bf16[2,2,96,256]{3,2,1,0:T(8,128)(2,1)S(1)}, u32[]{:S(2)}, u32[]{:S(2)}) collective-permute-start(bf16[2,2,96,256]{3,2,1,0:T(8,128)(2,1)S(1)} %pad_maximum_fusion.1.near_high), channel_id=1, source_target_pairs={{0,2},{1,3},{2,0},{3,1},{4,6},{5,7},{6,4},{7,5},{8,10},{9,11},{10,... | collective-permute-start | bytes 589832 | tf_op jit(solution)/shard_map/ppermute | solution.py:140
  26.6 0.3 collective-permute-start.7
  26.9 3.8 %collective-permute-done.8.far_low = bf16[2,2,96,256]{3,2,1,0:T(8,128)(2,1)S(1)} collective-permute-done((bf16[2,2,96,256]{3,2,1,0:T(8,128)(2,1)S(1)}, bf16[2,2,96,256]{3,2,1,0:T(8,128)(2,1)S(1)}, u32[]{:S(2)}, u32[]{:S(2)}) %collective-permute-start.8) | collective-permute-done | bytes 196640 | tf_op jit(solution)/shard_map/ppermute | solution.py:144
  30.7 0.9 collective-permute-done.9.far_high
  31.5 0.3 collective-permute-start.10
  31.9 5.6 %increments.3 = (f32[4,2,96,256]{3,2,1,0:T(8,128)S(1)}, bf16[2,2,96,256]{3,2,1,0:T(8,128)(2,1)S(1)}, bf16[2,2,96,256]{3,2,1,0:T(8,128)(2,1)S(1)}) custom-call(s32[3]{0:T(128)S(1)} %pad_add_fusion.ids, bf16[2,2,96,256]{3,2,1,0:T(8,128)(2,1)S(1)} %pad_maximum_fusion.near_low, bf16[2,2,96,256]{3,2,1,0:T(8,128)(2,1)S(1)} %pad_maximum_fusion.1.near_high, ...), custom_call_target="tpu_custom_call" | custom-call | flops 3221225472 | bytes 2097152 | tf_op jit(solution)/shard_map/increments/pallas_call | solution.py:382
  37.5 1.3 %collective-permute-start.17 = (bf16[2,2,96,256]{3,2,1,0:T(8,128)(2,1)S(1)}, bf16[2,2,96,256]{3,2,1,0:T(8,128)(2,1)S(1)}, u32[]{:S(2)}, u32[]{:S(2)}) collective-permute-start(bf16[2,2,96,256]{3,2,1,0:T(8,128)(2,1)S(1)} %get-tuple-element.65), channel_id=1, source_target_pairs={{0,2},{1,3},{2,0},{3,1},{4,6},{5,7},{6,4},{7,5},{8,10},{9,11},{10,... | collective-permute-start | bytes 589832 | tf_op jit(solution)/shard_map/ppermute | solution.py:140
  38.8 0.2 collective-permute-start.19
  39.1 5.8 %increments.2 = (f32[4,2,96,256]{3,2,1,0:T(8,128)S(1)}, bf16[2,2,96,256]{3,2,1,0:T(8,128)(2,1)S(1)}, bf16[2,2,96,256]{3,2,1,0:T(8,128)(2,1)S(1)}) custom-call(s32[3]{0:T(128)S(1)} %pad_add_fusion.ids, bf16[2,2,96,256]{3,2,1,0:T(8,128)(2,1)S(1)} %collective-permute-done.3.near_low, bf16[2,2,96,256]{3,2,1,0:T(8,128)(2,1)S(1)} %collective-permute-done.7.near_high, ...), custom_call_target="tpu_custom_call" | custom-call | flops 3221225472 | bytes 2097152 | tf_op jit(solution)/shard_map/increments/pallas_call | solution.py:382
  44.9 1.3 %collective-permute-start.12 = (bf16[2,2,96,256]{3,2,1,0:T(8,128)(2,1)S(1)}, bf16[2,2,96,256]{3,2,1,0:T(8,128)(2,1)S(1)}, u32[]{:S(2)}, u32[]{:S(2)}) collective-permute-start(bf16[2,2,96,256]{3,2,1,0:T(8,128)(2,1)S(1)} %get-tuple-element.55), channel_id=1, source_target_pairs={{0,2},{1,3},{2,0},{3,1},{4,6},{5,7},{6,4},{7,5},{8,10},{9,11},{10,... | collective-permute-start | bytes 589832 | tf_op jit(solution)/shard_map/ppermute | solution.py:140
  46.2 0.2 collective-permute-start.14
  46.5 0.3 collective-permute-start.18
  46.8 2.5 %collective-permute-start.20 = (bf16[2,96,256]{2,1,0:T(8,128)(2,1)S(1)}, bf16[2,96,256]{2,1,0:T(8,128)(2,1)S(1)}, u32[]{:S(2)}, u32[]{:S(2)}) collective-permute-start(bf16[2,96,256]{2,1,0:T(8,128)(2,1)S(1)} %get-tuple-element.69), channel_id=1, source_target_pairs={{0,8},{1,9},{2,10},{3,11},{4,12},{5,13},{6,14},{7,15},{8,0},{9,1},... | collective-permute-start | bytes 294920 | tf_op jit(solution)/shard_map/ppermute | solution.py:140
  49.3 0.9 collective-permute-start.21
  50.2 1.2 %collective-permute-done.12.came = bf16[2,2,96,256]{3,2,1,0:T(8,128)(2,1)S(1)} collective-permute-done((bf16[2,2,96,256]{3,2,1,0:T(8,128)(2,1)S(1)}, bf16[2,2,96,256]{3,2,1,0:T(8,128)(2,1)S(1)}, u32[]{:S(2)}, u32[]{:S(2)}) %collective-permute-start.12) | collective-permute-done | bytes 196640 | tf_op jit(solution)/shard_map/ppermute | solution.py:140
  51.4 0.3 collective-permute-start.13
  51.7 3.9 %collective-permute-done.14.came = bf16[2,2,96,256]{3,2,1,0:T(8,128)(2,1)S(1)} collective-permute-done((bf16[2,2,96,256]{3,2,1,0:T(8,128)(2,1)S(1)}, bf16[2,2,96,256]{3,2,1,0:T(8,128)(2,1)S(1)}, u32[]{:S(2)}, u32[]{:S(2)}) %collective-permute-start.14) | collective-permute-done | bytes 196640 | tf_op jit(solution)/shard_map/ppermute | solution.py:140
  55.6 2.0 %collective-permute-start.15 = (bf16[2,96,256]{2,1,0:T(8,128)(2,1)S(1)}, bf16[2,96,256]{2,1,0:T(8,128)(2,1)S(1)}, u32[]{:S(2)}, u32[]{:S(2)}) collective-permute-start(bf16[2,96,256]{2,1,0:T(8,128)(2,1)S(1)} %get-tuple-element.59), channel_id=1, source_target_pairs={{0,8},{1,9},{2,10},{3,11},{4,12},{5,13},{6,14},{7,15},{8,0},{9,1},... | collective-permute-start | bytes 294920 | tf_op jit(solution)/shard_map/ppermute | solution.py:140
  57.6 0.6 collective-permute-start.16
  58.1 0.2 renorm.3
  58.3 0.3 collective-permute-start.22
  58.6 2.6 %collective-permute-start.25 = (bf16[2,96,256]{2,1,0:T(8,128)(2,1)S(1)}, bf16[2,96,256]{2,1,0:T(8,128)(2,1)S(1)}, u32[]{:S(2)}, u32[]{:S(2)}) collective-permute-start(bf16[2,96,256]{2,1,0:T(8,128)(2,1)S(1)} %get-tuple-element.71), channel_id=1, source_target_pairs={{0,12},{1,13},{2,14},{3,15},{4,8},{5,9},{6,10},{7,11},{8,4},{9,5},... | collective-permute-start | bytes 294920 | tf_op jit(solution)/shard_map/ppermute | solution.py:140
  61.1 0.2 collective-permute-start.24
  61.4 2.0 %collective-permute-done.16.three = bf16[2,96,256]{2,1,0:T(8,128)(2,1)S(1)} collective-permute-done((bf16[2,96,256]{2,1,0:T(8,128)(2,1)S(1)}, bf16[2,96,256]{2,1,0:T(8,128)(2,1)S(1)}, u32[]{:S(2)}, u32[]{:S(2)}) %collective-permute-start.16) | collective-permute-done | bytes 98336 | tf_op jit(solution)/shard_map/ppermute | solution.py:140
  63.4 0.2 renorm.2
  63.6 8.2 %collective-permute-start.29 = (f32[2,96,256]{2,1,0:T(8,128)S(1)}, f32[2,96,256]{2,1,0:T(8,128)S(1)}, u32[]{:S(2)}, u32[]{:S(2)}) collective-permute-start(f32[2,96,256]{2,1,0:T(8,128)S(1)} %pad_maximum_fusion.6), channel_id=1, source_target_pairs={{0,1},{1,0},{2,3},{3,2},{4,5},{5,4},{6,7},{7,6},{8,9},{9,8},{10,11... | collective-permute-start | bytes 589832 | tf_op jit(solution)/shard_map/ppermute | solution.py:140
  71.8 1.4 %collective-permute-start.36 = (bf16[2,2,96,256]{3,2,1,0:T(8,128)(2,1)S(1)}, bf16[2,2,96,256]{3,2,1,0:T(8,128)(2,1)S(1)}, u32[]{:S(2)}, u32[]{:S(2)}) collective-permute-start(bf16[2,2,96,256]{3,2,1,0:T(8,128)(2,1)S(1)} %pad_maximum_fusion.2.near_low), channel_id=1, source_target_pairs={{0,2},{1,3},{2,0},{3,1},{4,6},{5,7},{6,4},{7,5},{8,10},{9,11},{10,... | collective-permute-start | bytes 589832 | tf_op jit(solution)/shard_map/ppermute | solution.py:140
  73.2 2.4 %collective-permute-start.23 = (bf16[2,96,256]{2,1,0:T(8,128)(2,1)S(1)}, bf16[2,96,256]{2,1,0:T(8,128)(2,1)S(1)}, u32[]{:S(2)}, u32[]{:S(2)}) collective-permute-start(bf16[2,96,256]{2,1,0:T(8,128)(2,1)S(1)} %get-tuple-element.74), channel_id=1, source_target_pairs={{0,4},{1,5},{2,6},{3,7},{4,0},{5,1},{6,2},{7,3},{8,12},{9,13},{10,... | collective-permute-start | bytes 294920 | tf_op jit(solution)/shard_map/ppermute | solution.py:140
  75.6 0.3 collective-permute-start.38
  75.9 2.6 %collective-permute-done.23 = bf16[2,96,256]{2,1,0:T(8,128)(2,1)S(1)} collective-permute-done((bf16[2,96,256]{2,1,0:T(8,128)(2,1)S(1)}, bf16[2,96,256]{2,1,0:T(8,128)(2,1)S(1)}, u32[]{:S(2)}, u32[]{:S(2)}) %collective-permute-start.23) | collective-permute-done | bytes 98336 | tf_op jit(solution)/shard_map/ppermute | solution.py:140
  78.5 1.9 %collective-permute-start.28 = (bf16[2,96,256]{2,1,0:T(8,128)(2,1)S(1)}, bf16[2,96,256]{2,1,0:T(8,128)(2,1)S(1)}, u32[]{:S(2)}, u32[]{:S(2)}) collective-permute-start(bf16[2,96,256]{2,1,0:T(8,128)(2,1)S(1)} %get-tuple-element.74), channel_id=1, source_target_pairs={{0,12},{1,13},{2,14},{3,15},{4,8},{5,9},{6,10},{7,11},{8,4},{9,5},... | collective-permute-start | bytes 294920 | tf_op jit(solution)/shard_map/ppermute | solution.py:140
  80.5 0.5 collective-permute-start.27
  80.9 1.7 %collective-permute-start.34 = (bf16[2,2,96,256]{3,2,1,0:T(8,128)(2,1)S(1)}, bf16[2,2,96,256]{3,2,1,0:T(8,128)(2,1)S(1)}, u32[]{:S(2)}, u32[]{:S(2)}) collective-permute-start(bf16[2,2,96,256]{3,2,1,0:T(8,128)(2,1)S(1)} %pad_maximum_fusion.2.near_low), channel_id=1, source_target_pairs={{0,1},{1,0},{2,3},{3,2},{4,5},{5,4},{6,7},{7,6},{8,9},{9,8},{10,11... | collective-permute-start | bytes 589832 | tf_op jit(solution)/shard_map/ppermute | solution.py:140
  82.6 1.3 %finish.1 = (f32[4,16,1024]{2,1,0:T(8,128)}, f32[4,32,256]{2,1,0:T(8,128)}) custom-call(s32[3]{0:T(128)S(1)} %pad_add_fusion.ids, f32[2,96,256]{2,1,0:T(8,128)S(1)} %get-tuple-element.75.one, f32[2,96,256]{2,1,0:T(8,128)S(1)} %get-tuple-element.76.two, f32[2,96,256]{2,1,0:T(8,128)S(1)} %collective-permute-done.29.came), custom_call_target="tpu_custom_call" | custom-call | tf_op jit(solution)/shard_map/finish/pallas_call | solution.py:546
  84.0 2.8 %collective-permute-start.35 = (bf16[2,2,96,256]{3,2,1,0:T(8,128)(2,1)S(1)}, bf16[2,2,96,256]{3,2,1,0:T(8,128)(2,1)S(1)}, u32[]{:S(2)}, u32[]{:S(2)}) collective-permute-start(bf16[2,2,96,256]{3,2,1,0:T(8,128)(2,1)S(1)} %pad_maximum_fusion.4.near_high), channel_id=1, source_target_pairs={{0,1},{1,0},{2,3},{3,2},{4,5},{5,4},{6,7},{7,6},{8,9},{9,8},{10,11... | collective-permute-start | bytes 589832 | tf_op jit(solution)/shard_map/ppermute | solution.py:140
  86.8 2.4 %collective-permute-done.27 = bf16[2,96,256]{2,1,0:T(8,128)(2,1)S(1)} collective-permute-done((bf16[2,96,256]{2,1,0:T(8,128)(2,1)S(1)}, bf16[2,96,256]{2,1,0:T(8,128)(2,1)S(1)}, u32[]{:S(2)}, u32[]{:S(2)}) %collective-permute-start.27) | collective-permute-done | bytes 98336 | tf_op jit(solution)/shard_map/ppermute | solution.py:140
  89.2 1.3 %collective-permute-start.31 = (bf16[2,2,96,256]{3,2,1,0:T(8,128)(2,1)S(1)}, bf16[2,2,96,256]{3,2,1,0:T(8,128)(2,1)S(1)}, u32[]{:S(2)}, u32[]{:S(2)}) collective-permute-start(bf16[2,2,96,256]{3,2,1,0:T(8,128)(2,1)S(1)} %pad_maximum_fusion.3.near_low), channel_id=1, source_target_pairs={{0,2},{1,3},{2,0},{3,1},{4,6},{5,7},{6,4},{7,5},{8,10},{9,11},{10,... | collective-permute-start | bytes 589832 | tf_op jit(solution)/shard_map/ppermute | solution.py:140
  90.5 1.4 %collective-permute-start.37 = (bf16[2,2,96,256]{3,2,1,0:T(8,128)(2,1)S(1)}, bf16[2,2,96,256]{3,2,1,0:T(8,128)(2,1)S(1)}, u32[]{:S(2)}, u32[]{:S(2)}) collective-permute-start(bf16[2,2,96,256]{3,2,1,0:T(8,128)(2,1)S(1)} %collective-permute-done.36.far_low), channel_id=1, source_target_pairs={{0,1},{1,0},{2,3},{3,2},{4,5},{5,4},{6,7},{7,6},{8,9},{9,8},{10,11... | collective-permute-start | bytes 589832 | tf_op jit(solution)/shard_map/ppermute | solution.py:140
  92.1 0.8 collective-permute-start.33
  92.9 2.5 %apply.4.rest_0_ = bf16[1024,1024]{1,0:T(8,128)(2,1)} custom-call(s32[3]{0:T(128)S(1)} %pad_add_fusion.ids, bf16[2,2,96,256]{3,2,1,0:T(8,128)(2,1)S(1)} %pad_maximum_fusion.2.near_low, bf16[2,2,96,256]{3,2,1,0:T(8,128)(2,1)S(1)} %pad_maximum_fusion.4.near_high, bf16[2,2,96,256]{3,2,1,0:T(8,128)(2,1)S(1)} %collective-permute-done.36.far_low, ...), custom_call_target="tpu_custom_call" | custom-call | flops 805306368 | bytes 1048576 | tf_op jit(solution)/shard_map/apply/pallas_call | solution.py:509
  95.4 0.8 collective-permute-start.26
  96.2 1.9 %collective-permute-start.30 = (bf16[2,2,96,256]{3,2,1,0:T(8,128)(2,1)S(1)}, bf16[2,2,96,256]{3,2,1,0:T(8,128)(2,1)S(1)}, u32[]{:S(2)}, u32[]{:S(2)}) collective-permute-start(bf16[2,2,96,256]{3,2,1,0:T(8,128)(2,1)S(1)} %pad_maximum_fusion.5.near_high), channel_id=1, source_target_pairs={{0,1},{1,0},{2,3},{3,2},{4,5},{5,4},{6,7},{7,6},{8,9},{9,8},{10,11... | collective-permute-start | bytes 589832 | tf_op jit(solution)/shard_map/ppermute | solution.py:140
  98.1 2.5 %apply.5.rest_0_ = bf16[1024,1024]{1,0:T(8,128)(2,1)} custom-call(s32[3]{0:T(128)S(1)} %pad_add_fusion.ids, bf16[2,2,96,256]{3,2,1,0:T(8,128)(2,1)S(1)} %collective-permute-done.34.near_low, bf16[2,2,96,256]{3,2,1,0:T(8,128)(2,1)S(1)} %collective-permute-done.35.near_high, ...), custom_call_target="tpu_custom_call", output_to_operand_aliasing={{}: (6, {})} | custom-call | flops 805306368 | bytes 1048576 | tf_op jit(solution)/shard_map/apply/pallas_call | solution.py:509
  100.7 0.6 collective-permute-start.40
  101.2 2.5 %apply.6.rest_0_ = bf16[1024,1024]{1,0:T(8,128)(2,1)} custom-call(s32[3]{0:T(128)S(1)} %pad_add_fusion.ids, bf16[2,2,96,256]{3,2,1,0:T(8,128)(2,1)S(1)} %pad_maximum_fusion.3.near_low, bf16[2,2,96,256]{3,2,1,0:T(8,128)(2,1)S(1)} %pad_maximum_fusion.5.near_high, ...), custom_call_target="tpu_custom_call", output_to_operand_aliasing={{}: (6, {})} | custom-call | flops 805306368 | bytes 1048576 | tf_op jit(solution)/shard_map/apply/pallas_call | solution.py:509
  103.8 2.5 %apply.7 = bf16[1024,1024]{1,0:T(8,128)(2,1)} custom-call(s32[3]{0:T(128)S(1)} %pad_add_fusion.ids, bf16[2,2,96,256]{3,2,1,0:T(8,128)(2,1)S(1)} %collective-permute-done.26.near_low, bf16[2,2,96,256]{3,2,1,0:T(8,128)(2,1)S(1)} %collective-permute-done.30.near_high, ...), custom_call_target="tpu_custom_call", output_to_operand_aliasing={{}: (6, {})} | custom-call | flops 805306368 | bytes 1048576 | tf_op jit(solution)/shard_map/apply/pallas_call | solution.py:509
  (57 shorter events, 0.6 us)
Async XLA Ops:
  0.7 1.6 %copy-start.3 = (bf16[1024,1024]{1,0:T(8,128)(2,1)S(1)}, bf16[1024,1024]{1,0:T(8,128)(2,1)}, u32[]{:S(2)}) copy-start(bf16[1024,1024]{1,0:T(8,128)(2,1)} %x_ref.2) | copy-start | bytes 6291460
  2.3 1.7 %copy-start.1 = (f32[4,16,1024]{2,1,0:T(8,128)S(1)}, f32[4,16,1024]{2,1,0:T(8,128)}, u32[]{:S(2)}) copy-start(f32[4,16,1024]{2,1,0:T(8,128)} %in_ref.1) | copy-start | bytes 786436
  2.3 1.7 %copy-start.2 = (f32[4,32,256]{2,1,0:T(8,128)S(1)}, f32[4,32,256]{2,1,0:T(8,128)}, u32[]{:S(2)}) copy-start(f32[4,32,256]{2,1,0:T(8,128)} %out_ref.1) | copy-start | bytes 393220
  2.3 18.7 %copy-start.4 = (bf16[1024,1024]{1,0:T(8,128)(2,1)S(1)}, bf16[1024,1024]{1,0:T(8,128)(2,1)}, u32[]{:S(2)}) copy-start(bf16[1024,1024]{1,0:T(8,128)(2,1)} %x_ref.3) | copy-start | bytes 6291460
  2.3 18.8 %copy-start.5 = (f32[4,1024]{1,0:T(4,128)S(1)}, f32[4,1024]{1,0:T(4,128)}, u32[]{:S(2)}) copy-start(f32[4,1024]{1,0:T(4,128)} %rest_0_.1) | copy-start | bytes 49156
  3.8 8.4 %collective-permute-start.2 = (bf16[1024,512]{1,0:T(8,128)(2,1)S(1)}, bf16[1024,512]{1,0:T(8,128)(2,1)S(1)}, u32[]{:S(2)}, u32[]{:S(2)}) collective-permute-start(bf16[1024,512]{1,0:T(8,128)(2,1)S(1)} %get-tuple-element.48), channel_id=1, source_target_pairs={{0,1},{1,0},{2,3},{3,2},{4,5},{5,4},{6,7},{7,6},{8,9},{9,8},{10,11... | collective-permute-start | bytes 3145736 | tf_op jit(solution)/shard_map/ppermute | solution.py:140
  4.6 2.3 %collective-permute-start = (f32[2,96,256]{2,1,0:T(8,128)S(1)}, f32[2,96,256]{2,1,0:T(8,128)S(1)}, u32[]{:S(2)}, u32[]{:S(2)}) collective-permute-start(f32[2,96,256]{2,1,0:T(8,128)S(1)} %get-tuple-element.45), channel_id=1, source_target_pairs={{0,1},{1,0},{2,3},{3,2},{4,5},{5,4},{6,7},{7,6},{8,9},{9,8},{10,11... | collective-permute-start | bytes 589832 | tf_op jit(solution)/shard_map/ppermute | solution.py:140
  6.9 5.4 %collective-permute-start.1 = (bf16[2,96,256]{2,1,0:T(8,128)(2,1)S(1)}, bf16[2,96,256]{2,1,0:T(8,128)(2,1)S(1)}, u32[]{:S(2)}, u32[]{:S(2)}) collective-permute-start(bf16[2,96,256]{2,1,0:T(8,128)(2,1)S(1)} %get-tuple-element.47), channel_id=1, source_target_pairs={{0,4},{1,5},{2,6},{3,7},{4,0},{5,1},{6,2},{7,3},{8,12},{9,13},{10,... | collective-permute-start | bytes 294920 | tf_op jit(solution)/shard_map/ppermute | solution.py:140
  9.4 6.8 %collective-permute-start.5 = (bf16[2,96,256]{2,1,0:T(8,128)(2,1)S(1)}, bf16[2,96,256]{2,1,0:T(8,128)(2,1)S(1)}, u32[]{:S(2)}, u32[]{:S(2)}) collective-permute-start(bf16[2,96,256]{2,1,0:T(8,128)(2,1)S(1)} %get-tuple-element.47), channel_id=1, source_target_pairs={{0,12},{1,13},{2,14},{3,15},{4,8},{5,9},{6,10},{7,11},{8,4},{9,5},... | collective-permute-start | bytes 294920 | tf_op jit(solution)/shard_map/ppermute | solution.py:140
  11.6 9.4 %collective-permute-start.4 = (bf16[2,96,256]{2,1,0:T(8,128)(2,1)S(1)}, bf16[2,96,256]{2,1,0:T(8,128)(2,1)S(1)}, u32[]{:S(2)}, u32[]{:S(2)}) collective-permute-start(bf16[2,96,256]{2,1,0:T(8,128)(2,1)S(1)} %get-tuple-element.47), channel_id=1, source_target_pairs={{0,8},{1,9},{2,10},{3,11},{4,12},{5,13},{6,14},{7,15},{8,0},{9,1},... | collective-permute-start | bytes 294920 | tf_op jit(solution)/shard_map/ppermute | solution.py:140
  12.3 8.8 %collective-permute-start.3 = (bf16[2,2,96,256]{3,2,1,0:T(8,128)(2,1)S(1)}, bf16[2,2,96,256]{3,2,1,0:T(8,128)(2,1)S(1)}, u32[]{:S(2)}, u32[]{:S(2)}) collective-permute-start(bf16[2,2,96,256]{3,2,1,0:T(8,128)(2,1)S(1)} %pad_maximum_fusion.near_low), channel_id=1, source_target_pairs={{0,16},{16,0},{1,17},{17,1},{2,18},{18,2},{3,19},{19,3},{4,20},{20... | collective-permute-start | bytes 589832 | tf_op jit(solution)/shard_map/ppermute | solution.py:144
  13.4 7.7 %collective-permute-start.6 = (bf16[2,2,96,256]{3,2,1,0:T(8,128)(2,1)S(1)}, bf16[2,2,96,256]{3,2,1,0:T(8,128)(2,1)S(1)}, u32[]{:S(2)}, u32[]{:S(2)}) collective-permute-start(bf16[2,2,96,256]{3,2,1,0:T(8,128)(2,1)S(1)} %pad_maximum_fusion.near_low), channel_id=1, source_target_pairs={{0,2},{1,3},{2,0},{3,1},{4,6},{5,7},{6,4},{7,5},{8,10},{9,11},{10,... | collective-permute-start | bytes 589832 | tf_op jit(solution)/shard_map/ppermute | solution.py:140
  23.4 8.5 %collective-permute-start.11 = (bf16[1024,512]{1,0:T(8,128)(2,1)S(1)}, bf16[1024,512]{1,0:T(8,128)(2,1)S(1)}, u32[]{:S(2)}, u32[]{:S(2)}) collective-permute-start(bf16[1024,512]{1,0:T(8,128)(2,1)S(1)} %get-tuple-element.53), channel_id=1, source_target_pairs={{0,1},{1,0},{2,3},{3,2},{4,5},{5,4},{6,7},{7,6},{8,9},{9,8},{10,11... | collective-permute-start | bytes 3145736 | tf_op jit(solution)/shard_map/ppermute | solution.py:140
  24.2 6.5 %collective-permute-start.8 = (bf16[2,2,96,256]{3,2,1,0:T(8,128)(2,1)S(1)}, bf16[2,2,96,256]{3,2,1,0:T(8,128)(2,1)S(1)}, u32[]{:S(2)}, u32[]{:S(2)}) collective-permute-start(bf16[2,2,96,256]{3,2,1,0:T(8,128)(2,1)S(1)} %collective-permute-done.6.far_low), channel_id=1, source_target_pairs={{0,16},{16,0},{1,17},{17,1},{2,18},{18,2},{3,19},{19,3},{4,20},{20... | collective-permute-start | bytes 589832 | tf_op jit(solution)/shard_map/ppermute | solution.py:144
  25.4 6.1 %collective-permute-start.9 = (bf16[2,2,96,256]{3,2,1,0:T(8,128)(2,1)S(1)}, bf16[2,2,96,256]{3,2,1,0:T(8,128)(2,1)S(1)}, u32[]{:S(2)}, u32[]{:S(2)}) collective-permute-start(bf16[2,2,96,256]{3,2,1,0:T(8,128)(2,1)S(1)} %pad_maximum_fusion.1.near_high), channel_id=1, source_target_pairs={{0,2},{1,3},{2,0},{3,1},{4,6},{5,7},{6,4},{7,5},{8,10},{9,11},{10,... | collective-permute-start | bytes 589832 | tf_op jit(solution)/shard_map/ppermute | solution.py:140
  26.6 12.4 %collective-permute-start.7 = (bf16[2,2,96,256]{3,2,1,0:T(8,128)(2,1)S(1)}, bf16[2,2,96,256]{3,2,1,0:T(8,128)(2,1)S(1)}, u32[]{:S(2)}, u32[]{:S(2)}) collective-permute-start(bf16[2,2,96,256]{3,2,1,0:T(8,128)(2,1)S(1)} %pad_maximum_fusion.1.near_high), channel_id=1, source_target_pairs={{0,16},{16,0},{1,17},{17,1},{2,18},{18,2},{3,19},{19,3},{4,20},{20... | collective-permute-start | bytes 589832 | tf_op jit(solution)/shard_map/ppermute | solution.py:144
  31.5 7.5 %collective-permute-start.10 = (bf16[2,2,96,256]{3,2,1,0:T(8,128)(2,1)S(1)}, bf16[2,2,96,256]{3,2,1,0:T(8,128)(2,1)S(1)}, u32[]{:S(2)}, u32[]{:S(2)}) collective-permute-start(bf16[2,2,96,256]{3,2,1,0:T(8,128)(2,1)S(1)} %collective-permute-done.9.far_high), channel_id=1, source_target_pairs={{0,16},{16,0},{1,17},{17,1},{2,18},{18,2},{3,19},{19,3},{4,20},{20... | collective-permute-start | bytes 589832 | tf_op jit(solution)/shard_map/ppermute | solution.py:144
  37.5 8.9 %collective-permute-start.17 = (bf16[2,2,96,256]{3,2,1,0:T(8,128)(2,1)S(1)}, bf16[2,2,96,256]{3,2,1,0:T(8,128)(2,1)S(1)}, u32[]{:S(2)}, u32[]{:S(2)}) collective-permute-start(bf16[2,2,96,256]{3,2,1,0:T(8,128)(2,1)S(1)} %get-tuple-element.65), channel_id=1, source_target_pairs={{0,2},{1,3},{2,0},{3,1},{4,6},{5,7},{6,4},{7,5},{8,10},{9,11},{10,... | collective-permute-start | bytes 589832 | tf_op jit(solution)/shard_map/ppermute | solution.py:140
  38.8 7.9 %collective-permute-start.19 = (bf16[2,2,96,256]{3,2,1,0:T(8,128)(2,1)S(1)}, bf16[2,2,96,256]{3,2,1,0:T(8,128)(2,1)S(1)}, u32[]{:S(2)}, u32[]{:S(2)}) collective-permute-start(bf16[2,2,96,256]{3,2,1,0:T(8,128)(2,1)S(1)} %get-tuple-element.68), channel_id=1, source_target_pairs={{0,2},{1,3},{2,0},{3,1},{4,6},{5,7},{6,4},{7,5},{8,10},{9,11},{10,... | collective-permute-start | bytes 589832 | tf_op jit(solution)/shard_map/ppermute | solution.py:140
  44.9 6.5 %collective-permute-start.12 = (bf16[2,2,96,256]{3,2,1,0:T(8,128)(2,1)S(1)}, bf16[2,2,96,256]{3,2,1,0:T(8,128)(2,1)S(1)}, u32[]{:S(2)}, u32[]{:S(2)}) collective-permute-start(bf16[2,2,96,256]{3,2,1,0:T(8,128)(2,1)S(1)} %get-tuple-element.55), channel_id=1, source_target_pairs={{0,2},{1,3},{2,0},{3,1},{4,6},{5,7},{6,4},{7,5},{8,10},{9,11},{10,... | collective-permute-start | bytes 589832 | tf_op jit(solution)/shard_map/ppermute | solution.py:140
  46.2 9.4 %collective-permute-start.14 = (bf16[2,2,96,256]{3,2,1,0:T(8,128)(2,1)S(1)}, bf16[2,2,96,256]{3,2,1,0:T(8,128)(2,1)S(1)}, u32[]{:S(2)}, u32[]{:S(2)}) collective-permute-start(bf16[2,2,96,256]{3,2,1,0:T(8,128)(2,1)S(1)} %get-tuple-element.58), channel_id=1, source_target_pairs={{0,2},{1,3},{2,0},{3,1},{4,6},{5,7},{6,4},{7,5},{8,10},{9,11},{10,... | collective-permute-start | bytes 589832 | tf_op jit(solution)/shard_map/ppermute | solution.py:140
  46.5 11.1 %collective-permute-start.18 = (bf16[2,96,256]{2,1,0:T(8,128)(2,1)S(1)}, bf16[2,96,256]{2,1,0:T(8,128)(2,1)S(1)}, u32[]{:S(2)}, u32[]{:S(2)}) collective-permute-start(bf16[2,96,256]{2,1,0:T(8,128)(2,1)S(1)} %get-tuple-element.67), channel_id=1, source_target_pairs={{0,4},{1,5},{2,6},{3,7},{4,0},{5,1},{6,2},{7,3},{8,12},{9,13},{10,... | collective-permute-start | bytes 294920 | tf_op jit(solution)/shard_map/ppermute | solution.py:140
  46.8 11.4 %collective-permute-start.20 = (bf16[2,96,256]{2,1,0:T(8,128)(2,1)S(1)}, bf16[2,96,256]{2,1,0:T(8,128)(2,1)S(1)}, u32[]{:S(2)}, u32[]{:S(2)}) collective-permute-start(bf16[2,96,256]{2,1,0:T(8,128)(2,1)S(1)} %get-tuple-element.69), channel_id=1, source_target_pairs={{0,8},{1,9},{2,10},{3,11},{4,12},{5,13},{6,14},{7,15},{8,0},{9,1},... | collective-permute-start | bytes 294920 | tf_op jit(solution)/shard_map/ppermute | solution.py:140
  49.3 8.9 %collective-permute-start.21 = (bf16[2,96,256]{2,1,0:T(8,128)(2,1)S(1)}, bf16[2,96,256]{2,1,0:T(8,128)(2,1)S(1)}, u32[]{:S(2)}, u32[]{:S(2)}) collective-permute-start(bf16[2,96,256]{2,1,0:T(8,128)(2,1)S(1)} %get-tuple-element.70), channel_id=1, source_target_pairs={{0,12},{1,13},{2,14},{3,15},{4,8},{5,9},{6,10},{7,11},{8,4},{9,5},... | collective-permute-start | bytes 294920 | tf_op jit(solution)/shard_map/ppermute | solution.py:140
  51.4 9.7 %collective-permute-start.13 = (bf16[2,96,256]{2,1,0:T(8,128)(2,1)S(1)}, bf16[2,96,256]{2,1,0:T(8,128)(2,1)S(1)}, u32[]{:S(2)}, u32[]{:S(2)}) collective-permute-start(bf16[2,96,256]{2,1,0:T(8,128)(2,1)S(1)} %get-tuple-element.57), channel_id=1, source_target_pairs={{0,4},{1,5},{2,6},{3,7},{4,0},{5,1},{6,2},{7,3},{8,12},{9,13},{10,... | collective-permute-start | bytes 294920 | tf_op jit(solution)/shard_map/ppermute | solution.py:140
  55.6 5.8 %collective-permute-start.15 = (bf16[2,96,256]{2,1,0:T(8,128)(2,1)S(1)}, bf16[2,96,256]{2,1,0:T(8,128)(2,1)S(1)}, u32[]{:S(2)}, u32[]{:S(2)}) collective-permute-start(bf16[2,96,256]{2,1,0:T(8,128)(2,1)S(1)} %get-tuple-element.59), channel_id=1, source_target_pairs={{0,8},{1,9},{2,10},{3,11},{4,12},{5,13},{6,14},{7,15},{8,0},{9,1},... | collective-permute-start | bytes 294920 | tf_op jit(solution)/shard_map/ppermute | solution.py:140
  57.6 5.8 %collective-permute-start.16 = (bf16[2,96,256]{2,1,0:T(8,128)(2,1)S(1)}, bf16[2,96,256]{2,1,0:T(8,128)(2,1)S(1)}, u32[]{:S(2)}, u32[]{:S(2)}) collective-permute-start(bf16[2,96,256]{2,1,0:T(8,128)(2,1)S(1)} %get-tuple-element.60), channel_id=1, source_target_pairs={{0,12},{1,13},{2,14},{3,15},{4,8},{5,9},{6,10},{7,11},{8,4},{9,5},... | collective-permute-start | bytes 294920 | tf_op jit(solution)/shard_map/ppermute | solution.py:140
  58.1 34.8 %copy-start = (bf16[1024,1024]{1,0:T(8,128)(2,1)S(1)}, bf16[1024,1024]{1,0:T(8,128)(2,1)}, u32[]{:S(2)}) copy-start(bf16[1024,1024]{1,0:T(8,128)(2,1)} %q_ref.7) | copy-start | bytes 6291460
  58.3 13.5 %collective-permute-start.22 = (bf16[2,96,256]{2,1,0:T(8,128)(2,1)S(1)}, bf16[2,96,256]{2,1,0:T(8,128)(2,1)S(1)}, u32[]{:S(2)}, u32[]{:S(2)}) collective-permute-start(bf16[2,96,256]{2,1,0:T(8,128)(2,1)S(1)} %get-tuple-element.71), channel_id=1, source_target_pairs={{0,4},{1,5},{2,6},{3,7},{4,0},{5,1},{6,2},{7,3},{8,12},{9,13},{10,... | collective-permute-start | bytes 294920 | tf_op jit(solution)/shard_map/ppermute | solution.py:140
  58.6 17.0 %collective-permute-start.25 = (bf16[2,96,256]{2,1,0:T(8,128)(2,1)S(1)}, bf16[2,96,256]{2,1,0:T(8,128)(2,1)S(1)}, u32[]{:S(2)}, u32[]{:S(2)}) collective-permute-start(bf16[2,96,256]{2,1,0:T(8,128)(2,1)S(1)} %get-tuple-element.71), channel_id=1, source_target_pairs={{0,12},{1,13},{2,14},{3,15},{4,8},{5,9},{6,10},{7,11},{8,4},{9,5},... | collective-permute-start | bytes 294920 | tf_op jit(solution)/shard_map/ppermute | solution.py:140
  61.1 14.4 %collective-permute-start.24 = (bf16[2,96,256]{2,1,0:T(8,128)(2,1)S(1)}, bf16[2,96,256]{2,1,0:T(8,128)(2,1)S(1)}, u32[]{:S(2)}, u32[]{:S(2)}) collective-permute-start(bf16[2,96,256]{2,1,0:T(8,128)(2,1)S(1)} %get-tuple-element.71), channel_id=1, source_target_pairs={{0,8},{1,9},{2,10},{3,11},{4,12},{5,13},{6,14},{7,15},{8,0},{9,1},... | collective-permute-start | bytes 294920 | tf_op jit(solution)/shard_map/ppermute | solution.py:140
  63.6 17.3 %collective-permute-start.29 = (f32[2,96,256]{2,1,0:T(8,128)S(1)}, f32[2,96,256]{2,1,0:T(8,128)S(1)}, u32[]{:S(2)}, u32[]{:S(2)}) collective-permute-start(f32[2,96,256]{2,1,0:T(8,128)S(1)} %pad_maximum_fusion.6), channel_id=1, source_target_pairs={{0,1},{1,0},{2,3},{3,2},{4,5},{5,4},{6,7},{7,6},{8,9},{9,8},{10,11... | collective-permute-start | bytes 589832 | tf_op jit(solution)/shard_map/ppermute | solution.py:140
  71.8 18.7 %collective-permute-start.36 = (bf16[2,2,96,256]{3,2,1,0:T(8,128)(2,1)S(1)}, bf16[2,2,96,256]{3,2,1,0:T(8,128)(2,1)S(1)}, u32[]{:S(2)}, u32[]{:S(2)}) collective-permute-start(bf16[2,2,96,256]{3,2,1,0:T(8,128)(2,1)S(1)} %pad_maximum_fusion.2.near_low), channel_id=1, source_target_pairs={{0,2},{1,3},{2,0},{3,1},{4,6},{5,7},{6,4},{7,5},{8,10},{9,11},{10,... | collective-permute-start | bytes 589832 | tf_op jit(solution)/shard_map/ppermute | solution.py:140
  73.2 5.3 %collective-permute-start.23 = (bf16[2,96,256]{2,1,0:T(8,128)(2,1)S(1)}, bf16[2,96,256]{2,1,0:T(8,128)(2,1)S(1)}, u32[]{:S(2)}, u32[]{:S(2)}) collective-permute-start(bf16[2,96,256]{2,1,0:T(8,128)(2,1)S(1)} %get-tuple-element.74), channel_id=1, source_target_pairs={{0,4},{1,5},{2,6},{3,7},{4,0},{5,1},{6,2},{7,3},{8,12},{9,13},{10,... | collective-permute-start | bytes 294920 | tf_op jit(solution)/shard_map/ppermute | solution.py:140
  75.6 16.4 %collective-permute-start.38 = (bf16[2,2,96,256]{3,2,1,0:T(8,128)(2,1)S(1)}, bf16[2,2,96,256]{3,2,1,0:T(8,128)(2,1)S(1)}, u32[]{:S(2)}, u32[]{:S(2)}) collective-permute-start(bf16[2,2,96,256]{3,2,1,0:T(8,128)(2,1)S(1)} %pad_maximum_fusion.4.near_high), channel_id=1, source_target_pairs={{0,2},{1,3},{2,0},{3,1},{4,6},{5,7},{6,4},{7,5},{8,10},{9,11},{10,... | collective-permute-start | bytes 589832 | tf_op jit(solution)/shard_map/ppermute | solution.py:140
  78.5 5.4 %collective-permute-start.28 = (bf16[2,96,256]{2,1,0:T(8,128)(2,1)S(1)}, bf16[2,96,256]{2,1,0:T(8,128)(2,1)S(1)}, u32[]{:S(2)}, u32[]{:S(2)}) collective-permute-start(bf16[2,96,256]{2,1,0:T(8,128)(2,1)S(1)} %get-tuple-element.74), channel_id=1, source_target_pairs={{0,12},{1,13},{2,14},{3,15},{4,8},{5,9},{6,10},{7,11},{8,4},{9,5},... | collective-permute-start | bytes 294920 | tf_op jit(solution)/shard_map/ppermute | solution.py:140
  80.5 8.7 %collective-permute-start.27 = (bf16[2,96,256]{2,1,0:T(8,128)(2,1)S(1)}, bf16[2,96,256]{2,1,0:T(8,128)(2,1)S(1)}, u32[]{:S(2)}, u32[]{:S(2)}) collective-permute-start(bf16[2,96,256]{2,1,0:T(8,128)(2,1)S(1)} %get-tuple-element.74), channel_id=1, source_target_pairs={{0,8},{1,9},{2,10},{3,11},{4,12},{5,13},{6,14},{7,15},{8,0},{9,1},... | collective-permute-start | bytes 294920 | tf_op jit(solution)/shard_map/ppermute | solution.py:140
  80.9 11.1 %collective-permute-start.34 = (bf16[2,2,96,256]{3,2,1,0:T(8,128)(2,1)S(1)}, bf16[2,2,96,256]{3,2,1,0:T(8,128)(2,1)S(1)}, u32[]{:S(2)}, u32[]{:S(2)}) collective-permute-start(bf16[2,2,96,256]{3,2,1,0:T(8,128)(2,1)S(1)} %pad_maximum_fusion.2.near_low), channel_id=1, source_target_pairs={{0,1},{1,0},{2,3},{3,2},{4,5},{5,4},{6,7},{7,6},{8,9},{9,8},{10,11... | collective-permute-start | bytes 589832 | tf_op jit(solution)/shard_map/ppermute | solution.py:140
  84.0 11.5 %collective-permute-start.35 = (bf16[2,2,96,256]{3,2,1,0:T(8,128)(2,1)S(1)}, bf16[2,2,96,256]{3,2,1,0:T(8,128)(2,1)S(1)}, u32[]{:S(2)}, u32[]{:S(2)}) collective-permute-start(bf16[2,2,96,256]{3,2,1,0:T(8,128)(2,1)S(1)} %pad_maximum_fusion.4.near_high), channel_id=1, source_target_pairs={{0,1},{1,0},{2,3},{3,2},{4,5},{5,4},{6,7},{7,6},{8,9},{9,8},{10,11... | collective-permute-start | bytes 589832 | tf_op jit(solution)/shard_map/ppermute | solution.py:140
  89.2 7.0 %collective-permute-start.31 = (bf16[2,2,96,256]{3,2,1,0:T(8,128)(2,1)S(1)}, bf16[2,2,96,256]{3,2,1,0:T(8,128)(2,1)S(1)}, u32[]{:S(2)}, u32[]{:S(2)}) collective-permute-start(bf16[2,2,96,256]{3,2,1,0:T(8,128)(2,1)S(1)} %pad_maximum_fusion.3.near_low), channel_id=1, source_target_pairs={{0,2},{1,3},{2,0},{3,1},{4,6},{5,7},{6,4},{7,5},{8,10},{9,11},{10,... | collective-permute-start | bytes 589832 | tf_op jit(solution)/shard_map/ppermute | solution.py:140
  90.5 7.6 %collective-permute-start.37 = (bf16[2,2,96,256]{3,2,1,0:T(8,128)(2,1)S(1)}, bf16[2,2,96,256]{3,2,1,0:T(8,128)(2,1)S(1)}, u32[]{:S(2)}, u32[]{:S(2)}) collective-permute-start(bf16[2,2,96,256]{3,2,1,0:T(8,128)(2,1)S(1)} %collective-permute-done.36.far_low), channel_id=1, source_target_pairs={{0,1},{1,0},{2,3},{3,2},{4,5},{5,4},{6,7},{7,6},{8,9},{9,8},{10,11... | collective-permute-start | bytes 589832 | tf_op jit(solution)/shard_map/ppermute | solution.py:140
  92.0 6.2 %collective-permute-start.39 = (bf16[2,2,96,256]{3,2,1,0:T(8,128)(2,1)S(1)}, bf16[2,2,96,256]{3,2,1,0:T(8,128)(2,1)S(1)}, u32[]{:S(2)}, u32[]{:S(2)}) collective-permute-start(bf16[2,2,96,256]{3,2,1,0:T(8,128)(2,1)S(1)} %collective-permute-done.38.far_high), channel_id=1, source_target_pairs={{0,1},{1,0},{2,3},{3,2},{4,5},{5,4},{6,7},{7,6},{8,9},{9,8},{10,11... | collective-permute-start | bytes 589832 | tf_op jit(solution)/shard_map/ppermute | solution.py:140
  92.1 8.6 %collective-permute-start.33 = (bf16[2,2,96,256]{3,2,1,0:T(8,128)(2,1)S(1)}, bf16[2,2,96,256]{3,2,1,0:T(8,128)(2,1)S(1)}, u32[]{:S(2)}, u32[]{:S(2)}) collective-permute-start(bf16[2,2,96,256]{3,2,1,0:T(8,128)(2,1)S(1)} %pad_maximum_fusion.5.near_high), channel_id=1, source_target_pairs={{0,2},{1,3},{2,0},{3,1},{4,6},{5,7},{6,4},{7,5},{8,10},{9,11},{10,... | collective-permute-start | bytes 589832 | tf_op jit(solution)/shard_map/ppermute | solution.py:140
  95.4 8.3 %collective-permute-start.26 = (bf16[2,2,96,256]{3,2,1,0:T(8,128)(2,1)S(1)}, bf16[2,2,96,256]{3,2,1,0:T(8,128)(2,1)S(1)}, u32[]{:S(2)}, u32[]{:S(2)}) collective-permute-start(bf16[2,2,96,256]{3,2,1,0:T(8,128)(2,1)S(1)} %pad_maximum_fusion.3.near_low), channel_id=1, source_target_pairs={{0,1},{1,0},{2,3},{3,2},{4,5},{5,4},{6,7},{7,6},{8,9},{9,8},{10,11... | collective-permute-start | bytes 589832 | tf_op jit(solution)/shard_map/ppermute | solution.py:140
  96.2 7.5 %collective-permute-start.30 = (bf16[2,2,96,256]{3,2,1,0:T(8,128)(2,1)S(1)}, bf16[2,2,96,256]{3,2,1,0:T(8,128)(2,1)S(1)}, u32[]{:S(2)}, u32[]{:S(2)}) collective-permute-start(bf16[2,2,96,256]{3,2,1,0:T(8,128)(2,1)S(1)} %pad_maximum_fusion.5.near_high), channel_id=1, source_target_pairs={{0,1},{1,0},{2,3},{3,2},{4,5},{5,4},{6,7},{7,6},{8,9},{9,8},{10,11... | collective-permute-start | bytes 589832 | tf_op jit(solution)/shard_map/ppermute | solution.py:140
  98.1 5.6 %collective-permute-start.32 = (bf16[2,2,96,256]{3,2,1,0:T(8,128)(2,1)S(1)}, bf16[2,2,96,256]{3,2,1,0:T(8,128)(2,1)S(1)}, u32[]{:S(2)}, u32[]{:S(2)}) collective-permute-start(bf16[2,2,96,256]{3,2,1,0:T(8,128)(2,1)S(1)} %collective-permute-done.31.far_low), channel_id=1, source_target_pairs={{0,1},{1,0},{2,3},{3,2},{4,5},{5,4},{6,7},{7,6},{8,9},{9,8},{10,11... | collective-permute-start | bytes 589832 | tf_op jit(solution)/shard_map/ppermute | solution.py:140
  100.7 3.1 %collective-permute-start.40 = (bf16[2,2,96,256]{3,2,1,0:T(8,128)(2,1)S(1)}, bf16[2,2,96,256]{3,2,1,0:T(8,128)(2,1)S(1)}, u32[]{:S(2)}, u32[]{:S(2)}) collective-permute-start(bf16[2,2,96,256]{3,2,1,0:T(8,128)(2,1)S(1)} %collective-permute-done.33.far_high), channel_id=1, source_target_pairs={{0,1},{1,0},{2,3},{3,2},{4,5},{5,4},{6,7},{7,6},{8,9},{9,8},{10,11... | collective-permute-start | bytes 589832 | tf_op jit(solution)/shard_map/ppermute | solution.py:140

commit v13 on v11

--- a/solution.py
+++ b/solution.py
@@ -607,10 +607,10 @@
     output = apply_fast(ids, 0, 0, mine, queries, None, fast)
     came = swap(jnp.stack([wide[0][1], wide[1][1]]), 1)
     updated = finish(ids, wide[0], wide[1], came, fast_in, fast_out)
-    near_low, near_high = second_low, after(second_high, *updated)
+    near_low, far_low = second_low, swap(second_low, 2)
+    near_high = after(second_high, far_low, output, *updated)
     output = apply_fast(ids, 0, 1, others, queries, output, fast)
-    far_low, far_high = swap(near_low, 2), swap(near_high, 2)
-    far_high = after(far_high, output)
+    far_high = after(swap(near_high, 2), output)
     mine = (near_low, near_high, far_low, far_high)
     others = tuple(swap(piece, 1) for piece in mine)
     output = apply_fast(ids, 1, 0, mine, queries, output, fast)

time: 101 us -> 101 us (level)
  waiting for transfers between devices: 23.2 us -> 16.4 us
  starting transfers between devices: 47.5 us -> 53.7 us
    ppermute x37, waiting for transfers between devices: 20 us -> 14.3 us  [swap(): lax.ppermute(value, 'tok', [(place, place ^ bits) for place in range(coun...]
    ppermute x37, starting transfers between devices: 44.4 us -> 49.7 us  [swap(): lax.ppermute(value, 'tok', [(place, place ^ bits) for place in range(coun...]
    ppermute x4, waiting for transfers between devices: 3.19 us -> 2.07 us  [swap_parts(): return lax.ppermute(value, 'parts', [(0, 1), (1, 0)])]
  transfers between devices with their start and end apart: 41 -> 41, of which waited for: 11 -> 12; matrix products, arithmetic and copies ran while one was open for 0% -> 0% of each run, Pallas kernels for 23% -> 17%
where the time goes in v13:
time: 101 us
  starting transfers between devices  53.7 us (53%)
  Pallas kernels  27.6 us (27%)
  waiting for transfers between devices  16.4 us (16%)
  local copies, waits for them, and re-layouts  1.63 us (2%)
  between operations  1.1 us (1%)
    ppermute x37, starting transfers between devices, swap(): lax.ppermute(value, 'tok', [(place, place ^ bits) for place in range(coun...  49.7 us
    ppermute x37, waiting for transfers between devices, swap(): lax.ppermute(value, 'tok', [(place, place ^ bits) for place in range(coun...  14.3 us
    pallas_call x2, Pallas kernels, increments(): pl.pallas_call(increments_kernel, grid_spec=pltpu.PrefetchScalarGridSpec(...  11.4 us
    pallas_call x4, Pallas kernels, apply_fast(): pl.pallas_call(functools.partial(apply_kernel, order, other), grid_spec=p...  9.97 us
    ppermute x4, starting transfers between devices, swap_parts(): return lax.ppermute(value, 'parts', [(0, 1), (1, 0)])  3.95 us
    pallas_call x2, Pallas kernels, prepare(): pl.pallas_call(functools.partial(prepare_kernel, heads, block_root), grid...  3.78 us
    ppermute x4, waiting for transfers between devices, swap_parts(): return lax.ppermute(value, 'parts', [(0, 1), (1, 0)])  2.07 us
  transfers between devices with their start and end apart: 41, of which 12 were waited for; matrix products, arithmetic and copies ran while one was open for 0% of the time, Pallas kernels for 17%

profile of v13, /device:TPU:1, one launch (start us, length us, event | category | flops | bytes accessed | tf_op | source)
XLA Modules:
  0.0 100.6 jit_solution(13957454098200447250)
XLA Ops:
  0.6 0.1 pad_add_fusion.ids
  0.7 1.6 %copy-done.3 = bf16[1024,1024]{1,0:T(8,128)(2,1)S(1)} copy-done((bf16[1024,1024]{1,0:T(8,128)(2,1)S(1)}, bf16[1024,1024]{1,0:T(8,128)(2,1)}, u32[]{:S(2)}) %copy-start.3) | copy-done | bytes 2097176
  2.3 1.5 %keys.1 = (bf16[1024,512]{1,0:T(8,128)(2,1)S(1)}, bf16[1024,512]{1,0:T(8,128)(2,1)S(1)}) custom-call(s32[3]{0:T(128)S(1)} %pad_add_fusion.ids, bf16[1024,1024]{1,0:T(8,128)(2,1)S(1)} %copy-done.3), custom_call_target="tpu_custom_call" | custom-call | flops 5242880000 | bytes 41943040 | tf_op jit(solution)/shard_map/keys/pallas_call | solution.py:248
  3.9 0.6 pack.1
  4.4 0.1 collective-permute-start
  4.6 0.5 collective-permute-start.2
  5.0 0.9 collective-permute-done.got
  6.0 2.3 %values.1 = (bf16[1024,512]{1,0:T(8,128)(2,1)S(1)}, bf16[1024,512]{1,0:T(8,128)(2,1)S(1)}) custom-call(s32[3]{0:T(128)S(1)} %pad_add_fusion.ids, bf16[1024,1024]{1,0:T(8,128)(2,1)S(1)} %copy-done.4, f32[4,1024]{1,0:T(4,128)S(1)} %copy-done.5), custom_call_target="tpu_custom_call" | custom-call | flops 5242880000 | bytes 41943040 | tf_op jit(solution)/shard_map/values/pallas_call | solution.py:248
  8.2 0.2 collective-permute-start.3
  8.5 2.7 %collective-permute-start.1 = (bf16[2,96,256]{2,1,0:T(8,128)(2,1)S(1)}, bf16[2,96,256]{2,1,0:T(8,128)(2,1)S(1)}, u32[]{:S(2)}, u32[]{:S(2)}) collective-permute-start(bf16[2,96,256]{2,1,0:T(8,128)(2,1)S(1)} %get-tuple-element.52), channel_id=1, source_target_pairs={{0,4},{1,5},{2,6},{3,7},{4,0},{5,1},{6,2},{7,3},{8,12},{9,13},{10,... | collective-permute-start | bytes 294920 | tf_op jit(solution)/shard_map/ppermute | solution.py:140
  11.2 2.3 %collective-permute-start.5 = (bf16[2,96,256]{2,1,0:T(8,128)(2,1)S(1)}, bf16[2,96,256]{2,1,0:T(8,128)(2,1)S(1)}, u32[]{:S(2)}, u32[]{:S(2)}) collective-permute-start(bf16[2,96,256]{2,1,0:T(8,128)(2,1)S(1)} %get-tuple-element.52), channel_id=1, source_target_pairs={{0,8},{1,9},{2,10},{3,11},{4,12},{5,13},{6,14},{7,15},{8,0},{9,1},... | collective-permute-start | bytes 294920 | tf_op jit(solution)/shard_map/ppermute | solution.py:140
  13.5 0.7 collective-permute-done.1
  14.3 1.2 %collective-permute-start.7 = (bf16[2,2,96,256]{3,2,1,0:T(8,128)(2,1)S(1)}, bf16[2,2,96,256]{3,2,1,0:T(8,128)(2,1)S(1)}, u32[]{:S(2)}, u32[]{:S(2)}) collective-permute-start(bf16[2,2,96,256]{3,2,1,0:T(8,128)(2,1)S(1)} %pad_maximum_fusion.near_low), channel_id=1, source_target_pairs={{0,2},{1,3},{2,0},{3,1},{4,6},{5,7},{6,4},{7,5},{8,10},{9,11},{10,... | collective-permute-start | bytes 589832 | tf_op jit(solution)/shard_map/ppermute | solution.py:140
  15.5 1.2 %collective-permute-start.4 = (bf16[2,2,96,256]{3,2,1,0:T(8,128)(2,1)S(1)}, bf16[2,2,96,256]{3,2,1,0:T(8,128)(2,1)S(1)}, u32[]{:S(2)}, u32[]{:S(2)}) collective-permute-start(bf16[2,2,96,256]{3,2,1,0:T(8,128)(2,1)S(1)} %pad_maximum_fusion.near_low), channel_id=1, source_target_pairs={{0,16},{16,0},{1,17},{17,1},{2,18},{18,2},{3,19},{19,3},{4,20},{20... | collective-permute-start | bytes 589832 | tf_op jit(solution)/shard_map/ppermute | solution.py:144
  16.7 3.7 %collective-permute-done.6 = bf16[2,96,256]{2,1,0:T(8,128)(2,1)S(1)} collective-permute-done((bf16[2,96,256]{2,1,0:T(8,128)(2,1)S(1)}, bf16[2,96,256]{2,1,0:T(8,128)(2,1)S(1)}, u32[]{:S(2)}, u32[]{:S(2)}) %collective-permute-start.6) | collective-permute-done | bytes 98336 | tf_op jit(solution)/shard_map/ppermute | solution.py:140
  20.5 1.3 %collective-permute-start.9 = (bf16[2,2,96,256]{3,2,1,0:T(8,128)(2,1)S(1)}, bf16[2,2,96,256]{3,2,1,0:T(8,128)(2,1)S(1)}, u32[]{:S(2)}, u32[]{:S(2)}) collective-permute-start(bf16[2,2,96,256]{3,2,1,0:T(8,128)(2,1)S(1)} %collective-permute-done.7.far_low), channel_id=1, source_target_pairs={{0,16},{16,0},{1,17},{17,1},{2,18},{18,2},{3,19},{19,3},{4,20},{20... | collective-permute-start | bytes 589832 | tf_op jit(solution)/shard_map/ppermute | solution.py:144
  21.8 1.2 %collective-permute-start.10 = (bf16[2,2,96,256]{3,2,1,0:T(8,128)(2,1)S(1)}, bf16[2,2,96,256]{3,2,1,0:T(8,128)(2,1)S(1)}, u32[]{:S(2)}, u32[]{:S(2)}) collective-permute-start(bf16[2,2,96,256]{3,2,1,0:T(8,128)(2,1)S(1)} %pad_maximum_fusion.1.near_high), channel_id=1, source_target_pairs={{0,2},{1,3},{2,0},{3,1},{4,6},{5,7},{6,4},{7,5},{8,10},{9,11},{10,... | collective-permute-start | bytes 589832 | tf_op jit(solution)/shard_map/ppermute | solution.py:140
  23.0 2.1 %collective-permute-done.9.far_low = bf16[2,2,96,256]{3,2,1,0:T(8,128)(2,1)S(1)} collective-permute-done((bf16[2,2,96,256]{3,2,1,0:T(8,128)(2,1)S(1)}, bf16[2,2,96,256]{3,2,1,0:T(8,128)(2,1)S(1)}, u32[]{:S(2)}, u32[]{:S(2)}) %collective-permute-start.9) | collective-permute-done | bytes 196640 | tf_op jit(solution)/shard_map/ppermute | solution.py:144
  25.1 1.5 %collective-permute-done.10.far_high = bf16[2,2,96,256]{3,2,1,0:T(8,128)(2,1)S(1)} collective-permute-done((bf16[2,2,96,256]{3,2,1,0:T(8,128)(2,1)S(1)}, bf16[2,2,96,256]{3,2,1,0:T(8,128)(2,1)S(1)}, u32[]{:S(2)}, u32[]{:S(2)}) %collective-permute-start.10) | collective-permute-done | bytes 196640 | tf_op jit(solution)/shard_map/ppermute | solution.py:140
  26.6 5.6 %increments.3 = (f32[4,2,96,256]{3,2,1,0:T(8,128)S(1)}, bf16[2,2,96,256]{3,2,1,0:T(8,128)(2,1)S(1)}, bf16[2,2,96,256]{3,2,1,0:T(8,128)(2,1)S(1)}) custom-call(s32[3]{0:T(128)S(1)} %pad_add_fusion.ids, bf16[2,2,96,256]{3,2,1,0:T(8,128)(2,1)S(1)} %pad_maximum_fusion.near_low, bf16[2,2,96,256]{3,2,1,0:T(8,128)(2,1)S(1)} %pad_maximum_fusion.1.near_high, ...), custom_call_target="tpu_custom_call" | custom-call | flops 3221225472 | bytes 2097152 | tf_op jit(solution)/shard_map/increments/pallas_call | solution.py:382
  32.2 1.3 %collective-permute-start.19 = (bf16[2,2,96,256]{3,2,1,0:T(8,128)(2,1)S(1)}, bf16[2,2,96,256]{3,2,1,0:T(8,128)(2,1)S(1)}, u32[]{:S(2)}, u32[]{:S(2)}) collective-permute-start(bf16[2,2,96,256]{3,2,1,0:T(8,128)(2,1)S(1)} %get-tuple-element.70), channel_id=1, source_target_pairs={{0,2},{1,3},{2,0},{3,1},{4,6},{5,7},{6,4},{7,5},{8,10},{9,11},{10,... | collective-permute-start | bytes 589832 | tf_op jit(solution)/shard_map/ppermute | solution.py:140
  33.5 0.3 collective-permute-start.8
  33.8 1.2 %collective-permute-start.11 = (bf16[2,2,96,256]{3,2,1,0:T(8,128)(2,1)S(1)}, bf16[2,2,96,256]{3,2,1,0:T(8,128)(2,1)S(1)}, u32[]{:S(2)}, u32[]{:S(2)}) collective-permute-start(bf16[2,2,96,256]{3,2,1,0:T(8,128)(2,1)S(1)} %collective-permute-done.10.far_high), channel_id=1, source_target_pairs={{0,16},{16,0},{1,17},{17,1},{2,18},{18,2},{3,19},{19,3},{4,20},{20... | collective-permute-start | bytes 589832 | tf_op jit(solution)/shard_map/ppermute | solution.py:144
  35.0 0.2 collective-permute-start.17
  35.2 1.6 %collective-permute-done.19.came = bf16[2,2,96,256]{3,2,1,0:T(8,128)(2,1)S(1)} collective-permute-done((bf16[2,2,96,256]{3,2,1,0:T(8,128)(2,1)S(1)}, bf16[2,2,96,256]{3,2,1,0:T(8,128)(2,1)S(1)}, u32[]{:S(2)}, u32[]{:S(2)}) %collective-permute-start.19) | collective-permute-done | bytes 196640 | tf_op jit(solution)/shard_map/ppermute | solution.py:140
  36.8 3.4 %collective-permute-start.20 = (bf16[2,96,256]{2,1,0:T(8,128)(2,1)S(1)}, bf16[2,96,256]{2,1,0:T(8,128)(2,1)S(1)}, u32[]{:S(2)}, u32[]{:S(2)}) collective-permute-start(bf16[2,96,256]{2,1,0:T(8,128)(2,1)S(1)} %get-tuple-element.71), channel_id=1, source_target_pairs={{0,8},{1,9},{2,10},{3,11},{4,12},{5,13},{6,14},{7,15},{8,0},{9,1},... | collective-permute-start | bytes 294920 | tf_op jit(solution)/shard_map/ppermute | solution.py:140
  40.2 1.2 %collective-permute-start.21 = (bf16[2,96,256]{2,1,0:T(8,128)(2,1)S(1)}, bf16[2,96,256]{2,1,0:T(8,128)(2,1)S(1)}, u32[]{:S(2)}, u32[]{:S(2)}) collective-permute-start(bf16[2,96,256]{2,1,0:T(8,128)(2,1)S(1)} %get-tuple-element.72), channel_id=1, source_target_pairs={{0,12},{1,13},{2,14},{3,15},{4,8},{5,9},{6,10},{7,11},{8,4},{9,5},... | collective-permute-start | bytes 294920 | tf_op jit(solution)/shard_map/ppermute | solution.py:140
  41.4 5.8 %increments.2 = (f32[4,2,96,256]{3,2,1,0:T(8,128)S(1)}, bf16[2,2,96,256]{3,2,1,0:T(8,128)(2,1)S(1)}, bf16[2,2,96,256]{3,2,1,0:T(8,128)(2,1)S(1)}) custom-call(s32[3]{0:T(128)S(1)} %pad_add_fusion.ids, bf16[2,2,96,256]{3,2,1,0:T(8,128)(2,1)S(1)} %collective-permute-done.4.near_low, bf16[2,2,96,256]{3,2,1,0:T(8,128)(2,1)S(1)} %collective-permute-done.8.near_high, ...), custom_call_target="tpu_custom_call" | custom-call | flops 3221225472 | bytes 2097152 | tf_op jit(solution)/shard_map/increments/pallas_call | solution.py:382
  47.2 1.3 %collective-permute-start.14 = (bf16[2,2,96,256]{3,2,1,0:T(8,128)(2,1)S(1)}, bf16[2,2,96,256]{3,2,1,0:T(8,128)(2,1)S(1)}, u32[]{:S(2)}, u32[]{:S(2)}) collective-permute-start(bf16[2,2,96,256]{3,2,1,0:T(8,128)(2,1)S(1)} %get-tuple-element.60), channel_id=1, source_target_pairs={{0,2},{1,3},{2,0},{3,1},{4,6},{5,7},{6,4},{7,5},{8,10},{9,11},{10,... | collective-permute-start | bytes 589832 | tf_op jit(solution)/shard_map/ppermute | solution.py:140
  48.5 1.5 %collective-permute-start.18 = (bf16[2,96,256]{2,1,0:T(8,128)(2,1)S(1)}, bf16[2,96,256]{2,1,0:T(8,128)(2,1)S(1)}, u32[]{:S(2)}, u32[]{:S(2)}) collective-permute-start(bf16[2,96,256]{2,1,0:T(8,128)(2,1)S(1)} %get-tuple-element.69), channel_id=1, source_target_pairs={{0,4},{1,5},{2,6},{3,7},{4,0},{5,1},{6,2},{7,3},{8,12},{9,13},{10,... | collective-permute-start | bytes 294920 | tf_op jit(solution)/shard_map/ppermute | solution.py:140
  50.0 1.3 %collective-permute-start.12 = (bf16[2,2,96,256]{3,2,1,0:T(8,128)(2,1)S(1)}, bf16[2,2,96,256]{3,2,1,0:T(8,128)(2,1)S(1)}, u32[]{:S(2)}, u32[]{:S(2)}) collective-permute-start(bf16[2,2,96,256]{3,2,1,0:T(8,128)(2,1)S(1)} %get-tuple-element.57), channel_id=1, source_target_pairs={{0,2},{1,3},{2,0},{3,1},{4,6},{5,7},{6,4},{7,5},{8,10},{9,11},{10,... | collective-permute-start | bytes 589832 | tf_op jit(solution)/shard_map/ppermute | solution.py:140
  51.3 1.5 %collective-permute-done.18.one = bf16[2,96,256]{2,1,0:T(8,128)(2,1)S(1)} collective-permute-done((bf16[2,96,256]{2,1,0:T(8,128)(2,1)S(1)}, bf16[2,96,256]{2,1,0:T(8,128)(2,1)S(1)}, u32[]{:S(2)}, u32[]{:S(2)}) %collective-permute-start.18) | collective-permute-done | bytes 98336 | tf_op jit(solution)/shard_map/ppermute | solution.py:140
  52.8 0.1 renorm.3
  52.9 1.6 %collective-permute-start.24 = (bf16[2,96,256]{2,1,0:T(8,128)(2,1)S(1)}, bf16[2,96,256]{2,1,0:T(8,128)(2,1)S(1)}, u32[]{:S(2)}, u32[]{:S(2)}) collective-permute-start(bf16[2,96,256]{2,1,0:T(8,128)(2,1)S(1)} %get-tuple-element.73), channel_id=1, source_target_pairs={{0,8},{1,9},{2,10},{3,11},{4,12},{5,13},{6,14},{7,15},{8,0},{9,1},... | collective-permute-start | bytes 294920 | tf_op jit(solution)/shard_map/ppermute | solution.py:140
  54.6 1.2 %collective-permute-start.25 = (bf16[2,96,256]{2,1,0:T(8,128)(2,1)S(1)}, bf16[2,96,256]{2,1,0:T(8,128)(2,1)S(1)}, u32[]{:S(2)}, u32[]{:S(2)}) collective-permute-start(bf16[2,96,256]{2,1,0:T(8,128)(2,1)S(1)} %get-tuple-element.73), channel_id=1, source_target_pairs={{0,12},{1,13},{2,14},{3,15},{4,8},{5,9},{6,10},{7,11},{8,4},{9,5},... | collective-permute-start | bytes 294920 | tf_op jit(solution)/shard_map/ppermute | solution.py:140
  55.9 2.4 %collective-permute-start.15 = (bf16[2,96,256]{2,1,0:T(8,128)(2,1)S(1)}, bf16[2,96,256]{2,1,0:T(8,128)(2,1)S(1)}, u32[]{:S(2)}, u32[]{:S(2)}) collective-permute-start(bf16[2,96,256]{2,1,0:T(8,128)(2,1)S(1)} %get-tuple-element.61), channel_id=1, source_target_pairs={{0,8},{1,9},{2,10},{3,11},{4,12},{5,13},{6,14},{7,15},{8,0},{9,1},... | collective-permute-start | bytes 294920 | tf_op jit(solution)/shard_map/ppermute | solution.py:140
  58.3 1.2 %collective-permute-start.16 = (bf16[2,96,256]{2,1,0:T(8,128)(2,1)S(1)}, bf16[2,96,256]{2,1,0:T(8,128)(2,1)S(1)}, u32[]{:S(2)}, u32[]{:S(2)}) collective-permute-start(bf16[2,96,256]{2,1,0:T(8,128)(2,1)S(1)} %get-tuple-element.62), channel_id=1, source_target_pairs={{0,12},{1,13},{2,14},{3,15},{4,8},{5,9},{6,10},{7,11},{8,4},{9,5},... | collective-permute-start | bytes 294920 | tf_op jit(solution)/shard_map/ppermute | solution.py:140
  59.5 0.1 collective-permute-start.13
  59.6 0.4 collective-permute-done.25
  60.1 1.3 %collective-permute-start.31 = (bf16[2,2,96,256]{3,2,1,0:T(8,128)(2,1)S(1)}, bf16[2,2,96,256]{3,2,1,0:T(8,128)(2,1)S(1)}, u32[]{:S(2)}, u32[]{:S(2)}) collective-permute-start(bf16[2,2,96,256]{3,2,1,0:T(8,128)(2,1)S(1)} %pad_maximum_fusion.4.near_high), channel_id=1, source_target_pairs={{0,2},{1,3},{2,0},{3,1},{4,6},{5,7},{6,4},{7,5},{8,10},{9,11},{10,... | collective-permute-start | bytes 589832 | tf_op jit(solution)/shard_map/ppermute | solution.py:140
  61.5 1.2 %collective-permute-start.30 = (bf16[2,2,96,256]{3,2,1,0:T(8,128)(2,1)S(1)}, bf16[2,2,96,256]{3,2,1,0:T(8,128)(2,1)S(1)}, u32[]{:S(2)}, u32[]{:S(2)}) collective-permute-start(bf16[2,2,96,256]{3,2,1,0:T(8,128)(2,1)S(1)} %pad_maximum_fusion.2.near_low), channel_id=1, source_target_pairs={{0,2},{1,3},{2,0},{3,1},{4,6},{5,7},{6,4},{7,5},{8,10},{9,11},{10,... | collective-permute-start | bytes 589832 | tf_op jit(solution)/shard_map/ppermute | solution.py:140
  62.7 1.3 %collective-permute-done.15.two = bf16[2,96,256]{2,1,0:T(8,128)(2,1)S(1)} collective-permute-done((bf16[2,96,256]{2,1,0:T(8,128)(2,1)S(1)}, bf16[2,96,256]{2,1,0:T(8,128)(2,1)S(1)}, u32[]{:S(2)}, u32[]{:S(2)}) %collective-permute-start.15) | collective-permute-done | bytes 98336 | tf_op jit(solution)/shard_map/ppermute | solution.py:140
  64.0 0.6 collective-permute-done.13.one
  64.6 0.1 renorm.2
  64.8 3.6 %collective-permute-start.23 = (bf16[2,96,256]{2,1,0:T(8,128)(2,1)S(1)}, bf16[2,96,256]{2,1,0:T(8,128)(2,1)S(1)}, u32[]{:S(2)}, u32[]{:S(2)}) collective-permute-start(bf16[2,96,256]{2,1,0:T(8,128)(2,1)S(1)} %get-tuple-element.76), channel_id=1, source_target_pairs={{0,4},{1,5},{2,6},{3,7},{4,0},{5,1},{6,2},{7,3},{8,12},{9,13},{10,... | collective-permute-start | bytes 294920 | tf_op jit(solution)/shard_map/ppermute | solution.py:140
  68.3 6.5 %collective-permute-start.32 = (f32[2,96,256]{2,1,0:T(8,128)S(1)}, f32[2,96,256]{2,1,0:T(8,128)S(1)}, u32[]{:S(2)}, u32[]{:S(2)}) collective-permute-start(f32[2,96,256]{2,1,0:T(8,128)S(1)} %pad_maximum_fusion.6), channel_id=1, source_target_pairs={{0,1},{1,0},{2,3},{3,2},{4,5},{5,4},{6,7},{7,6},{8,9},{9,8},{10,11... | collective-permute-start | bytes 589832 | tf_op jit(solution)/shard_map/ppermute | solution.py:140
  74.9 1.8 %collective-permute-start.27 = (bf16[2,96,256]{2,1,0:T(8,128)(2,1)S(1)}, bf16[2,96,256]{2,1,0:T(8,128)(2,1)S(1)}, u32[]{:S(2)}, u32[]{:S(2)}) collective-permute-start(bf16[2,96,256]{2,1,0:T(8,128)(2,1)S(1)} %get-tuple-element.76), channel_id=1, source_target_pairs={{0,8},{1,9},{2,10},{3,11},{4,12},{5,13},{6,14},{7,15},{8,0},{9,1},... | collective-permute-start | bytes 294920 | tf_op jit(solution)/shard_map/ppermute | solution.py:140
  76.7 1.7 %collective-permute-start.28 = (bf16[2,96,256]{2,1,0:T(8,128)(2,1)S(1)}, bf16[2,96,256]{2,1,0:T(8,128)(2,1)S(1)}, u32[]{:S(2)}, u32[]{:S(2)}) collective-permute-start(bf16[2,96,256]{2,1,0:T(8,128)(2,1)S(1)} %get-tuple-element.76), channel_id=1, source_target_pairs={{0,12},{1,13},{2,14},{3,15},{4,8},{5,9},{6,10},{7,11},{8,4},{9,5},... | collective-permute-start | bytes 294920 | tf_op jit(solution)/shard_map/ppermute | solution.py:140
  78.4 0.6 collective-permute-start.29
  79.0 4.5 %collective-permute-start.37 = (bf16[2,2,96,256]{3,2,1,0:T(8,128)(2,1)S(1)}, bf16[2,2,96,256]{3,2,1,0:T(8,128)(2,1)S(1)}, u32[]{:S(2)}, u32[]{:S(2)}) collective-permute-start(bf16[2,2,96,256]{3,2,1,0:T(8,128)(2,1)S(1)} %pad_maximum_fusion.4.near_high), channel_id=1, source_target_pairs={{0,1},{1,0},{2,3},{3,2},{4,5},{5,4},{6,7},{7,6},{8,9},{9,8},{10,11... | collective-permute-start | bytes 589832 | tf_op jit(solution)/shard_map/ppermute | solution.py:140
  83.5 2.5 %apply.4.rest_0_ = bf16[1024,1024]{1,0:T(8,128)(2,1)} custom-call(s32[3]{0:T(128)S(1)} %pad_add_fusion.ids, bf16[2,2,96,256]{3,2,1,0:T(8,128)(2,1)S(1)} %pad_maximum_fusion.2.near_low, bf16[2,2,96,256]{3,2,1,0:T(8,128)(2,1)S(1)} %pad_maximum_fusion.4.near_high, bf16[2,2,96,256]{3,2,1,0:T(8,128)(2,1)S(1)} %collective-permute-done.30.far_low, ...), custom_call_target="tpu_custom_call" | custom-call | flops 805306368 | bytes 1048576 | tf_op jit(solution)/shard_map/apply/pallas_call | solution.py:509
  86.0 0.1 collective-permute-start.36
  86.1 1.3 %finish.1 = (f32[4,16,1024]{2,1,0:T(8,128)}, f32[4,32,256]{2,1,0:T(8,128)}) custom-call(s32[3]{0:T(128)S(1)} %pad_add_fusion.ids, f32[2,96,256]{2,1,0:T(8,128)S(1)} %get-tuple-element.77.one, f32[2,96,256]{2,1,0:T(8,128)S(1)} %get-tuple-element.78.two, f32[2,96,256]{2,1,0:T(8,128)S(1)} %collective-permute-done.32.came), custom_call_target="tpu_custom_call" | custom-call | tf_op jit(solution)/shard_map/finish/pallas_call | solution.py:546
  87.4 0.5 collective-permute-start.39
  87.9 0.1 collective-permute-start.38
  88.0 0.4 collective-permute-start.35
  88.4 0.7 collective-permute-start.26
  89.2 0.1 collective-permute-start.33
  89.2 0.4 collective-permute-start.34
  89.7 2.5 %apply.5.rest_0_ = bf16[1024,1024]{1,0:T(8,128)(2,1)} custom-call(s32[3]{0:T(128)S(1)} %pad_add_fusion.ids, bf16[2,2,96,256]{3,2,1,0:T(8,128)(2,1)S(1)} %collective-permute-done.36.near_low, bf16[2,2,96,256]{3,2,1,0:T(8,128)(2,1)S(1)} %collective-permute-done.37.near_high, ...), custom_call_target="tpu_custom_call", output_to_operand_aliasing={{}: (6, {})} | custom-call | flops 805306368 | bytes 1048576 | tf_op jit(solution)/shard_map/apply/pallas_call | solution.py:509
  92.2 1.9 %collective-permute-done.35.far_high = bf16[2,2,96,256]{3,2,1,0:T(8,128)(2,1)S(1)} collective-permute-done((bf16[2,2,96,256]{3,2,1,0:T(8,128)(2,1)S(1)}, bf16[2,2,96,256]{3,2,1,0:T(8,128)(2,1)S(1)}, u32[]{:S(2)}, u32[]{:S(2)}) %collective-permute-start.35) | collective-permute-done | bytes 196640 | tf_op jit(solution)/shard_map/ppermute | solution.py:140
  94.1 1.3 %collective-permute-start.40 = (bf16[2,2,96,256]{3,2,1,0:T(8,128)(2,1)S(1)}, bf16[2,2,96,256]{3,2,1,0:T(8,128)(2,1)S(1)}, u32[]{:S(2)}, u32[]{:S(2)}) collective-permute-start(bf16[2,2,96,256]{3,2,1,0:T(8,128)(2,1)S(1)} %collective-permute-done.35.far_high), channel_id=1, source_target_pairs={{0,1},{1,0},{2,3},{3,2},{4,5},{5,4},{6,7},{7,6},{8,9},{9,8},{10,11... | collective-permute-start | bytes 589832 | tf_op jit(solution)/shard_map/ppermute | solution.py:140
  95.4 2.5 %apply.6.rest_0_ = bf16[1024,1024]{1,0:T(8,128)(2,1)} custom-call(s32[3]{0:T(128)S(1)} %pad_add_fusion.ids, bf16[2,2,96,256]{3,2,1,0:T(8,128)(2,1)S(1)} %pad_maximum_fusion.3.near_low, bf16[2,2,96,256]{3,2,1,0:T(8,128)(2,1)S(1)} %pad_maximum_fusion.5.near_high, ...), custom_call_target="tpu_custom_call", output_to_operand_aliasing={{}: (6, {})} | custom-call | flops 805306368 | bytes 1048576 | tf_op jit(solution)/shard_map/apply/pallas_call | solution.py:509
  97.9 2.5 %apply.7 = bf16[1024,1024]{1,0:T(8,128)(2,1)} custom-call(s32[3]{0:T(128)S(1)} %pad_add_fusion.ids, bf16[2,2,96,256]{3,2,1,0:T(8,128)(2,1)S(1)} %collective-permute-done.26.near_low, bf16[2,2,96,256]{3,2,1,0:T(8,128)(2,1)S(1)} %collective-permute-done.33.near_high, ...), custom_call_target="tpu_custom_call", output_to_operand_aliasing={{}: (6, {})} | custom-call | flops 805306368 | bytes 1048576 | tf_op jit(solution)/shard_map/apply/pallas_call | solution.py:509
  (57 shorter events, 0.5 us)
Async XLA Ops:
  0.7 1.6 %copy-start.3 = (bf16[1024,1024]{1,0:T(8,128)(2,1)S(1)}, bf16[1024,1024]{1,0:T(8,128)(2,1)}, u32[]{:S(2)}) copy-start(bf16[1024,1024]{1,0:T(8,128)(2,1)} %x_ref.2) | copy-start | bytes 6291460
  2.3 1.5 %copy-start.1 = (f32[4,16,1024]{2,1,0:T(8,128)S(1)}, f32[4,16,1024]{2,1,0:T(8,128)}, u32[]{:S(2)}) copy-start(f32[4,16,1024]{2,1,0:T(8,128)} %in_ref.1) | copy-start | bytes 786436
  2.3 1.5 %copy-start.2 = (f32[4,32,256]{2,1,0:T(8,128)S(1)}, f32[4,32,256]{2,1,0:T(8,128)}, u32[]{:S(2)}) copy-start(f32[4,32,256]{2,1,0:T(8,128)} %out_ref.1) | copy-start | bytes 393220
  2.3 3.6 %copy-start.4 = (bf16[1024,1024]{1,0:T(8,128)(2,1)S(1)}, bf16[1024,1024]{1,0:T(8,128)(2,1)}, u32[]{:S(2)}) copy-start(bf16[1024,1024]{1,0:T(8,128)(2,1)} %x_ref.3) | copy-start | bytes 6291460
  2.3 3.6 %copy-start.5 = (f32[4,1024]{1,0:T(4,128)S(1)}, f32[4,1024]{1,0:T(4,128)}, u32[]{:S(2)}) copy-start(f32[4,1024]{1,0:T(4,128)} %rest_0_.1) | copy-start | bytes 49156
  4.4 1.5 %collective-permute-start = (f32[2,96,256]{2,1,0:T(8,128)S(1)}, f32[2,96,256]{2,1,0:T(8,128)S(1)}, u32[]{:S(2)}, u32[]{:S(2)}) collective-permute-start(f32[2,96,256]{2,1,0:T(8,128)S(1)} %get-tuple-element.46), channel_id=1, source_target_pairs={{0,1},{1,0},{2,3},{3,2},{4,5},{5,4},{6,7},{7,6},{8,9},{9,8},{10,11... | collective-permute-start | bytes 589832 | tf_op jit(solution)/shard_map/ppermute | solution.py:140
  4.6 9.7 %collective-permute-start.2 = (bf16[1024,512]{1,0:T(8,128)(2,1)S(1)}, bf16[1024,512]{1,0:T(8,128)(2,1)S(1)}, u32[]{:S(2)}, u32[]{:S(2)}) collective-permute-start(bf16[1024,512]{1,0:T(8,128)(2,1)S(1)} %get-tuple-element.47), channel_id=1, source_target_pairs={{0,1},{1,0},{2,3},{3,2},{4,5},{5,4},{6,7},{7,6},{8,9},{9,8},{10,11... | collective-permute-start | bytes 3145736 | tf_op jit(solution)/shard_map/ppermute | solution.py:140
  8.2 6.0 %collective-permute-start.3 = (bf16[1024,512]{1,0:T(8,128)(2,1)S(1)}, bf16[1024,512]{1,0:T(8,128)(2,1)S(1)}, u32[]{:S(2)}, u32[]{:S(2)}) collective-permute-start(bf16[1024,512]{1,0:T(8,128)(2,1)S(1)} %get-tuple-element.49), channel_id=1, source_target_pairs={{0,1},{1,0},{2,3},{3,2},{4,5},{5,4},{6,7},{7,6},{8,9},{9,8},{10,11... | collective-permute-start | bytes 3145736 | tf_op jit(solution)/shard_map/ppermute | solution.py:140
  8.5 5.8 %collective-permute-start.1 = (bf16[2,96,256]{2,1,0:T(8,128)(2,1)S(1)}, bf16[2,96,256]{2,1,0:T(8,128)(2,1)S(1)}, u32[]{:S(2)}, u32[]{:S(2)}) collective-permute-start(bf16[2,96,256]{2,1,0:T(8,128)(2,1)S(1)} %get-tuple-element.52), channel_id=1, source_target_pairs={{0,4},{1,5},{2,6},{3,7},{4,0},{5,1},{6,2},{7,3},{8,12},{9,13},{10,... | collective-permute-start | bytes 294920 | tf_op jit(solution)/shard_map/ppermute | solution.py:140
  11.2 5.5 %collective-permute-start.5 = (bf16[2,96,256]{2,1,0:T(8,128)(2,1)S(1)}, bf16[2,96,256]{2,1,0:T(8,128)(2,1)S(1)}, u32[]{:S(2)}, u32[]{:S(2)}) collective-permute-start(bf16[2,96,256]{2,1,0:T(8,128)(2,1)S(1)} %get-tuple-element.52), channel_id=1, source_target_pairs={{0,8},{1,9},{2,10},{3,11},{4,12},{5,13},{6,14},{7,15},{8,0},{9,1},... | collective-permute-start | bytes 294920 | tf_op jit(solution)/shard_map/ppermute | solution.py:140
  13.5 6.9 %collective-permute-start.6 = (bf16[2,96,256]{2,1,0:T(8,128)(2,1)S(1)}, bf16[2,96,256]{2,1,0:T(8,128)(2,1)S(1)}, u32[]{:S(2)}, u32[]{:S(2)}) collective-permute-start(bf16[2,96,256]{2,1,0:T(8,128)(2,1)S(1)} %get-tuple-element.52), channel_id=1, source_target_pairs={{0,12},{1,13},{2,14},{3,15},{4,8},{5,9},{6,10},{7,11},{8,4},{9,5},... | collective-permute-start | bytes 294920 | tf_op jit(solution)/shard_map/ppermute | solution.py:140
  14.3 6.2 %collective-permute-start.7 = (bf16[2,2,96,256]{3,2,1,0:T(8,128)(2,1)S(1)}, bf16[2,2,96,256]{3,2,1,0:T(8,128)(2,1)S(1)}, u32[]{:S(2)}, u32[]{:S(2)}) collective-permute-start(bf16[2,2,96,256]{3,2,1,0:T(8,128)(2,1)S(1)} %pad_maximum_fusion.near_low), channel_id=1, source_target_pairs={{0,2},{1,3},{2,0},{3,1},{4,6},{5,7},{6,4},{7,5},{8,10},{9,11},{10,... | collective-permute-start | bytes 589832 | tf_op jit(solution)/shard_map/ppermute | solution.py:140
  15.5 6.2 %collective-permute-start.4 = (bf16[2,2,96,256]{3,2,1,0:T(8,128)(2,1)S(1)}, bf16[2,2,96,256]{3,2,1,0:T(8,128)(2,1)S(1)}, u32[]{:S(2)}, u32[]{:S(2)}) collective-permute-start(bf16[2,2,96,256]{3,2,1,0:T(8,128)(2,1)S(1)} %pad_maximum_fusion.near_low), channel_id=1, source_target_pairs={{0,16},{16,0},{1,17},{17,1},{2,18},{18,2},{3,19},{19,3},{4,20},{20... | collective-permute-start | bytes 589832 | tf_op jit(solution)/shard_map/ppermute | solution.py:144
  20.5 4.6 %collective-permute-start.9 = (bf16[2,2,96,256]{3,2,1,0:T(8,128)(2,1)S(1)}, bf16[2,2,96,256]{3,2,1,0:T(8,128)(2,1)S(1)}, u32[]{:S(2)}, u32[]{:S(2)}) collective-permute-start(bf16[2,2,96,256]{3,2,1,0:T(8,128)(2,1)S(1)} %collective-permute-done.7.far_low), channel_id=1, source_target_pairs={{0,16},{16,0},{1,17},{17,1},{2,18},{18,2},{3,19},{19,3},{4,20},{20... | collective-permute-start | bytes 589832 | tf_op jit(solution)/shard_map/ppermute | solution.py:144
  21.8 4.8 %collective-permute-start.10 = (bf16[2,2,96,256]{3,2,1,0:T(8,128)(2,1)S(1)}, bf16[2,2,96,256]{3,2,1,0:T(8,128)(2,1)S(1)}, u32[]{:S(2)}, u32[]{:S(2)}) collective-permute-start(bf16[2,2,96,256]{3,2,1,0:T(8,128)(2,1)S(1)} %pad_maximum_fusion.1.near_high), channel_id=1, source_target_pairs={{0,2},{1,3},{2,0},{3,1},{4,6},{5,7},{6,4},{7,5},{8,10},{9,11},{10,... | collective-permute-start | bytes 589832 | tf_op jit(solution)/shard_map/ppermute | solution.py:140
  32.2 4.6 %collective-permute-start.19 = (bf16[2,2,96,256]{3,2,1,0:T(8,128)(2,1)S(1)}, bf16[2,2,96,256]{3,2,1,0:T(8,128)(2,1)S(1)}, u32[]{:S(2)}, u32[]{:S(2)}) collective-permute-start(bf16[2,2,96,256]{3,2,1,0:T(8,128)(2,1)S(1)} %get-tuple-element.70), channel_id=1, source_target_pairs={{0,2},{1,3},{2,0},{3,1},{4,6},{5,7},{6,4},{7,5},{8,10},{9,11},{10,... | collective-permute-start | bytes 589832 | tf_op jit(solution)/shard_map/ppermute | solution.py:140
  33.5 7.9 %collective-permute-start.8 = (bf16[2,2,96,256]{3,2,1,0:T(8,128)(2,1)S(1)}, bf16[2,2,96,256]{3,2,1,0:T(8,128)(2,1)S(1)}, u32[]{:S(2)}, u32[]{:S(2)}) collective-permute-start(bf16[2,2,96,256]{3,2,1,0:T(8,128)(2,1)S(1)} %pad_maximum_fusion.1.near_high), channel_id=1, source_target_pairs={{0,16},{16,0},{1,17},{17,1},{2,18},{18,2},{3,19},{19,3},{4,20},{20... | collective-permute-start | bytes 589832 | tf_op jit(solution)/shard_map/ppermute | solution.py:144
  33.8 7.6 %collective-permute-start.11 = (bf16[2,2,96,256]{3,2,1,0:T(8,128)(2,1)S(1)}, bf16[2,2,96,256]{3,2,1,0:T(8,128)(2,1)S(1)}, u32[]{:S(2)}, u32[]{:S(2)}) collective-permute-start(bf16[2,2,96,256]{3,2,1,0:T(8,128)(2,1)S(1)} %collective-permute-done.10.far_high), channel_id=1, source_target_pairs={{0,16},{16,0},{1,17},{17,1},{2,18},{18,2},{3,19},{19,3},{4,20},{20... | collective-permute-start | bytes 589832 | tf_op jit(solution)/shard_map/ppermute | solution.py:144
  35.0 13.5 %collective-permute-start.17 = (bf16[2,2,96,256]{3,2,1,0:T(8,128)(2,1)S(1)}, bf16[2,2,96,256]{3,2,1,0:T(8,128)(2,1)S(1)}, u32[]{:S(2)}, u32[]{:S(2)}) collective-permute-start(bf16[2,2,96,256]{3,2,1,0:T(8,128)(2,1)S(1)} %get-tuple-element.67), channel_id=1, source_target_pairs={{0,2},{1,3},{2,0},{3,1},{4,6},{5,7},{6,4},{7,5},{8,10},{9,11},{10,... | collective-permute-start | bytes 589832 | tf_op jit(solution)/shard_map/ppermute | solution.py:140
  36.8 14.4 %collective-permute-start.20 = (bf16[2,96,256]{2,1,0:T(8,128)(2,1)S(1)}, bf16[2,96,256]{2,1,0:T(8,128)(2,1)S(1)}, u32[]{:S(2)}, u32[]{:S(2)}) collective-permute-start(bf16[2,96,256]{2,1,0:T(8,128)(2,1)S(1)} %get-tuple-element.71), channel_id=1, source_target_pairs={{0,8},{1,9},{2,10},{3,11},{4,12},{5,13},{6,14},{7,15},{8,0},{9,1},... | collective-permute-start | bytes 294920 | tf_op jit(solution)/shard_map/ppermute | solution.py:140
  40.2 11.1 %collective-permute-start.21 = (bf16[2,96,256]{2,1,0:T(8,128)(2,1)S(1)}, bf16[2,96,256]{2,1,0:T(8,128)(2,1)S(1)}, u32[]{:S(2)}, u32[]{:S(2)}) collective-permute-start(bf16[2,96,256]{2,1,0:T(8,128)(2,1)S(1)} %get-tuple-element.72), channel_id=1, source_target_pairs={{0,12},{1,13},{2,14},{3,15},{4,8},{5,9},{6,10},{7,11},{8,4},{9,5},... | collective-permute-start | bytes 294920 | tf_op jit(solution)/shard_map/ppermute | solution.py:140
  47.2 8.6 %collective-permute-start.14 = (bf16[2,2,96,256]{3,2,1,0:T(8,128)(2,1)S(1)}, bf16[2,2,96,256]{3,2,1,0:T(8,128)(2,1)S(1)}, u32[]{:S(2)}, u32[]{:S(2)}) collective-permute-start(bf16[2,2,96,256]{3,2,1,0:T(8,128)(2,1)S(1)} %get-tuple-element.60), channel_id=1, source_target_pairs={{0,2},{1,3},{2,0},{3,1},{4,6},{5,7},{6,4},{7,5},{8,10},{9,11},{10,... | collective-permute-start | bytes 589832 | tf_op jit(solution)/shard_map/ppermute | solution.py:140
  48.5 4.2 %collective-permute-start.18 = (bf16[2,96,256]{2,1,0:T(8,128)(2,1)S(1)}, bf16[2,96,256]{2,1,0:T(8,128)(2,1)S(1)}, u32[]{:S(2)}, u32[]{:S(2)}) collective-permute-start(bf16[2,96,256]{2,1,0:T(8,128)(2,1)S(1)} %get-tuple-element.69), channel_id=1, source_target_pairs={{0,4},{1,5},{2,6},{3,7},{4,0},{5,1},{6,2},{7,3},{8,12},{9,13},{10,... | collective-permute-start | bytes 294920 | tf_op jit(solution)/shard_map/ppermute | solution.py:140
  50.0 8.2 %collective-permute-start.12 = (bf16[2,2,96,256]{3,2,1,0:T(8,128)(2,1)S(1)}, bf16[2,2,96,256]{3,2,1,0:T(8,128)(2,1)S(1)}, u32[]{:S(2)}, u32[]{:S(2)}) collective-permute-start(bf16[2,2,96,256]{3,2,1,0:T(8,128)(2,1)S(1)} %get-tuple-element.57), channel_id=1, source_target_pairs={{0,2},{1,3},{2,0},{3,1},{4,6},{5,7},{6,4},{7,5},{8,10},{9,11},{10,... | collective-permute-start | bytes 589832 | tf_op jit(solution)/shard_map/ppermute | solution.py:140
  52.9 6.6 %collective-permute-start.24 = (bf16[2,96,256]{2,1,0:T(8,128)(2,1)S(1)}, bf16[2,96,256]{2,1,0:T(8,128)(2,1)S(1)}, u32[]{:S(2)}, u32[]{:S(2)}) collective-permute-start(bf16[2,96,256]{2,1,0:T(8,128)(2,1)S(1)} %get-tuple-element.73), channel_id=1, source_target_pairs={{0,8},{1,9},{2,10},{3,11},{4,12},{5,13},{6,14},{7,15},{8,0},{9,1},... | collective-permute-start | bytes 294920 | tf_op jit(solution)/shard_map/ppermute | solution.py:140
  54.6 5.5 %collective-permute-start.25 = (bf16[2,96,256]{2,1,0:T(8,128)(2,1)S(1)}, bf16[2,96,256]{2,1,0:T(8,128)(2,1)S(1)}, u32[]{:S(2)}, u32[]{:S(2)}) collective-permute-start(bf16[2,96,256]{2,1,0:T(8,128)(2,1)S(1)} %get-tuple-element.73), channel_id=1, source_target_pairs={{0,12},{1,13},{2,14},{3,15},{4,8},{5,9},{6,10},{7,11},{8,4},{9,5},... | collective-permute-start | bytes 294920 | tf_op jit(solution)/shard_map/ppermute | solution.py:140
  55.8 5.7 %collective-permute-start.22 = (bf16[2,96,256]{2,1,0:T(8,128)(2,1)S(1)}, bf16[2,96,256]{2,1,0:T(8,128)(2,1)S(1)}, u32[]{:S(2)}, u32[]{:S(2)}) collective-permute-start(bf16[2,96,256]{2,1,0:T(8,128)(2,1)S(1)} %get-tuple-element.73), channel_id=1, source_target_pairs={{0,4},{1,5},{2,6},{3,7},{4,0},{5,1},{6,2},{7,3},{8,12},{9,13},{10,... | collective-permute-start | bytes 294920 | tf_op jit(solution)/shard_map/ppermute | solution.py:140
  55.8 27.7 %copy-start = (bf16[1024,1024]{1,0:T(8,128)(2,1)S(1)}, bf16[1024,1024]{1,0:T(8,128)(2,1)}, u32[]{:S(2)}) copy-start(bf16[1024,1024]{1,0:T(8,128)(2,1)} %q_ref.7) | copy-start | bytes 6291460
  55.9 8.1 %collective-permute-start.15 = (bf16[2,96,256]{2,1,0:T(8,128)(2,1)S(1)}, bf16[2,96,256]{2,1,0:T(8,128)(2,1)S(1)}, u32[]{:S(2)}, u32[]{:S(2)}) collective-permute-start(bf16[2,96,256]{2,1,0:T(8,128)(2,1)S(1)} %get-tuple-element.61), channel_id=1, source_target_pairs={{0,8},{1,9},{2,10},{3,11},{4,12},{5,13},{6,14},{7,15},{8,0},{9,1},... | collective-permute-start | bytes 294920 | tf_op jit(solution)/shard_map/ppermute | solution.py:140
  58.3 5.8 %collective-permute-start.16 = (bf16[2,96,256]{2,1,0:T(8,128)(2,1)S(1)}, bf16[2,96,256]{2,1,0:T(8,128)(2,1)S(1)}, u32[]{:S(2)}, u32[]{:S(2)}) collective-permute-start(bf16[2,96,256]{2,1,0:T(8,128)(2,1)S(1)} %get-tuple-element.62), channel_id=1, source_target_pairs={{0,12},{1,13},{2,14},{3,15},{4,8},{5,9},{6,10},{7,11},{8,4},{9,5},... | collective-permute-start | bytes 294920 | tf_op jit(solution)/shard_map/ppermute | solution.py:140
  59.5 5.1 %collective-permute-start.13 = (bf16[2,96,256]{2,1,0:T(8,128)(2,1)S(1)}, bf16[2,96,256]{2,1,0:T(8,128)(2,1)S(1)}, u32[]{:S(2)}, u32[]{:S(2)}) collective-permute-start(bf16[2,96,256]{2,1,0:T(8,128)(2,1)S(1)} %get-tuple-element.59), channel_id=1, source_target_pairs={{0,4},{1,5},{2,6},{3,7},{4,0},{5,1},{6,2},{7,3},{8,12},{9,13},{10,... | collective-permute-start | bytes 294920 | tf_op jit(solution)/shard_map/ppermute | solution.py:140
  60.1 18.4 %collective-permute-start.31 = (bf16[2,2,96,256]{3,2,1,0:T(8,128)(2,1)S(1)}, bf16[2,2,96,256]{3,2,1,0:T(8,128)(2,1)S(1)}, u32[]{:S(2)}, u32[]{:S(2)}) collective-permute-start(bf16[2,2,96,256]{3,2,1,0:T(8,128)(2,1)S(1)} %pad_maximum_fusion.4.near_high), channel_id=1, source_target_pairs={{0,2},{1,3},{2,0},{3,1},{4,6},{5,7},{6,4},{7,5},{8,10},{9,11},{10,... | collective-permute-start | bytes 589832 | tf_op jit(solution)/shard_map/ppermute | solution.py:140
  61.5 17.5 %collective-permute-start.30 = (bf16[2,2,96,256]{3,2,1,0:T(8,128)(2,1)S(1)}, bf16[2,2,96,256]{3,2,1,0:T(8,128)(2,1)S(1)}, u32[]{:S(2)}, u32[]{:S(2)}) collective-permute-start(bf16[2,2,96,256]{3,2,1,0:T(8,128)(2,1)S(1)} %pad_maximum_fusion.2.near_low), channel_id=1, source_target_pairs={{0,2},{1,3},{2,0},{3,1},{4,6},{5,7},{6,4},{7,5},{8,10},{9,11},{10,... | collective-permute-start | bytes 589832 | tf_op jit(solution)/shard_map/ppermute | solution.py:140
  64.8 10.1 %collective-permute-start.23 = (bf16[2,96,256]{2,1,0:T(8,128)(2,1)S(1)}, bf16[2,96,256]{2,1,0:T(8,128)(2,1)S(1)}, u32[]{:S(2)}, u32[]{:S(2)}) collective-permute-start(bf16[2,96,256]{2,1,0:T(8,128)(2,1)S(1)} %get-tuple-element.76), channel_id=1, source_target_pairs={{0,4},{1,5},{2,6},{3,7},{4,0},{5,1},{6,2},{7,3},{8,12},{9,13},{10,... | collective-permute-start | bytes 294920 | tf_op jit(solution)/shard_map/ppermute | solution.py:140
  68.3 17.6 %collective-permute-start.32 = (f32[2,96,256]{2,1,0:T(8,128)S(1)}, f32[2,96,256]{2,1,0:T(8,128)S(1)}, u32[]{:S(2)}, u32[]{:S(2)}) collective-permute-start(f32[2,96,256]{2,1,0:T(8,128)S(1)} %pad_maximum_fusion.6), channel_id=1, source_target_pairs={{0,1},{1,0},{2,3},{3,2},{4,5},{5,4},{6,7},{7,6},{8,9},{9,8},{10,11... | collective-permute-start | bytes 589832 | tf_op jit(solution)/shard_map/ppermute | solution.py:140
  74.9 12.5 %collective-permute-start.27 = (bf16[2,96,256]{2,1,0:T(8,128)(2,1)S(1)}, bf16[2,96,256]{2,1,0:T(8,128)(2,1)S(1)}, u32[]{:S(2)}, u32[]{:S(2)}) collective-permute-start(bf16[2,96,256]{2,1,0:T(8,128)(2,1)S(1)} %get-tuple-element.76), channel_id=1, source_target_pairs={{0,8},{1,9},{2,10},{3,11},{4,12},{5,13},{6,14},{7,15},{8,0},{9,1},... | collective-permute-start | bytes 294920 | tf_op jit(solution)/shard_map/ppermute | solution.py:140
  76.7 11.2 %collective-permute-start.28 = (bf16[2,96,256]{2,1,0:T(8,128)(2,1)S(1)}, bf16[2,96,256]{2,1,0:T(8,128)(2,1)S(1)}, u32[]{:S(2)}, u32[]{:S(2)}) collective-permute-start(bf16[2,96,256]{2,1,0:T(8,128)(2,1)S(1)} %get-tuple-element.76), channel_id=1, source_target_pairs={{0,12},{1,13},{2,14},{3,15},{4,8},{5,9},{6,10},{7,11},{8,4},{9,5},... | collective-permute-start | bytes 294920 | tf_op jit(solution)/shard_map/ppermute | solution.py:140
  78.4 9.6 %collective-permute-start.29 = (bf16[2,2,96,256]{3,2,1,0:T(8,128)(2,1)S(1)}, bf16[2,2,96,256]{3,2,1,0:T(8,128)(2,1)S(1)}, u32[]{:S(2)}, u32[]{:S(2)}) collective-permute-start(bf16[2,2,96,256]{3,2,1,0:T(8,128)(2,1)S(1)} %pad_maximum_fusion.3.near_low), channel_id=1, source_target_pairs={{0,2},{1,3},{2,0},{3,1},{4,6},{5,7},{6,4},{7,5},{8,10},{9,11},{10,... | collective-permute-start | bytes 589832 | tf_op jit(solution)/shard_map/ppermute | solution.py:140
  79.0 9.4 %collective-permute-start.37 = (bf16[2,2,96,256]{3,2,1,0:T(8,128)(2,1)S(1)}, bf16[2,2,96,256]{3,2,1,0:T(8,128)(2,1)S(1)}, u32[]{:S(2)}, u32[]{:S(2)}) collective-permute-start(bf16[2,2,96,256]{3,2,1,0:T(8,128)(2,1)S(1)} %pad_maximum_fusion.4.near_high), channel_id=1, source_target_pairs={{0,1},{1,0},{2,3},{3,2},{4,5},{5,4},{6,7},{7,6},{8,9},{9,8},{10,11... | collective-permute-start | bytes 589832 | tf_op jit(solution)/shard_map/ppermute | solution.py:140
  86.0 3.2 %collective-permute-start.36 = (bf16[2,2,96,256]{3,2,1,0:T(8,128)(2,1)S(1)}, bf16[2,2,96,256]{3,2,1,0:T(8,128)(2,1)S(1)}, u32[]{:S(2)}, u32[]{:S(2)}) collective-permute-start(bf16[2,2,96,256]{3,2,1,0:T(8,128)(2,1)S(1)} %pad_maximum_fusion.2.near_low), channel_id=1, source_target_pairs={{0,1},{1,0},{2,3},{3,2},{4,5},{5,4},{6,7},{7,6},{8,9},{9,8},{10,11... | collective-permute-start | bytes 589832 | tf_op jit(solution)/shard_map/ppermute | solution.py:140
  87.4 1.8 %collective-permute-start.39 = (bf16[2,2,96,256]{3,2,1,0:T(8,128)(2,1)S(1)}, bf16[2,2,96,256]{3,2,1,0:T(8,128)(2,1)S(1)}, u32[]{:S(2)}, u32[]{:S(2)}) collective-permute-start(bf16[2,2,96,256]{3,2,1,0:T(8,128)(2,1)S(1)} %collective-permute-done.31.far_high), channel_id=1, source_target_pairs={{0,1},{1,0},{2,3},{3,2},{4,5},{5,4},{6,7},{7,6},{8,9},{9,8},{10,11... | collective-permute-start | bytes 589832 | tf_op jit(solution)/shard_map/ppermute | solution.py:140
  87.9 1.8 %collective-permute-start.38 = (bf16[2,2,96,256]{3,2,1,0:T(8,128)(2,1)S(1)}, bf16[2,2,96,256]{3,2,1,0:T(8,128)(2,1)S(1)}, u32[]{:S(2)}, u32[]{:S(2)}) collective-permute-start(bf16[2,2,96,256]{3,2,1,0:T(8,128)(2,1)S(1)} %collective-permute-done.30.far_low), channel_id=1, source_target_pairs={{0,1},{1,0},{2,3},{3,2},{4,5},{5,4},{6,7},{7,6},{8,9},{9,8},{10,11... | collective-permute-start | bytes 589832 | tf_op jit(solution)/shard_map/ppermute | solution.py:140
  88.0 6.1 %collective-permute-start.35 = (bf16[2,2,96,256]{3,2,1,0:T(8,128)(2,1)S(1)}, bf16[2,2,96,256]{3,2,1,0:T(8,128)(2,1)S(1)}, u32[]{:S(2)}, u32[]{:S(2)}) collective-permute-start(bf16[2,2,96,256]{3,2,1,0:T(8,128)(2,1)S(1)} %pad_maximum_fusion.5.near_high), channel_id=1, source_target_pairs={{0,2},{1,3},{2,0},{3,1},{4,6},{5,7},{6,4},{7,5},{8,10},{9,11},{10,... | collective-permute-start | bytes 589832 | tf_op jit(solution)/shard_map/ppermute | solution.py:140
  88.4 9.4 %collective-permute-start.26 = (bf16[2,2,96,256]{3,2,1,0:T(8,128)(2,1)S(1)}, bf16[2,2,96,256]{3,2,1,0:T(8,128)(2,1)S(1)}, u32[]{:S(2)}, u32[]{:S(2)}) collective-permute-start(bf16[2,2,96,256]{3,2,1,0:T(8,128)(2,1)S(1)} %pad_maximum_fusion.3.near_low), channel_id=1, source_target_pairs={{0,1},{1,0},{2,3},{3,2},{4,5},{5,4},{6,7},{7,6},{8,9},{9,8},{10,11... | collective-permute-start | bytes 589832 | tf_op jit(solution)/shard_map/ppermute | solution.py:140
  89.2 8.7 %collective-permute-start.33 = (bf16[2,2,96,256]{3,2,1,0:T(8,128)(2,1)S(1)}, bf16[2,2,96,256]{3,2,1,0:T(8,128)(2,1)S(1)}, u32[]{:S(2)}, u32[]{:S(2)}) collective-permute-start(bf16[2,2,96,256]{3,2,1,0:T(8,128)(2,1)S(1)} %pad_maximum_fusion.5.near_high), channel_id=1, source_target_pairs={{0,1},{1,0},{2,3},{3,2},{4,5},{5,4},{6,7},{7,6},{8,9},{9,8},{10,11... | collective-permute-start | bytes 589832 | tf_op jit(solution)/shard_map/ppermute | solution.py:140
  89.2 8.7 %collective-permute-start.34 = (bf16[2,2,96,256]{3,2,1,0:T(8,128)(2,1)S(1)}, bf16[2,2,96,256]{3,2,1,0:T(8,128)(2,1)S(1)}, u32[]{:S(2)}, u32[]{:S(2)}) collective-permute-start(bf16[2,2,96,256]{3,2,1,0:T(8,128)(2,1)S(1)} %collective-permute-done.29.far_low), channel_id=1, source_target_pairs={{0,1},{1,0},{2,3},{3,2},{4,5},{5,4},{6,7},{7,6},{8,9},{9,8},{10,11... | collective-permute-start | bytes 589832 | tf_op jit(solution)/shard_map/ppermute | solution.py:140
  94.1 3.8 %collective-permute-start.40 = (bf16[2,2,96,256]{3,2,1,0:T(8,128)(2,1)S(1)}, bf16[2,2,96,256]{3,2,1,0:T(8,128)(2,1)S(1)}, u32[]{:S(2)}, u32[]{:S(2)}) collective-permute-start(bf16[2,2,96,256]{3,2,1,0:T(8,128)(2,1)S(1)} %collective-permute-done.35.far_high), channel_id=1, source_target_pairs={{0,1},{1,0},{2,3},{3,2},{4,5},{5,4},{6,7},{7,6},{8,9},{9,8},{10,11... | collective-permute-start | bytes 589832 | tf_op jit(solution)/shard_map/ppermute | solution.py:140

commit v14 on v13

--- a/solution.py
+++ b/solution.py
@@ -599,13 +599,13 @@
     second = after(short[1], near_low)
     z1 = swap(second, 4)
     second_low = after(jnp.stack([second, z1]), near_high)
-    later = after(short[1], second_low)
+    later = second
     z3, z2 = swap(later, 12), swap(later, 8)
     second_high = jnp.stack([z2, z3])
     mine = (near_low, near_high, far_low, far_high)
     others = tuple(swap(piece, 1) for piece in mine)
     output = apply_fast(ids, 0, 0, mine, queries, None, fast)
-    came = swap(jnp.stack([wide[0][1], wide[1][1]]), 1)
+    came = swap(after(jnp.stack([wide[0][1], wide[1][1]]), second_low), 1)
     updated = finish(ids, wide[0], wide[1], came, fast_in, fast_out)
     near_low, far_low = second_low, swap(second_low, 2)
     near_high = after(second_high, far_low, output, *updated)

time: 101 us -> 104 us (1.030)
  waiting for transfers between devices: 16.4 us -> 19.2 us
    ppermute x37, waiting for transfers between devices: 14.3 us -> 17.1 us  [swap(): lax.ppermute(value, 'tok', [(place, place ^ bits) for place in range(coun...]
  transfers between devices with their start and end apart: 41 -> 41, of which waited for: 12 -> 13; matrix products, arithmetic and copies ran while one was open for 0% -> 0% of each run, Pallas kernels for 17% -> 17%
where the time goes in v14:
time: 104 us
  starting transfers between devices  54.3 us (52%)
  Pallas kernels  27.6 us (27%)
  waiting for transfers between devices  19.2 us (18%)
  local copies, waits for them, and re-layouts  1.63 us (2%)
  between operations  1.09 us (1%)
    ppermute x37, starting transfers between devices, swap(): lax.ppermute(value, 'tok', [(place, place ^ bits) for place in range(coun...  50.4 us
    ppermute x37, waiting for transfers between devices, swap(): lax.ppermute(value, 'tok', [(place, place ^ bits) for place in range(coun...  17.1 us
    pallas_call x2, Pallas kernels, increments(): pl.pallas_call(increments_kernel, grid_spec=pltpu.PrefetchScalarGridSpec(...  11.4 us
    pallas_call x4, Pallas kernels, apply_fast(): pl.pallas_call(functools.partial(apply_kernel, order, other), grid_spec=p...  9.98 us
    ppermute x4, starting transfers between devices, swap_parts(): return lax.ppermute(value, 'parts', [(0, 1), (1, 0)])  3.95 us
    pallas_call x2, Pallas kernels, prepare(): pl.pallas_call(functools.partial(prepare_kernel, heads, block_root), grid...  3.78 us
  transfers between devices with their start and end apart: 41, of which 13 were waited for; matrix products, arithmetic and copies ran while one was open for 0% of the time, Pallas kernels for 17%

profile of v14, /device:TPU:1, one launch (start us, length us, event | category | flops | bytes accessed | tf_op | source)
XLA Modules:
  0.0 104.0 jit_solution(14629446187869128062)
XLA Ops:
  0.6 0.1 pad_add_fusion.ids
  0.7 1.6 %copy-done.3 = bf16[1024,1024]{1,0:T(8,128)(2,1)S(1)} copy-done((bf16[1024,1024]{1,0:T(8,128)(2,1)S(1)}, bf16[1024,1024]{1,0:T(8,128)(2,1)}, u32[]{:S(2)}) %copy-start.3) | copy-done | bytes 2097176
  2.3 1.5 %keys.1 = (bf16[1024,512]{1,0:T(8,128)(2,1)S(1)}, bf16[1024,512]{1,0:T(8,128)(2,1)S(1)}) custom-call(s32[3]{0:T(128)S(1)} %pad_add_fusion.ids, bf16[1024,1024]{1,0:T(8,128)(2,1)S(1)} %copy-done.3), custom_call_target="tpu_custom_call" | custom-call | flops 5242880000 | bytes 41943040 | tf_op jit(solution)/shard_map/keys/pallas_call | solution.py:248
  3.9 0.6 pack.1
  4.4 0.1 collective-permute-start
  4.6 0.5 collective-permute-start.2
  5.0 0.9 collective-permute-done.got
  6.0 2.3 %values.1 = (bf16[1024,512]{1,0:T(8,128)(2,1)S(1)}, bf16[1024,512]{1,0:T(8,128)(2,1)S(1)}) custom-call(s32[3]{0:T(128)S(1)} %pad_add_fusion.ids, bf16[1024,1024]{1,0:T(8,128)(2,1)S(1)} %copy-done.4, f32[4,1024]{1,0:T(4,128)S(1)} %copy-done.5), custom_call_target="tpu_custom_call" | custom-call | flops 5242880000 | bytes 41943040 | tf_op jit(solution)/shard_map/values/pallas_call | solution.py:248
  8.2 0.2 collective-permute-start.3
  8.5 2.7 %collective-permute-start.1 = (bf16[2,96,256]{2,1,0:T(8,128)(2,1)S(1)}, bf16[2,96,256]{2,1,0:T(8,128)(2,1)S(1)}, u32[]{:S(2)}, u32[]{:S(2)}) collective-permute-start(bf16[2,96,256]{2,1,0:T(8,128)(2,1)S(1)} %get-tuple-element.52), channel_id=1, source_target_pairs={{0,4},{1,5},{2,6},{3,7},{4,0},{5,1},{6,2},{7,3},{8,12},{9,13},{10,... | collective-permute-start | bytes 294920 | tf_op jit(solution)/shard_map/ppermute | solution.py:140
  11.2 2.3 %collective-permute-start.5 = (bf16[2,96,256]{2,1,0:T(8,128)(2,1)S(1)}, bf16[2,96,256]{2,1,0:T(8,128)(2,1)S(1)}, u32[]{:S(2)}, u32[]{:S(2)}) collective-permute-start(bf16[2,96,256]{2,1,0:T(8,128)(2,1)S(1)} %get-tuple-element.52), channel_id=1, source_target_pairs={{0,8},{1,9},{2,10},{3,11},{4,12},{5,13},{6,14},{7,15},{8,0},{9,1},... | collective-permute-start | bytes 294920 | tf_op jit(solution)/shard_map/ppermute | solution.py:140
  13.5 0.7 collective-permute-done.1
  14.3 1.2 %collective-permute-start.7 = (bf16[2,2,96,256]{3,2,1,0:T(8,128)(2,1)S(1)}, bf16[2,2,96,256]{3,2,1,0:T(8,128)(2,1)S(1)}, u32[]{:S(2)}, u32[]{:S(2)}) collective-permute-start(bf16[2,2,96,256]{3,2,1,0:T(8,128)(2,1)S(1)} %pad_maximum_fusion.near_low), channel_id=1, source_target_pairs={{0,2},{1,3},{2,0},{3,1},{4,6},{5,7},{6,4},{7,5},{8,10},{9,11},{10,... | collective-permute-start | bytes 589832 | tf_op jit(solution)/shard_map/ppermute | solution.py:140
  15.5 1.2 %collective-permute-start.4 = (bf16[2,2,96,256]{3,2,1,0:T(8,128)(2,1)S(1)}, bf16[2,2,96,256]{3,2,1,0:T(8,128)(2,1)S(1)}, u32[]{:S(2)}, u32[]{:S(2)}) collective-permute-start(bf16[2,2,96,256]{3,2,1,0:T(8,128)(2,1)S(1)} %pad_maximum_fusion.near_low), channel_id=1, source_target_pairs={{0,16},{16,0},{1,17},{17,1},{2,18},{18,2},{3,19},{19,3},{4,20},{20... | collective-permute-start | bytes 589832 | tf_op jit(solution)/shard_map/ppermute | solution.py:144
  16.7 3.7 %collective-permute-done.6 = bf16[2,96,256]{2,1,0:T(8,128)(2,1)S(1)} collective-permute-done((bf16[2,96,256]{2,1,0:T(8,128)(2,1)S(1)}, bf16[2,96,256]{2,1,0:T(8,128)(2,1)S(1)}, u32[]{:S(2)}, u32[]{:S(2)}) %collective-permute-start.6) | collective-permute-done | bytes 98336 | tf_op jit(solution)/shard_map/ppermute | solution.py:140
  20.5 1.3 %collective-permute-start.9 = (bf16[2,2,96,256]{3,2,1,0:T(8,128)(2,1)S(1)}, bf16[2,2,96,256]{3,2,1,0:T(8,128)(2,1)S(1)}, u32[]{:S(2)}, u32[]{:S(2)}) collective-permute-start(bf16[2,2,96,256]{3,2,1,0:T(8,128)(2,1)S(1)} %collective-permute-done.7.far_low), channel_id=1, source_target_pairs={{0,16},{16,0},{1,17},{17,1},{2,18},{18,2},{3,19},{19,3},{4,20},{20... | collective-permute-start | bytes 589832 | tf_op jit(solution)/shard_map/ppermute | solution.py:144
  21.8 1.2 %collective-permute-start.10 = (bf16[2,2,96,256]{3,2,1,0:T(8,128)(2,1)S(1)}, bf16[2,2,96,256]{3,2,1,0:T(8,128)(2,1)S(1)}, u32[]{:S(2)}, u32[]{:S(2)}) collective-permute-start(bf16[2,2,96,256]{3,2,1,0:T(8,128)(2,1)S(1)} %pad_maximum_fusion.1.near_high), channel_id=1, source_target_pairs={{0,2},{1,3},{2,0},{3,1},{4,6},{5,7},{6,4},{7,5},{8,10},{9,11},{10,... | collective-permute-start | bytes 589832 | tf_op jit(solution)/shard_map/ppermute | solution.py:140
  23.0 2.1 %collective-permute-done.9.far_low = bf16[2,2,96,256]{3,2,1,0:T(8,128)(2,1)S(1)} collective-permute-done((bf16[2,2,96,256]{3,2,1,0:T(8,128)(2,1)S(1)}, bf16[2,2,96,256]{3,2,1,0:T(8,128)(2,1)S(1)}, u32[]{:S(2)}, u32[]{:S(2)}) %collective-permute-start.9) | collective-permute-done | bytes 196640 | tf_op jit(solution)/shard_map/ppermute | solution.py:144
  25.1 1.5 %collective-permute-done.10.far_high = bf16[2,2,96,256]{3,2,1,0:T(8,128)(2,1)S(1)} collective-permute-done((bf16[2,2,96,256]{3,2,1,0:T(8,128)(2,1)S(1)}, bf16[2,2,96,256]{3,2,1,0:T(8,128)(2,1)S(1)}, u32[]{:S(2)}, u32[]{:S(2)}) %collective-permute-start.10) | collective-permute-done | bytes 196640 | tf_op jit(solution)/shard_map/ppermute | solution.py:140
  26.6 5.6 %increments.3 = (f32[4,2,96,256]{3,2,1,0:T(8,128)S(1)}, bf16[2,2,96,256]{3,2,1,0:T(8,128)(2,1)S(1)}, bf16[2,2,96,256]{3,2,1,0:T(8,128)(2,1)S(1)}) custom-call(s32[3]{0:T(128)S(1)} %pad_add_fusion.ids, bf16[2,2,96,256]{3,2,1,0:T(8,128)(2,1)S(1)} %pad_maximum_fusion.near_low, bf16[2,2,96,256]{3,2,1,0:T(8,128)(2,1)S(1)} %pad_maximum_fusion.1.near_high, ...), custom_call_target="tpu_custom_call" | custom-call | flops 3221225472 | bytes 2097152 | tf_op jit(solution)/shard_map/increments/pallas_call | solution.py:382
  32.2 1.3 %collective-permute-start.19 = (bf16[2,2,96,256]{3,2,1,0:T(8,128)(2,1)S(1)}, bf16[2,2,96,256]{3,2,1,0:T(8,128)(2,1)S(1)}, u32[]{:S(2)}, u32[]{:S(2)}) collective-permute-start(bf16[2,2,96,256]{3,2,1,0:T(8,128)(2,1)S(1)} %get-tuple-element.70), channel_id=1, source_target_pairs={{0,2},{1,3},{2,0},{3,1},{4,6},{5,7},{6,4},{7,5},{8,10},{9,11},{10,... | collective-permute-start | bytes 589832 | tf_op jit(solution)/shard_map/ppermute | solution.py:140
  33.5 0.3 collective-permute-start.8
  33.8 1.2 %collective-permute-start.11 = (bf16[2,2,96,256]{3,2,1,0:T(8,128)(2,1)S(1)}, bf16[2,2,96,256]{3,2,1,0:T(8,128)(2,1)S(1)}, u32[]{:S(2)}, u32[]{:S(2)}) collective-permute-start(bf16[2,2,96,256]{3,2,1,0:T(8,128)(2,1)S(1)} %collective-permute-done.10.far_high), channel_id=1, source_target_pairs={{0,16},{16,0},{1,17},{17,1},{2,18},{18,2},{3,19},{19,3},{4,20},{20... | collective-permute-start | bytes 589832 | tf_op jit(solution)/shard_map/ppermute | solution.py:144
  35.0 0.2 collective-permute-start.17
  35.2 1.6 %collective-permute-done.19.came = bf16[2,2,96,256]{3,2,1,0:T(8,128)(2,1)S(1)} collective-permute-done((bf16[2,2,96,256]{3,2,1,0:T(8,128)(2,1)S(1)}, bf16[2,2,96,256]{3,2,1,0:T(8,128)(2,1)S(1)}, u32[]{:S(2)}, u32[]{:S(2)}) %collective-permute-start.19) | collective-permute-done | bytes 196640 | tf_op jit(solution)/shard_map/ppermute | solution.py:140
  36.8 3.4 %collective-permute-start.20 = (bf16[2,96,256]{2,1,0:T(8,128)(2,1)S(1)}, bf16[2,96,256]{2,1,0:T(8,128)(2,1)S(1)}, u32[]{:S(2)}, u32[]{:S(2)}) collective-permute-start(bf16[2,96,256]{2,1,0:T(8,128)(2,1)S(1)} %get-tuple-element.71), channel_id=1, source_target_pairs={{0,8},{1,9},{2,10},{3,11},{4,12},{5,13},{6,14},{7,15},{8,0},{9,1},... | collective-permute-start | bytes 294920 | tf_op jit(solution)/shard_map/ppermute | solution.py:140
  40.2 1.2 %collective-permute-start.21 = (bf16[2,96,256]{2,1,0:T(8,128)(2,1)S(1)}, bf16[2,96,256]{2,1,0:T(8,128)(2,1)S(1)}, u32[]{:S(2)}, u32[]{:S(2)}) collective-permute-start(bf16[2,96,256]{2,1,0:T(8,128)(2,1)S(1)} %get-tuple-element.72), channel_id=1, source_target_pairs={{0,12},{1,13},{2,14},{3,15},{4,8},{5,9},{6,10},{7,11},{8,4},{9,5},... | collective-permute-start | bytes 294920 | tf_op jit(solution)/shard_map/ppermute | solution.py:140
  41.4 5.8 %increments.2 = (f32[4,2,96,256]{3,2,1,0:T(8,128)S(1)}, bf16[2,2,96,256]{3,2,1,0:T(8,128)(2,1)S(1)}, bf16[2,2,96,256]{3,2,1,0:T(8,128)(2,1)S(1)}) custom-call(s32[3]{0:T(128)S(1)} %pad_add_fusion.ids, bf16[2,2,96,256]{3,2,1,0:T(8,128)(2,1)S(1)} %collective-permute-done.4.near_low, bf16[2,2,96,256]{3,2,1,0:T(8,128)(2,1)S(1)} %collective-permute-done.8.near_high, ...), custom_call_target="tpu_custom_call" | custom-call | flops 3221225472 | bytes 2097152 | tf_op jit(solution)/shard_map/increments/pallas_call | solution.py:382
  47.2 1.3 %collective-permute-start.14 = (bf16[2,2,96,256]{3,2,1,0:T(8,128)(2,1)S(1)}, bf16[2,2,96,256]{3,2,1,0:T(8,128)(2,1)S(1)}, u32[]{:S(2)}, u32[]{:S(2)}) collective-permute-start(bf16[2,2,96,256]{3,2,1,0:T(8,128)(2,1)S(1)} %get-tuple-element.60), channel_id=1, source_target_pairs={{0,2},{1,3},{2,0},{3,1},{4,6},{5,7},{6,4},{7,5},{8,10},{9,11},{10,... | collective-permute-start | bytes 589832 | tf_op jit(solution)/shard_map/ppermute | solution.py:140
  48.5 1.5 %collective-permute-start.18 = (bf16[2,96,256]{2,1,0:T(8,128)(2,1)S(1)}, bf16[2,96,256]{2,1,0:T(8,128)(2,1)S(1)}, u32[]{:S(2)}, u32[]{:S(2)}) collective-permute-start(bf16[2,96,256]{2,1,0:T(8,128)(2,1)S(1)} %get-tuple-element.69), channel_id=1, source_target_pairs={{0,4},{1,5},{2,6},{3,7},{4,0},{5,1},{6,2},{7,3},{8,12},{9,13},{10,... | collective-permute-start | bytes 294920 | tf_op jit(solution)/shard_map/ppermute | solution.py:140
  50.0 1.3 %collective-permute-start.12 = (bf16[2,2,96,256]{3,2,1,0:T(8,128)(2,1)S(1)}, bf16[2,2,96,256]{3,2,1,0:T(8,128)(2,1)S(1)}, u32[]{:S(2)}, u32[]{:S(2)}) collective-permute-start(bf16[2,2,96,256]{3,2,1,0:T(8,128)(2,1)S(1)} %get-tuple-element.57), channel_id=1, source_target_pairs={{0,2},{1,3},{2,0},{3,1},{4,6},{5,7},{6,4},{7,5},{8,10},{9,11},{10,... | collective-permute-start | bytes 589832 | tf_op jit(solution)/shard_map/ppermute | solution.py:140
  51.3 1.5 %collective-permute-done.18.one = bf16[2,96,256]{2,1,0:T(8,128)(2,1)S(1)} collective-permute-done((bf16[2,96,256]{2,1,0:T(8,128)(2,1)S(1)}, bf16[2,96,256]{2,1,0:T(8,128)(2,1)S(1)}, u32[]{:S(2)}, u32[]{:S(2)}) %collective-permute-start.18) | collective-permute-done | bytes 98336 | tf_op jit(solution)/shard_map/ppermute | solution.py:140
  52.8 0.1 renorm.3
  52.9 1.6 %collective-permute-start.24 = (bf16[2,96,256]{2,1,0:T(8,128)(2,1)S(1)}, bf16[2,96,256]{2,1,0:T(8,128)(2,1)S(1)}, u32[]{:S(2)}, u32[]{:S(2)}) collective-permute-start(bf16[2,96,256]{2,1,0:T(8,128)(2,1)S(1)} %get-tuple-element.73), channel_id=1, source_target_pairs={{0,8},{1,9},{2,10},{3,11},{4,12},{5,13},{6,14},{7,15},{8,0},{9,1},... | collective-permute-start | bytes 294920 | tf_op jit(solution)/shard_map/ppermute | solution.py:140
  54.6 1.2 %collective-permute-start.25 = (bf16[2,96,256]{2,1,0:T(8,128)(2,1)S(1)}, bf16[2,96,256]{2,1,0:T(8,128)(2,1)S(1)}, u32[]{:S(2)}, u32[]{:S(2)}) collective-permute-start(bf16[2,96,256]{2,1,0:T(8,128)(2,1)S(1)} %get-tuple-element.73), channel_id=1, source_target_pairs={{0,12},{1,13},{2,14},{3,15},{4,8},{5,9},{6,10},{7,11},{8,4},{9,5},... | collective-permute-start | bytes 294920 | tf_op jit(solution)/shard_map/ppermute | solution.py:140
  55.9 2.4 %collective-permute-start.15 = (bf16[2,96,256]{2,1,0:T(8,128)(2,1)S(1)}, bf16[2,96,256]{2,1,0:T(8,128)(2,1)S(1)}, u32[]{:S(2)}, u32[]{:S(2)}) collective-permute-start(bf16[2,96,256]{2,1,0:T(8,128)(2,1)S(1)} %get-tuple-element.61), channel_id=1, source_target_pairs={{0,8},{1,9},{2,10},{3,11},{4,12},{5,13},{6,14},{7,15},{8,0},{9,1},... | collective-permute-start | bytes 294920 | tf_op jit(solution)/shard_map/ppermute | solution.py:140
  58.3 1.2 %collective-permute-start.16 = (bf16[2,96,256]{2,1,0:T(8,128)(2,1)S(1)}, bf16[2,96,256]{2,1,0:T(8,128)(2,1)S(1)}, u32[]{:S(2)}, u32[]{:S(2)}) collective-permute-start(bf16[2,96,256]{2,1,0:T(8,128)(2,1)S(1)} %get-tuple-element.62), channel_id=1, source_target_pairs={{0,12},{1,13},{2,14},{3,15},{4,8},{5,9},{6,10},{7,11},{8,4},{9,5},... | collective-permute-start | bytes 294920 | tf_op jit(solution)/shard_map/ppermute | solution.py:140
  59.5 0.1 collective-permute-start.13
  59.6 0.4 collective-permute-done.25
  60.1 1.3 %collective-permute-start.31 = (bf16[2,2,96,256]{3,2,1,0:T(8,128)(2,1)S(1)}, bf16[2,2,96,256]{3,2,1,0:T(8,128)(2,1)S(1)}, u32[]{:S(2)}, u32[]{:S(2)}) collective-permute-start(bf16[2,2,96,256]{3,2,1,0:T(8,128)(2,1)S(1)} %pad_maximum_fusion.4.near_high), channel_id=1, source_target_pairs={{0,2},{1,3},{2,0},{3,1},{4,6},{5,7},{6,4},{7,5},{8,10},{9,11},{10,... | collective-permute-start | bytes 589832 | tf_op jit(solution)/shard_map/ppermute | solution.py:140
  61.5 1.2 %collective-permute-start.30 = (bf16[2,2,96,256]{3,2,1,0:T(8,128)(2,1)S(1)}, bf16[2,2,96,256]{3,2,1,0:T(8,128)(2,1)S(1)}, u32[]{:S(2)}, u32[]{:S(2)}) collective-permute-start(bf16[2,2,96,256]{3,2,1,0:T(8,128)(2,1)S(1)} %pad_maximum_fusion.2.near_low), channel_id=1, source_target_pairs={{0,2},{1,3},{2,0},{3,1},{4,6},{5,7},{6,4},{7,5},{8,10},{9,11},{10,... | collective-permute-start | bytes 589832 | tf_op jit(solution)/shard_map/ppermute | solution.py:140
  62.7 1.3 %collective-permute-done.15.two = bf16[2,96,256]{2,1,0:T(8,128)(2,1)S(1)} collective-permute-done((bf16[2,96,256]{2,1,0:T(8,128)(2,1)S(1)}, bf16[2,96,256]{2,1,0:T(8,128)(2,1)S(1)}, u32[]{:S(2)}, u32[]{:S(2)}) %collective-permute-start.15) | collective-permute-done | bytes 98336 | tf_op jit(solution)/shard_map/ppermute | solution.py:140
  64.0 0.6 collective-permute-done.13.one
  64.6 0.2 renorm.2
  64.8 3.6 %collective-permute-start.23 = (bf16[2,96,256]{2,1,0:T(8,128)(2,1)S(1)}, bf16[2,96,256]{2,1,0:T(8,128)(2,1)S(1)}, u32[]{:S(2)}, u32[]{:S(2)}) collective-permute-start(bf16[2,96,256]{2,1,0:T(8,128)(2,1)S(1)} %get-tuple-element.74), channel_id=1, source_target_pairs={{0,4},{1,5},{2,6},{3,7},{4,0},{5,1},{6,2},{7,3},{8,12},{9,13},{10,... | collective-permute-start | bytes 294920 | tf_op jit(solution)/shard_map/ppermute | solution.py:140
  68.3 0.5 collective-permute-start.27
  68.8 1.7 %collective-permute-start.28 = (bf16[2,96,256]{2,1,0:T(8,128)(2,1)S(1)}, bf16[2,96,256]{2,1,0:T(8,128)(2,1)S(1)}, u32[]{:S(2)}, u32[]{:S(2)}) collective-permute-start(bf16[2,96,256]{2,1,0:T(8,128)(2,1)S(1)} %get-tuple-element.74), channel_id=1, source_target_pairs={{0,12},{1,13},{2,14},{3,15},{4,8},{5,9},{6,10},{7,11},{8,4},{9,5},... | collective-permute-start | bytes 294920 | tf_op jit(solution)/shard_map/ppermute | solution.py:140
  70.5 2.8 %collective-permute-done.23 = bf16[2,96,256]{2,1,0:T(8,128)(2,1)S(1)} collective-permute-done((bf16[2,96,256]{2,1,0:T(8,128)(2,1)S(1)}, bf16[2,96,256]{2,1,0:T(8,128)(2,1)S(1)}, u32[]{:S(2)}, u32[]{:S(2)}) %collective-permute-start.23) | collective-permute-done | bytes 98336 | tf_op jit(solution)/shard_map/ppermute | solution.py:140
  73.4 7.6 %collective-permute-start.32 = (f32[2,96,256]{2,1,0:T(8,128)S(1)}, f32[2,96,256]{2,1,0:T(8,128)S(1)}, u32[]{:S(2)}, u32[]{:S(2)}) collective-permute-start(f32[2,96,256]{2,1,0:T(8,128)S(1)} %pad_maximum_fusion.6), channel_id=1, source_target_pairs={{0,1},{1,0},{2,3},{3,2},{4,5},{5,4},{6,7},{7,6},{8,9},{9,8},{10,11... | collective-permute-start | bytes 589832 | tf_op jit(solution)/shard_map/ppermute | solution.py:140
  81.0 0.8 collective-permute-start.29
  81.8 5.2 %collective-permute-start.37 = (bf16[2,2,96,256]{3,2,1,0:T(8,128)(2,1)S(1)}, bf16[2,2,96,256]{3,2,1,0:T(8,128)(2,1)S(1)}, u32[]{:S(2)}, u32[]{:S(2)}) collective-permute-start(bf16[2,2,96,256]{3,2,1,0:T(8,128)(2,1)S(1)} %pad_maximum_fusion.4.near_high), channel_id=1, source_target_pairs={{0,1},{1,0},{2,3},{3,2},{4,5},{5,4},{6,7},{7,6},{8,9},{9,8},{10,11... | collective-permute-start | bytes 589832 | tf_op jit(solution)/shard_map/ppermute | solution.py:140
  87.0 0.1 collective-permute-start.36
  87.1 0.5 collective-permute-start.39
  87.6 0.1 collective-permute-start.38
  87.7 2.5 %apply.4.rest_0_ = bf16[1024,1024]{1,0:T(8,128)(2,1)} custom-call(s32[3]{0:T(128)S(1)} %pad_add_fusion.ids, bf16[2,2,96,256]{3,2,1,0:T(8,128)(2,1)S(1)} %pad_maximum_fusion.2.near_low, bf16[2,2,96,256]{3,2,1,0:T(8,128)(2,1)S(1)} %pad_maximum_fusion.4.near_high, bf16[2,2,96,256]{3,2,1,0:T(8,128)(2,1)S(1)} %collective-permute-done.30.far_low, ...), custom_call_target="tpu_custom_call" | custom-call | flops 805306368 | bytes 1048576 | tf_op jit(solution)/shard_map/apply/pallas_call | solution.py:509
  90.2 1.3 %finish.1 = (f32[4,16,1024]{2,1,0:T(8,128)}, f32[4,32,256]{2,1,0:T(8,128)}) custom-call(s32[3]{0:T(128)S(1)} %pad_add_fusion.ids, f32[2,96,256]{2,1,0:T(8,128)S(1)} %get-tuple-element.76.one, f32[2,96,256]{2,1,0:T(8,128)S(1)} %get-tuple-element.77.two, f32[2,96,256]{2,1,0:T(8,128)S(1)} %collective-permute-done.32.came), custom_call_target="tpu_custom_call" | custom-call | tf_op jit(solution)/shard_map/finish/pallas_call | solution.py:546
  91.5 0.4 collective-permute-start.35
  92.0 0.7 collective-permute-start.26
  92.7 0.4 collective-permute-start.34
  93.2 2.5 %apply.5.rest_0_ = bf16[1024,1024]{1,0:T(8,128)(2,1)} custom-call(s32[3]{0:T(128)S(1)} %pad_add_fusion.ids, bf16[2,2,96,256]{3,2,1,0:T(8,128)(2,1)S(1)} %collective-permute-done.36.near_low, bf16[2,2,96,256]{3,2,1,0:T(8,128)(2,1)S(1)} %collective-permute-done.37.near_high, ...), custom_call_target="tpu_custom_call", output_to_operand_aliasing={{}: (6, {})} | custom-call | flops 805306368 | bytes 1048576 | tf_op jit(solution)/shard_map/apply/pallas_call | solution.py:509
  95.7 1.9 %collective-permute-done.35.far_high = bf16[2,2,96,256]{3,2,1,0:T(8,128)(2,1)S(1)} collective-permute-done((bf16[2,2,96,256]{3,2,1,0:T(8,128)(2,1)S(1)}, bf16[2,2,96,256]{3,2,1,0:T(8,128)(2,1)S(1)}, u32[]{:S(2)}, u32[]{:S(2)}) %collective-permute-start.35) | collective-permute-done | bytes 196640 | tf_op jit(solution)/shard_map/ppermute | solution.py:140
  97.6 1.3 %collective-permute-start.40 = (bf16[2,2,96,256]{3,2,1,0:T(8,128)(2,1)S(1)}, bf16[2,2,96,256]{3,2,1,0:T(8,128)(2,1)S(1)}, u32[]{:S(2)}, u32[]{:S(2)}) collective-permute-start(bf16[2,2,96,256]{3,2,1,0:T(8,128)(2,1)S(1)} %collective-permute-done.35.far_high), channel_id=1, source_target_pairs={{0,1},{1,0},{2,3},{3,2},{4,5},{5,4},{6,7},{7,6},{8,9},{9,8},{10,11... | collective-permute-start | bytes 589832 | tf_op jit(solution)/shard_map/ppermute | solution.py:140
  98.8 2.5 %apply.6.rest_0_ = bf16[1024,1024]{1,0:T(8,128)(2,1)} custom-call(s32[3]{0:T(128)S(1)} %pad_add_fusion.ids, bf16[2,2,96,256]{3,2,1,0:T(8,128)(2,1)S(1)} %pad_maximum_fusion.3.near_low, bf16[2,2,96,256]{3,2,1,0:T(8,128)(2,1)S(1)} %pad_maximum_fusion.5.near_high, ...), custom_call_target="tpu_custom_call", output_to_operand_aliasing={{}: (6, {})} | custom-call | flops 805306368 | bytes 1048576 | tf_op jit(solution)/shard_map/apply/pallas_call | solution.py:509
  101.4 2.5 %apply.7 = bf16[1024,1024]{1,0:T(8,128)(2,1)} custom-call(s32[3]{0:T(128)S(1)} %pad_add_fusion.ids, bf16[2,2,96,256]{3,2,1,0:T(8,128)(2,1)S(1)} %collective-permute-done.26.near_low, bf16[2,2,96,256]{3,2,1,0:T(8,128)(2,1)S(1)} %collective-permute-done.33.near_high, ...), custom_call_target="tpu_custom_call", output_to_operand_aliasing={{}: (6, {})} | custom-call | flops 805306368 | bytes 1048576 | tf_op jit(solution)/shard_map/apply/pallas_call | solution.py:509
  (57 shorter events, 0.6 us)
Async XLA Ops:
  0.7 1.6 %copy-start.3 = (bf16[1024,1024]{1,0:T(8,128)(2,1)S(1)}, bf16[1024,1024]{1,0:T(8,128)(2,1)}, u32[]{:S(2)}) copy-start(bf16[1024,1024]{1,0:T(8,128)(2,1)} %x_ref.2) | copy-start | bytes 6291460
  2.3 1.5 %copy-start.1 = (f32[4,16,1024]{2,1,0:T(8,128)S(1)}, f32[4,16,1024]{2,1,0:T(8,128)}, u32[]{:S(2)}) copy-start(f32[4,16,1024]{2,1,0:T(8,128)} %in_ref.1) | copy-start | bytes 786436
  2.3 1.5 %copy-start.2 = (f32[4,32,256]{2,1,0:T(8,128)S(1)}, f32[4,32,256]{2,1,0:T(8,128)}, u32[]{:S(2)}) copy-start(f32[4,32,256]{2,1,0:T(8,128)} %out_ref.1) | copy-start | bytes 393220
  2.3 3.6 %copy-start.4 = (bf16[1024,1024]{1,0:T(8,128)(2,1)S(1)}, bf16[1024,1024]{1,0:T(8,128)(2,1)}, u32[]{:S(2)}) copy-start(bf16[1024,1024]{1,0:T(8,128)(2,1)} %x_ref.3) | copy-start | bytes 6291460
  2.3 3.6 %copy-start.5 = (f32[4,1024]{1,0:T(4,128)S(1)}, f32[4,1024]{1,0:T(4,128)}, u32[]{:S(2)}) copy-start(f32[4,1024]{1,0:T(4,128)} %rest_0_.1) | copy-start | bytes 49156
  4.4 1.5 %collective-permute-start = (f32[2,96,256]{2,1,0:T(8,128)S(1)}, f32[2,96,256]{2,1,0:T(8,128)S(1)}, u32[]{:S(2)}, u32[]{:S(2)}) collective-permute-start(f32[2,96,256]{2,1,0:T(8,128)S(1)} %get-tuple-element.46), channel_id=1, source_target_pairs={{0,1},{1,0},{2,3},{3,2},{4,5},{5,4},{6,7},{7,6},{8,9},{9,8},{10,11... | collective-permute-start | bytes 589832 | tf_op jit(solution)/shard_map/ppermute | solution.py:140
  4.6 9.7 %collective-permute-start.2 = (bf16[1024,512]{1,0:T(8,128)(2,1)S(1)}, bf16[1024,512]{1,0:T(8,128)(2,1)S(1)}, u32[]{:S(2)}, u32[]{:S(2)}) collective-permute-start(bf16[1024,512]{1,0:T(8,128)(2,1)S(1)} %get-tuple-element.47), channel_id=1, source_target_pairs={{0,1},{1,0},{2,3},{3,2},{4,5},{5,4},{6,7},{7,6},{8,9},{9,8},{10,11... | collective-permute-start | bytes 3145736 | tf_op jit(solution)/shard_map/ppermute | solution.py:140
  8.2 6.0 %collective-permute-start.3 = (bf16[1024,512]{1,0:T(8,128)(2,1)S(1)}, bf16[1024,512]{1,0:T(8,128)(2,1)S(1)}, u32[]{:S(2)}, u32[]{:S(2)}) collective-permute-start(bf16[1024,512]{1,0:T(8,128)(2,1)S(1)} %get-tuple-element.49), channel_id=1, source_target_pairs={{0,1},{1,0},{2,3},{3,2},{4,5},{5,4},{6,7},{7,6},{8,9},{9,8},{10,11... | collective-permute-start | bytes 3145736 | tf_op jit(solution)/shard_map/ppermute | solution.py:140
  8.5 5.8 %collective-permute-start.1 = (bf16[2,96,256]{2,1,0:T(8,128)(2,1)S(1)}, bf16[2,96,256]{2,1,0:T(8,128)(2,1)S(1)}, u32[]{:S(2)}, u32[]{:S(2)}) collective-permute-start(bf16[2,96,256]{2,1,0:T(8,128)(2,1)S(1)} %get-tuple-element.52), channel_id=1, source_target_pairs={{0,4},{1,5},{2,6},{3,7},{4,0},{5,1},{6,2},{7,3},{8,12},{9,13},{10,... | collective-permute-start | bytes 294920 | tf_op jit(solution)/shard_map/ppermute | solution.py:140
  11.2 5.5 %collective-permute-start.5 = (bf16[2,96,256]{2,1,0:T(8,128)(2,1)S(1)}, bf16[2,96,256]{2,1,0:T(8,128)(2,1)S(1)}, u32[]{:S(2)}, u32[]{:S(2)}) collective-permute-start(bf16[2,96,256]{2,1,0:T(8,128)(2,1)S(1)} %get-tuple-element.52), channel_id=1, source_target_pairs={{0,8},{1,9},{2,10},{3,11},{4,12},{5,13},{6,14},{7,15},{8,0},{9,1},... | collective-permute-start | bytes 294920 | tf_op jit(solution)/shard_map/ppermute | solution.py:140
  13.5 6.9 %collective-permute-start.6 = (bf16[2,96,256]{2,1,0:T(8,128)(2,1)S(1)}, bf16[2,96,256]{2,1,0:T(8,128)(2,1)S(1)}, u32[]{:S(2)}, u32[]{:S(2)}) collective-permute-start(bf16[2,96,256]{2,1,0:T(8,128)(2,1)S(1)} %get-tuple-element.52), channel_id=1, source_target_pairs={{0,12},{1,13},{2,14},{3,15},{4,8},{5,9},{6,10},{7,11},{8,4},{9,5},... | collective-permute-start | bytes 294920 | tf_op jit(solution)/shard_map/ppermute | solution.py:140
  14.3 6.2 %collective-permute-start.7 = (bf16[2,2,96,256]{3,2,1,0:T(8,128)(2,1)S(1)}, bf16[2,2,96,256]{3,2,1,0:T(8,128)(2,1)S(1)}, u32[]{:S(2)}, u32[]{:S(2)}) collective-permute-start(bf16[2,2,96,256]{3,2,1,0:T(8,128)(2,1)S(1)} %pad_maximum_fusion.near_low), channel_id=1, source_target_pairs={{0,2},{1,3},{2,0},{3,1},{4,6},{5,7},{6,4},{7,5},{8,10},{9,11},{10,... | collective-permute-start | bytes 589832 | tf_op jit(solution)/shard_map/ppermute | solution.py:140
  15.5 6.2 %collective-permute-start.4 = (bf16[2,2,96,256]{3,2,1,0:T(8,128)(2,1)S(1)}, bf16[2,2,96,256]{3,2,1,0:T(8,128)(2,1)S(1)}, u32[]{:S(2)}, u32[]{:S(2)}) collective-permute-start(bf16[2,2,96,256]{3,2,1,0:T(8,128)(2,1)S(1)} %pad_maximum_fusion.near_low), channel_id=1, source_target_pairs={{0,16},{16,0},{1,17},{17,1},{2,18},{18,2},{3,19},{19,3},{4,20},{20... | collective-permute-start | bytes 589832 | tf_op jit(solution)/shard_map/ppermute | solution.py:144
  20.5 4.6 %collective-permute-start.9 = (bf16[2,2,96,256]{3,2,1,0:T(8,128)(2,1)S(1)}, bf16[2,2,96,256]{3,2,1,0:T(8,128)(2,1)S(1)}, u32[]{:S(2)}, u32[]{:S(2)}) collective-permute-start(bf16[2,2,96,256]{3,2,1,0:T(8,128)(2,1)S(1)} %collective-permute-done.7.far_low), channel_id=1, source_target_pairs={{0,16},{16,0},{1,17},{17,1},{2,18},{18,2},{3,19},{19,3},{4,20},{20... | collective-permute-start | bytes 589832 | tf_op jit(solution)/shard_map/ppermute | solution.py:144
  21.8 4.8 %collective-permute-start.10 = (bf16[2,2,96,256]{3,2,1,0:T(8,128)(2,1)S(1)}, bf16[2,2,96,256]{3,2,1,0:T(8,128)(2,1)S(1)}, u32[]{:S(2)}, u32[]{:S(2)}) collective-permute-start(bf16[2,2,96,256]{3,2,1,0:T(8,128)(2,1)S(1)} %pad_maximum_fusion.1.near_high), channel_id=1, source_target_pairs={{0,2},{1,3},{2,0},{3,1},{4,6},{5,7},{6,4},{7,5},{8,10},{9,11},{10,... | collective-permute-start | bytes 589832 | tf_op jit(solution)/shard_map/ppermute | solution.py:140
  32.2 4.6 %collective-permute-start.19 = (bf16[2,2,96,256]{3,2,1,0:T(8,128)(2,1)S(1)}, bf16[2,2,96,256]{3,2,1,0:T(8,128)(2,1)S(1)}, u32[]{:S(2)}, u32[]{:S(2)}) collective-permute-start(bf16[2,2,96,256]{3,2,1,0:T(8,128)(2,1)S(1)} %get-tuple-element.70), channel_id=1, source_target_pairs={{0,2},{1,3},{2,0},{3,1},{4,6},{5,7},{6,4},{7,5},{8,10},{9,11},{10,... | collective-permute-start | bytes 589832 | tf_op jit(solution)/shard_map/ppermute | solution.py:140
  33.5 7.9 %collective-permute-start.8 = (bf16[2,2,96,256]{3,2,1,0:T(8,128)(2,1)S(1)}, bf16[2,2,96,256]{3,2,1,0:T(8,128)(2,1)S(1)}, u32[]{:S(2)}, u32[]{:S(2)}) collective-permute-start(bf16[2,2,96,256]{3,2,1,0:T(8,128)(2,1)S(1)} %pad_maximum_fusion.1.near_high), channel_id=1, source_target_pairs={{0,16},{16,0},{1,17},{17,1},{2,18},{18,2},{3,19},{19,3},{4,20},{20... | collective-permute-start | bytes 589832 | tf_op jit(solution)/shard_map/ppermute | solution.py:144
  33.8 7.6 %collective-permute-start.11 = (bf16[2,2,96,256]{3,2,1,0:T(8,128)(2,1)S(1)}, bf16[2,2,96,256]{3,2,1,0:T(8,128)(2,1)S(1)}, u32[]{:S(2)}, u32[]{:S(2)}) collective-permute-start(bf16[2,2,96,256]{3,2,1,0:T(8,128)(2,1)S(1)} %collective-permute-done.10.far_high), channel_id=1, source_target_pairs={{0,16},{16,0},{1,17},{17,1},{2,18},{18,2},{3,19},{19,3},{4,20},{20... | collective-permute-start | bytes 589832 | tf_op jit(solution)/shard_map/ppermute | solution.py:144
  35.0 13.5 %collective-permute-start.17 = (bf16[2,2,96,256]{3,2,1,0:T(8,128)(2,1)S(1)}, bf16[2,2,96,256]{3,2,1,0:T(8,128)(2,1)S(1)}, u32[]{:S(2)}, u32[]{:S(2)}) collective-permute-start(bf16[2,2,96,256]{3,2,1,0:T(8,128)(2,1)S(1)} %get-tuple-element.67), channel_id=1, source_target_pairs={{0,2},{1,3},{2,0},{3,1},{4,6},{5,7},{6,4},{7,5},{8,10},{9,11},{10,... | collective-permute-start | bytes 589832 | tf_op jit(solution)/shard_map/ppermute | solution.py:140
  36.8 14.4 %collective-permute-start.20 = (bf16[2,96,256]{2,1,0:T(8,128)(2,1)S(1)}, bf16[2,96,256]{2,1,0:T(8,128)(2,1)S(1)}, u32[]{:S(2)}, u32[]{:S(2)}) collective-permute-start(bf16[2,96,256]{2,1,0:T(8,128)(2,1)S(1)} %get-tuple-element.71), channel_id=1, source_target_pairs={{0,8},{1,9},{2,10},{3,11},{4,12},{5,13},{6,14},{7,15},{8,0},{9,1},... | collective-permute-start | bytes 294920 | tf_op jit(solution)/shard_map/ppermute | solution.py:140
  40.2 11.1 %collective-permute-start.21 = (bf16[2,96,256]{2,1,0:T(8,128)(2,1)S(1)}, bf16[2,96,256]{2,1,0:T(8,128)(2,1)S(1)}, u32[]{:S(2)}, u32[]{:S(2)}) collective-permute-start(bf16[2,96,256]{2,1,0:T(8,128)(2,1)S(1)} %get-tuple-element.72), channel_id=1, source_target_pairs={{0,12},{1,13},{2,14},{3,15},{4,8},{5,9},{6,10},{7,11},{8,4},{9,5},... | collective-permute-start | bytes 294920 | tf_op jit(solution)/shard_map/ppermute | solution.py:140
  47.2 8.6 %collective-permute-start.14 = (bf16[2,2,96,256]{3,2,1,0:T(8,128)(2,1)S(1)}, bf16[2,2,96,256]{3,2,1,0:T(8,128)(2,1)S(1)}, u32[]{:S(2)}, u32[]{:S(2)}) collective-permute-start(bf16[2,2,96,256]{3,2,1,0:T(8,128)(2,1)S(1)} %get-tuple-element.60), channel_id=1, source_target_pairs={{0,2},{1,3},{2,0},{3,1},{4,6},{5,7},{6,4},{7,5},{8,10},{9,11},{10,... | collective-permute-start | bytes 589832 | tf_op jit(solution)/shard_map/ppermute | solution.py:140
  48.5 4.2 %collective-permute-start.18 = (bf16[2,96,256]{2,1,0:T(8,128)(2,1)S(1)}, bf16[2,96,256]{2,1,0:T(8,128)(2,1)S(1)}, u32[]{:S(2)}, u32[]{:S(2)}) collective-permute-start(bf16[2,96,256]{2,1,0:T(8,128)(2,1)S(1)} %get-tuple-element.69), channel_id=1, source_target_pairs={{0,4},{1,5},{2,6},{3,7},{4,0},{5,1},{6,2},{7,3},{8,12},{9,13},{10,... | collective-permute-start | bytes 294920 | tf_op jit(solution)/shard_map/ppermute | solution.py:140
  50.0 8.2 %collective-permute-start.12 = (bf16[2,2,96,256]{3,2,1,0:T(8,128)(2,1)S(1)}, bf16[2,2,96,256]{3,2,1,0:T(8,128)(2,1)S(1)}, u32[]{:S(2)}, u32[]{:S(2)}) collective-permute-start(bf16[2,2,96,256]{3,2,1,0:T(8,128)(2,1)S(1)} %get-tuple-element.57), channel_id=1, source_target_pairs={{0,2},{1,3},{2,0},{3,1},{4,6},{5,7},{6,4},{7,5},{8,10},{9,11},{10,... | collective-permute-start | bytes 589832 | tf_op jit(solution)/shard_map/ppermute | solution.py:140
  52.9 6.6 %collective-permute-start.24 = (bf16[2,96,256]{2,1,0:T(8,128)(2,1)S(1)}, bf16[2,96,256]{2,1,0:T(8,128)(2,1)S(1)}, u32[]{:S(2)}, u32[]{:S(2)}) collective-permute-start(bf16[2,96,256]{2,1,0:T(8,128)(2,1)S(1)} %get-tuple-element.73), channel_id=1, source_target_pairs={{0,8},{1,9},{2,10},{3,11},{4,12},{5,13},{6,14},{7,15},{8,0},{9,1},... | collective-permute-start | bytes 294920 | tf_op jit(solution)/shard_map/ppermute | solution.py:140
  54.6 5.5 %collective-permute-start.25 = (bf16[2,96,256]{2,1,0:T(8,128)(2,1)S(1)}, bf16[2,96,256]{2,1,0:T(8,128)(2,1)S(1)}, u32[]{:S(2)}, u32[]{:S(2)}) collective-permute-start(bf16[2,96,256]{2,1,0:T(8,128)(2,1)S(1)} %get-tuple-element.73), channel_id=1, source_target_pairs={{0,12},{1,13},{2,14},{3,15},{4,8},{5,9},{6,10},{7,11},{8,4},{9,5},... | collective-permute-start | bytes 294920 | tf_op jit(solution)/shard_map/ppermute | solution.py:140
  55.8 5.7 %collective-permute-start.22 = (bf16[2,96,256]{2,1,0:T(8,128)(2,1)S(1)}, bf16[2,96,256]{2,1,0:T(8,128)(2,1)S(1)}, u32[]{:S(2)}, u32[]{:S(2)}) collective-permute-start(bf16[2,96,256]{2,1,0:T(8,128)(2,1)S(1)} %get-tuple-element.73), channel_id=1, source_target_pairs={{0,4},{1,5},{2,6},{3,7},{4,0},{5,1},{6,2},{7,3},{8,12},{9,13},{10,... | collective-permute-start | bytes 294920 | tf_op jit(solution)/shard_map/ppermute | solution.py:140
  55.9 31.8 %copy-start = (bf16[1024,1024]{1,0:T(8,128)(2,1)S(1)}, bf16[1024,1024]{1,0:T(8,128)(2,1)}, u32[]{:S(2)}) copy-start(bf16[1024,1024]{1,0:T(8,128)(2,1)} %q_ref.7) | copy-start | bytes 6291460
  55.9 8.1 %collective-permute-start.15 = (bf16[2,96,256]{2,1,0:T(8,128)(2,1)S(1)}, bf16[2,96,256]{2,1,0:T(8,128)(2,1)S(1)}, u32[]{:S(2)}, u32[]{:S(2)}) collective-permute-start(bf16[2,96,256]{2,1,0:T(8,128)(2,1)S(1)} %get-tuple-element.61), channel_id=1, source_target_pairs={{0,8},{1,9},{2,10},{3,11},{4,12},{5,13},{6,14},{7,15},{8,0},{9,1},... | collective-permute-start | bytes 294920 | tf_op jit(solution)/shard_map/ppermute | solution.py:140
  58.3 5.8 %collective-permute-start.16 = (bf16[2,96,256]{2,1,0:T(8,128)(2,1)S(1)}, bf16[2,96,256]{2,1,0:T(8,128)(2,1)S(1)}, u32[]{:S(2)}, u32[]{:S(2)}) collective-permute-start(bf16[2,96,256]{2,1,0:T(8,128)(2,1)S(1)} %get-tuple-element.62), channel_id=1, source_target_pairs={{0,12},{1,13},{2,14},{3,15},{4,8},{5,9},{6,10},{7,11},{8,4},{9,5},... | collective-permute-start | bytes 294920 | tf_op jit(solution)/shard_map/ppermute | solution.py:140
  59.5 5.1 %collective-permute-start.13 = (bf16[2,96,256]{2,1,0:T(8,128)(2,1)S(1)}, bf16[2,96,256]{2,1,0:T(8,128)(2,1)S(1)}, u32[]{:S(2)}, u32[]{:S(2)}) collective-permute-start(bf16[2,96,256]{2,1,0:T(8,128)(2,1)S(1)} %get-tuple-element.59), channel_id=1, source_target_pairs={{0,4},{1,5},{2,6},{3,7},{4,0},{5,1},{6,2},{7,3},{8,12},{9,13},{10,... | collective-permute-start | bytes 294920 | tf_op jit(solution)/shard_map/ppermute | solution.py:140
  60.1 26.9 %collective-permute-start.31 = (bf16[2,2,96,256]{3,2,1,0:T(8,128)(2,1)S(1)}, bf16[2,2,96,256]{3,2,1,0:T(8,128)(2,1)S(1)}, u32[]{:S(2)}, u32[]{:S(2)}) collective-permute-start(bf16[2,2,96,256]{3,2,1,0:T(8,128)(2,1)S(1)} %pad_maximum_fusion.4.near_high), channel_id=1, source_target_pairs={{0,2},{1,3},{2,0},{3,1},{4,6},{5,7},{6,4},{7,5},{8,10},{9,11},{10,... | collective-permute-start | bytes 589832 | tf_op jit(solution)/shard_map/ppermute | solution.py:140
  61.5 25.6 %collective-permute-start.30 = (bf16[2,2,96,256]{3,2,1,0:T(8,128)(2,1)S(1)}, bf16[2,2,96,256]{3,2,1,0:T(8,128)(2,1)S(1)}, u32[]{:S(2)}, u32[]{:S(2)}) collective-permute-start(bf16[2,2,96,256]{3,2,1,0:T(8,128)(2,1)S(1)} %pad_maximum_fusion.2.near_low), channel_id=1, source_target_pairs={{0,2},{1,3},{2,0},{3,1},{4,6},{5,7},{6,4},{7,5},{8,10},{9,11},{10,... | collective-permute-start | bytes 589832 | tf_op jit(solution)/shard_map/ppermute | solution.py:140
  64.8 8.6 %collective-permute-start.23 = (bf16[2,96,256]{2,1,0:T(8,128)(2,1)S(1)}, bf16[2,96,256]{2,1,0:T(8,128)(2,1)S(1)}, u32[]{:S(2)}, u32[]{:S(2)}) collective-permute-start(bf16[2,96,256]{2,1,0:T(8,128)(2,1)S(1)} %get-tuple-element.74), channel_id=1, source_target_pairs={{0,4},{1,5},{2,6},{3,7},{4,0},{5,1},{6,2},{7,3},{8,12},{9,13},{10,... | collective-permute-start | bytes 294920 | tf_op jit(solution)/shard_map/ppermute | solution.py:140
  68.3 12.6 %collective-permute-start.27 = (bf16[2,96,256]{2,1,0:T(8,128)(2,1)S(1)}, bf16[2,96,256]{2,1,0:T(8,128)(2,1)S(1)}, u32[]{:S(2)}, u32[]{:S(2)}) collective-permute-start(bf16[2,96,256]{2,1,0:T(8,128)(2,1)S(1)} %get-tuple-element.74), channel_id=1, source_target_pairs={{0,8},{1,9},{2,10},{3,11},{4,12},{5,13},{6,14},{7,15},{8,0},{9,1},... | collective-permute-start | bytes 294920 | tf_op jit(solution)/shard_map/ppermute | solution.py:140
  68.8 13.0 %collective-permute-start.28 = (bf16[2,96,256]{2,1,0:T(8,128)(2,1)S(1)}, bf16[2,96,256]{2,1,0:T(8,128)(2,1)S(1)}, u32[]{:S(2)}, u32[]{:S(2)}) collective-permute-start(bf16[2,96,256]{2,1,0:T(8,128)(2,1)S(1)} %get-tuple-element.74), channel_id=1, source_target_pairs={{0,12},{1,13},{2,14},{3,15},{4,8},{5,9},{6,10},{7,11},{8,4},{9,5},... | collective-permute-start | bytes 294920 | tf_op jit(solution)/shard_map/ppermute | solution.py:140
  73.4 14.2 %collective-permute-start.32 = (f32[2,96,256]{2,1,0:T(8,128)S(1)}, f32[2,96,256]{2,1,0:T(8,128)S(1)}, u32[]{:S(2)}, u32[]{:S(2)}) collective-permute-start(f32[2,96,256]{2,1,0:T(8,128)S(1)} %pad_maximum_fusion.6), channel_id=1, source_target_pairs={{0,1},{1,0},{2,3},{3,2},{4,5},{5,4},{6,7},{7,6},{8,9},{9,8},{10,11... | collective-permute-start | bytes 589832 | tf_op jit(solution)/shard_map/ppermute | solution.py:140
  81.0 10.5 %collective-permute-start.29 = (bf16[2,2,96,256]{3,2,1,0:T(8,128)(2,1)S(1)}, bf16[2,2,96,256]{3,2,1,0:T(8,128)(2,1)S(1)}, u32[]{:S(2)}, u32[]{:S(2)}) collective-permute-start(bf16[2,2,96,256]{3,2,1,0:T(8,128)(2,1)S(1)} %pad_maximum_fusion.3.near_low), channel_id=1, source_target_pairs={{0,2},{1,3},{2,0},{3,1},{4,6},{5,7},{6,4},{7,5},{8,10},{9,11},{10,... | collective-permute-start | bytes 589832 | tf_op jit(solution)/shard_map/ppermute | solution.py:140
  81.8 10.2 %collective-permute-start.37 = (bf16[2,2,96,256]{3,2,1,0:T(8,128)(2,1)S(1)}, bf16[2,2,96,256]{3,2,1,0:T(8,128)(2,1)S(1)}, u32[]{:S(2)}, u32[]{:S(2)}) collective-permute-start(bf16[2,2,96,256]{3,2,1,0:T(8,128)(2,1)S(1)} %pad_maximum_fusion.4.near_high), channel_id=1, source_target_pairs={{0,1},{1,0},{2,3},{3,2},{4,5},{5,4},{6,7},{7,6},{8,9},{9,8},{10,11... | collective-permute-start | bytes 589832 | tf_op jit(solution)/shard_map/ppermute | solution.py:140
  87.0 5.6 %collective-permute-start.36 = (bf16[2,2,96,256]{3,2,1,0:T(8,128)(2,1)S(1)}, bf16[2,2,96,256]{3,2,1,0:T(8,128)(2,1)S(1)}, u32[]{:S(2)}, u32[]{:S(2)}) collective-permute-start(bf16[2,2,96,256]{3,2,1,0:T(8,128)(2,1)S(1)} %pad_maximum_fusion.2.near_low), channel_id=1, source_target_pairs={{0,1},{1,0},{2,3},{3,2},{4,5},{5,4},{6,7},{7,6},{8,9},{9,8},{10,11... | collective-permute-start | bytes 589832 | tf_op jit(solution)/shard_map/ppermute | solution.py:140
  87.1 5.6 %collective-permute-start.39 = (bf16[2,2,96,256]{3,2,1,0:T(8,128)(2,1)S(1)}, bf16[2,2,96,256]{3,2,1,0:T(8,128)(2,1)S(1)}, u32[]{:S(2)}, u32[]{:S(2)}) collective-permute-start(bf16[2,2,96,256]{3,2,1,0:T(8,128)(2,1)S(1)} %collective-permute-done.31.far_high), channel_id=1, source_target_pairs={{0,1},{1,0},{2,3},{3,2},{4,5},{5,4},{6,7},{7,6},{8,9},{9,8},{10,11... | collective-permute-start | bytes 589832 | tf_op jit(solution)/shard_map/ppermute | solution.py:140
  87.6 5.6 %collective-permute-start.38 = (bf16[2,2,96,256]{3,2,1,0:T(8,128)(2,1)S(1)}, bf16[2,2,96,256]{3,2,1,0:T(8,128)(2,1)S(1)}, u32[]{:S(2)}, u32[]{:S(2)}) collective-permute-start(bf16[2,2,96,256]{3,2,1,0:T(8,128)(2,1)S(1)} %collective-permute-done.30.far_low), channel_id=1, source_target_pairs={{0,1},{1,0},{2,3},{3,2},{4,5},{5,4},{6,7},{7,6},{8,9},{9,8},{10,11... | collective-permute-start | bytes 589832 | tf_op jit(solution)/shard_map/ppermute | solution.py:140
  91.5 6.1 %collective-permute-start.35 = (bf16[2,2,96,256]{3,2,1,0:T(8,128)(2,1)S(1)}, bf16[2,2,96,256]{3,2,1,0:T(8,128)(2,1)S(1)}, u32[]{:S(2)}, u32[]{:S(2)}) collective-permute-start(bf16[2,2,96,256]{3,2,1,0:T(8,128)(2,1)S(1)} %pad_maximum_fusion.5.near_high), channel_id=1, source_target_pairs={{0,2},{1,3},{2,0},{3,1},{4,6},{5,7},{6,4},{7,5},{8,10},{9,11},{10,... | collective-permute-start | bytes 589832 | tf_op jit(solution)/shard_map/ppermute | solution.py:140
  92.0 9.4 %collective-permute-start.26 = (bf16[2,2,96,256]{3,2,1,0:T(8,128)(2,1)S(1)}, bf16[2,2,96,256]{3,2,1,0:T(8,128)(2,1)S(1)}, u32[]{:S(2)}, u32[]{:S(2)}) collective-permute-start(bf16[2,2,96,256]{3,2,1,0:T(8,128)(2,1)S(1)} %pad_maximum_fusion.3.near_low), channel_id=1, source_target_pairs={{0,1},{1,0},{2,3},{3,2},{4,5},{5,4},{6,7},{7,6},{8,9},{9,8},{10,11... | collective-permute-start | bytes 589832 | tf_op jit(solution)/shard_map/ppermute | solution.py:140
  92.7 8.7 %collective-permute-start.33 = (bf16[2,2,96,256]{3,2,1,0:T(8,128)(2,1)S(1)}, bf16[2,2,96,256]{3,2,1,0:T(8,128)(2,1)S(1)}, u32[]{:S(2)}, u32[]{:S(2)}) collective-permute-start(bf16[2,2,96,256]{3,2,1,0:T(8,128)(2,1)S(1)} %pad_maximum_fusion.5.near_high), channel_id=1, source_target_pairs={{0,1},{1,0},{2,3},{3,2},{4,5},{5,4},{6,7},{7,6},{8,9},{9,8},{10,11... | collective-permute-start | bytes 589832 | tf_op jit(solution)/shard_map/ppermute | solution.py:140
  92.7 8.6 %collective-permute-start.34 = (bf16[2,2,96,256]{3,2,1,0:T(8,128)(2,1)S(1)}, bf16[2,2,96,256]{3,2,1,0:T(8,128)(2,1)S(1)}, u32[]{:S(2)}, u32[]{:S(2)}) collective-permute-start(bf16[2,2,96,256]{3,2,1,0:T(8,128)(2,1)S(1)} %collective-permute-done.29.far_low), channel_id=1, source_target_pairs={{0,1},{1,0},{2,3},{3,2},{4,5},{5,4},{6,7},{7,6},{8,9},{9,8},{10,11... | collective-permute-start | bytes 589832 | tf_op jit(solution)/shard_map/ppermute | solution.py:140
  97.6 3.8 %collective-permute-start.40 = (bf16[2,2,96,256]{3,2,1,0:T(8,128)(2,1)S(1)}, bf16[2,2,96,256]{3,2,1,0:T(8,128)(2,1)S(1)}, u32[]{:S(2)}, u32[]{:S(2)}) collective-permute-start(bf16[2,2,96,256]{3,2,1,0:T(8,128)(2,1)S(1)} %collective-permute-done.35.far_high), channel_id=1, source_target_pairs={{0,1},{1,0},{2,3},{3,2},{4,5},{5,4},{6,7},{7,6},{8,9},{9,8},{10,11... | collective-permute-start | bytes 589832 | tf_op jit(solution)/shard_map/ppermute | solution.py:140
